TPU v7x, 32 devices: a whole 2x2x4 slice. The times are simulated.
32 devices in a mesh: parts: 2 (over y), blk: 4 (over z), grp: 2 (over x), sub: 2 (over core).
Axes of the slice: x: 2, y: 2, z: 4, core: 2. Of those that a mesh axis runs over, the one named last changes fastest.
Arguments:
- features: bfloat16 [128, 8192], P(None, ('parts', 'blk', 'grp', 'sub')), parts along dimension 1, may hold values from -6 to 6
- lengthscale: float32 [256], P('parts'), parts along dimension 0, may hold values from 4 to 12
- noise_var: float32 [8192], P(('parts', 'blk', 'grp', 'sub')), parts along dimension 0, may hold values from 0.05 to 1
- probes: float32 [16, 8192], P(None, ('parts', 'blk', 'grp', 'sub')), parts along dimension 1, may hold values from -24 to 24
Outputs:
- solution: float32 [16, 8192], P(None, ('parts', 'blk', 'grp', 'sub')), parts along dimension 1
- residual: float32 [16, 8192], P(None, ('parts', 'blk', 'grp', 'sub')), parts along dimension 1
- direction: float32 [16, 8192], P(None, ('parts', 'blk', 'grp', 'sub')), parts along dimension 1
There are 2 independent parts, one for each index of `parts`. A program takes and returns all parts, laid end to end along the dimension named above; each array names one. Nothing has to cross between parts.
All inputs are finite; a program needn't handle non-finite values.
Results may differ from a plain program's by a relative error of at most 0.005.
Values may be sent and summed in bfloat16 or wider, within the bound.
No kernel may reach another device: no remote copies, remote signals or barrier semaphores. Data moves between devices by JAX's collectives and lax.ppermute only.
A program may use at most 64 MiB of HBM per device.

v0:
```python
import jax
import jax.numpy as jnp
from jax import lax
from jax.sharding import PartitionSpec as P


def kernel_block(running, row_scaled, row_norms, col_scaled, col_probes):
    inner = lax.dot_general(
        col_scaled, row_scaled, (((0,), (0,)), ((), ())), preferred_element_type=jnp.float32
    )
    col_norms = jnp.sum(jnp.square(col_scaled.astype(jnp.float32)), axis=0)
    weights = jnp.exp(-0.5 * (col_norms[:, None] + row_norms[None, :] - 2.0 * inner)).astype(
        jnp.bfloat16
    )
    return running + jnp.dot(col_probes, weights, preferred_element_type=jnp.float32)


def apply_columns(running, row_scaled, row_norms, col_scaled, col_probes):
    column_count = col_scaled.shape[1]
    row_count = row_scaled.shape[1]
    splits = 1
    while row_count * (column_count // splits) > 1048576 and column_count % (2 * splits) == 0:
        splits = splits * 2
    stride = column_count // splits

    def one_block(block_number, partial_value):
        offset = block_number * stride
        block_scaled = lax.dynamic_slice_in_dim(col_scaled, offset, stride, 1)
        block_probes = lax.dynamic_slice_in_dim(col_probes, offset, stride, 1)
        return kernel_block(partial_value, row_scaled, row_norms, block_scaled, block_probes)

    return lax.fori_loop(0, splits, one_block, running)


def local(features, lengthscale, noise_var, probes):
    scaled = (features.astype(jnp.float32) / lengthscale[:, None]).astype(jnp.bfloat16)
    probe_bf = probes.astype(jnp.bfloat16)
    start_norms = lax.psum(jnp.sum(probes * probes, axis=1), ("blk", "grp", "sub"))
    row_scaled = lax.all_gather(scaled, ("grp", "sub"), axis=1, tiled=True)
    row_norms = jnp.sum(jnp.square(row_scaled.astype(jnp.float32)), axis=0)
    empty = jnp.zeros((probes.shape[0], row_scaled.shape[1]), jnp.float32)
    partial_value = apply_columns(
        empty,
        row_scaled,
        row_norms,
        lax.all_gather(scaled, "blk", axis=1, tiled=True),
        lax.all_gather(probe_bf, "blk", axis=1, tiled=True),
    )
    kernel_part = lax.psum_scatter(partial_value, ("grp", "sub"), scatter_dimension=1, tiled=True)
    image = kernel_part + noise_var[None, :] * probes
    curvature = lax.psum(jnp.sum(probes * image, axis=1), ("blk", "grp", "sub"))
    alpha = start_norms / curvature
    residual = probes - alpha[:, None] * image
    new_norms = lax.psum(jnp.sum(residual * residual, axis=1), ("blk", "grp", "sub"))
    solution = alpha[:, None] * probes
    direction = residual + (new_norms / start_norms)[:, None] * probes
    return (solution, residual, direction)


def solution(mesh):
    return jax.shard_map(
        local,
        mesh=mesh,
        in_specs=(
            P(None, ("parts", "blk", "grp", "sub")),
            P("parts"),
            P(("parts", "blk", "grp", "sub")),
            P(None, ("parts", "blk", "grp", "sub")),
        ),
        out_specs=(
            P(None, ("parts", "blk", "grp", "sub")),
            P(None, ("parts", "blk", "grp", "sub")),
            P(None, ("parts", "blk", "grp", "sub")),
        ),
        check_vma=False,
    )
```

profile of v0, /device:TPU:0, one launch (start us, length us, event | category | flops | bytes accessed | tf_op | source)
XLA Modules:
  0.0 137.1 jit_solution(5059991542595644416)
XLA Ops:
  7.2 0.0 reduce-scatter.2.cloned.1.call-start
  7.2 0.9 divide_convert_fusion
  8.1 0.0 copy-start
  8.2 7.2 %all_gather.10 = bf16[128,1024]{1,0:T(8,128)(2,1)S(1)} all-gather(bf16[128,256]{1,0:T(8,128)(2,1)S(1)} %divide_convert_fusion), channel_id=1, replica_groups=mesh['parts'=2,'blk'=4,'grp'=2,'sub'=2] {'grp','sub'}, dimensions={1}, use_global_device_ids=true | all-gather | bytes 327680 | tf_op jit(solution)/shard_map/all_gather | solution.py:39
  15.4 14.1 %all_gather.9 = bf16[128,1024]{1,0:T(8,128)(2,1)S(1)} all-gather(bf16[128,256]{1,0:T(8,128)(2,1)S(1)} %divide_convert_fusion), channel_id=1, replica_groups=mesh['parts'=2,'blk'=4,'grp'=2,'sub'=2] {'blk'}, dimensions={1}, use_global_device_ids=true | all-gather | bytes 327680 | tf_op jit(solution)/shard_map/all_gather | solution.py:46
  29.5 0.0 copy-done
  29.5 13.2 %all_gather.11 = bf16[16,1024]{1,0:T(8,128)(2,1)S(1)} all-gather(bf16[16,256]{1,0:T(8,128)(2,1)S(1)} %convert_element_type.25), channel_id=1, replica_groups=mesh['parts'=2,'blk'=4,'grp'=2,'sub'=2] {'blk'}, dimensions={1}, use_global_device_ids=true | all-gather | bytes 40960 | tf_op jit(solution)/shard_map/all_gather | solution.py:47
  42.7 0.1 multiply_reduce_fusion
  42.8 0.1 multiply_reduce_fusion.1
  42.9 0.0 copy-start.2
  42.9 1.9 %fusion.1 = f32[16,1024]{1,0:T(8,128)} fusion(bf16[16,1024]{1,0:T(8,128)(2,1)S(1)} %all_gather.11, bf16[128,1024]{1,0:T(8,128)(2,1)S(1)} %all_gather.9, bf16[128,1024]{1,0:T(8,128)(2,1)S(1)} %all_gather.10, f32[1024]{0:T(1024)S(1)} %multiply_reduce_fusion, f32[1024]{0:T(1024)S(1)} %multiply_reduce_fusion.1), kind=kOutput, calls=%fused_computation.2 | convolution fusion | flops 307232768 | bytes 630784 | tf_op jit(solution)/shard_map/while/body/eval_jaxpr/dot_general | solution.py:15
  44.8 0.0 reduce-scatter.2.cloned.1.call-update
  44.8 21.1 %reduce-scatter.2.cloned.1.call-done = f32[16,256]{1,0:T(8,128)} async-done(((f32[16,1024]{1,0:T(8,128)}), f32[16,256]{1,0:T(8,128)}) %reduce-scatter.2.cloned.1.call-update) | async-done | bytes 16400 | tf_op jit(solution)/shard_map/reduce_scatter | solution.py:49
  65.9 0.0 copy-done.2
  65.9 0.8 multiply_reduce_fusion.3
  66.7 31.8 %all-reduce = (f32[16]{0:T(128)S(1)}, f32[16]{0:T(128)S(1)}) all-reduce(f32[16]{0:T(128)S(1)} %get-tuple-element.18, f32[16]{0:T(128)S(1)} %get-tuple-element.17), channel_id=1, replica_groups=mesh['parts'=2,'blk'=4,'grp'=2,'sub'=2] {'blk','grp','sub'}, use_global_device_ids=true, to_apply=%region_1.0 | all-reduce | flops 32 | bytes 256 | tf_op jit(solution)/shard_map/psum | solution.py:38
  98.5 1.5 %multiply_reduce_fusion.2 = (f32[16]{0:T(128)S(1)}, f32[16,256]{1,0:T(8,128)S(1)}, f32[16,256]{1,0:T(8,128)}) fusion(f32[16,256]{1,0:T(8,128)S(1)} %copy-done, f32[16,256]{1,0:T(8,128)} %reduce-scatter.2.cloned.1.call-done, f32[256]{0:T(256)S(1)} %copy-done.2, f32[16]{0:T(128)S(1)} %div.16), kind=kLoop, calls=%fused_computation.7 | loop fusion | flops 28656 | bytes 66688 | tf_op jit(solution)/shard_map/reduce_sum | solution.py:54
  100.0 0.0 copy-start.1
  100.0 29.5 %psum.23 = f32[16]{0:T(128)S(1)} all-reduce(f32[16]{0:T(128)S(1)} %get-tuple-element.28), channel_id=1, replica_groups=mesh['parts'=2,'blk'=4,'grp'=2,'sub'=2] {'blk','grp','sub'}, use_global_device_ids=true, to_apply=%region_8.0 | all-reduce | flops 16 | bytes 128 | tf_op jit(solution)/shard_map/psum | solution.py:54
  129.5 0.7 multiply_add_fusion
  130.2 0.0 copy-done.1
  (3 shorter events, 0.0 us)
Async XLA Ops:
  7.2 58.7 %reduce-scatter.2.cloned.1.call-start = ((), (), s32[]{:S(2)}) async-start(), calls=%async_computation.1 | async-start | bytes 81920 | tf_op jit(solution)/shard_map/reduce_scatter | solution.py:49
  8.1 21.3 %copy-start = (f32[16,256]{1,0:T(8,128)S(1)}, f32[16,256]{1,0:T(8,128)}, u32[]{:S(2)}) copy-start(f32[16,256]{1,0:T(8,128)} %param.7) | copy-start | bytes 49156
  42.9 23.1 %copy-start.2 = (f32[256]{0:T(256)S(1)}, f32[256]{0:T(256)}, u32[]{:S(2)}) copy-start(f32[256]{0:T(256)} %param.6) | copy-start | bytes 3076
  100.0 30.2 %copy-start.1 = (f32[16,256]{1,0:T(8,128)}, f32[16,256]{1,0:T(8,128)S(1)}, u32[]{:S(2)}) copy-start(f32[16,256]{1,0:T(8,128)S(1)} %get-tuple-element.29) | copy-start | bytes 49156
Sparse Core Ops, SparseCore 0:
  44.9 20.9 reduce-scatter.1
where the time goes:
time: 137 us
  blocking collectives  95.8 us (70%)
  waiting for transfers between devices  21.1 us (15%)
  between operations  14.1 us (10%)
  other arithmetic  4.11 us (3%)
  matrix products  1.91 us (1%)
    psum x1, blocking collectives, local(): lax.psum(jnp.sum(probes * probes, axis=1), ('blk', 'grp', 'sub'))  31.8 us
    psum x1, blocking collectives, local(): lax.psum(jnp.sum(residual * residual, axis=1), ('blk', 'grp', 'sub'))  29.5 us
    reduce_scatter x1, waiting for transfers between devices, local(): lax.psum_scatter(partial_value, ('grp', 'sub'), scatter_dimension=1, tile...  21.1 us
    all_gather x1, blocking collectives, local(): lax.all_gather(scaled, 'blk', axis=1, tiled=True)  14.1 us
    all_gather x1, blocking collectives, local(): lax.all_gather(probe_bf, 'blk', axis=1, tiled=True)  13.2 us
    all_gather x1, blocking collectives, local(): row_scaled = lax.all_gather(scaled, ('grp', 'sub'), axis=1, tiled=True)  7.19 us
  transfers between devices with their start and end apart: 1, of which 1 were waited for; matrix products, arithmetic and copies ran while one was open for 0% of the time, Pallas kernels for 0%

commit v1 on v0

v1 whole, which is shorter than its diff:
```python
import jax
import jax.numpy as jnp
from jax import lax
from jax.experimental import pallas as pl
from jax.experimental.pallas import tpu as pltpu
from jax.sharding import PartitionSpec as P

AXES = ("blk", "grp", "sub")


def image_kernel(feature_count, own_ref, noise_ref, probes_ref, packed_ref, image_ref, sums_ref):
    own = own_ref[:feature_count, :]
    own_norms = jnp.sum(jnp.square(own.astype(jnp.float32)), axis=0, keepdims=True)
    probes = probes_ref[...]

    def one_block(number, total):
        block = packed_ref[number]
        columns = block[:feature_count, :]
        inner = lax.dot_general(
            columns, own, (((0,), (0,)), ((), ())), preferred_element_type=jnp.float32
        )
        norms = jnp.sum(jnp.square(columns.astype(jnp.float32)), axis=0, keepdims=True)
        weights = jnp.exp(-0.5 * (norms.T + own_norms - 2.0 * inner)).astype(jnp.bfloat16)
        return total + jnp.dot(
            block[feature_count:, :], weights, preferred_element_type=jnp.float32
        )

    total = lax.fori_loop(0, packed_ref.shape[0], one_block, jnp.zeros_like(probes))
    image = total + noise_ref[...] * probes
    image_ref[...] = image
    sums_ref[0] = jnp.sum(probes * probes, axis=1, keepdims=True)
    sums_ref[1] = jnp.sum(probes * image, axis=1, keepdims=True)
    sums_ref[2] = jnp.sum(image * image, axis=1, keepdims=True)


def local(features, lengthscale, noise_var, probes):
    scaled = (features.astype(jnp.float32) / lengthscale[:, None]).astype(jnp.bfloat16)
    packed = jnp.concatenate([scaled, probes.astype(jnp.bfloat16)], axis=0)
    gathered = lax.all_gather(packed, AXES, axis=0, tiled=False)
    image, sums = pl.pallas_call(
        lambda *refs: image_kernel(features.shape[0], *refs),
        out_shape=(
            jax.ShapeDtypeStruct(probes.shape, jnp.float32),
            jax.ShapeDtypeStruct((3, probes.shape[0], 1), jnp.float32),
        ),
        in_specs=[pl.BlockSpec(memory_space=pltpu.VMEM)] * 4,
        out_specs=(pl.BlockSpec(memory_space=pltpu.VMEM),) * 2,
        compiler_params=pltpu.CompilerParams(vmem_limit_bytes=48 * 1024 * 1024),
    )(packed, noise_var[None, :], probes, gathered)
    sums = jnp.sum(lax.all_gather(sums.reshape(3, -1), AXES, axis=0, tiled=False), axis=0)
    start_norms, curvature, image_norms = sums[0], sums[1], sums[2]
    alpha = start_norms / curvature
    new_norms = start_norms - 2.0 * alpha * curvature + alpha * alpha * image_norms
    residual = probes - alpha[:, None] * image
    solution = alpha[:, None] * probes
    direction = residual + (new_norms / start_norms)[:, None] * probes
    return (solution, residual, direction)


def solution(mesh):
    spread = P(None, ("parts", "blk", "grp", "sub"))
    return jax.shard_map(
        local,
        mesh=mesh,
        in_specs=(spread, P("parts"), P(("parts", "blk", "grp", "sub")), spread),
        out_specs=(spread, spread, spread),
        check_vma=False,
    )
```

time: 137 us -> 89.9 us (0.66)
  blocking collectives: 95.8 us -> 19.4 us
  waiting for transfers between devices: 21.1 us -> 41.8 us
  Pallas kernels: 0 us -> 6.26 us
  local copies, waits for them, and re-layouts: 0.02 us -> 4.17 us
  matrix products: 1.91 us -> 0 us
    psum x2 -> x0, blocking collectives: 61.3 us -> none  [the longest x1 31.8 us: local(): lax.psum(jnp.sum(probes * probes, axis=1), ('blk', 'grp', 'sub'))]
    all_gather x0 -> x1, waiting for transfers between devices: none -> 41.8 us  [local(): gathered = lax.all_gather(packed, AXES, axis=0, tiled=False)]
    reduce_scatter x1 -> x0, waiting for transfers between devices: 21.1 us -> none  [local(): lax.psum_scatter(partial_value, ('grp', 'sub'), scatter_dimension=1, tile...]
    all_gather x3 -> x1, blocking collectives: 34.5 us -> 19.4 us  [local(): lax.all_gather(sums.reshape(3, -1), AXES, axis=0, tiled=False)]
    pallas_call x0 -> x1, Pallas kernels: none -> 6.26 us  [local(): pl.pallas_call(lambda *refs: image_kernel(features.shape[0], *refs), out_...]
    unnamed x6 -> x10, local copies, waits for them, and re-layouts: 0.02 us -> 3.56 us
    reduce_sum x4 -> x1, other arithmetic: 2.48 us -> 0.03 us  [local(): jnp.sum(lax.all_gather(sums.reshape(3, -1), AXES, axis=0, tiled=False), a...]
    dot_general x1 -> x0, matrix products: 1.91 us -> none  [kernel_block(): jnp.dot(col_probes, weights, preferred_element_type=jnp.float32)]
where the time goes in v1:
time: 89.9 us; the launch traced here: 89.5 us
  waiting for transfers between devices  41.8 us (46%)
  blocking collectives  19.4 us (22%)
  between operations  14.1 us (16%)
  Pallas kernels  6.26 us (7%)
  local copies, waits for them, and re-layouts  4.17 us (5%)
  other arithmetic  3.74 us (4%)
    all_gather x1, waiting for transfers between devices, local(): gathered = lax.all_gather(packed, AXES, axis=0, tiled=False)  41.8 us
    all_gather x1, blocking collectives, local(): lax.all_gather(sums.reshape(3, -1), AXES, axis=0, tiled=False)  19.4 us
    pallas_call x1, Pallas kernels, local(): pl.pallas_call(lambda *refs: image_kernel(features.shape[0], *refs), out_...  6.26 us
    unnamed x10, local copies, waits for them, and re-layouts  3.56 us
  transfers between devices with their start and end apart: 1, of which 1 were waited for; matrix products, arithmetic and copies ran while one was open for 0% of the time, Pallas kernels for 0%

profile of v1, /device:TPU:0, one launch (start us, length us, event | category | flops | bytes accessed | tf_op | source)
XLA Modules:
  0.0 89.5 jit_solution(3289229485051909955)
XLA Ops:
  7.2 0.0 copy-start.3
  7.2 0.0 all-gather.4.cloned.1.call-start
  7.2 0.7 convert_element_type.11
  8.0 0.9 %divide_convert_fusion = bf16[128,256]{1,0:T(8,128)(2,1)S(1)} fusion(bf16[128,256]{1,0:T(8,128)(2,1)} %param.4, f32[128]{0:T(128)} %param.5), kind=kLoop, calls=%fused_computation | loop fusion | flops 98304 | bytes 131584 | tf_op jit(solution)/shard_map/convert_element_type | solution.py:37
  8.9 0.6 pad_maximum_fusion.refs_0_
  9.5 0.0 all-gather.4.cloned.1.call-update
  9.6 41.8 %all-gather.4.cloned.1.call-done = bf16[2304,256]{1,0:T(8,128)(2,1)} async-done(((bf16[144,256]{1,0:T(8,128)(2,1)}), bf16[2304,256]{1,0:T(8,128)(2,1)}) %all-gather.4.cloned.1.call-update) | async-done | bytes 1179664 | tf_op jit(solution)/shard_map/all_gather | solution.py:39
  51.4 0.0 copy-start
  51.4 1.3 %copy-done = bf16[2304,256]{1,0:T(8,128)(2,1)S(1)} copy-done((bf16[2304,256]{1,0:T(8,128)(2,1)S(1)}, bf16[2304,256]{1,0:T(8,128)(2,1)}, u32[]{:S(2)}) %copy-start) | copy-done | bytes 1179672
  52.6 0.0 copy-start.1
  52.6 0.9 copy-done.1
  53.5 0.0 copy-start.2
  53.5 0.7 copy-done.2
  54.2 0.0 copy-start.4
  54.2 0.7 copy-done.4
  54.9 6.3 %shard_map.67 = (f32[16,256]{1,0:T(8,128)S(1)}, f32[3,16,1]{2,1,0:T(8,128)S(1)}) custom-call(bf16[144,256]{1,0:T(8,128)(2,1)S(1)} %copy-done.1, f32[1,256]{1,0:T(1,128)S(1)} %bitcast.23, f32[16,256]{1,0:T(8,128)S(1)} %copy-done.2, bf16[16,144,256]{2,1,0:T(8,128)(2,1)S(1)} %bitcast.22), custom_call_target="tpu_custom_call" | custom-call | tf_op jit(solution)/shard_map/pallas_call | solution.py:40
  61.2 0.1 copy.7
  61.3 19.4 %all-gather.1 = f32[48,16,1]{1,2,0:T(1,128)S(1)} all-gather(f32[3,16,1]{1,2,0:T(1,128)S(1)} %copy.7), channel_id=3, replica_groups=mesh['parts'=2,'blk'=4,'grp'=2,'sub'=2] {'blk','grp','sub'}, dimensions={0}, use_global_device_ids=true | all-gather | bytes 3264 | tf_op jit(solution)/shard_map/all_gather | solution.py:50
  80.7 0.5 broadcast.13
  81.2 0.7 reduce.3
  82.0 0.0 copy-done.3
  82.0 0.7 multiply_add_fusion
  (3 shorter events, 0.1 us)
Async XLA Ops:
  7.2 74.8 %copy-start.3 = (f32[16,256]{1,0:T(8,128)S(1)}, f32[16,256]{1,0:T(8,128)}, u32[]{:S(2)}) copy-start(f32[16,256]{1,0:T(8,128)} %refs_2_.1) | copy-start | bytes 49156
  7.2 44.2 %all-gather.4.cloned.1.call-start = ((), (), s32[]{:S(2)}) async-start(), calls=%async_computation | async-start | bytes 1253376 | tf_op jit(solution)/shard_map/all_gather | solution.py:39
  51.4 1.3 %copy-start = (bf16[2304,256]{1,0:T(8,128)(2,1)S(1)}, bf16[2304,256]{1,0:T(8,128)(2,1)}, u32[]{:S(2)}) copy-start(bf16[2304,256]{1,0:T(8,128)(2,1)} %all-gather.4.cloned.1.call-done) | copy-start | bytes 3538948
  52.6 0.9 copy-start.1
  53.5 0.7 copy-start.2
  54.2 0.7 copy-start.4
Sparse Core Ops, SparseCore 0:
  10.3 41.0 all-gather.3

commit v2 on v1

v2 whole, which is shorter than its diff:
```python
import jax
import jax.numpy as jnp
from jax import lax
from jax.experimental import pallas as pl
from jax.experimental.pallas import tpu as pltpu
from jax.sharding import PartitionSpec as P

AXES = ("blk", "grp", "sub")
DIRECT = 16
VMEM = pltpu.CompilerParams(vmem_limit_bytes=40 * 1024 * 1024)
HALF = 8


def pack_kernel(features_ref, lengthscale_ref, probes_ref, packed_ref):
    feature_count, width = features_ref.shape
    scale = jnp.broadcast_to(lengthscale_ref[...], (feature_count, feature_count)).T
    scale = jnp.concatenate([scale] * (width // feature_count), axis=1)
    scaled = (features_ref[...].astype(jnp.float32) / scale).astype(jnp.bfloat16)
    packed_ref[:feature_count, :] = scaled
    rest = -0.5 * jnp.sum(jnp.square(scaled.astype(jnp.float32)), axis=0, keepdims=True)
    row = lax.broadcasted_iota(jnp.int32, (2 * HALF, width), 0)
    rows = jnp.where((row >= HALF) & (row < HALF + 3), 1.0, 0.0)
    for piece in range(3):
        part = rest.astype(jnp.bfloat16).astype(jnp.float32)
        rows = jnp.where(row == piece, part, rows)
        rest = rest - part
    packed_ref[feature_count : feature_count + 2 * HALF, :] = rows.astype(jnp.bfloat16)
    packed_ref[feature_count + 2 * HALF :, :] = probes_ref[...].astype(jnp.bfloat16)


def image_kernel(feature_count, block_count, own_too, *refs):
    packed_ref, noise_ref, probes_ref = refs[:3]
    block_refs = refs[3 : 3 + block_count]
    image_ref, sums_ref, packed, noise, probes, *rest = refs[3 + block_count :]
    slots, semaphores = rest[:-1], rest[-1]
    first = [
        pltpu.make_async_copy(source, target, semaphores.at[number])
        for number, (source, target) in enumerate(
            ((packed_ref, packed), (noise_ref, noise), (probes_ref, probes))
        )
    ]
    copies = [
        pltpu.make_async_copy(source, slot, semaphores.at[3 + number])
        for number, (source, slot) in enumerate(zip(block_refs, slots))
    ]
    for copy in first + copies:
        copy.start()
    depth = feature_count + 2 * HALF
    first[0].wait()
    norm_rows = packed[feature_count:depth, :].astype(jnp.float32)
    own = jnp.concatenate(
        [packed[:feature_count, :].astype(jnp.float32), norm_rows[HALF:], norm_rows[:HALF]], axis=0
    )
    own = own.T.astype(jnp.bfloat16)

    def add_block(block, total):
        exponent = jnp.dot(own, block[:depth, :], preferred_element_type=jnp.float32)
        weights = jnp.exp(exponent).astype(jnp.bfloat16)
        return total + lax.dot_general(
            weights,
            block[depth:, :],
            (((1,), (1,)), ((), ())),
            preferred_element_type=jnp.float32,
        )

    total = jnp.zeros((own.shape[0], probes.shape[0]), jnp.float32)
    if own_too:
        total = add_block(packed, total)
    for copy, slot in zip(copies, slots):
        copy.wait()
        if len(slot.shape) == 2:
            total = add_block(slot, total)
        else:
            total = lax.fori_loop(
                0, slot.shape[0], lambda number, value: add_block(slot.at[number], value), total
            )
    first[1].wait()
    first[2].wait()
    own_probes = probes[...]
    image = total.T + noise[...] * own_probes
    image_ref[...] = image
    lane = lax.broadcasted_iota(jnp.int32, sums_ref.shape, 1)
    sums = jnp.where(lane == 0, jnp.sum(own_probes * own_probes, axis=1, keepdims=True), 0.0)
    sums = jnp.where(lane == 1, jnp.sum(own_probes * image, axis=1, keepdims=True), sums)
    sums_ref[...] = jnp.where(lane == 2, jnp.sum(image * image, axis=1, keepdims=True), sums)


def finish_kernel(image_ref, probes_ref, *refs):
    *sums_refs, solution_ref, residual_ref, direction_ref = refs
    sums = jnp.zeros(sums_refs[0].shape[-2:], jnp.float32)
    for ref in sums_refs:
        value = ref[...]
        sums = sums + (value if value.ndim == 2 else jnp.sum(value, axis=0))
    start_norms, curvature, image_norms = sums[:, 0:1], sums[:, 1:2], sums[:, 2:3]
    alpha = start_norms / curvature
    new_norms = start_norms - 2.0 * alpha * curvature + alpha * alpha * image_norms
    probes = probes_ref[...]
    residual = probes - alpha * image_ref[...]
    solution_ref[...] = alpha * probes
    residual_ref[...] = residual
    direction_ref[...] = residual + (new_norms / start_norms) * probes


def others(value, count):
    if count > DIRECT:
        return [lax.all_gather(value, AXES, axis=0, tiled=False)], False
    return [
        lax.ppermute(value, AXES, [(i, (i + step) % count) for i in range(count)])
        for step in range(1, count)
    ], True


def make_local(count):
    def local(features, lengthscale, noise_var, probes):
        feature_count, width = features.shape
        packed = pl.pallas_call(
            pack_kernel,
            out_shape=jax.ShapeDtypeStruct(
                (feature_count + 2 * HALF + probes.shape[0], width), jnp.bfloat16
            ),
            compiler_params=VMEM,
        )(features, lengthscale[None, :], probes)
        blocks, direct = others(packed, count)
        image, sums = pl.pallas_call(
            lambda *refs: image_kernel(feature_count, len(blocks), direct, *refs),
            out_shape=(
                jax.ShapeDtypeStruct(probes.shape, jnp.float32),
                jax.ShapeDtypeStruct((probes.shape[0], 128), jnp.float32),
            ),
            in_specs=[pl.BlockSpec(memory_space=pl.ANY)] * (3 + len(blocks)),
            scratch_shapes=[
                pltpu.VMEM(packed.shape, packed.dtype),
                pltpu.VMEM((1, width), jnp.float32),
                pltpu.VMEM(probes.shape, jnp.float32),
                *[pltpu.VMEM(block.shape, block.dtype) for block in blocks],
                pltpu.SemaphoreType.DMA((3 + len(blocks),)),
            ],
            compiler_params=VMEM,
        )(packed, noise_var[None, :], probes, *blocks)
        more, direct = others(sums, count)
        outs = (jax.ShapeDtypeStruct(probes.shape, jnp.float32),) * 3
        return pl.pallas_call(finish_kernel, out_shape=outs, compiler_params=VMEM)(
            image, probes, *(([sums] if direct else []) + more)
        )

    return local


def solution(mesh):
    count = 1
    for axis in AXES:
        count *= mesh.shape[axis]
    spread = P(None, ("parts", "blk", "grp", "sub"))
    return jax.shard_map(
        make_local(count),
        mesh=mesh,
        in_specs=(spread, P("parts"), P(("parts", "blk", "grp", "sub")), spread),
        out_specs=(spread, spread, spread),
        check_vma=False,
    )
```

time: 89.9 us -> 72 us (0.80)
  starting transfers between devices: 0.04 us -> 40.3 us
  waiting for transfers between devices: 41.8 us -> 21.9 us
  blocking collectives: 19.4 us -> 0 us
  between operations: 14.1 us -> 0.73 us
  other arithmetic: 3.74 us -> 0 us
  local copies, waits for them, and re-layouts: 4.17 us -> 2.21 us
    all_gather x1 -> x0, waiting for transfers between devices: 41.8 us -> none  [local(): gathered = lax.all_gather(packed, AXES, axis=0, tiled=False)]
    ppermute x0 -> x30, starting transfers between devices: none -> 40.3 us  [others(): lax.ppermute(value, AXES, [(i, (i + step) % count) for i in range(count)])]
    ppermute x0 -> x30, waiting for transfers between devices: none -> 21.9 us  [others(): lax.ppermute(value, AXES, [(i, (i + step) % count) for i in range(count)])]
    all_gather x1 -> x0, blocking collectives: 19.4 us -> none  [local(): lax.all_gather(sums.reshape(3, -1), AXES, axis=0, tiled=False)]
    convert_element_type x2 -> x0, other arithmetic: 1.67 us -> none  [the longest x1 0.93 us: local(): (features.astype(jnp.float32) / lengthscale[:, None]).astype(jnp.bfloat16)]
    unnamed x10, local copies, waits for them, and re-layouts: 3.56 us -> 2.21 us
    pallas_call x1 -> x3, Pallas kernels: 6.26 us -> 6.64 us  [the longest x1 5.73 us: local(): pl.pallas_call(lambda *refs: image_kernel(feature_count, len(blocks), dir...]
  transfers between devices with their start and end apart: 1 -> 30, of which waited for: 1 -> 11; matrix products, arithmetic and copies ran while one was open for 0% -> 0% of each run, Pallas kernels for 0% -> 0%
where the time goes in v2:
time: 72 us; the launch traced here: 71.8 us
  starting transfers between devices  40.3 us (56%)
  waiting for transfers between devices  21.9 us (30%)
  Pallas kernels  6.64 us (9%)
  local copies, waits for them, and re-layouts  2.21 us (3%)
  between operations  0.73 us (1%)
    ppermute x30, starting transfers between devices, others(): lax.ppermute(value, AXES, [(i, (i + step) % count) for i in range(count)])  40.3 us
    ppermute x30, waiting for transfers between devices, others(): lax.ppermute(value, AXES, [(i, (i + step) % count) for i in range(count)])  21.9 us
    pallas_call x1, Pallas kernels, local(): pl.pallas_call(lambda *refs: image_kernel(feature_count, len(blocks), dir...  5.73 us
    unnamed x10, local copies, waits for them, and re-layouts  2.21 us
  transfers between devices with their start and end apart: 30, of which 11 were waited for; matrix products, arithmetic and copies ran while one was open for 0% of the time, Pallas kernels for 0%

profile of v2, /device:TPU:0, one launch (start us, length us, event | category | flops | bytes accessed | tf_op | source)
XLA Modules:
  0.0 71.8 jit_solution(717186741323753394)
XLA Ops:
  0.6 0.6 copy-done.4
  1.3 0.7 copy-done
  2.0 0.8 %copy-done.2 = bf16[128,256]{1,0:T(8,128)(2,1)S(1)} copy-done((bf16[128,256]{1,0:T(8,128)(2,1)S(1)}, bf16[128,256]{1,0:T(8,128)(2,1)}, u32[]{:S(2)}) %copy-start.2) | copy-done | bytes 65560
  2.8 0.1 shard_map.67.refs_0_
  3.0 0.0 copy-start.3
  3.0 5.5 %collective-permute-start.14 = (bf16[160,256]{1,0:T(8,128)(2,1)S(1)}, bf16[160,256]{1,0:T(8,128)(2,1)S(1)}, u32[]{:S(2)}, u32[]{:S(2)}) collective-permute-start(bf16[160,256]{1,0:T(8,128)(2,1)S(1)} %shard_map.67.refs_0_), channel_id=1, source_target_pairs={{0,15},{1,0},{2,1},{3,2},{4,3},{5,4},{6,5},{7,6},{8,7},{9,8},{10,9... | collective-permute-start | bytes 245768 | tf_op jit(solution)/shard_map/ppermute | solution.py:108
  8.4 0.6 collective-permute-start.13
  9.1 0.2 collective-permute-start.12
  9.3 0.4 collective-permute-start.11
  9.7 0.1 collective-permute-start.10
  9.9 1.3 %collective-permute-done.14.refs_17_ = bf16[160,256]{1,0:T(8,128)(2,1)S(1)} collective-permute-done((bf16[160,256]{1,0:T(8,128)(2,1)S(1)}, bf16[160,256]{1,0:T(8,128)(2,1)S(1)}, u32[]{:S(2)}, u32[]{:S(2)}) %collective-permute-start.14) | collective-permute-done | bytes 81952 | tf_op jit(solution)/shard_map/ppermute | solution.py:108
  11.2 3.0 %collective-permute-start.9 = (bf16[160,256]{1,0:T(8,128)(2,1)S(1)}, bf16[160,256]{1,0:T(8,128)(2,1)S(1)}, u32[]{:S(2)}, u32[]{:S(2)}) collective-permute-start(bf16[160,256]{1,0:T(8,128)(2,1)S(1)} %shard_map.67.refs_0_), channel_id=1, source_target_pairs={{0,10},{1,11},{2,12},{3,13},{4,14},{5,15},{6,0},{7,1},{8,2},{9,3},... | collective-permute-start | bytes 245768 | tf_op jit(solution)/shard_map/ppermute | solution.py:108
  14.2 0.5 collective-permute-done.12.refs_15_
  14.7 1.0 %collective-permute-start.7 = (bf16[160,256]{1,0:T(8,128)(2,1)S(1)}, bf16[160,256]{1,0:T(8,128)(2,1)S(1)}, u32[]{:S(2)}, u32[]{:S(2)}) collective-permute-start(bf16[160,256]{1,0:T(8,128)(2,1)S(1)} %shard_map.67.refs_0_), channel_id=1, source_target_pairs={{0,8},{1,9},{2,10},{3,11},{4,12},{5,13},{6,14},{7,15},{8,0},{9,1},... | collective-permute-start | bytes 245768 | tf_op jit(solution)/shard_map/ppermute | solution.py:108
  15.8 0.7 collective-permute-done.11.refs_14_
  16.5 0.4 collective-permute-start.6
  16.9 1.3 %collective-permute-done.10.refs_13_ = bf16[160,256]{1,0:T(8,128)(2,1)S(1)} collective-permute-done((bf16[160,256]{1,0:T(8,128)(2,1)S(1)}, bf16[160,256]{1,0:T(8,128)(2,1)S(1)}, u32[]{:S(2)}, u32[]{:S(2)}) %collective-permute-start.10) | collective-permute-done | bytes 81952 | tf_op jit(solution)/shard_map/ppermute | solution.py:108
  18.2 3.8 %collective-permute-start.5 = (bf16[160,256]{1,0:T(8,128)(2,1)S(1)}, bf16[160,256]{1,0:T(8,128)(2,1)S(1)}, u32[]{:S(2)}, u32[]{:S(2)}) collective-permute-start(bf16[160,256]{1,0:T(8,128)(2,1)S(1)} %shard_map.67.refs_0_), channel_id=1, source_target_pairs={{0,6},{1,7},{2,8},{3,9},{4,10},{5,11},{6,12},{7,13},{8,14},{9,15},... | collective-permute-start | bytes 245768 | tf_op jit(solution)/shard_map/ppermute | solution.py:108
  22.1 4.5 %collective-permute-start.4 = (bf16[160,256]{1,0:T(8,128)(2,1)S(1)}, bf16[160,256]{1,0:T(8,128)(2,1)S(1)}, u32[]{:S(2)}, u32[]{:S(2)}) collective-permute-start(bf16[160,256]{1,0:T(8,128)(2,1)S(1)} %shard_map.67.refs_0_), channel_id=1, source_target_pairs={{0,5},{1,6},{2,7},{3,8},{4,9},{5,10},{6,11},{7,12},{8,13},{9,14},{... | collective-permute-start | bytes 245768 | tf_op jit(solution)/shard_map/ppermute | solution.py:108
  26.6 4.1 %collective-permute-start.3 = (bf16[160,256]{1,0:T(8,128)(2,1)S(1)}, bf16[160,256]{1,0:T(8,128)(2,1)S(1)}, u32[]{:S(2)}, u32[]{:S(2)}) collective-permute-start(bf16[160,256]{1,0:T(8,128)(2,1)S(1)} %shard_map.67.refs_0_), channel_id=1, source_target_pairs={{0,4},{1,5},{2,6},{3,7},{4,8},{5,9},{6,10},{7,11},{8,12},{9,13},{1... | collective-permute-start | bytes 245768 | tf_op jit(solution)/shard_map/ppermute | solution.py:108
  30.7 3.2 %collective-permute-done.7.refs_10_ = bf16[160,256]{1,0:T(8,128)(2,1)S(1)} collective-permute-done((bf16[160,256]{1,0:T(8,128)(2,1)S(1)}, bf16[160,256]{1,0:T(8,128)(2,1)S(1)}, u32[]{:S(2)}, u32[]{:S(2)}) %collective-permute-start.7) | collective-permute-done | bytes 81952 | tf_op jit(solution)/shard_map/ppermute | solution.py:108
  33.8 0.0 collective-permute-start.2
  33.8 1.1 %collective-permute-done.6.refs_9_ = bf16[160,256]{1,0:T(8,128)(2,1)S(1)} collective-permute-done((bf16[160,256]{1,0:T(8,128)(2,1)S(1)}, bf16[160,256]{1,0:T(8,128)(2,1)S(1)}, u32[]{:S(2)}, u32[]{:S(2)}) %collective-permute-start.6) | collective-permute-done | bytes 81952 | tf_op jit(solution)/shard_map/ppermute | solution.py:108
  34.9 0.0 collective-permute-start.1
  34.9 0.0 collective-permute-done.5.refs_8_
  34.9 0.0 collective-permute-start
  35.0 0.0 collective-permute-done.3.refs_6_
  35.0 4.5 %collective-permute-done.2.refs_5_ = bf16[160,256]{1,0:T(8,128)(2,1)S(1)} collective-permute-done((bf16[160,256]{1,0:T(8,128)(2,1)S(1)}, bf16[160,256]{1,0:T(8,128)(2,1)S(1)}, u32[]{:S(2)}, u32[]{:S(2)}) %collective-permute-start.2) | collective-permute-done | bytes 81952 | tf_op jit(solution)/shard_map/ppermute | solution.py:108
  39.5 3.3 %collective-permute-done.1.refs_4_ = bf16[160,256]{1,0:T(8,128)(2,1)S(1)} collective-permute-done((bf16[160,256]{1,0:T(8,128)(2,1)S(1)}, bf16[160,256]{1,0:T(8,128)(2,1)S(1)}, u32[]{:S(2)}, u32[]{:S(2)}) %collective-permute-start.1) | collective-permute-done | bytes 81952 | tf_op jit(solution)/shard_map/ppermute | solution.py:108
  42.8 5.7 %shard_map.68 = (f32[16,256]{1,0:T(8,128)S(1)}, f32[16,128]{1,0:T(8,128)S(1)}) custom-call(bf16[160,256]{1,0:T(8,128)(2,1)S(1)} %shard_map.67.refs_0_, f32[1,256]{1,0:T(1,128)S(1)} %bitcast.2, f32[16,256]{1,0:T(8,128)S(1)} %copy-done, bf16[160,256]{1,0:T(8,128)(2,1)S(1)} %collective-permute-done.refs_3_, ...), custom_call_target="tpu_custom_call" | custom-call | tf_op jit(solution)/shard_map/pallas_call | solution.py:124
  48.5 0.1 collective-permute-start.29
  48.6 0.8 %collective-permute-start.28 = (f32[16,128]{1,0:T(8,128)S(1)}, f32[16,128]{1,0:T(8,128)S(1)}, u32[]{:S(2)}, u32[]{:S(2)}) collective-permute-start(f32[16,128]{1,0:T(8,128)S(1)} %get-tuple-element.6.refs_0_), channel_id=1, source_target_pairs={{0,14},{1,15},{2,0},{3,1},{4,2},{5,3},{6,4},{7,5},{8,6},{9,7},{10,... | collective-permute-start | bytes 24584 | tf_op jit(solution)/shard_map/ppermute | solution.py:108
  49.5 0.1 collective-permute-start.27
  49.5 0.3 collective-permute-start.26
  49.8 3.0 %collective-permute-start.25 = (f32[16,128]{1,0:T(8,128)S(1)}, f32[16,128]{1,0:T(8,128)S(1)}, u32[]{:S(2)}, u32[]{:S(2)}) collective-permute-start(f32[16,128]{1,0:T(8,128)S(1)} %get-tuple-element.6.refs_0_), channel_id=1, source_target_pairs={{0,11},{1,12},{2,13},{3,14},{4,15},{5,0},{6,1},{7,2},{8,3},{9,4},{... | collective-permute-start | bytes 24584 | tf_op jit(solution)/shard_map/ppermute | solution.py:108
  52.8 1.9 %collective-permute-start.24 = (f32[16,128]{1,0:T(8,128)S(1)}, f32[16,128]{1,0:T(8,128)S(1)}, u32[]{:S(2)}, u32[]{:S(2)}) collective-permute-start(f32[16,128]{1,0:T(8,128)S(1)} %get-tuple-element.6.refs_0_), channel_id=1, source_target_pairs={{0,10},{1,11},{2,12},{3,13},{4,14},{5,15},{6,0},{7,1},{8,2},{9,3},... | collective-permute-start | bytes 24584 | tf_op jit(solution)/shard_map/ppermute | solution.py:108
  54.8 0.0 collective-permute-done.28.refs_14_
  54.8 1.8 %collective-permute-start.22 = (f32[16,128]{1,0:T(8,128)S(1)}, f32[16,128]{1,0:T(8,128)S(1)}, u32[]{:S(2)}, u32[]{:S(2)}) collective-permute-start(f32[16,128]{1,0:T(8,128)S(1)} %get-tuple-element.6.refs_0_), channel_id=1, source_target_pairs={{0,8},{1,9},{2,10},{3,11},{4,12},{5,13},{6,14},{7,15},{8,0},{9,1},... | collective-permute-start | bytes 24584 | tf_op jit(solution)/shard_map/ppermute | solution.py:108
  56.6 0.9 %collective-permute-start.21 = (f32[16,128]{1,0:T(8,128)S(1)}, f32[16,128]{1,0:T(8,128)S(1)}, u32[]{:S(2)}, u32[]{:S(2)}) collective-permute-start(f32[16,128]{1,0:T(8,128)S(1)} %get-tuple-element.6.refs_0_), channel_id=1, source_target_pairs={{0,7},{1,8},{2,9},{3,10},{4,11},{5,12},{6,13},{7,14},{8,15},{9,0},... | collective-permute-start | bytes 24584 | tf_op jit(solution)/shard_map/ppermute | solution.py:108
  57.5 2.3 %collective-permute-start.20 = (f32[16,128]{1,0:T(8,128)S(1)}, f32[16,128]{1,0:T(8,128)S(1)}, u32[]{:S(2)}, u32[]{:S(2)}) collective-permute-start(f32[16,128]{1,0:T(8,128)S(1)} %get-tuple-element.6.refs_0_), channel_id=1, source_target_pairs={{0,6},{1,7},{2,8},{3,9},{4,10},{5,11},{6,12},{7,13},{8,14},{9,15},... | collective-permute-start | bytes 24584 | tf_op jit(solution)/shard_map/ppermute | solution.py:108
  59.8 0.6 collective-permute-start.19
  60.4 2.1 %collective-permute-start.18 = (f32[16,128]{1,0:T(8,128)S(1)}, f32[16,128]{1,0:T(8,128)S(1)}, u32[]{:S(2)}, u32[]{:S(2)}) collective-permute-start(f32[16,128]{1,0:T(8,128)S(1)} %get-tuple-element.6.refs_0_), channel_id=1, source_target_pairs={{0,4},{1,5},{2,6},{3,7},{4,8},{5,9},{6,10},{7,11},{8,12},{9,13},{1... | collective-permute-start | bytes 24584 | tf_op jit(solution)/shard_map/ppermute | solution.py:108
  62.5 2.1 %collective-permute-start.17 = (f32[16,128]{1,0:T(8,128)S(1)}, f32[16,128]{1,0:T(8,128)S(1)}, u32[]{:S(2)}, u32[]{:S(2)}) collective-permute-start(f32[16,128]{1,0:T(8,128)S(1)} %get-tuple-element.6.refs_0_), channel_id=1, source_target_pairs={{0,3},{1,4},{2,5},{3,6},{4,7},{5,8},{6,9},{7,10},{8,11},{9,12},{10... | collective-permute-start | bytes 24584 | tf_op jit(solution)/shard_map/ppermute | solution.py:108
  64.6 0.5 collective-permute-start.16
  65.1 0.8 %collective-permute-done.18.refs_4_ = f32[16,128]{1,0:T(8,128)S(1)} collective-permute-done((f32[16,128]{1,0:T(8,128)S(1)}, f32[16,128]{1,0:T(8,128)S(1)}, u32[]{:S(2)}, u32[]{:S(2)}) %collective-permute-start.18) | collective-permute-done | bytes 8224 | tf_op jit(solution)/shard_map/ppermute | solution.py:108
  65.9 1.9 %collective-permute-done.17.refs_3_ = f32[16,128]{1,0:T(8,128)S(1)} collective-permute-done((f32[16,128]{1,0:T(8,128)S(1)}, f32[16,128]{1,0:T(8,128)S(1)}, u32[]{:S(2)}, u32[]{:S(2)}) %collective-permute-start.17) | collective-permute-done | bytes 8224 | tf_op jit(solution)/shard_map/ppermute | solution.py:108
  67.8 3.2 %collective-permute-done.16.refs_2_ = f32[16,128]{1,0:T(8,128)S(1)} collective-permute-done((f32[16,128]{1,0:T(8,128)S(1)}, f32[16,128]{1,0:T(8,128)S(1)}, u32[]{:S(2)}, u32[]{:S(2)}) %collective-permute-start.16) | collective-permute-done | bytes 8224 | tf_op jit(solution)/shard_map/ppermute | solution.py:108
  71.0 0.8 %shard_map.69 = (f32[16,256]{1,0:T(8,128)}, f32[16,256]{1,0:T(8,128)}, f32[16,256]{1,0:T(8,128)}) custom-call(f32[16,256]{1,0:T(8,128)S(1)} %get-tuple-element.5.image_ref, f32[16,256]{1,0:T(8,128)S(1)} %copy-done.1, f32[16,128]{1,0:T(8,128)S(1)} %get-tuple-element.6.refs_0_, f32[16,128]{1,0:T(8,128)S(1)} %collective-permute-done.15.refs_1_, ...), custom_call_target="tpu_custom_call" | custom-call | tf_op jit(solution)/shard_map/pallas_call | solution.py:142
  (25 shorter events, 0.1 us)
Async XLA Ops:
  0.6 0.7 copy-start.4
  1.3 0.7 copy-start
  2.0 0.8 %copy-start.2 = (bf16[128,256]{1,0:T(8,128)(2,1)S(1)}, bf16[128,256]{1,0:T(8,128)(2,1)}, u32[]{:S(2)}) copy-start(bf16[128,256]{1,0:T(8,128)(2,1)} %features_ref.1) | copy-start | bytes 196612
  3.0 39.8 %copy-start.3 = (f32[256]{0:T(256)S(1)}, f32[256]{0:T(256)}, u32[]{:S(2)}) copy-start(f32[256]{0:T(256)} %param.6) | copy-start | bytes 3076
  3.0 8.2 %collective-permute-start.14 = (bf16[160,256]{1,0:T(8,128)(2,1)S(1)}, bf16[160,256]{1,0:T(8,128)(2,1)S(1)}, u32[]{:S(2)}, u32[]{:S(2)}) collective-permute-start(bf16[160,256]{1,0:T(8,128)(2,1)S(1)} %shard_map.67.refs_0_), channel_id=1, source_target_pairs={{0,15},{1,0},{2,1},{3,2},{4,3},{5,4},{6,5},{7,6},{8,7},{9,8},{10,9... | collective-permute-start | bytes 245768 | tf_op jit(solution)/shard_map/ppermute | solution.py:108
  8.4 5.7 %collective-permute-start.13 = (bf16[160,256]{1,0:T(8,128)(2,1)S(1)}, bf16[160,256]{1,0:T(8,128)(2,1)S(1)}, u32[]{:S(2)}, u32[]{:S(2)}) collective-permute-start(bf16[160,256]{1,0:T(8,128)(2,1)S(1)} %shard_map.67.refs_0_), channel_id=1, source_target_pairs={{0,14},{1,15},{2,0},{3,1},{4,2},{5,3},{6,4},{7,5},{8,6},{9,7},{10,... | collective-permute-start | bytes 245768 | tf_op jit(solution)/shard_map/ppermute | solution.py:108
  9.1 5.7 %collective-permute-start.12 = (bf16[160,256]{1,0:T(8,128)(2,1)S(1)}, bf16[160,256]{1,0:T(8,128)(2,1)S(1)}, u32[]{:S(2)}, u32[]{:S(2)}) collective-permute-start(bf16[160,256]{1,0:T(8,128)(2,1)S(1)} %shard_map.67.refs_0_), channel_id=1, source_target_pairs={{0,13},{1,14},{2,15},{3,0},{4,1},{5,2},{6,3},{7,4},{8,5},{9,6},{10... | collective-permute-start | bytes 245768 | tf_op jit(solution)/shard_map/ppermute | solution.py:108
  9.3 7.2 %collective-permute-start.11 = (bf16[160,256]{1,0:T(8,128)(2,1)S(1)}, bf16[160,256]{1,0:T(8,128)(2,1)S(1)}, u32[]{:S(2)}, u32[]{:S(2)}) collective-permute-start(bf16[160,256]{1,0:T(8,128)(2,1)S(1)} %shard_map.67.refs_0_), channel_id=1, source_target_pairs={{0,12},{1,13},{2,14},{3,15},{4,0},{5,1},{6,2},{7,3},{8,4},{9,5},{1... | collective-permute-start | bytes 245768 | tf_op jit(solution)/shard_map/ppermute | solution.py:108
  9.7 8.5 %collective-permute-start.10 = (bf16[160,256]{1,0:T(8,128)(2,1)S(1)}, bf16[160,256]{1,0:T(8,128)(2,1)S(1)}, u32[]{:S(2)}, u32[]{:S(2)}) collective-permute-start(bf16[160,256]{1,0:T(8,128)(2,1)S(1)} %shard_map.67.refs_0_), channel_id=1, source_target_pairs={{0,11},{1,12},{2,13},{3,14},{4,15},{5,0},{6,1},{7,2},{8,3},{9,4},{... | collective-permute-start | bytes 245768 | tf_op jit(solution)/shard_map/ppermute | solution.py:108
  11.2 10.9 %collective-permute-start.9 = (bf16[160,256]{1,0:T(8,128)(2,1)S(1)}, bf16[160,256]{1,0:T(8,128)(2,1)S(1)}, u32[]{:S(2)}, u32[]{:S(2)}) collective-permute-start(bf16[160,256]{1,0:T(8,128)(2,1)S(1)} %shard_map.67.refs_0_), channel_id=1, source_target_pairs={{0,10},{1,11},{2,12},{3,13},{4,14},{5,15},{6,0},{7,1},{8,2},{9,3},... | collective-permute-start | bytes 245768 | tf_op jit(solution)/shard_map/ppermute | solution.py:108
  14.2 12.4 %collective-permute-start.8 = (bf16[160,256]{1,0:T(8,128)(2,1)S(1)}, bf16[160,256]{1,0:T(8,128)(2,1)S(1)}, u32[]{:S(2)}, u32[]{:S(2)}) collective-permute-start(bf16[160,256]{1,0:T(8,128)(2,1)S(1)} %shard_map.67.refs_0_), channel_id=1, source_target_pairs={{0,9},{1,10},{2,11},{3,12},{4,13},{5,14},{6,15},{7,0},{8,1},{9,2},... | collective-permute-start | bytes 245768 | tf_op jit(solution)/shard_map/ppermute | solution.py:108
  14.7 19.1 %collective-permute-start.7 = (bf16[160,256]{1,0:T(8,128)(2,1)S(1)}, bf16[160,256]{1,0:T(8,128)(2,1)S(1)}, u32[]{:S(2)}, u32[]{:S(2)}) collective-permute-start(bf16[160,256]{1,0:T(8,128)(2,1)S(1)} %shard_map.67.refs_0_), channel_id=1, source_target_pairs={{0,8},{1,9},{2,10},{3,11},{4,12},{5,13},{6,14},{7,15},{8,0},{9,1},... | collective-permute-start | bytes 245768 | tf_op jit(solution)/shard_map/ppermute | solution.py:108
  16.5 18.4 %collective-permute-start.6 = (bf16[160,256]{1,0:T(8,128)(2,1)S(1)}, bf16[160,256]{1,0:T(8,128)(2,1)S(1)}, u32[]{:S(2)}, u32[]{:S(2)}) collective-permute-start(bf16[160,256]{1,0:T(8,128)(2,1)S(1)} %shard_map.67.refs_0_), channel_id=1, source_target_pairs={{0,7},{1,8},{2,9},{3,10},{4,11},{5,12},{6,13},{7,14},{8,15},{9,0},... | collective-permute-start | bytes 245768 | tf_op jit(solution)/shard_map/ppermute | solution.py:108
  18.2 16.7 %collective-permute-start.5 = (bf16[160,256]{1,0:T(8,128)(2,1)S(1)}, bf16[160,256]{1,0:T(8,128)(2,1)S(1)}, u32[]{:S(2)}, u32[]{:S(2)}) collective-permute-start(bf16[160,256]{1,0:T(8,128)(2,1)S(1)} %shard_map.67.refs_0_), channel_id=1, source_target_pairs={{0,6},{1,7},{2,8},{3,9},{4,10},{5,11},{6,12},{7,13},{8,14},{9,15},... | collective-permute-start | bytes 245768 | tf_op jit(solution)/shard_map/ppermute | solution.py:108
  22.1 12.9 %collective-permute-start.4 = (bf16[160,256]{1,0:T(8,128)(2,1)S(1)}, bf16[160,256]{1,0:T(8,128)(2,1)S(1)}, u32[]{:S(2)}, u32[]{:S(2)}) collective-permute-start(bf16[160,256]{1,0:T(8,128)(2,1)S(1)} %shard_map.67.refs_0_), channel_id=1, source_target_pairs={{0,5},{1,6},{2,7},{3,8},{4,9},{5,10},{6,11},{7,12},{8,13},{9,14},{... | collective-permute-start | bytes 245768 | tf_op jit(solution)/shard_map/ppermute | solution.py:108
  26.6 8.4 %collective-permute-start.3 = (bf16[160,256]{1,0:T(8,128)(2,1)S(1)}, bf16[160,256]{1,0:T(8,128)(2,1)S(1)}, u32[]{:S(2)}, u32[]{:S(2)}) collective-permute-start(bf16[160,256]{1,0:T(8,128)(2,1)S(1)} %shard_map.67.refs_0_), channel_id=1, source_target_pairs={{0,4},{1,5},{2,6},{3,7},{4,8},{5,9},{6,10},{7,11},{8,12},{9,13},{1... | collective-permute-start | bytes 245768 | tf_op jit(solution)/shard_map/ppermute | solution.py:108
  33.8 5.7 %collective-permute-start.2 = (bf16[160,256]{1,0:T(8,128)(2,1)S(1)}, bf16[160,256]{1,0:T(8,128)(2,1)S(1)}, u32[]{:S(2)}, u32[]{:S(2)}) collective-permute-start(bf16[160,256]{1,0:T(8,128)(2,1)S(1)} %shard_map.67.refs_0_), channel_id=1, source_target_pairs={{0,3},{1,4},{2,5},{3,6},{4,7},{5,8},{6,9},{7,10},{8,11},{9,12},{10... | collective-permute-start | bytes 245768 | tf_op jit(solution)/shard_map/ppermute | solution.py:108
  34.9 7.9 %collective-permute-start.1 = (bf16[160,256]{1,0:T(8,128)(2,1)S(1)}, bf16[160,256]{1,0:T(8,128)(2,1)S(1)}, u32[]{:S(2)}, u32[]{:S(2)}) collective-permute-start(bf16[160,256]{1,0:T(8,128)(2,1)S(1)} %shard_map.67.refs_0_), channel_id=1, source_target_pairs={{0,2},{1,3},{2,4},{3,5},{4,6},{5,7},{6,8},{7,9},{8,10},{9,11},{10,... | collective-permute-start | bytes 245768 | tf_op jit(solution)/shard_map/ppermute | solution.py:108
  34.9 7.9 %collective-permute-start = (bf16[160,256]{1,0:T(8,128)(2,1)S(1)}, bf16[160,256]{1,0:T(8,128)(2,1)S(1)}, u32[]{:S(2)}, u32[]{:S(2)}) collective-permute-start(bf16[160,256]{1,0:T(8,128)(2,1)S(1)} %shard_map.67.refs_0_), channel_id=1, source_target_pairs={{0,1},{1,2},{2,3},{3,4},{4,5},{5,6},{6,7},{7,8},{8,9},{9,10},{10,1... | collective-permute-start | bytes 245768 | tf_op jit(solution)/shard_map/ppermute | solution.py:108
  42.8 28.2 %copy-start.1 = (f32[16,256]{1,0:T(8,128)S(1)}, f32[16,256]{1,0:T(8,128)}, u32[]{:S(2)}) copy-start(f32[16,256]{1,0:T(8,128)} %probes_ref.3) | copy-start | bytes 49156
  48.5 4.3 %collective-permute-start.29 = (f32[16,128]{1,0:T(8,128)S(1)}, f32[16,128]{1,0:T(8,128)S(1)}, u32[]{:S(2)}, u32[]{:S(2)}) collective-permute-start(f32[16,128]{1,0:T(8,128)S(1)} %get-tuple-element.6.refs_0_), channel_id=1, source_target_pairs={{0,15},{1,0},{2,1},{3,2},{4,3},{5,4},{6,5},{7,6},{8,7},{9,8},{10,9... | collective-permute-start | bytes 24584 | tf_op jit(solution)/shard_map/ppermute | solution.py:108
  48.6 6.1 %collective-permute-start.28 = (f32[16,128]{1,0:T(8,128)S(1)}, f32[16,128]{1,0:T(8,128)S(1)}, u32[]{:S(2)}, u32[]{:S(2)}) collective-permute-start(f32[16,128]{1,0:T(8,128)S(1)} %get-tuple-element.6.refs_0_), channel_id=1, source_target_pairs={{0,14},{1,15},{2,0},{3,1},{4,2},{5,3},{6,4},{7,5},{8,6},{9,7},{10,... | collective-permute-start | bytes 24584 | tf_op jit(solution)/shard_map/ppermute | solution.py:108
  49.5 5.3 %collective-permute-start.27 = (f32[16,128]{1,0:T(8,128)S(1)}, f32[16,128]{1,0:T(8,128)S(1)}, u32[]{:S(2)}, u32[]{:S(2)}) collective-permute-start(f32[16,128]{1,0:T(8,128)S(1)} %get-tuple-element.6.refs_0_), channel_id=1, source_target_pairs={{0,13},{1,14},{2,15},{3,0},{4,1},{5,2},{6,3},{7,4},{8,5},{9,6},{10... | collective-permute-start | bytes 24584 | tf_op jit(solution)/shard_map/ppermute | solution.py:108
  49.5 7.0 %collective-permute-start.26 = (f32[16,128]{1,0:T(8,128)S(1)}, f32[16,128]{1,0:T(8,128)S(1)}, u32[]{:S(2)}, u32[]{:S(2)}) collective-permute-start(f32[16,128]{1,0:T(8,128)S(1)} %get-tuple-element.6.refs_0_), channel_id=1, source_target_pairs={{0,12},{1,13},{2,14},{3,15},{4,0},{5,1},{6,2},{7,3},{8,4},{9,5},{1... | collective-permute-start | bytes 24584 | tf_op jit(solution)/shard_map/ppermute | solution.py:108
  49.8 7.7 %collective-permute-start.25 = (f32[16,128]{1,0:T(8,128)S(1)}, f32[16,128]{1,0:T(8,128)S(1)}, u32[]{:S(2)}, u32[]{:S(2)}) collective-permute-start(f32[16,128]{1,0:T(8,128)S(1)} %get-tuple-element.6.refs_0_), channel_id=1, source_target_pairs={{0,11},{1,12},{2,13},{3,14},{4,15},{5,0},{6,1},{7,2},{8,3},{9,4},{... | collective-permute-start | bytes 24584 | tf_op jit(solution)/shard_map/ppermute | solution.py:108
  52.8 6.9 %collective-permute-start.24 = (f32[16,128]{1,0:T(8,128)S(1)}, f32[16,128]{1,0:T(8,128)S(1)}, u32[]{:S(2)}, u32[]{:S(2)}) collective-permute-start(f32[16,128]{1,0:T(8,128)S(1)} %get-tuple-element.6.refs_0_), channel_id=1, source_target_pairs={{0,10},{1,11},{2,12},{3,13},{4,14},{5,15},{6,0},{7,1},{8,2},{9,3},... | collective-permute-start | bytes 24584 | tf_op jit(solution)/shard_map/ppermute | solution.py:108
  54.8 5.6 %collective-permute-start.23 = (f32[16,128]{1,0:T(8,128)S(1)}, f32[16,128]{1,0:T(8,128)S(1)}, u32[]{:S(2)}, u32[]{:S(2)}) collective-permute-start(f32[16,128]{1,0:T(8,128)S(1)} %get-tuple-element.6.refs_0_), channel_id=1, source_target_pairs={{0,9},{1,10},{2,11},{3,12},{4,13},{5,14},{6,15},{7,0},{8,1},{9,2},... | collective-permute-start | bytes 24584 | tf_op jit(solution)/shard_map/ppermute | solution.py:108
  54.8 7.7 %collective-permute-start.22 = (f32[16,128]{1,0:T(8,128)S(1)}, f32[16,128]{1,0:T(8,128)S(1)}, u32[]{:S(2)}, u32[]{:S(2)}) collective-permute-start(f32[16,128]{1,0:T(8,128)S(1)} %get-tuple-element.6.refs_0_), channel_id=1, source_target_pairs={{0,8},{1,9},{2,10},{3,11},{4,12},{5,13},{6,14},{7,15},{8,0},{9,1},... | collective-permute-start | bytes 24584 | tf_op jit(solution)/shard_map/ppermute | solution.py:108
  56.6 8.0 %collective-permute-start.21 = (f32[16,128]{1,0:T(8,128)S(1)}, f32[16,128]{1,0:T(8,128)S(1)}, u32[]{:S(2)}, u32[]{:S(2)}) collective-permute-start(f32[16,128]{1,0:T(8,128)S(1)} %get-tuple-element.6.refs_0_), channel_id=1, source_target_pairs={{0,7},{1,8},{2,9},{3,10},{4,11},{5,12},{6,13},{7,14},{8,15},{9,0},... | collective-permute-start | bytes 24584 | tf_op jit(solution)/shard_map/ppermute | solution.py:108
  57.5 7.6 %collective-permute-start.20 = (f32[16,128]{1,0:T(8,128)S(1)}, f32[16,128]{1,0:T(8,128)S(1)}, u32[]{:S(2)}, u32[]{:S(2)}) collective-permute-start(f32[16,128]{1,0:T(8,128)S(1)} %get-tuple-element.6.refs_0_), channel_id=1, source_target_pairs={{0,6},{1,7},{2,8},{3,9},{4,10},{5,11},{6,12},{7,13},{8,14},{9,15},... | collective-permute-start | bytes 24584 | tf_op jit(solution)/shard_map/ppermute | solution.py:108
  59.8 5.3 %collective-permute-start.19 = (f32[16,128]{1,0:T(8,128)S(1)}, f32[16,128]{1,0:T(8,128)S(1)}, u32[]{:S(2)}, u32[]{:S(2)}) collective-permute-start(f32[16,128]{1,0:T(8,128)S(1)} %get-tuple-element.6.refs_0_), channel_id=1, source_target_pairs={{0,5},{1,6},{2,7},{3,8},{4,9},{5,10},{6,11},{7,12},{8,13},{9,14},{... | collective-permute-start | bytes 24584 | tf_op jit(solution)/shard_map/ppermute | solution.py:108
  60.4 5.5 %collective-permute-start.18 = (f32[16,128]{1,0:T(8,128)S(1)}, f32[16,128]{1,0:T(8,128)S(1)}, u32[]{:S(2)}, u32[]{:S(2)}) collective-permute-start(f32[16,128]{1,0:T(8,128)S(1)} %get-tuple-element.6.refs_0_), channel_id=1, source_target_pairs={{0,4},{1,5},{2,6},{3,7},{4,8},{5,9},{6,10},{7,11},{8,12},{9,13},{1... | collective-permute-start | bytes 24584 | tf_op jit(solution)/shard_map/ppermute | solution.py:108
  62.5 5.3 %collective-permute-start.17 = (f32[16,128]{1,0:T(8,128)S(1)}, f32[16,128]{1,0:T(8,128)S(1)}, u32[]{:S(2)}, u32[]{:S(2)}) collective-permute-start(f32[16,128]{1,0:T(8,128)S(1)} %get-tuple-element.6.refs_0_), channel_id=1, source_target_pairs={{0,3},{1,4},{2,5},{3,6},{4,7},{5,8},{6,9},{7,10},{8,11},{9,12},{10... | collective-permute-start | bytes 24584 | tf_op jit(solution)/shard_map/ppermute | solution.py:108
  64.6 6.4 %collective-permute-start.16 = (f32[16,128]{1,0:T(8,128)S(1)}, f32[16,128]{1,0:T(8,128)S(1)}, u32[]{:S(2)}, u32[]{:S(2)}) collective-permute-start(f32[16,128]{1,0:T(8,128)S(1)} %get-tuple-element.6.refs_0_), channel_id=1, source_target_pairs={{0,2},{1,3},{2,4},{3,5},{4,6},{5,7},{6,8},{7,9},{8,10},{9,11},{10,... | collective-permute-start | bytes 24584 | tf_op jit(solution)/shard_map/ppermute | solution.py:108
  65.1 5.9 %collective-permute-start.15 = (f32[16,128]{1,0:T(8,128)S(1)}, f32[16,128]{1,0:T(8,128)S(1)}, u32[]{:S(2)}, u32[]{:S(2)}) collective-permute-start(f32[16,128]{1,0:T(8,128)S(1)} %get-tuple-element.6.refs_0_), channel_id=1, source_target_pairs={{0,1},{1,2},{2,3},{3,4},{4,5},{5,6},{6,7},{7,8},{8,9},{9,10},{10,1... | collective-permute-start | bytes 24584 | tf_op jit(solution)/shard_map/ppermute | solution.py:108

commit v3 on v1

v3 whole, which is shorter than its diff:
```python
import jax
import jax.numpy as jnp
from jax import lax
from jax.experimental import pallas as pl
from jax.experimental.pallas import tpu as pltpu
from jax.sharding import PartitionSpec as P

PLANE = ("grp", "sub")
LINE = ("blk",)
DIRECT = 8
VMEM = pltpu.CompilerParams(vmem_limit_bytes=40 * 1024 * 1024)
HALF = 8


def pieces_of(value):
    pieces = []
    for _ in range(3):
        piece = value.astype(jnp.bfloat16).astype(jnp.float32)
        pieces.append(piece)
        value = value - piece
    return pieces


def pack_kernel(features_hbm, lengthscale_hbm, probes_hbm, line_ref, plane_ref, *scratch):
    features_ref, lengthscale_ref, probes_ref, semaphores = scratch
    copies = [
        pltpu.make_async_copy(source, target, semaphores.at[number])
        for number, (source, target) in enumerate(
            (
                (features_hbm, features_ref),
                (lengthscale_hbm, lengthscale_ref),
                (probes_hbm, probes_ref),
            )
        )
    ]
    for copy in copies:
        copy.start()
    for copy in copies:
        copy.wait()
    feature_count, width = features_ref.shape
    scale = jnp.broadcast_to(lengthscale_ref[...], (feature_count, feature_count)).T
    scale = jnp.concatenate([scale] * (width // feature_count), axis=1)
    scaled = (features_ref[...].astype(jnp.float32) / scale).astype(jnp.bfloat16)
    norms = -0.5 * jnp.sum(jnp.square(scaled.astype(jnp.float32)), axis=0, keepdims=True)
    row = lax.broadcasted_iota(jnp.int32, (2 * HALF, width), 0)
    rows = jnp.where((row >= HALF) & (row < HALF + 3), 1.0, 0.0)
    for number, piece in enumerate(pieces_of(norms)):
        rows = jnp.where(row == number, piece, rows)
    probes = jnp.concatenate(pieces_of(probes_ref[...]), axis=0)
    packed = jnp.concatenate([scaled, rows.astype(jnp.bfloat16), probes.astype(jnp.bfloat16)], axis=0)
    plane_ref[...] = packed
    line_ref[...] = packed[: line_ref.shape[0], :]


def image_kernel(depth, plane_count, *refs):
    plane_refs = refs[:plane_count]
    line_refs = refs[plane_count:-2]
    noise_ref, partial_ref = refs[-2:]
    rows = [ref[:depth, :] for ref in plane_refs]
    probe_count = partial_ref.shape[1]

    def add_block(block_ref, totals):
        block = block_ref[:depth, :].astype(jnp.float32)
        first, last = depth - 2 * HALF, depth - HALF
        columns = jnp.concatenate([block[:first], block[last:], block[first:last]], axis=0)
        columns = columns.T.astype(jnp.bfloat16)
        probes = block_ref[depth : depth + probe_count, :]
        result = []
        for own, total in zip(rows, totals):
            exponent = jnp.dot(columns, own, preferred_element_type=jnp.float32)
            weights = jnp.exp(exponent).astype(jnp.bfloat16)
            result.append(total + jnp.dot(probes, weights, preferred_element_type=jnp.float32))
        return result

    own_probes = probes_of(plane_refs[0], depth, probe_count)
    totals = [noise_ref[...] * own_probes]
    totals += [jnp.zeros(own_probes.shape, jnp.float32)] * (plane_count - 1)
    for ref in line_refs:
        if len(ref.shape) == 2:
            totals = add_block(ref, totals)
        else:
            totals = lax.fori_loop(
                0, ref.shape[0], lambda number, value: add_block(ref.at[number], value), totals
            )
    for number, total in enumerate(totals):
        partial_ref[number] = total


def probes_of(ref, depth, probe_count):
    parts = [
        ref[depth + number * probe_count : depth + (number + 1) * probe_count, :].astype(jnp.float32)
        for number in range(3)
    ]
    return parts[0] + (parts[1] + parts[2])


def combine_kernel(depth, plane_count, *refs):
    plane_refs = refs[:plane_count]
    partial_refs = refs[plane_count:-2]
    image_ref, sums_ref = refs[-2:]
    probe_count = image_ref.shape[0]
    lane = lax.broadcasted_iota(jnp.int32, sums_ref.shape, 1)
    products = [0.0, 0.0, 0.0]
    for number, plane_ref in enumerate(plane_refs):
        probes = probes_of(plane_ref, depth, probe_count)
        image = sum(
            ref[place_of(step, number, plane_count)] for step, ref in enumerate(partial_refs)
        )
        if number == 0:
            image_ref[...] = image
        products[0] += probes * probes
        products[1] += probes * image
        products[2] += image * image
    sums = jnp.zeros(sums_ref.shape, jnp.float32)
    for number, product in enumerate(products):
        sums = jnp.where(lane == number, jnp.sum(product, axis=1, keepdims=True), sums)
    sums_ref[...] = sums


def finish_kernel(image_ref, probes_ref, *refs):
    *sums_refs, solution_ref, residual_ref, direction_ref = refs
    sums = jnp.zeros(sums_refs[0].shape[-2:], jnp.float32)
    for ref in sums_refs:
        value = ref[...]
        sums = sums + (value if value.ndim == 2 else jnp.sum(value, axis=0))
    start_norms, curvature, image_norms = sums[:, 0:1], sums[:, 1:2], sums[:, 2:3]
    alpha = start_norms / curvature
    new_norms = start_norms - 2.0 * alpha * curvature + alpha * alpha * image_norms
    probes = probes_ref[...]
    residual = probes - alpha * image_ref[...]
    solution_ref[...] = alpha * probes
    residual_ref[...] = residual
    direction_ref[...] = residual + (new_norms / start_norms) * probes


def paired(count):
    return count & (count - 1) == 0


def source_of(device, step, count):
    return device ^ step if paired(count) else (device - step) % count


def place_of(step, number, count):
    return step ^ number if paired(count) else (number - step) % count


def everywhere(value, axes, count):
    if count > DIRECT:
        return [lax.all_gather(value, axes, axis=0, tiled=False)]
    return [value] + [
        lax.ppermute(value, axes, [(source_of(i, step, count), i) for i in range(count)])
        for step in range(1, count)
    ]


def make_local(plane_count, line_count):
    def local(features, lengthscale, noise_var, probes):
        feature_count, width = features.shape
        probe_count = probes.shape[0]
        depth = feature_count + 2 * HALF
        line, plane = pl.pallas_call(
            pack_kernel,
            out_shape=(
                jax.ShapeDtypeStruct((depth + probe_count, width), jnp.bfloat16),
                jax.ShapeDtypeStruct((depth + 3 * probe_count, width), jnp.bfloat16),
            ),
            in_specs=[pl.BlockSpec(memory_space=pl.ANY)] * 3,
            scratch_shapes=[
                pltpu.VMEM(features.shape, features.dtype),
                pltpu.VMEM((1, feature_count), jnp.float32),
                pltpu.VMEM(probes.shape, jnp.float32),
                pltpu.SemaphoreType.DMA((3,)),
            ],
            compiler_params=VMEM,
        )(features, lengthscale[None, :], probes)
        lines = everywhere(line, LINE, line_count)
        planes = everywhere(plane, PLANE, plane_count)
        partial = pl.pallas_call(
            lambda *refs: image_kernel(depth, plane_count, *refs),
            out_shape=jax.ShapeDtypeStruct((plane_count, probe_count, width), jnp.float32),
            compiler_params=VMEM,
        )(*planes, *lines, noise_var[None, :])
        image, sums = pl.pallas_call(
            lambda *refs: combine_kernel(depth, plane_count, *refs),
            out_shape=(
                jax.ShapeDtypeStruct(probes.shape, jnp.float32),
                jax.ShapeDtypeStruct((probe_count, 128), jnp.float32),
            ),
            compiler_params=VMEM,
        )(*planes, *everywhere(partial, PLANE, plane_count))
        outs = (jax.ShapeDtypeStruct(probes.shape, jnp.float32),) * 3
        return pl.pallas_call(finish_kernel, out_shape=outs, compiler_params=VMEM)(
            image, probes, *everywhere(sums, LINE, line_count)
        )

    return local


def solution(mesh):
    plane_count = mesh.shape["grp"] * mesh.shape["sub"]
    spread = P(None, ("parts", "blk", "grp", "sub"))
    return jax.shard_map(
        make_local(plane_count, mesh.shape["blk"]),
        mesh=mesh,
        in_specs=(spread, P("parts"), P(("parts", "blk", "grp", "sub")), spread),
        out_specs=(spread, spread, spread),
        check_vma=False,
    )
```

time: 89.9 us -> 33.3 us (0.37)
  waiting for transfers between devices: 41.8 us -> 11.6 us
  blocking collectives: 19.4 us -> 0 us
  starting transfers between devices: 0.04 us -> 14.6 us
  between operations: 14.1 us -> 0.67 us
  other arithmetic: 3.74 us -> 0 us
  Pallas kernels: 6.26 us -> 4.04 us
  local copies, waits for them, and re-layouts: 4.17 us -> 2.21 us
    all_gather x1 -> x0, waiting for transfers between devices: 41.8 us -> none  [local(): gathered = lax.all_gather(packed, AXES, axis=0, tiled=False)]
    all_gather x1 -> x0, blocking collectives: 19.4 us -> none  [local(): lax.all_gather(sums.reshape(3, -1), AXES, axis=0, tiled=False)]
    ppermute x0 -> x12, starting transfers between devices: none -> 14.6 us  [everywhere(): lax.ppermute(value, axes, [(source_of(i, step, count), i) for i in range(...]
    ppermute x0 -> x12, waiting for transfers between devices: none -> 11.6 us  [everywhere(): lax.ppermute(value, axes, [(source_of(i, step, count), i) for i in range(...]
    pallas_call x1 -> x4, Pallas kernels: 6.26 us -> 4.04 us  [the longest x1 2.93 us: local(): pl.pallas_call(lambda *refs: image_kernel(depth, plane_count, *refs), out...]
    convert_element_type x2 -> x0, other arithmetic: 1.67 us -> none  [the longest x1 0.93 us: local(): (features.astype(jnp.float32) / lengthscale[:, None]).astype(jnp.bfloat16)]
    unnamed x10, local copies, waits for them, and re-layouts: 3.56 us -> 2.21 us
  transfers between devices with their start and end apart: 1 -> 12, of which waited for: 1 -> 7; matrix products, arithmetic and copies ran while one was open for 0% -> 0% of each run, Pallas kernels for 0% -> 0%
where the time goes in v3:
time: 33.3 us; the launch traced here: 33.1 us
  starting transfers between devices  14.6 us (44%)
  waiting for transfers between devices  11.6 us (35%)
  Pallas kernels  4.04 us (12%)
  local copies, waits for them, and re-layouts  2.21 us (7%)
  between operations  0.67 us (2%)
    ppermute x12, starting transfers between devices, everywhere(): lax.ppermute(value, axes, [(source_of(i, step, count), i) for i in range(...  14.6 us
    ppermute x12, waiting for transfers between devices, everywhere(): lax.ppermute(value, axes, [(source_of(i, step, count), i) for i in range(...  11.6 us
    pallas_call x1, Pallas kernels, local(): pl.pallas_call(lambda *refs: image_kernel(depth, plane_count, *refs), out...  2.93 us
    unnamed x10, local copies, waits for them, and re-layouts  2.21 us
    pallas_call x1, Pallas kernels, local(): pl.pallas_call(finish_kernel, out_shape=outs, compiler_params=VMEM)  0.77 us
  transfers between devices with their start and end apart: 12, of which 7 were waited for; matrix products, arithmetic and copies ran while one was open for 0% of the time, Pallas kernels for 0%

profile of v3, /device:TPU:0, one launch (start us, length us, event | category | flops | bytes accessed | tf_op | source)
XLA Modules:
  0.0 33.1 jit_solution(5652042500519213299)
XLA Ops:
  0.6 0.0 copy-start.4
  0.6 0.6 %copy-done.4 = f32[128]{0:T(128)S(1)} copy-done((f32[128]{0:T(128)S(1)}, f32[128]{0:T(128)}, u32[]{:S(2)}) %copy-start.4) | copy-done | bytes 536
  1.3 0.0 copy-start
  1.3 0.8 %copy-done = bf16[128,256]{1,0:T(8,128)(2,1)S(1)} copy-done((bf16[128,256]{1,0:T(8,128)(2,1)S(1)}, bf16[128,256]{1,0:T(8,128)(2,1)}, u32[]{:S(2)}) %copy-start) | copy-done | bytes 65560
  2.1 0.0 copy-start.1
  2.1 0.7 %copy-done.1 = f32[16,256]{1,0:T(8,128)S(1)} copy-done((f32[16,256]{1,0:T(8,128)S(1)}, f32[16,256]{1,0:T(8,128)}, u32[]{:S(2)}) %copy-start.1) | copy-done | bytes 16408
  2.8 0.2 shard_map.67
  3.1 5.1 %collective-permute-start.5 = (bf16[160,256]{1,0:T(8,128)(2,1)S(1)}, bf16[160,256]{1,0:T(8,128)(2,1)S(1)}, u32[]{:S(2)}, u32[]{:S(2)}) collective-permute-start(bf16[160,256]{1,0:T(8,128)(2,1)S(1)} %get-tuple-element.8.refs_4_), channel_id=1, source_target_pairs={{12,0},{8,4},{4,8},{0,12},{13,1},{9,5},{5,9},{1,13},{14,2},{10,6},... | collective-permute-start | bytes 245768 | tf_op jit(solution)/shard_map/ppermute | solution.py:152
  8.2 0.0 copy-start.3
  8.2 0.7 %collective-permute-start.2 = (bf16[192,256]{1,0:T(8,128)(2,1)S(1)}, bf16[192,256]{1,0:T(8,128)(2,1)S(1)}, u32[]{:S(2)}, u32[]{:S(2)}) collective-permute-start(bf16[192,256]{1,0:T(8,128)(2,1)S(1)} %get-tuple-element.7.refs_0_), channel_id=1, source_target_pairs={{3,0},{2,1},{1,2},{0,3},{7,4},{6,5},{5,6},{4,7},{11,8},{10,9},{9,1... | collective-permute-start | bytes 294920 | tf_op jit(solution)/shard_map/ppermute | solution.py:152
  8.9 0.9 %collective-permute-start.1 = (bf16[192,256]{1,0:T(8,128)(2,1)S(1)}, bf16[192,256]{1,0:T(8,128)(2,1)S(1)}, u32[]{:S(2)}, u32[]{:S(2)}) collective-permute-start(bf16[192,256]{1,0:T(8,128)(2,1)S(1)} %get-tuple-element.7.refs_0_), channel_id=1, source_target_pairs={{2,0},{3,1},{0,2},{1,3},{6,4},{7,5},{4,6},{5,7},{10,8},{11,9},{8,1... | collective-permute-start | bytes 294920 | tf_op jit(solution)/shard_map/ppermute | solution.py:152
  9.7 0.3 %collective-permute-start = (bf16[192,256]{1,0:T(8,128)(2,1)S(1)}, bf16[192,256]{1,0:T(8,128)(2,1)S(1)}, u32[]{:S(2)}, u32[]{:S(2)}) collective-permute-start(bf16[192,256]{1,0:T(8,128)(2,1)S(1)} %get-tuple-element.7.refs_0_), channel_id=1, source_target_pairs={{1,0},{0,1},{3,2},{2,3},{5,4},{4,5},{7,6},{6,7},{9,8},{8,9},{11,10... | collective-permute-start | bytes 294920 | tf_op jit(solution)/shard_map/ppermute | solution.py:152
  10.1 0.0 collective-permute-start.4
  10.1 0.7 %collective-permute-done.5.refs_7_ = bf16[160,256]{1,0:T(8,128)(2,1)S(1)} collective-permute-done((bf16[160,256]{1,0:T(8,128)(2,1)S(1)}, bf16[160,256]{1,0:T(8,128)(2,1)S(1)}, u32[]{:S(2)}, u32[]{:S(2)}) %collective-permute-start.5) | collective-permute-done | bytes 81952 | tf_op jit(solution)/shard_map/ppermute | solution.py:152
  10.7 1.4 %collective-permute-start.3 = (bf16[160,256]{1,0:T(8,128)(2,1)S(1)}, bf16[160,256]{1,0:T(8,128)(2,1)S(1)}, u32[]{:S(2)}, u32[]{:S(2)}) collective-permute-start(bf16[160,256]{1,0:T(8,128)(2,1)S(1)} %get-tuple-element.8.refs_4_), channel_id=1, source_target_pairs={{4,0},{0,4},{12,8},{8,12},{5,1},{1,5},{13,9},{9,13},{6,2},{2,6},{1... | collective-permute-start | bytes 245768 | tf_op jit(solution)/shard_map/ppermute | solution.py:152
  12.1 4.2 %collective-permute-done.4.refs_6_ = bf16[160,256]{1,0:T(8,128)(2,1)S(1)} collective-permute-done((bf16[160,256]{1,0:T(8,128)(2,1)S(1)}, bf16[160,256]{1,0:T(8,128)(2,1)S(1)}, u32[]{:S(2)}, u32[]{:S(2)}) %collective-permute-start.4) | collective-permute-done | bytes 81952 | tf_op jit(solution)/shard_map/ppermute | solution.py:152
  16.3 0.6 %collective-permute-done.3.refs_5_ = bf16[160,256]{1,0:T(8,128)(2,1)S(1)} collective-permute-done((bf16[160,256]{1,0:T(8,128)(2,1)S(1)}, bf16[160,256]{1,0:T(8,128)(2,1)S(1)}, u32[]{:S(2)}, u32[]{:S(2)}) %collective-permute-start.3) | collective-permute-done | bytes 81952 | tf_op jit(solution)/shard_map/ppermute | solution.py:152
  16.9 0.0 collective-permute-done.2.refs_3_
  16.9 0.0 collective-permute-done.1.refs_2_
  16.9 0.0 collective-permute-done.refs_1_
  16.9 0.0 copy-done.3
  16.9 2.9 %shard_map.68.refs_4_ = f32[4,16,256]{2,1,0:T(8,128)S(1)} custom-call(bf16[192,256]{1,0:T(8,128)(2,1)S(1)} %get-tuple-element.7.refs_0_, bf16[192,256]{1,0:T(8,128)(2,1)S(1)} %collective-permute-done.refs_1_, bf16[192,256]{1,0:T(8,128)(2,1)S(1)} %collective-permute-done.1.refs_2_, bf16[192,256]{1,0:T(8,128)(2,1)S(1)} %collective-permute-done.2.refs_3_, ...), custom_call_target="tpu_custom_call" | custom-call | tf_op jit(solution)/shard_map/pallas_call | solution.py:179
  19.8 0.0 copy-start.2
  19.8 0.4 %collective-permute-start.8 = (f32[4,16,256]{2,1,0:T(8,128)S(1)}, f32[4,16,256]{2,1,0:T(8,128)S(1)}, u32[]{:S(2)}, u32[]{:S(2)}) collective-permute-start(f32[4,16,256]{2,1,0:T(8,128)S(1)} %shard_map.68.refs_4_), channel_id=1, source_target_pairs={{3,0},{2,1},{1,2},{0,3},{7,4},{6,5},{5,6},{4,7},{11,8},{10,9},{9,1... | collective-permute-start | bytes 196616 | tf_op jit(solution)/shard_map/ppermute | solution.py:152
  20.2 1.3 %collective-permute-start.7 = (f32[4,16,256]{2,1,0:T(8,128)S(1)}, f32[4,16,256]{2,1,0:T(8,128)S(1)}, u32[]{:S(2)}, u32[]{:S(2)}) collective-permute-start(f32[4,16,256]{2,1,0:T(8,128)S(1)} %shard_map.68.refs_4_), channel_id=1, source_target_pairs={{2,0},{3,1},{0,2},{1,3},{6,4},{7,5},{4,6},{5,7},{10,8},{11,9},{8,1... | collective-permute-start | bytes 196616 | tf_op jit(solution)/shard_map/ppermute | solution.py:152
  21.5 0.2 collective-permute-start.6
  21.7 2.4 %collective-permute-done.8.refs_7_ = f32[4,16,256]{2,1,0:T(8,128)S(1)} collective-permute-done((f32[4,16,256]{2,1,0:T(8,128)S(1)}, f32[4,16,256]{2,1,0:T(8,128)S(1)}, u32[]{:S(2)}, u32[]{:S(2)}) %collective-permute-start.8) | collective-permute-done | bytes 65568 | tf_op jit(solution)/shard_map/ppermute | solution.py:152
  24.1 1.6 %collective-permute-done.7.refs_6_ = f32[4,16,256]{2,1,0:T(8,128)S(1)} collective-permute-done((f32[4,16,256]{2,1,0:T(8,128)S(1)}, f32[4,16,256]{2,1,0:T(8,128)S(1)}, u32[]{:S(2)}, u32[]{:S(2)}) %collective-permute-start.7) | collective-permute-done | bytes 65568 | tf_op jit(solution)/shard_map/ppermute | solution.py:152
  25.6 0.0 collective-permute-done.6.refs_5_
  25.6 0.1 shard_map.69
  25.8 2.0 %collective-permute-start.11 = (f32[16,128]{1,0:T(8,128)S(1)}, f32[16,128]{1,0:T(8,128)S(1)}, u32[]{:S(2)}, u32[]{:S(2)}) collective-permute-start(f32[16,128]{1,0:T(8,128)S(1)} %get-tuple-element.10.refs_0_), channel_id=1, source_target_pairs={{12,0},{8,4},{4,8},{0,12},{13,1},{9,5},{5,9},{1,13},{14,2},{10,6},... | collective-permute-start | bytes 24584 | tf_op jit(solution)/shard_map/ppermute | solution.py:152
  27.8 0.0 collective-permute-start.10
  27.8 2.4 %collective-permute-start.9 = (f32[16,128]{1,0:T(8,128)S(1)}, f32[16,128]{1,0:T(8,128)S(1)}, u32[]{:S(2)}, u32[]{:S(2)}) collective-permute-start(f32[16,128]{1,0:T(8,128)S(1)} %get-tuple-element.10.refs_0_), channel_id=1, source_target_pairs={{4,0},{0,4},{12,8},{8,12},{5,1},{1,5},{13,9},{9,13},{6,2},{2,6},{1... | collective-permute-start | bytes 24584 | tf_op jit(solution)/shard_map/ppermute | solution.py:152
  30.2 1.1 %collective-permute-done.11.refs_3_ = f32[16,128]{1,0:T(8,128)S(1)} collective-permute-done((f32[16,128]{1,0:T(8,128)S(1)}, f32[16,128]{1,0:T(8,128)S(1)}, u32[]{:S(2)}, u32[]{:S(2)}) %collective-permute-start.11) | collective-permute-done | bytes 8224 | tf_op jit(solution)/shard_map/ppermute | solution.py:152
  31.2 1.1 %collective-permute-done.10.refs_2_ = f32[16,128]{1,0:T(8,128)S(1)} collective-permute-done((f32[16,128]{1,0:T(8,128)S(1)}, f32[16,128]{1,0:T(8,128)S(1)}, u32[]{:S(2)}, u32[]{:S(2)}) %collective-permute-start.10) | collective-permute-done | bytes 8224 | tf_op jit(solution)/shard_map/ppermute | solution.py:152
  32.3 0.0 collective-permute-done.9.refs_1_
  32.3 0.0 copy-done.2
  32.3 0.8 %shard_map.70 = (f32[16,256]{1,0:T(8,128)}, f32[16,256]{1,0:T(8,128)}, f32[16,256]{1,0:T(8,128)}) custom-call(f32[16,256]{1,0:T(8,128)S(1)} %get-tuple-element.9.image_ref, f32[16,256]{1,0:T(8,128)S(1)} %copy-done.2, f32[16,128]{1,0:T(8,128)S(1)} %get-tuple-element.10.refs_0_, f32[16,128]{1,0:T(8,128)S(1)} %collective-permute-done.9.refs_1_, ...), custom_call_target="tpu_custom_call" | custom-call | tf_op jit(solution)/shard_map/pallas_call | solution.py:193
Async XLA Ops:
  0.6 0.7 %copy-start.4 = (f32[128]{0:T(128)S(1)}, f32[128]{0:T(128)}, u32[]{:S(2)}) copy-start(f32[128]{0:T(128)} %param.5) | copy-start | bytes 1540
  1.3 0.8 %copy-start = (bf16[128,256]{1,0:T(8,128)(2,1)S(1)}, bf16[128,256]{1,0:T(8,128)(2,1)}, u32[]{:S(2)}) copy-start(bf16[128,256]{1,0:T(8,128)(2,1)} %features_hbm.1) | copy-start | bytes 196612
  2.1 0.7 %copy-start.1 = (f32[16,256]{1,0:T(8,128)S(1)}, f32[16,256]{1,0:T(8,128)}, u32[]{:S(2)}) copy-start(f32[16,256]{1,0:T(8,128)} %probes_ref.1) | copy-start | bytes 49156
  3.1 7.7 %collective-permute-start.5 = (bf16[160,256]{1,0:T(8,128)(2,1)S(1)}, bf16[160,256]{1,0:T(8,128)(2,1)S(1)}, u32[]{:S(2)}, u32[]{:S(2)}) collective-permute-start(bf16[160,256]{1,0:T(8,128)(2,1)S(1)} %get-tuple-element.8.refs_4_), channel_id=1, source_target_pairs={{12,0},{8,4},{4,8},{0,12},{13,1},{9,5},{5,9},{1,13},{14,2},{10,6},... | collective-permute-start | bytes 245768 | tf_op jit(solution)/shard_map/ppermute | solution.py:152
  8.2 8.7 %copy-start.3 = (f32[256]{0:T(256)S(1)}, f32[256]{0:T(256)}, u32[]{:S(2)}) copy-start(f32[256]{0:T(256)} %param.6) | copy-start | bytes 3076
  8.2 8.7 %collective-permute-start.2 = (bf16[192,256]{1,0:T(8,128)(2,1)S(1)}, bf16[192,256]{1,0:T(8,128)(2,1)S(1)}, u32[]{:S(2)}, u32[]{:S(2)}) collective-permute-start(bf16[192,256]{1,0:T(8,128)(2,1)S(1)} %get-tuple-element.7.refs_0_), channel_id=1, source_target_pairs={{3,0},{2,1},{1,2},{0,3},{7,4},{6,5},{5,6},{4,7},{11,8},{10,9},{9,1... | collective-permute-start | bytes 294920 | tf_op jit(solution)/shard_map/ppermute | solution.py:152
  8.9 8.0 %collective-permute-start.1 = (bf16[192,256]{1,0:T(8,128)(2,1)S(1)}, bf16[192,256]{1,0:T(8,128)(2,1)S(1)}, u32[]{:S(2)}, u32[]{:S(2)}) collective-permute-start(bf16[192,256]{1,0:T(8,128)(2,1)S(1)} %get-tuple-element.7.refs_0_), channel_id=1, source_target_pairs={{2,0},{3,1},{0,2},{1,3},{6,4},{7,5},{4,6},{5,7},{10,8},{11,9},{8,1... | collective-permute-start | bytes 294920 | tf_op jit(solution)/shard_map/ppermute | solution.py:152
  9.7 7.2 %collective-permute-start = (bf16[192,256]{1,0:T(8,128)(2,1)S(1)}, bf16[192,256]{1,0:T(8,128)(2,1)S(1)}, u32[]{:S(2)}, u32[]{:S(2)}) collective-permute-start(bf16[192,256]{1,0:T(8,128)(2,1)S(1)} %get-tuple-element.7.refs_0_), channel_id=1, source_target_pairs={{1,0},{0,1},{3,2},{2,3},{5,4},{4,5},{7,6},{6,7},{9,8},{8,9},{11,10... | collective-permute-start | bytes 294920 | tf_op jit(solution)/shard_map/ppermute | solution.py:152
  10.1 6.3 %collective-permute-start.4 = (bf16[160,256]{1,0:T(8,128)(2,1)S(1)}, bf16[160,256]{1,0:T(8,128)(2,1)S(1)}, u32[]{:S(2)}, u32[]{:S(2)}) collective-permute-start(bf16[160,256]{1,0:T(8,128)(2,1)S(1)} %get-tuple-element.8.refs_4_), channel_id=1, source_target_pairs={{8,0},{12,4},{0,8},{4,12},{9,1},{13,5},{1,9},{5,13},{10,2},{14,6},... | collective-permute-start | bytes 245768 | tf_op jit(solution)/shard_map/ppermute | solution.py:152
  10.7 6.1 %collective-permute-start.3 = (bf16[160,256]{1,0:T(8,128)(2,1)S(1)}, bf16[160,256]{1,0:T(8,128)(2,1)S(1)}, u32[]{:S(2)}, u32[]{:S(2)}) collective-permute-start(bf16[160,256]{1,0:T(8,128)(2,1)S(1)} %get-tuple-element.8.refs_4_), channel_id=1, source_target_pairs={{4,0},{0,4},{12,8},{8,12},{5,1},{1,5},{13,9},{9,13},{6,2},{2,6},{1... | collective-permute-start | bytes 245768 | tf_op jit(solution)/shard_map/ppermute | solution.py:152
  19.8 12.5 %copy-start.2 = (f32[16,256]{1,0:T(8,128)S(1)}, f32[16,256]{1,0:T(8,128)}, u32[]{:S(2)}) copy-start(f32[16,256]{1,0:T(8,128)} %probes_ref.1) | copy-start | bytes 49156
  19.8 4.2 %collective-permute-start.8 = (f32[4,16,256]{2,1,0:T(8,128)S(1)}, f32[4,16,256]{2,1,0:T(8,128)S(1)}, u32[]{:S(2)}, u32[]{:S(2)}) collective-permute-start(f32[4,16,256]{2,1,0:T(8,128)S(1)} %shard_map.68.refs_4_), channel_id=1, source_target_pairs={{3,0},{2,1},{1,2},{0,3},{7,4},{6,5},{5,6},{4,7},{11,8},{10,9},{9,1... | collective-permute-start | bytes 196616 | tf_op jit(solution)/shard_map/ppermute | solution.py:152
  20.2 5.4 %collective-permute-start.7 = (f32[4,16,256]{2,1,0:T(8,128)S(1)}, f32[4,16,256]{2,1,0:T(8,128)S(1)}, u32[]{:S(2)}, u32[]{:S(2)}) collective-permute-start(f32[4,16,256]{2,1,0:T(8,128)S(1)} %shard_map.68.refs_4_), channel_id=1, source_target_pairs={{2,0},{3,1},{0,2},{1,3},{6,4},{7,5},{4,6},{5,7},{10,8},{11,9},{8,1... | collective-permute-start | bytes 196616 | tf_op jit(solution)/shard_map/ppermute | solution.py:152
  21.5 4.1 %collective-permute-start.6 = (f32[4,16,256]{2,1,0:T(8,128)S(1)}, f32[4,16,256]{2,1,0:T(8,128)S(1)}, u32[]{:S(2)}, u32[]{:S(2)}) collective-permute-start(f32[4,16,256]{2,1,0:T(8,128)S(1)} %shard_map.68.refs_4_), channel_id=1, source_target_pairs={{1,0},{0,1},{3,2},{2,3},{5,4},{4,5},{7,6},{6,7},{9,8},{8,9},{11,10... | collective-permute-start | bytes 196616 | tf_op jit(solution)/shard_map/ppermute | solution.py:152
  25.8 5.5 %collective-permute-start.11 = (f32[16,128]{1,0:T(8,128)S(1)}, f32[16,128]{1,0:T(8,128)S(1)}, u32[]{:S(2)}, u32[]{:S(2)}) collective-permute-start(f32[16,128]{1,0:T(8,128)S(1)} %get-tuple-element.10.refs_0_), channel_id=1, source_target_pairs={{12,0},{8,4},{4,8},{0,12},{13,1},{9,5},{5,9},{1,13},{14,2},{10,6},... | collective-permute-start | bytes 24584 | tf_op jit(solution)/shard_map/ppermute | solution.py:152
  27.8 4.5 %collective-permute-start.10 = (f32[16,128]{1,0:T(8,128)S(1)}, f32[16,128]{1,0:T(8,128)S(1)}, u32[]{:S(2)}, u32[]{:S(2)}) collective-permute-start(f32[16,128]{1,0:T(8,128)S(1)} %get-tuple-element.10.refs_0_), channel_id=1, source_target_pairs={{8,0},{12,4},{0,8},{4,12},{9,1},{13,5},{1,9},{5,13},{10,2},{14,6},... | collective-permute-start | bytes 24584 | tf_op jit(solution)/shard_map/ppermute | solution.py:152
  27.8 4.5 %collective-permute-start.9 = (f32[16,128]{1,0:T(8,128)S(1)}, f32[16,128]{1,0:T(8,128)S(1)}, u32[]{:S(2)}, u32[]{:S(2)}) collective-permute-start(f32[16,128]{1,0:T(8,128)S(1)} %get-tuple-element.10.refs_0_), channel_id=1, source_target_pairs={{4,0},{0,4},{12,8},{8,12},{5,1},{1,5},{13,9},{9,13},{6,2},{2,6},{1... | collective-permute-start | bytes 24584 | tf_op jit(solution)/shard_map/ppermute | solution.py:152

commit v4 on v3

--- a/solution.py
+++ b/solution.py
@@ -165,7 +165,7 @@
                 jax.ShapeDtypeStruct((depth + probe_count, width), jnp.bfloat16),
                 jax.ShapeDtypeStruct((depth + 3 * probe_count, width), jnp.bfloat16),
             ),
-            in_specs=[pl.BlockSpec(memory_space=pl.ANY)] * 3,
+            in_specs=[pl.BlockSpec(memory_space=pltpu.HBM)] * 3,
             scratch_shapes=[
                 pltpu.VMEM(features.shape, features.dtype),
                 pltpu.VMEM((1, feature_count), jnp.float32),
@@ -191,7 +191,11 @@
         )(*planes, *everywhere(partial, PLANE, plane_count))
         outs = (jax.ShapeDtypeStruct(probes.shape, jnp.float32),) * 3
         return pl.pallas_call(finish_kernel, out_shape=outs, compiler_params=VMEM)(
-            image, probes, *everywhere(sums, LINE, line_count)
+            image,
+            probes,
+            lax.all_to_all(
+                jnp.broadcast_to(sums, (line_count, *sums.shape)), LINE, split_axis=0, concat_axis=0
+            ),
         )
 
     return local

time: 33.3 us -> 35.7 us (1.072)
  blocking collectives: 0 us -> 8.85 us
  starting transfers between devices: 14.6 us -> 10.2 us
  waiting for transfers between devices: 11.6 us -> 9.4 us
    all_to_all x0 -> x1, blocking collectives: none -> 8.85 us  [local(): lax.all_to_all(jnp.broadcast_to(sums, (line_count, *sums.shape)), LINE, s...]
    ppermute x12 -> x9, starting transfers between devices: 14.6 us -> 10.2 us  [everywhere(): lax.ppermute(value, axes, [(source_of(i, step, count), i) for i in range(...]
    ppermute x12 -> x9, waiting for transfers between devices: 11.6 us -> 9.4 us  [everywhere(): lax.ppermute(value, axes, [(source_of(i, step, count), i) for i in range(...]
  transfers between devices with their start and end apart: 12 -> 9, of which waited for: 7 -> 5; matrix products, arithmetic and copies ran while one was open for 0% -> 0% of each run, Pallas kernels for 0% -> 0%
where the time goes in v4:
time: 35.7 us; the launch traced here: 35.4 us
  starting transfers between devices  10.2 us (29%)
  waiting for transfers between devices  9.4 us (26%)
  blocking collectives  8.85 us (25%)
  Pallas kernels  4.04 us (11%)
  local copies, waits for them, and re-layouts  2.22 us (6%)
  between operations  0.68 us (2%)
    ppermute x9, starting transfers between devices, everywhere(): lax.ppermute(value, axes, [(source_of(i, step, count), i) for i in range(...  10.2 us
    ppermute x9, waiting for transfers between devices, everywhere(): lax.ppermute(value, axes, [(source_of(i, step, count), i) for i in range(...  9.4 us
    all_to_all x1, blocking collectives, local(): lax.all_to_all(jnp.broadcast_to(sums, (line_count, *sums.shape)), LINE, s...  8.85 us
    pallas_call x1, Pallas kernels, local(): pl.pallas_call(lambda *refs: image_kernel(depth, plane_count, *refs), out...  2.93 us
    unnamed x10, local copies, waits for them, and re-layouts  2.21 us
    pallas_call x1, Pallas kernels, local(): pl.pallas_call(finish_kernel, out_shape=outs, compiler_params=VMEM)  0.77 us
  transfers between devices with their start and end apart: 9, of which 5 were waited for; matrix products, arithmetic and copies ran while one was open for 0% of the time, Pallas kernels for 0%

profile of v4, /device:TPU:0, one launch (start us, length us, event | category | flops | bytes accessed | tf_op | source)
XLA Modules:
  0.0 35.4 jit_solution(7476452118512815415)
XLA Ops:
  0.6 0.0 copy-start.4
  0.6 0.6 %copy-done.4 = f32[128]{0:T(128)S(1)} copy-done((f32[128]{0:T(128)S(1)}, f32[128]{0:T(128)}, u32[]{:S(2)}) %copy-start.4) | copy-done | bytes 536
  1.3 0.0 copy-start
  1.3 0.8 %copy-done = bf16[128,256]{1,0:T(8,128)(2,1)S(1)} copy-done((bf16[128,256]{1,0:T(8,128)(2,1)S(1)}, bf16[128,256]{1,0:T(8,128)(2,1)}, u32[]{:S(2)}) %copy-start) | copy-done | bytes 65560
  2.1 0.0 copy-start.1
  2.1 0.7 %copy-done.1 = f32[16,256]{1,0:T(8,128)S(1)} copy-done((f32[16,256]{1,0:T(8,128)S(1)}, f32[16,256]{1,0:T(8,128)}, u32[]{:S(2)}) %copy-start.1) | copy-done | bytes 16408
  2.8 0.2 shard_map.67
  3.1 5.1 %collective-permute-start.5 = (bf16[160,256]{1,0:T(8,128)(2,1)S(1)}, bf16[160,256]{1,0:T(8,128)(2,1)S(1)}, u32[]{:S(2)}, u32[]{:S(2)}) collective-permute-start(bf16[160,256]{1,0:T(8,128)(2,1)S(1)} %get-tuple-element.8.refs_4_), channel_id=1, source_target_pairs={{12,0},{8,4},{4,8},{0,12},{13,1},{9,5},{5,9},{1,13},{14,2},{10,6},... | collective-permute-start | bytes 245768 | tf_op jit(solution)/shard_map/ppermute | solution.py:152
  8.2 0.0 copy-start.3
  8.2 0.7 %collective-permute-start.2 = (bf16[192,256]{1,0:T(8,128)(2,1)S(1)}, bf16[192,256]{1,0:T(8,128)(2,1)S(1)}, u32[]{:S(2)}, u32[]{:S(2)}) collective-permute-start(bf16[192,256]{1,0:T(8,128)(2,1)S(1)} %get-tuple-element.7.refs_0_), channel_id=1, source_target_pairs={{3,0},{2,1},{1,2},{0,3},{7,4},{6,5},{5,6},{4,7},{11,8},{10,9},{9,1... | collective-permute-start | bytes 294920 | tf_op jit(solution)/shard_map/ppermute | solution.py:152
  8.9 0.9 %collective-permute-start.1 = (bf16[192,256]{1,0:T(8,128)(2,1)S(1)}, bf16[192,256]{1,0:T(8,128)(2,1)S(1)}, u32[]{:S(2)}, u32[]{:S(2)}) collective-permute-start(bf16[192,256]{1,0:T(8,128)(2,1)S(1)} %get-tuple-element.7.refs_0_), channel_id=1, source_target_pairs={{2,0},{3,1},{0,2},{1,3},{6,4},{7,5},{4,6},{5,7},{10,8},{11,9},{8,1... | collective-permute-start | bytes 294920 | tf_op jit(solution)/shard_map/ppermute | solution.py:152
  9.7 0.3 collective-permute-start
  10.1 0.0 collective-permute-start.4
  10.1 0.7 %collective-permute-done.5.refs_7_ = bf16[160,256]{1,0:T(8,128)(2,1)S(1)} collective-permute-done((bf16[160,256]{1,0:T(8,128)(2,1)S(1)}, bf16[160,256]{1,0:T(8,128)(2,1)S(1)}, u32[]{:S(2)}, u32[]{:S(2)}) %collective-permute-start.5) | collective-permute-done | bytes 81952 | tf_op jit(solution)/shard_map/ppermute | solution.py:152
  10.7 1.4 %collective-permute-start.3 = (bf16[160,256]{1,0:T(8,128)(2,1)S(1)}, bf16[160,256]{1,0:T(8,128)(2,1)S(1)}, u32[]{:S(2)}, u32[]{:S(2)}) collective-permute-start(bf16[160,256]{1,0:T(8,128)(2,1)S(1)} %get-tuple-element.8.refs_4_), channel_id=1, source_target_pairs={{4,0},{0,4},{12,8},{8,12},{5,1},{1,5},{13,9},{9,13},{6,2},{2,6},{1... | collective-permute-start | bytes 245768 | tf_op jit(solution)/shard_map/ppermute | solution.py:152
  12.1 4.2 %collective-permute-done.4.refs_6_ = bf16[160,256]{1,0:T(8,128)(2,1)S(1)} collective-permute-done((bf16[160,256]{1,0:T(8,128)(2,1)S(1)}, bf16[160,256]{1,0:T(8,128)(2,1)S(1)}, u32[]{:S(2)}, u32[]{:S(2)}) %collective-permute-start.4) | collective-permute-done | bytes 81952 | tf_op jit(solution)/shard_map/ppermute | solution.py:152
  16.3 0.6 %collective-permute-done.3.refs_5_ = bf16[160,256]{1,0:T(8,128)(2,1)S(1)} collective-permute-done((bf16[160,256]{1,0:T(8,128)(2,1)S(1)}, bf16[160,256]{1,0:T(8,128)(2,1)S(1)}, u32[]{:S(2)}, u32[]{:S(2)}) %collective-permute-start.3) | collective-permute-done | bytes 81952 | tf_op jit(solution)/shard_map/ppermute | solution.py:152
  16.9 0.0 collective-permute-done.2.refs_3_
  16.9 0.0 collective-permute-done.1.refs_2_
  16.9 0.0 collective-permute-done.refs_1_
  16.9 0.0 copy-done.3
  16.9 2.9 %shard_map.68.refs_4_ = f32[4,16,256]{2,1,0:T(8,128)S(1)} custom-call(bf16[192,256]{1,0:T(8,128)(2,1)S(1)} %get-tuple-element.7.refs_0_, bf16[192,256]{1,0:T(8,128)(2,1)S(1)} %collective-permute-done.refs_1_, bf16[192,256]{1,0:T(8,128)(2,1)S(1)} %collective-permute-done.1.refs_2_, bf16[192,256]{1,0:T(8,128)(2,1)S(1)} %collective-permute-done.2.refs_3_, ...), custom_call_target="tpu_custom_call" | custom-call | tf_op jit(solution)/shard_map/pallas_call | solution.py:179
  19.8 0.4 %collective-permute-start.8 = (f32[4,16,256]{2,1,0:T(8,128)S(1)}, f32[4,16,256]{2,1,0:T(8,128)S(1)}, u32[]{:S(2)}, u32[]{:S(2)}) collective-permute-start(f32[4,16,256]{2,1,0:T(8,128)S(1)} %shard_map.68.refs_4_), channel_id=1, source_target_pairs={{3,0},{2,1},{1,2},{0,3},{7,4},{6,5},{5,6},{4,7},{11,8},{10,9},{9,1... | collective-permute-start | bytes 196616 | tf_op jit(solution)/shard_map/ppermute | solution.py:152
  20.2 1.3 %collective-permute-start.7 = (f32[4,16,256]{2,1,0:T(8,128)S(1)}, f32[4,16,256]{2,1,0:T(8,128)S(1)}, u32[]{:S(2)}, u32[]{:S(2)}) collective-permute-start(f32[4,16,256]{2,1,0:T(8,128)S(1)} %shard_map.68.refs_4_), channel_id=1, source_target_pairs={{2,0},{3,1},{0,2},{1,3},{6,4},{7,5},{4,6},{5,7},{10,8},{11,9},{8,1... | collective-permute-start | bytes 196616 | tf_op jit(solution)/shard_map/ppermute | solution.py:152
  21.5 0.2 collective-permute-start.6
  21.7 2.4 %collective-permute-done.8.refs_7_ = f32[4,16,256]{2,1,0:T(8,128)S(1)} collective-permute-done((f32[4,16,256]{2,1,0:T(8,128)S(1)}, f32[4,16,256]{2,1,0:T(8,128)S(1)}, u32[]{:S(2)}, u32[]{:S(2)}) %collective-permute-start.8) | collective-permute-done | bytes 65568 | tf_op jit(solution)/shard_map/ppermute | solution.py:152
  24.1 1.6 %collective-permute-done.7.refs_6_ = f32[4,16,256]{2,1,0:T(8,128)S(1)} collective-permute-done((f32[4,16,256]{2,1,0:T(8,128)S(1)}, f32[4,16,256]{2,1,0:T(8,128)S(1)}, u32[]{:S(2)}, u32[]{:S(2)}) %collective-permute-start.7) | collective-permute-done | bytes 65568 | tf_op jit(solution)/shard_map/ppermute | solution.py:152
  25.6 0.0 collective-permute-done.6.refs_5_
  25.6 0.1 shard_map.69
  25.8 0.0 copy-start.2
  25.8 8.8 %all_to_all.5.refs_0_ = f32[4,16,128]{2,1,0:T(8,128)S(1)} all-to-all(f32[4,16,128]{2,1,0:T(8,128)S(1)} %broadcast_in_dim.11), channel_id=1, replica_groups=mesh['parts'=2,'blk'=4,'grp'=2,'sub'=2] {'blk'}, dimensions={0} | all-to-all | bytes 65536 | tf_op jit(solution)/shard_map/all_to_all | solution.py:196
  34.6 0.0 copy-done.2
  34.6 0.8 %shard_map.70 = (f32[16,256]{1,0:T(8,128)}, f32[16,256]{1,0:T(8,128)}, f32[16,256]{1,0:T(8,128)}) custom-call(f32[16,256]{1,0:T(8,128)S(1)} %get-tuple-element.9.image_ref, f32[16,256]{1,0:T(8,128)S(1)} %copy-done.2, f32[4,16,128]{2,1,0:T(8,128)S(1)} %all_to_all.5.refs_0_), custom_call_target="tpu_custom_call" | custom-call | tf_op jit(solution)/shard_map/pallas_call | solution.py:193
  (1 shorter events, 0.0 us)
Async XLA Ops:
  0.6 0.7 %copy-start.4 = (f32[128]{0:T(128)S(1)}, f32[128]{0:T(128)}, u32[]{:S(2)}) copy-start(f32[128]{0:T(128)} %param.5) | copy-start | bytes 1540
  1.3 0.8 %copy-start = (bf16[128,256]{1,0:T(8,128)(2,1)S(1)}, bf16[128,256]{1,0:T(8,128)(2,1)}, u32[]{:S(2)}) copy-start(bf16[128,256]{1,0:T(8,128)(2,1)} %features_hbm.1) | copy-start | bytes 196612
  2.1 0.7 %copy-start.1 = (f32[16,256]{1,0:T(8,128)S(1)}, f32[16,256]{1,0:T(8,128)}, u32[]{:S(2)}) copy-start(f32[16,256]{1,0:T(8,128)} %probes_ref.1) | copy-start | bytes 49156
  3.1 7.7 %collective-permute-start.5 = (bf16[160,256]{1,0:T(8,128)(2,1)S(1)}, bf16[160,256]{1,0:T(8,128)(2,1)S(1)}, u32[]{:S(2)}, u32[]{:S(2)}) collective-permute-start(bf16[160,256]{1,0:T(8,128)(2,1)S(1)} %get-tuple-element.8.refs_4_), channel_id=1, source_target_pairs={{12,0},{8,4},{4,8},{0,12},{13,1},{9,5},{5,9},{1,13},{14,2},{10,6},... | collective-permute-start | bytes 245768 | tf_op jit(solution)/shard_map/ppermute | solution.py:152
  8.2 8.7 %copy-start.3 = (f32[256]{0:T(256)S(1)}, f32[256]{0:T(256)}, u32[]{:S(2)}) copy-start(f32[256]{0:T(256)} %param.6) | copy-start | bytes 3076
  8.2 8.7 %collective-permute-start.2 = (bf16[192,256]{1,0:T(8,128)(2,1)S(1)}, bf16[192,256]{1,0:T(8,128)(2,1)S(1)}, u32[]{:S(2)}, u32[]{:S(2)}) collective-permute-start(bf16[192,256]{1,0:T(8,128)(2,1)S(1)} %get-tuple-element.7.refs_0_), channel_id=1, source_target_pairs={{3,0},{2,1},{1,2},{0,3},{7,4},{6,5},{5,6},{4,7},{11,8},{10,9},{9,1... | collective-permute-start | bytes 294920 | tf_op jit(solution)/shard_map/ppermute | solution.py:152
  8.9 8.0 %collective-permute-start.1 = (bf16[192,256]{1,0:T(8,128)(2,1)S(1)}, bf16[192,256]{1,0:T(8,128)(2,1)S(1)}, u32[]{:S(2)}, u32[]{:S(2)}) collective-permute-start(bf16[192,256]{1,0:T(8,128)(2,1)S(1)} %get-tuple-element.7.refs_0_), channel_id=1, source_target_pairs={{2,0},{3,1},{0,2},{1,3},{6,4},{7,5},{4,6},{5,7},{10,8},{11,9},{8,1... | collective-permute-start | bytes 294920 | tf_op jit(solution)/shard_map/ppermute | solution.py:152
  9.7 7.2 %collective-permute-start = (bf16[192,256]{1,0:T(8,128)(2,1)S(1)}, bf16[192,256]{1,0:T(8,128)(2,1)S(1)}, u32[]{:S(2)}, u32[]{:S(2)}) collective-permute-start(bf16[192,256]{1,0:T(8,128)(2,1)S(1)} %get-tuple-element.7.refs_0_), channel_id=1, source_target_pairs={{1,0},{0,1},{3,2},{2,3},{5,4},{4,5},{7,6},{6,7},{9,8},{8,9},{11,10... | collective-permute-start | bytes 294920 | tf_op jit(solution)/shard_map/ppermute | solution.py:152
  10.1 6.3 %collective-permute-start.4 = (bf16[160,256]{1,0:T(8,128)(2,1)S(1)}, bf16[160,256]{1,0:T(8,128)(2,1)S(1)}, u32[]{:S(2)}, u32[]{:S(2)}) collective-permute-start(bf16[160,256]{1,0:T(8,128)(2,1)S(1)} %get-tuple-element.8.refs_4_), channel_id=1, source_target_pairs={{8,0},{12,4},{0,8},{4,12},{9,1},{13,5},{1,9},{5,13},{10,2},{14,6},... | collective-permute-start | bytes 245768 | tf_op jit(solution)/shard_map/ppermute | solution.py:152
  10.7 6.1 %collective-permute-start.3 = (bf16[160,256]{1,0:T(8,128)(2,1)S(1)}, bf16[160,256]{1,0:T(8,128)(2,1)S(1)}, u32[]{:S(2)}, u32[]{:S(2)}) collective-permute-start(bf16[160,256]{1,0:T(8,128)(2,1)S(1)} %get-tuple-element.8.refs_4_), channel_id=1, source_target_pairs={{4,0},{0,4},{12,8},{8,12},{5,1},{1,5},{13,9},{9,13},{6,2},{2,6},{1... | collective-permute-start | bytes 245768 | tf_op jit(solution)/shard_map/ppermute | solution.py:152
  19.8 4.2 %collective-permute-start.8 = (f32[4,16,256]{2,1,0:T(8,128)S(1)}, f32[4,16,256]{2,1,0:T(8,128)S(1)}, u32[]{:S(2)}, u32[]{:S(2)}) collective-permute-start(f32[4,16,256]{2,1,0:T(8,128)S(1)} %shard_map.68.refs_4_), channel_id=1, source_target_pairs={{3,0},{2,1},{1,2},{0,3},{7,4},{6,5},{5,6},{4,7},{11,8},{10,9},{9,1... | collective-permute-start | bytes 196616 | tf_op jit(solution)/shard_map/ppermute | solution.py:152
  20.2 5.4 %collective-permute-start.7 = (f32[4,16,256]{2,1,0:T(8,128)S(1)}, f32[4,16,256]{2,1,0:T(8,128)S(1)}, u32[]{:S(2)}, u32[]{:S(2)}) collective-permute-start(f32[4,16,256]{2,1,0:T(8,128)S(1)} %shard_map.68.refs_4_), channel_id=1, source_target_pairs={{2,0},{3,1},{0,2},{1,3},{6,4},{7,5},{4,6},{5,7},{10,8},{11,9},{8,1... | collective-permute-start | bytes 196616 | tf_op jit(solution)/shard_map/ppermute | solution.py:152
  21.5 4.1 %collective-permute-start.6 = (f32[4,16,256]{2,1,0:T(8,128)S(1)}, f32[4,16,256]{2,1,0:T(8,128)S(1)}, u32[]{:S(2)}, u32[]{:S(2)}) collective-permute-start(f32[4,16,256]{2,1,0:T(8,128)S(1)} %shard_map.68.refs_4_), channel_id=1, source_target_pairs={{1,0},{0,1},{3,2},{2,3},{5,4},{4,5},{7,6},{6,7},{9,8},{8,9},{11,10... | collective-permute-start | bytes 196616 | tf_op jit(solution)/shard_map/ppermute | solution.py:152
  25.8 8.9 %copy-start.2 = (f32[16,256]{1,0:T(8,128)S(1)}, f32[16,256]{1,0:T(8,128)}, u32[]{:S(2)}) copy-start(f32[16,256]{1,0:T(8,128)} %probes_ref.1) | copy-start | bytes 49156

commit v5 on v3

v5 whole, which is shorter than its diff:
```python
import jax
import jax.numpy as jnp
from jax import lax
from jax.experimental import pallas as pl
from jax.experimental.pallas import tpu as pltpu
from jax.sharding import PartitionSpec as P

PLANE = ("grp", "sub")
LINE = ("blk",)
DIRECT = 8
VMEM = pltpu.CompilerParams(vmem_limit_bytes=40 * 1024 * 1024)
HALF = 8


def pieces_of(value):
    pieces = []
    for _ in range(3):
        piece = value.astype(jnp.bfloat16).astype(jnp.float32)
        pieces.append(piece)
        value = value - piece
    return pieces


def norm_rows(scaled, place):
    norms = -0.5 * jnp.sum(jnp.square(scaled.astype(jnp.float32)), axis=0, keepdims=True)
    row = lax.broadcasted_iota(jnp.int32, (2 * HALF, scaled.shape[1]), 0)
    here, there = place * HALF, (1 - place) * HALF
    rows = jnp.where((row >= there) & (row < there + 3), 1.0, 0.0)
    for number, piece in enumerate(pieces_of(norms)):
        rows = jnp.where(row == here + number, piece, rows)
    return rows.astype(jnp.bfloat16)


def pack_kernel(scaled_ref, probes_ref, line_ref, plane_ref):
    scaled = scaled_ref[...]
    rows = norm_rows(scaled, 0)
    high, low, _ = pieces_of(probes_ref[...])
    high, low = high.astype(jnp.bfloat16), low.astype(jnp.bfloat16)
    line_ref[...] = jnp.concatenate([scaled, rows.astype(jnp.bfloat16), high], axis=0)
    plane_ref[...] = jnp.concatenate([scaled, high, low], axis=0)


def image_kernel(feature_count, plane_count, *refs):
    plane_refs = refs[:plane_count]
    line_refs = refs[plane_count:-3]
    noise_ref, probes_ref, partial_ref = refs[-3:]
    depth = feature_count + 2 * HALF
    rows = []
    for ref in plane_refs:
        scaled = ref[:feature_count, :]
        rows.append(jnp.concatenate([scaled, norm_rows(scaled, 1)], axis=0))

    def add_block(block_ref, totals):
        columns = block_ref[:depth, :].astype(jnp.float32).T.astype(jnp.bfloat16)
        probes = block_ref[depth:, :]
        result = []
        for own, total in zip(rows, totals):
            exponent = jnp.dot(columns, own, preferred_element_type=jnp.float32)
            weights = jnp.exp(exponent).astype(jnp.bfloat16)
            result.append(total + jnp.dot(probes, weights, preferred_element_type=jnp.float32))
        return result

    totals = [noise_ref[...] * probes_ref[...]]
    totals += [jnp.zeros(probes_ref.shape, jnp.float32)] * (plane_count - 1)
    for ref in line_refs:
        if len(ref.shape) == 2:
            totals = add_block(ref, totals)
        else:
            totals = lax.fori_loop(
                0, ref.shape[0], lambda number, value: add_block(ref.at[number], value), totals
            )
    for number, total in enumerate(totals):
        partial_ref[number] = total


def combine_kernel(feature_count, plane_count, *refs):
    plane_refs = refs[:plane_count]
    probes_ref = refs[plane_count]
    partial_refs = refs[plane_count + 1 : -2]
    image_ref, sums_ref = refs[-2:]
    probe_count = image_ref.shape[0]
    lane = lax.broadcasted_iota(jnp.int32, sums_ref.shape, 1)
    products = [0.0, 0.0, 0.0]
    for number, plane_ref in enumerate(plane_refs):
        image = sum(
            ref[place_of(step, number, plane_count)] for step, ref in enumerate(partial_refs)
        )
        if number == 0:
            image_ref[...] = image
            probes = probes_ref[...]
        else:
            middle = feature_count + probe_count
            probes = plane_ref[feature_count:middle, :].astype(jnp.float32)
            probes = probes + plane_ref[middle:, :].astype(jnp.float32)
        products[0] += probes * probes
        products[1] += probes * image
        products[2] += image * image
    sums = jnp.zeros(sums_ref.shape, jnp.float32)
    for number, product in enumerate(products):
        sums = jnp.where(lane == number, jnp.sum(product, axis=1, keepdims=True), sums)
    sums_ref[...] = sums


def finish_kernel(image_ref, probes_ref, *refs):
    *sums_refs, solution_ref, residual_ref, direction_ref = refs
    sums = jnp.zeros(sums_refs[0].shape[-2:], jnp.float32)
    for ref in sums_refs:
        value = ref[...]
        sums = sums + (value if value.ndim == 2 else jnp.sum(value, axis=0))
    start_norms, curvature, image_norms = sums[:, 0:1], sums[:, 1:2], sums[:, 2:3]
    alpha = start_norms / curvature
    new_norms = start_norms - 2.0 * alpha * curvature + alpha * alpha * image_norms
    probes = probes_ref[...]
    residual = probes - alpha * image_ref[...]
    solution_ref[...] = alpha * probes
    residual_ref[...] = residual
    direction_ref[...] = residual + (new_norms / start_norms) * probes


def paired(count):
    return count & (count - 1) == 0


def source_of(device, step, count):
    return device ^ step if paired(count) else (device - step) % count


def place_of(step, number, count):
    return step ^ number if paired(count) else (number - step) % count


def everywhere(value, axes, count):
    if count > DIRECT:
        return [lax.all_gather(value, axes, axis=0, tiled=False)]
    return [value] + [
        lax.ppermute(value, axes, [(source_of(i, step, count), i) for i in range(count)])
        for step in range(1, count)
    ]


def plane_blocks(value, shape):
    grp_count, sub_count = shape
    if sub_count != 2 or not paired(grp_count):
        return everywhere(value, PLANE, grp_count * sub_count)
    blocks = everywhere(value, ("sub",), sub_count)
    moved = [everywhere(block, ("grp",), grp_count) for block in blocks]
    return [moved[sub][grp] for grp in range(grp_count) for sub in range(sub_count)]


def make_local(plane_shape, line_count):
    plane_count = plane_shape[0] * plane_shape[1]

    def local(features, lengthscale, noise_var, probes):
        feature_count, width = features.shape
        probe_count = probes.shape[0]
        scaled = (features.astype(jnp.float32) / lengthscale[:, None]).astype(jnp.bfloat16)
        line, plane = pl.pallas_call(
            pack_kernel,
            out_shape=(
                jax.ShapeDtypeStruct((feature_count + 2 * HALF + probe_count, width), jnp.bfloat16),
                jax.ShapeDtypeStruct((feature_count + 2 * probe_count, width), jnp.bfloat16),
            ),
            compiler_params=VMEM,
        )(scaled, probes)
        lines = everywhere(line, LINE, line_count)
        planes = plane_blocks(plane, plane_shape)
        partial = pl.pallas_call(
            lambda *refs: image_kernel(feature_count, plane_count, *refs),
            out_shape=jax.ShapeDtypeStruct((plane_count, probe_count, width), jnp.float32),
            compiler_params=VMEM,
        )(*planes, *lines, noise_var[None, :], probes)
        image, sums = pl.pallas_call(
            lambda *refs: combine_kernel(feature_count, plane_count, *refs),
            out_shape=(
                jax.ShapeDtypeStruct(probes.shape, jnp.float32),
                jax.ShapeDtypeStruct((probe_count, 128), jnp.float32),
            ),
            compiler_params=VMEM,
        )(*planes, probes, *everywhere(partial, PLANE, plane_count))
        outs = (jax.ShapeDtypeStruct(probes.shape, jnp.float32),) * 3
        return pl.pallas_call(finish_kernel, out_shape=outs, compiler_params=VMEM)(
            image, probes, *everywhere(sums, LINE, line_count)
        )

    return local


def solution(mesh):
    plane_shape = (mesh.shape["grp"], mesh.shape["sub"])
    spread = P(None, ("parts", "blk", "grp", "sub"))
    return jax.shard_map(
        make_local(plane_shape, mesh.shape["blk"]),
        mesh=mesh,
        in_specs=(spread, P("parts"), P(("parts", "blk", "grp", "sub")), spread),
        out_specs=(spread, spread, spread),
        check_vma=False,
    )
```

time: 33.3 us -> 31.5 us (0.946)
  local copies, waits for them, and re-layouts: 2.21 us -> 0.01 us
  other arithmetic: 0 us -> 0.93 us
  starting transfers between devices: 14.6 us -> 14 us
    unnamed x10 -> x4, local copies, waits for them, and re-layouts: 2.21 us -> 0.01 us
    convert_element_type x0 -> x1, other arithmetic: none -> 0.93 us  [local(): (features.astype(jnp.float32) / lengthscale[:, None]).astype(jnp.bfloat16)]
    ppermute x12, starting transfers between devices: 14.6 us -> 14 us  [everywhere(): lax.ppermute(value, axes, [(source_of(i, step, count), i) for i in range(...]
  transfers between devices with their start and end apart: 12 -> 12, of which waited for: 7 -> 6; matrix products, arithmetic and copies ran while one was open for 0% -> 0% of each run, Pallas kernels for 0% -> 0%
where the time goes in v5:
time: 31.5 us; the launch traced here: 31.3 us
  starting transfers between devices  14 us (44%)
  waiting for transfers between devices  11.8 us (37%)
  Pallas kernels  3.83 us (12%)
  other arithmetic  0.93 us (3%)
  between operations  0.67 us (2%)
    ppermute x12, starting transfers between devices, everywhere(): lax.ppermute(value, axes, [(source_of(i, step, count), i) for i in range(...  14 us
    ppermute x12, waiting for transfers between devices, everywhere(): lax.ppermute(value, axes, [(source_of(i, step, count), i) for i in range(...  11.8 us
    pallas_call x1, Pallas kernels, local(): pl.pallas_call(lambda *refs: image_kernel(feature_count, plane_count, *re...  2.92 us
    convert_element_type x1, other arithmetic, local(): (features.astype(jnp.float32) / lengthscale[:, None]).astype(jnp.bfloat16)  0.93 us
    pallas_call x1, Pallas kernels, local(): pl.pallas_call(finish_kernel, out_shape=outs, compiler_params=VMEM)  0.77 us
  transfers between devices with their start and end apart: 12, of which 6 were waited for; matrix products, arithmetic and copies ran while one was open for 0% of the time, Pallas kernels for 0%

profile of v5, /device:TPU:0, one launch (start us, length us, event | category | flops | bytes accessed | tf_op | source)
XLA Modules:
  0.0 31.3 jit_solution(2605979483122928677)
XLA Ops:
  0.6 0.0 copy-start
  0.6 0.9 %divide_convert_fusion.scaled_ref = bf16[128,256]{1,0:T(8,128)(2,1)S(1)} fusion(bf16[128,256]{1,0:T(8,128)(2,1)} %param.4, f32[128]{0:T(128)} %param.5), kind=kLoop, calls=%fused_computation | loop fusion | flops 98304 | bytes 131584 | tf_op jit(solution)/shard_map/convert_element_type | solution.py:156
  1.6 0.0 copy-done
  1.6 0.5 %collective-permute-start = (bf16[160,256]{1,0:T(8,128)(2,1)S(1)}, bf16[160,256]{1,0:T(8,128)(2,1)S(1)}, u32[]{:S(2)}, u32[]{:S(2)}) collective-permute-start(bf16[160,256]{1,0:T(8,128)(2,1)S(1)} %get-tuple-element.7.refs_0_), channel_id=1, source_target_pairs={{1,0},{0,1},{3,2},{2,3},{5,4},{4,5},{7,6},{6,7},{9,8},{8,9},{11,10... | collective-permute-start | bytes 245768 | tf_op jit(solution)/shard_map/ppermute | solution.py:136
  2.1 2.6 %collective-permute-start.1 = (bf16[160,256]{1,0:T(8,128)(2,1)S(1)}, bf16[160,256]{1,0:T(8,128)(2,1)S(1)}, u32[]{:S(2)}, u32[]{:S(2)}) collective-permute-start(bf16[160,256]{1,0:T(8,128)(2,1)S(1)} %get-tuple-element.7.refs_0_), channel_id=1, source_target_pairs={{2,0},{0,2},{3,1},{1,3},{6,4},{4,6},{7,5},{5,7},{10,8},{8,10},{11,... | collective-permute-start | bytes 245768 | tf_op jit(solution)/shard_map/ppermute | solution.py:136
  4.7 0.0 copy-start.1
  4.7 3.6 %collective-permute-start.5 = (bf16[160,256]{1,0:T(8,128)(2,1)S(1)}, bf16[160,256]{1,0:T(8,128)(2,1)S(1)}, u32[]{:S(2)}, u32[]{:S(2)}) collective-permute-start(bf16[160,256]{1,0:T(8,128)(2,1)S(1)} %get-tuple-element.8.refs_4_), channel_id=1, source_target_pairs={{12,0},{8,4},{4,8},{0,12},{13,1},{9,5},{5,9},{1,13},{14,2},{10,6},... | collective-permute-start | bytes 245768 | tf_op jit(solution)/shard_map/ppermute | solution.py:136
  8.3 0.0 collective-permute-start.4
  8.3 0.8 %collective-permute-start.3 = (bf16[160,256]{1,0:T(8,128)(2,1)S(1)}, bf16[160,256]{1,0:T(8,128)(2,1)S(1)}, u32[]{:S(2)}, u32[]{:S(2)}) collective-permute-start(bf16[160,256]{1,0:T(8,128)(2,1)S(1)} %get-tuple-element.8.refs_4_), channel_id=1, source_target_pairs={{4,0},{0,4},{12,8},{8,12},{5,1},{1,5},{13,9},{9,13},{6,2},{2,6},{1... | collective-permute-start | bytes 245768 | tf_op jit(solution)/shard_map/ppermute | solution.py:136
  9.1 0.0 collective-permute-done.refs_1_
  9.1 0.3 %collective-permute-start.2 = (bf16[160,256]{1,0:T(8,128)(2,1)S(1)}, bf16[160,256]{1,0:T(8,128)(2,1)S(1)}, u32[]{:S(2)}, u32[]{:S(2)}) collective-permute-start(bf16[160,256]{1,0:T(8,128)(2,1)S(1)} %collective-permute-done.refs_1_), channel_id=1, source_target_pairs={{2,0},{0,2},{3,1},{1,3},{6,4},{4,6},{7,5},{5,7},{10,8},{8,10},{11,... | collective-permute-start | bytes 245768 | tf_op jit(solution)/shard_map/ppermute | solution.py:136
  9.4 0.0 collective-permute-done.1.refs_2_
  9.4 2.3 %collective-permute-done.5.refs_7_ = bf16[160,256]{1,0:T(8,128)(2,1)S(1)} collective-permute-done((bf16[160,256]{1,0:T(8,128)(2,1)S(1)}, bf16[160,256]{1,0:T(8,128)(2,1)S(1)}, u32[]{:S(2)}, u32[]{:S(2)}) %collective-permute-start.5) | collective-permute-done | bytes 81952 | tf_op jit(solution)/shard_map/ppermute | solution.py:136
  11.7 3.8 %collective-permute-done.4.refs_6_ = bf16[160,256]{1,0:T(8,128)(2,1)S(1)} collective-permute-done((bf16[160,256]{1,0:T(8,128)(2,1)S(1)}, bf16[160,256]{1,0:T(8,128)(2,1)S(1)}, u32[]{:S(2)}, u32[]{:S(2)}) %collective-permute-start.4) | collective-permute-done | bytes 81952 | tf_op jit(solution)/shard_map/ppermute | solution.py:136
  15.5 0.0 collective-permute-done.3.refs_5_
  15.5 0.0 collective-permute-done.2.refs_3_
  15.5 0.0 copy-done.1
  15.5 2.9 %shard_map.68.refs_5_ = f32[4,16,256]{2,1,0:T(8,128)S(1)} custom-call(bf16[160,256]{1,0:T(8,128)(2,1)S(1)} %get-tuple-element.7.refs_0_, bf16[160,256]{1,0:T(8,128)(2,1)S(1)} %collective-permute-done.refs_1_, bf16[160,256]{1,0:T(8,128)(2,1)S(1)} %collective-permute-done.1.refs_2_, bf16[160,256]{1,0:T(8,128)(2,1)S(1)} %collective-permute-done.2.refs_3_, ...), custom_call_target="tpu_custom_call" | custom-call | tf_op jit(solution)/shard_map/pallas_call | solution.py:167
  18.4 0.0 collective-permute-start.8
  18.4 1.0 %collective-permute-start.7 = (f32[4,16,256]{2,1,0:T(8,128)S(1)}, f32[4,16,256]{2,1,0:T(8,128)S(1)}, u32[]{:S(2)}, u32[]{:S(2)}) collective-permute-start(f32[4,16,256]{2,1,0:T(8,128)S(1)} %shard_map.68.refs_5_), channel_id=1, source_target_pairs={{2,0},{3,1},{0,2},{1,3},{6,4},{7,5},{4,6},{5,7},{10,8},{11,9},{8,1... | collective-permute-start | bytes 196616 | tf_op jit(solution)/shard_map/ppermute | solution.py:136
  19.4 0.9 %collective-permute-start.6 = (f32[4,16,256]{2,1,0:T(8,128)S(1)}, f32[4,16,256]{2,1,0:T(8,128)S(1)}, u32[]{:S(2)}, u32[]{:S(2)}) collective-permute-start(f32[4,16,256]{2,1,0:T(8,128)S(1)} %shard_map.68.refs_5_), channel_id=1, source_target_pairs={{1,0},{0,1},{3,2},{2,3},{5,4},{4,5},{7,6},{6,7},{9,8},{8,9},{11,10... | collective-permute-start | bytes 196616 | tf_op jit(solution)/shard_map/ppermute | solution.py:136
  20.3 2.4 %collective-permute-done.8.refs_8_ = f32[4,16,256]{2,1,0:T(8,128)S(1)} collective-permute-done((f32[4,16,256]{2,1,0:T(8,128)S(1)}, f32[4,16,256]{2,1,0:T(8,128)S(1)}, u32[]{:S(2)}, u32[]{:S(2)}) %collective-permute-start.8) | collective-permute-done | bytes 65568 | tf_op jit(solution)/shard_map/ppermute | solution.py:136
  22.7 0.7 %collective-permute-done.7.refs_7_ = f32[4,16,256]{2,1,0:T(8,128)S(1)} collective-permute-done((f32[4,16,256]{2,1,0:T(8,128)S(1)}, f32[4,16,256]{2,1,0:T(8,128)S(1)}, u32[]{:S(2)}, u32[]{:S(2)}) %collective-permute-start.7) | collective-permute-done | bytes 65568 | tf_op jit(solution)/shard_map/ppermute | solution.py:136
  23.4 0.0 collective-permute-done.6.refs_6_
  23.4 0.1 shard_map.69
  23.5 2.5 %collective-permute-start.11 = (f32[16,128]{1,0:T(8,128)S(1)}, f32[16,128]{1,0:T(8,128)S(1)}, u32[]{:S(2)}, u32[]{:S(2)}) collective-permute-start(f32[16,128]{1,0:T(8,128)S(1)} %get-tuple-element.10.refs_0_), channel_id=1, source_target_pairs={{12,0},{8,4},{4,8},{0,12},{13,1},{9,5},{5,9},{1,13},{14,2},{10,6},... | collective-permute-start | bytes 24584 | tf_op jit(solution)/shard_map/ppermute | solution.py:136
  26.0 0.0 collective-permute-start.10
  26.0 1.9 %collective-permute-start.9 = (f32[16,128]{1,0:T(8,128)S(1)}, f32[16,128]{1,0:T(8,128)S(1)}, u32[]{:S(2)}, u32[]{:S(2)}) collective-permute-start(f32[16,128]{1,0:T(8,128)S(1)} %get-tuple-element.10.refs_0_), channel_id=1, source_target_pairs={{4,0},{0,4},{12,8},{8,12},{5,1},{1,5},{13,9},{9,13},{6,2},{2,6},{1... | collective-permute-start | bytes 24584 | tf_op jit(solution)/shard_map/ppermute | solution.py:136
  27.9 1.1 %collective-permute-done.11.refs_3_ = f32[16,128]{1,0:T(8,128)S(1)} collective-permute-done((f32[16,128]{1,0:T(8,128)S(1)}, f32[16,128]{1,0:T(8,128)S(1)}, u32[]{:S(2)}, u32[]{:S(2)}) %collective-permute-start.11) | collective-permute-done | bytes 8224 | tf_op jit(solution)/shard_map/ppermute | solution.py:136
  29.0 1.6 %collective-permute-done.10.refs_2_ = f32[16,128]{1,0:T(8,128)S(1)} collective-permute-done((f32[16,128]{1,0:T(8,128)S(1)}, f32[16,128]{1,0:T(8,128)S(1)}, u32[]{:S(2)}, u32[]{:S(2)}) %collective-permute-start.10) | collective-permute-done | bytes 8224 | tf_op jit(solution)/shard_map/ppermute | solution.py:136
  30.5 0.0 collective-permute-done.9.refs_1_
  30.5 0.8 %shard_map.70 = (f32[16,256]{1,0:T(8,128)}, f32[16,256]{1,0:T(8,128)}, f32[16,256]{1,0:T(8,128)}) custom-call(f32[16,256]{1,0:T(8,128)S(1)} %get-tuple-element.9.image_ref, f32[16,256]{1,0:T(8,128)S(1)} %copy-done, f32[16,128]{1,0:T(8,128)S(1)} %get-tuple-element.10.refs_0_, f32[16,128]{1,0:T(8,128)S(1)} %collective-permute-done.9.refs_1_, ...), custom_call_target="tpu_custom_call" | custom-call | tf_op jit(solution)/shard_map/pallas_call | solution.py:181
  (1 shorter events, 0.0 us)
Async XLA Ops:
  0.6 1.0 %copy-start = (f32[16,256]{1,0:T(8,128)S(1)}, f32[16,256]{1,0:T(8,128)}, u32[]{:S(2)}) copy-start(f32[16,256]{1,0:T(8,128)} %probes_ref.3) | copy-start | bytes 49156
  1.6 7.5 %collective-permute-start = (bf16[160,256]{1,0:T(8,128)(2,1)S(1)}, bf16[160,256]{1,0:T(8,128)(2,1)S(1)}, u32[]{:S(2)}, u32[]{:S(2)}) collective-permute-start(bf16[160,256]{1,0:T(8,128)(2,1)S(1)} %get-tuple-element.7.refs_0_), channel_id=1, source_target_pairs={{1,0},{0,1},{3,2},{2,3},{5,4},{4,5},{7,6},{6,7},{9,8},{8,9},{11,10... | collective-permute-start | bytes 245768 | tf_op jit(solution)/shard_map/ppermute | solution.py:136
  2.1 7.3 %collective-permute-start.1 = (bf16[160,256]{1,0:T(8,128)(2,1)S(1)}, bf16[160,256]{1,0:T(8,128)(2,1)S(1)}, u32[]{:S(2)}, u32[]{:S(2)}) collective-permute-start(bf16[160,256]{1,0:T(8,128)(2,1)S(1)} %get-tuple-element.7.refs_0_), channel_id=1, source_target_pairs={{2,0},{0,2},{3,1},{1,3},{6,4},{4,6},{7,5},{5,7},{10,8},{8,10},{11,... | collective-permute-start | bytes 245768 | tf_op jit(solution)/shard_map/ppermute | solution.py:136
  4.7 10.8 %copy-start.1 = (f32[256]{0:T(256)S(1)}, f32[256]{0:T(256)}, u32[]{:S(2)}) copy-start(f32[256]{0:T(256)} %param.6) | copy-start | bytes 3076
  4.7 7.0 %collective-permute-start.5 = (bf16[160,256]{1,0:T(8,128)(2,1)S(1)}, bf16[160,256]{1,0:T(8,128)(2,1)S(1)}, u32[]{:S(2)}, u32[]{:S(2)}) collective-permute-start(bf16[160,256]{1,0:T(8,128)(2,1)S(1)} %get-tuple-element.8.refs_4_), channel_id=1, source_target_pairs={{12,0},{8,4},{4,8},{0,12},{13,1},{9,5},{5,9},{1,13},{14,2},{10,6},... | collective-permute-start | bytes 245768 | tf_op jit(solution)/shard_map/ppermute | solution.py:136
  8.3 7.2 %collective-permute-start.4 = (bf16[160,256]{1,0:T(8,128)(2,1)S(1)}, bf16[160,256]{1,0:T(8,128)(2,1)S(1)}, u32[]{:S(2)}, u32[]{:S(2)}) collective-permute-start(bf16[160,256]{1,0:T(8,128)(2,1)S(1)} %get-tuple-element.8.refs_4_), channel_id=1, source_target_pairs={{8,0},{12,4},{0,8},{4,12},{9,1},{13,5},{1,9},{5,13},{10,2},{14,6},... | collective-permute-start | bytes 245768 | tf_op jit(solution)/shard_map/ppermute | solution.py:136
  8.3 7.2 %collective-permute-start.3 = (bf16[160,256]{1,0:T(8,128)(2,1)S(1)}, bf16[160,256]{1,0:T(8,128)(2,1)S(1)}, u32[]{:S(2)}, u32[]{:S(2)}) collective-permute-start(bf16[160,256]{1,0:T(8,128)(2,1)S(1)} %get-tuple-element.8.refs_4_), channel_id=1, source_target_pairs={{4,0},{0,4},{12,8},{8,12},{5,1},{1,5},{13,9},{9,13},{6,2},{2,6},{1... | collective-permute-start | bytes 245768 | tf_op jit(solution)/shard_map/ppermute | solution.py:136
  9.1 6.4 %collective-permute-start.2 = (bf16[160,256]{1,0:T(8,128)(2,1)S(1)}, bf16[160,256]{1,0:T(8,128)(2,1)S(1)}, u32[]{:S(2)}, u32[]{:S(2)}) collective-permute-start(bf16[160,256]{1,0:T(8,128)(2,1)S(1)} %collective-permute-done.refs_1_), channel_id=1, source_target_pairs={{2,0},{0,2},{3,1},{1,3},{6,4},{4,6},{7,5},{5,7},{10,8},{8,10},{11,... | collective-permute-start | bytes 245768 | tf_op jit(solution)/shard_map/ppermute | solution.py:136
  18.4 4.3 %collective-permute-start.8 = (f32[4,16,256]{2,1,0:T(8,128)S(1)}, f32[4,16,256]{2,1,0:T(8,128)S(1)}, u32[]{:S(2)}, u32[]{:S(2)}) collective-permute-start(f32[4,16,256]{2,1,0:T(8,128)S(1)} %shard_map.68.refs_5_), channel_id=1, source_target_pairs={{3,0},{2,1},{1,2},{0,3},{7,4},{6,5},{5,6},{4,7},{11,8},{10,9},{9,1... | collective-permute-start | bytes 196616 | tf_op jit(solution)/shard_map/ppermute | solution.py:136
  18.4 5.0 %collective-permute-start.7 = (f32[4,16,256]{2,1,0:T(8,128)S(1)}, f32[4,16,256]{2,1,0:T(8,128)S(1)}, u32[]{:S(2)}, u32[]{:S(2)}) collective-permute-start(f32[4,16,256]{2,1,0:T(8,128)S(1)} %shard_map.68.refs_5_), channel_id=1, source_target_pairs={{2,0},{3,1},{0,2},{1,3},{6,4},{7,5},{4,6},{5,7},{10,8},{11,9},{8,1... | collective-permute-start | bytes 196616 | tf_op jit(solution)/shard_map/ppermute | solution.py:136
  19.4 4.0 %collective-permute-start.6 = (f32[4,16,256]{2,1,0:T(8,128)S(1)}, f32[4,16,256]{2,1,0:T(8,128)S(1)}, u32[]{:S(2)}, u32[]{:S(2)}) collective-permute-start(f32[4,16,256]{2,1,0:T(8,128)S(1)} %shard_map.68.refs_5_), channel_id=1, source_target_pairs={{1,0},{0,1},{3,2},{2,3},{5,4},{4,5},{7,6},{6,7},{9,8},{8,9},{11,10... | collective-permute-start | bytes 196616 | tf_op jit(solution)/shard_map/ppermute | solution.py:136
  23.5 5.5 %collective-permute-start.11 = (f32[16,128]{1,0:T(8,128)S(1)}, f32[16,128]{1,0:T(8,128)S(1)}, u32[]{:S(2)}, u32[]{:S(2)}) collective-permute-start(f32[16,128]{1,0:T(8,128)S(1)} %get-tuple-element.10.refs_0_), channel_id=1, source_target_pairs={{12,0},{8,4},{4,8},{0,12},{13,1},{9,5},{5,9},{1,13},{14,2},{10,6},... | collective-permute-start | bytes 24584 | tf_op jit(solution)/shard_map/ppermute | solution.py:136
  26.0 4.5 %collective-permute-start.10 = (f32[16,128]{1,0:T(8,128)S(1)}, f32[16,128]{1,0:T(8,128)S(1)}, u32[]{:S(2)}, u32[]{:S(2)}) collective-permute-start(f32[16,128]{1,0:T(8,128)S(1)} %get-tuple-element.10.refs_0_), channel_id=1, source_target_pairs={{8,0},{12,4},{0,8},{4,12},{9,1},{13,5},{1,9},{5,13},{10,2},{14,6},... | collective-permute-start | bytes 24584 | tf_op jit(solution)/shard_map/ppermute | solution.py:136
  26.0 4.5 %collective-permute-start.9 = (f32[16,128]{1,0:T(8,128)S(1)}, f32[16,128]{1,0:T(8,128)S(1)}, u32[]{:S(2)}, u32[]{:S(2)}) collective-permute-start(f32[16,128]{1,0:T(8,128)S(1)} %get-tuple-element.10.refs_0_), channel_id=1, source_target_pairs={{4,0},{0,4},{12,8},{8,12},{5,1},{1,5},{13,9},{9,13},{6,2},{2,6},{1... | collective-permute-start | bytes 24584 | tf_op jit(solution)/shard_map/ppermute | solution.py:136

commit v6 on v5

--- a/solution.py
+++ b/solution.py
@@ -31,28 +31,23 @@
     return rows.astype(jnp.bfloat16)
 
 
-def pack_kernel(scaled_ref, probes_ref, line_ref, plane_ref):
-    scaled = scaled_ref[...]
-    rows = norm_rows(scaled, 0)
-    high, low, _ = pieces_of(probes_ref[...])
-    high, low = high.astype(jnp.bfloat16), low.astype(jnp.bfloat16)
-    line_ref[...] = jnp.concatenate([scaled, rows.astype(jnp.bfloat16), high], axis=0)
-    plane_ref[...] = jnp.concatenate([scaled, high, low], axis=0)
+def pack_kernel(scaled_ref, probes_ref, line_ref):
+    line_ref[...] = jnp.concatenate(
+        [scaled_ref[...], probes_ref[...].astype(jnp.bfloat16)], axis=0
+    )
 
 
 def image_kernel(feature_count, plane_count, *refs):
     plane_refs = refs[:plane_count]
     line_refs = refs[plane_count:-3]
     noise_ref, probes_ref, partial_ref = refs[-3:]
-    depth = feature_count + 2 * HALF
-    rows = []
-    for ref in plane_refs:
-        scaled = ref[:feature_count, :]
-        rows.append(jnp.concatenate([scaled, norm_rows(scaled, 1)], axis=0))
+    rows = [jnp.concatenate([ref[...], norm_rows(ref[...], 1)], axis=0) for ref in plane_refs]
 
     def add_block(block_ref, totals):
-        columns = block_ref[:depth, :].astype(jnp.float32).T.astype(jnp.bfloat16)
-        probes = block_ref[depth:, :]
+        scaled = block_ref[:feature_count, :]
+        columns = jnp.concatenate([scaled, norm_rows(scaled, 0)], axis=0)
+        columns = columns.astype(jnp.float32).T.astype(jnp.bfloat16)
+        probes = block_ref[feature_count:, :]
         result = []
         for own, total in zip(rows, totals):
             exponent = jnp.dot(columns, own, preferred_element_type=jnp.float32)
@@ -71,27 +66,21 @@
             )
     for number, total in enumerate(totals):
         partial_ref[number] = total
+    partial_ref[plane_count] = probes_ref[...]
 
 
-def combine_kernel(feature_count, plane_count, *refs):
-    plane_refs = refs[:plane_count]
-    probes_ref = refs[plane_count]
-    partial_refs = refs[plane_count + 1 : -2]
+def combine_kernel(plane_count, *refs):
+    partial_refs = refs[:-2]
     image_ref, sums_ref = refs[-2:]
-    probe_count = image_ref.shape[0]
     lane = lax.broadcasted_iota(jnp.int32, sums_ref.shape, 1)
     products = [0.0, 0.0, 0.0]
-    for number, plane_ref in enumerate(plane_refs):
+    for number, own_ref in enumerate(partial_refs):
         image = sum(
             ref[place_of(step, number, plane_count)] for step, ref in enumerate(partial_refs)
         )
         if number == 0:
             image_ref[...] = image
-            probes = probes_ref[...]
-        else:
-            middle = feature_count + probe_count
-            probes = plane_ref[feature_count:middle, :].astype(jnp.float32)
-            probes = probes + plane_ref[middle:, :].astype(jnp.float32)
+        probes = own_ref[plane_count]
         products[0] += probes * probes
         products[1] += probes * image
         products[2] += image * image
@@ -154,29 +143,26 @@
         feature_count, width = features.shape
         probe_count = probes.shape[0]
         scaled = (features.astype(jnp.float32) / lengthscale[:, None]).astype(jnp.bfloat16)
-        line, plane = pl.pallas_call(
+        line = pl.pallas_call(
             pack_kernel,
-            out_shape=(
-                jax.ShapeDtypeStruct((feature_count + 2 * HALF + probe_count, width), jnp.bfloat16),
-                jax.ShapeDtypeStruct((feature_count + 2 * probe_count, width), jnp.bfloat16),
-            ),
+            out_shape=jax.ShapeDtypeStruct((feature_count + probe_count, width), jnp.bfloat16),
             compiler_params=VMEM,
         )(scaled, probes)
         lines = everywhere(line, LINE, line_count)
-        planes = plane_blocks(plane, plane_shape)
+        planes = plane_blocks(scaled, plane_shape)
         partial = pl.pallas_call(
             lambda *refs: image_kernel(feature_count, plane_count, *refs),
-            out_shape=jax.ShapeDtypeStruct((plane_count, probe_count, width), jnp.float32),
+            out_shape=jax.ShapeDtypeStruct((plane_count + 1, probe_count, width), jnp.float32),
             compiler_params=VMEM,
         )(*planes, *lines, noise_var[None, :], probes)
         image, sums = pl.pallas_call(
-            lambda *refs: combine_kernel(feature_count, plane_count, *refs),
+            lambda *refs: combine_kernel(plane_count, *refs),
             out_shape=(
                 jax.ShapeDtypeStruct(probes.shape, jnp.float32),
                 jax.ShapeDtypeStruct((probe_count, 128), jnp.float32),
             ),
             compiler_params=VMEM,
-        )(*planes, probes, *everywhere(partial, PLANE, plane_count))
+        )(*everywhere(partial, PLANE, plane_count))
         outs = (jax.ShapeDtypeStruct(probes.shape, jnp.float32),) * 3
         return pl.pallas_call(finish_kernel, out_shape=outs, compiler_params=VMEM)(
             image, probes, *everywhere(sums, LINE, line_count)

time: 31.5 us -> 30.8 us (0.978)
  waiting for transfers between devices: 11.8 us -> 11.1 us
    ppermute x12, waiting for transfers between devices: 11.8 us -> 11.1 us  [everywhere(): lax.ppermute(value, axes, [(source_of(i, step, count), i) for i in range(...]
where the time goes in v6:
time: 30.8 us; the launch traced here: 30.7 us
  starting transfers between devices  14.1 us (46%)
  waiting for transfers between devices  11.1 us (36%)
  Pallas kernels  3.84 us (12%)
  other arithmetic  0.93 us (3%)
  between operations  0.68 us (2%)
    ppermute x12, starting transfers between devices, everywhere(): lax.ppermute(value, axes, [(source_of(i, step, count), i) for i in range(...  14.1 us
    ppermute x12, waiting for transfers between devices, everywhere(): lax.ppermute(value, axes, [(source_of(i, step, count), i) for i in range(...  11.1 us
    pallas_call x1, Pallas kernels, local(): pl.pallas_call(lambda *refs: image_kernel(feature_count, plane_count, *re...  2.96 us
    convert_element_type x1, other arithmetic, local(): (features.astype(jnp.float32) / lengthscale[:, None]).astype(jnp.bfloat16)  0.93 us
    pallas_call x1, Pallas kernels, local(): pl.pallas_call(finish_kernel, out_shape=outs, compiler_params=VMEM)  0.77 us
  transfers between devices with their start and end apart: 12, of which 6 were waited for; matrix products, arithmetic and copies ran while one was open for 0% of the time, Pallas kernels for 0%

profile of v6, /device:TPU:0, one launch (start us, length us, event | category | flops | bytes accessed | tf_op | source)
XLA Modules:
  0.0 30.7 jit_solution(13792199791917295881)
XLA Ops:
  0.6 0.0 copy-start
  0.6 0.9 %divide_convert_fusion.scaled_ref.refs_0_ = bf16[128,256]{1,0:T(8,128)(2,1)S(1)} fusion(bf16[128,256]{1,0:T(8,128)(2,1)} %param.4, f32[128]{0:T(128)} %param.5), kind=kLoop, calls=%fused_computation | loop fusion | flops 98304 | bytes 131584 | tf_op jit(solution)/shard_map/convert_element_type | solution.py:145
  1.6 0.5 %collective-permute-start = (bf16[128,256]{1,0:T(8,128)(2,1)S(1)}, bf16[128,256]{1,0:T(8,128)(2,1)S(1)}, u32[]{:S(2)}, u32[]{:S(2)}) collective-permute-start(bf16[128,256]{1,0:T(8,128)(2,1)S(1)} %divide_convert_fusion.scaled_ref.refs_0_), channel_id=1, source_target_pairs={{1,0},{0,1},{3,2},{2,3},{5,4},{4,5},{7,6},{6,7},{9,8},{8,9},{11,10... | collective-permute-start | bytes 196616 | tf_op jit(solution)/shard_map/ppermute | solution.py:125
  2.1 0.0 copy-done
  2.1 0.0 copy-start.1
  2.1 4.7 %collective-permute-start.5 = (bf16[144,256]{1,0:T(8,128)(2,1)S(1)}, bf16[144,256]{1,0:T(8,128)(2,1)S(1)}, u32[]{:S(2)}, u32[]{:S(2)}) collective-permute-start(bf16[144,256]{1,0:T(8,128)(2,1)S(1)} %shard_map.67.refs_4_), channel_id=1, source_target_pairs={{12,0},{8,4},{4,8},{0,12},{13,1},{9,5},{5,9},{1,13},{14,2},{10,6},... | collective-permute-start | bytes 221192 | tf_op jit(solution)/shard_map/ppermute | solution.py:125
  6.8 0.0 collective-permute-start.4
  6.8 0.6 %collective-permute-start.3 = (bf16[144,256]{1,0:T(8,128)(2,1)S(1)}, bf16[144,256]{1,0:T(8,128)(2,1)S(1)}, u32[]{:S(2)}, u32[]{:S(2)}) collective-permute-start(bf16[144,256]{1,0:T(8,128)(2,1)S(1)} %shard_map.67.refs_4_), channel_id=1, source_target_pairs={{4,0},{0,4},{12,8},{8,12},{5,1},{1,5},{13,9},{9,13},{6,2},{2,6},{1... | collective-permute-start | bytes 221192 | tf_op jit(solution)/shard_map/ppermute | solution.py:125
  7.5 1.6 %collective-permute-start.1 = (bf16[128,256]{1,0:T(8,128)(2,1)S(1)}, bf16[128,256]{1,0:T(8,128)(2,1)S(1)}, u32[]{:S(2)}, u32[]{:S(2)}) collective-permute-start(bf16[128,256]{1,0:T(8,128)(2,1)S(1)} %divide_convert_fusion.scaled_ref.refs_0_), channel_id=1, source_target_pairs={{2,0},{0,2},{3,1},{1,3},{6,4},{4,6},{7,5},{5,7},{10,8},{8,10},{11,... | collective-permute-start | bytes 196616 | tf_op jit(solution)/shard_map/ppermute | solution.py:125
  9.1 0.0 collective-permute-done.refs_1_
  9.1 0.4 %collective-permute-start.2 = (bf16[128,256]{1,0:T(8,128)(2,1)S(1)}, bf16[128,256]{1,0:T(8,128)(2,1)S(1)}, u32[]{:S(2)}, u32[]{:S(2)}) collective-permute-start(bf16[128,256]{1,0:T(8,128)(2,1)S(1)} %collective-permute-done.refs_1_), channel_id=1, source_target_pairs={{2,0},{0,2},{3,1},{1,3},{6,4},{4,6},{7,5},{5,7},{10,8},{8,10},{11,... | collective-permute-start | bytes 196616 | tf_op jit(solution)/shard_map/ppermute | solution.py:125
  9.5 2.8 %collective-permute-done.1.refs_2_ = bf16[128,256]{1,0:T(8,128)(2,1)S(1)} collective-permute-done((bf16[128,256]{1,0:T(8,128)(2,1)S(1)}, bf16[128,256]{1,0:T(8,128)(2,1)S(1)}, u32[]{:S(2)}, u32[]{:S(2)}) %collective-permute-start.1) | collective-permute-done | bytes 65568 | tf_op jit(solution)/shard_map/ppermute | solution.py:125
  12.3 0.0 collective-permute-done.5.refs_7_
  12.3 1.4 %collective-permute-done.4.refs_6_ = bf16[144,256]{1,0:T(8,128)(2,1)S(1)} collective-permute-done((bf16[144,256]{1,0:T(8,128)(2,1)S(1)}, bf16[144,256]{1,0:T(8,128)(2,1)S(1)}, u32[]{:S(2)}, u32[]{:S(2)}) %collective-permute-start.4) | collective-permute-done | bytes 73760 | tf_op jit(solution)/shard_map/ppermute | solution.py:125
  13.6 0.0 collective-permute-done.3.refs_5_
  13.6 0.0 collective-permute-done.2.refs_3_
  13.6 0.0 copy-done.1
  13.6 3.0 %shard_map.68.refs_0_ = f32[5,16,256]{2,1,0:T(8,128)S(1)} custom-call(bf16[128,256]{1,0:T(8,128)(2,1)S(1)} %divide_convert_fusion.scaled_ref.refs_0_, bf16[128,256]{1,0:T(8,128)(2,1)S(1)} %collective-permute-done.refs_1_, bf16[128,256]{1,0:T(8,128)(2,1)S(1)} %collective-permute-done.1.refs_2_, bf16[128,256]{1,0:T(8,128)(2,1)S(1)} %collective-permute-done.2.refs_3_, ...), custom_call_target="tpu_custom_call" | custom-call | tf_op jit(solution)/shard_map/pallas_call | solution.py:153
  16.6 0.8 %collective-permute-start.8 = (f32[5,16,256]{2,1,0:T(8,128)S(1)}, f32[5,16,256]{2,1,0:T(8,128)S(1)}, u32[]{:S(2)}, u32[]{:S(2)}) collective-permute-start(f32[5,16,256]{2,1,0:T(8,128)S(1)} %shard_map.68.refs_0_), channel_id=1, source_target_pairs={{3,0},{2,1},{1,2},{0,3},{7,4},{6,5},{5,6},{4,7},{11,8},{10,9},{9,1... | collective-permute-start | bytes 245768 | tf_op jit(solution)/shard_map/ppermute | solution.py:125
  17.4 0.7 %collective-permute-start.7 = (f32[5,16,256]{2,1,0:T(8,128)S(1)}, f32[5,16,256]{2,1,0:T(8,128)S(1)}, u32[]{:S(2)}, u32[]{:S(2)}) collective-permute-start(f32[5,16,256]{2,1,0:T(8,128)S(1)} %shard_map.68.refs_0_), channel_id=1, source_target_pairs={{2,0},{3,1},{0,2},{1,3},{6,4},{7,5},{4,6},{5,7},{10,8},{11,9},{8,1... | collective-permute-start | bytes 245768 | tf_op jit(solution)/shard_map/ppermute | solution.py:125
  18.1 0.3 %collective-permute-start.6 = (f32[5,16,256]{2,1,0:T(8,128)S(1)}, f32[5,16,256]{2,1,0:T(8,128)S(1)}, u32[]{:S(2)}, u32[]{:S(2)}) collective-permute-start(f32[5,16,256]{2,1,0:T(8,128)S(1)} %shard_map.68.refs_0_), channel_id=1, source_target_pairs={{1,0},{0,1},{3,2},{2,3},{5,4},{4,5},{7,6},{6,7},{9,8},{8,9},{11,10... | collective-permute-start | bytes 245768 | tf_op jit(solution)/shard_map/ppermute | solution.py:125
  18.5 2.8 %collective-permute-done.8.refs_3_ = f32[5,16,256]{2,1,0:T(8,128)S(1)} collective-permute-done((f32[5,16,256]{2,1,0:T(8,128)S(1)}, f32[5,16,256]{2,1,0:T(8,128)S(1)}, u32[]{:S(2)}, u32[]{:S(2)}) %collective-permute-start.8) | collective-permute-done | bytes 81952 | tf_op jit(solution)/shard_map/ppermute | solution.py:125
  21.3 1.8 %collective-permute-done.7.refs_2_ = f32[5,16,256]{2,1,0:T(8,128)S(1)} collective-permute-done((f32[5,16,256]{2,1,0:T(8,128)S(1)}, f32[5,16,256]{2,1,0:T(8,128)S(1)}, u32[]{:S(2)}, u32[]{:S(2)}) %collective-permute-start.7) | collective-permute-done | bytes 81952 | tf_op jit(solution)/shard_map/ppermute | solution.py:125
  23.1 0.0 collective-permute-done.6.refs_1_
  23.1 0.1 shard_map.69
  23.2 2.1 %collective-permute-start.11 = (f32[16,128]{1,0:T(8,128)S(1)}, f32[16,128]{1,0:T(8,128)S(1)}, u32[]{:S(2)}, u32[]{:S(2)}) collective-permute-start(f32[16,128]{1,0:T(8,128)S(1)} %get-tuple-element.6.refs_0_), channel_id=1, source_target_pairs={{12,0},{8,4},{4,8},{0,12},{13,1},{9,5},{5,9},{1,13},{14,2},{10,6},... | collective-permute-start | bytes 24584 | tf_op jit(solution)/shard_map/ppermute | solution.py:125
  25.4 0.4 %collective-permute-start.10 = (f32[16,128]{1,0:T(8,128)S(1)}, f32[16,128]{1,0:T(8,128)S(1)}, u32[]{:S(2)}, u32[]{:S(2)}) collective-permute-start(f32[16,128]{1,0:T(8,128)S(1)} %get-tuple-element.6.refs_0_), channel_id=1, source_target_pairs={{8,0},{12,4},{0,8},{4,12},{9,1},{13,5},{1,9},{5,13},{10,2},{14,6},... | collective-permute-start | bytes 24584 | tf_op jit(solution)/shard_map/ppermute | solution.py:125
  25.7 1.9 %collective-permute-start.9 = (f32[16,128]{1,0:T(8,128)S(1)}, f32[16,128]{1,0:T(8,128)S(1)}, u32[]{:S(2)}, u32[]{:S(2)}) collective-permute-start(f32[16,128]{1,0:T(8,128)S(1)} %get-tuple-element.6.refs_0_), channel_id=1, source_target_pairs={{4,0},{0,4},{12,8},{8,12},{5,1},{1,5},{13,9},{9,13},{6,2},{2,6},{1... | collective-permute-start | bytes 24584 | tf_op jit(solution)/shard_map/ppermute | solution.py:125
  27.6 1.1 %collective-permute-done.11.refs_3_ = f32[16,128]{1,0:T(8,128)S(1)} collective-permute-done((f32[16,128]{1,0:T(8,128)S(1)}, f32[16,128]{1,0:T(8,128)S(1)}, u32[]{:S(2)}, u32[]{:S(2)}) %collective-permute-start.11) | collective-permute-done | bytes 8224 | tf_op jit(solution)/shard_map/ppermute | solution.py:125
  28.7 1.2 %collective-permute-done.10.refs_2_ = f32[16,128]{1,0:T(8,128)S(1)} collective-permute-done((f32[16,128]{1,0:T(8,128)S(1)}, f32[16,128]{1,0:T(8,128)S(1)}, u32[]{:S(2)}, u32[]{:S(2)}) %collective-permute-start.10) | collective-permute-done | bytes 8224 | tf_op jit(solution)/shard_map/ppermute | solution.py:125
  29.9 0.0 collective-permute-done.9.refs_1_
  29.9 0.8 %shard_map.70 = (f32[16,256]{1,0:T(8,128)}, f32[16,256]{1,0:T(8,128)}, f32[16,256]{1,0:T(8,128)}) custom-call(f32[16,256]{1,0:T(8,128)S(1)} %get-tuple-element.5.image_ref, f32[16,256]{1,0:T(8,128)S(1)} %copy-done, f32[16,128]{1,0:T(8,128)S(1)} %get-tuple-element.6.refs_0_, f32[16,128]{1,0:T(8,128)S(1)} %collective-permute-done.9.refs_1_, ...), custom_call_target="tpu_custom_call" | custom-call | tf_op jit(solution)/shard_map/pallas_call | solution.py:167
  (1 shorter events, 0.0 us)
Async XLA Ops:
  0.6 1.5 %copy-start = (f32[16,256]{1,0:T(8,128)S(1)}, f32[16,256]{1,0:T(8,128)}, u32[]{:S(2)}) copy-start(f32[16,256]{1,0:T(8,128)} %probes_ref.3) | copy-start | bytes 49156
  1.6 7.5 %collective-permute-start = (bf16[128,256]{1,0:T(8,128)(2,1)S(1)}, bf16[128,256]{1,0:T(8,128)(2,1)S(1)}, u32[]{:S(2)}, u32[]{:S(2)}) collective-permute-start(bf16[128,256]{1,0:T(8,128)(2,1)S(1)} %divide_convert_fusion.scaled_ref.refs_0_), channel_id=1, source_target_pairs={{1,0},{0,1},{3,2},{2,3},{5,4},{4,5},{7,6},{6,7},{9,8},{8,9},{11,10... | collective-permute-start | bytes 196616 | tf_op jit(solution)/shard_map/ppermute | solution.py:125
  2.1 11.5 %copy-start.1 = (f32[256]{0:T(256)S(1)}, f32[256]{0:T(256)}, u32[]{:S(2)}) copy-start(f32[256]{0:T(256)} %param.6) | copy-start | bytes 3076
  2.1 10.1 %collective-permute-start.5 = (bf16[144,256]{1,0:T(8,128)(2,1)S(1)}, bf16[144,256]{1,0:T(8,128)(2,1)S(1)}, u32[]{:S(2)}, u32[]{:S(2)}) collective-permute-start(bf16[144,256]{1,0:T(8,128)(2,1)S(1)} %shard_map.67.refs_4_), channel_id=1, source_target_pairs={{12,0},{8,4},{4,8},{0,12},{13,1},{9,5},{5,9},{1,13},{14,2},{10,6},... | collective-permute-start | bytes 221192 | tf_op jit(solution)/shard_map/ppermute | solution.py:125
  6.8 6.8 %collective-permute-start.4 = (bf16[144,256]{1,0:T(8,128)(2,1)S(1)}, bf16[144,256]{1,0:T(8,128)(2,1)S(1)}, u32[]{:S(2)}, u32[]{:S(2)}) collective-permute-start(bf16[144,256]{1,0:T(8,128)(2,1)S(1)} %shard_map.67.refs_4_), channel_id=1, source_target_pairs={{8,0},{12,4},{0,8},{4,12},{9,1},{13,5},{1,9},{5,13},{10,2},{14,6},... | collective-permute-start | bytes 221192 | tf_op jit(solution)/shard_map/ppermute | solution.py:125
  6.8 6.8 %collective-permute-start.3 = (bf16[144,256]{1,0:T(8,128)(2,1)S(1)}, bf16[144,256]{1,0:T(8,128)(2,1)S(1)}, u32[]{:S(2)}, u32[]{:S(2)}) collective-permute-start(bf16[144,256]{1,0:T(8,128)(2,1)S(1)} %shard_map.67.refs_4_), channel_id=1, source_target_pairs={{4,0},{0,4},{12,8},{8,12},{5,1},{1,5},{13,9},{9,13},{6,2},{2,6},{1... | collective-permute-start | bytes 221192 | tf_op jit(solution)/shard_map/ppermute | solution.py:125
  7.5 4.8 %collective-permute-start.1 = (bf16[128,256]{1,0:T(8,128)(2,1)S(1)}, bf16[128,256]{1,0:T(8,128)(2,1)S(1)}, u32[]{:S(2)}, u32[]{:S(2)}) collective-permute-start(bf16[128,256]{1,0:T(8,128)(2,1)S(1)} %divide_convert_fusion.scaled_ref.refs_0_), channel_id=1, source_target_pairs={{2,0},{0,2},{3,1},{1,3},{6,4},{4,6},{7,5},{5,7},{10,8},{8,10},{11,... | collective-permute-start | bytes 196616 | tf_op jit(solution)/shard_map/ppermute | solution.py:125
  9.1 4.5 %collective-permute-start.2 = (bf16[128,256]{1,0:T(8,128)(2,1)S(1)}, bf16[128,256]{1,0:T(8,128)(2,1)S(1)}, u32[]{:S(2)}, u32[]{:S(2)}) collective-permute-start(bf16[128,256]{1,0:T(8,128)(2,1)S(1)} %collective-permute-done.refs_1_), channel_id=1, source_target_pairs={{2,0},{0,2},{3,1},{1,3},{6,4},{4,6},{7,5},{5,7},{10,8},{8,10},{11,... | collective-permute-start | bytes 196616 | tf_op jit(solution)/shard_map/ppermute | solution.py:125
  16.6 4.7 %collective-permute-start.8 = (f32[5,16,256]{2,1,0:T(8,128)S(1)}, f32[5,16,256]{2,1,0:T(8,128)S(1)}, u32[]{:S(2)}, u32[]{:S(2)}) collective-permute-start(f32[5,16,256]{2,1,0:T(8,128)S(1)} %shard_map.68.refs_0_), channel_id=1, source_target_pairs={{3,0},{2,1},{1,2},{0,3},{7,4},{6,5},{5,6},{4,7},{11,8},{10,9},{9,1... | collective-permute-start | bytes 245768 | tf_op jit(solution)/shard_map/ppermute | solution.py:125
  17.4 5.7 %collective-permute-start.7 = (f32[5,16,256]{2,1,0:T(8,128)S(1)}, f32[5,16,256]{2,1,0:T(8,128)S(1)}, u32[]{:S(2)}, u32[]{:S(2)}) collective-permute-start(f32[5,16,256]{2,1,0:T(8,128)S(1)} %shard_map.68.refs_0_), channel_id=1, source_target_pairs={{2,0},{3,1},{0,2},{1,3},{6,4},{7,5},{4,6},{5,7},{10,8},{11,9},{8,1... | collective-permute-start | bytes 245768 | tf_op jit(solution)/shard_map/ppermute | solution.py:125
  18.1 5.0 %collective-permute-start.6 = (f32[5,16,256]{2,1,0:T(8,128)S(1)}, f32[5,16,256]{2,1,0:T(8,128)S(1)}, u32[]{:S(2)}, u32[]{:S(2)}) collective-permute-start(f32[5,16,256]{2,1,0:T(8,128)S(1)} %shard_map.68.refs_0_), channel_id=1, source_target_pairs={{1,0},{0,1},{3,2},{2,3},{5,4},{4,5},{7,6},{6,7},{9,8},{8,9},{11,10... | collective-permute-start | bytes 245768 | tf_op jit(solution)/shard_map/ppermute | solution.py:125
  23.2 5.5 %collective-permute-start.11 = (f32[16,128]{1,0:T(8,128)S(1)}, f32[16,128]{1,0:T(8,128)S(1)}, u32[]{:S(2)}, u32[]{:S(2)}) collective-permute-start(f32[16,128]{1,0:T(8,128)S(1)} %get-tuple-element.6.refs_0_), channel_id=1, source_target_pairs={{12,0},{8,4},{4,8},{0,12},{13,1},{9,5},{5,9},{1,13},{14,2},{10,6},... | collective-permute-start | bytes 24584 | tf_op jit(solution)/shard_map/ppermute | solution.py:125
  25.4 4.5 %collective-permute-start.10 = (f32[16,128]{1,0:T(8,128)S(1)}, f32[16,128]{1,0:T(8,128)S(1)}, u32[]{:S(2)}, u32[]{:S(2)}) collective-permute-start(f32[16,128]{1,0:T(8,128)S(1)} %get-tuple-element.6.refs_0_), channel_id=1, source_target_pairs={{8,0},{12,4},{0,8},{4,12},{9,1},{13,5},{1,9},{5,13},{10,2},{14,6},... | collective-permute-start | bytes 24584 | tf_op jit(solution)/shard_map/ppermute | solution.py:125
  25.7 4.2 %collective-permute-start.9 = (f32[16,128]{1,0:T(8,128)S(1)}, f32[16,128]{1,0:T(8,128)S(1)}, u32[]{:S(2)}, u32[]{:S(2)}) collective-permute-start(f32[16,128]{1,0:T(8,128)S(1)} %get-tuple-element.6.refs_0_), channel_id=1, source_target_pairs={{4,0},{0,4},{12,8},{8,12},{5,1},{1,5},{13,9},{9,13},{6,2},{2,6},{1... | collective-permute-start | bytes 24584 | tf_op jit(solution)/shard_map/ppermute | solution.py:125

commit v7 on v6

--- a/solution.py
+++ b/solution.py
@@ -43,11 +43,14 @@
     noise_ref, probes_ref, partial_ref = refs[-3:]
     rows = [jnp.concatenate([ref[...], norm_rows(ref[...], 1)], axis=0) for ref in plane_refs]
 
-    def add_block(block_ref, totals):
-        scaled = block_ref[:feature_count, :]
-        columns = jnp.concatenate([scaled, norm_rows(scaled, 0)], axis=0)
-        columns = columns.astype(jnp.float32).T.astype(jnp.bfloat16)
-        probes = block_ref[feature_count:, :]
+    def add_blocks(blocks, totals):
+        columns = []
+        for block in blocks:
+            scaled = block[:feature_count, :]
+            block_columns = jnp.concatenate([scaled, norm_rows(scaled, 0)], axis=0)
+            columns.append(block_columns.astype(jnp.float32).T.astype(jnp.bfloat16))
+        columns = jnp.concatenate(columns, axis=0)
+        probes = jnp.concatenate([block[feature_count:, :] for block in blocks], axis=1)
         result = []
         for own, total in zip(rows, totals):
             exponent = jnp.dot(columns, own, preferred_element_type=jnp.float32)
@@ -57,13 +60,15 @@
 
     totals = [noise_ref[...] * probes_ref[...]]
     totals += [jnp.zeros(probes_ref.shape, jnp.float32)] * (plane_count - 1)
-    for ref in line_refs:
-        if len(ref.shape) == 2:
-            totals = add_block(ref, totals)
-        else:
-            totals = lax.fori_loop(
-                0, ref.shape[0], lambda number, value: add_block(ref.at[number], value), totals
-            )
+    if len(line_refs[0].shape) == 2:
+        totals = add_blocks([ref[...] for ref in line_refs], totals)
+    else:
+        totals = lax.fori_loop(
+            0,
+            line_refs[0].shape[0],
+            lambda number, value: add_blocks([line_refs[0][number]], value),
+            totals,
+        )
     for number, total in enumerate(totals):
         partial_ref[number] = total
     partial_ref[plane_count] = probes_ref[...]

time: 30.8 us -> 29.8 us (0.968)
  Pallas kernels: 3.84 us -> 2.78 us
    pallas_call x1, Pallas kernels: 2.96 us -> 1.9 us  [local(): pl.pallas_call(lambda *refs: image_kernel(feature_count, plane_count, *re...]
where the time goes in v7:
time: 29.8 us; the launch traced here: 29.6 us
  starting transfers between devices  14.1 us (47%)
  waiting for transfers between devices  11.1 us (37%)
  Pallas kernels  2.78 us (9%)
  other arithmetic  0.93 us (3%)
  between operations  0.68 us (2%)
    ppermute x12, starting transfers between devices, everywhere(): lax.ppermute(value, axes, [(source_of(i, step, count), i) for i in range(...  14.1 us
    ppermute x12, waiting for transfers between devices, everywhere(): lax.ppermute(value, axes, [(source_of(i, step, count), i) for i in range(...  11.1 us
    pallas_call x1, Pallas kernels, local(): pl.pallas_call(lambda *refs: image_kernel(feature_count, plane_count, *re...  1.9 us
    convert_element_type x1, other arithmetic, local(): (features.astype(jnp.float32) / lengthscale[:, None]).astype(jnp.bfloat16)  0.93 us
    pallas_call x1, Pallas kernels, local(): pl.pallas_call(finish_kernel, out_shape=outs, compiler_params=VMEM)  0.77 us
  transfers between devices with their start and end apart: 12, of which 6 were waited for; matrix products, arithmetic and copies ran while one was open for 0% of the time, Pallas kernels for 0%

profile of v7, /device:TPU:0, one launch (start us, length us, event | category | flops | bytes accessed | tf_op | source)
XLA Modules:
  0.0 29.6 jit_solution(3856383073509606600)
XLA Ops:
  0.6 0.0 copy-start
  0.6 0.9 %divide_convert_fusion.scaled_ref.refs_0_ = bf16[128,256]{1,0:T(8,128)(2,1)S(1)} fusion(bf16[128,256]{1,0:T(8,128)(2,1)} %param.4, f32[128]{0:T(128)} %param.5), kind=kLoop, calls=%fused_computation | loop fusion | flops 98304 | bytes 131584 | tf_op jit(solution)/shard_map/convert_element_type | solution.py:150
  1.6 0.5 %collective-permute-start = (bf16[128,256]{1,0:T(8,128)(2,1)S(1)}, bf16[128,256]{1,0:T(8,128)(2,1)S(1)}, u32[]{:S(2)}, u32[]{:S(2)}) collective-permute-start(bf16[128,256]{1,0:T(8,128)(2,1)S(1)} %divide_convert_fusion.scaled_ref.refs_0_), channel_id=1, source_target_pairs={{1,0},{0,1},{3,2},{2,3},{5,4},{4,5},{7,6},{6,7},{9,8},{8,9},{11,10... | collective-permute-start | bytes 196616 | tf_op jit(solution)/shard_map/ppermute | solution.py:130
  2.1 0.0 copy-done
  2.1 0.0 copy-start.1
  2.1 4.7 %collective-permute-start.5 = (bf16[144,256]{1,0:T(8,128)(2,1)S(1)}, bf16[144,256]{1,0:T(8,128)(2,1)S(1)}, u32[]{:S(2)}, u32[]{:S(2)}) collective-permute-start(bf16[144,256]{1,0:T(8,128)(2,1)S(1)} %shard_map.67.refs_4_), channel_id=1, source_target_pairs={{12,0},{8,4},{4,8},{0,12},{13,1},{9,5},{5,9},{1,13},{14,2},{10,6},... | collective-permute-start | bytes 221192 | tf_op jit(solution)/shard_map/ppermute | solution.py:130
  6.8 0.0 collective-permute-start.4
  6.8 0.6 %collective-permute-start.3 = (bf16[144,256]{1,0:T(8,128)(2,1)S(1)}, bf16[144,256]{1,0:T(8,128)(2,1)S(1)}, u32[]{:S(2)}, u32[]{:S(2)}) collective-permute-start(bf16[144,256]{1,0:T(8,128)(2,1)S(1)} %shard_map.67.refs_4_), channel_id=1, source_target_pairs={{4,0},{0,4},{12,8},{8,12},{5,1},{1,5},{13,9},{9,13},{6,2},{2,6},{1... | collective-permute-start | bytes 221192 | tf_op jit(solution)/shard_map/ppermute | solution.py:130
  7.5 1.6 %collective-permute-start.1 = (bf16[128,256]{1,0:T(8,128)(2,1)S(1)}, bf16[128,256]{1,0:T(8,128)(2,1)S(1)}, u32[]{:S(2)}, u32[]{:S(2)}) collective-permute-start(bf16[128,256]{1,0:T(8,128)(2,1)S(1)} %divide_convert_fusion.scaled_ref.refs_0_), channel_id=1, source_target_pairs={{2,0},{0,2},{3,1},{1,3},{6,4},{4,6},{7,5},{5,7},{10,8},{8,10},{11,... | collective-permute-start | bytes 196616 | tf_op jit(solution)/shard_map/ppermute | solution.py:130
  9.1 0.0 collective-permute-done.refs_1_
  9.1 0.4 %collective-permute-start.2 = (bf16[128,256]{1,0:T(8,128)(2,1)S(1)}, bf16[128,256]{1,0:T(8,128)(2,1)S(1)}, u32[]{:S(2)}, u32[]{:S(2)}) collective-permute-start(bf16[128,256]{1,0:T(8,128)(2,1)S(1)} %collective-permute-done.refs_1_), channel_id=1, source_target_pairs={{2,0},{0,2},{3,1},{1,3},{6,4},{4,6},{7,5},{5,7},{10,8},{8,10},{11,... | collective-permute-start | bytes 196616 | tf_op jit(solution)/shard_map/ppermute | solution.py:130
  9.5 2.8 %collective-permute-done.1.refs_2_ = bf16[128,256]{1,0:T(8,128)(2,1)S(1)} collective-permute-done((bf16[128,256]{1,0:T(8,128)(2,1)S(1)}, bf16[128,256]{1,0:T(8,128)(2,1)S(1)}, u32[]{:S(2)}, u32[]{:S(2)}) %collective-permute-start.1) | collective-permute-done | bytes 65568 | tf_op jit(solution)/shard_map/ppermute | solution.py:130
  12.3 0.0 collective-permute-done.5.refs_7_
  12.3 1.4 %collective-permute-done.4.refs_6_ = bf16[144,256]{1,0:T(8,128)(2,1)S(1)} collective-permute-done((bf16[144,256]{1,0:T(8,128)(2,1)S(1)}, bf16[144,256]{1,0:T(8,128)(2,1)S(1)}, u32[]{:S(2)}, u32[]{:S(2)}) %collective-permute-start.4) | collective-permute-done | bytes 73760 | tf_op jit(solution)/shard_map/ppermute | solution.py:130
  13.6 0.0 collective-permute-done.3.refs_5_
  13.6 0.0 collective-permute-done.2.refs_3_
  13.6 0.0 copy-done.1
  13.6 1.9 %shard_map.68.refs_0_ = f32[5,16,256]{2,1,0:T(8,128)S(1)} custom-call(bf16[128,256]{1,0:T(8,128)(2,1)S(1)} %divide_convert_fusion.scaled_ref.refs_0_, bf16[128,256]{1,0:T(8,128)(2,1)S(1)} %collective-permute-done.refs_1_, bf16[128,256]{1,0:T(8,128)(2,1)S(1)} %collective-permute-done.1.refs_2_, bf16[128,256]{1,0:T(8,128)(2,1)S(1)} %collective-permute-done.2.refs_3_, ...), custom_call_target="tpu_custom_call" | custom-call | tf_op jit(solution)/shard_map/pallas_call | solution.py:158
  15.5 0.8 %collective-permute-start.8 = (f32[5,16,256]{2,1,0:T(8,128)S(1)}, f32[5,16,256]{2,1,0:T(8,128)S(1)}, u32[]{:S(2)}, u32[]{:S(2)}) collective-permute-start(f32[5,16,256]{2,1,0:T(8,128)S(1)} %shard_map.68.refs_0_), channel_id=1, source_target_pairs={{3,0},{2,1},{1,2},{0,3},{7,4},{6,5},{5,6},{4,7},{11,8},{10,9},{9,1... | collective-permute-start | bytes 245768 | tf_op jit(solution)/shard_map/ppermute | solution.py:130
  16.3 0.7 %collective-permute-start.7 = (f32[5,16,256]{2,1,0:T(8,128)S(1)}, f32[5,16,256]{2,1,0:T(8,128)S(1)}, u32[]{:S(2)}, u32[]{:S(2)}) collective-permute-start(f32[5,16,256]{2,1,0:T(8,128)S(1)} %shard_map.68.refs_0_), channel_id=1, source_target_pairs={{2,0},{3,1},{0,2},{1,3},{6,4},{7,5},{4,6},{5,7},{10,8},{11,9},{8,1... | collective-permute-start | bytes 245768 | tf_op jit(solution)/shard_map/ppermute | solution.py:130
  17.1 0.3 %collective-permute-start.6 = (f32[5,16,256]{2,1,0:T(8,128)S(1)}, f32[5,16,256]{2,1,0:T(8,128)S(1)}, u32[]{:S(2)}, u32[]{:S(2)}) collective-permute-start(f32[5,16,256]{2,1,0:T(8,128)S(1)} %shard_map.68.refs_0_), channel_id=1, source_target_pairs={{1,0},{0,1},{3,2},{2,3},{5,4},{4,5},{7,6},{6,7},{9,8},{8,9},{11,10... | collective-permute-start | bytes 245768 | tf_op jit(solution)/shard_map/ppermute | solution.py:130
  17.4 2.8 %collective-permute-done.8.refs_3_ = f32[5,16,256]{2,1,0:T(8,128)S(1)} collective-permute-done((f32[5,16,256]{2,1,0:T(8,128)S(1)}, f32[5,16,256]{2,1,0:T(8,128)S(1)}, u32[]{:S(2)}, u32[]{:S(2)}) %collective-permute-start.8) | collective-permute-done | bytes 81952 | tf_op jit(solution)/shard_map/ppermute | solution.py:130
  20.2 1.8 %collective-permute-done.7.refs_2_ = f32[5,16,256]{2,1,0:T(8,128)S(1)} collective-permute-done((f32[5,16,256]{2,1,0:T(8,128)S(1)}, f32[5,16,256]{2,1,0:T(8,128)S(1)}, u32[]{:S(2)}, u32[]{:S(2)}) %collective-permute-start.7) | collective-permute-done | bytes 81952 | tf_op jit(solution)/shard_map/ppermute | solution.py:130
  22.0 0.0 collective-permute-done.6.refs_1_
  22.0 0.1 shard_map.69
  22.2 2.1 %collective-permute-start.11 = (f32[16,128]{1,0:T(8,128)S(1)}, f32[16,128]{1,0:T(8,128)S(1)}, u32[]{:S(2)}, u32[]{:S(2)}) collective-permute-start(f32[16,128]{1,0:T(8,128)S(1)} %get-tuple-element.6.refs_0_), channel_id=1, source_target_pairs={{12,0},{8,4},{4,8},{0,12},{13,1},{9,5},{5,9},{1,13},{14,2},{10,6},... | collective-permute-start | bytes 24584 | tf_op jit(solution)/shard_map/ppermute | solution.py:130
  24.3 0.4 %collective-permute-start.10 = (f32[16,128]{1,0:T(8,128)S(1)}, f32[16,128]{1,0:T(8,128)S(1)}, u32[]{:S(2)}, u32[]{:S(2)}) collective-permute-start(f32[16,128]{1,0:T(8,128)S(1)} %get-tuple-element.6.refs_0_), channel_id=1, source_target_pairs={{8,0},{12,4},{0,8},{4,12},{9,1},{13,5},{1,9},{5,13},{10,2},{14,6},... | collective-permute-start | bytes 24584 | tf_op jit(solution)/shard_map/ppermute | solution.py:130
  24.7 1.9 %collective-permute-start.9 = (f32[16,128]{1,0:T(8,128)S(1)}, f32[16,128]{1,0:T(8,128)S(1)}, u32[]{:S(2)}, u32[]{:S(2)}) collective-permute-start(f32[16,128]{1,0:T(8,128)S(1)} %get-tuple-element.6.refs_0_), channel_id=1, source_target_pairs={{4,0},{0,4},{12,8},{8,12},{5,1},{1,5},{13,9},{9,13},{6,2},{2,6},{1... | collective-permute-start | bytes 24584 | tf_op jit(solution)/shard_map/ppermute | solution.py:130
  26.5 1.1 %collective-permute-done.11.refs_3_ = f32[16,128]{1,0:T(8,128)S(1)} collective-permute-done((f32[16,128]{1,0:T(8,128)S(1)}, f32[16,128]{1,0:T(8,128)S(1)}, u32[]{:S(2)}, u32[]{:S(2)}) %collective-permute-start.11) | collective-permute-done | bytes 8224 | tf_op jit(solution)/shard_map/ppermute | solution.py:130
  27.6 1.2 %collective-permute-done.10.refs_2_ = f32[16,128]{1,0:T(8,128)S(1)} collective-permute-done((f32[16,128]{1,0:T(8,128)S(1)}, f32[16,128]{1,0:T(8,128)S(1)}, u32[]{:S(2)}, u32[]{:S(2)}) %collective-permute-start.10) | collective-permute-done | bytes 8224 | tf_op jit(solution)/shard_map/ppermute | solution.py:130
  28.8 0.0 collective-permute-done.9.refs_1_
  28.8 0.8 %shard_map.70 = (f32[16,256]{1,0:T(8,128)}, f32[16,256]{1,0:T(8,128)}, f32[16,256]{1,0:T(8,128)}) custom-call(f32[16,256]{1,0:T(8,128)S(1)} %get-tuple-element.5.image_ref, f32[16,256]{1,0:T(8,128)S(1)} %copy-done, f32[16,128]{1,0:T(8,128)S(1)} %get-tuple-element.6.refs_0_, f32[16,128]{1,0:T(8,128)S(1)} %collective-permute-done.9.refs_1_, ...), custom_call_target="tpu_custom_call" | custom-call | tf_op jit(solution)/shard_map/pallas_call | solution.py:172
  (1 shorter events, 0.0 us)
Async XLA Ops:
  0.6 1.5 %copy-start = (f32[16,256]{1,0:T(8,128)S(1)}, f32[16,256]{1,0:T(8,128)}, u32[]{:S(2)}) copy-start(f32[16,256]{1,0:T(8,128)} %probes_ref.3) | copy-start | bytes 49156
  1.6 7.5 %collective-permute-start = (bf16[128,256]{1,0:T(8,128)(2,1)S(1)}, bf16[128,256]{1,0:T(8,128)(2,1)S(1)}, u32[]{:S(2)}, u32[]{:S(2)}) collective-permute-start(bf16[128,256]{1,0:T(8,128)(2,1)S(1)} %divide_convert_fusion.scaled_ref.refs_0_), channel_id=1, source_target_pairs={{1,0},{0,1},{3,2},{2,3},{5,4},{4,5},{7,6},{6,7},{9,8},{8,9},{11,10... | collective-permute-start | bytes 196616 | tf_op jit(solution)/shard_map/ppermute | solution.py:130
  2.1 11.5 %copy-start.1 = (f32[256]{0:T(256)S(1)}, f32[256]{0:T(256)}, u32[]{:S(2)}) copy-start(f32[256]{0:T(256)} %param.6) | copy-start | bytes 3076
  2.1 10.1 %collective-permute-start.5 = (bf16[144,256]{1,0:T(8,128)(2,1)S(1)}, bf16[144,256]{1,0:T(8,128)(2,1)S(1)}, u32[]{:S(2)}, u32[]{:S(2)}) collective-permute-start(bf16[144,256]{1,0:T(8,128)(2,1)S(1)} %shard_map.67.refs_4_), channel_id=1, source_target_pairs={{12,0},{8,4},{4,8},{0,12},{13,1},{9,5},{5,9},{1,13},{14,2},{10,6},... | collective-permute-start | bytes 221192 | tf_op jit(solution)/shard_map/ppermute | solution.py:130
  6.8 6.8 %collective-permute-start.4 = (bf16[144,256]{1,0:T(8,128)(2,1)S(1)}, bf16[144,256]{1,0:T(8,128)(2,1)S(1)}, u32[]{:S(2)}, u32[]{:S(2)}) collective-permute-start(bf16[144,256]{1,0:T(8,128)(2,1)S(1)} %shard_map.67.refs_4_), channel_id=1, source_target_pairs={{8,0},{12,4},{0,8},{4,12},{9,1},{13,5},{1,9},{5,13},{10,2},{14,6},... | collective-permute-start | bytes 221192 | tf_op jit(solution)/shard_map/ppermute | solution.py:130
  6.8 6.8 %collective-permute-start.3 = (bf16[144,256]{1,0:T(8,128)(2,1)S(1)}, bf16[144,256]{1,0:T(8,128)(2,1)S(1)}, u32[]{:S(2)}, u32[]{:S(2)}) collective-permute-start(bf16[144,256]{1,0:T(8,128)(2,1)S(1)} %shard_map.67.refs_4_), channel_id=1, source_target_pairs={{4,0},{0,4},{12,8},{8,12},{5,1},{1,5},{13,9},{9,13},{6,2},{2,6},{1... | collective-permute-start | bytes 221192 | tf_op jit(solution)/shard_map/ppermute | solution.py:130
  7.5 4.8 %collective-permute-start.1 = (bf16[128,256]{1,0:T(8,128)(2,1)S(1)}, bf16[128,256]{1,0:T(8,128)(2,1)S(1)}, u32[]{:S(2)}, u32[]{:S(2)}) collective-permute-start(bf16[128,256]{1,0:T(8,128)(2,1)S(1)} %divide_convert_fusion.scaled_ref.refs_0_), channel_id=1, source_target_pairs={{2,0},{0,2},{3,1},{1,3},{6,4},{4,6},{7,5},{5,7},{10,8},{8,10},{11,... | collective-permute-start | bytes 196616 | tf_op jit(solution)/shard_map/ppermute | solution.py:130
  9.1 4.5 %collective-permute-start.2 = (bf16[128,256]{1,0:T(8,128)(2,1)S(1)}, bf16[128,256]{1,0:T(8,128)(2,1)S(1)}, u32[]{:S(2)}, u32[]{:S(2)}) collective-permute-start(bf16[128,256]{1,0:T(8,128)(2,1)S(1)} %collective-permute-done.refs_1_), channel_id=1, source_target_pairs={{2,0},{0,2},{3,1},{1,3},{6,4},{4,6},{7,5},{5,7},{10,8},{8,10},{11,... | collective-permute-start | bytes 196616 | tf_op jit(solution)/shard_map/ppermute | solution.py:130
  15.5 4.7 %collective-permute-start.8 = (f32[5,16,256]{2,1,0:T(8,128)S(1)}, f32[5,16,256]{2,1,0:T(8,128)S(1)}, u32[]{:S(2)}, u32[]{:S(2)}) collective-permute-start(f32[5,16,256]{2,1,0:T(8,128)S(1)} %shard_map.68.refs_0_), channel_id=1, source_target_pairs={{3,0},{2,1},{1,2},{0,3},{7,4},{6,5},{5,6},{4,7},{11,8},{10,9},{9,1... | collective-permute-start | bytes 245768 | tf_op jit(solution)/shard_map/ppermute | solution.py:130
  16.3 5.7 %collective-permute-start.7 = (f32[5,16,256]{2,1,0:T(8,128)S(1)}, f32[5,16,256]{2,1,0:T(8,128)S(1)}, u32[]{:S(2)}, u32[]{:S(2)}) collective-permute-start(f32[5,16,256]{2,1,0:T(8,128)S(1)} %shard_map.68.refs_0_), channel_id=1, source_target_pairs={{2,0},{3,1},{0,2},{1,3},{6,4},{7,5},{4,6},{5,7},{10,8},{11,9},{8,1... | collective-permute-start | bytes 245768 | tf_op jit(solution)/shard_map/ppermute | solution.py:130
  17.1 5.0 %collective-permute-start.6 = (f32[5,16,256]{2,1,0:T(8,128)S(1)}, f32[5,16,256]{2,1,0:T(8,128)S(1)}, u32[]{:S(2)}, u32[]{:S(2)}) collective-permute-start(f32[5,16,256]{2,1,0:T(8,128)S(1)} %shard_map.68.refs_0_), channel_id=1, source_target_pairs={{1,0},{0,1},{3,2},{2,3},{5,4},{4,5},{7,6},{6,7},{9,8},{8,9},{11,10... | collective-permute-start | bytes 245768 | tf_op jit(solution)/shard_map/ppermute | solution.py:130
  22.2 5.5 %collective-permute-start.11 = (f32[16,128]{1,0:T(8,128)S(1)}, f32[16,128]{1,0:T(8,128)S(1)}, u32[]{:S(2)}, u32[]{:S(2)}) collective-permute-start(f32[16,128]{1,0:T(8,128)S(1)} %get-tuple-element.6.refs_0_), channel_id=1, source_target_pairs={{12,0},{8,4},{4,8},{0,12},{13,1},{9,5},{5,9},{1,13},{14,2},{10,6},... | collective-permute-start | bytes 24584 | tf_op jit(solution)/shard_map/ppermute | solution.py:130
  24.3 4.5 %collective-permute-start.10 = (f32[16,128]{1,0:T(8,128)S(1)}, f32[16,128]{1,0:T(8,128)S(1)}, u32[]{:S(2)}, u32[]{:S(2)}) collective-permute-start(f32[16,128]{1,0:T(8,128)S(1)} %get-tuple-element.6.refs_0_), channel_id=1, source_target_pairs={{8,0},{12,4},{0,8},{4,12},{9,1},{13,5},{1,9},{5,13},{10,2},{14,6},... | collective-permute-start | bytes 24584 | tf_op jit(solution)/shard_map/ppermute | solution.py:130
  24.7 4.2 %collective-permute-start.9 = (f32[16,128]{1,0:T(8,128)S(1)}, f32[16,128]{1,0:T(8,128)S(1)}, u32[]{:S(2)}, u32[]{:S(2)}) collective-permute-start(f32[16,128]{1,0:T(8,128)S(1)} %get-tuple-element.6.refs_0_), channel_id=1, source_target_pairs={{4,0},{0,4},{12,8},{8,12},{5,1},{1,5},{13,9},{9,13},{6,2},{2,6},{1... | collective-permute-start | bytes 24584 | tf_op jit(solution)/shard_map/ppermute | solution.py:130

commit v8 on v7

--- a/solution.py
+++ b/solution.py
@@ -37,10 +37,10 @@
     )
 
 
-def image_kernel(feature_count, plane_count, *refs):
+def image_kernel(feature_count, plane_count, first, *refs):
     plane_refs = refs[:plane_count]
     line_refs = refs[plane_count:-3]
-    noise_ref, probes_ref, partial_ref = refs[-3:]
+    start_ref, probes_ref, partial_ref = refs[-3:]
     rows = [jnp.concatenate([ref[...], norm_rows(ref[...], 1)], axis=0) for ref in plane_refs]
 
     def add_blocks(blocks, totals):
@@ -58,8 +58,11 @@
             result.append(total + jnp.dot(probes, weights, preferred_element_type=jnp.float32))
         return result
 
-    totals = [noise_ref[...] * probes_ref[...]]
-    totals += [jnp.zeros(probes_ref.shape, jnp.float32)] * (plane_count - 1)
+    if first:
+        totals = [start_ref[...] * probes_ref[...]]
+        totals += [jnp.zeros(probes_ref.shape, jnp.float32)] * (plane_count - 1)
+    else:
+        totals = [start_ref[number] for number in range(plane_count)]
     if len(line_refs[0].shape) == 2:
         totals = add_blocks([ref[...] for ref in line_refs], totals)
     else:
@@ -155,11 +158,23 @@
         )(scaled, probes)
         lines = everywhere(line, LINE, line_count)
         planes = plane_blocks(scaled, plane_shape)
-        partial = pl.pallas_call(
-            lambda *refs: image_kernel(feature_count, plane_count, *refs),
-            out_shape=jax.ShapeDtypeStruct((plane_count + 1, probe_count, width), jnp.float32),
-            compiler_params=VMEM,
-        )(*planes, *lines, noise_var[None, :], probes)
+
+        def partial_of(blocks, start, first):
+            work = plane_count * len(blocks) * width * width
+            return pl.pallas_call(
+                lambda *refs: image_kernel(feature_count, plane_count, first, *refs),
+                out_shape=jax.ShapeDtypeStruct((plane_count + 1, probe_count, width), jnp.float32),
+                compiler_params=VMEM,
+                cost_estimate=pl.CostEstimate(
+                    flops=2 * work * (feature_count + probe_count),
+                    bytes_accessed=4 * width * plane_count * feature_count,
+                    transcendentals=work,
+                ),
+            )(*planes, *blocks, start, probes)
+
+        partial = partial_of(lines[:3], noise_var[None, :], True)
+        if len(lines) > 3:
+            partial = partial_of(lines[3:], partial, False)
         image, sums = pl.pallas_call(
             lambda *refs: combine_kernel(plane_count, *refs),
             out_shape=(

time: 29.8 us -> 30.2 us (1.013)
  Pallas kernels: 2.78 us -> 3.54 us
    pallas_call x1 -> x2, Pallas kernels: 1.9 us -> 2.66 us  [partial_of(): pl.pallas_call(lambda *refs: image_kernel(feature_count, plane_count, fir...]
    ppermute x12, waiting for transfers between devices: 11.1 us -> 10.8 us  [everywhere(): lax.ppermute(value, axes, [(source_of(i, step, count), i) for i in range(...]
  transfers between devices with their start and end apart: 12 -> 12, of which waited for: 6 -> 7; matrix products, arithmetic and copies ran while one was open for 0% -> 0% of each run, Pallas kernels for 0% -> 5%
where the time goes in v8:
time: 30.2 us; the launch traced here: 30 us
  starting transfers between devices  14.1 us (47%)
  waiting for transfers between devices  10.8 us (36%)
  Pallas kernels  3.54 us (12%)
  other arithmetic  0.93 us (3%)
  between operations  0.67 us (2%)
    ppermute x12, starting transfers between devices, everywhere(): lax.ppermute(value, axes, [(source_of(i, step, count), i) for i in range(...  14.1 us
    ppermute x12, waiting for transfers between devices, everywhere(): lax.ppermute(value, axes, [(source_of(i, step, count), i) for i in range(...  10.8 us
    pallas_call x2, Pallas kernels, partial_of(): pl.pallas_call(lambda *refs: image_kernel(feature_count, plane_count, fir...  2.66 us
    convert_element_type x1, other arithmetic, local(): (features.astype(jnp.float32) / lengthscale[:, None]).astype(jnp.bfloat16)  0.93 us
    pallas_call x1, Pallas kernels, local(): pl.pallas_call(finish_kernel, out_shape=outs, compiler_params=VMEM)  0.77 us
  transfers between devices with their start and end apart: 12, of which 7 were waited for; matrix products, arithmetic and copies ran while one was open for 0% of the time, Pallas kernels for 5%

profile of v8, /device:TPU:0, one launch (start us, length us, event | category | flops | bytes accessed | tf_op | source)
XLA Modules:
  0.0 30.0 jit_solution(13203114769896422430)
XLA Ops:
  0.6 0.0 copy-start
  0.6 0.9 %divide_convert_fusion.scaled_ref.refs_0_ = bf16[128,256]{1,0:T(8,128)(2,1)S(1)} fusion(bf16[128,256]{1,0:T(8,128)(2,1)} %param.4, f32[128]{0:T(128)} %param.5), kind=kLoop, calls=%fused_computation | loop fusion | flops 98304 | bytes 131584 | tf_op jit(solution)/shard_map/convert_element_type | solution.py:153
  1.6 0.5 %collective-permute-start = (bf16[128,256]{1,0:T(8,128)(2,1)S(1)}, bf16[128,256]{1,0:T(8,128)(2,1)S(1)}, u32[]{:S(2)}, u32[]{:S(2)}) collective-permute-start(bf16[128,256]{1,0:T(8,128)(2,1)S(1)} %divide_convert_fusion.scaled_ref.refs_0_), channel_id=1, source_target_pairs={{1,0},{0,1},{3,2},{2,3},{5,4},{4,5},{7,6},{6,7},{9,8},{8,9},{11,10... | collective-permute-start | bytes 196616 | tf_op jit(solution)/shard_map/ppermute | solution.py:133
  2.1 0.0 copy-done
  2.1 0.0 copy-start.1
  2.1 3.7 %collective-permute-start.5 = (bf16[144,256]{1,0:T(8,128)(2,1)S(1)}, bf16[144,256]{1,0:T(8,128)(2,1)S(1)}, u32[]{:S(2)}, u32[]{:S(2)}) collective-permute-start(bf16[144,256]{1,0:T(8,128)(2,1)S(1)} %shard_map.67.refs_4_), channel_id=1, source_target_pairs={{8,0},{12,4},{0,8},{4,12},{9,1},{13,5},{1,9},{5,13},{10,2},{14,6},... | collective-permute-start | bytes 221192 | tf_op jit(solution)/shard_map/ppermute | solution.py:133
  5.8 1.6 %collective-permute-start.4 = (bf16[144,256]{1,0:T(8,128)(2,1)S(1)}, bf16[144,256]{1,0:T(8,128)(2,1)S(1)}, u32[]{:S(2)}, u32[]{:S(2)}) collective-permute-start(bf16[144,256]{1,0:T(8,128)(2,1)S(1)} %shard_map.67.refs_4_), channel_id=1, source_target_pairs={{4,0},{0,4},{12,8},{8,12},{5,1},{1,5},{13,9},{9,13},{6,2},{2,6},{1... | collective-permute-start | bytes 221192 | tf_op jit(solution)/shard_map/ppermute | solution.py:133
  7.4 1.5 %collective-permute-start.1 = (bf16[128,256]{1,0:T(8,128)(2,1)S(1)}, bf16[128,256]{1,0:T(8,128)(2,1)S(1)}, u32[]{:S(2)}, u32[]{:S(2)}) collective-permute-start(bf16[128,256]{1,0:T(8,128)(2,1)S(1)} %divide_convert_fusion.scaled_ref.refs_0_), channel_id=1, source_target_pairs={{2,0},{0,2},{3,1},{1,3},{6,4},{4,6},{7,5},{5,7},{10,8},{8,10},{11,... | collective-permute-start | bytes 196616 | tf_op jit(solution)/shard_map/ppermute | solution.py:133
  8.9 0.0 collective-permute-done.refs_1_
  8.9 0.5 %collective-permute-start.2 = (bf16[128,256]{1,0:T(8,128)(2,1)S(1)}, bf16[128,256]{1,0:T(8,128)(2,1)S(1)}, u32[]{:S(2)}, u32[]{:S(2)}) collective-permute-start(bf16[128,256]{1,0:T(8,128)(2,1)S(1)} %collective-permute-done.refs_1_), channel_id=1, source_target_pairs={{2,0},{0,2},{3,1},{1,3},{6,4},{4,6},{7,5},{5,7},{10,8},{8,10},{11,... | collective-permute-start | bytes 196616 | tf_op jit(solution)/shard_map/ppermute | solution.py:133
  9.4 0.0 collective-permute-start.3
  9.4 2.7 %collective-permute-done.1.refs_2_ = bf16[128,256]{1,0:T(8,128)(2,1)S(1)} collective-permute-done((bf16[128,256]{1,0:T(8,128)(2,1)S(1)}, bf16[128,256]{1,0:T(8,128)(2,1)S(1)}, u32[]{:S(2)}, u32[]{:S(2)}) %collective-permute-start.1) | collective-permute-done | bytes 65568 | tf_op jit(solution)/shard_map/ppermute | solution.py:133
  12.2 0.0 collective-permute-done.5.refs_6_
  12.2 0.0 collective-permute-done.4.refs_5_
  12.2 1.0 %collective-permute-done.2.refs_3_ = bf16[128,256]{1,0:T(8,128)(2,1)S(1)} collective-permute-done((bf16[128,256]{1,0:T(8,128)(2,1)S(1)}, bf16[128,256]{1,0:T(8,128)(2,1)S(1)}, u32[]{:S(2)}, u32[]{:S(2)}) %collective-permute-start.2) | collective-permute-done | bytes 65568 | tf_op jit(solution)/shard_map/ppermute | solution.py:133
  13.1 0.0 copy-done.1
  13.1 1.6 %shard_map.68.refs_5_ = f32[5,16,256]{2,1,0:T(8,128)S(1)} custom-call(bf16[128,256]{1,0:T(8,128)(2,1)S(1)} %divide_convert_fusion.scaled_ref.refs_0_, bf16[128,256]{1,0:T(8,128)(2,1)S(1)} %collective-permute-done.refs_1_, bf16[128,256]{1,0:T(8,128)(2,1)S(1)} %collective-permute-done.1.refs_2_, bf16[128,256]{1,0:T(8,128)(2,1)S(1)} %collective-permute-done.2.refs_3_, ...), custom_call_target="tpu_custom_call" | custom-call | flops 226492416 | bytes 524288 | tf_op jit(solution)/shard_map/pallas_call | solution.py:164
  14.8 0.8 %collective-permute-done.3.refs_4_ = bf16[144,256]{1,0:T(8,128)(2,1)S(1)} collective-permute-done((bf16[144,256]{1,0:T(8,128)(2,1)S(1)}, bf16[144,256]{1,0:T(8,128)(2,1)S(1)}, u32[]{:S(2)}, u32[]{:S(2)}) %collective-permute-start.3) | collective-permute-done | bytes 73760 | tf_op jit(solution)/shard_map/ppermute | solution.py:133
  15.6 1.0 %shard_map.69.refs_0_ = f32[5,16,256]{2,1,0:T(8,128)S(1)} custom-call(bf16[128,256]{1,0:T(8,128)(2,1)S(1)} %divide_convert_fusion.scaled_ref.refs_0_, bf16[128,256]{1,0:T(8,128)(2,1)S(1)} %collective-permute-done.refs_1_, bf16[128,256]{1,0:T(8,128)(2,1)S(1)} %collective-permute-done.1.refs_2_, bf16[128,256]{1,0:T(8,128)(2,1)S(1)} %collective-permute-done.2.refs_3_, ...), custom_call_target="tpu_custom_call" | custom-call | flops 75497472 | bytes 524288 | tf_op jit(solution)/shard_map/pallas_call | solution.py:164
  16.6 0.0 collective-permute-start.8
  16.6 1.5 %collective-permute-start.7 = (f32[5,16,256]{2,1,0:T(8,128)S(1)}, f32[5,16,256]{2,1,0:T(8,128)S(1)}, u32[]{:S(2)}, u32[]{:S(2)}) collective-permute-start(f32[5,16,256]{2,1,0:T(8,128)S(1)} %shard_map.69.refs_0_), channel_id=1, source_target_pairs={{2,0},{3,1},{0,2},{1,3},{6,4},{7,5},{4,6},{5,7},{10,8},{11,9},{8,1... | collective-permute-start | bytes 245768 | tf_op jit(solution)/shard_map/ppermute | solution.py:133
  18.1 0.3 %collective-permute-start.6 = (f32[5,16,256]{2,1,0:T(8,128)S(1)}, f32[5,16,256]{2,1,0:T(8,128)S(1)}, u32[]{:S(2)}, u32[]{:S(2)}) collective-permute-start(f32[5,16,256]{2,1,0:T(8,128)S(1)} %shard_map.69.refs_0_), channel_id=1, source_target_pairs={{1,0},{0,1},{3,2},{2,3},{5,4},{4,5},{7,6},{6,7},{9,8},{8,9},{11,10... | collective-permute-start | bytes 245768 | tf_op jit(solution)/shard_map/ppermute | solution.py:133
  18.5 2.8 %collective-permute-done.8.refs_3_ = f32[5,16,256]{2,1,0:T(8,128)S(1)} collective-permute-done((f32[5,16,256]{2,1,0:T(8,128)S(1)}, f32[5,16,256]{2,1,0:T(8,128)S(1)}, u32[]{:S(2)}, u32[]{:S(2)}) %collective-permute-start.8) | collective-permute-done | bytes 81952 | tf_op jit(solution)/shard_map/ppermute | solution.py:133
  21.3 1.8 %collective-permute-done.7.refs_2_ = f32[5,16,256]{2,1,0:T(8,128)S(1)} collective-permute-done((f32[5,16,256]{2,1,0:T(8,128)S(1)}, f32[5,16,256]{2,1,0:T(8,128)S(1)}, u32[]{:S(2)}, u32[]{:S(2)}) %collective-permute-start.7) | collective-permute-done | bytes 81952 | tf_op jit(solution)/shard_map/ppermute | solution.py:133
  23.1 0.0 collective-permute-done.6.refs_1_
  23.1 0.1 shard_map.70
  23.2 0.8 %collective-permute-start.11 = (f32[16,128]{1,0:T(8,128)S(1)}, f32[16,128]{1,0:T(8,128)S(1)}, u32[]{:S(2)}, u32[]{:S(2)}) collective-permute-start(f32[16,128]{1,0:T(8,128)S(1)} %get-tuple-element.6.refs_0_), channel_id=1, source_target_pairs={{12,0},{8,4},{4,8},{0,12},{13,1},{9,5},{5,9},{1,13},{14,2},{10,6},... | collective-permute-start | bytes 24584 | tf_op jit(solution)/shard_map/ppermute | solution.py:133
  24.0 0.0 collective-permute-start.10
  24.0 3.6 %collective-permute-start.9 = (f32[16,128]{1,0:T(8,128)S(1)}, f32[16,128]{1,0:T(8,128)S(1)}, u32[]{:S(2)}, u32[]{:S(2)}) collective-permute-start(f32[16,128]{1,0:T(8,128)S(1)} %get-tuple-element.6.refs_0_), channel_id=1, source_target_pairs={{4,0},{0,4},{12,8},{8,12},{5,1},{1,5},{13,9},{9,13},{6,2},{2,6},{1... | collective-permute-start | bytes 24584 | tf_op jit(solution)/shard_map/ppermute | solution.py:133
  27.6 1.1 %collective-permute-done.11.refs_3_ = f32[16,128]{1,0:T(8,128)S(1)} collective-permute-done((f32[16,128]{1,0:T(8,128)S(1)}, f32[16,128]{1,0:T(8,128)S(1)}, u32[]{:S(2)}, u32[]{:S(2)}) %collective-permute-start.11) | collective-permute-done | bytes 8224 | tf_op jit(solution)/shard_map/ppermute | solution.py:133
  28.7 0.0 collective-permute-done.10.refs_2_
  28.7 0.6 %collective-permute-done.9.refs_1_ = f32[16,128]{1,0:T(8,128)S(1)} collective-permute-done((f32[16,128]{1,0:T(8,128)S(1)}, f32[16,128]{1,0:T(8,128)S(1)}, u32[]{:S(2)}, u32[]{:S(2)}) %collective-permute-start.9) | collective-permute-done | bytes 8224 | tf_op jit(solution)/shard_map/ppermute | solution.py:133
  29.2 0.8 %shard_map.71 = (f32[16,256]{1,0:T(8,128)}, f32[16,256]{1,0:T(8,128)}, f32[16,256]{1,0:T(8,128)}) custom-call(f32[16,256]{1,0:T(8,128)S(1)} %get-tuple-element.5.image_ref, f32[16,256]{1,0:T(8,128)S(1)} %copy-done, f32[16,128]{1,0:T(8,128)S(1)} %get-tuple-element.6.refs_0_, f32[16,128]{1,0:T(8,128)S(1)} %collective-permute-done.9.refs_1_, ...), custom_call_target="tpu_custom_call" | custom-call | tf_op jit(solution)/shard_map/pallas_call | solution.py:187
  (1 shorter events, 0.0 us)
Async XLA Ops:
  0.6 1.5 %copy-start = (f32[16,256]{1,0:T(8,128)S(1)}, f32[16,256]{1,0:T(8,128)}, u32[]{:S(2)}) copy-start(f32[16,256]{1,0:T(8,128)} %probes_ref.3) | copy-start | bytes 49156
  1.6 7.3 %collective-permute-start = (bf16[128,256]{1,0:T(8,128)(2,1)S(1)}, bf16[128,256]{1,0:T(8,128)(2,1)S(1)}, u32[]{:S(2)}, u32[]{:S(2)}) collective-permute-start(bf16[128,256]{1,0:T(8,128)(2,1)S(1)} %divide_convert_fusion.scaled_ref.refs_0_), channel_id=1, source_target_pairs={{1,0},{0,1},{3,2},{2,3},{5,4},{4,5},{7,6},{6,7},{9,8},{8,9},{11,10... | collective-permute-start | bytes 196616 | tf_op jit(solution)/shard_map/ppermute | solution.py:133
  2.1 11.0 %copy-start.1 = (f32[256]{0:T(256)S(1)}, f32[256]{0:T(256)}, u32[]{:S(2)}) copy-start(f32[256]{0:T(256)} %param.6) | copy-start | bytes 3076
  2.1 10.1 %collective-permute-start.5 = (bf16[144,256]{1,0:T(8,128)(2,1)S(1)}, bf16[144,256]{1,0:T(8,128)(2,1)S(1)}, u32[]{:S(2)}, u32[]{:S(2)}) collective-permute-start(bf16[144,256]{1,0:T(8,128)(2,1)S(1)} %shard_map.67.refs_4_), channel_id=1, source_target_pairs={{8,0},{12,4},{0,8},{4,12},{9,1},{13,5},{1,9},{5,13},{10,2},{14,6},... | collective-permute-start | bytes 221192 | tf_op jit(solution)/shard_map/ppermute | solution.py:133
  5.8 6.4 %collective-permute-start.4 = (bf16[144,256]{1,0:T(8,128)(2,1)S(1)}, bf16[144,256]{1,0:T(8,128)(2,1)S(1)}, u32[]{:S(2)}, u32[]{:S(2)}) collective-permute-start(bf16[144,256]{1,0:T(8,128)(2,1)S(1)} %shard_map.67.refs_4_), channel_id=1, source_target_pairs={{4,0},{0,4},{12,8},{8,12},{5,1},{1,5},{13,9},{9,13},{6,2},{2,6},{1... | collective-permute-start | bytes 221192 | tf_op jit(solution)/shard_map/ppermute | solution.py:133
  7.4 4.8 %collective-permute-start.1 = (bf16[128,256]{1,0:T(8,128)(2,1)S(1)}, bf16[128,256]{1,0:T(8,128)(2,1)S(1)}, u32[]{:S(2)}, u32[]{:S(2)}) collective-permute-start(bf16[128,256]{1,0:T(8,128)(2,1)S(1)} %divide_convert_fusion.scaled_ref.refs_0_), channel_id=1, source_target_pairs={{2,0},{0,2},{3,1},{1,3},{6,4},{4,6},{7,5},{5,7},{10,8},{8,10},{11,... | collective-permute-start | bytes 196616 | tf_op jit(solution)/shard_map/ppermute | solution.py:133
  8.9 4.3 %collective-permute-start.2 = (bf16[128,256]{1,0:T(8,128)(2,1)S(1)}, bf16[128,256]{1,0:T(8,128)(2,1)S(1)}, u32[]{:S(2)}, u32[]{:S(2)}) collective-permute-start(bf16[128,256]{1,0:T(8,128)(2,1)S(1)} %collective-permute-done.refs_1_), channel_id=1, source_target_pairs={{2,0},{0,2},{3,1},{1,3},{6,4},{4,6},{7,5},{5,7},{10,8},{8,10},{11,... | collective-permute-start | bytes 196616 | tf_op jit(solution)/shard_map/ppermute | solution.py:133
  9.4 6.2 %collective-permute-start.3 = (bf16[144,256]{1,0:T(8,128)(2,1)S(1)}, bf16[144,256]{1,0:T(8,128)(2,1)S(1)}, u32[]{:S(2)}, u32[]{:S(2)}) collective-permute-start(bf16[144,256]{1,0:T(8,128)(2,1)S(1)} %shard_map.67.refs_4_), channel_id=1, source_target_pairs={{12,0},{8,4},{4,8},{0,12},{13,1},{9,5},{5,9},{1,13},{14,2},{10,6},... | collective-permute-start | bytes 221192 | tf_op jit(solution)/shard_map/ppermute | solution.py:133
  16.6 4.7 %collective-permute-start.8 = (f32[5,16,256]{2,1,0:T(8,128)S(1)}, f32[5,16,256]{2,1,0:T(8,128)S(1)}, u32[]{:S(2)}, u32[]{:S(2)}) collective-permute-start(f32[5,16,256]{2,1,0:T(8,128)S(1)} %shard_map.69.refs_0_), channel_id=1, source_target_pairs={{3,0},{2,1},{1,2},{0,3},{7,4},{6,5},{5,6},{4,7},{11,8},{10,9},{9,1... | collective-permute-start | bytes 245768 | tf_op jit(solution)/shard_map/ppermute | solution.py:133
  16.6 6.5 %collective-permute-start.7 = (f32[5,16,256]{2,1,0:T(8,128)S(1)}, f32[5,16,256]{2,1,0:T(8,128)S(1)}, u32[]{:S(2)}, u32[]{:S(2)}) collective-permute-start(f32[5,16,256]{2,1,0:T(8,128)S(1)} %shard_map.69.refs_0_), channel_id=1, source_target_pairs={{2,0},{3,1},{0,2},{1,3},{6,4},{7,5},{4,6},{5,7},{10,8},{11,9},{8,1... | collective-permute-start | bytes 245768 | tf_op jit(solution)/shard_map/ppermute | solution.py:133
  18.1 5.0 %collective-permute-start.6 = (f32[5,16,256]{2,1,0:T(8,128)S(1)}, f32[5,16,256]{2,1,0:T(8,128)S(1)}, u32[]{:S(2)}, u32[]{:S(2)}) collective-permute-start(f32[5,16,256]{2,1,0:T(8,128)S(1)} %shard_map.69.refs_0_), channel_id=1, source_target_pairs={{1,0},{0,1},{3,2},{2,3},{5,4},{4,5},{7,6},{6,7},{9,8},{8,9},{11,10... | collective-permute-start | bytes 245768 | tf_op jit(solution)/shard_map/ppermute | solution.py:133
  23.2 5.5 %collective-permute-start.11 = (f32[16,128]{1,0:T(8,128)S(1)}, f32[16,128]{1,0:T(8,128)S(1)}, u32[]{:S(2)}, u32[]{:S(2)}) collective-permute-start(f32[16,128]{1,0:T(8,128)S(1)} %get-tuple-element.6.refs_0_), channel_id=1, source_target_pairs={{12,0},{8,4},{4,8},{0,12},{13,1},{9,5},{5,9},{1,13},{14,2},{10,6},... | collective-permute-start | bytes 24584 | tf_op jit(solution)/shard_map/ppermute | solution.py:133
  24.0 4.7 %collective-permute-start.10 = (f32[16,128]{1,0:T(8,128)S(1)}, f32[16,128]{1,0:T(8,128)S(1)}, u32[]{:S(2)}, u32[]{:S(2)}) collective-permute-start(f32[16,128]{1,0:T(8,128)S(1)} %get-tuple-element.6.refs_0_), channel_id=1, source_target_pairs={{8,0},{12,4},{0,8},{4,12},{9,1},{13,5},{1,9},{5,13},{10,2},{14,6},... | collective-permute-start | bytes 24584 | tf_op jit(solution)/shard_map/ppermute | solution.py:133
  24.0 5.3 %collective-permute-start.9 = (f32[16,128]{1,0:T(8,128)S(1)}, f32[16,128]{1,0:T(8,128)S(1)}, u32[]{:S(2)}, u32[]{:S(2)}) collective-permute-start(f32[16,128]{1,0:T(8,128)S(1)} %get-tuple-element.6.refs_0_), channel_id=1, source_target_pairs={{4,0},{0,4},{12,8},{8,12},{5,1},{1,5},{13,9},{9,13},{6,2},{2,6},{1... | collective-permute-start | bytes 24584 | tf_op jit(solution)/shard_map/ppermute | solution.py:133

commit v9 on v7

--- a/solution.py
+++ b/solution.py
@@ -75,7 +75,7 @@
 
 
 def combine_kernel(plane_count, *refs):
-    partial_refs = refs[:-2]
+    partial_refs = [refs[number] for number in exchange_order(plane_count)]
     image_ref, sums_ref = refs[-2:]
     lane = lax.broadcasted_iota(jnp.int32, sums_ref.shape, 1)
     products = [0.0, 0.0, 0.0]
@@ -123,6 +123,10 @@
     return step ^ number if paired(count) else (number - step) % count
 
 
+def exchange_order(count):
+    return (0, 1, 3, 2) if count == 4 else tuple(range(count))
+
+
 def everywhere(value, axes, count):
     if count > DIRECT:
         return [lax.all_gather(value, axes, axis=0, tiled=False)]
@@ -160,6 +164,7 @@
             out_shape=jax.ShapeDtypeStruct((plane_count + 1, probe_count, width), jnp.float32),
             compiler_params=VMEM,
         )(*planes, *lines, noise_var[None, :], probes)
+        partials = everywhere(partial, PLANE, plane_count)
         image, sums = pl.pallas_call(
             lambda *refs: combine_kernel(plane_count, *refs),
             out_shape=(
@@ -167,7 +172,7 @@
                 jax.ShapeDtypeStruct((probe_count, 128), jnp.float32),
             ),
             compiler_params=VMEM,
-        )(*everywhere(partial, PLANE, plane_count))
+        )(*[partials[number] for number in exchange_order(plane_count)])
         outs = (jax.ShapeDtypeStruct(probes.shape, jnp.float32),) * 3
         return pl.pallas_call(finish_kernel, out_shape=outs, compiler_params=VMEM)(
             image, probes, *everywhere(sums, LINE, line_count)

time: 29.8 us -> 30 us (level)
  starting transfers between devices: 14.1 us -> 14.4 us
where the time goes in v9:
time: 30 us; the launch traced here: 29.8 us
  starting transfers between devices  14.4 us (48%)
  waiting for transfers between devices  11 us (37%)
  Pallas kernels  2.78 us (9%)
  other arithmetic  0.93 us (3%)
  between operations  0.68 us (2%)
    ppermute x12, starting transfers between devices, everywhere(): lax.ppermute(value, axes, [(source_of(i, step, count), i) for i in range(...  14.4 us
    ppermute x12, waiting for transfers between devices, everywhere(): lax.ppermute(value, axes, [(source_of(i, step, count), i) for i in range(...  11 us
    pallas_call x1, Pallas kernels, local(): pl.pallas_call(lambda *refs: image_kernel(feature_count, plane_count, *re...  1.9 us
    convert_element_type x1, other arithmetic, local(): (features.astype(jnp.float32) / lengthscale[:, None]).astype(jnp.bfloat16)  0.93 us
    pallas_call x1, Pallas kernels, local(): pl.pallas_call(finish_kernel, out_shape=outs, compiler_params=VMEM)  0.77 us
  transfers between devices with their start and end apart: 12, of which 6 were waited for; matrix products, arithmetic and copies ran while one was open for 0% of the time, Pallas kernels for 0%

profile of v9, /device:TPU:0, one launch (start us, length us, event | category | flops | bytes accessed | tf_op | source)
XLA Modules:
  0.0 29.8 jit_solution(16767856230585116573)
XLA Ops:
  0.6 0.0 copy-start
  0.6 0.9 %divide_convert_fusion.scaled_ref.refs_0_ = bf16[128,256]{1,0:T(8,128)(2,1)S(1)} fusion(bf16[128,256]{1,0:T(8,128)(2,1)} %param.4, f32[128]{0:T(128)} %param.5), kind=kLoop, calls=%fused_computation | loop fusion | flops 98304 | bytes 131584 | tf_op jit(solution)/shard_map/convert_element_type | solution.py:154
  1.6 0.5 %collective-permute-start = (bf16[128,256]{1,0:T(8,128)(2,1)S(1)}, bf16[128,256]{1,0:T(8,128)(2,1)S(1)}, u32[]{:S(2)}, u32[]{:S(2)}) collective-permute-start(bf16[128,256]{1,0:T(8,128)(2,1)S(1)} %divide_convert_fusion.scaled_ref.refs_0_), channel_id=1, source_target_pairs={{1,0},{0,1},{3,2},{2,3},{5,4},{4,5},{7,6},{6,7},{9,8},{8,9},{11,10... | collective-permute-start | bytes 196616 | tf_op jit(solution)/shard_map/ppermute | solution.py:134
  2.1 0.0 copy-done
  2.1 0.0 copy-start.1
  2.1 4.7 %collective-permute-start.5 = (bf16[144,256]{1,0:T(8,128)(2,1)S(1)}, bf16[144,256]{1,0:T(8,128)(2,1)S(1)}, u32[]{:S(2)}, u32[]{:S(2)}) collective-permute-start(bf16[144,256]{1,0:T(8,128)(2,1)S(1)} %shard_map.67.refs_4_), channel_id=1, source_target_pairs={{12,0},{8,4},{4,8},{0,12},{13,1},{9,5},{5,9},{1,13},{14,2},{10,6},... | collective-permute-start | bytes 221192 | tf_op jit(solution)/shard_map/ppermute | solution.py:134
  6.8 0.0 collective-permute-start.4
  6.8 0.6 %collective-permute-start.3 = (bf16[144,256]{1,0:T(8,128)(2,1)S(1)}, bf16[144,256]{1,0:T(8,128)(2,1)S(1)}, u32[]{:S(2)}, u32[]{:S(2)}) collective-permute-start(bf16[144,256]{1,0:T(8,128)(2,1)S(1)} %shard_map.67.refs_4_), channel_id=1, source_target_pairs={{4,0},{0,4},{12,8},{8,12},{5,1},{1,5},{13,9},{9,13},{6,2},{2,6},{1... | collective-permute-start | bytes 221192 | tf_op jit(solution)/shard_map/ppermute | solution.py:134
  7.5 1.6 %collective-permute-start.1 = (bf16[128,256]{1,0:T(8,128)(2,1)S(1)}, bf16[128,256]{1,0:T(8,128)(2,1)S(1)}, u32[]{:S(2)}, u32[]{:S(2)}) collective-permute-start(bf16[128,256]{1,0:T(8,128)(2,1)S(1)} %divide_convert_fusion.scaled_ref.refs_0_), channel_id=1, source_target_pairs={{2,0},{0,2},{3,1},{1,3},{6,4},{4,6},{7,5},{5,7},{10,8},{8,10},{11,... | collective-permute-start | bytes 196616 | tf_op jit(solution)/shard_map/ppermute | solution.py:134
  9.1 0.0 collective-permute-done.refs_1_
  9.1 0.4 %collective-permute-start.2 = (bf16[128,256]{1,0:T(8,128)(2,1)S(1)}, bf16[128,256]{1,0:T(8,128)(2,1)S(1)}, u32[]{:S(2)}, u32[]{:S(2)}) collective-permute-start(bf16[128,256]{1,0:T(8,128)(2,1)S(1)} %collective-permute-done.refs_1_), channel_id=1, source_target_pairs={{2,0},{0,2},{3,1},{1,3},{6,4},{4,6},{7,5},{5,7},{10,8},{8,10},{11,... | collective-permute-start | bytes 196616 | tf_op jit(solution)/shard_map/ppermute | solution.py:134
  9.5 2.8 %collective-permute-done.1.refs_2_ = bf16[128,256]{1,0:T(8,128)(2,1)S(1)} collective-permute-done((bf16[128,256]{1,0:T(8,128)(2,1)S(1)}, bf16[128,256]{1,0:T(8,128)(2,1)S(1)}, u32[]{:S(2)}, u32[]{:S(2)}) %collective-permute-start.1) | collective-permute-done | bytes 65568 | tf_op jit(solution)/shard_map/ppermute | solution.py:134
  12.3 0.0 collective-permute-done.5.refs_7_
  12.3 1.4 %collective-permute-done.4.refs_6_ = bf16[144,256]{1,0:T(8,128)(2,1)S(1)} collective-permute-done((bf16[144,256]{1,0:T(8,128)(2,1)S(1)}, bf16[144,256]{1,0:T(8,128)(2,1)S(1)}, u32[]{:S(2)}, u32[]{:S(2)}) %collective-permute-start.4) | collective-permute-done | bytes 73760 | tf_op jit(solution)/shard_map/ppermute | solution.py:134
  13.6 0.0 collective-permute-done.3.refs_5_
  13.6 0.0 collective-permute-done.2.refs_3_
  13.6 0.0 copy-done.1
  13.6 1.9 %shard_map.68.refs_0_ = f32[5,16,256]{2,1,0:T(8,128)S(1)} custom-call(bf16[128,256]{1,0:T(8,128)(2,1)S(1)} %divide_convert_fusion.scaled_ref.refs_0_, bf16[128,256]{1,0:T(8,128)(2,1)S(1)} %collective-permute-done.refs_1_, bf16[128,256]{1,0:T(8,128)(2,1)S(1)} %collective-permute-done.1.refs_2_, bf16[128,256]{1,0:T(8,128)(2,1)S(1)} %collective-permute-done.2.refs_3_, ...), custom_call_target="tpu_custom_call" | custom-call | tf_op jit(solution)/shard_map/pallas_call | solution.py:162
  15.5 1.5 %collective-permute-start.8 = (f32[5,16,256]{2,1,0:T(8,128)S(1)}, f32[5,16,256]{2,1,0:T(8,128)S(1)}, u32[]{:S(2)}, u32[]{:S(2)}) collective-permute-start(f32[5,16,256]{2,1,0:T(8,128)S(1)} %shard_map.68.refs_0_), channel_id=1, source_target_pairs={{2,0},{3,1},{0,2},{1,3},{6,4},{7,5},{4,6},{5,7},{10,8},{11,9},{8,1... | collective-permute-start | bytes 245768 | tf_op jit(solution)/shard_map/ppermute | solution.py:134
  17.0 0.0 collective-permute-start.7
  17.0 0.6 %collective-permute-start.6 = (f32[5,16,256]{2,1,0:T(8,128)S(1)}, f32[5,16,256]{2,1,0:T(8,128)S(1)}, u32[]{:S(2)}, u32[]{:S(2)}) collective-permute-start(f32[5,16,256]{2,1,0:T(8,128)S(1)} %shard_map.68.refs_0_), channel_id=1, source_target_pairs={{1,0},{0,1},{3,2},{2,3},{5,4},{4,5},{7,6},{6,7},{9,8},{8,9},{11,10... | collective-permute-start | bytes 245768 | tf_op jit(solution)/shard_map/ppermute | solution.py:134
  17.7 2.3 %collective-permute-done.8.refs_3_ = f32[5,16,256]{2,1,0:T(8,128)S(1)} collective-permute-done((f32[5,16,256]{2,1,0:T(8,128)S(1)}, f32[5,16,256]{2,1,0:T(8,128)S(1)}, u32[]{:S(2)}, u32[]{:S(2)}) %collective-permute-start.8) | collective-permute-done | bytes 81952 | tf_op jit(solution)/shard_map/ppermute | solution.py:134
  20.0 1.8 %collective-permute-done.7.refs_2_ = f32[5,16,256]{2,1,0:T(8,128)S(1)} collective-permute-done((f32[5,16,256]{2,1,0:T(8,128)S(1)}, f32[5,16,256]{2,1,0:T(8,128)S(1)}, u32[]{:S(2)}, u32[]{:S(2)}) %collective-permute-start.7) | collective-permute-done | bytes 81952 | tf_op jit(solution)/shard_map/ppermute | solution.py:134
  21.7 0.0 collective-permute-done.6.refs_1_
  21.7 0.1 shard_map.69
  21.9 2.7 %collective-permute-start.11 = (f32[16,128]{1,0:T(8,128)S(1)}, f32[16,128]{1,0:T(8,128)S(1)}, u32[]{:S(2)}, u32[]{:S(2)}) collective-permute-start(f32[16,128]{1,0:T(8,128)S(1)} %get-tuple-element.6.refs_0_), channel_id=1, source_target_pairs={{12,0},{8,4},{4,8},{0,12},{13,1},{9,5},{5,9},{1,13},{14,2},{10,6},... | collective-permute-start | bytes 24584 | tf_op jit(solution)/shard_map/ppermute | solution.py:134
  24.5 0.0 collective-permute-start.10
  24.5 1.7 %collective-permute-start.9 = (f32[16,128]{1,0:T(8,128)S(1)}, f32[16,128]{1,0:T(8,128)S(1)}, u32[]{:S(2)}, u32[]{:S(2)}) collective-permute-start(f32[16,128]{1,0:T(8,128)S(1)} %get-tuple-element.6.refs_0_), channel_id=1, source_target_pairs={{4,0},{0,4},{12,8},{8,12},{5,1},{1,5},{13,9},{9,13},{6,2},{2,6},{1... | collective-permute-start | bytes 24584 | tf_op jit(solution)/shard_map/ppermute | solution.py:134
  26.2 1.1 %collective-permute-done.11.refs_3_ = f32[16,128]{1,0:T(8,128)S(1)} collective-permute-done((f32[16,128]{1,0:T(8,128)S(1)}, f32[16,128]{1,0:T(8,128)S(1)}, u32[]{:S(2)}, u32[]{:S(2)}) %collective-permute-start.11) | collective-permute-done | bytes 8224 | tf_op jit(solution)/shard_map/ppermute | solution.py:134
  27.3 1.8 %collective-permute-done.10.refs_2_ = f32[16,128]{1,0:T(8,128)S(1)} collective-permute-done((f32[16,128]{1,0:T(8,128)S(1)}, f32[16,128]{1,0:T(8,128)S(1)}, u32[]{:S(2)}, u32[]{:S(2)}) %collective-permute-start.10) | collective-permute-done | bytes 8224 | tf_op jit(solution)/shard_map/ppermute | solution.py:134
  29.1 0.0 collective-permute-done.9.refs_1_
  29.1 0.8 %shard_map.70 = (f32[16,256]{1,0:T(8,128)}, f32[16,256]{1,0:T(8,128)}, f32[16,256]{1,0:T(8,128)}) custom-call(f32[16,256]{1,0:T(8,128)S(1)} %get-tuple-element.5.image_ref, f32[16,256]{1,0:T(8,128)S(1)} %copy-done, f32[16,128]{1,0:T(8,128)S(1)} %get-tuple-element.6.refs_0_, f32[16,128]{1,0:T(8,128)S(1)} %collective-permute-done.9.refs_1_, ...), custom_call_target="tpu_custom_call" | custom-call | tf_op jit(solution)/shard_map/pallas_call | solution.py:177
  (1 shorter events, 0.0 us)
Async XLA Ops:
  0.6 1.5 %copy-start = (f32[16,256]{1,0:T(8,128)S(1)}, f32[16,256]{1,0:T(8,128)}, u32[]{:S(2)}) copy-start(f32[16,256]{1,0:T(8,128)} %probes_ref.3) | copy-start | bytes 49156
  1.6 7.5 %collective-permute-start = (bf16[128,256]{1,0:T(8,128)(2,1)S(1)}, bf16[128,256]{1,0:T(8,128)(2,1)S(1)}, u32[]{:S(2)}, u32[]{:S(2)}) collective-permute-start(bf16[128,256]{1,0:T(8,128)(2,1)S(1)} %divide_convert_fusion.scaled_ref.refs_0_), channel_id=1, source_target_pairs={{1,0},{0,1},{3,2},{2,3},{5,4},{4,5},{7,6},{6,7},{9,8},{8,9},{11,10... | collective-permute-start | bytes 196616 | tf_op jit(solution)/shard_map/ppermute | solution.py:134
  2.1 11.5 %copy-start.1 = (f32[256]{0:T(256)S(1)}, f32[256]{0:T(256)}, u32[]{:S(2)}) copy-start(f32[256]{0:T(256)} %param.6) | copy-start | bytes 3076
  2.1 10.1 %collective-permute-start.5 = (bf16[144,256]{1,0:T(8,128)(2,1)S(1)}, bf16[144,256]{1,0:T(8,128)(2,1)S(1)}, u32[]{:S(2)}, u32[]{:S(2)}) collective-permute-start(bf16[144,256]{1,0:T(8,128)(2,1)S(1)} %shard_map.67.refs_4_), channel_id=1, source_target_pairs={{12,0},{8,4},{4,8},{0,12},{13,1},{9,5},{5,9},{1,13},{14,2},{10,6},... | collective-permute-start | bytes 221192 | tf_op jit(solution)/shard_map/ppermute | solution.py:134
  6.8 6.8 %collective-permute-start.4 = (bf16[144,256]{1,0:T(8,128)(2,1)S(1)}, bf16[144,256]{1,0:T(8,128)(2,1)S(1)}, u32[]{:S(2)}, u32[]{:S(2)}) collective-permute-start(bf16[144,256]{1,0:T(8,128)(2,1)S(1)} %shard_map.67.refs_4_), channel_id=1, source_target_pairs={{8,0},{12,4},{0,8},{4,12},{9,1},{13,5},{1,9},{5,13},{10,2},{14,6},... | collective-permute-start | bytes 221192 | tf_op jit(solution)/shard_map/ppermute | solution.py:134
  6.8 6.8 %collective-permute-start.3 = (bf16[144,256]{1,0:T(8,128)(2,1)S(1)}, bf16[144,256]{1,0:T(8,128)(2,1)S(1)}, u32[]{:S(2)}, u32[]{:S(2)}) collective-permute-start(bf16[144,256]{1,0:T(8,128)(2,1)S(1)} %shard_map.67.refs_4_), channel_id=1, source_target_pairs={{4,0},{0,4},{12,8},{8,12},{5,1},{1,5},{13,9},{9,13},{6,2},{2,6},{1... | collective-permute-start | bytes 221192 | tf_op jit(solution)/shard_map/ppermute | solution.py:134
  7.5 4.8 %collective-permute-start.1 = (bf16[128,256]{1,0:T(8,128)(2,1)S(1)}, bf16[128,256]{1,0:T(8,128)(2,1)S(1)}, u32[]{:S(2)}, u32[]{:S(2)}) collective-permute-start(bf16[128,256]{1,0:T(8,128)(2,1)S(1)} %divide_convert_fusion.scaled_ref.refs_0_), channel_id=1, source_target_pairs={{2,0},{0,2},{3,1},{1,3},{6,4},{4,6},{7,5},{5,7},{10,8},{8,10},{11,... | collective-permute-start | bytes 196616 | tf_op jit(solution)/shard_map/ppermute | solution.py:134
  9.1 4.5 %collective-permute-start.2 = (bf16[128,256]{1,0:T(8,128)(2,1)S(1)}, bf16[128,256]{1,0:T(8,128)(2,1)S(1)}, u32[]{:S(2)}, u32[]{:S(2)}) collective-permute-start(bf16[128,256]{1,0:T(8,128)(2,1)S(1)} %collective-permute-done.refs_1_), channel_id=1, source_target_pairs={{2,0},{0,2},{3,1},{1,3},{6,4},{4,6},{7,5},{5,7},{10,8},{8,10},{11,... | collective-permute-start | bytes 196616 | tf_op jit(solution)/shard_map/ppermute | solution.py:134
  15.5 4.4 %collective-permute-start.8 = (f32[5,16,256]{2,1,0:T(8,128)S(1)}, f32[5,16,256]{2,1,0:T(8,128)S(1)}, u32[]{:S(2)}, u32[]{:S(2)}) collective-permute-start(f32[5,16,256]{2,1,0:T(8,128)S(1)} %shard_map.68.refs_0_), channel_id=1, source_target_pairs={{2,0},{3,1},{0,2},{1,3},{6,4},{7,5},{4,6},{5,7},{10,8},{11,9},{8,1... | collective-permute-start | bytes 245768 | tf_op jit(solution)/shard_map/ppermute | solution.py:134
  17.0 4.7 %collective-permute-start.7 = (f32[5,16,256]{2,1,0:T(8,128)S(1)}, f32[5,16,256]{2,1,0:T(8,128)S(1)}, u32[]{:S(2)}, u32[]{:S(2)}) collective-permute-start(f32[5,16,256]{2,1,0:T(8,128)S(1)} %shard_map.68.refs_0_), channel_id=1, source_target_pairs={{3,0},{2,1},{1,2},{0,3},{7,4},{6,5},{5,6},{4,7},{11,8},{10,9},{9,1... | collective-permute-start | bytes 245768 | tf_op jit(solution)/shard_map/ppermute | solution.py:134
  17.0 4.7 %collective-permute-start.6 = (f32[5,16,256]{2,1,0:T(8,128)S(1)}, f32[5,16,256]{2,1,0:T(8,128)S(1)}, u32[]{:S(2)}, u32[]{:S(2)}) collective-permute-start(f32[5,16,256]{2,1,0:T(8,128)S(1)} %shard_map.68.refs_0_), channel_id=1, source_target_pairs={{1,0},{0,1},{3,2},{2,3},{5,4},{4,5},{7,6},{6,7},{9,8},{8,9},{11,10... | collective-permute-start | bytes 245768 | tf_op jit(solution)/shard_map/ppermute | solution.py:134
  21.9 5.5 %collective-permute-start.11 = (f32[16,128]{1,0:T(8,128)S(1)}, f32[16,128]{1,0:T(8,128)S(1)}, u32[]{:S(2)}, u32[]{:S(2)}) collective-permute-start(f32[16,128]{1,0:T(8,128)S(1)} %get-tuple-element.6.refs_0_), channel_id=1, source_target_pairs={{12,0},{8,4},{4,8},{0,12},{13,1},{9,5},{5,9},{1,13},{14,2},{10,6},... | collective-permute-start | bytes 24584 | tf_op jit(solution)/shard_map/ppermute | solution.py:134
  24.5 4.5 %collective-permute-start.10 = (f32[16,128]{1,0:T(8,128)S(1)}, f32[16,128]{1,0:T(8,128)S(1)}, u32[]{:S(2)}, u32[]{:S(2)}) collective-permute-start(f32[16,128]{1,0:T(8,128)S(1)} %get-tuple-element.6.refs_0_), channel_id=1, source_target_pairs={{8,0},{12,4},{0,8},{4,12},{9,1},{13,5},{1,9},{5,13},{10,2},{14,6},... | collective-permute-start | bytes 24584 | tf_op jit(solution)/shard_map/ppermute | solution.py:134
  24.5 4.5 %collective-permute-start.9 = (f32[16,128]{1,0:T(8,128)S(1)}, f32[16,128]{1,0:T(8,128)S(1)}, u32[]{:S(2)}, u32[]{:S(2)}) collective-permute-start(f32[16,128]{1,0:T(8,128)S(1)} %get-tuple-element.6.refs_0_), channel_id=1, source_target_pairs={{4,0},{0,4},{12,8},{8,12},{5,1},{1,5},{13,9},{9,13},{6,2},{2,6},{1... | collective-permute-start | bytes 24584 | tf_op jit(solution)/shard_map/ppermute | solution.py:134

commit v10 on v5

--- a/solution.py
+++ b/solution.py
@@ -9,7 +9,9 @@
 LINE = ("blk",)
 DIRECT = 8
 VMEM = pltpu.CompilerParams(vmem_limit_bytes=40 * 1024 * 1024)
-HALF = 8
+FORTH = (0, 4, 1, 3, 5, 6, 7, 2)
+BACK = (0, 2, 7, 3, 1, 4, 5, 6)
+EXCHANGE = {count: tuple(range(count)) for count in range(1, DIRECT + 1)} | {4: (0, 1, 3, 2)}
 
 
 def pieces_of(value):
@@ -21,54 +23,58 @@
     return pieces
 
 
-def norm_rows(scaled, place):
-    norms = -0.5 * jnp.sum(jnp.square(scaled.astype(jnp.float32)), axis=0, keepdims=True)
-    row = lax.broadcasted_iota(jnp.int32, (2 * HALF, scaled.shape[1]), 0)
-    here, there = place * HALF, (1 - place) * HALF
-    rows = jnp.where((row >= there) & (row < there + 3), 1.0, 0.0)
-    for number, piece in enumerate(pieces_of(norms)):
-        rows = jnp.where(row == here + number, piece, rows)
-    return rows.astype(jnp.bfloat16)
+def half_norms(scaled, axis):
+    return 0.5 * jnp.sum(jnp.square(scaled), axis=axis, keepdims=True)
+
+
+def arranged(blocks, places):
+    return [blocks[place] for place in places] if len(blocks) == len(places) else list(blocks)
 
 
 def pack_kernel(scaled_ref, probes_ref, line_ref, plane_ref):
-    scaled = scaled_ref[...]
-    rows = norm_rows(scaled, 0)
     high, low, _ = pieces_of(probes_ref[...])
     high, low = high.astype(jnp.bfloat16), low.astype(jnp.bfloat16)
-    line_ref[...] = jnp.concatenate([scaled, rows.astype(jnp.bfloat16), high], axis=0)
-    plane_ref[...] = jnp.concatenate([scaled, high, low], axis=0)
+    line_ref[...] = jnp.concatenate([scaled_ref[...], high], axis=0)
+    plane_ref[...] = jnp.concatenate([scaled_ref[...], high, low], axis=0)
 
 
 def image_kernel(feature_count, plane_count, *refs):
-    plane_refs = refs[:plane_count]
-    line_refs = refs[plane_count:-3]
     noise_ref, probes_ref, partial_ref = refs[-3:]
-    depth = feature_count + 2 * HALF
+    block_refs = arranged(refs[:-3], BACK)
+    plane_refs = block_refs[:plane_count]
+    line_refs = block_refs[plane_count:]
     rows = []
     for ref in plane_refs:
         scaled = ref[:feature_count, :]
-        rows.append(jnp.concatenate([scaled, norm_rows(scaled, 1)], axis=0))
-
-    def add_block(block_ref, totals):
-        columns = block_ref[:depth, :].astype(jnp.float32).T.astype(jnp.bfloat16)
-        probes = block_ref[depth:, :]
+        rows.append((scaled, half_norms(scaled.astype(jnp.float32), 0)))
+
+    def add_blocks(blocks, totals):
+        columns, column_norms = [], []
+        for block in blocks:
+            scaled = block[:feature_count, :].astype(jnp.float32).T
+            columns.append(scaled.astype(jnp.bfloat16))
+            column_norms.append(half_norms(scaled, 1))
+        columns = jnp.concatenate(columns, axis=0)
+        column_norms = jnp.concatenate(column_norms, axis=0)
+        probes = jnp.concatenate([block[feature_count:, :] for block in blocks], axis=1)
         result = []
-        for own, total in zip(rows, totals):
-            exponent = jnp.dot(columns, own, preferred_element_type=jnp.float32)
-            weights = jnp.exp(exponent).astype(jnp.bfloat16)
+        for (own, own_norms), total in zip(rows, totals):
+            inner = jnp.dot(columns, own, preferred_element_type=jnp.float32)
+            weights = jnp.exp(inner - (column_norms + own_norms)).astype(jnp.bfloat16)
             result.append(total + jnp.dot(probes, weights, preferred_element_type=jnp.float32))
         return result
 
     totals = [noise_ref[...] * probes_ref[...]]
     totals += [jnp.zeros(probes_ref.shape, jnp.float32)] * (plane_count - 1)
-    for ref in line_refs:
-        if len(ref.shape) == 2:
-            totals = add_block(ref, totals)
-        else:
-            totals = lax.fori_loop(
-                0, ref.shape[0], lambda number, value: add_block(ref.at[number], value), totals
-            )
+    if len(line_refs[0].shape) == 2:
+        totals = add_blocks([ref[...] for ref in line_refs], totals)
+    else:
+        totals = lax.fori_loop(
+            0,
+            line_refs[0].shape[0],
+            lambda number, value: add_blocks([line_refs[0][number]], value),
+            totals,
+        )
     for number, total in enumerate(totals):
         partial_ref[number] = total
 
@@ -77,6 +83,7 @@
     plane_refs = refs[:plane_count]
     probes_ref = refs[plane_count]
     partial_refs = refs[plane_count + 1 : -2]
+    partial_refs = [partial_refs[number] for number in EXCHANGE[plane_count]]
     image_ref, sums_ref = refs[-2:]
     probe_count = image_ref.shape[0]
     lane = lax.broadcasted_iota(jnp.int32, sums_ref.shape, 1)
@@ -132,10 +139,11 @@
 def everywhere(value, axes, count):
     if count > DIRECT:
         return [lax.all_gather(value, axes, axis=0, tiled=False)]
-    return [value] + [
-        lax.ppermute(value, axes, [(source_of(i, step, count), i) for i in range(count)])
-        for step in range(1, count)
-    ]
+    blocks = {0: value}
+    for step in range(1, count):
+        pairs = [(source_of(i, step, count), i) for i in range(count)]
+        blocks[step] = lax.ppermute(value, axes, pairs)
+    return [blocks[step] for step in range(count)]
 
 
 def plane_blocks(value, shape):
@@ -157,18 +165,19 @@
         line, plane = pl.pallas_call(
             pack_kernel,
             out_shape=(
-                jax.ShapeDtypeStruct((feature_count + 2 * HALF + probe_count, width), jnp.bfloat16),
+                jax.ShapeDtypeStruct((feature_count + probe_count, width), jnp.bfloat16),
                 jax.ShapeDtypeStruct((feature_count + 2 * probe_count, width), jnp.bfloat16),
             ),
             compiler_params=VMEM,
         )(scaled, probes)
         lines = everywhere(line, LINE, line_count)
-        planes = plane_blocks(plane, plane_shape)
+        planes = everywhere(plane, PLANE, plane_count)
         partial = pl.pallas_call(
             lambda *refs: image_kernel(feature_count, plane_count, *refs),
             out_shape=jax.ShapeDtypeStruct((plane_count, probe_count, width), jnp.float32),
             compiler_params=VMEM,
-        )(*planes, *lines, noise_var[None, :], probes)
+        )(*arranged(planes + lines, FORTH), noise_var[None, :], probes)
+        partials = everywhere(partial, PLANE, plane_count)
         image, sums = pl.pallas_call(
             lambda *refs: combine_kernel(feature_count, plane_count, *refs),
             out_shape=(
@@ -176,7 +185,7 @@
                 jax.ShapeDtypeStruct((probe_count, 128), jnp.float32),
             ),
             compiler_params=VMEM,
-        )(*planes, probes, *everywhere(partial, PLANE, plane_count))
+        )(*planes, probes, *[partials[number] for number in EXCHANGE[plane_count]])
         outs = (jax.ShapeDtypeStruct(probes.shape, jnp.float32),) * 3
         return pl.pallas_call(finish_kernel, out_shape=outs, compiler_params=VMEM)(
             image, probes, *everywhere(sums, LINE, line_count)

time: 31.5 us -> 30.5 us (0.968)
  Pallas kernels: 3.83 us -> 2.81 us
  waiting for transfers between devices: 11.8 us -> 11.1 us
  starting transfers between devices: 14 us -> 14.7 us
    pallas_call x1, Pallas kernels: 2.92 us -> 1.92 us  [local(): pl.pallas_call(lambda *refs: image_kernel(feature_count, plane_count, *re...]
    ppermute x12, starting transfers between devices: 14 us -> 14.7 us  [everywhere(): blocks[step] = lax.ppermute(value, axes, pairs)]
    ppermute x12, waiting for transfers between devices: 11.8 us -> 11.1 us  [everywhere(): blocks[step] = lax.ppermute(value, axes, pairs)]
  transfers between devices with their start and end apart: 12 -> 12, of which waited for: 6 -> 7; matrix products, arithmetic and copies ran while one was open for 0% -> 0% of each run, Pallas kernels for 0% -> 0%
where the time goes in v10:
time: 30.5 us; the launch traced here: 30.3 us
  starting transfers between devices  14.7 us (48%)
  waiting for transfers between devices  11.1 us (36%)
  Pallas kernels  2.81 us (9%)
  other arithmetic  0.93 us (3%)
  between operations  0.69 us (2%)
    ppermute x12, starting transfers between devices, everywhere(): blocks[step] = lax.ppermute(value, axes, pairs)  14.7 us
    ppermute x12, waiting for transfers between devices, everywhere(): blocks[step] = lax.ppermute(value, axes, pairs)  11.1 us
    pallas_call x1, Pallas kernels, local(): pl.pallas_call(lambda *refs: image_kernel(feature_count, plane_count, *re...  1.92 us
    convert_element_type x1, other arithmetic, local(): (features.astype(jnp.float32) / lengthscale[:, None]).astype(jnp.bfloat16)  0.93 us
    pallas_call x1, Pallas kernels, local(): pl.pallas_call(finish_kernel, out_shape=outs, compiler_params=VMEM)  0.77 us
  transfers between devices with their start and end apart: 12, of which 7 were waited for; matrix products, arithmetic and copies ran while one was open for 0% of the time, Pallas kernels for 0%

profile of v10, /device:TPU:0, one launch (start us, length us, event | category | flops | bytes accessed | tf_op | source)
XLA Modules:
  0.0 30.3 jit_solution(9221321992204430301)
XLA Ops:
  0.6 0.0 copy-start
  0.6 0.9 %divide_convert_fusion.scaled_ref = bf16[128,256]{1,0:T(8,128)(2,1)S(1)} fusion(bf16[128,256]{1,0:T(8,128)(2,1)} %param.4, f32[128]{0:T(128)} %param.5), kind=kLoop, calls=%fused_computation | loop fusion | flops 98304 | bytes 131584 | tf_op jit(solution)/shard_map/convert_element_type | solution.py:164
  1.6 0.0 copy-done
  1.6 5.1 %collective-permute-start.5 = (bf16[144,256]{1,0:T(8,128)(2,1)S(1)}, bf16[144,256]{1,0:T(8,128)(2,1)S(1)}, u32[]{:S(2)}, u32[]{:S(2)}) collective-permute-start(bf16[144,256]{1,0:T(8,128)(2,1)S(1)} %get-tuple-element.8.refs_1_), channel_id=1, source_target_pairs={{12,0},{8,4},{4,8},{0,12},{13,1},{9,5},{5,9},{1,13},{14,2},{10,6},... | collective-permute-start | bytes 221192 | tf_op jit(solution)/shard_map/ppermute | solution.py:145
  6.7 0.0 copy-start.1
  6.7 0.7 %collective-permute-start.2 = (bf16[160,256]{1,0:T(8,128)(2,1)S(1)}, bf16[160,256]{1,0:T(8,128)(2,1)S(1)}, u32[]{:S(2)}, u32[]{:S(2)}) collective-permute-start(bf16[160,256]{1,0:T(8,128)(2,1)S(1)} %get-tuple-element.7.refs_0_), channel_id=1, source_target_pairs={{3,0},{2,1},{1,2},{0,3},{7,4},{6,5},{5,6},{4,7},{11,8},{10,9},{9,1... | collective-permute-start | bytes 245768 | tf_op jit(solution)/shard_map/ppermute | solution.py:145
  7.4 0.9 %collective-permute-start.1 = (bf16[160,256]{1,0:T(8,128)(2,1)S(1)}, bf16[160,256]{1,0:T(8,128)(2,1)S(1)}, u32[]{:S(2)}, u32[]{:S(2)}) collective-permute-start(bf16[160,256]{1,0:T(8,128)(2,1)S(1)} %get-tuple-element.7.refs_0_), channel_id=1, source_target_pairs={{2,0},{3,1},{0,2},{1,3},{6,4},{7,5},{4,6},{5,7},{10,8},{11,9},{8,1... | collective-permute-start | bytes 245768 | tf_op jit(solution)/shard_map/ppermute | solution.py:145
  8.3 0.3 %collective-permute-start = (bf16[160,256]{1,0:T(8,128)(2,1)S(1)}, bf16[160,256]{1,0:T(8,128)(2,1)S(1)}, u32[]{:S(2)}, u32[]{:S(2)}) collective-permute-start(bf16[160,256]{1,0:T(8,128)(2,1)S(1)} %get-tuple-element.7.refs_0_), channel_id=1, source_target_pairs={{1,0},{0,1},{3,2},{2,3},{5,4},{4,5},{7,6},{6,7},{9,8},{8,9},{11,10... | collective-permute-start | bytes 245768 | tf_op jit(solution)/shard_map/ppermute | solution.py:145
  8.6 0.0 collective-permute-start.4
  8.6 0.5 %collective-permute-done.5.refs_6_ = bf16[144,256]{1,0:T(8,128)(2,1)S(1)} collective-permute-done((bf16[144,256]{1,0:T(8,128)(2,1)S(1)}, bf16[144,256]{1,0:T(8,128)(2,1)S(1)}, u32[]{:S(2)}, u32[]{:S(2)}) %collective-permute-start.5) | collective-permute-done | bytes 73760 | tf_op jit(solution)/shard_map/ppermute | solution.py:145
  9.1 1.2 %collective-permute-start.3 = (bf16[144,256]{1,0:T(8,128)(2,1)S(1)}, bf16[144,256]{1,0:T(8,128)(2,1)S(1)}, u32[]{:S(2)}, u32[]{:S(2)}) collective-permute-start(bf16[144,256]{1,0:T(8,128)(2,1)S(1)} %get-tuple-element.8.refs_1_), channel_id=1, source_target_pairs={{4,0},{0,4},{12,8},{8,12},{5,1},{1,5},{13,9},{9,13},{6,2},{2,6},{1... | collective-permute-start | bytes 221192 | tf_op jit(solution)/shard_map/ppermute | solution.py:145
  10.3 4.2 %collective-permute-done.4.refs_5_ = bf16[144,256]{1,0:T(8,128)(2,1)S(1)} collective-permute-done((bf16[144,256]{1,0:T(8,128)(2,1)S(1)}, bf16[144,256]{1,0:T(8,128)(2,1)S(1)}, u32[]{:S(2)}, u32[]{:S(2)}) %collective-permute-start.4) | collective-permute-done | bytes 73760 | tf_op jit(solution)/shard_map/ppermute | solution.py:145
  14.5 0.5 %collective-permute-done.3.refs_4_ = bf16[144,256]{1,0:T(8,128)(2,1)S(1)} collective-permute-done((bf16[144,256]{1,0:T(8,128)(2,1)S(1)}, bf16[144,256]{1,0:T(8,128)(2,1)S(1)}, u32[]{:S(2)}, u32[]{:S(2)}) %collective-permute-start.3) | collective-permute-done | bytes 73760 | tf_op jit(solution)/shard_map/ppermute | solution.py:145
  15.0 0.0 collective-permute-done.2.refs_3_
  15.0 0.0 collective-permute-done.1.refs_7_.refs_2_
  15.0 0.0 collective-permute-done.refs_2_.refs_1_
  15.0 0.0 copy-done.1
  15.0 1.9 %shard_map.68.refs_5_ = f32[4,16,256]{2,1,0:T(8,128)S(1)} custom-call(bf16[160,256]{1,0:T(8,128)(2,1)S(1)} %get-tuple-element.7.refs_0_, bf16[144,256]{1,0:T(8,128)(2,1)S(1)} %get-tuple-element.8.refs_1_, bf16[160,256]{1,0:T(8,128)(2,1)S(1)} %collective-permute-done.refs_2_.refs_1_, bf16[160,256]{1,0:T(8,128)(2,1)S(1)} %collective-permute-done.2.refs_3_, ...), custom_call_target="tpu_custom_call" | custom-call | tf_op jit(solution)/shard_map/pallas_call | solution.py:175
  17.0 1.7 %collective-permute-start.8 = (f32[4,16,256]{2,1,0:T(8,128)S(1)}, f32[4,16,256]{2,1,0:T(8,128)S(1)}, u32[]{:S(2)}, u32[]{:S(2)}) collective-permute-start(f32[4,16,256]{2,1,0:T(8,128)S(1)} %shard_map.68.refs_5_), channel_id=1, source_target_pairs={{2,0},{3,1},{0,2},{1,3},{6,4},{7,5},{4,6},{5,7},{10,8},{11,9},{8,1... | collective-permute-start | bytes 196616 | tf_op jit(solution)/shard_map/ppermute | solution.py:145
  18.6 0.0 collective-permute-start.7
  18.6 0.5 %collective-permute-start.6 = (f32[4,16,256]{2,1,0:T(8,128)S(1)}, f32[4,16,256]{2,1,0:T(8,128)S(1)}, u32[]{:S(2)}, u32[]{:S(2)}) collective-permute-start(f32[4,16,256]{2,1,0:T(8,128)S(1)} %shard_map.68.refs_5_), channel_id=1, source_target_pairs={{1,0},{0,1},{3,2},{2,3},{5,4},{4,5},{7,6},{6,7},{9,8},{8,9},{11,10... | collective-permute-start | bytes 196616 | tf_op jit(solution)/shard_map/ppermute | solution.py:145
  19.1 2.1 %collective-permute-done.8.refs_8_ = f32[4,16,256]{2,1,0:T(8,128)S(1)} collective-permute-done((f32[4,16,256]{2,1,0:T(8,128)S(1)}, f32[4,16,256]{2,1,0:T(8,128)S(1)}, u32[]{:S(2)}, u32[]{:S(2)}) %collective-permute-start.8) | collective-permute-done | bytes 65568 | tf_op jit(solution)/shard_map/ppermute | solution.py:145
  21.2 1.4 %collective-permute-done.7.refs_7_ = f32[4,16,256]{2,1,0:T(8,128)S(1)} collective-permute-done((f32[4,16,256]{2,1,0:T(8,128)S(1)}, f32[4,16,256]{2,1,0:T(8,128)S(1)}, u32[]{:S(2)}, u32[]{:S(2)}) %collective-permute-start.7) | collective-permute-done | bytes 65568 | tf_op jit(solution)/shard_map/ppermute | solution.py:145
  22.6 0.0 collective-permute-done.6.refs_6_
  22.6 0.1 shard_map.69
  22.7 2.3 %collective-permute-start.11 = (f32[16,128]{1,0:T(8,128)S(1)}, f32[16,128]{1,0:T(8,128)S(1)}, u32[]{:S(2)}, u32[]{:S(2)}) collective-permute-start(f32[16,128]{1,0:T(8,128)S(1)} %get-tuple-element.10.refs_0_), channel_id=1, source_target_pairs={{12,0},{8,4},{4,8},{0,12},{13,1},{9,5},{5,9},{1,13},{14,2},{10,6},... | collective-permute-start | bytes 24584 | tf_op jit(solution)/shard_map/ppermute | solution.py:145
  25.0 0.0 collective-permute-start.10
  25.0 2.1 %collective-permute-start.9 = (f32[16,128]{1,0:T(8,128)S(1)}, f32[16,128]{1,0:T(8,128)S(1)}, u32[]{:S(2)}, u32[]{:S(2)}) collective-permute-start(f32[16,128]{1,0:T(8,128)S(1)} %get-tuple-element.10.refs_0_), channel_id=1, source_target_pairs={{4,0},{0,4},{12,8},{8,12},{5,1},{1,5},{13,9},{9,13},{6,2},{2,6},{1... | collective-permute-start | bytes 24584 | tf_op jit(solution)/shard_map/ppermute | solution.py:145
  27.1 1.1 %collective-permute-done.11.refs_3_ = f32[16,128]{1,0:T(8,128)S(1)} collective-permute-done((f32[16,128]{1,0:T(8,128)S(1)}, f32[16,128]{1,0:T(8,128)S(1)}, u32[]{:S(2)}, u32[]{:S(2)}) %collective-permute-start.11) | collective-permute-done | bytes 8224 | tf_op jit(solution)/shard_map/ppermute | solution.py:145
  28.2 1.4 %collective-permute-done.10.refs_2_ = f32[16,128]{1,0:T(8,128)S(1)} collective-permute-done((f32[16,128]{1,0:T(8,128)S(1)}, f32[16,128]{1,0:T(8,128)S(1)}, u32[]{:S(2)}, u32[]{:S(2)}) %collective-permute-start.10) | collective-permute-done | bytes 8224 | tf_op jit(solution)/shard_map/ppermute | solution.py:145
  29.6 0.0 collective-permute-done.9.refs_1_
  29.6 0.8 %shard_map.70 = (f32[16,256]{1,0:T(8,128)}, f32[16,256]{1,0:T(8,128)}, f32[16,256]{1,0:T(8,128)}) custom-call(f32[16,256]{1,0:T(8,128)S(1)} %get-tuple-element.9.image_ref, f32[16,256]{1,0:T(8,128)S(1)} %copy-done, f32[16,128]{1,0:T(8,128)S(1)} %get-tuple-element.10.refs_0_, f32[16,128]{1,0:T(8,128)S(1)} %collective-permute-done.9.refs_1_, ...), custom_call_target="tpu_custom_call" | custom-call | tf_op jit(solution)/shard_map/pallas_call | solution.py:190
  (1 shorter events, 0.0 us)
Async XLA Ops:
  0.6 1.0 %copy-start = (f32[16,256]{1,0:T(8,128)S(1)}, f32[16,256]{1,0:T(8,128)}, u32[]{:S(2)}) copy-start(f32[16,256]{1,0:T(8,128)} %probes_ref.3) | copy-start | bytes 49156
  1.6 7.5 %collective-permute-start.5 = (bf16[144,256]{1,0:T(8,128)(2,1)S(1)}, bf16[144,256]{1,0:T(8,128)(2,1)S(1)}, u32[]{:S(2)}, u32[]{:S(2)}) collective-permute-start(bf16[144,256]{1,0:T(8,128)(2,1)S(1)} %get-tuple-element.8.refs_1_), channel_id=1, source_target_pairs={{12,0},{8,4},{4,8},{0,12},{13,1},{9,5},{5,9},{1,13},{14,2},{10,6},... | collective-permute-start | bytes 221192 | tf_op jit(solution)/shard_map/ppermute | solution.py:145
  6.7 8.3 %copy-start.1 = (f32[256]{0:T(256)S(1)}, f32[256]{0:T(256)}, u32[]{:S(2)}) copy-start(f32[256]{0:T(256)} %param.6) | copy-start | bytes 3076
  6.7 8.3 %collective-permute-start.2 = (bf16[160,256]{1,0:T(8,128)(2,1)S(1)}, bf16[160,256]{1,0:T(8,128)(2,1)S(1)}, u32[]{:S(2)}, u32[]{:S(2)}) collective-permute-start(bf16[160,256]{1,0:T(8,128)(2,1)S(1)} %get-tuple-element.7.refs_0_), channel_id=1, source_target_pairs={{3,0},{2,1},{1,2},{0,3},{7,4},{6,5},{5,6},{4,7},{11,8},{10,9},{9,1... | collective-permute-start | bytes 245768 | tf_op jit(solution)/shard_map/ppermute | solution.py:145
  7.4 7.6 %collective-permute-start.1 = (bf16[160,256]{1,0:T(8,128)(2,1)S(1)}, bf16[160,256]{1,0:T(8,128)(2,1)S(1)}, u32[]{:S(2)}, u32[]{:S(2)}) collective-permute-start(bf16[160,256]{1,0:T(8,128)(2,1)S(1)} %get-tuple-element.7.refs_0_), channel_id=1, source_target_pairs={{2,0},{3,1},{0,2},{1,3},{6,4},{7,5},{4,6},{5,7},{10,8},{11,9},{8,1... | collective-permute-start | bytes 245768 | tf_op jit(solution)/shard_map/ppermute | solution.py:145
  8.3 6.8 %collective-permute-start = (bf16[160,256]{1,0:T(8,128)(2,1)S(1)}, bf16[160,256]{1,0:T(8,128)(2,1)S(1)}, u32[]{:S(2)}, u32[]{:S(2)}) collective-permute-start(bf16[160,256]{1,0:T(8,128)(2,1)S(1)} %get-tuple-element.7.refs_0_), channel_id=1, source_target_pairs={{1,0},{0,1},{3,2},{2,3},{5,4},{4,5},{7,6},{6,7},{9,8},{8,9},{11,10... | collective-permute-start | bytes 245768 | tf_op jit(solution)/shard_map/ppermute | solution.py:145
  8.6 5.9 %collective-permute-start.4 = (bf16[144,256]{1,0:T(8,128)(2,1)S(1)}, bf16[144,256]{1,0:T(8,128)(2,1)S(1)}, u32[]{:S(2)}, u32[]{:S(2)}) collective-permute-start(bf16[144,256]{1,0:T(8,128)(2,1)S(1)} %get-tuple-element.8.refs_1_), channel_id=1, source_target_pairs={{8,0},{12,4},{0,8},{4,12},{9,1},{13,5},{1,9},{5,13},{10,2},{14,6},... | collective-permute-start | bytes 221192 | tf_op jit(solution)/shard_map/ppermute | solution.py:145
  9.1 5.9 %collective-permute-start.3 = (bf16[144,256]{1,0:T(8,128)(2,1)S(1)}, bf16[144,256]{1,0:T(8,128)(2,1)S(1)}, u32[]{:S(2)}, u32[]{:S(2)}) collective-permute-start(bf16[144,256]{1,0:T(8,128)(2,1)S(1)} %get-tuple-element.8.refs_1_), channel_id=1, source_target_pairs={{4,0},{0,4},{12,8},{8,12},{5,1},{1,5},{13,9},{9,13},{6,2},{2,6},{1... | collective-permute-start | bytes 221192 | tf_op jit(solution)/shard_map/ppermute | solution.py:145
  17.0 4.3 %collective-permute-start.8 = (f32[4,16,256]{2,1,0:T(8,128)S(1)}, f32[4,16,256]{2,1,0:T(8,128)S(1)}, u32[]{:S(2)}, u32[]{:S(2)}) collective-permute-start(f32[4,16,256]{2,1,0:T(8,128)S(1)} %shard_map.68.refs_5_), channel_id=1, source_target_pairs={{2,0},{3,1},{0,2},{1,3},{6,4},{7,5},{4,6},{5,7},{10,8},{11,9},{8,1... | collective-permute-start | bytes 196616 | tf_op jit(solution)/shard_map/ppermute | solution.py:145
  18.6 4.0 %collective-permute-start.7 = (f32[4,16,256]{2,1,0:T(8,128)S(1)}, f32[4,16,256]{2,1,0:T(8,128)S(1)}, u32[]{:S(2)}, u32[]{:S(2)}) collective-permute-start(f32[4,16,256]{2,1,0:T(8,128)S(1)} %shard_map.68.refs_5_), channel_id=1, source_target_pairs={{3,0},{2,1},{1,2},{0,3},{7,4},{6,5},{5,6},{4,7},{11,8},{10,9},{9,1... | collective-permute-start | bytes 196616 | tf_op jit(solution)/shard_map/ppermute | solution.py:145
  18.6 4.0 %collective-permute-start.6 = (f32[4,16,256]{2,1,0:T(8,128)S(1)}, f32[4,16,256]{2,1,0:T(8,128)S(1)}, u32[]{:S(2)}, u32[]{:S(2)}) collective-permute-start(f32[4,16,256]{2,1,0:T(8,128)S(1)} %shard_map.68.refs_5_), channel_id=1, source_target_pairs={{1,0},{0,1},{3,2},{2,3},{5,4},{4,5},{7,6},{6,7},{9,8},{8,9},{11,10... | collective-permute-start | bytes 196616 | tf_op jit(solution)/shard_map/ppermute | solution.py:145
  22.7 5.5 %collective-permute-start.11 = (f32[16,128]{1,0:T(8,128)S(1)}, f32[16,128]{1,0:T(8,128)S(1)}, u32[]{:S(2)}, u32[]{:S(2)}) collective-permute-start(f32[16,128]{1,0:T(8,128)S(1)} %get-tuple-element.10.refs_0_), channel_id=1, source_target_pairs={{12,0},{8,4},{4,8},{0,12},{13,1},{9,5},{5,9},{1,13},{14,2},{10,6},... | collective-permute-start | bytes 24584 | tf_op jit(solution)/shard_map/ppermute | solution.py:145
  25.0 4.5 %collective-permute-start.10 = (f32[16,128]{1,0:T(8,128)S(1)}, f32[16,128]{1,0:T(8,128)S(1)}, u32[]{:S(2)}, u32[]{:S(2)}) collective-permute-start(f32[16,128]{1,0:T(8,128)S(1)} %get-tuple-element.10.refs_0_), channel_id=1, source_target_pairs={{8,0},{12,4},{0,8},{4,12},{9,1},{13,5},{1,9},{5,13},{10,2},{14,6},... | collective-permute-start | bytes 24584 | tf_op jit(solution)/shard_map/ppermute | solution.py:145
  25.0 4.5 %collective-permute-start.9 = (f32[16,128]{1,0:T(8,128)S(1)}, f32[16,128]{1,0:T(8,128)S(1)}, u32[]{:S(2)}, u32[]{:S(2)}) collective-permute-start(f32[16,128]{1,0:T(8,128)S(1)} %get-tuple-element.10.refs_0_), channel_id=1, source_target_pairs={{4,0},{0,4},{12,8},{8,12},{5,1},{1,5},{13,9},{9,13},{6,2},{2,6},{1... | collective-permute-start | bytes 24584 | tf_op jit(solution)/shard_map/ppermute | solution.py:145

commit v11 on v9

--- a/solution.py
+++ b/solution.py
@@ -9,6 +9,7 @@
 LINE = ("blk",)
 DIRECT = 8
 VMEM = pltpu.CompilerParams(vmem_limit_bytes=40 * 1024 * 1024)
+LOG2_E = 1.4426950408889634
 HALF = 8
 
 
@@ -54,7 +55,7 @@
         result = []
         for own, total in zip(rows, totals):
             exponent = jnp.dot(columns, own, preferred_element_type=jnp.float32)
-            weights = jnp.exp(exponent).astype(jnp.bfloat16)
+            weights = jnp.exp2(exponent * LOG2_E).astype(jnp.bfloat16)
             result.append(total + jnp.dot(probes, weights, preferred_element_type=jnp.float32))
         return result
 

time: 30 us -> 30 us (level)
  no operation moved by 1% of the time
where the time goes in v11:
time: 30 us; the launch traced here: 29.8 us
  starting transfers between devices  14.4 us (48%)
  waiting for transfers between devices  11 us (37%)
  Pallas kernels  2.78 us (9%)
  other arithmetic  0.93 us (3%)
  between operations  0.68 us (2%)
    ppermute x12, starting transfers between devices, everywhere(): lax.ppermute(value, axes, [(source_of(i, step, count), i) for i in range(...  14.4 us
    ppermute x12, waiting for transfers between devices, everywhere(): lax.ppermute(value, axes, [(source_of(i, step, count), i) for i in range(...  11 us
    pallas_call x1, Pallas kernels, local(): pl.pallas_call(lambda *refs: image_kernel(feature_count, plane_count, *re...  1.9 us
    convert_element_type x1, other arithmetic, local(): (features.astype(jnp.float32) / lengthscale[:, None]).astype(jnp.bfloat16)  0.93 us
    pallas_call x1, Pallas kernels, local(): pl.pallas_call(finish_kernel, out_shape=outs, compiler_params=VMEM)  0.77 us
  transfers between devices with their start and end apart: 12, of which 6 were waited for; matrix products, arithmetic and copies ran while one was open for 0% of the time, Pallas kernels for 0%

profile of v11, /device:TPU:0, one launch (start us, length us, event | category | flops | bytes accessed | tf_op | source)
XLA Modules:
  0.0 29.8 jit_solution(16767856230585116573)
XLA Ops:
  0.6 0.0 copy-start
  0.6 0.9 %divide_convert_fusion.scaled_ref.refs_0_ = bf16[128,256]{1,0:T(8,128)(2,1)S(1)} fusion(bf16[128,256]{1,0:T(8,128)(2,1)} %param.4, f32[128]{0:T(128)} %param.5), kind=kLoop, calls=%fused_computation | loop fusion | flops 98304 | bytes 131584 | tf_op jit(solution)/shard_map/convert_element_type | solution.py:155
  1.6 0.5 %collective-permute-start = (bf16[128,256]{1,0:T(8,128)(2,1)S(1)}, bf16[128,256]{1,0:T(8,128)(2,1)S(1)}, u32[]{:S(2)}, u32[]{:S(2)}) collective-permute-start(bf16[128,256]{1,0:T(8,128)(2,1)S(1)} %divide_convert_fusion.scaled_ref.refs_0_), channel_id=1, source_target_pairs={{1,0},{0,1},{3,2},{2,3},{5,4},{4,5},{7,6},{6,7},{9,8},{8,9},{11,10... | collective-permute-start | bytes 196616 | tf_op jit(solution)/shard_map/ppermute | solution.py:135
  2.1 0.0 copy-done
  2.1 0.0 copy-start.1
  2.1 4.7 %collective-permute-start.5 = (bf16[144,256]{1,0:T(8,128)(2,1)S(1)}, bf16[144,256]{1,0:T(8,128)(2,1)S(1)}, u32[]{:S(2)}, u32[]{:S(2)}) collective-permute-start(bf16[144,256]{1,0:T(8,128)(2,1)S(1)} %shard_map.67.refs_4_), channel_id=1, source_target_pairs={{12,0},{8,4},{4,8},{0,12},{13,1},{9,5},{5,9},{1,13},{14,2},{10,6},... | collective-permute-start | bytes 221192 | tf_op jit(solution)/shard_map/ppermute | solution.py:135
  6.8 0.0 collective-permute-start.4
  6.8 0.6 %collective-permute-start.3 = (bf16[144,256]{1,0:T(8,128)(2,1)S(1)}, bf16[144,256]{1,0:T(8,128)(2,1)S(1)}, u32[]{:S(2)}, u32[]{:S(2)}) collective-permute-start(bf16[144,256]{1,0:T(8,128)(2,1)S(1)} %shard_map.67.refs_4_), channel_id=1, source_target_pairs={{4,0},{0,4},{12,8},{8,12},{5,1},{1,5},{13,9},{9,13},{6,2},{2,6},{1... | collective-permute-start | bytes 221192 | tf_op jit(solution)/shard_map/ppermute | solution.py:135
  7.5 1.6 %collective-permute-start.1 = (bf16[128,256]{1,0:T(8,128)(2,1)S(1)}, bf16[128,256]{1,0:T(8,128)(2,1)S(1)}, u32[]{:S(2)}, u32[]{:S(2)}) collective-permute-start(bf16[128,256]{1,0:T(8,128)(2,1)S(1)} %divide_convert_fusion.scaled_ref.refs_0_), channel_id=1, source_target_pairs={{2,0},{0,2},{3,1},{1,3},{6,4},{4,6},{7,5},{5,7},{10,8},{8,10},{11,... | collective-permute-start | bytes 196616 | tf_op jit(solution)/shard_map/ppermute | solution.py:135
  9.1 0.0 collective-permute-done.refs_1_
  9.1 0.4 %collective-permute-start.2 = (bf16[128,256]{1,0:T(8,128)(2,1)S(1)}, bf16[128,256]{1,0:T(8,128)(2,1)S(1)}, u32[]{:S(2)}, u32[]{:S(2)}) collective-permute-start(bf16[128,256]{1,0:T(8,128)(2,1)S(1)} %collective-permute-done.refs_1_), channel_id=1, source_target_pairs={{2,0},{0,2},{3,1},{1,3},{6,4},{4,6},{7,5},{5,7},{10,8},{8,10},{11,... | collective-permute-start | bytes 196616 | tf_op jit(solution)/shard_map/ppermute | solution.py:135
  9.5 2.8 %collective-permute-done.1.refs_2_ = bf16[128,256]{1,0:T(8,128)(2,1)S(1)} collective-permute-done((bf16[128,256]{1,0:T(8,128)(2,1)S(1)}, bf16[128,256]{1,0:T(8,128)(2,1)S(1)}, u32[]{:S(2)}, u32[]{:S(2)}) %collective-permute-start.1) | collective-permute-done | bytes 65568 | tf_op jit(solution)/shard_map/ppermute | solution.py:135
  12.3 0.0 collective-permute-done.5.refs_7_
  12.3 1.4 %collective-permute-done.4.refs_6_ = bf16[144,256]{1,0:T(8,128)(2,1)S(1)} collective-permute-done((bf16[144,256]{1,0:T(8,128)(2,1)S(1)}, bf16[144,256]{1,0:T(8,128)(2,1)S(1)}, u32[]{:S(2)}, u32[]{:S(2)}) %collective-permute-start.4) | collective-permute-done | bytes 73760 | tf_op jit(solution)/shard_map/ppermute | solution.py:135
  13.6 0.0 collective-permute-done.3.refs_5_
  13.6 0.0 collective-permute-done.2.refs_3_
  13.6 0.0 copy-done.1
  13.6 1.9 %shard_map.68.refs_0_ = f32[5,16,256]{2,1,0:T(8,128)S(1)} custom-call(bf16[128,256]{1,0:T(8,128)(2,1)S(1)} %divide_convert_fusion.scaled_ref.refs_0_, bf16[128,256]{1,0:T(8,128)(2,1)S(1)} %collective-permute-done.refs_1_, bf16[128,256]{1,0:T(8,128)(2,1)S(1)} %collective-permute-done.1.refs_2_, bf16[128,256]{1,0:T(8,128)(2,1)S(1)} %collective-permute-done.2.refs_3_, ...), custom_call_target="tpu_custom_call" | custom-call | tf_op jit(solution)/shard_map/pallas_call | solution.py:163
  15.5 1.5 %collective-permute-start.8 = (f32[5,16,256]{2,1,0:T(8,128)S(1)}, f32[5,16,256]{2,1,0:T(8,128)S(1)}, u32[]{:S(2)}, u32[]{:S(2)}) collective-permute-start(f32[5,16,256]{2,1,0:T(8,128)S(1)} %shard_map.68.refs_0_), channel_id=1, source_target_pairs={{2,0},{3,1},{0,2},{1,3},{6,4},{7,5},{4,6},{5,7},{10,8},{11,9},{8,1... | collective-permute-start | bytes 245768 | tf_op jit(solution)/shard_map/ppermute | solution.py:135
  17.0 0.0 collective-permute-start.7
  17.0 0.6 %collective-permute-start.6 = (f32[5,16,256]{2,1,0:T(8,128)S(1)}, f32[5,16,256]{2,1,0:T(8,128)S(1)}, u32[]{:S(2)}, u32[]{:S(2)}) collective-permute-start(f32[5,16,256]{2,1,0:T(8,128)S(1)} %shard_map.68.refs_0_), channel_id=1, source_target_pairs={{1,0},{0,1},{3,2},{2,3},{5,4},{4,5},{7,6},{6,7},{9,8},{8,9},{11,10... | collective-permute-start | bytes 245768 | tf_op jit(solution)/shard_map/ppermute | solution.py:135
  17.7 2.3 %collective-permute-done.8.refs_3_ = f32[5,16,256]{2,1,0:T(8,128)S(1)} collective-permute-done((f32[5,16,256]{2,1,0:T(8,128)S(1)}, f32[5,16,256]{2,1,0:T(8,128)S(1)}, u32[]{:S(2)}, u32[]{:S(2)}) %collective-permute-start.8) | collective-permute-done | bytes 81952 | tf_op jit(solution)/shard_map/ppermute | solution.py:135
  20.0 1.8 %collective-permute-done.7.refs_2_ = f32[5,16,256]{2,1,0:T(8,128)S(1)} collective-permute-done((f32[5,16,256]{2,1,0:T(8,128)S(1)}, f32[5,16,256]{2,1,0:T(8,128)S(1)}, u32[]{:S(2)}, u32[]{:S(2)}) %collective-permute-start.7) | collective-permute-done | bytes 81952 | tf_op jit(solution)/shard_map/ppermute | solution.py:135
  21.7 0.0 collective-permute-done.6.refs_1_
  21.7 0.1 shard_map.69
  21.9 2.7 %collective-permute-start.11 = (f32[16,128]{1,0:T(8,128)S(1)}, f32[16,128]{1,0:T(8,128)S(1)}, u32[]{:S(2)}, u32[]{:S(2)}) collective-permute-start(f32[16,128]{1,0:T(8,128)S(1)} %get-tuple-element.6.refs_0_), channel_id=1, source_target_pairs={{12,0},{8,4},{4,8},{0,12},{13,1},{9,5},{5,9},{1,13},{14,2},{10,6},... | collective-permute-start | bytes 24584 | tf_op jit(solution)/shard_map/ppermute | solution.py:135
  24.5 0.0 collective-permute-start.10
  24.5 1.7 %collective-permute-start.9 = (f32[16,128]{1,0:T(8,128)S(1)}, f32[16,128]{1,0:T(8,128)S(1)}, u32[]{:S(2)}, u32[]{:S(2)}) collective-permute-start(f32[16,128]{1,0:T(8,128)S(1)} %get-tuple-element.6.refs_0_), channel_id=1, source_target_pairs={{4,0},{0,4},{12,8},{8,12},{5,1},{1,5},{13,9},{9,13},{6,2},{2,6},{1... | collective-permute-start | bytes 24584 | tf_op jit(solution)/shard_map/ppermute | solution.py:135
  26.2 1.1 %collective-permute-done.11.refs_3_ = f32[16,128]{1,0:T(8,128)S(1)} collective-permute-done((f32[16,128]{1,0:T(8,128)S(1)}, f32[16,128]{1,0:T(8,128)S(1)}, u32[]{:S(2)}, u32[]{:S(2)}) %collective-permute-start.11) | collective-permute-done | bytes 8224 | tf_op jit(solution)/shard_map/ppermute | solution.py:135
  27.3 1.8 %collective-permute-done.10.refs_2_ = f32[16,128]{1,0:T(8,128)S(1)} collective-permute-done((f32[16,128]{1,0:T(8,128)S(1)}, f32[16,128]{1,0:T(8,128)S(1)}, u32[]{:S(2)}, u32[]{:S(2)}) %collective-permute-start.10) | collective-permute-done | bytes 8224 | tf_op jit(solution)/shard_map/ppermute | solution.py:135
  29.1 0.0 collective-permute-done.9.refs_1_
  29.1 0.8 %shard_map.70 = (f32[16,256]{1,0:T(8,128)}, f32[16,256]{1,0:T(8,128)}, f32[16,256]{1,0:T(8,128)}) custom-call(f32[16,256]{1,0:T(8,128)S(1)} %get-tuple-element.5.image_ref, f32[16,256]{1,0:T(8,128)S(1)} %copy-done, f32[16,128]{1,0:T(8,128)S(1)} %get-tuple-element.6.refs_0_, f32[16,128]{1,0:T(8,128)S(1)} %collective-permute-done.9.refs_1_, ...), custom_call_target="tpu_custom_call" | custom-call | tf_op jit(solution)/shard_map/pallas_call | solution.py:178
  (1 shorter events, 0.0 us)
Async XLA Ops:
  0.6 1.5 %copy-start = (f32[16,256]{1,0:T(8,128)S(1)}, f32[16,256]{1,0:T(8,128)}, u32[]{:S(2)}) copy-start(f32[16,256]{1,0:T(8,128)} %probes_ref.3) | copy-start | bytes 49156
  1.6 7.5 %collective-permute-start = (bf16[128,256]{1,0:T(8,128)(2,1)S(1)}, bf16[128,256]{1,0:T(8,128)(2,1)S(1)}, u32[]{:S(2)}, u32[]{:S(2)}) collective-permute-start(bf16[128,256]{1,0:T(8,128)(2,1)S(1)} %divide_convert_fusion.scaled_ref.refs_0_), channel_id=1, source_target_pairs={{1,0},{0,1},{3,2},{2,3},{5,4},{4,5},{7,6},{6,7},{9,8},{8,9},{11,10... | collective-permute-start | bytes 196616 | tf_op jit(solution)/shard_map/ppermute | solution.py:135
  2.1 11.5 %copy-start.1 = (f32[256]{0:T(256)S(1)}, f32[256]{0:T(256)}, u32[]{:S(2)}) copy-start(f32[256]{0:T(256)} %param.6) | copy-start | bytes 3076
  2.1 10.1 %collective-permute-start.5 = (bf16[144,256]{1,0:T(8,128)(2,1)S(1)}, bf16[144,256]{1,0:T(8,128)(2,1)S(1)}, u32[]{:S(2)}, u32[]{:S(2)}) collective-permute-start(bf16[144,256]{1,0:T(8,128)(2,1)S(1)} %shard_map.67.refs_4_), channel_id=1, source_target_pairs={{12,0},{8,4},{4,8},{0,12},{13,1},{9,5},{5,9},{1,13},{14,2},{10,6},... | collective-permute-start | bytes 221192 | tf_op jit(solution)/shard_map/ppermute | solution.py:135
  6.8 6.8 %collective-permute-start.4 = (bf16[144,256]{1,0:T(8,128)(2,1)S(1)}, bf16[144,256]{1,0:T(8,128)(2,1)S(1)}, u32[]{:S(2)}, u32[]{:S(2)}) collective-permute-start(bf16[144,256]{1,0:T(8,128)(2,1)S(1)} %shard_map.67.refs_4_), channel_id=1, source_target_pairs={{8,0},{12,4},{0,8},{4,12},{9,1},{13,5},{1,9},{5,13},{10,2},{14,6},... | collective-permute-start | bytes 221192 | tf_op jit(solution)/shard_map/ppermute | solution.py:135
  6.8 6.8 %collective-permute-start.3 = (bf16[144,256]{1,0:T(8,128)(2,1)S(1)}, bf16[144,256]{1,0:T(8,128)(2,1)S(1)}, u32[]{:S(2)}, u32[]{:S(2)}) collective-permute-start(bf16[144,256]{1,0:T(8,128)(2,1)S(1)} %shard_map.67.refs_4_), channel_id=1, source_target_pairs={{4,0},{0,4},{12,8},{8,12},{5,1},{1,5},{13,9},{9,13},{6,2},{2,6},{1... | collective-permute-start | bytes 221192 | tf_op jit(solution)/shard_map/ppermute | solution.py:135
  7.5 4.8 %collective-permute-start.1 = (bf16[128,256]{1,0:T(8,128)(2,1)S(1)}, bf16[128,256]{1,0:T(8,128)(2,1)S(1)}, u32[]{:S(2)}, u32[]{:S(2)}) collective-permute-start(bf16[128,256]{1,0:T(8,128)(2,1)S(1)} %divide_convert_fusion.scaled_ref.refs_0_), channel_id=1, source_target_pairs={{2,0},{0,2},{3,1},{1,3},{6,4},{4,6},{7,5},{5,7},{10,8},{8,10},{11,... | collective-permute-start | bytes 196616 | tf_op jit(solution)/shard_map/ppermute | solution.py:135
  9.1 4.5 %collective-permute-start.2 = (bf16[128,256]{1,0:T(8,128)(2,1)S(1)}, bf16[128,256]{1,0:T(8,128)(2,1)S(1)}, u32[]{:S(2)}, u32[]{:S(2)}) collective-permute-start(bf16[128,256]{1,0:T(8,128)(2,1)S(1)} %collective-permute-done.refs_1_), channel_id=1, source_target_pairs={{2,0},{0,2},{3,1},{1,3},{6,4},{4,6},{7,5},{5,7},{10,8},{8,10},{11,... | collective-permute-start | bytes 196616 | tf_op jit(solution)/shard_map/ppermute | solution.py:135
  15.5 4.4 %collective-permute-start.8 = (f32[5,16,256]{2,1,0:T(8,128)S(1)}, f32[5,16,256]{2,1,0:T(8,128)S(1)}, u32[]{:S(2)}, u32[]{:S(2)}) collective-permute-start(f32[5,16,256]{2,1,0:T(8,128)S(1)} %shard_map.68.refs_0_), channel_id=1, source_target_pairs={{2,0},{3,1},{0,2},{1,3},{6,4},{7,5},{4,6},{5,7},{10,8},{11,9},{8,1... | collective-permute-start | bytes 245768 | tf_op jit(solution)/shard_map/ppermute | solution.py:135
  17.0 4.7 %collective-permute-start.7 = (f32[5,16,256]{2,1,0:T(8,128)S(1)}, f32[5,16,256]{2,1,0:T(8,128)S(1)}, u32[]{:S(2)}, u32[]{:S(2)}) collective-permute-start(f32[5,16,256]{2,1,0:T(8,128)S(1)} %shard_map.68.refs_0_), channel_id=1, source_target_pairs={{3,0},{2,1},{1,2},{0,3},{7,4},{6,5},{5,6},{4,7},{11,8},{10,9},{9,1... | collective-permute-start | bytes 245768 | tf_op jit(solution)/shard_map/ppermute | solution.py:135
  17.0 4.7 %collective-permute-start.6 = (f32[5,16,256]{2,1,0:T(8,128)S(1)}, f32[5,16,256]{2,1,0:T(8,128)S(1)}, u32[]{:S(2)}, u32[]{:S(2)}) collective-permute-start(f32[5,16,256]{2,1,0:T(8,128)S(1)} %shard_map.68.refs_0_), channel_id=1, source_target_pairs={{1,0},{0,1},{3,2},{2,3},{5,4},{4,5},{7,6},{6,7},{9,8},{8,9},{11,10... | collective-permute-start | bytes 245768 | tf_op jit(solution)/shard_map/ppermute | solution.py:135
  21.9 5.5 %collective-permute-start.11 = (f32[16,128]{1,0:T(8,128)S(1)}, f32[16,128]{1,0:T(8,128)S(1)}, u32[]{:S(2)}, u32[]{:S(2)}) collective-permute-start(f32[16,128]{1,0:T(8,128)S(1)} %get-tuple-element.6.refs_0_), channel_id=1, source_target_pairs={{12,0},{8,4},{4,8},{0,12},{13,1},{9,5},{5,9},{1,13},{14,2},{10,6},... | collective-permute-start | bytes 24584 | tf_op jit(solution)/shard_map/ppermute | solution.py:135
  24.5 4.5 %collective-permute-start.10 = (f32[16,128]{1,0:T(8,128)S(1)}, f32[16,128]{1,0:T(8,128)S(1)}, u32[]{:S(2)}, u32[]{:S(2)}) collective-permute-start(f32[16,128]{1,0:T(8,128)S(1)} %get-tuple-element.6.refs_0_), channel_id=1, source_target_pairs={{8,0},{12,4},{0,8},{4,12},{9,1},{13,5},{1,9},{5,13},{10,2},{14,6},... | collective-permute-start | bytes 24584 | tf_op jit(solution)/shard_map/ppermute | solution.py:135
  24.5 4.5 %collective-permute-start.9 = (f32[16,128]{1,0:T(8,128)S(1)}, f32[16,128]{1,0:T(8,128)S(1)}, u32[]{:S(2)}, u32[]{:S(2)}) collective-permute-start(f32[16,128]{1,0:T(8,128)S(1)} %get-tuple-element.6.refs_0_), channel_id=1, source_target_pairs={{4,0},{0,4},{12,8},{8,12},{5,1},{1,5},{13,9},{9,13},{6,2},{2,6},{1... | collective-permute-start | bytes 24584 | tf_op jit(solution)/shard_map/ppermute | solution.py:135

commit v12 on v11

--- a/solution.py
+++ b/solution.py
@@ -42,36 +42,39 @@
     plane_refs = refs[:plane_count]
     line_refs = refs[plane_count:-3]
     noise_ref, probes_ref, partial_ref = refs[-3:]
-    rows = [jnp.concatenate([ref[...], norm_rows(ref[...], 1)], axis=0) for ref in plane_refs]
+    width = partial_ref.shape[2]
+    rows = []
+    for ref in plane_refs:
+        own = jnp.concatenate([ref[...], norm_rows(ref[...], 1)], axis=0)
+        rows.append(own.astype(jnp.float32).T.astype(jnp.bfloat16))
+    rows = jnp.concatenate(rows, axis=0)
 
-    def add_blocks(blocks, totals):
-        columns = []
-        for block in blocks:
-            scaled = block[:feature_count, :]
-            block_columns = jnp.concatenate([scaled, norm_rows(scaled, 0)], axis=0)
-            columns.append(block_columns.astype(jnp.float32).T.astype(jnp.bfloat16))
-        columns = jnp.concatenate(columns, axis=0)
-        probes = jnp.concatenate([block[feature_count:, :] for block in blocks], axis=1)
-        result = []
-        for own, total in zip(rows, totals):
-            exponent = jnp.dot(columns, own, preferred_element_type=jnp.float32)
-            weights = jnp.exp2(exponent * LOG2_E).astype(jnp.bfloat16)
-            result.append(total + jnp.dot(probes, weights, preferred_element_type=jnp.float32))
-        return result
+    def add_block(block, total):
+        scaled = block[:feature_count, :]
+        columns = jnp.concatenate([scaled, norm_rows(scaled, 0)], axis=0)
+        exponent = jnp.dot(rows, columns, preferred_element_type=jnp.float32)
+        weights = jnp.exp2(exponent * LOG2_E).astype(jnp.bfloat16)
+        return total + lax.dot_general(
+            weights,
+            block[feature_count:, :],
+            (((1,), (1,)), ((), ())),
+            preferred_element_type=jnp.float32,
+        )
 
-    totals = [noise_ref[...] * probes_ref[...]]
-    totals += [jnp.zeros(probes_ref.shape, jnp.float32)] * (plane_count - 1)
+    total = jnp.zeros((plane_count * width, probes_ref.shape[0]), jnp.float32)
     if len(line_refs[0].shape) == 2:
-        totals = add_blocks([ref[...] for ref in line_refs], totals)
+        for ref in line_refs:
+            total = add_block(ref[...], total)
     else:
-        totals = lax.fori_loop(
+        total = lax.fori_loop(
             0,
             line_refs[0].shape[0],
-            lambda number, value: add_blocks([line_refs[0][number]], value),
-            totals,
+            lambda number, value: add_block(line_refs[0][number], value),
+            total,
         )
-    for number, total in enumerate(totals):
-        partial_ref[number] = total
+    for number in range(plane_count):
+        partial_ref[number] = total[number * width : (number + 1) * width, :].T
+    partial_ref[0] += noise_ref[...] * probes_ref[...]
     partial_ref[plane_count] = probes_ref[...]
 
 

time: 30 us -> 30 us (level)
  no operation moved by 1% of the time
where the time goes in v12:
time: 30 us; the launch traced here: 29.9 us
  starting transfers between devices  14.4 us (48%)
  waiting for transfers between devices  11 us (37%)
  Pallas kernels  2.78 us (9%)
  other arithmetic  0.93 us (3%)
  between operations  0.68 us (2%)
    ppermute x12, starting transfers between devices, everywhere(): lax.ppermute(value, axes, [(source_of(i, step, count), i) for i in range(...  14.4 us
    ppermute x12, waiting for transfers between devices, everywhere(): lax.ppermute(value, axes, [(source_of(i, step, count), i) for i in range(...  11 us
    pallas_call x1, Pallas kernels, local(): pl.pallas_call(lambda *refs: image_kernel(feature_count, plane_count, *re...  1.9 us
    convert_element_type x1, other arithmetic, local(): (features.astype(jnp.float32) / lengthscale[:, None]).astype(jnp.bfloat16)  0.93 us
    pallas_call x1, Pallas kernels, local(): pl.pallas_call(finish_kernel, out_shape=outs, compiler_params=VMEM)  0.77 us
  transfers between devices with their start and end apart: 12, of which 6 were waited for; matrix products, arithmetic and copies ran while one was open for 0% of the time, Pallas kernels for 0%

profile of v12, /device:TPU:0, one launch (start us, length us, event | category | flops | bytes accessed | tf_op | source)
XLA Modules:
  0.0 29.9 jit_solution(17693508083565789197)
XLA Ops:
  0.6 0.0 copy-start
  0.6 0.9 %divide_convert_fusion.scaled_ref.refs_0_ = bf16[128,256]{1,0:T(8,128)(2,1)S(1)} fusion(bf16[128,256]{1,0:T(8,128)(2,1)} %param.4, f32[128]{0:T(128)} %param.5), kind=kLoop, calls=%fused_computation | loop fusion | flops 98304 | bytes 131584 | tf_op jit(solution)/shard_map/convert_element_type | solution.py:158
  1.6 0.5 %collective-permute-start = (bf16[128,256]{1,0:T(8,128)(2,1)S(1)}, bf16[128,256]{1,0:T(8,128)(2,1)S(1)}, u32[]{:S(2)}, u32[]{:S(2)}) collective-permute-start(bf16[128,256]{1,0:T(8,128)(2,1)S(1)} %divide_convert_fusion.scaled_ref.refs_0_), channel_id=1, source_target_pairs={{1,0},{0,1},{3,2},{2,3},{5,4},{4,5},{7,6},{6,7},{9,8},{8,9},{11,10... | collective-permute-start | bytes 196616 | tf_op jit(solution)/shard_map/ppermute | solution.py:138
  2.1 0.0 copy-done
  2.1 0.0 copy-start.1
  2.1 4.7 %collective-permute-start.5 = (bf16[144,256]{1,0:T(8,128)(2,1)S(1)}, bf16[144,256]{1,0:T(8,128)(2,1)S(1)}, u32[]{:S(2)}, u32[]{:S(2)}) collective-permute-start(bf16[144,256]{1,0:T(8,128)(2,1)S(1)} %shard_map.67.refs_4_), channel_id=1, source_target_pairs={{12,0},{8,4},{4,8},{0,12},{13,1},{9,5},{5,9},{1,13},{14,2},{10,6},... | collective-permute-start | bytes 221192 | tf_op jit(solution)/shard_map/ppermute | solution.py:138
  6.8 0.0 collective-permute-start.4
  6.8 0.6 %collective-permute-start.3 = (bf16[144,256]{1,0:T(8,128)(2,1)S(1)}, bf16[144,256]{1,0:T(8,128)(2,1)S(1)}, u32[]{:S(2)}, u32[]{:S(2)}) collective-permute-start(bf16[144,256]{1,0:T(8,128)(2,1)S(1)} %shard_map.67.refs_4_), channel_id=1, source_target_pairs={{4,0},{0,4},{12,8},{8,12},{5,1},{1,5},{13,9},{9,13},{6,2},{2,6},{1... | collective-permute-start | bytes 221192 | tf_op jit(solution)/shard_map/ppermute | solution.py:138
  7.5 1.6 %collective-permute-start.1 = (bf16[128,256]{1,0:T(8,128)(2,1)S(1)}, bf16[128,256]{1,0:T(8,128)(2,1)S(1)}, u32[]{:S(2)}, u32[]{:S(2)}) collective-permute-start(bf16[128,256]{1,0:T(8,128)(2,1)S(1)} %divide_convert_fusion.scaled_ref.refs_0_), channel_id=1, source_target_pairs={{2,0},{0,2},{3,1},{1,3},{6,4},{4,6},{7,5},{5,7},{10,8},{8,10},{11,... | collective-permute-start | bytes 196616 | tf_op jit(solution)/shard_map/ppermute | solution.py:138
  9.1 0.0 collective-permute-done.refs_1_
  9.1 0.4 %collective-permute-start.2 = (bf16[128,256]{1,0:T(8,128)(2,1)S(1)}, bf16[128,256]{1,0:T(8,128)(2,1)S(1)}, u32[]{:S(2)}, u32[]{:S(2)}) collective-permute-start(bf16[128,256]{1,0:T(8,128)(2,1)S(1)} %collective-permute-done.refs_1_), channel_id=1, source_target_pairs={{2,0},{0,2},{3,1},{1,3},{6,4},{4,6},{7,5},{5,7},{10,8},{8,10},{11,... | collective-permute-start | bytes 196616 | tf_op jit(solution)/shard_map/ppermute | solution.py:138
  9.5 2.8 %collective-permute-done.1.refs_2_ = bf16[128,256]{1,0:T(8,128)(2,1)S(1)} collective-permute-done((bf16[128,256]{1,0:T(8,128)(2,1)S(1)}, bf16[128,256]{1,0:T(8,128)(2,1)S(1)}, u32[]{:S(2)}, u32[]{:S(2)}) %collective-permute-start.1) | collective-permute-done | bytes 65568 | tf_op jit(solution)/shard_map/ppermute | solution.py:138
  12.3 0.0 collective-permute-done.5.refs_7_
  12.3 1.4 %collective-permute-done.4.refs_6_ = bf16[144,256]{1,0:T(8,128)(2,1)S(1)} collective-permute-done((bf16[144,256]{1,0:T(8,128)(2,1)S(1)}, bf16[144,256]{1,0:T(8,128)(2,1)S(1)}, u32[]{:S(2)}, u32[]{:S(2)}) %collective-permute-start.4) | collective-permute-done | bytes 73760 | tf_op jit(solution)/shard_map/ppermute | solution.py:138
  13.6 0.0 collective-permute-done.3.refs_5_
  13.6 0.0 collective-permute-done.2.refs_3_
  13.6 0.0 copy-done.1
  13.6 1.9 %shard_map.68.refs_0_ = f32[5,16,256]{2,1,0:T(8,128)S(1)} custom-call(bf16[128,256]{1,0:T(8,128)(2,1)S(1)} %divide_convert_fusion.scaled_ref.refs_0_, bf16[128,256]{1,0:T(8,128)(2,1)S(1)} %collective-permute-done.refs_1_, bf16[128,256]{1,0:T(8,128)(2,1)S(1)} %collective-permute-done.1.refs_2_, bf16[128,256]{1,0:T(8,128)(2,1)S(1)} %collective-permute-done.2.refs_3_, ...), custom_call_target="tpu_custom_call" | custom-call | tf_op jit(solution)/shard_map/pallas_call | solution.py:166
  15.5 1.5 %collective-permute-start.8 = (f32[5,16,256]{2,1,0:T(8,128)S(1)}, f32[5,16,256]{2,1,0:T(8,128)S(1)}, u32[]{:S(2)}, u32[]{:S(2)}) collective-permute-start(f32[5,16,256]{2,1,0:T(8,128)S(1)} %shard_map.68.refs_0_), channel_id=1, source_target_pairs={{2,0},{3,1},{0,2},{1,3},{6,4},{7,5},{4,6},{5,7},{10,8},{11,9},{8,1... | collective-permute-start | bytes 245768 | tf_op jit(solution)/shard_map/ppermute | solution.py:138
  17.1 0.0 collective-permute-start.7
  17.1 0.6 %collective-permute-start.6 = (f32[5,16,256]{2,1,0:T(8,128)S(1)}, f32[5,16,256]{2,1,0:T(8,128)S(1)}, u32[]{:S(2)}, u32[]{:S(2)}) collective-permute-start(f32[5,16,256]{2,1,0:T(8,128)S(1)} %shard_map.68.refs_0_), channel_id=1, source_target_pairs={{1,0},{0,1},{3,2},{2,3},{5,4},{4,5},{7,6},{6,7},{9,8},{8,9},{11,10... | collective-permute-start | bytes 245768 | tf_op jit(solution)/shard_map/ppermute | solution.py:138
  17.7 2.3 %collective-permute-done.8.refs_3_ = f32[5,16,256]{2,1,0:T(8,128)S(1)} collective-permute-done((f32[5,16,256]{2,1,0:T(8,128)S(1)}, f32[5,16,256]{2,1,0:T(8,128)S(1)}, u32[]{:S(2)}, u32[]{:S(2)}) %collective-permute-start.8) | collective-permute-done | bytes 81952 | tf_op jit(solution)/shard_map/ppermute | solution.py:138
  20.0 1.8 %collective-permute-done.7.refs_2_ = f32[5,16,256]{2,1,0:T(8,128)S(1)} collective-permute-done((f32[5,16,256]{2,1,0:T(8,128)S(1)}, f32[5,16,256]{2,1,0:T(8,128)S(1)}, u32[]{:S(2)}, u32[]{:S(2)}) %collective-permute-start.7) | collective-permute-done | bytes 81952 | tf_op jit(solution)/shard_map/ppermute | solution.py:138
  21.8 0.0 collective-permute-done.6.refs_1_
  21.8 0.1 shard_map.69
  21.9 2.7 %collective-permute-start.11 = (f32[16,128]{1,0:T(8,128)S(1)}, f32[16,128]{1,0:T(8,128)S(1)}, u32[]{:S(2)}, u32[]{:S(2)}) collective-permute-start(f32[16,128]{1,0:T(8,128)S(1)} %get-tuple-element.6.refs_0_), channel_id=1, source_target_pairs={{12,0},{8,4},{4,8},{0,12},{13,1},{9,5},{5,9},{1,13},{14,2},{10,6},... | collective-permute-start | bytes 24584 | tf_op jit(solution)/shard_map/ppermute | solution.py:138
  24.5 0.0 collective-permute-start.10
  24.5 1.7 %collective-permute-start.9 = (f32[16,128]{1,0:T(8,128)S(1)}, f32[16,128]{1,0:T(8,128)S(1)}, u32[]{:S(2)}, u32[]{:S(2)}) collective-permute-start(f32[16,128]{1,0:T(8,128)S(1)} %get-tuple-element.6.refs_0_), channel_id=1, source_target_pairs={{4,0},{0,4},{12,8},{8,12},{5,1},{1,5},{13,9},{9,13},{6,2},{2,6},{1... | collective-permute-start | bytes 24584 | tf_op jit(solution)/shard_map/ppermute | solution.py:138
  26.3 1.1 %collective-permute-done.11.refs_3_ = f32[16,128]{1,0:T(8,128)S(1)} collective-permute-done((f32[16,128]{1,0:T(8,128)S(1)}, f32[16,128]{1,0:T(8,128)S(1)}, u32[]{:S(2)}, u32[]{:S(2)}) %collective-permute-start.11) | collective-permute-done | bytes 8224 | tf_op jit(solution)/shard_map/ppermute | solution.py:138
  27.3 1.8 %collective-permute-done.10.refs_2_ = f32[16,128]{1,0:T(8,128)S(1)} collective-permute-done((f32[16,128]{1,0:T(8,128)S(1)}, f32[16,128]{1,0:T(8,128)S(1)}, u32[]{:S(2)}, u32[]{:S(2)}) %collective-permute-start.10) | collective-permute-done | bytes 8224 | tf_op jit(solution)/shard_map/ppermute | solution.py:138
  29.1 0.0 collective-permute-done.9.refs_1_
  29.1 0.8 %shard_map.70 = (f32[16,256]{1,0:T(8,128)}, f32[16,256]{1,0:T(8,128)}, f32[16,256]{1,0:T(8,128)}) custom-call(f32[16,256]{1,0:T(8,128)S(1)} %get-tuple-element.5.image_ref, f32[16,256]{1,0:T(8,128)S(1)} %copy-done, f32[16,128]{1,0:T(8,128)S(1)} %get-tuple-element.6.refs_0_, f32[16,128]{1,0:T(8,128)S(1)} %collective-permute-done.9.refs_1_, ...), custom_call_target="tpu_custom_call" | custom-call | tf_op jit(solution)/shard_map/pallas_call | solution.py:181
  (1 shorter events, 0.0 us)
Async XLA Ops:
  0.6 1.5 %copy-start = (f32[16,256]{1,0:T(8,128)S(1)}, f32[16,256]{1,0:T(8,128)}, u32[]{:S(2)}) copy-start(f32[16,256]{1,0:T(8,128)} %probes_ref.3) | copy-start | bytes 49156
  1.6 7.5 %collective-permute-start = (bf16[128,256]{1,0:T(8,128)(2,1)S(1)}, bf16[128,256]{1,0:T(8,128)(2,1)S(1)}, u32[]{:S(2)}, u32[]{:S(2)}) collective-permute-start(bf16[128,256]{1,0:T(8,128)(2,1)S(1)} %divide_convert_fusion.scaled_ref.refs_0_), channel_id=1, source_target_pairs={{1,0},{0,1},{3,2},{2,3},{5,4},{4,5},{7,6},{6,7},{9,8},{8,9},{11,10... | collective-permute-start | bytes 196616 | tf_op jit(solution)/shard_map/ppermute | solution.py:138
  2.1 11.5 %copy-start.1 = (f32[256]{0:T(256)S(1)}, f32[256]{0:T(256)}, u32[]{:S(2)}) copy-start(f32[256]{0:T(256)} %param.6) | copy-start | bytes 3076
  2.1 10.1 %collective-permute-start.5 = (bf16[144,256]{1,0:T(8,128)(2,1)S(1)}, bf16[144,256]{1,0:T(8,128)(2,1)S(1)}, u32[]{:S(2)}, u32[]{:S(2)}) collective-permute-start(bf16[144,256]{1,0:T(8,128)(2,1)S(1)} %shard_map.67.refs_4_), channel_id=1, source_target_pairs={{12,0},{8,4},{4,8},{0,12},{13,1},{9,5},{5,9},{1,13},{14,2},{10,6},... | collective-permute-start | bytes 221192 | tf_op jit(solution)/shard_map/ppermute | solution.py:138
  6.8 6.8 %collective-permute-start.4 = (bf16[144,256]{1,0:T(8,128)(2,1)S(1)}, bf16[144,256]{1,0:T(8,128)(2,1)S(1)}, u32[]{:S(2)}, u32[]{:S(2)}) collective-permute-start(bf16[144,256]{1,0:T(8,128)(2,1)S(1)} %shard_map.67.refs_4_), channel_id=1, source_target_pairs={{8,0},{12,4},{0,8},{4,12},{9,1},{13,5},{1,9},{5,13},{10,2},{14,6},... | collective-permute-start | bytes 221192 | tf_op jit(solution)/shard_map/ppermute | solution.py:138
  6.8 6.8 %collective-permute-start.3 = (bf16[144,256]{1,0:T(8,128)(2,1)S(1)}, bf16[144,256]{1,0:T(8,128)(2,1)S(1)}, u32[]{:S(2)}, u32[]{:S(2)}) collective-permute-start(bf16[144,256]{1,0:T(8,128)(2,1)S(1)} %shard_map.67.refs_4_), channel_id=1, source_target_pairs={{4,0},{0,4},{12,8},{8,12},{5,1},{1,5},{13,9},{9,13},{6,2},{2,6},{1... | collective-permute-start | bytes 221192 | tf_op jit(solution)/shard_map/ppermute | solution.py:138
  7.5 4.8 %collective-permute-start.1 = (bf16[128,256]{1,0:T(8,128)(2,1)S(1)}, bf16[128,256]{1,0:T(8,128)(2,1)S(1)}, u32[]{:S(2)}, u32[]{:S(2)}) collective-permute-start(bf16[128,256]{1,0:T(8,128)(2,1)S(1)} %divide_convert_fusion.scaled_ref.refs_0_), channel_id=1, source_target_pairs={{2,0},{0,2},{3,1},{1,3},{6,4},{4,6},{7,5},{5,7},{10,8},{8,10},{11,... | collective-permute-start | bytes 196616 | tf_op jit(solution)/shard_map/ppermute | solution.py:138
  9.1 4.5 %collective-permute-start.2 = (bf16[128,256]{1,0:T(8,128)(2,1)S(1)}, bf16[128,256]{1,0:T(8,128)(2,1)S(1)}, u32[]{:S(2)}, u32[]{:S(2)}) collective-permute-start(bf16[128,256]{1,0:T(8,128)(2,1)S(1)} %collective-permute-done.refs_1_), channel_id=1, source_target_pairs={{2,0},{0,2},{3,1},{1,3},{6,4},{4,6},{7,5},{5,7},{10,8},{8,10},{11,... | collective-permute-start | bytes 196616 | tf_op jit(solution)/shard_map/ppermute | solution.py:138
  15.5 4.5 %collective-permute-start.8 = (f32[5,16,256]{2,1,0:T(8,128)S(1)}, f32[5,16,256]{2,1,0:T(8,128)S(1)}, u32[]{:S(2)}, u32[]{:S(2)}) collective-permute-start(f32[5,16,256]{2,1,0:T(8,128)S(1)} %shard_map.68.refs_0_), channel_id=1, source_target_pairs={{2,0},{3,1},{0,2},{1,3},{6,4},{7,5},{4,6},{5,7},{10,8},{11,9},{8,1... | collective-permute-start | bytes 245768 | tf_op jit(solution)/shard_map/ppermute | solution.py:138
  17.1 4.7 %collective-permute-start.7 = (f32[5,16,256]{2,1,0:T(8,128)S(1)}, f32[5,16,256]{2,1,0:T(8,128)S(1)}, u32[]{:S(2)}, u32[]{:S(2)}) collective-permute-start(f32[5,16,256]{2,1,0:T(8,128)S(1)} %shard_map.68.refs_0_), channel_id=1, source_target_pairs={{3,0},{2,1},{1,2},{0,3},{7,4},{6,5},{5,6},{4,7},{11,8},{10,9},{9,1... | collective-permute-start | bytes 245768 | tf_op jit(solution)/shard_map/ppermute | solution.py:138
  17.1 4.7 %collective-permute-start.6 = (f32[5,16,256]{2,1,0:T(8,128)S(1)}, f32[5,16,256]{2,1,0:T(8,128)S(1)}, u32[]{:S(2)}, u32[]{:S(2)}) collective-permute-start(f32[5,16,256]{2,1,0:T(8,128)S(1)} %shard_map.68.refs_0_), channel_id=1, source_target_pairs={{1,0},{0,1},{3,2},{2,3},{5,4},{4,5},{7,6},{6,7},{9,8},{8,9},{11,10... | collective-permute-start | bytes 245768 | tf_op jit(solution)/shard_map/ppermute | solution.py:138
  21.9 5.5 %collective-permute-start.11 = (f32[16,128]{1,0:T(8,128)S(1)}, f32[16,128]{1,0:T(8,128)S(1)}, u32[]{:S(2)}, u32[]{:S(2)}) collective-permute-start(f32[16,128]{1,0:T(8,128)S(1)} %get-tuple-element.6.refs_0_), channel_id=1, source_target_pairs={{12,0},{8,4},{4,8},{0,12},{13,1},{9,5},{5,9},{1,13},{14,2},{10,6},... | collective-permute-start | bytes 24584 | tf_op jit(solution)/shard_map/ppermute | solution.py:138
  24.5 4.5 %collective-permute-start.10 = (f32[16,128]{1,0:T(8,128)S(1)}, f32[16,128]{1,0:T(8,128)S(1)}, u32[]{:S(2)}, u32[]{:S(2)}) collective-permute-start(f32[16,128]{1,0:T(8,128)S(1)} %get-tuple-element.6.refs_0_), channel_id=1, source_target_pairs={{8,0},{12,4},{0,8},{4,12},{9,1},{13,5},{1,9},{5,13},{10,2},{14,6},... | collective-permute-start | bytes 24584 | tf_op jit(solution)/shard_map/ppermute | solution.py:138
  24.5 4.5 %collective-permute-start.9 = (f32[16,128]{1,0:T(8,128)S(1)}, f32[16,128]{1,0:T(8,128)S(1)}, u32[]{:S(2)}, u32[]{:S(2)}) collective-permute-start(f32[16,128]{1,0:T(8,128)S(1)} %get-tuple-element.6.refs_0_), channel_id=1, source_target_pairs={{4,0},{0,4},{12,8},{8,12},{5,1},{1,5},{13,9},{9,13},{6,2},{2,6},{1... | collective-permute-start | bytes 24584 | tf_op jit(solution)/shard_map/ppermute | solution.py:138

commit v13 on v9

--- a/solution.py
+++ b/solution.py
@@ -136,6 +136,20 @@
     ]
 
 
+def along_line(value, line_count, sub_count):
+    if line_count > DIRECT or sub_count != 2:
+        return everywhere(value, LINE, line_count)
+    blocks = [value]
+    for step in range(1, line_count):
+        pairs = [
+            (2 * source_of(place, step, line_count) + 1 - core, 2 * place + core)
+            for place in range(line_count)
+            for core in range(2)
+        ]
+        blocks.append(lax.ppermute(value, LINE + ("sub",), pairs))
+    return blocks
+
+
 def plane_blocks(value, shape):
     grp_count, sub_count = shape
     if sub_count != 2 or not paired(grp_count):
@@ -157,7 +171,7 @@
             out_shape=jax.ShapeDtypeStruct((feature_count + probe_count, width), jnp.bfloat16),
             compiler_params=VMEM,
         )(scaled, probes)
-        lines = everywhere(line, LINE, line_count)
+        lines = along_line(line, line_count, plane_shape[1])
         planes = plane_blocks(scaled, plane_shape)
         partial = pl.pallas_call(
             lambda *refs: image_kernel(feature_count, plane_count, *refs),
@@ -175,7 +189,7 @@
         )(*[partials[number] for number in exchange_order(plane_count)])
         outs = (jax.ShapeDtypeStruct(probes.shape, jnp.float32),) * 3
         return pl.pallas_call(finish_kernel, out_shape=outs, compiler_params=VMEM)(
-            image, probes, *everywhere(sums, LINE, line_count)
+            image, probes, *along_line(sums, line_count, plane_shape[1])
         )
 
     return local

time: 30 us -> 29.3 us (0.977)
  starting transfers between devices: 14.4 us -> 13.6 us
    ppermute x12 -> x6, starting transfers between devices: 14.4 us -> 4.69 us  [everywhere(): lax.ppermute(value, axes, [(source_of(i, step, count), i) for i in range(...]
    ppermute x0 -> x6, starting transfers between devices: none -> 8.88 us  [along_line(): blocks.append(lax.ppermute(value, LINE + ('sub',), pairs))]
    ppermute x0 -> x6, waiting for transfers between devices: none -> 4.38 us  [along_line(): blocks.append(lax.ppermute(value, LINE + ('sub',), pairs))]
    ppermute x12 -> x6, waiting for transfers between devices: 11 us -> 6.82 us  [everywhere(): lax.ppermute(value, axes, [(source_of(i, step, count), i) for i in range(...]
  transfers between devices with their start and end apart: 12 -> 12, of which waited for: 6 -> 7; matrix products, arithmetic and copies ran while one was open for 0% -> 0% of each run, Pallas kernels for 0% -> 0%
where the time goes in v13:
time: 29.3 us; the launch traced here: 29.2 us
  starting transfers between devices  13.6 us (46%)
  waiting for transfers between devices  11.2 us (38%)
  Pallas kernels  2.78 us (9%)
  other arithmetic  0.93 us (3%)
  between operations  0.67 us (2%)
    ppermute x6, starting transfers between devices, along_line(): blocks.append(lax.ppermute(value, LINE + ('sub',), pairs))  8.88 us
    ppermute x6, waiting for transfers between devices, everywhere(): lax.ppermute(value, axes, [(source_of(i, step, count), i) for i in range(...  6.82 us
    ppermute x6, starting transfers between devices, everywhere(): lax.ppermute(value, axes, [(source_of(i, step, count), i) for i in range(...  4.69 us
    ppermute x6, waiting for transfers between devices, along_line(): blocks.append(lax.ppermute(value, LINE + ('sub',), pairs))  4.38 us
    pallas_call x1, Pallas kernels, local(): pl.pallas_call(lambda *refs: image_kernel(feature_count, plane_count, *re...  1.9 us
    convert_element_type x1, other arithmetic, local(): (features.astype(jnp.float32) / lengthscale[:, None]).astype(jnp.bfloat16)  0.93 us
    pallas_call x1, Pallas kernels, local(): pl.pallas_call(finish_kernel, out_shape=outs, compiler_params=VMEM)  0.77 us
  transfers between devices with their start and end apart: 12, of which 7 were waited for; matrix products, arithmetic and copies ran while one was open for 0% of the time, Pallas kernels for 0%

profile of v13, /device:TPU:0, one launch (start us, length us, event | category | flops | bytes accessed | tf_op | source)
XLA Modules:
  0.0 29.2 jit_solution(10752129166301065768)
XLA Ops:
  0.6 0.0 copy-start
  0.6 0.9 %divide_convert_fusion.scaled_ref.refs_0_ = bf16[128,256]{1,0:T(8,128)(2,1)S(1)} fusion(bf16[128,256]{1,0:T(8,128)(2,1)} %param.4, f32[128]{0:T(128)} %param.5), kind=kLoop, calls=%fused_computation | loop fusion | flops 98304 | bytes 131584 | tf_op jit(solution)/shard_map/convert_element_type | solution.py:168
  1.6 0.5 %collective-permute-start = (bf16[128,256]{1,0:T(8,128)(2,1)S(1)}, bf16[128,256]{1,0:T(8,128)(2,1)S(1)}, u32[]{:S(2)}, u32[]{:S(2)}) collective-permute-start(bf16[128,256]{1,0:T(8,128)(2,1)S(1)} %divide_convert_fusion.scaled_ref.refs_0_), channel_id=1, source_target_pairs={{1,0},{0,1},{3,2},{2,3},{5,4},{4,5},{7,6},{6,7},{9,8},{8,9},{11,10... | collective-permute-start | bytes 196616 | tf_op jit(solution)/shard_map/ppermute | solution.py:134
  2.1 0.0 copy-done
  2.1 0.0 copy-start.1
  2.1 4.8 %collective-permute-start.5 = (bf16[144,256]{1,0:T(8,128)(2,1)S(1)}, bf16[144,256]{1,0:T(8,128)(2,1)S(1)}, u32[]{:S(2)}, u32[]{:S(2)}) collective-permute-start(bf16[144,256]{1,0:T(8,128)(2,1)S(1)} %shard_map.67.refs_4_), channel_id=1, source_target_pairs={{13,0},{12,1},{9,4},{8,5},{5,8},{4,9},{1,12},{0,13},{15,2},{14,3},... | collective-permute-start | bytes 221192 | tf_op jit(solution)/shard_map/ppermute | solution.py:149
  6.9 0.0 collective-permute-start.4
  6.9 0.3 collective-permute-start.3
  7.2 1.7 %collective-permute-start.1 = (bf16[128,256]{1,0:T(8,128)(2,1)S(1)}, bf16[128,256]{1,0:T(8,128)(2,1)S(1)}, u32[]{:S(2)}, u32[]{:S(2)}) collective-permute-start(bf16[128,256]{1,0:T(8,128)(2,1)S(1)} %divide_convert_fusion.scaled_ref.refs_0_), channel_id=1, source_target_pairs={{2,0},{0,2},{3,1},{1,3},{6,4},{4,6},{7,5},{5,7},{10,8},{8,10},{11,... | collective-permute-start | bytes 196616 | tf_op jit(solution)/shard_map/ppermute | solution.py:134
  8.9 0.0 collective-permute-done.refs_1_
  8.9 0.3 %collective-permute-start.2 = (bf16[128,256]{1,0:T(8,128)(2,1)S(1)}, bf16[128,256]{1,0:T(8,128)(2,1)S(1)}, u32[]{:S(2)}, u32[]{:S(2)}) collective-permute-start(bf16[128,256]{1,0:T(8,128)(2,1)S(1)} %collective-permute-done.refs_1_), channel_id=1, source_target_pairs={{2,0},{0,2},{3,1},{1,3},{6,4},{4,6},{7,5},{5,7},{10,8},{8,10},{11,... | collective-permute-start | bytes 196616 | tf_op jit(solution)/shard_map/ppermute | solution.py:134
  9.2 2.7 %collective-permute-done.1.refs_2_ = bf16[128,256]{1,0:T(8,128)(2,1)S(1)} collective-permute-done((bf16[128,256]{1,0:T(8,128)(2,1)S(1)}, bf16[128,256]{1,0:T(8,128)(2,1)S(1)}, u32[]{:S(2)}, u32[]{:S(2)}) %collective-permute-start.1) | collective-permute-done | bytes 65568 | tf_op jit(solution)/shard_map/ppermute | solution.py:134
  11.9 0.0 collective-permute-done.5.refs_7_
  11.9 1.1 %collective-permute-done.4.refs_6_ = bf16[144,256]{1,0:T(8,128)(2,1)S(1)} collective-permute-done((bf16[144,256]{1,0:T(8,128)(2,1)S(1)}, bf16[144,256]{1,0:T(8,128)(2,1)S(1)}, u32[]{:S(2)}, u32[]{:S(2)}) %collective-permute-start.4) | collective-permute-done | bytes 73760 | tf_op jit(solution)/shard_map/ppermute | solution.py:149
  13.0 0.0 collective-permute-done.3.refs_5_
  13.0 0.2 collective-permute-done.2.refs_3_
  13.2 0.0 copy-done.1
  13.2 1.9 %shard_map.68.refs_0_ = f32[5,16,256]{2,1,0:T(8,128)S(1)} custom-call(bf16[128,256]{1,0:T(8,128)(2,1)S(1)} %divide_convert_fusion.scaled_ref.refs_0_, bf16[128,256]{1,0:T(8,128)(2,1)S(1)} %collective-permute-done.refs_1_, bf16[128,256]{1,0:T(8,128)(2,1)S(1)} %collective-permute-done.1.refs_2_, bf16[128,256]{1,0:T(8,128)(2,1)S(1)} %collective-permute-done.2.refs_3_, ...), custom_call_target="tpu_custom_call" | custom-call | tf_op jit(solution)/shard_map/pallas_call | solution.py:176
  15.1 1.4 %collective-permute-start.8 = (f32[5,16,256]{2,1,0:T(8,128)S(1)}, f32[5,16,256]{2,1,0:T(8,128)S(1)}, u32[]{:S(2)}, u32[]{:S(2)}) collective-permute-start(f32[5,16,256]{2,1,0:T(8,128)S(1)} %shard_map.68.refs_0_), channel_id=1, source_target_pairs={{2,0},{3,1},{0,2},{1,3},{6,4},{7,5},{4,6},{5,7},{10,8},{11,9},{8,1... | collective-permute-start | bytes 245768 | tf_op jit(solution)/shard_map/ppermute | solution.py:134
  16.5 0.2 collective-permute-start.7
  16.6 0.6 %collective-permute-start.6 = (f32[5,16,256]{2,1,0:T(8,128)S(1)}, f32[5,16,256]{2,1,0:T(8,128)S(1)}, u32[]{:S(2)}, u32[]{:S(2)}) collective-permute-start(f32[5,16,256]{2,1,0:T(8,128)S(1)} %shard_map.68.refs_0_), channel_id=1, source_target_pairs={{1,0},{0,1},{3,2},{2,3},{5,4},{4,5},{7,6},{6,7},{9,8},{8,9},{11,10... | collective-permute-start | bytes 245768 | tf_op jit(solution)/shard_map/ppermute | solution.py:134
  17.2 2.6 %collective-permute-done.8.refs_3_ = f32[5,16,256]{2,1,0:T(8,128)S(1)} collective-permute-done((f32[5,16,256]{2,1,0:T(8,128)S(1)}, f32[5,16,256]{2,1,0:T(8,128)S(1)}, u32[]{:S(2)}, u32[]{:S(2)}) %collective-permute-start.8) | collective-permute-done | bytes 81952 | tf_op jit(solution)/shard_map/ppermute | solution.py:134
  19.8 1.4 %collective-permute-done.7.refs_2_ = f32[5,16,256]{2,1,0:T(8,128)S(1)} collective-permute-done((f32[5,16,256]{2,1,0:T(8,128)S(1)}, f32[5,16,256]{2,1,0:T(8,128)S(1)}, u32[]{:S(2)}, u32[]{:S(2)}) %collective-permute-start.7) | collective-permute-done | bytes 81952 | tf_op jit(solution)/shard_map/ppermute | solution.py:134
  21.2 0.0 collective-permute-done.6.refs_1_
  21.2 0.1 shard_map.69
  21.3 3.1 %collective-permute-start.11 = (f32[16,128]{1,0:T(8,128)S(1)}, f32[16,128]{1,0:T(8,128)S(1)}, u32[]{:S(2)}, u32[]{:S(2)}) collective-permute-start(f32[16,128]{1,0:T(8,128)S(1)} %get-tuple-element.6.refs_0_), channel_id=1, source_target_pairs={{13,0},{12,1},{9,4},{8,5},{5,8},{4,9},{1,12},{0,13},{15,2},{14,3},... | collective-permute-start | bytes 24584 | tf_op jit(solution)/shard_map/ppermute | solution.py:149
  24.4 0.0 collective-permute-start.10
  24.4 0.7 %collective-permute-start.9 = (f32[16,128]{1,0:T(8,128)S(1)}, f32[16,128]{1,0:T(8,128)S(1)}, u32[]{:S(2)}, u32[]{:S(2)}) collective-permute-start(f32[16,128]{1,0:T(8,128)S(1)} %get-tuple-element.6.refs_0_), channel_id=1, source_target_pairs={{5,0},{4,1},{1,4},{0,5},{13,8},{12,9},{9,12},{8,13},{7,2},{6,3},{3... | collective-permute-start | bytes 24584 | tf_op jit(solution)/shard_map/ppermute | solution.py:149
  25.1 1.0 %collective-permute-done.11.refs_3_ = f32[16,128]{1,0:T(8,128)S(1)} collective-permute-done((f32[16,128]{1,0:T(8,128)S(1)}, f32[16,128]{1,0:T(8,128)S(1)}, u32[]{:S(2)}, u32[]{:S(2)}) %collective-permute-start.11) | collective-permute-done | bytes 8224 | tf_op jit(solution)/shard_map/ppermute | solution.py:149
  26.2 2.2 %collective-permute-done.10.refs_2_ = f32[16,128]{1,0:T(8,128)S(1)} collective-permute-done((f32[16,128]{1,0:T(8,128)S(1)}, f32[16,128]{1,0:T(8,128)S(1)}, u32[]{:S(2)}, u32[]{:S(2)}) %collective-permute-start.10) | collective-permute-done | bytes 8224 | tf_op jit(solution)/shard_map/ppermute | solution.py:149
  28.4 0.0 collective-permute-done.9.refs_1_
  28.4 0.8 %shard_map.70 = (f32[16,256]{1,0:T(8,128)}, f32[16,256]{1,0:T(8,128)}, f32[16,256]{1,0:T(8,128)}) custom-call(f32[16,256]{1,0:T(8,128)S(1)} %get-tuple-element.5.image_ref, f32[16,256]{1,0:T(8,128)S(1)} %copy-done, f32[16,128]{1,0:T(8,128)S(1)} %get-tuple-element.6.refs_0_, f32[16,128]{1,0:T(8,128)S(1)} %collective-permute-done.9.refs_1_, ...), custom_call_target="tpu_custom_call" | custom-call | tf_op jit(solution)/shard_map/pallas_call | solution.py:191
  (1 shorter events, 0.0 us)
Async XLA Ops:
  0.6 1.5 %copy-start = (f32[16,256]{1,0:T(8,128)S(1)}, f32[16,256]{1,0:T(8,128)}, u32[]{:S(2)}) copy-start(f32[16,256]{1,0:T(8,128)} %probes_ref.3) | copy-start | bytes 49156
  1.6 7.3 %collective-permute-start = (bf16[128,256]{1,0:T(8,128)(2,1)S(1)}, bf16[128,256]{1,0:T(8,128)(2,1)S(1)}, u32[]{:S(2)}, u32[]{:S(2)}) collective-permute-start(bf16[128,256]{1,0:T(8,128)(2,1)S(1)} %divide_convert_fusion.scaled_ref.refs_0_), channel_id=1, source_target_pairs={{1,0},{0,1},{3,2},{2,3},{5,4},{4,5},{7,6},{6,7},{9,8},{8,9},{11,10... | collective-permute-start | bytes 196616 | tf_op jit(solution)/shard_map/ppermute | solution.py:134
  2.1 11.1 %copy-start.1 = (f32[256]{0:T(256)S(1)}, f32[256]{0:T(256)}, u32[]{:S(2)}) copy-start(f32[256]{0:T(256)} %param.6) | copy-start | bytes 3076
  2.1 9.8 %collective-permute-start.5 = (bf16[144,256]{1,0:T(8,128)(2,1)S(1)}, bf16[144,256]{1,0:T(8,128)(2,1)S(1)}, u32[]{:S(2)}, u32[]{:S(2)}) collective-permute-start(bf16[144,256]{1,0:T(8,128)(2,1)S(1)} %shard_map.67.refs_4_), channel_id=1, source_target_pairs={{13,0},{12,1},{9,4},{8,5},{5,8},{4,9},{1,12},{0,13},{15,2},{14,3},... | collective-permute-start | bytes 221192 | tf_op jit(solution)/shard_map/ppermute | solution.py:149
  6.9 6.1 %collective-permute-start.4 = (bf16[144,256]{1,0:T(8,128)(2,1)S(1)}, bf16[144,256]{1,0:T(8,128)(2,1)S(1)}, u32[]{:S(2)}, u32[]{:S(2)}) collective-permute-start(bf16[144,256]{1,0:T(8,128)(2,1)S(1)} %shard_map.67.refs_4_), channel_id=1, source_target_pairs={{9,0},{8,1},{13,4},{12,5},{1,8},{0,9},{5,12},{4,13},{11,2},{10,3},... | collective-permute-start | bytes 221192 | tf_op jit(solution)/shard_map/ppermute | solution.py:149
  6.9 6.1 %collective-permute-start.3 = (bf16[144,256]{1,0:T(8,128)(2,1)S(1)}, bf16[144,256]{1,0:T(8,128)(2,1)S(1)}, u32[]{:S(2)}, u32[]{:S(2)}) collective-permute-start(bf16[144,256]{1,0:T(8,128)(2,1)S(1)} %shard_map.67.refs_4_), channel_id=1, source_target_pairs={{5,0},{4,1},{1,4},{0,5},{13,8},{12,9},{9,12},{8,13},{7,2},{6,3},{3... | collective-permute-start | bytes 221192 | tf_op jit(solution)/shard_map/ppermute | solution.py:149
  7.2 4.7 %collective-permute-start.1 = (bf16[128,256]{1,0:T(8,128)(2,1)S(1)}, bf16[128,256]{1,0:T(8,128)(2,1)S(1)}, u32[]{:S(2)}, u32[]{:S(2)}) collective-permute-start(bf16[128,256]{1,0:T(8,128)(2,1)S(1)} %divide_convert_fusion.scaled_ref.refs_0_), channel_id=1, source_target_pairs={{2,0},{0,2},{3,1},{1,3},{6,4},{4,6},{7,5},{5,7},{10,8},{8,10},{11,... | collective-permute-start | bytes 196616 | tf_op jit(solution)/shard_map/ppermute | solution.py:134
  8.9 4.3 %collective-permute-start.2 = (bf16[128,256]{1,0:T(8,128)(2,1)S(1)}, bf16[128,256]{1,0:T(8,128)(2,1)S(1)}, u32[]{:S(2)}, u32[]{:S(2)}) collective-permute-start(bf16[128,256]{1,0:T(8,128)(2,1)S(1)} %collective-permute-done.refs_1_), channel_id=1, source_target_pairs={{2,0},{0,2},{3,1},{1,3},{6,4},{4,6},{7,5},{5,7},{10,8},{8,10},{11,... | collective-permute-start | bytes 196616 | tf_op jit(solution)/shard_map/ppermute | solution.py:134
  15.1 4.7 %collective-permute-start.8 = (f32[5,16,256]{2,1,0:T(8,128)S(1)}, f32[5,16,256]{2,1,0:T(8,128)S(1)}, u32[]{:S(2)}, u32[]{:S(2)}) collective-permute-start(f32[5,16,256]{2,1,0:T(8,128)S(1)} %shard_map.68.refs_0_), channel_id=1, source_target_pairs={{2,0},{3,1},{0,2},{1,3},{6,4},{7,5},{4,6},{5,7},{10,8},{11,9},{8,1... | collective-permute-start | bytes 245768 | tf_op jit(solution)/shard_map/ppermute | solution.py:134
  16.5 4.7 %collective-permute-start.7 = (f32[5,16,256]{2,1,0:T(8,128)S(1)}, f32[5,16,256]{2,1,0:T(8,128)S(1)}, u32[]{:S(2)}, u32[]{:S(2)}) collective-permute-start(f32[5,16,256]{2,1,0:T(8,128)S(1)} %shard_map.68.refs_0_), channel_id=1, source_target_pairs={{3,0},{2,1},{1,2},{0,3},{7,4},{6,5},{5,6},{4,7},{11,8},{10,9},{9,1... | collective-permute-start | bytes 245768 | tf_op jit(solution)/shard_map/ppermute | solution.py:134
  16.6 4.6 %collective-permute-start.6 = (f32[5,16,256]{2,1,0:T(8,128)S(1)}, f32[5,16,256]{2,1,0:T(8,128)S(1)}, u32[]{:S(2)}, u32[]{:S(2)}) collective-permute-start(f32[5,16,256]{2,1,0:T(8,128)S(1)} %shard_map.68.refs_0_), channel_id=1, source_target_pairs={{1,0},{0,1},{3,2},{2,3},{5,4},{4,5},{7,6},{6,7},{9,8},{8,9},{11,10... | collective-permute-start | bytes 245768 | tf_op jit(solution)/shard_map/ppermute | solution.py:134
  21.3 4.9 %collective-permute-start.11 = (f32[16,128]{1,0:T(8,128)S(1)}, f32[16,128]{1,0:T(8,128)S(1)}, u32[]{:S(2)}, u32[]{:S(2)}) collective-permute-start(f32[16,128]{1,0:T(8,128)S(1)} %get-tuple-element.6.refs_0_), channel_id=1, source_target_pairs={{13,0},{12,1},{9,4},{8,5},{5,8},{4,9},{1,12},{0,13},{15,2},{14,3},... | collective-permute-start | bytes 24584 | tf_op jit(solution)/shard_map/ppermute | solution.py:149
  24.4 4.0 %collective-permute-start.10 = (f32[16,128]{1,0:T(8,128)S(1)}, f32[16,128]{1,0:T(8,128)S(1)}, u32[]{:S(2)}, u32[]{:S(2)}) collective-permute-start(f32[16,128]{1,0:T(8,128)S(1)} %get-tuple-element.6.refs_0_), channel_id=1, source_target_pairs={{9,0},{8,1},{13,4},{12,5},{1,8},{0,9},{5,12},{4,13},{11,2},{10,3},... | collective-permute-start | bytes 24584 | tf_op jit(solution)/shard_map/ppermute | solution.py:149
  24.4 4.0 %collective-permute-start.9 = (f32[16,128]{1,0:T(8,128)S(1)}, f32[16,128]{1,0:T(8,128)S(1)}, u32[]{:S(2)}, u32[]{:S(2)}) collective-permute-start(f32[16,128]{1,0:T(8,128)S(1)} %get-tuple-element.6.refs_0_), channel_id=1, source_target_pairs={{5,0},{4,1},{1,4},{0,5},{13,8},{12,9},{9,12},{8,13},{7,2},{6,3},{3... | collective-permute-start | bytes 24584 | tf_op jit(solution)/shard_map/ppermute | solution.py:149

commit v14 on v13

--- a/solution.py
+++ b/solution.py
@@ -37,41 +37,54 @@
     )
 
 
+def apply_blocks(feature_count, rows, blocks, totals):
+    columns = []
+    for block in blocks:
+        scaled = block[:feature_count, :]
+        block_columns = jnp.concatenate([scaled, norm_rows(scaled, 0)], axis=0)
+        columns.append(block_columns.astype(jnp.float32).T.astype(jnp.bfloat16))
+    columns = jnp.concatenate(columns, axis=0)
+    probes = jnp.concatenate([block[feature_count:, :] for block in blocks], axis=1)
+    result = []
+    for own, total in zip(rows, totals):
+        exponent = jnp.dot(columns, own, preferred_element_type=jnp.float32)
+        weights = jnp.exp(exponent).astype(jnp.bfloat16)
+        result.append(total + jnp.dot(probes, weights, preferred_element_type=jnp.float32))
+    return result
+
+
 def image_kernel(feature_count, plane_count, *refs):
     plane_refs = refs[:plane_count]
-    line_refs = refs[plane_count:-3]
-    noise_ref, probes_ref, partial_ref = refs[-3:]
+    line_refs = refs[plane_count:-4]
+    noise_ref, probes_ref, partial_ref, rows_ref = refs[-4:]
     rows = [jnp.concatenate([ref[...], norm_rows(ref[...], 1)], axis=0) for ref in plane_refs]
-
-    def add_blocks(blocks, totals):
-        columns = []
-        for block in blocks:
-            scaled = block[:feature_count, :]
-            block_columns = jnp.concatenate([scaled, norm_rows(scaled, 0)], axis=0)
-            columns.append(block_columns.astype(jnp.float32).T.astype(jnp.bfloat16))
-        columns = jnp.concatenate(columns, axis=0)
-        probes = jnp.concatenate([block[feature_count:, :] for block in blocks], axis=1)
-        result = []
-        for own, total in zip(rows, totals):
-            exponent = jnp.dot(columns, own, preferred_element_type=jnp.float32)
-            weights = jnp.exp(exponent).astype(jnp.bfloat16)
-            result.append(total + jnp.dot(probes, weights, preferred_element_type=jnp.float32))
-        return result
-
+    for number, own in enumerate(rows):
+        rows_ref[number] = own
     totals = [noise_ref[...] * probes_ref[...]]
     totals += [jnp.zeros(probes_ref.shape, jnp.float32)] * (plane_count - 1)
     if len(line_refs[0].shape) == 2:
-        totals = add_blocks([ref[...] for ref in line_refs], totals)
+        totals = apply_blocks(feature_count, rows, [ref[...] for ref in line_refs], totals)
     else:
         totals = lax.fori_loop(
             0,
             line_refs[0].shape[0],
-            lambda number, value: add_blocks([line_refs[0][number]], value),
+            lambda number, value: apply_blocks(
+                feature_count, rows, [line_refs[0][number]], value
+            ),
             totals,
         )
     for number, total in enumerate(totals):
         partial_ref[number] = total
     partial_ref[plane_count] = probes_ref[...]
+
+
+def add_kernel(feature_count, plane_count, rows_ref, start_ref, line_ref, partial_ref):
+    rows = [rows_ref[number] for number in range(plane_count)]
+    totals = [start_ref[number] for number in range(plane_count)]
+    totals = apply_blocks(feature_count, rows, [line_ref[...]], totals)
+    for number, total in enumerate(totals):
+        partial_ref[number] = total
+    partial_ref[plane_count] = start_ref[plane_count]
 
 
 def combine_kernel(plane_count, *refs):
@@ -173,11 +186,22 @@
         )(scaled, probes)
         lines = along_line(line, line_count, plane_shape[1])
         planes = plane_blocks(scaled, plane_shape)
-        partial = pl.pallas_call(
+        early, late = lines[:1] + lines[2:], lines[1:2]
+        partial_shape = jax.ShapeDtypeStruct((plane_count + 1, probe_count, width), jnp.float32)
+        partial, rows = pl.pallas_call(
             lambda *refs: image_kernel(feature_count, plane_count, *refs),
-            out_shape=jax.ShapeDtypeStruct((plane_count + 1, probe_count, width), jnp.float32),
+            out_shape=(
+                partial_shape,
+                jax.ShapeDtypeStruct((plane_count, feature_count + 2 * HALF, width), jnp.bfloat16),
+            ),
             compiler_params=VMEM,
-        )(*planes, *lines, noise_var[None, :], probes)
+        )(*planes, *early, noise_var[None, :], probes)
+        for block in late:
+            partial = pl.pallas_call(
+                lambda *refs: add_kernel(feature_count, plane_count, *refs),
+                out_shape=partial_shape,
+                compiler_params=VMEM,
+            )(rows, partial, block)
         partials = everywhere(partial, PLANE, plane_count)
         image, sums = pl.pallas_call(
             lambda *refs: combine_kernel(plane_count, *refs),

time: 29.3 us -> 30.9 us (1.055); the launches traced: 29.2 us -> 30.3 us
  Pallas kernels: 2.78 us -> 3.53 us
  waiting for transfers between devices: 11.2 us -> 11.6 us
    ppermute x6, waiting for transfers between devices: 6.82 us -> 7.85 us  [everywhere(): lax.ppermute(value, axes, [(source_of(i, step, count), i) for i in range(...]
    pallas_call x0 -> x1, Pallas kernels: none -> 1.03 us  [local(): pl.pallas_call(lambda *refs: add_kernel(feature_count, plane_count, *refs...]
    ppermute x6, waiting for transfers between devices: 4.38 us -> 3.79 us  [along_line(): blocks.append(lax.ppermute(value, LINE + ('sub',), pairs))]
  transfers between devices with their start and end apart: 12 -> 12, of which waited for: 7 -> 7; matrix products, arithmetic and copies ran while one was open for 0% -> 0% of each run, Pallas kernels for 0% -> 5%
where the time goes in v14:
time: 30.9 us; the launch traced here: 30.3 us
  starting transfers between devices  13.5 us (44%)
  waiting for transfers between devices  11.6 us (38%)
  Pallas kernels  3.53 us (11%)
  other arithmetic  0.93 us (3%)
  between operations  0.67 us (2%)
    ppermute x6, starting transfers between devices, along_line(): blocks.append(lax.ppermute(value, LINE + ('sub',), pairs))  8.82 us
    ppermute x6, waiting for transfers between devices, everywhere(): lax.ppermute(value, axes, [(source_of(i, step, count), i) for i in range(...  7.85 us
    ppermute x6, starting transfers between devices, everywhere(): lax.ppermute(value, axes, [(source_of(i, step, count), i) for i in range(...  4.69 us
    ppermute x6, waiting for transfers between devices, along_line(): blocks.append(lax.ppermute(value, LINE + ('sub',), pairs))  3.79 us
    pallas_call x1, Pallas kernels, local(): pl.pallas_call(lambda *refs: image_kernel(feature_count, plane_count, *re...  1.62 us
    pallas_call x1, Pallas kernels, local(): pl.pallas_call(lambda *refs: add_kernel(feature_count, plane_count, *refs...  1.03 us
    convert_element_type x1, other arithmetic, local(): (features.astype(jnp.float32) / lengthscale[:, None]).astype(jnp.bfloat16)  0.93 us
    pallas_call x1, Pallas kernels, local(): pl.pallas_call(finish_kernel, out_shape=outs, compiler_params=VMEM)  0.77 us
  transfers between devices with their start and end apart: 12, of which 7 were waited for; matrix products, arithmetic and copies ran while one was open for 0% of the time, Pallas kernels for 5%

profile of v14, /device:TPU:0, one launch (start us, length us, event | category | flops | bytes accessed | tf_op | source)
XLA Modules:
  0.0 30.3 jit_solution(4480825673161589883)
XLA Ops:
  0.6 0.0 copy-start
  0.6 0.9 %divide_convert_fusion.scaled_ref.refs_0_ = bf16[128,256]{1,0:T(8,128)(2,1)S(1)} fusion(bf16[128,256]{1,0:T(8,128)(2,1)} %param.4, f32[128]{0:T(128)} %param.5), kind=kLoop, calls=%fused_computation | loop fusion | flops 98304 | bytes 131584 | tf_op jit(solution)/shard_map/convert_element_type | solution.py:181
  1.6 0.5 %collective-permute-start = (bf16[128,256]{1,0:T(8,128)(2,1)S(1)}, bf16[128,256]{1,0:T(8,128)(2,1)S(1)}, u32[]{:S(2)}, u32[]{:S(2)}) collective-permute-start(bf16[128,256]{1,0:T(8,128)(2,1)S(1)} %divide_convert_fusion.scaled_ref.refs_0_), channel_id=1, source_target_pairs={{1,0},{0,1},{3,2},{2,3},{5,4},{4,5},{7,6},{6,7},{9,8},{8,9},{11,10... | collective-permute-start | bytes 196616 | tf_op jit(solution)/shard_map/ppermute | solution.py:147
  2.1 0.0 copy-done
  2.1 0.0 copy-start.1
  2.1 3.8 %collective-permute-start.3 = (bf16[144,256]{1,0:T(8,128)(2,1)S(1)}, bf16[144,256]{1,0:T(8,128)(2,1)S(1)}, u32[]{:S(2)}, u32[]{:S(2)}) collective-permute-start(bf16[144,256]{1,0:T(8,128)(2,1)S(1)} %shard_map.67.refs_4_), channel_id=1, source_target_pairs={{9,0},{8,1},{13,4},{12,5},{1,8},{0,9},{5,12},{4,13},{11,2},{10,3},... | collective-permute-start | bytes 221192 | tf_op jit(solution)/shard_map/ppermute | solution.py:162
  5.9 1.1 %collective-permute-start.4 = (bf16[144,256]{1,0:T(8,128)(2,1)S(1)}, bf16[144,256]{1,0:T(8,128)(2,1)S(1)}, u32[]{:S(2)}, u32[]{:S(2)}) collective-permute-start(bf16[144,256]{1,0:T(8,128)(2,1)S(1)} %shard_map.67.refs_4_), channel_id=1, source_target_pairs={{13,0},{12,1},{9,4},{8,5},{5,8},{4,9},{1,12},{0,13},{15,2},{14,3},... | collective-permute-start | bytes 221192 | tf_op jit(solution)/shard_map/ppermute | solution.py:162
  7.0 0.1 collective-permute-start.5
  7.1 1.5 %collective-permute-start.1 = (bf16[128,256]{1,0:T(8,128)(2,1)S(1)}, bf16[128,256]{1,0:T(8,128)(2,1)S(1)}, u32[]{:S(2)}, u32[]{:S(2)}) collective-permute-start(bf16[128,256]{1,0:T(8,128)(2,1)S(1)} %divide_convert_fusion.scaled_ref.refs_0_), channel_id=1, source_target_pairs={{2,0},{0,2},{3,1},{1,3},{6,4},{4,6},{7,5},{5,7},{10,8},{8,10},{11,... | collective-permute-start | bytes 196616 | tf_op jit(solution)/shard_map/ppermute | solution.py:147
  8.6 0.0 collective-permute-done.refs_1_
  8.6 0.5 %collective-permute-start.2 = (bf16[128,256]{1,0:T(8,128)(2,1)S(1)}, bf16[128,256]{1,0:T(8,128)(2,1)S(1)}, u32[]{:S(2)}, u32[]{:S(2)}) collective-permute-start(bf16[128,256]{1,0:T(8,128)(2,1)S(1)} %collective-permute-done.refs_1_), channel_id=1, source_target_pairs={{2,0},{0,2},{3,1},{1,3},{6,4},{4,6},{7,5},{5,7},{10,8},{8,10},{11,... | collective-permute-start | bytes 196616 | tf_op jit(solution)/shard_map/ppermute | solution.py:147
  9.1 2.7 %collective-permute-done.1.refs_2_ = bf16[128,256]{1,0:T(8,128)(2,1)S(1)} collective-permute-done((bf16[128,256]{1,0:T(8,128)(2,1)S(1)}, bf16[128,256]{1,0:T(8,128)(2,1)S(1)}, u32[]{:S(2)}, u32[]{:S(2)}) %collective-permute-start.1) | collective-permute-done | bytes 65568 | tf_op jit(solution)/shard_map/ppermute | solution.py:147
  11.8 0.0 collective-permute-done.3.refs_5_
  11.8 0.4 %collective-permute-done.4.refs_6_ = bf16[144,256]{1,0:T(8,128)(2,1)S(1)} collective-permute-done((bf16[144,256]{1,0:T(8,128)(2,1)S(1)}, bf16[144,256]{1,0:T(8,128)(2,1)S(1)}, u32[]{:S(2)}, u32[]{:S(2)}) %collective-permute-start.4) | collective-permute-done | bytes 73760 | tf_op jit(solution)/shard_map/ppermute | solution.py:162
  12.2 0.8 %collective-permute-done.2.refs_3_ = bf16[128,256]{1,0:T(8,128)(2,1)S(1)} collective-permute-done((bf16[128,256]{1,0:T(8,128)(2,1)S(1)}, bf16[128,256]{1,0:T(8,128)(2,1)S(1)}, u32[]{:S(2)}, u32[]{:S(2)}) %collective-permute-start.2) | collective-permute-done | bytes 65568 | tf_op jit(solution)/shard_map/ppermute | solution.py:147
  13.0 0.0 copy-done.1
  13.0 1.6 %shard_map.68 = (f32[5,16,256]{2,1,0:T(8,128)S(1)}, bf16[4,144,256]{2,1,0:T(8,128)(2,1)S(1)}) custom-call(bf16[128,256]{1,0:T(8,128)(2,1)S(1)} %divide_convert_fusion.scaled_ref.refs_0_, bf16[128,256]{1,0:T(8,128)(2,1)S(1)} %collective-permute-done.refs_1_, bf16[128,256]{1,0:T(8,128)(2,1)S(1)} %collective-permute-done.1.refs_2_, ...), custom_call_target="tpu_custom_call" | custom-call | tf_op jit(solution)/shard_map/pallas_call | solution.py:191
  14.6 0.0 collective-permute-done.5.refs_2_
  14.6 1.0 %shard_map.69.refs_0_ = f32[5,16,256]{2,1,0:T(8,128)S(1)} custom-call(bf16[4,144,256]{2,1,0:T(8,128)(2,1)S(1)} %get-tuple-element.7.refs_0_, f32[5,16,256]{2,1,0:T(8,128)S(1)} %get-tuple-element.8.refs_1_, bf16[144,256]{1,0:T(8,128)(2,1)S(1)} %collective-permute-done.5.refs_2_), custom_call_target="tpu_custom_call" | custom-call | tf_op jit(solution)/shard_map/pallas_call | solution.py:200
  15.7 0.0 collective-permute-start.6
  15.7 1.6 %collective-permute-start.7 = (f32[5,16,256]{2,1,0:T(8,128)S(1)}, f32[5,16,256]{2,1,0:T(8,128)S(1)}, u32[]{:S(2)}, u32[]{:S(2)}) collective-permute-start(f32[5,16,256]{2,1,0:T(8,128)S(1)} %shard_map.69.refs_0_), channel_id=1, source_target_pairs={{3,0},{2,1},{1,2},{0,3},{7,4},{6,5},{5,6},{4,7},{11,8},{10,9},{9,1... | collective-permute-start | bytes 245768 | tf_op jit(solution)/shard_map/ppermute | solution.py:147
  17.3 0.5 %collective-permute-start.8 = (f32[5,16,256]{2,1,0:T(8,128)S(1)}, f32[5,16,256]{2,1,0:T(8,128)S(1)}, u32[]{:S(2)}, u32[]{:S(2)}) collective-permute-start(f32[5,16,256]{2,1,0:T(8,128)S(1)} %shard_map.69.refs_0_), channel_id=1, source_target_pairs={{2,0},{3,1},{0,2},{1,3},{6,4},{7,5},{4,6},{5,7},{10,8},{11,9},{8,1... | collective-permute-start | bytes 245768 | tf_op jit(solution)/shard_map/ppermute | solution.py:147
  17.8 0.0 collective-permute-done.6.refs_1_
  17.8 2.2 %collective-permute-done.7.refs_2_ = f32[5,16,256]{2,1,0:T(8,128)S(1)} collective-permute-done((f32[5,16,256]{2,1,0:T(8,128)S(1)}, f32[5,16,256]{2,1,0:T(8,128)S(1)}, u32[]{:S(2)}, u32[]{:S(2)}) %collective-permute-start.7) | collective-permute-done | bytes 81952 | tf_op jit(solution)/shard_map/ppermute | solution.py:147
  20.0 2.1 %collective-permute-done.8.refs_3_ = f32[5,16,256]{2,1,0:T(8,128)S(1)} collective-permute-done((f32[5,16,256]{2,1,0:T(8,128)S(1)}, f32[5,16,256]{2,1,0:T(8,128)S(1)}, u32[]{:S(2)}, u32[]{:S(2)}) %collective-permute-start.8) | collective-permute-done | bytes 81952 | tf_op jit(solution)/shard_map/ppermute | solution.py:147
  22.2 0.1 shard_map.70
  22.3 2.4 %collective-permute-start.10 = (f32[16,128]{1,0:T(8,128)S(1)}, f32[16,128]{1,0:T(8,128)S(1)}, u32[]{:S(2)}, u32[]{:S(2)}) collective-permute-start(f32[16,128]{1,0:T(8,128)S(1)} %get-tuple-element.10.refs_0_), channel_id=1, source_target_pairs={{9,0},{8,1},{13,4},{12,5},{1,8},{0,9},{5,12},{4,13},{11,2},{10,3},... | collective-permute-start | bytes 24584 | tf_op jit(solution)/shard_map/ppermute | solution.py:162
  24.7 1.5 %collective-permute-start.11 = (f32[16,128]{1,0:T(8,128)S(1)}, f32[16,128]{1,0:T(8,128)S(1)}, u32[]{:S(2)}, u32[]{:S(2)}) collective-permute-start(f32[16,128]{1,0:T(8,128)S(1)} %get-tuple-element.10.refs_0_), channel_id=1, source_target_pairs={{13,0},{12,1},{9,4},{8,5},{5,8},{4,9},{1,12},{0,13},{15,2},{14,3},... | collective-permute-start | bytes 24584 | tf_op jit(solution)/shard_map/ppermute | solution.py:162
  26.1 0.0 collective-permute-start.9
  26.1 0.1 collective-permute-done.10.refs_2_
  26.3 3.3 %collective-permute-done.11.refs_3_ = f32[16,128]{1,0:T(8,128)S(1)} collective-permute-done((f32[16,128]{1,0:T(8,128)S(1)}, f32[16,128]{1,0:T(8,128)S(1)}, u32[]{:S(2)}, u32[]{:S(2)}) %collective-permute-start.11) | collective-permute-done | bytes 8224 | tf_op jit(solution)/shard_map/ppermute | solution.py:162
  29.5 0.0 collective-permute-done.9.refs_1_
  29.5 0.8 %shard_map.71 = (f32[16,256]{1,0:T(8,128)}, f32[16,256]{1,0:T(8,128)}, f32[16,256]{1,0:T(8,128)}) custom-call(f32[16,256]{1,0:T(8,128)S(1)} %get-tuple-element.9.image_ref, f32[16,256]{1,0:T(8,128)S(1)} %copy-done, f32[16,128]{1,0:T(8,128)S(1)} %get-tuple-element.10.refs_0_, f32[16,128]{1,0:T(8,128)S(1)} %collective-permute-done.9.refs_1_, ...), custom_call_target="tpu_custom_call" | custom-call | tf_op jit(solution)/shard_map/pallas_call | solution.py:215
  (1 shorter events, 0.0 us)
Async XLA Ops:
  0.6 1.5 %copy-start = (f32[16,256]{1,0:T(8,128)S(1)}, f32[16,256]{1,0:T(8,128)}, u32[]{:S(2)}) copy-start(f32[16,256]{1,0:T(8,128)} %probes_ref.3) | copy-start | bytes 49156
  1.6 7.0 %collective-permute-start = (bf16[128,256]{1,0:T(8,128)(2,1)S(1)}, bf16[128,256]{1,0:T(8,128)(2,1)S(1)}, u32[]{:S(2)}, u32[]{:S(2)}) collective-permute-start(bf16[128,256]{1,0:T(8,128)(2,1)S(1)} %divide_convert_fusion.scaled_ref.refs_0_), channel_id=1, source_target_pairs={{1,0},{0,1},{3,2},{2,3},{5,4},{4,5},{7,6},{6,7},{9,8},{8,9},{11,10... | collective-permute-start | bytes 196616 | tf_op jit(solution)/shard_map/ppermute | solution.py:147
  2.1 10.9 %copy-start.1 = (f32[256]{0:T(256)S(1)}, f32[256]{0:T(256)}, u32[]{:S(2)}) copy-start(f32[256]{0:T(256)} %param.6) | copy-start | bytes 3076
  2.1 9.7 %collective-permute-start.3 = (bf16[144,256]{1,0:T(8,128)(2,1)S(1)}, bf16[144,256]{1,0:T(8,128)(2,1)S(1)}, u32[]{:S(2)}, u32[]{:S(2)}) collective-permute-start(bf16[144,256]{1,0:T(8,128)(2,1)S(1)} %shard_map.67.refs_4_), channel_id=1, source_target_pairs={{9,0},{8,1},{13,4},{12,5},{1,8},{0,9},{5,12},{4,13},{11,2},{10,3},... | collective-permute-start | bytes 221192 | tf_op jit(solution)/shard_map/ppermute | solution.py:162
  5.9 6.3 %collective-permute-start.4 = (bf16[144,256]{1,0:T(8,128)(2,1)S(1)}, bf16[144,256]{1,0:T(8,128)(2,1)S(1)}, u32[]{:S(2)}, u32[]{:S(2)}) collective-permute-start(bf16[144,256]{1,0:T(8,128)(2,1)S(1)} %shard_map.67.refs_4_), channel_id=1, source_target_pairs={{13,0},{12,1},{9,4},{8,5},{5,8},{4,9},{1,12},{0,13},{15,2},{14,3},... | collective-permute-start | bytes 221192 | tf_op jit(solution)/shard_map/ppermute | solution.py:162
  7.0 7.6 %collective-permute-start.5 = (bf16[144,256]{1,0:T(8,128)(2,1)S(1)}, bf16[144,256]{1,0:T(8,128)(2,1)S(1)}, u32[]{:S(2)}, u32[]{:S(2)}) collective-permute-start(bf16[144,256]{1,0:T(8,128)(2,1)S(1)} %shard_map.67.refs_4_), channel_id=1, source_target_pairs={{5,0},{4,1},{1,4},{0,5},{13,8},{12,9},{9,12},{8,13},{7,2},{6,3},{3... | collective-permute-start | bytes 221192 | tf_op jit(solution)/shard_map/ppermute | solution.py:162
  7.1 4.7 %collective-permute-start.1 = (bf16[128,256]{1,0:T(8,128)(2,1)S(1)}, bf16[128,256]{1,0:T(8,128)(2,1)S(1)}, u32[]{:S(2)}, u32[]{:S(2)}) collective-permute-start(bf16[128,256]{1,0:T(8,128)(2,1)S(1)} %divide_convert_fusion.scaled_ref.refs_0_), channel_id=1, source_target_pairs={{2,0},{0,2},{3,1},{1,3},{6,4},{4,6},{7,5},{5,7},{10,8},{8,10},{11,... | collective-permute-start | bytes 196616 | tf_op jit(solution)/shard_map/ppermute | solution.py:147
  8.6 4.4 %collective-permute-start.2 = (bf16[128,256]{1,0:T(8,128)(2,1)S(1)}, bf16[128,256]{1,0:T(8,128)(2,1)S(1)}, u32[]{:S(2)}, u32[]{:S(2)}) collective-permute-start(bf16[128,256]{1,0:T(8,128)(2,1)S(1)} %collective-permute-done.refs_1_), channel_id=1, source_target_pairs={{2,0},{0,2},{3,1},{1,3},{6,4},{4,6},{7,5},{5,7},{10,8},{8,10},{11,... | collective-permute-start | bytes 196616 | tf_op jit(solution)/shard_map/ppermute | solution.py:147
  15.7 2.1 %collective-permute-start.6 = (f32[5,16,256]{2,1,0:T(8,128)S(1)}, f32[5,16,256]{2,1,0:T(8,128)S(1)}, u32[]{:S(2)}, u32[]{:S(2)}) collective-permute-start(f32[5,16,256]{2,1,0:T(8,128)S(1)} %shard_map.69.refs_0_), channel_id=1, source_target_pairs={{1,0},{0,1},{3,2},{2,3},{5,4},{4,5},{7,6},{6,7},{9,8},{8,9},{11,10... | collective-permute-start | bytes 245768 | tf_op jit(solution)/shard_map/ppermute | solution.py:147
  15.7 4.4 %collective-permute-start.7 = (f32[5,16,256]{2,1,0:T(8,128)S(1)}, f32[5,16,256]{2,1,0:T(8,128)S(1)}, u32[]{:S(2)}, u32[]{:S(2)}) collective-permute-start(f32[5,16,256]{2,1,0:T(8,128)S(1)} %shard_map.69.refs_0_), channel_id=1, source_target_pairs={{3,0},{2,1},{1,2},{0,3},{7,4},{6,5},{5,6},{4,7},{11,8},{10,9},{9,1... | collective-permute-start | bytes 245768 | tf_op jit(solution)/shard_map/ppermute | solution.py:147
  17.3 4.9 %collective-permute-start.8 = (f32[5,16,256]{2,1,0:T(8,128)S(1)}, f32[5,16,256]{2,1,0:T(8,128)S(1)}, u32[]{:S(2)}, u32[]{:S(2)}) collective-permute-start(f32[5,16,256]{2,1,0:T(8,128)S(1)} %shard_map.69.refs_0_), channel_id=1, source_target_pairs={{2,0},{3,1},{0,2},{1,3},{6,4},{7,5},{4,6},{5,7},{10,8},{11,9},{8,1... | collective-permute-start | bytes 245768 | tf_op jit(solution)/shard_map/ppermute | solution.py:147
  22.3 4.0 %collective-permute-start.10 = (f32[16,128]{1,0:T(8,128)S(1)}, f32[16,128]{1,0:T(8,128)S(1)}, u32[]{:S(2)}, u32[]{:S(2)}) collective-permute-start(f32[16,128]{1,0:T(8,128)S(1)} %get-tuple-element.10.refs_0_), channel_id=1, source_target_pairs={{9,0},{8,1},{13,4},{12,5},{1,8},{0,9},{5,12},{4,13},{11,2},{10,3},... | collective-permute-start | bytes 24584 | tf_op jit(solution)/shard_map/ppermute | solution.py:162
  24.7 4.9 %collective-permute-start.11 = (f32[16,128]{1,0:T(8,128)S(1)}, f32[16,128]{1,0:T(8,128)S(1)}, u32[]{:S(2)}, u32[]{:S(2)}) collective-permute-start(f32[16,128]{1,0:T(8,128)S(1)} %get-tuple-element.10.refs_0_), channel_id=1, source_target_pairs={{13,0},{12,1},{9,4},{8,5},{5,8},{4,9},{1,12},{0,13},{15,2},{14,3},... | collective-permute-start | bytes 24584 | tf_op jit(solution)/shard_map/ppermute | solution.py:162
  26.1 3.4 %collective-permute-start.9 = (f32[16,128]{1,0:T(8,128)S(1)}, f32[16,128]{1,0:T(8,128)S(1)}, u32[]{:S(2)}, u32[]{:S(2)}) collective-permute-start(f32[16,128]{1,0:T(8,128)S(1)} %get-tuple-element.10.refs_0_), channel_id=1, source_target_pairs={{5,0},{4,1},{1,4},{0,5},{13,8},{12,9},{9,12},{8,13},{7,2},{6,3},{3... | collective-permute-start | bytes 24584 | tf_op jit(solution)/shard_map/ppermute | solution.py:162

commit v15 on v14

--- a/solution.py
+++ b/solution.py
@@ -55,11 +55,9 @@
 
 def image_kernel(feature_count, plane_count, *refs):
     plane_refs = refs[:plane_count]
-    line_refs = refs[plane_count:-4]
-    noise_ref, probes_ref, partial_ref, rows_ref = refs[-4:]
+    line_refs = refs[plane_count:-3]
+    noise_ref, probes_ref, partial_ref = refs[-3:]
     rows = [jnp.concatenate([ref[...], norm_rows(ref[...], 1)], axis=0) for ref in plane_refs]
-    for number, own in enumerate(rows):
-        rows_ref[number] = own
     totals = [noise_ref[...] * probes_ref[...]]
     totals += [jnp.zeros(probes_ref.shape, jnp.float32)] * (plane_count - 1)
     if len(line_refs[0].shape) == 2:
@@ -78,8 +76,10 @@
     partial_ref[plane_count] = probes_ref[...]
 
 
-def add_kernel(feature_count, plane_count, rows_ref, start_ref, line_ref, partial_ref):
-    rows = [rows_ref[number] for number in range(plane_count)]
+def add_kernel(feature_count, plane_count, *refs):
+    plane_refs = refs[:plane_count]
+    line_ref, start_ref, partial_ref = refs[plane_count:]
+    rows = [jnp.concatenate([ref[...], norm_rows(ref[...], 1)], axis=0) for ref in plane_refs]
     totals = [start_ref[number] for number in range(plane_count)]
     totals = apply_blocks(feature_count, rows, [line_ref[...]], totals)
     for number, total in enumerate(totals):
@@ -188,20 +188,22 @@
         planes = plane_blocks(scaled, plane_shape)
         early, late = lines[:1] + lines[2:], lines[1:2]
         partial_shape = jax.ShapeDtypeStruct((plane_count + 1, probe_count, width), jnp.float32)
-        partial, rows = pl.pallas_call(
+        partial = pl.pallas_call(
             lambda *refs: image_kernel(feature_count, plane_count, *refs),
-            out_shape=(
-                partial_shape,
-                jax.ShapeDtypeStruct((plane_count, feature_count + 2 * HALF, width), jnp.bfloat16),
+            out_shape=partial_shape,
+            compiler_params=VMEM,
+            cost_estimate=pl.CostEstimate(
+                flops=2 * plane_count * len(early) * width * width * (feature_count + probe_count),
+                bytes_accessed=4 * width * plane_count * feature_count,
+                transcendentals=plane_count * len(early) * width * width,
             ),
-            compiler_params=VMEM,
         )(*planes, *early, noise_var[None, :], probes)
         for block in late:
             partial = pl.pallas_call(
                 lambda *refs: add_kernel(feature_count, plane_count, *refs),
                 out_shape=partial_shape,
                 compiler_params=VMEM,
-            )(rows, partial, block)
+            )(*planes, block, partial)
         partials = everywhere(partial, PLANE, plane_count)
         image, sums = pl.pallas_call(
             lambda *refs: combine_kernel(plane_count, *refs),

time: 30.9 us -> 29.5 us (0.955); the launches traced: 30.3 us -> 29.3 us
  waiting for transfers between devices: 11.6 us -> 10.9 us
    ppermute x6, waiting for transfers between devices: 7.85 us -> 6.74 us  [everywhere(): lax.ppermute(value, axes, [(source_of(i, step, count), i) for i in range(...]
    ppermute x6, waiting for transfers between devices: 3.79 us -> 4.11 us  [along_line(): blocks.append(lax.ppermute(value, LINE + ('sub',), pairs))]
  transfers between devices with their start and end apart: 12 -> 12, of which waited for: 7 -> 6; matrix products, arithmetic and copies ran while one was open for 0% -> 0% of each run, Pallas kernels for 5% -> 6%
where the time goes in v15:
time: 29.5 us; the launch traced here: 29.3 us
  starting transfers between devices  13.3 us (45%)
  waiting for transfers between devices  10.9 us (37%)
  Pallas kernels  3.55 us (12%)
  other arithmetic  0.93 us (3%)
  between operations  0.67 us (2%)
    ppermute x6, starting transfers between devices, along_line(): blocks.append(lax.ppermute(value, LINE + ('sub',), pairs))  8.61 us
    ppermute x6, waiting for transfers between devices, everywhere(): lax.ppermute(value, axes, [(source_of(i, step, count), i) for i in range(...  6.74 us
    ppermute x6, starting transfers between devices, everywhere(): lax.ppermute(value, axes, [(source_of(i, step, count), i) for i in range(...  4.7 us
    ppermute x6, waiting for transfers between devices, along_line(): blocks.append(lax.ppermute(value, LINE + ('sub',), pairs))  4.11 us
    pallas_call x1, Pallas kernels, local(): pl.pallas_call(lambda *refs: image_kernel(feature_count, plane_count, *re...  1.62 us
    pallas_call x1, Pallas kernels, local(): pl.pallas_call(lambda *refs: add_kernel(feature_count, plane_count, *refs...  1.05 us
    convert_element_type x1, other arithmetic, local(): (features.astype(jnp.float32) / lengthscale[:, None]).astype(jnp.bfloat16)  0.93 us
    pallas_call x1, Pallas kernels, local(): pl.pallas_call(finish_kernel, out_shape=outs, compiler_params=VMEM)  0.77 us
  transfers between devices with their start and end apart: 12, of which 6 were waited for; matrix products, arithmetic and copies ran while one was open for 0% of the time, Pallas kernels for 6%

profile of v15, /device:TPU:0, one launch (start us, length us, event | category | flops | bytes accessed | tf_op | source)
XLA Modules:
  0.0 29.3 jit_solution(335945801635047093)
XLA Ops:
  0.6 0.0 copy-start
  0.6 0.9 %divide_convert_fusion.scaled_ref.refs_0_ = bf16[128,256]{1,0:T(8,128)(2,1)S(1)} fusion(bf16[128,256]{1,0:T(8,128)(2,1)} %param.4, f32[128]{0:T(128)} %param.5), kind=kLoop, calls=%fused_computation | loop fusion | flops 98304 | bytes 131584 | tf_op jit(solution)/shard_map/convert_element_type | solution.py:181
  1.6 0.5 %collective-permute-start = (bf16[128,256]{1,0:T(8,128)(2,1)S(1)}, bf16[128,256]{1,0:T(8,128)(2,1)S(1)}, u32[]{:S(2)}, u32[]{:S(2)}) collective-permute-start(bf16[128,256]{1,0:T(8,128)(2,1)S(1)} %divide_convert_fusion.scaled_ref.refs_0_), channel_id=1, source_target_pairs={{1,0},{0,1},{3,2},{2,3},{5,4},{4,5},{7,6},{6,7},{9,8},{8,9},{11,10... | collective-permute-start | bytes 196616 | tf_op jit(solution)/shard_map/ppermute | solution.py:147
  2.1 0.0 copy-done
  2.1 0.0 copy-start.1
  2.1 4.8 %collective-permute-start.5 = (bf16[144,256]{1,0:T(8,128)(2,1)S(1)}, bf16[144,256]{1,0:T(8,128)(2,1)S(1)}, u32[]{:S(2)}, u32[]{:S(2)}) collective-permute-start(bf16[144,256]{1,0:T(8,128)(2,1)S(1)} %shard_map.67.refs_4_), channel_id=1, source_target_pairs={{13,0},{12,1},{9,4},{8,5},{5,8},{4,9},{1,12},{0,13},{15,2},{14,3},... | collective-permute-start | bytes 221192 | tf_op jit(solution)/shard_map/ppermute | solution.py:162
  6.9 0.0 collective-permute-start.4
  6.9 1.5 %collective-permute-start.1 = (bf16[128,256]{1,0:T(8,128)(2,1)S(1)}, bf16[128,256]{1,0:T(8,128)(2,1)S(1)}, u32[]{:S(2)}, u32[]{:S(2)}) collective-permute-start(bf16[128,256]{1,0:T(8,128)(2,1)S(1)} %divide_convert_fusion.scaled_ref.refs_0_), channel_id=1, source_target_pairs={{2,0},{0,2},{3,1},{1,3},{6,4},{4,6},{7,5},{5,7},{10,8},{8,10},{11,... | collective-permute-start | bytes 196616 | tf_op jit(solution)/shard_map/ppermute | solution.py:147
  8.4 0.0 collective-permute-done.refs_1_
  8.4 0.5 %collective-permute-start.2 = (bf16[128,256]{1,0:T(8,128)(2,1)S(1)}, bf16[128,256]{1,0:T(8,128)(2,1)S(1)}, u32[]{:S(2)}, u32[]{:S(2)}) collective-permute-start(bf16[128,256]{1,0:T(8,128)(2,1)S(1)} %collective-permute-done.refs_1_), channel_id=1, source_target_pairs={{2,0},{0,2},{3,1},{1,3},{6,4},{4,6},{7,5},{5,7},{10,8},{8,10},{11,... | collective-permute-start | bytes 196616 | tf_op jit(solution)/shard_map/ppermute | solution.py:147
  8.9 0.0 collective-permute-start.3
  8.9 2.7 %collective-permute-done.1.refs_2_ = bf16[128,256]{1,0:T(8,128)(2,1)S(1)} collective-permute-done((bf16[128,256]{1,0:T(8,128)(2,1)S(1)}, bf16[128,256]{1,0:T(8,128)(2,1)S(1)}, u32[]{:S(2)}, u32[]{:S(2)}) %collective-permute-start.1) | collective-permute-done | bytes 65568 | tf_op jit(solution)/shard_map/ppermute | solution.py:147
  11.6 0.0 collective-permute-done.5.refs_6_
  11.6 1.5 %collective-permute-done.4.refs_5_ = bf16[144,256]{1,0:T(8,128)(2,1)S(1)} collective-permute-done((bf16[144,256]{1,0:T(8,128)(2,1)S(1)}, bf16[144,256]{1,0:T(8,128)(2,1)S(1)}, u32[]{:S(2)}, u32[]{:S(2)}) %collective-permute-start.4) | collective-permute-done | bytes 73760 | tf_op jit(solution)/shard_map/ppermute | solution.py:162
  13.1 0.0 collective-permute-done.2.refs_3_
  13.1 0.0 copy-done.1
  13.1 1.6 %shard_map.68.refs_5_ = f32[5,16,256]{2,1,0:T(8,128)S(1)} custom-call(bf16[128,256]{1,0:T(8,128)(2,1)S(1)} %divide_convert_fusion.scaled_ref.refs_0_, bf16[128,256]{1,0:T(8,128)(2,1)S(1)} %collective-permute-done.refs_1_, bf16[128,256]{1,0:T(8,128)(2,1)S(1)} %collective-permute-done.1.refs_2_, bf16[128,256]{1,0:T(8,128)(2,1)S(1)} %collective-permute-done.2.refs_3_, ...), custom_call_target="tpu_custom_call" | custom-call | flops 226492416 | bytes 524288 | tf_op jit(solution)/shard_map/pallas_call | solution.py:191
  14.7 0.0 collective-permute-done.3.refs_4_
  14.7 1.0 %shard_map.69.refs_0_ = f32[5,16,256]{2,1,0:T(8,128)S(1)} custom-call(bf16[128,256]{1,0:T(8,128)(2,1)S(1)} %divide_convert_fusion.scaled_ref.refs_0_, bf16[128,256]{1,0:T(8,128)(2,1)S(1)} %collective-permute-done.refs_1_, bf16[128,256]{1,0:T(8,128)(2,1)S(1)} %collective-permute-done.1.refs_2_, bf16[128,256]{1,0:T(8,128)(2,1)S(1)} %collective-permute-done.2.refs_3_, ...), custom_call_target="tpu_custom_call" | custom-call | tf_op jit(solution)/shard_map/pallas_call | solution.py:202
  15.8 1.5 %collective-permute-start.8 = (f32[5,16,256]{2,1,0:T(8,128)S(1)}, f32[5,16,256]{2,1,0:T(8,128)S(1)}, u32[]{:S(2)}, u32[]{:S(2)}) collective-permute-start(f32[5,16,256]{2,1,0:T(8,128)S(1)} %shard_map.69.refs_0_), channel_id=1, source_target_pairs={{2,0},{3,1},{0,2},{1,3},{6,4},{7,5},{4,6},{5,7},{10,8},{11,9},{8,1... | collective-permute-start | bytes 245768 | tf_op jit(solution)/shard_map/ppermute | solution.py:147
  17.3 0.2 collective-permute-start.7
  17.5 0.4 %collective-permute-start.6 = (f32[5,16,256]{2,1,0:T(8,128)S(1)}, f32[5,16,256]{2,1,0:T(8,128)S(1)}, u32[]{:S(2)}, u32[]{:S(2)}) collective-permute-start(f32[5,16,256]{2,1,0:T(8,128)S(1)} %shard_map.69.refs_0_), channel_id=1, source_target_pairs={{1,0},{0,1},{3,2},{2,3},{5,4},{4,5},{7,6},{6,7},{9,8},{8,9},{11,10... | collective-permute-start | bytes 245768 | tf_op jit(solution)/shard_map/ppermute | solution.py:147
  17.9 2.8 %collective-permute-done.8.refs_3_ = f32[5,16,256]{2,1,0:T(8,128)S(1)} collective-permute-done((f32[5,16,256]{2,1,0:T(8,128)S(1)}, f32[5,16,256]{2,1,0:T(8,128)S(1)}, u32[]{:S(2)}, u32[]{:S(2)}) %collective-permute-start.8) | collective-permute-done | bytes 81952 | tf_op jit(solution)/shard_map/ppermute | solution.py:147
  20.7 1.3 %collective-permute-done.7.refs_2_ = f32[5,16,256]{2,1,0:T(8,128)S(1)} collective-permute-done((f32[5,16,256]{2,1,0:T(8,128)S(1)}, f32[5,16,256]{2,1,0:T(8,128)S(1)}, u32[]{:S(2)}, u32[]{:S(2)}) %collective-permute-start.7) | collective-permute-done | bytes 81952 | tf_op jit(solution)/shard_map/ppermute | solution.py:147
  22.0 0.0 collective-permute-done.6.refs_1_
  22.0 0.1 shard_map.70
  22.1 2.5 %collective-permute-start.11 = (f32[16,128]{1,0:T(8,128)S(1)}, f32[16,128]{1,0:T(8,128)S(1)}, u32[]{:S(2)}, u32[]{:S(2)}) collective-permute-start(f32[16,128]{1,0:T(8,128)S(1)} %get-tuple-element.6.refs_0_), channel_id=1, source_target_pairs={{13,0},{12,1},{9,4},{8,5},{5,8},{4,9},{1,12},{0,13},{15,2},{14,3},... | collective-permute-start | bytes 24584 | tf_op jit(solution)/shard_map/ppermute | solution.py:162
  24.6 0.0 collective-permute-start.10
  24.6 1.4 %collective-permute-start.9 = (f32[16,128]{1,0:T(8,128)S(1)}, f32[16,128]{1,0:T(8,128)S(1)}, u32[]{:S(2)}, u32[]{:S(2)}) collective-permute-start(f32[16,128]{1,0:T(8,128)S(1)} %get-tuple-element.6.refs_0_), channel_id=1, source_target_pairs={{5,0},{4,1},{1,4},{0,5},{13,8},{12,9},{9,12},{8,13},{7,2},{6,3},{3... | collective-permute-start | bytes 24584 | tf_op jit(solution)/shard_map/ppermute | solution.py:162
  25.9 1.0 %collective-permute-done.11.refs_3_ = f32[16,128]{1,0:T(8,128)S(1)} collective-permute-done((f32[16,128]{1,0:T(8,128)S(1)}, f32[16,128]{1,0:T(8,128)S(1)}, u32[]{:S(2)}, u32[]{:S(2)}) %collective-permute-start.11) | collective-permute-done | bytes 8224 | tf_op jit(solution)/shard_map/ppermute | solution.py:162
  27.0 1.6 %collective-permute-done.10.refs_2_ = f32[16,128]{1,0:T(8,128)S(1)} collective-permute-done((f32[16,128]{1,0:T(8,128)S(1)}, f32[16,128]{1,0:T(8,128)S(1)}, u32[]{:S(2)}, u32[]{:S(2)}) %collective-permute-start.10) | collective-permute-done | bytes 8224 | tf_op jit(solution)/shard_map/ppermute | solution.py:162
  28.6 0.0 collective-permute-done.9.refs_1_
  28.6 0.8 %shard_map.71 = (f32[16,256]{1,0:T(8,128)}, f32[16,256]{1,0:T(8,128)}, f32[16,256]{1,0:T(8,128)}) custom-call(f32[16,256]{1,0:T(8,128)S(1)} %get-tuple-element.5.image_ref, f32[16,256]{1,0:T(8,128)S(1)} %copy-done, f32[16,128]{1,0:T(8,128)S(1)} %get-tuple-element.6.refs_0_, f32[16,128]{1,0:T(8,128)S(1)} %collective-permute-done.9.refs_1_, ...), custom_call_target="tpu_custom_call" | custom-call | tf_op jit(solution)/shard_map/pallas_call | solution.py:217
  (1 shorter events, 0.0 us)
Async XLA Ops:
  0.6 1.5 %copy-start = (f32[16,256]{1,0:T(8,128)S(1)}, f32[16,256]{1,0:T(8,128)}, u32[]{:S(2)}) copy-start(f32[16,256]{1,0:T(8,128)} %probes_ref.3) | copy-start | bytes 49156
  1.6 6.8 %collective-permute-start = (bf16[128,256]{1,0:T(8,128)(2,1)S(1)}, bf16[128,256]{1,0:T(8,128)(2,1)S(1)}, u32[]{:S(2)}, u32[]{:S(2)}) collective-permute-start(bf16[128,256]{1,0:T(8,128)(2,1)S(1)} %divide_convert_fusion.scaled_ref.refs_0_), channel_id=1, source_target_pairs={{1,0},{0,1},{3,2},{2,3},{5,4},{4,5},{7,6},{6,7},{9,8},{8,9},{11,10... | collective-permute-start | bytes 196616 | tf_op jit(solution)/shard_map/ppermute | solution.py:147
  2.1 11.0 %copy-start.1 = (f32[256]{0:T(256)S(1)}, f32[256]{0:T(256)}, u32[]{:S(2)}) copy-start(f32[256]{0:T(256)} %param.6) | copy-start | bytes 3076
  2.1 9.5 %collective-permute-start.5 = (bf16[144,256]{1,0:T(8,128)(2,1)S(1)}, bf16[144,256]{1,0:T(8,128)(2,1)S(1)}, u32[]{:S(2)}, u32[]{:S(2)}) collective-permute-start(bf16[144,256]{1,0:T(8,128)(2,1)S(1)} %shard_map.67.refs_4_), channel_id=1, source_target_pairs={{13,0},{12,1},{9,4},{8,5},{5,8},{4,9},{1,12},{0,13},{15,2},{14,3},... | collective-permute-start | bytes 221192 | tf_op jit(solution)/shard_map/ppermute | solution.py:162
  6.9 6.2 %collective-permute-start.4 = (bf16[144,256]{1,0:T(8,128)(2,1)S(1)}, bf16[144,256]{1,0:T(8,128)(2,1)S(1)}, u32[]{:S(2)}, u32[]{:S(2)}) collective-permute-start(bf16[144,256]{1,0:T(8,128)(2,1)S(1)} %shard_map.67.refs_4_), channel_id=1, source_target_pairs={{9,0},{8,1},{13,4},{12,5},{1,8},{0,9},{5,12},{4,13},{11,2},{10,3},... | collective-permute-start | bytes 221192 | tf_op jit(solution)/shard_map/ppermute | solution.py:162
  6.9 4.7 %collective-permute-start.1 = (bf16[128,256]{1,0:T(8,128)(2,1)S(1)}, bf16[128,256]{1,0:T(8,128)(2,1)S(1)}, u32[]{:S(2)}, u32[]{:S(2)}) collective-permute-start(bf16[128,256]{1,0:T(8,128)(2,1)S(1)} %divide_convert_fusion.scaled_ref.refs_0_), channel_id=1, source_target_pairs={{2,0},{0,2},{3,1},{1,3},{6,4},{4,6},{7,5},{5,7},{10,8},{8,10},{11,... | collective-permute-start | bytes 196616 | tf_op jit(solution)/shard_map/ppermute | solution.py:147
  8.4 4.7 %collective-permute-start.2 = (bf16[128,256]{1,0:T(8,128)(2,1)S(1)}, bf16[128,256]{1,0:T(8,128)(2,1)S(1)}, u32[]{:S(2)}, u32[]{:S(2)}) collective-permute-start(bf16[128,256]{1,0:T(8,128)(2,1)S(1)} %collective-permute-done.refs_1_), channel_id=1, source_target_pairs={{2,0},{0,2},{3,1},{1,3},{6,4},{4,6},{7,5},{5,7},{10,8},{8,10},{11,... | collective-permute-start | bytes 196616 | tf_op jit(solution)/shard_map/ppermute | solution.py:147
  8.9 5.8 %collective-permute-start.3 = (bf16[144,256]{1,0:T(8,128)(2,1)S(1)}, bf16[144,256]{1,0:T(8,128)(2,1)S(1)}, u32[]{:S(2)}, u32[]{:S(2)}) collective-permute-start(bf16[144,256]{1,0:T(8,128)(2,1)S(1)} %shard_map.67.refs_4_), channel_id=1, source_target_pairs={{5,0},{4,1},{1,4},{0,5},{13,8},{12,9},{9,12},{8,13},{7,2},{6,3},{3... | collective-permute-start | bytes 221192 | tf_op jit(solution)/shard_map/ppermute | solution.py:162
  15.8 5.0 %collective-permute-start.8 = (f32[5,16,256]{2,1,0:T(8,128)S(1)}, f32[5,16,256]{2,1,0:T(8,128)S(1)}, u32[]{:S(2)}, u32[]{:S(2)}) collective-permute-start(f32[5,16,256]{2,1,0:T(8,128)S(1)} %shard_map.69.refs_0_), channel_id=1, source_target_pairs={{2,0},{3,1},{0,2},{1,3},{6,4},{7,5},{4,6},{5,7},{10,8},{11,9},{8,1... | collective-permute-start | bytes 245768 | tf_op jit(solution)/shard_map/ppermute | solution.py:147
  17.3 4.7 %collective-permute-start.7 = (f32[5,16,256]{2,1,0:T(8,128)S(1)}, f32[5,16,256]{2,1,0:T(8,128)S(1)}, u32[]{:S(2)}, u32[]{:S(2)}) collective-permute-start(f32[5,16,256]{2,1,0:T(8,128)S(1)} %shard_map.69.refs_0_), channel_id=1, source_target_pairs={{3,0},{2,1},{1,2},{0,3},{7,4},{6,5},{5,6},{4,7},{11,8},{10,9},{9,1... | collective-permute-start | bytes 245768 | tf_op jit(solution)/shard_map/ppermute | solution.py:147
  17.5 4.5 %collective-permute-start.6 = (f32[5,16,256]{2,1,0:T(8,128)S(1)}, f32[5,16,256]{2,1,0:T(8,128)S(1)}, u32[]{:S(2)}, u32[]{:S(2)}) collective-permute-start(f32[5,16,256]{2,1,0:T(8,128)S(1)} %shard_map.69.refs_0_), channel_id=1, source_target_pairs={{1,0},{0,1},{3,2},{2,3},{5,4},{4,5},{7,6},{6,7},{9,8},{8,9},{11,10... | collective-permute-start | bytes 245768 | tf_op jit(solution)/shard_map/ppermute | solution.py:147
  22.1 4.9 %collective-permute-start.11 = (f32[16,128]{1,0:T(8,128)S(1)}, f32[16,128]{1,0:T(8,128)S(1)}, u32[]{:S(2)}, u32[]{:S(2)}) collective-permute-start(f32[16,128]{1,0:T(8,128)S(1)} %get-tuple-element.6.refs_0_), channel_id=1, source_target_pairs={{13,0},{12,1},{9,4},{8,5},{5,8},{4,9},{1,12},{0,13},{15,2},{14,3},... | collective-permute-start | bytes 24584 | tf_op jit(solution)/shard_map/ppermute | solution.py:162
  24.6 4.0 %collective-permute-start.10 = (f32[16,128]{1,0:T(8,128)S(1)}, f32[16,128]{1,0:T(8,128)S(1)}, u32[]{:S(2)}, u32[]{:S(2)}) collective-permute-start(f32[16,128]{1,0:T(8,128)S(1)} %get-tuple-element.6.refs_0_), channel_id=1, source_target_pairs={{9,0},{8,1},{13,4},{12,5},{1,8},{0,9},{5,12},{4,13},{11,2},{10,3},... | collective-permute-start | bytes 24584 | tf_op jit(solution)/shard_map/ppermute | solution.py:162
  24.6 4.0 %collective-permute-start.9 = (f32[16,128]{1,0:T(8,128)S(1)}, f32[16,128]{1,0:T(8,128)S(1)}, u32[]{:S(2)}, u32[]{:S(2)}) collective-permute-start(f32[16,128]{1,0:T(8,128)S(1)} %get-tuple-element.6.refs_0_), channel_id=1, source_target_pairs={{5,0},{4,1},{1,4},{0,5},{13,8},{12,9},{9,12},{8,13},{7,2},{6,3},{3... | collective-permute-start | bytes 24584 | tf_op jit(solution)/shard_map/ppermute | solution.py:162

commit v16 on v13

--- a/solution.py
+++ b/solution.py
@@ -9,6 +9,8 @@
 LINE = ("blk",)
 DIRECT = 8
 VMEM = pltpu.CompilerParams(vmem_limit_bytes=40 * 1024 * 1024)
+PARTIALS, PARTIALS_BACK = (0, 2, 3, 1), (0, 3, 1, 2)
+SUMS = (0, 1, 3, 2)
 HALF = 8
 
 
@@ -37,45 +39,58 @@
     )
 
 
+def columns_of(block, feature_count):
+    scaled = block[:feature_count, :]
+    columns = jnp.concatenate([scaled, norm_rows(scaled, 0)], axis=0)
+    return columns.astype(jnp.float32).T.astype(jnp.bfloat16)
+
+
+def prepare_kernel(feature_count, plane_count, *refs):
+    plane_refs, line_refs = refs[:plane_count], refs[plane_count:-2]
+    rows_ref, columns_ref = refs[-2:]
+    for number, ref in enumerate(plane_refs):
+        rows_ref[number] = jnp.concatenate([ref[...], norm_rows(ref[...], 1)], axis=0)
+    for number, ref in enumerate(line_refs):
+        columns_ref[number] = columns_of(ref[...], feature_count)
+
+
 def image_kernel(feature_count, plane_count, *refs):
-    plane_refs = refs[:plane_count]
-    line_refs = refs[plane_count:-3]
-    noise_ref, probes_ref, partial_ref = refs[-3:]
-    rows = [jnp.concatenate([ref[...], norm_rows(ref[...], 1)], axis=0) for ref in plane_refs]
-
-    def add_blocks(blocks, totals):
-        columns = []
-        for block in blocks:
-            scaled = block[:feature_count, :]
-            block_columns = jnp.concatenate([scaled, norm_rows(scaled, 0)], axis=0)
-            columns.append(block_columns.astype(jnp.float32).T.astype(jnp.bfloat16))
-        columns = jnp.concatenate(columns, axis=0)
-        probes = jnp.concatenate([block[feature_count:, :] for block in blocks], axis=1)
+    rows_ref, noise_ref, probes_ref = refs[:3]
+    columns_ref, *line_refs = refs[3:-1]
+    partial_ref = refs[-1]
+    totals = [noise_ref[...] * probes_ref[...]]
+    totals += [jnp.zeros(probes_ref.shape, jnp.float32)] * (plane_count - 1)
+
+    def add_columns(columns, probes, totals):
         result = []
-        for own, total in zip(rows, totals):
-            exponent = jnp.dot(columns, own, preferred_element_type=jnp.float32)
+        for number, total in enumerate(totals):
+            exponent = jnp.dot(columns, rows_ref[number], preferred_element_type=jnp.float32)
             weights = jnp.exp(exponent).astype(jnp.bfloat16)
             result.append(total + jnp.dot(probes, weights, preferred_element_type=jnp.float32))
         return result
 
-    totals = [noise_ref[...] * probes_ref[...]]
-    totals += [jnp.zeros(probes_ref.shape, jnp.float32)] * (plane_count - 1)
     if len(line_refs[0].shape) == 2:
-        totals = add_blocks([ref[...] for ref in line_refs], totals)
+        *early, late = [ref[...] for ref in line_refs]
+        columns = [columns_ref[number] for number in range(len(early))]
+        columns = jnp.concatenate(columns + [columns_of(late, feature_count)], axis=0)
+        probes = [block[feature_count:, :] for block in early + [late]]
+        totals = add_columns(columns, jnp.concatenate(probes, axis=1), totals)
     else:
-        totals = lax.fori_loop(
-            0,
-            line_refs[0].shape[0],
-            lambda number, value: add_blocks([line_refs[0][number]], value),
-            totals,
-        )
+
+        def add_block(number, totals):
+            block = line_refs[0][number]
+            return add_columns(
+                columns_of(block, feature_count), block[feature_count:, :], totals
+            )
+
+        totals = lax.fori_loop(0, line_refs[0].shape[0], add_block, totals)
     for number, total in enumerate(totals):
         partial_ref[number] = total
     partial_ref[plane_count] = probes_ref[...]
 
 
 def combine_kernel(plane_count, *refs):
-    partial_refs = [refs[number] for number in exchange_order(plane_count)]
+    partial_refs = in_order(refs[:-2], PARTIALS_BACK)
     image_ref, sums_ref = refs[-2:]
     lane = lax.broadcasted_iota(jnp.int32, sums_ref.shape, 1)
     products = [0.0, 0.0, 0.0]
@@ -123,8 +138,8 @@
     return step ^ number if paired(count) else (number - step) % count
 
 
-def exchange_order(count):
-    return (0, 1, 3, 2) if count == 4 else tuple(range(count))
+def in_order(blocks, places):
+    return [blocks[place] for place in places] if len(blocks) == len(places) else blocks
 
 
 def everywhere(value, axes, count):
@@ -173,11 +188,28 @@
         )(scaled, probes)
         lines = along_line(line, line_count, plane_shape[1])
         planes = plane_blocks(scaled, plane_shape)
+        if len(lines) > 1:
+            early, late = lines[:1] + lines[:1:-1], lines[1]
+        else:
+            early, late = [], lines[0]
+        depth = feature_count + 2 * HALF
+        work = plane_count * width * width
+        rows, columns = pl.pallas_call(
+            lambda *refs: prepare_kernel(feature_count, plane_count, *refs),
+            out_shape=(
+                jax.ShapeDtypeStruct((plane_count, depth, width), jnp.bfloat16),
+                jax.ShapeDtypeStruct((max(len(early), 1), width, depth), jnp.bfloat16),
+            ),
+            compiler_params=VMEM,
+            cost_estimate=pl.CostEstimate(
+                flops=6 * work * depth, bytes_accessed=4 * plane_count * width, transcendentals=3 * work
+            ),
+        )(*planes, *early)
         partial = pl.pallas_call(
             lambda *refs: image_kernel(feature_count, plane_count, *refs),
             out_shape=jax.ShapeDtypeStruct((plane_count + 1, probe_count, width), jnp.float32),
             compiler_params=VMEM,
-        )(*planes, *lines, noise_var[None, :], probes)
+        )(rows, noise_var[None, :], probes, columns, *early, late)
         partials = everywhere(partial, PLANE, plane_count)
         image, sums = pl.pallas_call(
             lambda *refs: combine_kernel(plane_count, *refs),
@@ -186,10 +218,10 @@
                 jax.ShapeDtypeStruct((probe_count, 128), jnp.float32),
             ),
             compiler_params=VMEM,
-        )(*[partials[number] for number in exchange_order(plane_count)])
+        )(*in_order(partials, PARTIALS))
         outs = (jax.ShapeDtypeStruct(probes.shape, jnp.float32),) * 3
         return pl.pallas_call(finish_kernel, out_shape=outs, compiler_params=VMEM)(
-            image, probes, *along_line(sums, line_count, plane_shape[1])
+            image, probes, *in_order(along_line(sums, line_count, plane_shape[1]), SUMS)
         )
 
     return local

time: 29.3 us -> 29.6 us (1.010)
  local copies, waits for them, and re-layouts: 0.01 us -> 0.68 us
  starting transfers between devices: 13.6 us -> 13.3 us
    unnamed x4, local copies, waits for them, and re-layouts: 0.01 us -> 0.68 us
    ppermute x6, starting transfers between devices: 8.88 us -> 8.58 us  [along_line(): blocks.append(lax.ppermute(value, LINE + ('sub',), pairs))]
  transfers between devices with their start and end apart: 12 -> 12, of which waited for: 7 -> 7; matrix products, arithmetic and copies ran while one was open for 0% -> 0% of each run, Pallas kernels for 0% -> 1%
where the time goes in v16:
time: 29.6 us; the launch traced here: 29.5 us
  starting transfers between devices  13.3 us (45%)
  waiting for transfers between devices  11.1 us (38%)
  Pallas kernels  2.86 us (10%)
  other arithmetic  0.93 us (3%)
  local copies, waits for them, and re-layouts  0.68 us (2%)
  between operations  0.67 us (2%)
    ppermute x6, starting transfers between devices, along_line(): blocks.append(lax.ppermute(value, LINE + ('sub',), pairs))  8.58 us
    ppermute x6, waiting for transfers between devices, everywhere(): lax.ppermute(value, axes, [(source_of(i, step, count), i) for i in range(...  6.72 us
    ppermute x6, starting transfers between devices, everywhere(): lax.ppermute(value, axes, [(source_of(i, step, count), i) for i in range(...  4.69 us
    ppermute x6, waiting for transfers between devices, along_line(): blocks.append(lax.ppermute(value, LINE + ('sub',), pairs))  4.34 us
    pallas_call x1, Pallas kernels, local(): pl.pallas_call(lambda *refs: image_kernel(feature_count, plane_count, *re...  1.76 us
    convert_element_type x1, other arithmetic, local(): (features.astype(jnp.float32) / lengthscale[:, None]).astype(jnp.bfloat16)  0.93 us
    pallas_call x1, Pallas kernels, local(): pl.pallas_call(finish_kernel, out_shape=outs, compiler_params=VMEM)  0.77 us
    unnamed x4, local copies, waits for them, and re-layouts  0.68 us
  transfers between devices with their start and end apart: 12, of which 7 were waited for; matrix products, arithmetic and copies ran while one was open for 0% of the time, Pallas kernels for 1%

profile of v16, /device:TPU:0, one launch (start us, length us, event | category | flops | bytes accessed | tf_op | source)
XLA Modules:
  0.0 29.5 jit_solution(14998274153453239086)
XLA Ops:
  0.6 0.0 copy-start
  0.6 0.9 %divide_convert_fusion.scaled_ref.refs_0_ = bf16[128,256]{1,0:T(8,128)(2,1)S(1)} fusion(bf16[128,256]{1,0:T(8,128)(2,1)} %param.4, f32[128]{0:T(128)} %param.5), kind=kLoop, calls=%fused_computation | loop fusion | flops 98304 | bytes 131584 | tf_op jit(solution)/shard_map/convert_element_type | solution.py:183
  1.6 0.5 %collective-permute-start = (bf16[128,256]{1,0:T(8,128)(2,1)S(1)}, bf16[128,256]{1,0:T(8,128)(2,1)S(1)}, u32[]{:S(2)}, u32[]{:S(2)}) collective-permute-start(bf16[128,256]{1,0:T(8,128)(2,1)S(1)} %divide_convert_fusion.scaled_ref.refs_0_), channel_id=1, source_target_pairs={{1,0},{0,1},{3,2},{2,3},{5,4},{4,5},{7,6},{6,7},{9,8},{8,9},{11,10... | collective-permute-start | bytes 196616 | tf_op jit(solution)/shard_map/ppermute | solution.py:149
  2.1 0.0 copy-done
  2.1 4.8 %collective-permute-start.3 = (bf16[144,256]{1,0:T(8,128)(2,1)S(1)}, bf16[144,256]{1,0:T(8,128)(2,1)S(1)}, u32[]{:S(2)}, u32[]{:S(2)}) collective-permute-start(bf16[144,256]{1,0:T(8,128)(2,1)S(1)} %shard_map.67.refs_4_), channel_id=1, source_target_pairs={{13,0},{12,1},{9,4},{8,5},{5,8},{4,9},{1,12},{0,13},{15,2},{14,3},... | collective-permute-start | bytes 221192 | tf_op jit(solution)/shard_map/ppermute | solution.py:164
  6.9 0.0 collective-permute-start.4
  6.9 1.5 %collective-permute-start.1 = (bf16[128,256]{1,0:T(8,128)(2,1)S(1)}, bf16[128,256]{1,0:T(8,128)(2,1)S(1)}, u32[]{:S(2)}, u32[]{:S(2)}) collective-permute-start(bf16[128,256]{1,0:T(8,128)(2,1)S(1)} %divide_convert_fusion.scaled_ref.refs_0_), channel_id=1, source_target_pairs={{2,0},{0,2},{3,1},{1,3},{6,4},{4,6},{7,5},{5,7},{10,8},{8,10},{11,... | collective-permute-start | bytes 196616 | tf_op jit(solution)/shard_map/ppermute | solution.py:149
  8.4 0.0 collective-permute-done.refs_1_
  8.4 0.5 %collective-permute-start.2 = (bf16[128,256]{1,0:T(8,128)(2,1)S(1)}, bf16[128,256]{1,0:T(8,128)(2,1)S(1)}, u32[]{:S(2)}, u32[]{:S(2)}) collective-permute-start(bf16[128,256]{1,0:T(8,128)(2,1)S(1)} %collective-permute-done.refs_1_), channel_id=1, source_target_pairs={{2,0},{0,2},{3,1},{1,3},{6,4},{4,6},{7,5},{5,7},{10,8},{8,10},{11,... | collective-permute-start | bytes 196616 | tf_op jit(solution)/shard_map/ppermute | solution.py:149
  8.9 0.0 collective-permute-start.5
  8.9 2.7 %collective-permute-done.1.refs_2_ = bf16[128,256]{1,0:T(8,128)(2,1)S(1)} collective-permute-done((bf16[128,256]{1,0:T(8,128)(2,1)S(1)}, bf16[128,256]{1,0:T(8,128)(2,1)S(1)}, u32[]{:S(2)}, u32[]{:S(2)}) %collective-permute-start.1) | collective-permute-done | bytes 65568 | tf_op jit(solution)/shard_map/ppermute | solution.py:149
  11.6 0.0 collective-permute-done.3.refs_5_
  11.6 1.5 %collective-permute-done.4.refs_6_ = bf16[144,256]{1,0:T(8,128)(2,1)S(1)} collective-permute-done((bf16[144,256]{1,0:T(8,128)(2,1)S(1)}, bf16[144,256]{1,0:T(8,128)(2,1)S(1)}, u32[]{:S(2)}, u32[]{:S(2)}) %collective-permute-start.4) | collective-permute-done | bytes 73760 | tf_op jit(solution)/shard_map/ppermute | solution.py:164
  13.1 0.0 collective-permute-done.2.refs_3_
  13.1 0.2 shard_map.68
  13.3 1.3 %collective-permute-done.5.refs_7_ = bf16[144,256]{1,0:T(8,128)(2,1)S(1)} collective-permute-done((bf16[144,256]{1,0:T(8,128)(2,1)S(1)}, bf16[144,256]{1,0:T(8,128)(2,1)S(1)}, u32[]{:S(2)}, u32[]{:S(2)}) %collective-permute-start.5) | collective-permute-done | bytes 73760 | tf_op jit(solution)/shard_map/ppermute | solution.py:164
  14.6 0.0 copy-start.1
  14.6 0.7 %copy-done.1 = f32[256]{0:T(256)S(1)} copy-done((f32[256]{0:T(256)S(1)}, f32[256]{0:T(256)}, u32[]{:S(2)}) %copy-start.1) | copy-done | bytes 1048
  15.3 1.8 %shard_map.69.refs_0_ = f32[5,16,256]{2,1,0:T(8,128)S(1)} custom-call(bf16[4,144,256]{2,1,0:T(8,128)(2,1)S(1)} %get-tuple-element.7.refs_0_, f32[1,256]{1,0:T(1,128)S(1)} %bitcast.1, f32[16,256]{1,0:T(8,128)S(1)} %copy-done, bf16[3,256,144]{2,1,0:T(8,128)(2,1)S(1)} %get-tuple-element.8.refs_3_, bf16[144,256]{1,0:T(8,128)(2,1)S(1)} %shard_map.67.refs_4_, ...), custom_call_target="tpu_custom_call" | custom-call | tf_op jit(solution)/shard_map/pallas_call | solution.py:208
  17.1 1.5 %collective-permute-start.6 = (f32[5,16,256]{2,1,0:T(8,128)S(1)}, f32[5,16,256]{2,1,0:T(8,128)S(1)}, u32[]{:S(2)}, u32[]{:S(2)}) collective-permute-start(f32[5,16,256]{2,1,0:T(8,128)S(1)} %shard_map.69.refs_0_), channel_id=1, source_target_pairs={{2,0},{3,1},{0,2},{1,3},{6,4},{7,5},{4,6},{5,7},{10,8},{11,9},{8,1... | collective-permute-start | bytes 245768 | tf_op jit(solution)/shard_map/ppermute | solution.py:149
  18.6 0.0 collective-permute-start.7
  18.6 0.6 %collective-permute-start.8 = (f32[5,16,256]{2,1,0:T(8,128)S(1)}, f32[5,16,256]{2,1,0:T(8,128)S(1)}, u32[]{:S(2)}, u32[]{:S(2)}) collective-permute-start(f32[5,16,256]{2,1,0:T(8,128)S(1)} %shard_map.69.refs_0_), channel_id=1, source_target_pairs={{1,0},{0,1},{3,2},{2,3},{5,4},{4,5},{7,6},{6,7},{9,8},{8,9},{11,10... | collective-permute-start | bytes 245768 | tf_op jit(solution)/shard_map/ppermute | solution.py:149
  19.2 2.3 %collective-permute-done.6.refs_1_ = f32[5,16,256]{2,1,0:T(8,128)S(1)} collective-permute-done((f32[5,16,256]{2,1,0:T(8,128)S(1)}, f32[5,16,256]{2,1,0:T(8,128)S(1)}, u32[]{:S(2)}, u32[]{:S(2)}) %collective-permute-start.6) | collective-permute-done | bytes 81952 | tf_op jit(solution)/shard_map/ppermute | solution.py:149
  21.5 1.8 %collective-permute-done.7.refs_2_ = f32[5,16,256]{2,1,0:T(8,128)S(1)} collective-permute-done((f32[5,16,256]{2,1,0:T(8,128)S(1)}, f32[5,16,256]{2,1,0:T(8,128)S(1)}, u32[]{:S(2)}, u32[]{:S(2)}) %collective-permute-start.7) | collective-permute-done | bytes 81952 | tf_op jit(solution)/shard_map/ppermute | solution.py:149
  23.3 0.0 collective-permute-done.8.refs_3_
  23.3 0.1 shard_map.70
  23.4 1.2 %collective-permute-start.10 = (f32[16,128]{1,0:T(8,128)S(1)}, f32[16,128]{1,0:T(8,128)S(1)}, u32[]{:S(2)}, u32[]{:S(2)}) collective-permute-start(f32[16,128]{1,0:T(8,128)S(1)} %get-tuple-element.10.refs_0_), channel_id=1, source_target_pairs={{13,0},{12,1},{9,4},{8,5},{5,8},{4,9},{1,12},{0,13},{15,2},{14,3},... | collective-permute-start | bytes 24584 | tf_op jit(solution)/shard_map/ppermute | solution.py:164
  24.6 0.0 collective-permute-start.11
  24.6 2.6 %collective-permute-start.9 = (f32[16,128]{1,0:T(8,128)S(1)}, f32[16,128]{1,0:T(8,128)S(1)}, u32[]{:S(2)}, u32[]{:S(2)}) collective-permute-start(f32[16,128]{1,0:T(8,128)S(1)} %get-tuple-element.10.refs_0_), channel_id=1, source_target_pairs={{5,0},{4,1},{1,4},{0,5},{13,8},{12,9},{9,12},{8,13},{7,2},{6,3},{3... | collective-permute-start | bytes 24584 | tf_op jit(solution)/shard_map/ppermute | solution.py:164
  27.2 1.1 %collective-permute-done.10.refs_2_ = f32[16,128]{1,0:T(8,128)S(1)} collective-permute-done((f32[16,128]{1,0:T(8,128)S(1)}, f32[16,128]{1,0:T(8,128)S(1)}, u32[]{:S(2)}, u32[]{:S(2)}) %collective-permute-start.10) | collective-permute-done | bytes 8224 | tf_op jit(solution)/shard_map/ppermute | solution.py:164
  28.3 0.4 %collective-permute-done.11.refs_3_ = f32[16,128]{1,0:T(8,128)S(1)} collective-permute-done((f32[16,128]{1,0:T(8,128)S(1)}, f32[16,128]{1,0:T(8,128)S(1)}, u32[]{:S(2)}, u32[]{:S(2)}) %collective-permute-start.11) | collective-permute-done | bytes 8224 | tf_op jit(solution)/shard_map/ppermute | solution.py:164
  28.7 0.0 collective-permute-done.9.refs_1_
  28.7 0.8 %shard_map.71 = (f32[16,256]{1,0:T(8,128)}, f32[16,256]{1,0:T(8,128)}, f32[16,256]{1,0:T(8,128)}) custom-call(f32[16,256]{1,0:T(8,128)S(1)} %get-tuple-element.9.image_ref, f32[16,256]{1,0:T(8,128)S(1)} %copy-done, f32[16,128]{1,0:T(8,128)S(1)} %get-tuple-element.10.refs_0_, f32[16,128]{1,0:T(8,128)S(1)} %collective-permute-done.9.refs_1_, ...), custom_call_target="tpu_custom_call" | custom-call | tf_op jit(solution)/shard_map/pallas_call | solution.py:223
  (1 shorter events, 0.0 us)
Async XLA Ops:
  0.6 1.5 %copy-start = (f32[16,256]{1,0:T(8,128)S(1)}, f32[16,256]{1,0:T(8,128)}, u32[]{:S(2)}) copy-start(f32[16,256]{1,0:T(8,128)} %probes_ref.3) | copy-start | bytes 49156
  1.6 6.8 %collective-permute-start = (bf16[128,256]{1,0:T(8,128)(2,1)S(1)}, bf16[128,256]{1,0:T(8,128)(2,1)S(1)}, u32[]{:S(2)}, u32[]{:S(2)}) collective-permute-start(bf16[128,256]{1,0:T(8,128)(2,1)S(1)} %divide_convert_fusion.scaled_ref.refs_0_), channel_id=1, source_target_pairs={{1,0},{0,1},{3,2},{2,3},{5,4},{4,5},{7,6},{6,7},{9,8},{8,9},{11,10... | collective-permute-start | bytes 196616 | tf_op jit(solution)/shard_map/ppermute | solution.py:149
  2.1 9.5 %collective-permute-start.3 = (bf16[144,256]{1,0:T(8,128)(2,1)S(1)}, bf16[144,256]{1,0:T(8,128)(2,1)S(1)}, u32[]{:S(2)}, u32[]{:S(2)}) collective-permute-start(bf16[144,256]{1,0:T(8,128)(2,1)S(1)} %shard_map.67.refs_4_), channel_id=1, source_target_pairs={{13,0},{12,1},{9,4},{8,5},{5,8},{4,9},{1,12},{0,13},{15,2},{14,3},... | collective-permute-start | bytes 221192 | tf_op jit(solution)/shard_map/ppermute | solution.py:164
  6.9 6.2 %collective-permute-start.4 = (bf16[144,256]{1,0:T(8,128)(2,1)S(1)}, bf16[144,256]{1,0:T(8,128)(2,1)S(1)}, u32[]{:S(2)}, u32[]{:S(2)}) collective-permute-start(bf16[144,256]{1,0:T(8,128)(2,1)S(1)} %shard_map.67.refs_4_), channel_id=1, source_target_pairs={{9,0},{8,1},{13,4},{12,5},{1,8},{0,9},{5,12},{4,13},{11,2},{10,3},... | collective-permute-start | bytes 221192 | tf_op jit(solution)/shard_map/ppermute | solution.py:164
  6.9 4.7 %collective-permute-start.1 = (bf16[128,256]{1,0:T(8,128)(2,1)S(1)}, bf16[128,256]{1,0:T(8,128)(2,1)S(1)}, u32[]{:S(2)}, u32[]{:S(2)}) collective-permute-start(bf16[128,256]{1,0:T(8,128)(2,1)S(1)} %divide_convert_fusion.scaled_ref.refs_0_), channel_id=1, source_target_pairs={{2,0},{0,2},{3,1},{1,3},{6,4},{4,6},{7,5},{5,7},{10,8},{8,10},{11,... | collective-permute-start | bytes 196616 | tf_op jit(solution)/shard_map/ppermute | solution.py:149
  8.4 4.7 %collective-permute-start.2 = (bf16[128,256]{1,0:T(8,128)(2,1)S(1)}, bf16[128,256]{1,0:T(8,128)(2,1)S(1)}, u32[]{:S(2)}, u32[]{:S(2)}) collective-permute-start(bf16[128,256]{1,0:T(8,128)(2,1)S(1)} %collective-permute-done.refs_1_), channel_id=1, source_target_pairs={{2,0},{0,2},{3,1},{1,3},{6,4},{4,6},{7,5},{5,7},{10,8},{8,10},{11,... | collective-permute-start | bytes 196616 | tf_op jit(solution)/shard_map/ppermute | solution.py:149
  8.9 5.7 %collective-permute-start.5 = (bf16[144,256]{1,0:T(8,128)(2,1)S(1)}, bf16[144,256]{1,0:T(8,128)(2,1)S(1)}, u32[]{:S(2)}, u32[]{:S(2)}) collective-permute-start(bf16[144,256]{1,0:T(8,128)(2,1)S(1)} %shard_map.67.refs_4_), channel_id=1, source_target_pairs={{5,0},{4,1},{1,4},{0,5},{13,8},{12,9},{9,12},{8,13},{7,2},{6,3},{3... | collective-permute-start | bytes 221192 | tf_op jit(solution)/shard_map/ppermute | solution.py:164
  14.6 0.7 %copy-start.1 = (f32[256]{0:T(256)S(1)}, f32[256]{0:T(256)}, u32[]{:S(2)}) copy-start(f32[256]{0:T(256)} %param.6) | copy-start | bytes 3076
  17.1 4.4 %collective-permute-start.6 = (f32[5,16,256]{2,1,0:T(8,128)S(1)}, f32[5,16,256]{2,1,0:T(8,128)S(1)}, u32[]{:S(2)}, u32[]{:S(2)}) collective-permute-start(f32[5,16,256]{2,1,0:T(8,128)S(1)} %shard_map.69.refs_0_), channel_id=1, source_target_pairs={{2,0},{3,1},{0,2},{1,3},{6,4},{7,5},{4,6},{5,7},{10,8},{11,9},{8,1... | collective-permute-start | bytes 245768 | tf_op jit(solution)/shard_map/ppermute | solution.py:149
  18.6 4.7 %collective-permute-start.7 = (f32[5,16,256]{2,1,0:T(8,128)S(1)}, f32[5,16,256]{2,1,0:T(8,128)S(1)}, u32[]{:S(2)}, u32[]{:S(2)}) collective-permute-start(f32[5,16,256]{2,1,0:T(8,128)S(1)} %shard_map.69.refs_0_), channel_id=1, source_target_pairs={{3,0},{2,1},{1,2},{0,3},{7,4},{6,5},{5,6},{4,7},{11,8},{10,9},{9,1... | collective-permute-start | bytes 245768 | tf_op jit(solution)/shard_map/ppermute | solution.py:149
  18.6 4.7 %collective-permute-start.8 = (f32[5,16,256]{2,1,0:T(8,128)S(1)}, f32[5,16,256]{2,1,0:T(8,128)S(1)}, u32[]{:S(2)}, u32[]{:S(2)}) collective-permute-start(f32[5,16,256]{2,1,0:T(8,128)S(1)} %shard_map.69.refs_0_), channel_id=1, source_target_pairs={{1,0},{0,1},{3,2},{2,3},{5,4},{4,5},{7,6},{6,7},{9,8},{8,9},{11,10... | collective-permute-start | bytes 245768 | tf_op jit(solution)/shard_map/ppermute | solution.py:149
  23.4 4.9 %collective-permute-start.10 = (f32[16,128]{1,0:T(8,128)S(1)}, f32[16,128]{1,0:T(8,128)S(1)}, u32[]{:S(2)}, u32[]{:S(2)}) collective-permute-start(f32[16,128]{1,0:T(8,128)S(1)} %get-tuple-element.10.refs_0_), channel_id=1, source_target_pairs={{13,0},{12,1},{9,4},{8,5},{5,8},{4,9},{1,12},{0,13},{15,2},{14,3},... | collective-permute-start | bytes 24584 | tf_op jit(solution)/shard_map/ppermute | solution.py:164
  24.6 4.1 %collective-permute-start.11 = (f32[16,128]{1,0:T(8,128)S(1)}, f32[16,128]{1,0:T(8,128)S(1)}, u32[]{:S(2)}, u32[]{:S(2)}) collective-permute-start(f32[16,128]{1,0:T(8,128)S(1)} %get-tuple-element.10.refs_0_), channel_id=1, source_target_pairs={{9,0},{8,1},{13,4},{12,5},{1,8},{0,9},{5,12},{4,13},{11,2},{10,3},... | collective-permute-start | bytes 24584 | tf_op jit(solution)/shard_map/ppermute | solution.py:164
  24.6 4.1 %collective-permute-start.9 = (f32[16,128]{1,0:T(8,128)S(1)}, f32[16,128]{1,0:T(8,128)S(1)}, u32[]{:S(2)}, u32[]{:S(2)}) collective-permute-start(f32[16,128]{1,0:T(8,128)S(1)} %get-tuple-element.10.refs_0_), channel_id=1, source_target_pairs={{5,0},{4,1},{1,4},{0,5},{13,8},{12,9},{9,12},{8,13},{7,2},{6,3},{3... | collective-permute-start | bytes 24584 | tf_op jit(solution)/shard_map/ppermute | solution.py:164

commit v17 on v16

--- a/solution.py
+++ b/solution.py
@@ -46,8 +46,9 @@
 
 
 def prepare_kernel(feature_count, plane_count, *refs):
-    plane_refs, line_refs = refs[:plane_count], refs[plane_count:-2]
-    rows_ref, columns_ref = refs[-2:]
+    plane_refs, line_refs = refs[:plane_count], refs[plane_count:-5]
+    noise_ref, probes_ref, rows_ref, columns_ref, start_ref = refs[-5:]
+    start_ref[...] = noise_ref[...] * probes_ref[...]
     for number, ref in enumerate(plane_refs):
         rows_ref[number] = jnp.concatenate([ref[...], norm_rows(ref[...], 1)], axis=0)
     for number, ref in enumerate(line_refs):
@@ -55,10 +56,10 @@
 
 
 def image_kernel(feature_count, plane_count, *refs):
-    rows_ref, noise_ref, probes_ref = refs[:3]
+    rows_ref, start_ref, probes_ref = refs[:3]
     columns_ref, *line_refs = refs[3:-1]
     partial_ref = refs[-1]
-    totals = [noise_ref[...] * probes_ref[...]]
+    totals = [start_ref[...]]
     totals += [jnp.zeros(probes_ref.shape, jnp.float32)] * (plane_count - 1)
 
     def add_columns(columns, probes, totals):
@@ -194,22 +195,23 @@
             early, late = [], lines[0]
         depth = feature_count + 2 * HALF
         work = plane_count * width * width
-        rows, columns = pl.pallas_call(
+        rows, columns, start = pl.pallas_call(
             lambda *refs: prepare_kernel(feature_count, plane_count, *refs),
             out_shape=(
                 jax.ShapeDtypeStruct((plane_count, depth, width), jnp.bfloat16),
                 jax.ShapeDtypeStruct((max(len(early), 1), width, depth), jnp.bfloat16),
+                jax.ShapeDtypeStruct(probes.shape, jnp.float32),
             ),
             compiler_params=VMEM,
             cost_estimate=pl.CostEstimate(
                 flops=6 * work * depth, bytes_accessed=4 * plane_count * width, transcendentals=3 * work
             ),
-        )(*planes, *early)
+        )(*planes, *early, noise_var[None, :], probes)
         partial = pl.pallas_call(
             lambda *refs: image_kernel(feature_count, plane_count, *refs),
             out_shape=jax.ShapeDtypeStruct((plane_count + 1, probe_count, width), jnp.float32),
             compiler_params=VMEM,
-        )(rows, noise_var[None, :], probes, columns, *early, late)
+        )(rows, start, probes, columns, *early, late)
         partials = everywhere(partial, PLANE, plane_count)
         image, sums = pl.pallas_call(
             lambda *refs: combine_kernel(plane_count, *refs),

time: 29.6 us -> 29 us (0.980)
  local copies, waits for them, and re-layouts: 0.68 us -> 0.01 us
    unnamed x4, local copies, waits for them, and re-layouts: 0.68 us -> 0.01 us
  transfers between devices with their start and end apart: 12 -> 12, of which waited for: 7 -> 8; matrix products, arithmetic and copies ran while one was open for 0% -> 0% of each run, Pallas kernels for 1% -> 1%
where the time goes in v17:
time: 29 us; the launch traced here: 28.8 us
  starting transfers between devices  13.3 us (46%)
  waiting for transfers between devices  11 us (38%)
  Pallas kernels  2.86 us (10%)
  other arithmetic  0.93 us (3%)
  between operations  0.68 us (2%)
    ppermute x6, starting transfers between devices, along_line(): blocks.append(lax.ppermute(value, LINE + ('sub',), pairs))  8.59 us
    ppermute x6, waiting for transfers between devices, everywhere(): lax.ppermute(value, axes, [(source_of(i, step, count), i) for i in range(...  6.72 us
    ppermute x6, starting transfers between devices, everywhere(): lax.ppermute(value, axes, [(source_of(i, step, count), i) for i in range(...  4.69 us
    ppermute x6, waiting for transfers between devices, along_line(): blocks.append(lax.ppermute(value, LINE + ('sub',), pairs))  4.33 us
    pallas_call x1, Pallas kernels, local(): pl.pallas_call(lambda *refs: image_kernel(feature_count, plane_count, *re...  1.77 us
    convert_element_type x1, other arithmetic, local(): (features.astype(jnp.float32) / lengthscale[:, None]).astype(jnp.bfloat16)  0.93 us
    pallas_call x1, Pallas kernels, local(): pl.pallas_call(finish_kernel, out_shape=outs, compiler_params=VMEM)  0.77 us
  transfers between devices with their start and end apart: 12, of which 8 were waited for; matrix products, arithmetic and copies ran while one was open for 0% of the time, Pallas kernels for 1%

profile of v17, /device:TPU:0, one launch (start us, length us, event | category | flops | bytes accessed | tf_op | source)
XLA Modules:
  0.0 28.8 jit_solution(3023366887853229311)
XLA Ops:
  0.6 0.0 copy-start
  0.6 0.9 %divide_convert_fusion.scaled_ref.refs_0_ = bf16[128,256]{1,0:T(8,128)(2,1)S(1)} fusion(bf16[128,256]{1,0:T(8,128)(2,1)} %param.4, f32[128]{0:T(128)} %param.5), kind=kLoop, calls=%fused_computation | loop fusion | flops 98304 | bytes 131584 | tf_op jit(solution)/shard_map/convert_element_type | solution.py:184
  1.6 0.5 %collective-permute-start = (bf16[128,256]{1,0:T(8,128)(2,1)S(1)}, bf16[128,256]{1,0:T(8,128)(2,1)S(1)}, u32[]{:S(2)}, u32[]{:S(2)}) collective-permute-start(bf16[128,256]{1,0:T(8,128)(2,1)S(1)} %divide_convert_fusion.scaled_ref.refs_0_), channel_id=1, source_target_pairs={{1,0},{0,1},{3,2},{2,3},{5,4},{4,5},{7,6},{6,7},{9,8},{8,9},{11,10... | collective-permute-start | bytes 196616 | tf_op jit(solution)/shard_map/ppermute | solution.py:150
  2.1 0.0 copy-done
  2.1 0.0 copy-start.1
  2.1 4.8 %collective-permute-start.3 = (bf16[144,256]{1,0:T(8,128)(2,1)S(1)}, bf16[144,256]{1,0:T(8,128)(2,1)S(1)}, u32[]{:S(2)}, u32[]{:S(2)}) collective-permute-start(bf16[144,256]{1,0:T(8,128)(2,1)S(1)} %shard_map.67.refs_4_), channel_id=1, source_target_pairs={{13,0},{12,1},{9,4},{8,5},{5,8},{4,9},{1,12},{0,13},{15,2},{14,3},... | collective-permute-start | bytes 221192 | tf_op jit(solution)/shard_map/ppermute | solution.py:165
  6.9 0.0 collective-permute-start.4
  6.9 1.5 %collective-permute-start.1 = (bf16[128,256]{1,0:T(8,128)(2,1)S(1)}, bf16[128,256]{1,0:T(8,128)(2,1)S(1)}, u32[]{:S(2)}, u32[]{:S(2)}) collective-permute-start(bf16[128,256]{1,0:T(8,128)(2,1)S(1)} %divide_convert_fusion.scaled_ref.refs_0_), channel_id=1, source_target_pairs={{2,0},{0,2},{3,1},{1,3},{6,4},{4,6},{7,5},{5,7},{10,8},{8,10},{11,... | collective-permute-start | bytes 196616 | tf_op jit(solution)/shard_map/ppermute | solution.py:150
  8.4 0.0 collective-permute-done.refs_1_
  8.4 0.5 %collective-permute-start.2 = (bf16[128,256]{1,0:T(8,128)(2,1)S(1)}, bf16[128,256]{1,0:T(8,128)(2,1)S(1)}, u32[]{:S(2)}, u32[]{:S(2)}) collective-permute-start(bf16[128,256]{1,0:T(8,128)(2,1)S(1)} %collective-permute-done.refs_1_), channel_id=1, source_target_pairs={{2,0},{0,2},{3,1},{1,3},{6,4},{4,6},{7,5},{5,7},{10,8},{8,10},{11,... | collective-permute-start | bytes 196616 | tf_op jit(solution)/shard_map/ppermute | solution.py:150
  8.9 0.0 collective-permute-start.5
  8.9 2.7 %collective-permute-done.1.refs_2_ = bf16[128,256]{1,0:T(8,128)(2,1)S(1)} collective-permute-done((bf16[128,256]{1,0:T(8,128)(2,1)S(1)}, bf16[128,256]{1,0:T(8,128)(2,1)S(1)}, u32[]{:S(2)}, u32[]{:S(2)}) %collective-permute-start.1) | collective-permute-done | bytes 65568 | tf_op jit(solution)/shard_map/ppermute | solution.py:150
  11.6 0.0 collective-permute-done.3.refs_5_
  11.6 1.5 %collective-permute-done.4.refs_6_ = bf16[144,256]{1,0:T(8,128)(2,1)S(1)} collective-permute-done((bf16[144,256]{1,0:T(8,128)(2,1)S(1)}, bf16[144,256]{1,0:T(8,128)(2,1)S(1)}, u32[]{:S(2)}, u32[]{:S(2)}) %collective-permute-start.4) | collective-permute-done | bytes 73760 | tf_op jit(solution)/shard_map/ppermute | solution.py:165
  13.1 0.0 collective-permute-done.2.refs_3_
  13.1 0.0 copy-done.1
  13.1 0.2 shard_map.68
  13.3 1.3 %collective-permute-done.5.refs_7_ = bf16[144,256]{1,0:T(8,128)(2,1)S(1)} collective-permute-done((bf16[144,256]{1,0:T(8,128)(2,1)S(1)}, bf16[144,256]{1,0:T(8,128)(2,1)S(1)}, u32[]{:S(2)}, u32[]{:S(2)}) %collective-permute-start.5) | collective-permute-done | bytes 73760 | tf_op jit(solution)/shard_map/ppermute | solution.py:165
  14.7 1.8 %shard_map.69.refs_0_ = f32[5,16,256]{2,1,0:T(8,128)S(1)} custom-call(bf16[4,144,256]{2,1,0:T(8,128)(2,1)S(1)} %get-tuple-element.8.refs_0_, f32[16,256]{1,0:T(8,128)S(1)} %get-tuple-element.9.refs_1_, f32[16,256]{1,0:T(8,128)S(1)} %copy-done, bf16[3,256,144]{2,1,0:T(8,128)(2,1)S(1)} %get-tuple-element.10.refs_3_, bf16[144,256]{1,0:T(8,128)(2,1)S(1)} %shard_map.67.refs_4_, ...), custom_call_target="tpu_custom_call" | custom-call | tf_op jit(solution)/shard_map/pallas_call | solution.py:210
  16.4 1.5 %collective-permute-start.6 = (f32[5,16,256]{2,1,0:T(8,128)S(1)}, f32[5,16,256]{2,1,0:T(8,128)S(1)}, u32[]{:S(2)}, u32[]{:S(2)}) collective-permute-start(f32[5,16,256]{2,1,0:T(8,128)S(1)} %shard_map.69.refs_0_), channel_id=1, source_target_pairs={{2,0},{3,1},{0,2},{1,3},{6,4},{7,5},{4,6},{5,7},{10,8},{11,9},{8,1... | collective-permute-start | bytes 245768 | tf_op jit(solution)/shard_map/ppermute | solution.py:150
  17.9 0.0 collective-permute-start.7
  17.9 0.6 %collective-permute-start.8 = (f32[5,16,256]{2,1,0:T(8,128)S(1)}, f32[5,16,256]{2,1,0:T(8,128)S(1)}, u32[]{:S(2)}, u32[]{:S(2)}) collective-permute-start(f32[5,16,256]{2,1,0:T(8,128)S(1)} %shard_map.69.refs_0_), channel_id=1, source_target_pairs={{1,0},{0,1},{3,2},{2,3},{5,4},{4,5},{7,6},{6,7},{9,8},{8,9},{11,10... | collective-permute-start | bytes 245768 | tf_op jit(solution)/shard_map/ppermute | solution.py:150
  18.6 2.3 %collective-permute-done.6.refs_1_ = f32[5,16,256]{2,1,0:T(8,128)S(1)} collective-permute-done((f32[5,16,256]{2,1,0:T(8,128)S(1)}, f32[5,16,256]{2,1,0:T(8,128)S(1)}, u32[]{:S(2)}, u32[]{:S(2)}) %collective-permute-start.6) | collective-permute-done | bytes 81952 | tf_op jit(solution)/shard_map/ppermute | solution.py:150
  20.9 1.8 %collective-permute-done.7.refs_2_ = f32[5,16,256]{2,1,0:T(8,128)S(1)} collective-permute-done((f32[5,16,256]{2,1,0:T(8,128)S(1)}, f32[5,16,256]{2,1,0:T(8,128)S(1)}, u32[]{:S(2)}, u32[]{:S(2)}) %collective-permute-start.7) | collective-permute-done | bytes 81952 | tf_op jit(solution)/shard_map/ppermute | solution.py:150
  22.6 0.0 collective-permute-done.8.refs_3_
  22.6 0.1 shard_map.70
  22.7 1.2 %collective-permute-start.10 = (f32[16,128]{1,0:T(8,128)S(1)}, f32[16,128]{1,0:T(8,128)S(1)}, u32[]{:S(2)}, u32[]{:S(2)}) collective-permute-start(f32[16,128]{1,0:T(8,128)S(1)} %get-tuple-element.12.refs_0_), channel_id=1, source_target_pairs={{13,0},{12,1},{9,4},{8,5},{5,8},{4,9},{1,12},{0,13},{15,2},{14,3},... | collective-permute-start | bytes 24584 | tf_op jit(solution)/shard_map/ppermute | solution.py:165
  23.9 0.0 collective-permute-start.11
  23.9 2.6 %collective-permute-start.9 = (f32[16,128]{1,0:T(8,128)S(1)}, f32[16,128]{1,0:T(8,128)S(1)}, u32[]{:S(2)}, u32[]{:S(2)}) collective-permute-start(f32[16,128]{1,0:T(8,128)S(1)} %get-tuple-element.12.refs_0_), channel_id=1, source_target_pairs={{5,0},{4,1},{1,4},{0,5},{13,8},{12,9},{9,12},{8,13},{7,2},{6,3},{3... | collective-permute-start | bytes 24584 | tf_op jit(solution)/shard_map/ppermute | solution.py:165
  26.5 1.1 %collective-permute-done.10.refs_2_ = f32[16,128]{1,0:T(8,128)S(1)} collective-permute-done((f32[16,128]{1,0:T(8,128)S(1)}, f32[16,128]{1,0:T(8,128)S(1)}, u32[]{:S(2)}, u32[]{:S(2)}) %collective-permute-start.10) | collective-permute-done | bytes 8224 | tf_op jit(solution)/shard_map/ppermute | solution.py:165
  27.6 0.3 collective-permute-done.11.refs_3_
  27.9 0.2 collective-permute-done.9.refs_1_
  28.0 0.8 %shard_map.71 = (f32[16,256]{1,0:T(8,128)}, f32[16,256]{1,0:T(8,128)}, f32[16,256]{1,0:T(8,128)}) custom-call(f32[16,256]{1,0:T(8,128)S(1)} %get-tuple-element.11.image_ref, f32[16,256]{1,0:T(8,128)S(1)} %copy-done, f32[16,128]{1,0:T(8,128)S(1)} %get-tuple-element.12.refs_0_, f32[16,128]{1,0:T(8,128)S(1)} %collective-permute-done.9.refs_1_, ...), custom_call_target="tpu_custom_call" | custom-call | tf_op jit(solution)/shard_map/pallas_call | solution.py:225
  (1 shorter events, 0.0 us)
Async XLA Ops:
  0.6 1.5 %copy-start = (f32[16,256]{1,0:T(8,128)S(1)}, f32[16,256]{1,0:T(8,128)}, u32[]{:S(2)}) copy-start(f32[16,256]{1,0:T(8,128)} %probes_ref.3) | copy-start | bytes 49156
  1.6 6.8 %collective-permute-start = (bf16[128,256]{1,0:T(8,128)(2,1)S(1)}, bf16[128,256]{1,0:T(8,128)(2,1)S(1)}, u32[]{:S(2)}, u32[]{:S(2)}) collective-permute-start(bf16[128,256]{1,0:T(8,128)(2,1)S(1)} %divide_convert_fusion.scaled_ref.refs_0_), channel_id=1, source_target_pairs={{1,0},{0,1},{3,2},{2,3},{5,4},{4,5},{7,6},{6,7},{9,8},{8,9},{11,10... | collective-permute-start | bytes 196616 | tf_op jit(solution)/shard_map/ppermute | solution.py:150
  2.1 11.0 %copy-start.1 = (f32[256]{0:T(256)S(1)}, f32[256]{0:T(256)}, u32[]{:S(2)}) copy-start(f32[256]{0:T(256)} %param.6) | copy-start | bytes 3076
  2.1 9.5 %collective-permute-start.3 = (bf16[144,256]{1,0:T(8,128)(2,1)S(1)}, bf16[144,256]{1,0:T(8,128)(2,1)S(1)}, u32[]{:S(2)}, u32[]{:S(2)}) collective-permute-start(bf16[144,256]{1,0:T(8,128)(2,1)S(1)} %shard_map.67.refs_4_), channel_id=1, source_target_pairs={{13,0},{12,1},{9,4},{8,5},{5,8},{4,9},{1,12},{0,13},{15,2},{14,3},... | collective-permute-start | bytes 221192 | tf_op jit(solution)/shard_map/ppermute | solution.py:165
  6.9 6.2 %collective-permute-start.4 = (bf16[144,256]{1,0:T(8,128)(2,1)S(1)}, bf16[144,256]{1,0:T(8,128)(2,1)S(1)}, u32[]{:S(2)}, u32[]{:S(2)}) collective-permute-start(bf16[144,256]{1,0:T(8,128)(2,1)S(1)} %shard_map.67.refs_4_), channel_id=1, source_target_pairs={{9,0},{8,1},{13,4},{12,5},{1,8},{0,9},{5,12},{4,13},{11,2},{10,3},... | collective-permute-start | bytes 221192 | tf_op jit(solution)/shard_map/ppermute | solution.py:165
  6.9 4.7 %collective-permute-start.1 = (bf16[128,256]{1,0:T(8,128)(2,1)S(1)}, bf16[128,256]{1,0:T(8,128)(2,1)S(1)}, u32[]{:S(2)}, u32[]{:S(2)}) collective-permute-start(bf16[128,256]{1,0:T(8,128)(2,1)S(1)} %divide_convert_fusion.scaled_ref.refs_0_), channel_id=1, source_target_pairs={{2,0},{0,2},{3,1},{1,3},{6,4},{4,6},{7,5},{5,7},{10,8},{8,10},{11,... | collective-permute-start | bytes 196616 | tf_op jit(solution)/shard_map/ppermute | solution.py:150
  8.4 4.7 %collective-permute-start.2 = (bf16[128,256]{1,0:T(8,128)(2,1)S(1)}, bf16[128,256]{1,0:T(8,128)(2,1)S(1)}, u32[]{:S(2)}, u32[]{:S(2)}) collective-permute-start(bf16[128,256]{1,0:T(8,128)(2,1)S(1)} %collective-permute-done.refs_1_), channel_id=1, source_target_pairs={{2,0},{0,2},{3,1},{1,3},{6,4},{4,6},{7,5},{5,7},{10,8},{8,10},{11,... | collective-permute-start | bytes 196616 | tf_op jit(solution)/shard_map/ppermute | solution.py:150
  8.9 5.7 %collective-permute-start.5 = (bf16[144,256]{1,0:T(8,128)(2,1)S(1)}, bf16[144,256]{1,0:T(8,128)(2,1)S(1)}, u32[]{:S(2)}, u32[]{:S(2)}) collective-permute-start(bf16[144,256]{1,0:T(8,128)(2,1)S(1)} %shard_map.67.refs_4_), channel_id=1, source_target_pairs={{5,0},{4,1},{1,4},{0,5},{13,8},{12,9},{9,12},{8,13},{7,2},{6,3},{3... | collective-permute-start | bytes 221192 | tf_op jit(solution)/shard_map/ppermute | solution.py:165
  16.4 4.4 %collective-permute-start.6 = (f32[5,16,256]{2,1,0:T(8,128)S(1)}, f32[5,16,256]{2,1,0:T(8,128)S(1)}, u32[]{:S(2)}, u32[]{:S(2)}) collective-permute-start(f32[5,16,256]{2,1,0:T(8,128)S(1)} %shard_map.69.refs_0_), channel_id=1, source_target_pairs={{2,0},{3,1},{0,2},{1,3},{6,4},{7,5},{4,6},{5,7},{10,8},{11,9},{8,1... | collective-permute-start | bytes 245768 | tf_op jit(solution)/shard_map/ppermute | solution.py:150
  17.9 4.7 %collective-permute-start.7 = (f32[5,16,256]{2,1,0:T(8,128)S(1)}, f32[5,16,256]{2,1,0:T(8,128)S(1)}, u32[]{:S(2)}, u32[]{:S(2)}) collective-permute-start(f32[5,16,256]{2,1,0:T(8,128)S(1)} %shard_map.69.refs_0_), channel_id=1, source_target_pairs={{3,0},{2,1},{1,2},{0,3},{7,4},{6,5},{5,6},{4,7},{11,8},{10,9},{9,1... | collective-permute-start | bytes 245768 | tf_op jit(solution)/shard_map/ppermute | solution.py:150
  17.9 4.7 %collective-permute-start.8 = (f32[5,16,256]{2,1,0:T(8,128)S(1)}, f32[5,16,256]{2,1,0:T(8,128)S(1)}, u32[]{:S(2)}, u32[]{:S(2)}) collective-permute-start(f32[5,16,256]{2,1,0:T(8,128)S(1)} %shard_map.69.refs_0_), channel_id=1, source_target_pairs={{1,0},{0,1},{3,2},{2,3},{5,4},{4,5},{7,6},{6,7},{9,8},{8,9},{11,10... | collective-permute-start | bytes 245768 | tf_op jit(solution)/shard_map/ppermute | solution.py:150
  22.7 4.9 %collective-permute-start.10 = (f32[16,128]{1,0:T(8,128)S(1)}, f32[16,128]{1,0:T(8,128)S(1)}, u32[]{:S(2)}, u32[]{:S(2)}) collective-permute-start(f32[16,128]{1,0:T(8,128)S(1)} %get-tuple-element.12.refs_0_), channel_id=1, source_target_pairs={{13,0},{12,1},{9,4},{8,5},{5,8},{4,9},{1,12},{0,13},{15,2},{14,3},... | collective-permute-start | bytes 24584 | tf_op jit(solution)/shard_map/ppermute | solution.py:165
  23.9 4.0 %collective-permute-start.11 = (f32[16,128]{1,0:T(8,128)S(1)}, f32[16,128]{1,0:T(8,128)S(1)}, u32[]{:S(2)}, u32[]{:S(2)}) collective-permute-start(f32[16,128]{1,0:T(8,128)S(1)} %get-tuple-element.12.refs_0_), channel_id=1, source_target_pairs={{9,0},{8,1},{13,4},{12,5},{1,8},{0,9},{5,12},{4,13},{11,2},{10,3},... | collective-permute-start | bytes 24584 | tf_op jit(solution)/shard_map/ppermute | solution.py:165
  23.9 4.2 %collective-permute-start.9 = (f32[16,128]{1,0:T(8,128)S(1)}, f32[16,128]{1,0:T(8,128)S(1)}, u32[]{:S(2)}, u32[]{:S(2)}) collective-permute-start(f32[16,128]{1,0:T(8,128)S(1)} %get-tuple-element.12.refs_0_), channel_id=1, source_target_pairs={{5,0},{4,1},{1,4},{0,5},{13,8},{12,9},{9,12},{8,13},{7,2},{6,3},{3... | collective-permute-start | bytes 24584 | tf_op jit(solution)/shard_map/ppermute | solution.py:165

commit v18 on v17

--- a/solution.py
+++ b/solution.py
@@ -168,11 +168,19 @@
 
 def plane_blocks(value, shape):
     grp_count, sub_count = shape
-    if sub_count != 2 or not paired(grp_count):
+    if sub_count != 2 or not paired(grp_count) or grp_count > DIRECT:
         return everywhere(value, PLANE, grp_count * sub_count)
-    blocks = everywhere(value, ("sub",), sub_count)
-    moved = [everywhere(block, ("grp",), grp_count) for block in blocks]
-    return [moved[sub][grp] for grp in range(grp_count) for sub in range(sub_count)]
+    own, other = everywhere(value, ("sub",), sub_count)
+    blocks = [own, other]
+    for step in range(1, grp_count):
+        pairs = [
+            (2 * (place ^ step) + 1 - core, 2 * place + core)
+            for place in range(grp_count)
+            for core in range(2)
+        ]
+        crossed = [lax.ppermute(block, PLANE, pairs) for block in (own, other)]
+        blocks += [crossed[1], crossed[0]]
+    return blocks
 
 
 def make_local(plane_shape, line_count):

time: 29 us -> 29.3 us (1.010)
  waiting for transfers between devices: 11 us -> 11.3 us
    ppermute x6 -> x4, waiting for transfers between devices: 6.72 us -> 4.11 us  [everywhere(): lax.ppermute(value, axes, [(source_of(i, step, count), i) for i in range(...]
    ppermute x0 -> x2, waiting for transfers between devices: none -> 2.16 us  [plane_blocks(): crossed = [lax.ppermute(block, PLANE, pairs) for block in (own, other)]]
    ppermute x6 -> x4, starting transfers between devices: 4.69 us -> 2.66 us  [everywhere(): lax.ppermute(value, axes, [(source_of(i, step, count), i) for i in range(...]
    ppermute x0 -> x2, starting transfers between devices: none -> 1.75 us  [plane_blocks(): crossed = [lax.ppermute(block, PLANE, pairs) for block in (own, other)]]
    ppermute x6, waiting for transfers between devices: 4.33 us -> 5.05 us  [along_line(): blocks.append(lax.ppermute(value, LINE + ('sub',), pairs))]
  transfers between devices with their start and end apart: 12 -> 12, of which waited for: 8 -> 7; matrix products, arithmetic and copies ran while one was open for 0% -> 0% of each run, Pallas kernels for 1% -> 1%
where the time goes in v18:
time: 29.3 us; the launch traced here: 29.1 us
  starting transfers between devices  13.3 us (45%)
  waiting for transfers between devices  11.3 us (39%)
  Pallas kernels  2.86 us (10%)
  other arithmetic  0.93 us (3%)
  between operations  0.68 us (2%)
    ppermute x6, starting transfers between devices, along_line(): blocks.append(lax.ppermute(value, LINE + ('sub',), pairs))  8.88 us
    ppermute x6, waiting for transfers between devices, along_line(): blocks.append(lax.ppermute(value, LINE + ('sub',), pairs))  5.05 us
    ppermute x4, waiting for transfers between devices, everywhere(): lax.ppermute(value, axes, [(source_of(i, step, count), i) for i in range(...  4.11 us
    ppermute x4, starting transfers between devices, everywhere(): lax.ppermute(value, axes, [(source_of(i, step, count), i) for i in range(...  2.66 us
    ppermute x2, waiting for transfers between devices, plane_blocks(): crossed = [lax.ppermute(block, PLANE, pairs) for block in (own, other)]  2.16 us
    pallas_call x1, Pallas kernels, local(): pl.pallas_call(lambda *refs: image_kernel(feature_count, plane_count, *re...  1.77 us
    ppermute x2, starting transfers between devices, plane_blocks(): crossed = [lax.ppermute(block, PLANE, pairs) for block in (own, other)]  1.75 us
    convert_element_type x1, other arithmetic, local(): (features.astype(jnp.float32) / lengthscale[:, None]).astype(jnp.bfloat16)  0.93 us
  transfers between devices with their start and end apart: 12, of which 7 were waited for; matrix products, arithmetic and copies ran while one was open for 0% of the time, Pallas kernels for 1%

profile of v18, /device:TPU:0, one launch (start us, length us, event | category | flops | bytes accessed | tf_op | source)
XLA Modules:
  0.0 29.1 jit_solution(13195677033504497456)
XLA Ops:
  0.6 0.0 copy-start
  0.6 0.9 %divide_convert_fusion.scaled_ref.refs_0_ = bf16[128,256]{1,0:T(8,128)(2,1)S(1)} fusion(bf16[128,256]{1,0:T(8,128)(2,1)} %param.4, f32[128]{0:T(128)} %param.5), kind=kLoop, calls=%fused_computation | loop fusion | flops 98304 | bytes 131584 | tf_op jit(solution)/shard_map/convert_element_type | solution.py:192
  1.6 0.5 %collective-permute-start = (bf16[128,256]{1,0:T(8,128)(2,1)S(1)}, bf16[128,256]{1,0:T(8,128)(2,1)S(1)}, u32[]{:S(2)}, u32[]{:S(2)}) collective-permute-start(bf16[128,256]{1,0:T(8,128)(2,1)S(1)} %divide_convert_fusion.scaled_ref.refs_0_), channel_id=1, source_target_pairs={{1,0},{0,1},{3,2},{2,3},{5,4},{4,5},{7,6},{6,7},{9,8},{8,9},{11,10... | collective-permute-start | bytes 196616 | tf_op jit(solution)/shard_map/ppermute | solution.py:150
  2.1 0.0 copy-done
  2.1 0.0 copy-start.1
  2.1 4.8 %collective-permute-start.3 = (bf16[144,256]{1,0:T(8,128)(2,1)S(1)}, bf16[144,256]{1,0:T(8,128)(2,1)S(1)}, u32[]{:S(2)}, u32[]{:S(2)}) collective-permute-start(bf16[144,256]{1,0:T(8,128)(2,1)S(1)} %shard_map.67.refs_4_), channel_id=1, source_target_pairs={{13,0},{12,1},{9,4},{8,5},{5,8},{4,9},{1,12},{0,13},{15,2},{14,3},... | collective-permute-start | bytes 221192 | tf_op jit(solution)/shard_map/ppermute | solution.py:165
  6.9 0.0 collective-permute-start.4
  6.9 1.1 %collective-permute-start.2 = (bf16[128,256]{1,0:T(8,128)(2,1)S(1)}, bf16[128,256]{1,0:T(8,128)(2,1)S(1)}, u32[]{:S(2)}, u32[]{:S(2)}) collective-permute-start(bf16[128,256]{1,0:T(8,128)(2,1)S(1)} %divide_convert_fusion.scaled_ref.refs_0_), channel_id=1, source_target_pairs={{3,0},{2,1},{1,2},{0,3},{7,4},{6,5},{5,6},{4,7},{11,8},{10,9},{9,1... | collective-permute-start | bytes 196616 | tf_op jit(solution)/shard_map/ppermute | solution.py:181
  8.0 0.0 collective-permute-done.refs_1_
  8.0 0.6 %collective-permute-start.1 = (bf16[128,256]{1,0:T(8,128)(2,1)S(1)}, bf16[128,256]{1,0:T(8,128)(2,1)S(1)}, u32[]{:S(2)}, u32[]{:S(2)}) collective-permute-start(bf16[128,256]{1,0:T(8,128)(2,1)S(1)} %collective-permute-done.refs_1_), channel_id=1, source_target_pairs={{3,0},{2,1},{1,2},{0,3},{7,4},{6,5},{5,6},{4,7},{11,8},{10,9},{9,1... | collective-permute-start | bytes 196616 | tf_op jit(solution)/shard_map/ppermute | solution.py:181
  8.7 0.3 collective-permute-start.5
  8.9 2.2 %collective-permute-done.2.refs_3_ = bf16[128,256]{1,0:T(8,128)(2,1)S(1)} collective-permute-done((bf16[128,256]{1,0:T(8,128)(2,1)S(1)}, bf16[128,256]{1,0:T(8,128)(2,1)S(1)}, u32[]{:S(2)}, u32[]{:S(2)}) %collective-permute-start.2) | collective-permute-done | bytes 65568 | tf_op jit(solution)/shard_map/ppermute | solution.py:181
  11.1 0.0 collective-permute-done.3.refs_5_
  11.1 2.0 %collective-permute-done.4.refs_6_ = bf16[144,256]{1,0:T(8,128)(2,1)S(1)} collective-permute-done((bf16[144,256]{1,0:T(8,128)(2,1)S(1)}, bf16[144,256]{1,0:T(8,128)(2,1)S(1)}, u32[]{:S(2)}, u32[]{:S(2)}) %collective-permute-start.4) | collective-permute-done | bytes 73760 | tf_op jit(solution)/shard_map/ppermute | solution.py:165
  13.1 0.0 collective-permute-done.1.refs_2_
  13.1 0.0 copy-done.1
  13.1 0.2 shard_map.68
  13.3 1.3 %collective-permute-done.5.refs_7_ = bf16[144,256]{1,0:T(8,128)(2,1)S(1)} collective-permute-done((bf16[144,256]{1,0:T(8,128)(2,1)S(1)}, bf16[144,256]{1,0:T(8,128)(2,1)S(1)}, u32[]{:S(2)}, u32[]{:S(2)}) %collective-permute-start.5) | collective-permute-done | bytes 73760 | tf_op jit(solution)/shard_map/ppermute | solution.py:165
  14.6 1.8 %shard_map.69.refs_0_ = f32[5,16,256]{2,1,0:T(8,128)S(1)} custom-call(bf16[4,144,256]{2,1,0:T(8,128)(2,1)S(1)} %get-tuple-element.8.refs_0_, f32[16,256]{1,0:T(8,128)S(1)} %get-tuple-element.9.refs_1_, f32[16,256]{1,0:T(8,128)S(1)} %copy-done, bf16[3,256,144]{2,1,0:T(8,128)(2,1)S(1)} %get-tuple-element.10.refs_3_, bf16[144,256]{1,0:T(8,128)(2,1)S(1)} %shard_map.67.refs_4_, ...), custom_call_target="tpu_custom_call" | custom-call | tf_op jit(solution)/shard_map/pallas_call | solution.py:218
  16.3 1.5 %collective-permute-start.6 = (f32[5,16,256]{2,1,0:T(8,128)S(1)}, f32[5,16,256]{2,1,0:T(8,128)S(1)}, u32[]{:S(2)}, u32[]{:S(2)}) collective-permute-start(f32[5,16,256]{2,1,0:T(8,128)S(1)} %shard_map.69.refs_0_), channel_id=1, source_target_pairs={{2,0},{3,1},{0,2},{1,3},{6,4},{7,5},{4,6},{5,7},{10,8},{11,9},{8,1... | collective-permute-start | bytes 245768 | tf_op jit(solution)/shard_map/ppermute | solution.py:150
  17.9 0.0 collective-permute-start.7
  17.9 0.6 %collective-permute-start.8 = (f32[5,16,256]{2,1,0:T(8,128)S(1)}, f32[5,16,256]{2,1,0:T(8,128)S(1)}, u32[]{:S(2)}, u32[]{:S(2)}) collective-permute-start(f32[5,16,256]{2,1,0:T(8,128)S(1)} %shard_map.69.refs_0_), channel_id=1, source_target_pairs={{1,0},{0,1},{3,2},{2,3},{5,4},{4,5},{7,6},{6,7},{9,8},{8,9},{11,10... | collective-permute-start | bytes 245768 | tf_op jit(solution)/shard_map/ppermute | solution.py:150
  18.5 2.3 %collective-permute-done.6.refs_1_ = f32[5,16,256]{2,1,0:T(8,128)S(1)} collective-permute-done((f32[5,16,256]{2,1,0:T(8,128)S(1)}, f32[5,16,256]{2,1,0:T(8,128)S(1)}, u32[]{:S(2)}, u32[]{:S(2)}) %collective-permute-start.6) | collective-permute-done | bytes 81952 | tf_op jit(solution)/shard_map/ppermute | solution.py:150
  20.8 1.8 %collective-permute-done.7.refs_2_ = f32[5,16,256]{2,1,0:T(8,128)S(1)} collective-permute-done((f32[5,16,256]{2,1,0:T(8,128)S(1)}, f32[5,16,256]{2,1,0:T(8,128)S(1)}, u32[]{:S(2)}, u32[]{:S(2)}) %collective-permute-start.7) | collective-permute-done | bytes 81952 | tf_op jit(solution)/shard_map/ppermute | solution.py:150
  22.6 0.0 collective-permute-done.8.refs_3_
  22.6 0.1 shard_map.70
  22.7 1.6 %collective-permute-start.10 = (f32[16,128]{1,0:T(8,128)S(1)}, f32[16,128]{1,0:T(8,128)S(1)}, u32[]{:S(2)}, u32[]{:S(2)}) collective-permute-start(f32[16,128]{1,0:T(8,128)S(1)} %get-tuple-element.12.refs_0_), channel_id=1, source_target_pairs={{13,0},{12,1},{9,4},{8,5},{5,8},{4,9},{1,12},{0,13},{15,2},{14,3},... | collective-permute-start | bytes 24584 | tf_op jit(solution)/shard_map/ppermute | solution.py:165
  24.3 0.0 collective-permute-start.11
  24.3 2.2 %collective-permute-start.9 = (f32[16,128]{1,0:T(8,128)S(1)}, f32[16,128]{1,0:T(8,128)S(1)}, u32[]{:S(2)}, u32[]{:S(2)}) collective-permute-start(f32[16,128]{1,0:T(8,128)S(1)} %get-tuple-element.12.refs_0_), channel_id=1, source_target_pairs={{5,0},{4,1},{1,4},{0,5},{13,8},{12,9},{9,12},{8,13},{7,2},{6,3},{3... | collective-permute-start | bytes 24584 | tf_op jit(solution)/shard_map/ppermute | solution.py:165
  26.5 1.1 %collective-permute-done.10.refs_2_ = f32[16,128]{1,0:T(8,128)S(1)} collective-permute-done((f32[16,128]{1,0:T(8,128)S(1)}, f32[16,128]{1,0:T(8,128)S(1)}, u32[]{:S(2)}, u32[]{:S(2)}) %collective-permute-start.10) | collective-permute-done | bytes 8224 | tf_op jit(solution)/shard_map/ppermute | solution.py:165
  27.6 0.7 %collective-permute-done.11.refs_3_ = f32[16,128]{1,0:T(8,128)S(1)} collective-permute-done((f32[16,128]{1,0:T(8,128)S(1)}, f32[16,128]{1,0:T(8,128)S(1)}, u32[]{:S(2)}, u32[]{:S(2)}) %collective-permute-start.11) | collective-permute-done | bytes 8224 | tf_op jit(solution)/shard_map/ppermute | solution.py:165
  28.3 0.0 collective-permute-done.9.refs_1_
  28.3 0.8 %shard_map.71 = (f32[16,256]{1,0:T(8,128)}, f32[16,256]{1,0:T(8,128)}, f32[16,256]{1,0:T(8,128)}) custom-call(f32[16,256]{1,0:T(8,128)S(1)} %get-tuple-element.11.image_ref, f32[16,256]{1,0:T(8,128)S(1)} %copy-done, f32[16,128]{1,0:T(8,128)S(1)} %get-tuple-element.12.refs_0_, f32[16,128]{1,0:T(8,128)S(1)} %collective-permute-done.9.refs_1_, ...), custom_call_target="tpu_custom_call" | custom-call | tf_op jit(solution)/shard_map/pallas_call | solution.py:233
  (1 shorter events, 0.0 us)
Async XLA Ops:
  0.6 1.5 %copy-start = (f32[16,256]{1,0:T(8,128)S(1)}, f32[16,256]{1,0:T(8,128)}, u32[]{:S(2)}) copy-start(f32[16,256]{1,0:T(8,128)} %probes_ref.3) | copy-start | bytes 49156
  1.6 6.5 %collective-permute-start = (bf16[128,256]{1,0:T(8,128)(2,1)S(1)}, bf16[128,256]{1,0:T(8,128)(2,1)S(1)}, u32[]{:S(2)}, u32[]{:S(2)}) collective-permute-start(bf16[128,256]{1,0:T(8,128)(2,1)S(1)} %divide_convert_fusion.scaled_ref.refs_0_), channel_id=1, source_target_pairs={{1,0},{0,1},{3,2},{2,3},{5,4},{4,5},{7,6},{6,7},{9,8},{8,9},{11,10... | collective-permute-start | bytes 196616 | tf_op jit(solution)/shard_map/ppermute | solution.py:150
  2.1 11.0 %copy-start.1 = (f32[256]{0:T(256)S(1)}, f32[256]{0:T(256)}, u32[]{:S(2)}) copy-start(f32[256]{0:T(256)} %param.6) | copy-start | bytes 3076
  2.1 9.0 %collective-permute-start.3 = (bf16[144,256]{1,0:T(8,128)(2,1)S(1)}, bf16[144,256]{1,0:T(8,128)(2,1)S(1)}, u32[]{:S(2)}, u32[]{:S(2)}) collective-permute-start(bf16[144,256]{1,0:T(8,128)(2,1)S(1)} %shard_map.67.refs_4_), channel_id=1, source_target_pairs={{13,0},{12,1},{9,4},{8,5},{5,8},{4,9},{1,12},{0,13},{15,2},{14,3},... | collective-permute-start | bytes 221192 | tf_op jit(solution)/shard_map/ppermute | solution.py:165
  6.9 6.2 %collective-permute-start.4 = (bf16[144,256]{1,0:T(8,128)(2,1)S(1)}, bf16[144,256]{1,0:T(8,128)(2,1)S(1)}, u32[]{:S(2)}, u32[]{:S(2)}) collective-permute-start(bf16[144,256]{1,0:T(8,128)(2,1)S(1)} %shard_map.67.refs_4_), channel_id=1, source_target_pairs={{9,0},{8,1},{13,4},{12,5},{1,8},{0,9},{5,12},{4,13},{11,2},{10,3},... | collective-permute-start | bytes 221192 | tf_op jit(solution)/shard_map/ppermute | solution.py:165
  6.9 4.2 %collective-permute-start.2 = (bf16[128,256]{1,0:T(8,128)(2,1)S(1)}, bf16[128,256]{1,0:T(8,128)(2,1)S(1)}, u32[]{:S(2)}, u32[]{:S(2)}) collective-permute-start(bf16[128,256]{1,0:T(8,128)(2,1)S(1)} %divide_convert_fusion.scaled_ref.refs_0_), channel_id=1, source_target_pairs={{3,0},{2,1},{1,2},{0,3},{7,4},{6,5},{5,6},{4,7},{11,8},{10,9},{9,1... | collective-permute-start | bytes 196616 | tf_op jit(solution)/shard_map/ppermute | solution.py:181
  8.0 5.1 %collective-permute-start.1 = (bf16[128,256]{1,0:T(8,128)(2,1)S(1)}, bf16[128,256]{1,0:T(8,128)(2,1)S(1)}, u32[]{:S(2)}, u32[]{:S(2)}) collective-permute-start(bf16[128,256]{1,0:T(8,128)(2,1)S(1)} %collective-permute-done.refs_1_), channel_id=1, source_target_pairs={{3,0},{2,1},{1,2},{0,3},{7,4},{6,5},{5,6},{4,7},{11,8},{10,9},{9,1... | collective-permute-start | bytes 196616 | tf_op jit(solution)/shard_map/ppermute | solution.py:181
  8.7 5.9 %collective-permute-start.5 = (bf16[144,256]{1,0:T(8,128)(2,1)S(1)}, bf16[144,256]{1,0:T(8,128)(2,1)S(1)}, u32[]{:S(2)}, u32[]{:S(2)}) collective-permute-start(bf16[144,256]{1,0:T(8,128)(2,1)S(1)} %shard_map.67.refs_4_), channel_id=1, source_target_pairs={{5,0},{4,1},{1,4},{0,5},{13,8},{12,9},{9,12},{8,13},{7,2},{6,3},{3... | collective-permute-start | bytes 221192 | tf_op jit(solution)/shard_map/ppermute | solution.py:165
  16.3 4.5 %collective-permute-start.6 = (f32[5,16,256]{2,1,0:T(8,128)S(1)}, f32[5,16,256]{2,1,0:T(8,128)S(1)}, u32[]{:S(2)}, u32[]{:S(2)}) collective-permute-start(f32[5,16,256]{2,1,0:T(8,128)S(1)} %shard_map.69.refs_0_), channel_id=1, source_target_pairs={{2,0},{3,1},{0,2},{1,3},{6,4},{7,5},{4,6},{5,7},{10,8},{11,9},{8,1... | collective-permute-start | bytes 245768 | tf_op jit(solution)/shard_map/ppermute | solution.py:150
  17.9 4.7 %collective-permute-start.7 = (f32[5,16,256]{2,1,0:T(8,128)S(1)}, f32[5,16,256]{2,1,0:T(8,128)S(1)}, u32[]{:S(2)}, u32[]{:S(2)}) collective-permute-start(f32[5,16,256]{2,1,0:T(8,128)S(1)} %shard_map.69.refs_0_), channel_id=1, source_target_pairs={{3,0},{2,1},{1,2},{0,3},{7,4},{6,5},{5,6},{4,7},{11,8},{10,9},{9,1... | collective-permute-start | bytes 245768 | tf_op jit(solution)/shard_map/ppermute | solution.py:150
  17.9 4.7 %collective-permute-start.8 = (f32[5,16,256]{2,1,0:T(8,128)S(1)}, f32[5,16,256]{2,1,0:T(8,128)S(1)}, u32[]{:S(2)}, u32[]{:S(2)}) collective-permute-start(f32[5,16,256]{2,1,0:T(8,128)S(1)} %shard_map.69.refs_0_), channel_id=1, source_target_pairs={{1,0},{0,1},{3,2},{2,3},{5,4},{4,5},{7,6},{6,7},{9,8},{8,9},{11,10... | collective-permute-start | bytes 245768 | tf_op jit(solution)/shard_map/ppermute | solution.py:150
  22.7 4.9 %collective-permute-start.10 = (f32[16,128]{1,0:T(8,128)S(1)}, f32[16,128]{1,0:T(8,128)S(1)}, u32[]{:S(2)}, u32[]{:S(2)}) collective-permute-start(f32[16,128]{1,0:T(8,128)S(1)} %get-tuple-element.12.refs_0_), channel_id=1, source_target_pairs={{13,0},{12,1},{9,4},{8,5},{5,8},{4,9},{1,12},{0,13},{15,2},{14,3},... | collective-permute-start | bytes 24584 | tf_op jit(solution)/shard_map/ppermute | solution.py:165
  24.3 4.0 %collective-permute-start.11 = (f32[16,128]{1,0:T(8,128)S(1)}, f32[16,128]{1,0:T(8,128)S(1)}, u32[]{:S(2)}, u32[]{:S(2)}) collective-permute-start(f32[16,128]{1,0:T(8,128)S(1)} %get-tuple-element.12.refs_0_), channel_id=1, source_target_pairs={{9,0},{8,1},{13,4},{12,5},{1,8},{0,9},{5,12},{4,13},{11,2},{10,3},... | collective-permute-start | bytes 24584 | tf_op jit(solution)/shard_map/ppermute | solution.py:165
  24.3 4.0 %collective-permute-start.9 = (f32[16,128]{1,0:T(8,128)S(1)}, f32[16,128]{1,0:T(8,128)S(1)}, u32[]{:S(2)}, u32[]{:S(2)}) collective-permute-start(f32[16,128]{1,0:T(8,128)S(1)} %get-tuple-element.12.refs_0_), channel_id=1, source_target_pairs={{5,0},{4,1},{1,4},{0,5},{13,8},{12,9},{9,12},{8,13},{7,2},{6,3},{3... | collective-permute-start | bytes 24584 | tf_op jit(solution)/shard_map/ppermute | solution.py:165

commit v19 on v17

--- a/solution.py
+++ b/solution.py
@@ -9,8 +9,8 @@
 LINE = ("blk",)
 DIRECT = 8
 VMEM = pltpu.CompilerParams(vmem_limit_bytes=40 * 1024 * 1024)
-PARTIALS, PARTIALS_BACK = (0, 2, 3, 1), (0, 3, 1, 2)
-SUMS = (0, 1, 3, 2)
+PARTIALS, PARTIALS_BACK = (0, 1, 3, 2), (0, 1, 3, 2)
+SUMS = (0, 1, 2, 3)
 HALF = 8
 
 
@@ -33,16 +33,22 @@
     return rows.astype(jnp.bfloat16)
 
 
-def pack_kernel(scaled_ref, probes_ref, line_ref):
-    line_ref[...] = jnp.concatenate(
-        [scaled_ref[...], probes_ref[...].astype(jnp.bfloat16)], axis=0
-    )
+def pack_kernel(scaled_ref, probes_ref, line_ref, plane_ref):
+    high, low, _ = pieces_of(probes_ref[...])
+    high, low = high.astype(jnp.bfloat16), low.astype(jnp.bfloat16)
+    line_ref[...] = jnp.concatenate([scaled_ref[...], high], axis=0)
+    plane_ref[...] = jnp.concatenate([scaled_ref[...], high, low], axis=0)
 
 
 def columns_of(block, feature_count):
     scaled = block[:feature_count, :]
     columns = jnp.concatenate([scaled, norm_rows(scaled, 0)], axis=0)
     return columns.astype(jnp.float32).T.astype(jnp.bfloat16)
+
+
+def rows_of(ref, feature_count):
+    scaled = ref[:feature_count, :]
+    return jnp.concatenate([scaled, norm_rows(scaled, 1)], axis=0)
 
 
 def prepare_kernel(feature_count, plane_count, *refs):
@@ -50,22 +56,25 @@
     noise_ref, probes_ref, rows_ref, columns_ref, start_ref = refs[-5:]
     start_ref[...] = noise_ref[...] * probes_ref[...]
     for number, ref in enumerate(plane_refs):
-        rows_ref[number] = jnp.concatenate([ref[...], norm_rows(ref[...], 1)], axis=0)
+        rows_ref[number] = rows_of(ref, feature_count)
     for number, ref in enumerate(line_refs):
         columns_ref[number] = columns_of(ref[...], feature_count)
 
 
 def image_kernel(feature_count, plane_count, *refs):
-    rows_ref, start_ref, probes_ref = refs[:3]
-    columns_ref, *line_refs = refs[3:-1]
+    rows_ref, start_ref = refs[:2]
+    plane_refs = refs[2:plane_count]
+    columns_ref, *line_refs = refs[plane_count:-1]
     partial_ref = refs[-1]
+    rows = [rows_ref[number] for number in range(2)]
+    rows += [rows_of(ref, feature_count) for ref in plane_refs]
     totals = [start_ref[...]]
-    totals += [jnp.zeros(probes_ref.shape, jnp.float32)] * (plane_count - 1)
+    totals += [jnp.zeros(start_ref.shape, jnp.float32)] * (plane_count - 1)
 
     def add_columns(columns, probes, totals):
         result = []
-        for number, total in enumerate(totals):
-            exponent = jnp.dot(columns, rows_ref[number], preferred_element_type=jnp.float32)
+        for own, total in zip(rows, totals):
+            exponent = jnp.dot(columns, own, preferred_element_type=jnp.float32)
             weights = jnp.exp(exponent).astype(jnp.bfloat16)
             result.append(total + jnp.dot(probes, weights, preferred_element_type=jnp.float32))
         return result
@@ -87,21 +96,26 @@
         totals = lax.fori_loop(0, line_refs[0].shape[0], add_block, totals)
     for number, total in enumerate(totals):
         partial_ref[number] = total
-    partial_ref[plane_count] = probes_ref[...]
-
-
-def combine_kernel(plane_count, *refs):
-    partial_refs = in_order(refs[:-2], PARTIALS_BACK)
+
+
+def combine_kernel(feature_count, plane_count, *refs):
+    plane_refs, probes_ref = refs[:plane_count], refs[plane_count]
+    partial_refs = in_order(refs[plane_count + 1 : -2], PARTIALS_BACK)
     image_ref, sums_ref = refs[-2:]
+    probe_count = image_ref.shape[0]
     lane = lax.broadcasted_iota(jnp.int32, sums_ref.shape, 1)
     products = [0.0, 0.0, 0.0]
-    for number, own_ref in enumerate(partial_refs):
+    for number, plane_ref in enumerate(plane_refs):
         image = sum(
             ref[place_of(step, number, plane_count)] for step, ref in enumerate(partial_refs)
         )
         if number == 0:
             image_ref[...] = image
-        probes = own_ref[plane_count]
+            probes = probes_ref[...]
+        else:
+            middle = feature_count + probe_count
+            probes = plane_ref[feature_count:middle, :].astype(jnp.float32)
+            probes = probes + plane_ref[middle:, :].astype(jnp.float32)
         products[0] += probes * probes
         products[1] += probes * image
         products[2] += image * image
@@ -182,23 +196,26 @@
         feature_count, width = features.shape
         probe_count = probes.shape[0]
         scaled = (features.astype(jnp.float32) / lengthscale[:, None]).astype(jnp.bfloat16)
-        line = pl.pallas_call(
+        line, plane = pl.pallas_call(
             pack_kernel,
-            out_shape=jax.ShapeDtypeStruct((feature_count + probe_count, width), jnp.bfloat16),
+            out_shape=(
+                jax.ShapeDtypeStruct((feature_count + probe_count, width), jnp.bfloat16),
+                jax.ShapeDtypeStruct((feature_count + 2 * probe_count, width), jnp.bfloat16),
+            ),
             compiler_params=VMEM,
         )(scaled, probes)
         lines = along_line(line, line_count, plane_shape[1])
-        planes = plane_blocks(scaled, plane_shape)
+        planes = plane_blocks(plane, plane_shape)
         if len(lines) > 1:
-            early, late = lines[:1] + lines[:1:-1], lines[1]
+            early, late = lines[:1] + lines[2:], lines[1]
         else:
             early, late = [], lines[0]
         depth = feature_count + 2 * HALF
         work = plane_count * width * width
         rows, columns, start = pl.pallas_call(
-            lambda *refs: prepare_kernel(feature_count, plane_count, *refs),
+            lambda *refs: prepare_kernel(feature_count, 2, *refs),
             out_shape=(
-                jax.ShapeDtypeStruct((plane_count, depth, width), jnp.bfloat16),
+                jax.ShapeDtypeStruct((2, depth, width), jnp.bfloat16),
                 jax.ShapeDtypeStruct((max(len(early), 1), width, depth), jnp.bfloat16),
                 jax.ShapeDtypeStruct(probes.shape, jnp.float32),
             ),
@@ -206,21 +223,21 @@
             cost_estimate=pl.CostEstimate(
                 flops=6 * work * depth, bytes_accessed=4 * plane_count * width, transcendentals=3 * work
             ),
-        )(*planes, *early, noise_var[None, :], probes)
+        )(*planes[:2], *early, noise_var[None, :], probes)
         partial = pl.pallas_call(
             lambda *refs: image_kernel(feature_count, plane_count, *refs),
-            out_shape=jax.ShapeDtypeStruct((plane_count + 1, probe_count, width), jnp.float32),
-            compiler_params=VMEM,
-        )(rows, start, probes, columns, *early, late)
+            out_shape=jax.ShapeDtypeStruct((plane_count, probe_count, width), jnp.float32),
+            compiler_params=VMEM,
+        )(rows, start, *planes[2:], columns, *early, late)
         partials = everywhere(partial, PLANE, plane_count)
         image, sums = pl.pallas_call(
-            lambda *refs: combine_kernel(plane_count, *refs),
+            lambda *refs: combine_kernel(feature_count, plane_count, *refs),
             out_shape=(
                 jax.ShapeDtypeStruct(probes.shape, jnp.float32),
                 jax.ShapeDtypeStruct((probe_count, 128), jnp.float32),
             ),
             compiler_params=VMEM,
-        )(*in_order(partials, PARTIALS))
+        )(*planes, probes, *in_order(partials, PARTIALS))
         outs = (jax.ShapeDtypeStruct(probes.shape, jnp.float32),) * 3
         return pl.pallas_call(finish_kernel, out_shape=outs, compiler_params=VMEM)(
             image, probes, *in_order(along_line(sums, line_count, plane_shape[1]), SUMS)

time: 29 us -> 28.4 us (0.979)
  waiting for transfers between devices: 11 us -> 10.6 us
    ppermute x6, waiting for transfers between devices: 6.72 us -> 3.61 us  [everywhere(): lax.ppermute(value, axes, [(source_of(i, step, count), i) for i in range(...]
    ppermute x6, waiting for transfers between devices: 4.33 us -> 6.99 us  [along_line(): blocks.append(lax.ppermute(value, LINE + ('sub',), pairs))]
where the time goes in v19:
time: 28.4 us; the launch traced here: 28.2 us
  starting transfers between devices  13.1 us (46%)
  waiting for transfers between devices  10.6 us (37%)
  Pallas kernels  2.86 us (10%)
  other arithmetic  0.93 us (3%)
  between operations  0.68 us (2%)
    ppermute x6, starting transfers between devices, along_line(): blocks.append(lax.ppermute(value, LINE + ('sub',), pairs))  8.42 us
    ppermute x6, waiting for transfers between devices, along_line(): blocks.append(lax.ppermute(value, LINE + ('sub',), pairs))  6.99 us
    ppermute x6, starting transfers between devices, everywhere(): lax.ppermute(value, axes, [(source_of(i, step, count), i) for i in range(...  4.69 us
    ppermute x6, waiting for transfers between devices, everywhere(): lax.ppermute(value, axes, [(source_of(i, step, count), i) for i in range(...  3.61 us
    pallas_call x1, Pallas kernels, local(): pl.pallas_call(lambda *refs: image_kernel(feature_count, plane_count, *re...  1.77 us
    convert_element_type x1, other arithmetic, local(): (features.astype(jnp.float32) / lengthscale[:, None]).astype(jnp.bfloat16)  0.93 us
    pallas_call x1, Pallas kernels, local(): pl.pallas_call(finish_kernel, out_shape=outs, compiler_params=VMEM)  0.77 us
  transfers between devices with their start and end apart: 12, of which 8 were waited for; matrix products, arithmetic and copies ran while one was open for 0% of the time, Pallas kernels for 1%

profile of v19, /device:TPU:0, one launch (start us, length us, event | category | flops | bytes accessed | tf_op | source)
XLA Modules:
  0.0 28.2 jit_solution(10023214155057996085)
XLA Ops:
  0.6 0.0 copy-start
  0.6 0.9 %divide_convert_fusion.scaled_ref = bf16[128,256]{1,0:T(8,128)(2,1)S(1)} fusion(bf16[128,256]{1,0:T(8,128)(2,1)} %param.4, f32[128]{0:T(128)} %param.5), kind=kLoop, calls=%fused_computation | loop fusion | flops 98304 | bytes 131584 | tf_op jit(solution)/shard_map/convert_element_type | solution.py:198
  1.6 0.0 copy-done
  1.6 0.5 %collective-permute-start = (bf16[160,256]{1,0:T(8,128)(2,1)S(1)}, bf16[160,256]{1,0:T(8,128)(2,1)S(1)}, u32[]{:S(2)}, u32[]{:S(2)}) collective-permute-start(bf16[160,256]{1,0:T(8,128)(2,1)S(1)} %get-tuple-element.10.refs_0_), channel_id=1, source_target_pairs={{1,0},{0,1},{3,2},{2,3},{5,4},{4,5},{7,6},{6,7},{9,8},{8,9},{11,10... | collective-permute-start | bytes 245768 | tf_op jit(solution)/shard_map/ppermute | solution.py:164
  2.1 0.0 copy-start.1
  2.1 4.7 %collective-permute-start.4 = (bf16[144,256]{1,0:T(8,128)(2,1)S(1)}, bf16[144,256]{1,0:T(8,128)(2,1)S(1)}, u32[]{:S(2)}, u32[]{:S(2)}) collective-permute-start(bf16[144,256]{1,0:T(8,128)(2,1)S(1)} %get-tuple-element.11.refs_2_.refs_5_), channel_id=1, source_target_pairs={{13,0},{12,1},{9,4},{8,5},{5,8},{4,9},{1,12},{0,13},{15,2},{14,3},... | collective-permute-start | bytes 221192 | tf_op jit(solution)/shard_map/ppermute | solution.py:179
  6.9 0.0 collective-permute-start.3
  6.9 1.5 %collective-permute-start.1 = (bf16[160,256]{1,0:T(8,128)(2,1)S(1)}, bf16[160,256]{1,0:T(8,128)(2,1)S(1)}, u32[]{:S(2)}, u32[]{:S(2)}) collective-permute-start(bf16[160,256]{1,0:T(8,128)(2,1)S(1)} %get-tuple-element.10.refs_0_), channel_id=1, source_target_pairs={{2,0},{0,2},{3,1},{1,3},{6,4},{4,6},{7,5},{5,7},{10,8},{8,10},{11,... | collective-permute-start | bytes 245768 | tf_op jit(solution)/shard_map/ppermute | solution.py:164
  8.4 0.0 collective-permute-done.refs_1_
  8.4 0.5 %collective-permute-start.2 = (bf16[160,256]{1,0:T(8,128)(2,1)S(1)}, bf16[160,256]{1,0:T(8,128)(2,1)S(1)}, u32[]{:S(2)}, u32[]{:S(2)}) collective-permute-start(bf16[160,256]{1,0:T(8,128)(2,1)S(1)} %collective-permute-done.refs_1_), channel_id=1, source_target_pairs={{2,0},{0,2},{3,1},{1,3},{6,4},{4,6},{7,5},{5,7},{10,8},{8,10},{11,... | collective-permute-start | bytes 245768 | tf_op jit(solution)/shard_map/ppermute | solution.py:164
  8.9 0.0 collective-permute-start.5
  8.9 0.6 %collective-permute-done.4.refs_4_.refs_7_ = bf16[144,256]{1,0:T(8,128)(2,1)S(1)} collective-permute-done((bf16[144,256]{1,0:T(8,128)(2,1)S(1)}, bf16[144,256]{1,0:T(8,128)(2,1)S(1)}, u32[]{:S(2)}, u32[]{:S(2)}) %collective-permute-start.4) | collective-permute-done | bytes 73760 | tf_op jit(solution)/shard_map/ppermute | solution.py:179
  9.5 3.6 %collective-permute-done.3.refs_3_.refs_6_ = bf16[144,256]{1,0:T(8,128)(2,1)S(1)} collective-permute-done((bf16[144,256]{1,0:T(8,128)(2,1)S(1)}, bf16[144,256]{1,0:T(8,128)(2,1)S(1)}, u32[]{:S(2)}, u32[]{:S(2)}) %collective-permute-start.3) | collective-permute-done | bytes 73760 | tf_op jit(solution)/shard_map/ppermute | solution.py:179
  13.1 0.0 copy-done.1
  13.1 0.2 shard_map.68
  13.3 1.4 %collective-permute-done.5.refs_8_ = bf16[144,256]{1,0:T(8,128)(2,1)S(1)} collective-permute-done((bf16[144,256]{1,0:T(8,128)(2,1)S(1)}, bf16[144,256]{1,0:T(8,128)(2,1)S(1)}, u32[]{:S(2)}, u32[]{:S(2)}) %collective-permute-start.5) | collective-permute-done | bytes 73760 | tf_op jit(solution)/shard_map/ppermute | solution.py:179
  14.6 0.0 collective-permute-done.1.refs_2_
  14.7 0.0 collective-permute-done.2.refs_3_
  14.7 1.8 %shard_map.69.refs_5_ = f32[4,16,256]{2,1,0:T(8,128)S(1)} custom-call(bf16[2,144,256]{2,1,0:T(8,128)(2,1)S(1)} %get-tuple-element.12.refs_0_, f32[16,256]{1,0:T(8,128)S(1)} %get-tuple-element.13.refs_1_, bf16[160,256]{1,0:T(8,128)(2,1)S(1)} %collective-permute-done.1.refs_2_, bf16[160,256]{1,0:T(8,128)(2,1)S(1)} %collective-permute-done.2.refs_3_, ...), custom_call_target="tpu_custom_call" | custom-call | tf_op jit(solution)/shard_map/pallas_call | solution.py:227
  16.4 1.5 %collective-permute-start.8 = (f32[4,16,256]{2,1,0:T(8,128)S(1)}, f32[4,16,256]{2,1,0:T(8,128)S(1)}, u32[]{:S(2)}, u32[]{:S(2)}) collective-permute-start(f32[4,16,256]{2,1,0:T(8,128)S(1)} %shard_map.69.refs_5_), channel_id=1, source_target_pairs={{2,0},{3,1},{0,2},{1,3},{6,4},{7,5},{4,6},{5,7},{10,8},{11,9},{8,1... | collective-permute-start | bytes 196616 | tf_op jit(solution)/shard_map/ppermute | solution.py:164
  17.9 0.0 collective-permute-start.7
  17.9 0.6 %collective-permute-start.6 = (f32[4,16,256]{2,1,0:T(8,128)S(1)}, f32[4,16,256]{2,1,0:T(8,128)S(1)}, u32[]{:S(2)}, u32[]{:S(2)}) collective-permute-start(f32[4,16,256]{2,1,0:T(8,128)S(1)} %shard_map.69.refs_5_), channel_id=1, source_target_pairs={{1,0},{0,1},{3,2},{2,3},{5,4},{4,5},{7,6},{6,7},{9,8},{8,9},{11,10... | collective-permute-start | bytes 196616 | tf_op jit(solution)/shard_map/ppermute | solution.py:164
  18.6 2.1 %collective-permute-done.8.refs_8_ = f32[4,16,256]{2,1,0:T(8,128)S(1)} collective-permute-done((f32[4,16,256]{2,1,0:T(8,128)S(1)}, f32[4,16,256]{2,1,0:T(8,128)S(1)}, u32[]{:S(2)}, u32[]{:S(2)}) %collective-permute-start.8) | collective-permute-done | bytes 65568 | tf_op jit(solution)/shard_map/ppermute | solution.py:164
  20.7 1.5 %collective-permute-done.7.refs_7_ = f32[4,16,256]{2,1,0:T(8,128)S(1)} collective-permute-done((f32[4,16,256]{2,1,0:T(8,128)S(1)}, f32[4,16,256]{2,1,0:T(8,128)S(1)}, u32[]{:S(2)}, u32[]{:S(2)}) %collective-permute-start.7) | collective-permute-done | bytes 65568 | tf_op jit(solution)/shard_map/ppermute | solution.py:164
  22.2 0.0 collective-permute-done.6.refs_6_
  22.2 0.1 shard_map.70
  22.3 1.0 %collective-permute-start.11 = (f32[16,128]{1,0:T(8,128)S(1)}, f32[16,128]{1,0:T(8,128)S(1)}, u32[]{:S(2)}, u32[]{:S(2)}) collective-permute-start(f32[16,128]{1,0:T(8,128)S(1)} %get-tuple-element.16.refs_0_), channel_id=1, source_target_pairs={{13,0},{12,1},{9,4},{8,5},{5,8},{4,9},{1,12},{0,13},{15,2},{14,3},... | collective-permute-start | bytes 24584 | tf_op jit(solution)/shard_map/ppermute | solution.py:179
  23.3 0.3 %collective-permute-start.10 = (f32[16,128]{1,0:T(8,128)S(1)}, f32[16,128]{1,0:T(8,128)S(1)}, u32[]{:S(2)}, u32[]{:S(2)}) collective-permute-start(f32[16,128]{1,0:T(8,128)S(1)} %get-tuple-element.16.refs_0_), channel_id=1, source_target_pairs={{9,0},{8,1},{13,4},{12,5},{1,8},{0,9},{5,12},{4,13},{11,2},{10,3},... | collective-permute-start | bytes 24584 | tf_op jit(solution)/shard_map/ppermute | solution.py:179
  23.6 2.4 %collective-permute-start.9 = (f32[16,128]{1,0:T(8,128)S(1)}, f32[16,128]{1,0:T(8,128)S(1)}, u32[]{:S(2)}, u32[]{:S(2)}) collective-permute-start(f32[16,128]{1,0:T(8,128)S(1)} %get-tuple-element.16.refs_0_), channel_id=1, source_target_pairs={{5,0},{4,1},{1,4},{0,5},{13,8},{12,9},{9,12},{8,13},{7,2},{6,3},{3... | collective-permute-start | bytes 24584 | tf_op jit(solution)/shard_map/ppermute | solution.py:179
  26.0 1.2 %collective-permute-done.11.refs_3_ = f32[16,128]{1,0:T(8,128)S(1)} collective-permute-done((f32[16,128]{1,0:T(8,128)S(1)}, f32[16,128]{1,0:T(8,128)S(1)}, u32[]{:S(2)}, u32[]{:S(2)}) %collective-permute-start.11) | collective-permute-done | bytes 8224 | tf_op jit(solution)/shard_map/ppermute | solution.py:179
  27.2 0.1 collective-permute-done.10.refs_2_
  27.3 0.2 collective-permute-done.9.refs_1_
  27.4 0.8 %shard_map.71 = (f32[16,256]{1,0:T(8,128)}, f32[16,256]{1,0:T(8,128)}, f32[16,256]{1,0:T(8,128)}) custom-call(f32[16,256]{1,0:T(8,128)S(1)} %get-tuple-element.15.image_ref, f32[16,256]{1,0:T(8,128)S(1)} %copy-done, f32[16,128]{1,0:T(8,128)S(1)} %get-tuple-element.16.refs_0_, f32[16,128]{1,0:T(8,128)S(1)} %collective-permute-done.9.refs_1_, ...), custom_call_target="tpu_custom_call" | custom-call | tf_op jit(solution)/shard_map/pallas_call | solution.py:242
  (1 shorter events, 0.0 us)
Async XLA Ops:
  0.6 1.0 %copy-start = (f32[16,256]{1,0:T(8,128)S(1)}, f32[16,256]{1,0:T(8,128)}, u32[]{:S(2)}) copy-start(f32[16,256]{1,0:T(8,128)} %probes_ref.3) | copy-start | bytes 49156
  1.6 6.7 %collective-permute-start = (bf16[160,256]{1,0:T(8,128)(2,1)S(1)}, bf16[160,256]{1,0:T(8,128)(2,1)S(1)}, u32[]{:S(2)}, u32[]{:S(2)}) collective-permute-start(bf16[160,256]{1,0:T(8,128)(2,1)S(1)} %get-tuple-element.10.refs_0_), channel_id=1, source_target_pairs={{1,0},{0,1},{3,2},{2,3},{5,4},{4,5},{7,6},{6,7},{9,8},{8,9},{11,10... | collective-permute-start | bytes 245768 | tf_op jit(solution)/shard_map/ppermute | solution.py:164
  2.1 10.9 %copy-start.1 = (f32[256]{0:T(256)S(1)}, f32[256]{0:T(256)}, u32[]{:S(2)}) copy-start(f32[256]{0:T(256)} %param.6) | copy-start | bytes 3076
  2.1 7.4 %collective-permute-start.4 = (bf16[144,256]{1,0:T(8,128)(2,1)S(1)}, bf16[144,256]{1,0:T(8,128)(2,1)S(1)}, u32[]{:S(2)}, u32[]{:S(2)}) collective-permute-start(bf16[144,256]{1,0:T(8,128)(2,1)S(1)} %get-tuple-element.11.refs_2_.refs_5_), channel_id=1, source_target_pairs={{13,0},{12,1},{9,4},{8,5},{5,8},{4,9},{1,12},{0,13},{15,2},{14,3},... | collective-permute-start | bytes 221192 | tf_op jit(solution)/shard_map/ppermute | solution.py:179
  6.9 6.2 %collective-permute-start.3 = (bf16[144,256]{1,0:T(8,128)(2,1)S(1)}, bf16[144,256]{1,0:T(8,128)(2,1)S(1)}, u32[]{:S(2)}, u32[]{:S(2)}) collective-permute-start(bf16[144,256]{1,0:T(8,128)(2,1)S(1)} %get-tuple-element.11.refs_2_.refs_5_), channel_id=1, source_target_pairs={{9,0},{8,1},{13,4},{12,5},{1,8},{0,9},{5,12},{4,13},{11,2},{10,3},... | collective-permute-start | bytes 221192 | tf_op jit(solution)/shard_map/ppermute | solution.py:179
  6.9 7.8 %collective-permute-start.1 = (bf16[160,256]{1,0:T(8,128)(2,1)S(1)}, bf16[160,256]{1,0:T(8,128)(2,1)S(1)}, u32[]{:S(2)}, u32[]{:S(2)}) collective-permute-start(bf16[160,256]{1,0:T(8,128)(2,1)S(1)} %get-tuple-element.10.refs_0_), channel_id=1, source_target_pairs={{2,0},{0,2},{3,1},{1,3},{6,4},{4,6},{7,5},{5,7},{10,8},{8,10},{11,... | collective-permute-start | bytes 245768 | tf_op jit(solution)/shard_map/ppermute | solution.py:164
  8.4 6.3 %collective-permute-start.2 = (bf16[160,256]{1,0:T(8,128)(2,1)S(1)}, bf16[160,256]{1,0:T(8,128)(2,1)S(1)}, u32[]{:S(2)}, u32[]{:S(2)}) collective-permute-start(bf16[160,256]{1,0:T(8,128)(2,1)S(1)} %collective-permute-done.refs_1_), channel_id=1, source_target_pairs={{2,0},{0,2},{3,1},{1,3},{6,4},{4,6},{7,5},{5,7},{10,8},{8,10},{11,... | collective-permute-start | bytes 245768 | tf_op jit(solution)/shard_map/ppermute | solution.py:164
  8.9 5.8 %collective-permute-start.5 = (bf16[144,256]{1,0:T(8,128)(2,1)S(1)}, bf16[144,256]{1,0:T(8,128)(2,1)S(1)}, u32[]{:S(2)}, u32[]{:S(2)}) collective-permute-start(bf16[144,256]{1,0:T(8,128)(2,1)S(1)} %get-tuple-element.11.refs_2_.refs_5_), channel_id=1, source_target_pairs={{5,0},{4,1},{1,4},{0,5},{13,8},{12,9},{9,12},{8,13},{7,2},{6,3},{3... | collective-permute-start | bytes 221192 | tf_op jit(solution)/shard_map/ppermute | solution.py:179
  16.4 4.3 %collective-permute-start.8 = (f32[4,16,256]{2,1,0:T(8,128)S(1)}, f32[4,16,256]{2,1,0:T(8,128)S(1)}, u32[]{:S(2)}, u32[]{:S(2)}) collective-permute-start(f32[4,16,256]{2,1,0:T(8,128)S(1)} %shard_map.69.refs_5_), channel_id=1, source_target_pairs={{2,0},{3,1},{0,2},{1,3},{6,4},{7,5},{4,6},{5,7},{10,8},{11,9},{8,1... | collective-permute-start | bytes 196616 | tf_op jit(solution)/shard_map/ppermute | solution.py:164
  17.9 4.3 %collective-permute-start.7 = (f32[4,16,256]{2,1,0:T(8,128)S(1)}, f32[4,16,256]{2,1,0:T(8,128)S(1)}, u32[]{:S(2)}, u32[]{:S(2)}) collective-permute-start(f32[4,16,256]{2,1,0:T(8,128)S(1)} %shard_map.69.refs_5_), channel_id=1, source_target_pairs={{3,0},{2,1},{1,2},{0,3},{7,4},{6,5},{5,6},{4,7},{11,8},{10,9},{9,1... | collective-permute-start | bytes 196616 | tf_op jit(solution)/shard_map/ppermute | solution.py:164
  17.9 4.3 %collective-permute-start.6 = (f32[4,16,256]{2,1,0:T(8,128)S(1)}, f32[4,16,256]{2,1,0:T(8,128)S(1)}, u32[]{:S(2)}, u32[]{:S(2)}) collective-permute-start(f32[4,16,256]{2,1,0:T(8,128)S(1)} %shard_map.69.refs_5_), channel_id=1, source_target_pairs={{1,0},{0,1},{3,2},{2,3},{5,4},{4,5},{7,6},{6,7},{9,8},{8,9},{11,10... | collective-permute-start | bytes 196616 | tf_op jit(solution)/shard_map/ppermute | solution.py:164
  22.3 4.9 %collective-permute-start.11 = (f32[16,128]{1,0:T(8,128)S(1)}, f32[16,128]{1,0:T(8,128)S(1)}, u32[]{:S(2)}, u32[]{:S(2)}) collective-permute-start(f32[16,128]{1,0:T(8,128)S(1)} %get-tuple-element.16.refs_0_), channel_id=1, source_target_pairs={{13,0},{12,1},{9,4},{8,5},{5,8},{4,9},{1,12},{0,13},{15,2},{14,3},... | collective-permute-start | bytes 24584 | tf_op jit(solution)/shard_map/ppermute | solution.py:179
  23.3 4.0 %collective-permute-start.10 = (f32[16,128]{1,0:T(8,128)S(1)}, f32[16,128]{1,0:T(8,128)S(1)}, u32[]{:S(2)}, u32[]{:S(2)}) collective-permute-start(f32[16,128]{1,0:T(8,128)S(1)} %get-tuple-element.16.refs_0_), channel_id=1, source_target_pairs={{9,0},{8,1},{13,4},{12,5},{1,8},{0,9},{5,12},{4,13},{11,2},{10,3},... | collective-permute-start | bytes 24584 | tf_op jit(solution)/shard_map/ppermute | solution.py:179
  23.6 3.8 %collective-permute-start.9 = (f32[16,128]{1,0:T(8,128)S(1)}, f32[16,128]{1,0:T(8,128)S(1)}, u32[]{:S(2)}, u32[]{:S(2)}) collective-permute-start(f32[16,128]{1,0:T(8,128)S(1)} %get-tuple-element.16.refs_0_), channel_id=1, source_target_pairs={{5,0},{4,1},{1,4},{0,5},{13,8},{12,9},{9,12},{8,13},{7,2},{6,3},{3... | collective-permute-start | bytes 24584 | tf_op jit(solution)/shard_map/ppermute | solution.py:179

commit v20 on v19

--- a/solution.py
+++ b/solution.py
@@ -68,16 +68,20 @@
     partial_ref = refs[-1]
     rows = [rows_ref[number] for number in range(2)]
     rows += [rows_of(ref, feature_count) for ref in plane_refs]
-    totals = [start_ref[...]]
-    totals += [jnp.zeros(start_ref.shape, jnp.float32)] * (plane_count - 1)
+    start = start_ref[...]
+    width = start.shape[1]
+    rows = [
+        jnp.concatenate(rows[number : number + 2], axis=1) for number in range(0, plane_count, 2)
+    ]
+    totals = [jnp.zeros((start.shape[0], own.shape[1]), jnp.float32) for own in rows]
 
     def add_columns(columns, probes, totals):
-        result = []
-        for own, total in zip(rows, totals):
-            exponent = jnp.dot(columns, own, preferred_element_type=jnp.float32)
-            weights = jnp.exp(exponent).astype(jnp.bfloat16)
-            result.append(total + jnp.dot(probes, weights, preferred_element_type=jnp.float32))
-        return result
+        exponent = [jnp.dot(columns, own, preferred_element_type=jnp.float32) for own in rows]
+        weights = [jnp.exp(value).astype(jnp.bfloat16) for value in exponent]
+        return [
+            total + jnp.dot(probes, value, preferred_element_type=jnp.float32)
+            for total, value in zip(totals, weights)
+        ]
 
     if len(line_refs[0].shape) == 2:
         *early, late = [ref[...] for ref in line_refs]
@@ -94,8 +98,10 @@
             )
 
         totals = lax.fori_loop(0, line_refs[0].shape[0], add_block, totals)
-    for number, total in enumerate(totals):
-        partial_ref[number] = total
+    for number in range(plane_count):
+        place = number % 2 * width
+        total = totals[number // 2][:, place : place + width]
+        partial_ref[number] = total + start if number == 0 else total
 
 
 def combine_kernel(feature_count, plane_count, *refs):

time: 28.4 us -> 27.6 us (0.972)
  Pallas kernels: 2.86 us -> 2.06 us
    pallas_call x1, Pallas kernels: 1.77 us -> 0.98 us  [local(): pl.pallas_call(lambda *refs: image_kernel(feature_count, plane_count, *re...]
where the time goes in v20:
time: 27.6 us; the launch traced here: 27.4 us
  starting transfers between devices  13.1 us (47%)
  waiting for transfers between devices  10.6 us (38%)
  Pallas kernels  2.06 us (7%)
  other arithmetic  0.93 us (3%)
  between operations  0.68 us (2%)
    ppermute x6, starting transfers between devices, along_line(): blocks.append(lax.ppermute(value, LINE + ('sub',), pairs))  8.43 us
    ppermute x6, waiting for transfers between devices, along_line(): blocks.append(lax.ppermute(value, LINE + ('sub',), pairs))  6.98 us
    ppermute x6, starting transfers between devices, everywhere(): lax.ppermute(value, axes, [(source_of(i, step, count), i) for i in range(...  4.7 us
    ppermute x6, waiting for transfers between devices, everywhere(): lax.ppermute(value, axes, [(source_of(i, step, count), i) for i in range(...  3.61 us
    pallas_call x1, Pallas kernels, local(): pl.pallas_call(lambda *refs: image_kernel(feature_count, plane_count, *re...  0.98 us
    convert_element_type x1, other arithmetic, local(): (features.astype(jnp.float32) / lengthscale[:, None]).astype(jnp.bfloat16)  0.93 us
    pallas_call x1, Pallas kernels, local(): pl.pallas_call(finish_kernel, out_shape=outs, compiler_params=VMEM)  0.77 us
  transfers between devices with their start and end apart: 12, of which 8 were waited for; matrix products, arithmetic and copies ran while one was open for 0% of the time, Pallas kernels for 1%

profile of v20, /device:TPU:0, one launch (start us, length us, event | category | flops | bytes accessed | tf_op | source)
XLA Modules:
  0.0 27.4 jit_solution(13090926404179107878)
XLA Ops:
  0.6 0.0 copy-start
  0.6 0.9 %divide_convert_fusion.scaled_ref = bf16[128,256]{1,0:T(8,128)(2,1)S(1)} fusion(bf16[128,256]{1,0:T(8,128)(2,1)} %param.4, f32[128]{0:T(128)} %param.5), kind=kLoop, calls=%fused_computation | loop fusion | flops 98304 | bytes 131584 | tf_op jit(solution)/shard_map/convert_element_type | solution.py:204
  1.6 0.0 copy-done
  1.6 0.5 %collective-permute-start = (bf16[160,256]{1,0:T(8,128)(2,1)S(1)}, bf16[160,256]{1,0:T(8,128)(2,1)S(1)}, u32[]{:S(2)}, u32[]{:S(2)}) collective-permute-start(bf16[160,256]{1,0:T(8,128)(2,1)S(1)} %get-tuple-element.10.refs_0_), channel_id=1, source_target_pairs={{1,0},{0,1},{3,2},{2,3},{5,4},{4,5},{7,6},{6,7},{9,8},{8,9},{11,10... | collective-permute-start | bytes 245768 | tf_op jit(solution)/shard_map/ppermute | solution.py:170
  2.1 0.0 copy-start.1
  2.1 4.7 %collective-permute-start.4 = (bf16[144,256]{1,0:T(8,128)(2,1)S(1)}, bf16[144,256]{1,0:T(8,128)(2,1)S(1)}, u32[]{:S(2)}, u32[]{:S(2)}) collective-permute-start(bf16[144,256]{1,0:T(8,128)(2,1)S(1)} %get-tuple-element.11.refs_2_.refs_5_), channel_id=1, source_target_pairs={{13,0},{12,1},{9,4},{8,5},{5,8},{4,9},{1,12},{0,13},{15,2},{14,3},... | collective-permute-start | bytes 221192 | tf_op jit(solution)/shard_map/ppermute | solution.py:185
  6.9 0.0 collective-permute-start.3
  6.9 1.5 %collective-permute-start.1 = (bf16[160,256]{1,0:T(8,128)(2,1)S(1)}, bf16[160,256]{1,0:T(8,128)(2,1)S(1)}, u32[]{:S(2)}, u32[]{:S(2)}) collective-permute-start(bf16[160,256]{1,0:T(8,128)(2,1)S(1)} %get-tuple-element.10.refs_0_), channel_id=1, source_target_pairs={{2,0},{0,2},{3,1},{1,3},{6,4},{4,6},{7,5},{5,7},{10,8},{8,10},{11,... | collective-permute-start | bytes 245768 | tf_op jit(solution)/shard_map/ppermute | solution.py:170
  8.4 0.0 collective-permute-done.refs_1_
  8.4 0.5 %collective-permute-start.2 = (bf16[160,256]{1,0:T(8,128)(2,1)S(1)}, bf16[160,256]{1,0:T(8,128)(2,1)S(1)}, u32[]{:S(2)}, u32[]{:S(2)}) collective-permute-start(bf16[160,256]{1,0:T(8,128)(2,1)S(1)} %collective-permute-done.refs_1_), channel_id=1, source_target_pairs={{2,0},{0,2},{3,1},{1,3},{6,4},{4,6},{7,5},{5,7},{10,8},{8,10},{11,... | collective-permute-start | bytes 245768 | tf_op jit(solution)/shard_map/ppermute | solution.py:170
  8.9 0.0 collective-permute-start.5
  8.9 0.6 %collective-permute-done.4.refs_4_.refs_7_ = bf16[144,256]{1,0:T(8,128)(2,1)S(1)} collective-permute-done((bf16[144,256]{1,0:T(8,128)(2,1)S(1)}, bf16[144,256]{1,0:T(8,128)(2,1)S(1)}, u32[]{:S(2)}, u32[]{:S(2)}) %collective-permute-start.4) | collective-permute-done | bytes 73760 | tf_op jit(solution)/shard_map/ppermute | solution.py:185
  9.5 3.6 %collective-permute-done.3.refs_3_.refs_6_ = bf16[144,256]{1,0:T(8,128)(2,1)S(1)} collective-permute-done((bf16[144,256]{1,0:T(8,128)(2,1)S(1)}, bf16[144,256]{1,0:T(8,128)(2,1)S(1)}, u32[]{:S(2)}, u32[]{:S(2)}) %collective-permute-start.3) | collective-permute-done | bytes 73760 | tf_op jit(solution)/shard_map/ppermute | solution.py:185
  13.1 0.0 copy-done.1
  13.1 0.2 shard_map.68
  13.3 1.4 %collective-permute-done.5.refs_8_ = bf16[144,256]{1,0:T(8,128)(2,1)S(1)} collective-permute-done((bf16[144,256]{1,0:T(8,128)(2,1)S(1)}, bf16[144,256]{1,0:T(8,128)(2,1)S(1)}, u32[]{:S(2)}, u32[]{:S(2)}) %collective-permute-start.5) | collective-permute-done | bytes 73760 | tf_op jit(solution)/shard_map/ppermute | solution.py:185
  14.6 0.0 collective-permute-done.1.refs_2_
  14.7 0.0 collective-permute-done.2.refs_3_
  14.7 1.0 %shard_map.69.refs_5_ = f32[4,16,256]{2,1,0:T(8,128)S(1)} custom-call(bf16[2,144,256]{2,1,0:T(8,128)(2,1)S(1)} %get-tuple-element.12.refs_0_, f32[16,256]{1,0:T(8,128)S(1)} %get-tuple-element.13.refs_1_, bf16[160,256]{1,0:T(8,128)(2,1)S(1)} %collective-permute-done.1.refs_2_, bf16[160,256]{1,0:T(8,128)(2,1)S(1)} %collective-permute-done.2.refs_3_, ...), custom_call_target="tpu_custom_call" | custom-call | tf_op jit(solution)/shard_map/pallas_call | solution.py:233
  15.6 1.5 %collective-permute-start.8 = (f32[4,16,256]{2,1,0:T(8,128)S(1)}, f32[4,16,256]{2,1,0:T(8,128)S(1)}, u32[]{:S(2)}, u32[]{:S(2)}) collective-permute-start(f32[4,16,256]{2,1,0:T(8,128)S(1)} %shard_map.69.refs_5_), channel_id=1, source_target_pairs={{2,0},{3,1},{0,2},{1,3},{6,4},{7,5},{4,6},{5,7},{10,8},{11,9},{8,1... | collective-permute-start | bytes 196616 | tf_op jit(solution)/shard_map/ppermute | solution.py:170
  17.1 0.0 collective-permute-start.7
  17.1 0.7 %collective-permute-start.6 = (f32[4,16,256]{2,1,0:T(8,128)S(1)}, f32[4,16,256]{2,1,0:T(8,128)S(1)}, u32[]{:S(2)}, u32[]{:S(2)}) collective-permute-start(f32[4,16,256]{2,1,0:T(8,128)S(1)} %shard_map.69.refs_5_), channel_id=1, source_target_pairs={{1,0},{0,1},{3,2},{2,3},{5,4},{4,5},{7,6},{6,7},{9,8},{8,9},{11,10... | collective-permute-start | bytes 196616 | tf_op jit(solution)/shard_map/ppermute | solution.py:170
  17.8 2.1 %collective-permute-done.8.refs_8_ = f32[4,16,256]{2,1,0:T(8,128)S(1)} collective-permute-done((f32[4,16,256]{2,1,0:T(8,128)S(1)}, f32[4,16,256]{2,1,0:T(8,128)S(1)}, u32[]{:S(2)}, u32[]{:S(2)}) %collective-permute-start.8) | collective-permute-done | bytes 65568 | tf_op jit(solution)/shard_map/ppermute | solution.py:170
  19.9 1.5 %collective-permute-done.7.refs_7_ = f32[4,16,256]{2,1,0:T(8,128)S(1)} collective-permute-done((f32[4,16,256]{2,1,0:T(8,128)S(1)}, f32[4,16,256]{2,1,0:T(8,128)S(1)}, u32[]{:S(2)}, u32[]{:S(2)}) %collective-permute-start.7) | collective-permute-done | bytes 65568 | tf_op jit(solution)/shard_map/ppermute | solution.py:170
  21.4 0.0 collective-permute-done.6.refs_6_
  21.4 0.1 shard_map.70
  21.5 1.0 %collective-permute-start.11 = (f32[16,128]{1,0:T(8,128)S(1)}, f32[16,128]{1,0:T(8,128)S(1)}, u32[]{:S(2)}, u32[]{:S(2)}) collective-permute-start(f32[16,128]{1,0:T(8,128)S(1)} %get-tuple-element.16.refs_0_), channel_id=1, source_target_pairs={{13,0},{12,1},{9,4},{8,5},{5,8},{4,9},{1,12},{0,13},{15,2},{14,3},... | collective-permute-start | bytes 24584 | tf_op jit(solution)/shard_map/ppermute | solution.py:185
  22.5 0.3 %collective-permute-start.10 = (f32[16,128]{1,0:T(8,128)S(1)}, f32[16,128]{1,0:T(8,128)S(1)}, u32[]{:S(2)}, u32[]{:S(2)}) collective-permute-start(f32[16,128]{1,0:T(8,128)S(1)} %get-tuple-element.16.refs_0_), channel_id=1, source_target_pairs={{9,0},{8,1},{13,4},{12,5},{1,8},{0,9},{5,12},{4,13},{11,2},{10,3},... | collective-permute-start | bytes 24584 | tf_op jit(solution)/shard_map/ppermute | solution.py:185
  22.8 2.4 %collective-permute-start.9 = (f32[16,128]{1,0:T(8,128)S(1)}, f32[16,128]{1,0:T(8,128)S(1)}, u32[]{:S(2)}, u32[]{:S(2)}) collective-permute-start(f32[16,128]{1,0:T(8,128)S(1)} %get-tuple-element.16.refs_0_), channel_id=1, source_target_pairs={{5,0},{4,1},{1,4},{0,5},{13,8},{12,9},{9,12},{8,13},{7,2},{6,3},{3... | collective-permute-start | bytes 24584 | tf_op jit(solution)/shard_map/ppermute | solution.py:185
  25.2 1.2 %collective-permute-done.11.refs_3_ = f32[16,128]{1,0:T(8,128)S(1)} collective-permute-done((f32[16,128]{1,0:T(8,128)S(1)}, f32[16,128]{1,0:T(8,128)S(1)}, u32[]{:S(2)}, u32[]{:S(2)}) %collective-permute-start.11) | collective-permute-done | bytes 8224 | tf_op jit(solution)/shard_map/ppermute | solution.py:185
  26.4 0.1 collective-permute-done.10.refs_2_
  26.5 0.2 collective-permute-done.9.refs_1_
  26.6 0.8 %shard_map.71 = (f32[16,256]{1,0:T(8,128)}, f32[16,256]{1,0:T(8,128)}, f32[16,256]{1,0:T(8,128)}) custom-call(f32[16,256]{1,0:T(8,128)S(1)} %get-tuple-element.15.image_ref, f32[16,256]{1,0:T(8,128)S(1)} %copy-done, f32[16,128]{1,0:T(8,128)S(1)} %get-tuple-element.16.refs_0_, f32[16,128]{1,0:T(8,128)S(1)} %collective-permute-done.9.refs_1_, ...), custom_call_target="tpu_custom_call" | custom-call | tf_op jit(solution)/shard_map/pallas_call | solution.py:248
  (1 shorter events, 0.0 us)
Async XLA Ops:
  0.6 1.0 %copy-start = (f32[16,256]{1,0:T(8,128)S(1)}, f32[16,256]{1,0:T(8,128)}, u32[]{:S(2)}) copy-start(f32[16,256]{1,0:T(8,128)} %probes_ref.3) | copy-start | bytes 49156
  1.6 6.7 %collective-permute-start = (bf16[160,256]{1,0:T(8,128)(2,1)S(1)}, bf16[160,256]{1,0:T(8,128)(2,1)S(1)}, u32[]{:S(2)}, u32[]{:S(2)}) collective-permute-start(bf16[160,256]{1,0:T(8,128)(2,1)S(1)} %get-tuple-element.10.refs_0_), channel_id=1, source_target_pairs={{1,0},{0,1},{3,2},{2,3},{5,4},{4,5},{7,6},{6,7},{9,8},{8,9},{11,10... | collective-permute-start | bytes 245768 | tf_op jit(solution)/shard_map/ppermute | solution.py:170
  2.1 10.9 %copy-start.1 = (f32[256]{0:T(256)S(1)}, f32[256]{0:T(256)}, u32[]{:S(2)}) copy-start(f32[256]{0:T(256)} %param.6) | copy-start | bytes 3076
  2.1 7.4 %collective-permute-start.4 = (bf16[144,256]{1,0:T(8,128)(2,1)S(1)}, bf16[144,256]{1,0:T(8,128)(2,1)S(1)}, u32[]{:S(2)}, u32[]{:S(2)}) collective-permute-start(bf16[144,256]{1,0:T(8,128)(2,1)S(1)} %get-tuple-element.11.refs_2_.refs_5_), channel_id=1, source_target_pairs={{13,0},{12,1},{9,4},{8,5},{5,8},{4,9},{1,12},{0,13},{15,2},{14,3},... | collective-permute-start | bytes 221192 | tf_op jit(solution)/shard_map/ppermute | solution.py:185
  6.9 6.2 %collective-permute-start.3 = (bf16[144,256]{1,0:T(8,128)(2,1)S(1)}, bf16[144,256]{1,0:T(8,128)(2,1)S(1)}, u32[]{:S(2)}, u32[]{:S(2)}) collective-permute-start(bf16[144,256]{1,0:T(8,128)(2,1)S(1)} %get-tuple-element.11.refs_2_.refs_5_), channel_id=1, source_target_pairs={{9,0},{8,1},{13,4},{12,5},{1,8},{0,9},{5,12},{4,13},{11,2},{10,3},... | collective-permute-start | bytes 221192 | tf_op jit(solution)/shard_map/ppermute | solution.py:185
  6.9 7.8 %collective-permute-start.1 = (bf16[160,256]{1,0:T(8,128)(2,1)S(1)}, bf16[160,256]{1,0:T(8,128)(2,1)S(1)}, u32[]{:S(2)}, u32[]{:S(2)}) collective-permute-start(bf16[160,256]{1,0:T(8,128)(2,1)S(1)} %get-tuple-element.10.refs_0_), channel_id=1, source_target_pairs={{2,0},{0,2},{3,1},{1,3},{6,4},{4,6},{7,5},{5,7},{10,8},{8,10},{11,... | collective-permute-start | bytes 245768 | tf_op jit(solution)/shard_map/ppermute | solution.py:170
  8.4 6.3 %collective-permute-start.2 = (bf16[160,256]{1,0:T(8,128)(2,1)S(1)}, bf16[160,256]{1,0:T(8,128)(2,1)S(1)}, u32[]{:S(2)}, u32[]{:S(2)}) collective-permute-start(bf16[160,256]{1,0:T(8,128)(2,1)S(1)} %collective-permute-done.refs_1_), channel_id=1, source_target_pairs={{2,0},{0,2},{3,1},{1,3},{6,4},{4,6},{7,5},{5,7},{10,8},{8,10},{11,... | collective-permute-start | bytes 245768 | tf_op jit(solution)/shard_map/ppermute | solution.py:170
  8.9 5.8 %collective-permute-start.5 = (bf16[144,256]{1,0:T(8,128)(2,1)S(1)}, bf16[144,256]{1,0:T(8,128)(2,1)S(1)}, u32[]{:S(2)}, u32[]{:S(2)}) collective-permute-start(bf16[144,256]{1,0:T(8,128)(2,1)S(1)} %get-tuple-element.11.refs_2_.refs_5_), channel_id=1, source_target_pairs={{5,0},{4,1},{1,4},{0,5},{13,8},{12,9},{9,12},{8,13},{7,2},{6,3},{3... | collective-permute-start | bytes 221192 | tf_op jit(solution)/shard_map/ppermute | solution.py:185
  15.6 4.3 %collective-permute-start.8 = (f32[4,16,256]{2,1,0:T(8,128)S(1)}, f32[4,16,256]{2,1,0:T(8,128)S(1)}, u32[]{:S(2)}, u32[]{:S(2)}) collective-permute-start(f32[4,16,256]{2,1,0:T(8,128)S(1)} %shard_map.69.refs_5_), channel_id=1, source_target_pairs={{2,0},{3,1},{0,2},{1,3},{6,4},{7,5},{4,6},{5,7},{10,8},{11,9},{8,1... | collective-permute-start | bytes 196616 | tf_op jit(solution)/shard_map/ppermute | solution.py:170
  17.1 4.3 %collective-permute-start.7 = (f32[4,16,256]{2,1,0:T(8,128)S(1)}, f32[4,16,256]{2,1,0:T(8,128)S(1)}, u32[]{:S(2)}, u32[]{:S(2)}) collective-permute-start(f32[4,16,256]{2,1,0:T(8,128)S(1)} %shard_map.69.refs_5_), channel_id=1, source_target_pairs={{3,0},{2,1},{1,2},{0,3},{7,4},{6,5},{5,6},{4,7},{11,8},{10,9},{9,1... | collective-permute-start | bytes 196616 | tf_op jit(solution)/shard_map/ppermute | solution.py:170
  17.1 4.3 %collective-permute-start.6 = (f32[4,16,256]{2,1,0:T(8,128)S(1)}, f32[4,16,256]{2,1,0:T(8,128)S(1)}, u32[]{:S(2)}, u32[]{:S(2)}) collective-permute-start(f32[4,16,256]{2,1,0:T(8,128)S(1)} %shard_map.69.refs_5_), channel_id=1, source_target_pairs={{1,0},{0,1},{3,2},{2,3},{5,4},{4,5},{7,6},{6,7},{9,8},{8,9},{11,10... | collective-permute-start | bytes 196616 | tf_op jit(solution)/shard_map/ppermute | solution.py:170
  21.5 4.9 %collective-permute-start.11 = (f32[16,128]{1,0:T(8,128)S(1)}, f32[16,128]{1,0:T(8,128)S(1)}, u32[]{:S(2)}, u32[]{:S(2)}) collective-permute-start(f32[16,128]{1,0:T(8,128)S(1)} %get-tuple-element.16.refs_0_), channel_id=1, source_target_pairs={{13,0},{12,1},{9,4},{8,5},{5,8},{4,9},{1,12},{0,13},{15,2},{14,3},... | collective-permute-start | bytes 24584 | tf_op jit(solution)/shard_map/ppermute | solution.py:185
  22.5 4.0 %collective-permute-start.10 = (f32[16,128]{1,0:T(8,128)S(1)}, f32[16,128]{1,0:T(8,128)S(1)}, u32[]{:S(2)}, u32[]{:S(2)}) collective-permute-start(f32[16,128]{1,0:T(8,128)S(1)} %get-tuple-element.16.refs_0_), channel_id=1, source_target_pairs={{9,0},{8,1},{13,4},{12,5},{1,8},{0,9},{5,12},{4,13},{11,2},{10,3},... | collective-permute-start | bytes 24584 | tf_op jit(solution)/shard_map/ppermute | solution.py:185
  22.8 3.8 %collective-permute-start.9 = (f32[16,128]{1,0:T(8,128)S(1)}, f32[16,128]{1,0:T(8,128)S(1)}, u32[]{:S(2)}, u32[]{:S(2)}) collective-permute-start(f32[16,128]{1,0:T(8,128)S(1)} %get-tuple-element.16.refs_0_), channel_id=1, source_target_pairs={{5,0},{4,1},{1,4},{0,5},{13,8},{12,9},{9,12},{8,13},{7,2},{6,3},{3... | collective-permute-start | bytes 24584 | tf_op jit(solution)/shard_map/ppermute | solution.py:185

commit v21 on v20

--- a/solution.py
+++ b/solution.py
@@ -11,6 +11,7 @@
 VMEM = pltpu.CompilerParams(vmem_limit_bytes=40 * 1024 * 1024)
 PARTIALS, PARTIALS_BACK = (0, 1, 3, 2), (0, 1, 3, 2)
 SUMS = (0, 1, 2, 3)
+ABREAST = 4
 HALF = 8
 
 
@@ -71,7 +72,8 @@
     start = start_ref[...]
     width = start.shape[1]
     rows = [
-        jnp.concatenate(rows[number : number + 2], axis=1) for number in range(0, plane_count, 2)
+        jnp.concatenate(rows[number : number + ABREAST], axis=1)
+        for number in range(0, plane_count, ABREAST)
     ]
     totals = [jnp.zeros((start.shape[0], own.shape[1]), jnp.float32) for own in rows]
 
@@ -99,8 +101,8 @@
 
         totals = lax.fori_loop(0, line_refs[0].shape[0], add_block, totals)
     for number in range(plane_count):
-        place = number % 2 * width
-        total = totals[number // 2][:, place : place + width]
+        place = number % ABREAST * width
+        total = totals[number // ABREAST][:, place : place + width]
         partial_ref[number] = total + start if number == 0 else total
 
 

time: 27.6 us -> 27.6 us (level)
  no operation moved by 1% of the time
where the time goes in v21:
time: 27.6 us; the launch traced here: 27.4 us
  starting transfers between devices  13.1 us (47%)
  waiting for transfers between devices  10.6 us (38%)
  Pallas kernels  2.06 us (7%)
  other arithmetic  0.93 us (3%)
  between operations  0.68 us (2%)
    ppermute x6, starting transfers between devices, along_line(): blocks.append(lax.ppermute(value, LINE + ('sub',), pairs))  8.43 us
    ppermute x6, waiting for transfers between devices, along_line(): blocks.append(lax.ppermute(value, LINE + ('sub',), pairs))  6.98 us
    ppermute x6, starting transfers between devices, everywhere(): lax.ppermute(value, axes, [(source_of(i, step, count), i) for i in range(...  4.7 us
    ppermute x6, waiting for transfers between devices, everywhere(): lax.ppermute(value, axes, [(source_of(i, step, count), i) for i in range(...  3.61 us
    pallas_call x1, Pallas kernels, local(): pl.pallas_call(lambda *refs: image_kernel(feature_count, plane_count, *re...  0.98 us
    convert_element_type x1, other arithmetic, local(): (features.astype(jnp.float32) / lengthscale[:, None]).astype(jnp.bfloat16)  0.93 us
    pallas_call x1, Pallas kernels, local(): pl.pallas_call(finish_kernel, out_shape=outs, compiler_params=VMEM)  0.77 us
  transfers between devices with their start and end apart: 12, of which 8 were waited for; matrix products, arithmetic and copies ran while one was open for 0% of the time, Pallas kernels for 1%

profile of v21, /device:TPU:0, one launch (start us, length us, event | category | flops | bytes accessed | tf_op | source)
XLA Modules:
  0.0 27.4 jit_solution(13090926404179107878)
XLA Ops:
  0.6 0.0 copy-start
  0.6 0.9 %divide_convert_fusion.scaled_ref = bf16[128,256]{1,0:T(8,128)(2,1)S(1)} fusion(bf16[128,256]{1,0:T(8,128)(2,1)} %param.4, f32[128]{0:T(128)} %param.5), kind=kLoop, calls=%fused_computation | loop fusion | flops 98304 | bytes 131584 | tf_op jit(solution)/shard_map/convert_element_type | solution.py:206
  1.6 0.0 copy-done
  1.6 0.5 %collective-permute-start = (bf16[160,256]{1,0:T(8,128)(2,1)S(1)}, bf16[160,256]{1,0:T(8,128)(2,1)S(1)}, u32[]{:S(2)}, u32[]{:S(2)}) collective-permute-start(bf16[160,256]{1,0:T(8,128)(2,1)S(1)} %get-tuple-element.10.refs_0_), channel_id=1, source_target_pairs={{1,0},{0,1},{3,2},{2,3},{5,4},{4,5},{7,6},{6,7},{9,8},{8,9},{11,10... | collective-permute-start | bytes 245768 | tf_op jit(solution)/shard_map/ppermute | solution.py:172
  2.1 0.0 copy-start.1
  2.1 4.7 %collective-permute-start.4 = (bf16[144,256]{1,0:T(8,128)(2,1)S(1)}, bf16[144,256]{1,0:T(8,128)(2,1)S(1)}, u32[]{:S(2)}, u32[]{:S(2)}) collective-permute-start(bf16[144,256]{1,0:T(8,128)(2,1)S(1)} %get-tuple-element.11.refs_2_.refs_5_), channel_id=1, source_target_pairs={{13,0},{12,1},{9,4},{8,5},{5,8},{4,9},{1,12},{0,13},{15,2},{14,3},... | collective-permute-start | bytes 221192 | tf_op jit(solution)/shard_map/ppermute | solution.py:187
  6.9 0.0 collective-permute-start.3
  6.9 1.5 %collective-permute-start.1 = (bf16[160,256]{1,0:T(8,128)(2,1)S(1)}, bf16[160,256]{1,0:T(8,128)(2,1)S(1)}, u32[]{:S(2)}, u32[]{:S(2)}) collective-permute-start(bf16[160,256]{1,0:T(8,128)(2,1)S(1)} %get-tuple-element.10.refs_0_), channel_id=1, source_target_pairs={{2,0},{0,2},{3,1},{1,3},{6,4},{4,6},{7,5},{5,7},{10,8},{8,10},{11,... | collective-permute-start | bytes 245768 | tf_op jit(solution)/shard_map/ppermute | solution.py:172
  8.4 0.0 collective-permute-done.refs_1_
  8.4 0.5 %collective-permute-start.2 = (bf16[160,256]{1,0:T(8,128)(2,1)S(1)}, bf16[160,256]{1,0:T(8,128)(2,1)S(1)}, u32[]{:S(2)}, u32[]{:S(2)}) collective-permute-start(bf16[160,256]{1,0:T(8,128)(2,1)S(1)} %collective-permute-done.refs_1_), channel_id=1, source_target_pairs={{2,0},{0,2},{3,1},{1,3},{6,4},{4,6},{7,5},{5,7},{10,8},{8,10},{11,... | collective-permute-start | bytes 245768 | tf_op jit(solution)/shard_map/ppermute | solution.py:172
  8.9 0.0 collective-permute-start.5
  8.9 0.6 %collective-permute-done.4.refs_4_.refs_7_ = bf16[144,256]{1,0:T(8,128)(2,1)S(1)} collective-permute-done((bf16[144,256]{1,0:T(8,128)(2,1)S(1)}, bf16[144,256]{1,0:T(8,128)(2,1)S(1)}, u32[]{:S(2)}, u32[]{:S(2)}) %collective-permute-start.4) | collective-permute-done | bytes 73760 | tf_op jit(solution)/shard_map/ppermute | solution.py:187
  9.5 3.6 %collective-permute-done.3.refs_3_.refs_6_ = bf16[144,256]{1,0:T(8,128)(2,1)S(1)} collective-permute-done((bf16[144,256]{1,0:T(8,128)(2,1)S(1)}, bf16[144,256]{1,0:T(8,128)(2,1)S(1)}, u32[]{:S(2)}, u32[]{:S(2)}) %collective-permute-start.3) | collective-permute-done | bytes 73760 | tf_op jit(solution)/shard_map/ppermute | solution.py:187
  13.1 0.0 copy-done.1
  13.1 0.2 shard_map.68
  13.3 1.4 %collective-permute-done.5.refs_8_ = bf16[144,256]{1,0:T(8,128)(2,1)S(1)} collective-permute-done((bf16[144,256]{1,0:T(8,128)(2,1)S(1)}, bf16[144,256]{1,0:T(8,128)(2,1)S(1)}, u32[]{:S(2)}, u32[]{:S(2)}) %collective-permute-start.5) | collective-permute-done | bytes 73760 | tf_op jit(solution)/shard_map/ppermute | solution.py:187
  14.6 0.0 collective-permute-done.1.refs_2_
  14.7 0.0 collective-permute-done.2.refs_3_
  14.7 1.0 %shard_map.69.refs_5_ = f32[4,16,256]{2,1,0:T(8,128)S(1)} custom-call(bf16[2,144,256]{2,1,0:T(8,128)(2,1)S(1)} %get-tuple-element.12.refs_0_, f32[16,256]{1,0:T(8,128)S(1)} %get-tuple-element.13.refs_1_, bf16[160,256]{1,0:T(8,128)(2,1)S(1)} %collective-permute-done.1.refs_2_, bf16[160,256]{1,0:T(8,128)(2,1)S(1)} %collective-permute-done.2.refs_3_, ...), custom_call_target="tpu_custom_call" | custom-call | tf_op jit(solution)/shard_map/pallas_call | solution.py:235
  15.6 1.5 %collective-permute-start.8 = (f32[4,16,256]{2,1,0:T(8,128)S(1)}, f32[4,16,256]{2,1,0:T(8,128)S(1)}, u32[]{:S(2)}, u32[]{:S(2)}) collective-permute-start(f32[4,16,256]{2,1,0:T(8,128)S(1)} %shard_map.69.refs_5_), channel_id=1, source_target_pairs={{2,0},{3,1},{0,2},{1,3},{6,4},{7,5},{4,6},{5,7},{10,8},{11,9},{8,1... | collective-permute-start | bytes 196616 | tf_op jit(solution)/shard_map/ppermute | solution.py:172
  17.1 0.0 collective-permute-start.7
  17.1 0.7 %collective-permute-start.6 = (f32[4,16,256]{2,1,0:T(8,128)S(1)}, f32[4,16,256]{2,1,0:T(8,128)S(1)}, u32[]{:S(2)}, u32[]{:S(2)}) collective-permute-start(f32[4,16,256]{2,1,0:T(8,128)S(1)} %shard_map.69.refs_5_), channel_id=1, source_target_pairs={{1,0},{0,1},{3,2},{2,3},{5,4},{4,5},{7,6},{6,7},{9,8},{8,9},{11,10... | collective-permute-start | bytes 196616 | tf_op jit(solution)/shard_map/ppermute | solution.py:172
  17.8 2.1 %collective-permute-done.8.refs_8_ = f32[4,16,256]{2,1,0:T(8,128)S(1)} collective-permute-done((f32[4,16,256]{2,1,0:T(8,128)S(1)}, f32[4,16,256]{2,1,0:T(8,128)S(1)}, u32[]{:S(2)}, u32[]{:S(2)}) %collective-permute-start.8) | collective-permute-done | bytes 65568 | tf_op jit(solution)/shard_map/ppermute | solution.py:172
  19.9 1.5 %collective-permute-done.7.refs_7_ = f32[4,16,256]{2,1,0:T(8,128)S(1)} collective-permute-done((f32[4,16,256]{2,1,0:T(8,128)S(1)}, f32[4,16,256]{2,1,0:T(8,128)S(1)}, u32[]{:S(2)}, u32[]{:S(2)}) %collective-permute-start.7) | collective-permute-done | bytes 65568 | tf_op jit(solution)/shard_map/ppermute | solution.py:172
  21.4 0.0 collective-permute-done.6.refs_6_
  21.4 0.1 shard_map.70
  21.5 1.0 %collective-permute-start.11 = (f32[16,128]{1,0:T(8,128)S(1)}, f32[16,128]{1,0:T(8,128)S(1)}, u32[]{:S(2)}, u32[]{:S(2)}) collective-permute-start(f32[16,128]{1,0:T(8,128)S(1)} %get-tuple-element.16.refs_0_), channel_id=1, source_target_pairs={{13,0},{12,1},{9,4},{8,5},{5,8},{4,9},{1,12},{0,13},{15,2},{14,3},... | collective-permute-start | bytes 24584 | tf_op jit(solution)/shard_map/ppermute | solution.py:187
  22.5 0.3 %collective-permute-start.10 = (f32[16,128]{1,0:T(8,128)S(1)}, f32[16,128]{1,0:T(8,128)S(1)}, u32[]{:S(2)}, u32[]{:S(2)}) collective-permute-start(f32[16,128]{1,0:T(8,128)S(1)} %get-tuple-element.16.refs_0_), channel_id=1, source_target_pairs={{9,0},{8,1},{13,4},{12,5},{1,8},{0,9},{5,12},{4,13},{11,2},{10,3},... | collective-permute-start | bytes 24584 | tf_op jit(solution)/shard_map/ppermute | solution.py:187
  22.8 2.4 %collective-permute-start.9 = (f32[16,128]{1,0:T(8,128)S(1)}, f32[16,128]{1,0:T(8,128)S(1)}, u32[]{:S(2)}, u32[]{:S(2)}) collective-permute-start(f32[16,128]{1,0:T(8,128)S(1)} %get-tuple-element.16.refs_0_), channel_id=1, source_target_pairs={{5,0},{4,1},{1,4},{0,5},{13,8},{12,9},{9,12},{8,13},{7,2},{6,3},{3... | collective-permute-start | bytes 24584 | tf_op jit(solution)/shard_map/ppermute | solution.py:187
  25.2 1.2 %collective-permute-done.11.refs_3_ = f32[16,128]{1,0:T(8,128)S(1)} collective-permute-done((f32[16,128]{1,0:T(8,128)S(1)}, f32[16,128]{1,0:T(8,128)S(1)}, u32[]{:S(2)}, u32[]{:S(2)}) %collective-permute-start.11) | collective-permute-done | bytes 8224 | tf_op jit(solution)/shard_map/ppermute | solution.py:187
  26.4 0.1 collective-permute-done.10.refs_2_
  26.5 0.2 collective-permute-done.9.refs_1_
  26.6 0.8 %shard_map.71 = (f32[16,256]{1,0:T(8,128)}, f32[16,256]{1,0:T(8,128)}, f32[16,256]{1,0:T(8,128)}) custom-call(f32[16,256]{1,0:T(8,128)S(1)} %get-tuple-element.15.image_ref, f32[16,256]{1,0:T(8,128)S(1)} %copy-done, f32[16,128]{1,0:T(8,128)S(1)} %get-tuple-element.16.refs_0_, f32[16,128]{1,0:T(8,128)S(1)} %collective-permute-done.9.refs_1_, ...), custom_call_target="tpu_custom_call" | custom-call | tf_op jit(solution)/shard_map/pallas_call | solution.py:250
  (1 shorter events, 0.0 us)
Async XLA Ops:
  0.6 1.0 %copy-start = (f32[16,256]{1,0:T(8,128)S(1)}, f32[16,256]{1,0:T(8,128)}, u32[]{:S(2)}) copy-start(f32[16,256]{1,0:T(8,128)} %probes_ref.3) | copy-start | bytes 49156
  1.6 6.7 %collective-permute-start = (bf16[160,256]{1,0:T(8,128)(2,1)S(1)}, bf16[160,256]{1,0:T(8,128)(2,1)S(1)}, u32[]{:S(2)}, u32[]{:S(2)}) collective-permute-start(bf16[160,256]{1,0:T(8,128)(2,1)S(1)} %get-tuple-element.10.refs_0_), channel_id=1, source_target_pairs={{1,0},{0,1},{3,2},{2,3},{5,4},{4,5},{7,6},{6,7},{9,8},{8,9},{11,10... | collective-permute-start | bytes 245768 | tf_op jit(solution)/shard_map/ppermute | solution.py:172
  2.1 10.9 %copy-start.1 = (f32[256]{0:T(256)S(1)}, f32[256]{0:T(256)}, u32[]{:S(2)}) copy-start(f32[256]{0:T(256)} %param.6) | copy-start | bytes 3076
  2.1 7.4 %collective-permute-start.4 = (bf16[144,256]{1,0:T(8,128)(2,1)S(1)}, bf16[144,256]{1,0:T(8,128)(2,1)S(1)}, u32[]{:S(2)}, u32[]{:S(2)}) collective-permute-start(bf16[144,256]{1,0:T(8,128)(2,1)S(1)} %get-tuple-element.11.refs_2_.refs_5_), channel_id=1, source_target_pairs={{13,0},{12,1},{9,4},{8,5},{5,8},{4,9},{1,12},{0,13},{15,2},{14,3},... | collective-permute-start | bytes 221192 | tf_op jit(solution)/shard_map/ppermute | solution.py:187
  6.9 6.2 %collective-permute-start.3 = (bf16[144,256]{1,0:T(8,128)(2,1)S(1)}, bf16[144,256]{1,0:T(8,128)(2,1)S(1)}, u32[]{:S(2)}, u32[]{:S(2)}) collective-permute-start(bf16[144,256]{1,0:T(8,128)(2,1)S(1)} %get-tuple-element.11.refs_2_.refs_5_), channel_id=1, source_target_pairs={{9,0},{8,1},{13,4},{12,5},{1,8},{0,9},{5,12},{4,13},{11,2},{10,3},... | collective-permute-start | bytes 221192 | tf_op jit(solution)/shard_map/ppermute | solution.py:187
  6.9 7.8 %collective-permute-start.1 = (bf16[160,256]{1,0:T(8,128)(2,1)S(1)}, bf16[160,256]{1,0:T(8,128)(2,1)S(1)}, u32[]{:S(2)}, u32[]{:S(2)}) collective-permute-start(bf16[160,256]{1,0:T(8,128)(2,1)S(1)} %get-tuple-element.10.refs_0_), channel_id=1, source_target_pairs={{2,0},{0,2},{3,1},{1,3},{6,4},{4,6},{7,5},{5,7},{10,8},{8,10},{11,... | collective-permute-start | bytes 245768 | tf_op jit(solution)/shard_map/ppermute | solution.py:172
  8.4 6.3 %collective-permute-start.2 = (bf16[160,256]{1,0:T(8,128)(2,1)S(1)}, bf16[160,256]{1,0:T(8,128)(2,1)S(1)}, u32[]{:S(2)}, u32[]{:S(2)}) collective-permute-start(bf16[160,256]{1,0:T(8,128)(2,1)S(1)} %collective-permute-done.refs_1_), channel_id=1, source_target_pairs={{2,0},{0,2},{3,1},{1,3},{6,4},{4,6},{7,5},{5,7},{10,8},{8,10},{11,... | collective-permute-start | bytes 245768 | tf_op jit(solution)/shard_map/ppermute | solution.py:172
  8.9 5.8 %collective-permute-start.5 = (bf16[144,256]{1,0:T(8,128)(2,1)S(1)}, bf16[144,256]{1,0:T(8,128)(2,1)S(1)}, u32[]{:S(2)}, u32[]{:S(2)}) collective-permute-start(bf16[144,256]{1,0:T(8,128)(2,1)S(1)} %get-tuple-element.11.refs_2_.refs_5_), channel_id=1, source_target_pairs={{5,0},{4,1},{1,4},{0,5},{13,8},{12,9},{9,12},{8,13},{7,2},{6,3},{3... | collective-permute-start | bytes 221192 | tf_op jit(solution)/shard_map/ppermute | solution.py:187
  15.6 4.3 %collective-permute-start.8 = (f32[4,16,256]{2,1,0:T(8,128)S(1)}, f32[4,16,256]{2,1,0:T(8,128)S(1)}, u32[]{:S(2)}, u32[]{:S(2)}) collective-permute-start(f32[4,16,256]{2,1,0:T(8,128)S(1)} %shard_map.69.refs_5_), channel_id=1, source_target_pairs={{2,0},{3,1},{0,2},{1,3},{6,4},{7,5},{4,6},{5,7},{10,8},{11,9},{8,1... | collective-permute-start | bytes 196616 | tf_op jit(solution)/shard_map/ppermute | solution.py:172
  17.1 4.3 %collective-permute-start.7 = (f32[4,16,256]{2,1,0:T(8,128)S(1)}, f32[4,16,256]{2,1,0:T(8,128)S(1)}, u32[]{:S(2)}, u32[]{:S(2)}) collective-permute-start(f32[4,16,256]{2,1,0:T(8,128)S(1)} %shard_map.69.refs_5_), channel_id=1, source_target_pairs={{3,0},{2,1},{1,2},{0,3},{7,4},{6,5},{5,6},{4,7},{11,8},{10,9},{9,1... | collective-permute-start | bytes 196616 | tf_op jit(solution)/shard_map/ppermute | solution.py:172
  17.1 4.3 %collective-permute-start.6 = (f32[4,16,256]{2,1,0:T(8,128)S(1)}, f32[4,16,256]{2,1,0:T(8,128)S(1)}, u32[]{:S(2)}, u32[]{:S(2)}) collective-permute-start(f32[4,16,256]{2,1,0:T(8,128)S(1)} %shard_map.69.refs_5_), channel_id=1, source_target_pairs={{1,0},{0,1},{3,2},{2,3},{5,4},{4,5},{7,6},{6,7},{9,8},{8,9},{11,10... | collective-permute-start | bytes 196616 | tf_op jit(solution)/shard_map/ppermute | solution.py:172
  21.5 4.9 %collective-permute-start.11 = (f32[16,128]{1,0:T(8,128)S(1)}, f32[16,128]{1,0:T(8,128)S(1)}, u32[]{:S(2)}, u32[]{:S(2)}) collective-permute-start(f32[16,128]{1,0:T(8,128)S(1)} %get-tuple-element.16.refs_0_), channel_id=1, source_target_pairs={{13,0},{12,1},{9,4},{8,5},{5,8},{4,9},{1,12},{0,13},{15,2},{14,3},... | collective-permute-start | bytes 24584 | tf_op jit(solution)/shard_map/ppermute | solution.py:187
  22.5 4.0 %collective-permute-start.10 = (f32[16,128]{1,0:T(8,128)S(1)}, f32[16,128]{1,0:T(8,128)S(1)}, u32[]{:S(2)}, u32[]{:S(2)}) collective-permute-start(f32[16,128]{1,0:T(8,128)S(1)} %get-tuple-element.16.refs_0_), channel_id=1, source_target_pairs={{9,0},{8,1},{13,4},{12,5},{1,8},{0,9},{5,12},{4,13},{11,2},{10,3},... | collective-permute-start | bytes 24584 | tf_op jit(solution)/shard_map/ppermute | solution.py:187
  22.8 3.8 %collective-permute-start.9 = (f32[16,128]{1,0:T(8,128)S(1)}, f32[16,128]{1,0:T(8,128)S(1)}, u32[]{:S(2)}, u32[]{:S(2)}) collective-permute-start(f32[16,128]{1,0:T(8,128)S(1)} %get-tuple-element.16.refs_0_), channel_id=1, source_target_pairs={{5,0},{4,1},{1,4},{0,5},{13,8},{12,9},{9,12},{8,13},{7,2},{6,3},{3... | collective-permute-start | bytes 24584 | tf_op jit(solution)/shard_map/ppermute | solution.py:187

commit v22 on v19

--- a/solution.py
+++ b/solution.py
@@ -9,8 +9,8 @@
 LINE = ("blk",)
 DIRECT = 8
 VMEM = pltpu.CompilerParams(vmem_limit_bytes=40 * 1024 * 1024)
-PARTIALS, PARTIALS_BACK = (0, 1, 3, 2), (0, 1, 3, 2)
-SUMS = (0, 1, 2, 3)
+PARTIALS, PARTIALS_BACK = (0, 2, 3, 1), (0, 3, 1, 2)
+SUMS = (0, 1, 3, 2)
 HALF = 8
 
 
@@ -58,44 +58,76 @@
     for number, ref in enumerate(plane_refs):
         rows_ref[number] = rows_of(ref, feature_count)
     for number, ref in enumerate(line_refs):
-        columns_ref[number] = columns_of(ref[...], feature_count)
+        if len(ref.shape) == 2:
+            columns_ref[number] = columns_of(ref[...], feature_count)
+
+
+def add_columns(columns, probes, rows, totals):
+    exponents = [jnp.dot(columns, own, preferred_element_type=jnp.float32) for own in rows]
+    weights = [jnp.exp(value).astype(jnp.bfloat16) for value in exponents]
+    return [
+        total + jnp.dot(probes, value, preferred_element_type=jnp.float32)
+        for total, value in zip(totals, weights)
+    ]
+
+
+def paired_rows(rows_ref, plane_refs, feature_count):
+    rows = [rows_ref[number] for number in range(2)]
+    rows += [rows_of(ref, feature_count) for ref in plane_refs]
+    return [jnp.concatenate(rows[place : place + 2], axis=1) for place in range(0, len(rows), 2)]
+
+
+def paired_totals(ref):
+    totals = [ref[number] for number in range(ref.shape[0])]
+    return [jnp.concatenate(totals[place : place + 2], axis=1) for place in range(0, len(totals), 2)]
+
+
+def store_totals(totals, ref):
+    width = ref.shape[2]
+    for number in range(ref.shape[0]):
+        place = number % 2 * width
+        ref[number] = totals[number // 2][:, place : place + width]
 
 
 def image_kernel(feature_count, plane_count, *refs):
     rows_ref, start_ref = refs[:2]
-    plane_refs = refs[2:plane_count]
     columns_ref, *line_refs = refs[plane_count:-1]
     partial_ref = refs[-1]
-    rows = [rows_ref[number] for number in range(2)]
-    rows += [rows_of(ref, feature_count) for ref in plane_refs]
-    totals = [start_ref[...]]
-    totals += [jnp.zeros(start_ref.shape, jnp.float32)] * (plane_count - 1)
-
-    def add_columns(columns, probes, totals):
-        result = []
-        for own, total in zip(rows, totals):
-            exponent = jnp.dot(columns, own, preferred_element_type=jnp.float32)
-            weights = jnp.exp(exponent).astype(jnp.bfloat16)
-            result.append(total + jnp.dot(probes, weights, preferred_element_type=jnp.float32))
-        return result
-
+    rows = paired_rows(rows_ref, refs[2:plane_count], feature_count)
+    start = start_ref[...]
+    none = jnp.zeros_like(start)
+    totals = [jnp.concatenate([start, none], axis=1)]
+    totals += [jnp.concatenate([none, none], axis=1)] * (len(rows) - 1)
     if len(line_refs[0].shape) == 2:
-        *early, late = [ref[...] for ref in line_refs]
-        columns = [columns_ref[number] for number in range(len(early))]
-        columns = jnp.concatenate(columns + [columns_of(late, feature_count)], axis=0)
-        probes = [block[feature_count:, :] for block in early + [late]]
-        totals = add_columns(columns, jnp.concatenate(probes, axis=1), totals)
+        columns = [columns_ref[number] for number in range(len(line_refs))]
+        probes = [ref[feature_count:, :] for ref in line_refs]
+        totals = add_columns(
+            jnp.concatenate(columns, axis=0), jnp.concatenate(probes, axis=1), rows, totals
+        )
     else:
 
         def add_block(number, totals):
             block = line_refs[0][number]
             return add_columns(
-                columns_of(block, feature_count), block[feature_count:, :], totals
+                columns_of(block, feature_count), block[feature_count:, :], rows, totals
             )
 
         totals = lax.fori_loop(0, line_refs[0].shape[0], add_block, totals)
-    for number, total in enumerate(totals):
-        partial_ref[number] = total
+    store_totals(totals, partial_ref)
+
+
+def late_kernel(feature_count, plane_count, *refs):
+    rows_ref, start_ref = refs[:2]
+    block_ref, partial_ref = refs[plane_count:]
+    rows = paired_rows(rows_ref, refs[2:plane_count], feature_count)
+    block = block_ref[...]
+    totals = add_columns(
+        columns_of(block, feature_count),
+        block[feature_count:, :],
+        rows,
+        paired_totals(start_ref),
+    )
+    store_totals(totals, partial_ref)
 
 
 def combine_kernel(feature_count, plane_count, *refs):
@@ -207,16 +239,16 @@
         lines = along_line(line, line_count, plane_shape[1])
         planes = plane_blocks(plane, plane_shape)
         if len(lines) > 1:
-            early, late = lines[:1] + lines[2:], lines[1]
+            early, late = lines[:1] + lines[:1:-1], lines[1:2]
         else:
-            early, late = [], lines[0]
+            early, late = lines, []
         depth = feature_count + 2 * HALF
         work = plane_count * width * width
         rows, columns, start = pl.pallas_call(
             lambda *refs: prepare_kernel(feature_count, 2, *refs),
             out_shape=(
                 jax.ShapeDtypeStruct((2, depth, width), jnp.bfloat16),
-                jax.ShapeDtypeStruct((max(len(early), 1), width, depth), jnp.bfloat16),
+                jax.ShapeDtypeStruct((len(early), width, depth), jnp.bfloat16),
                 jax.ShapeDtypeStruct(probes.shape, jnp.float32),
             ),
             compiler_params=VMEM,
@@ -224,11 +256,18 @@
                 flops=6 * work * depth, bytes_accessed=4 * plane_count * width, transcendentals=3 * work
             ),
         )(*planes[:2], *early, noise_var[None, :], probes)
+        shape = jax.ShapeDtypeStruct((plane_count, probe_count, width), jnp.float32)
         partial = pl.pallas_call(
             lambda *refs: image_kernel(feature_count, plane_count, *refs),
-            out_shape=jax.ShapeDtypeStruct((plane_count, probe_count, width), jnp.float32),
-            compiler_params=VMEM,
-        )(rows, start, *planes[2:], columns, *early, late)
+            out_shape=shape,
+            compiler_params=VMEM,
+        )(rows, start, *planes[2:], columns, *early)
+        for block in late:
+            partial = pl.pallas_call(
+                lambda *refs: late_kernel(feature_count, plane_count, *refs),
+                out_shape=shape,
+                compiler_params=VMEM,
+            )(rows, partial, *planes[2:], block)
         partials = everywhere(partial, PLANE, plane_count)
         image, sums = pl.pallas_call(
             lambda *refs: combine_kernel(feature_count, plane_count, *refs),

time: 28.4 us -> 27.8 us (0.979)
  Pallas kernels: 2.86 us -> 2.32 us
    pallas_call x1, Pallas kernels: 1.77 us -> 0.74 us  [local(): pl.pallas_call(lambda *refs: image_kernel(feature_count, plane_count, *re...]
    pallas_call x0 -> x1, Pallas kernels: none -> 0.5 us  [local(): pl.pallas_call(lambda *refs: late_kernel(feature_count, plane_count, *ref...]
  transfers between devices with their start and end apart: 12 -> 12, of which waited for: 8 -> 7; matrix products, arithmetic and copies ran while one was open for 0% -> 0% of each run, Pallas kernels for 1% -> 3%
where the time goes in v22:
time: 27.8 us; the launch traced here: 27.6 us
  starting transfers between devices  13.1 us (47%)
  waiting for transfers between devices  10.5 us (38%)
  Pallas kernels  2.32 us (8%)
  other arithmetic  0.93 us (3%)
  between operations  0.7 us (3%)
    ppermute x6, starting transfers between devices, along_line(): blocks.append(lax.ppermute(value, LINE + ('sub',), pairs))  8.42 us
    ppermute x6, waiting for transfers between devices, along_line(): blocks.append(lax.ppermute(value, LINE + ('sub',), pairs))  6.93 us
    ppermute x6, starting transfers between devices, everywhere(): lax.ppermute(value, axes, [(source_of(i, step, count), i) for i in range(...  4.69 us
    ppermute x6, waiting for transfers between devices, everywhere(): lax.ppermute(value, axes, [(source_of(i, step, count), i) for i in range(...  3.61 us
    convert_element_type x1, other arithmetic, local(): (features.astype(jnp.float32) / lengthscale[:, None]).astype(jnp.bfloat16)  0.93 us
    pallas_call x1, Pallas kernels, local(): pl.pallas_call(finish_kernel, out_shape=outs, compiler_params=VMEM)  0.77 us
    pallas_call x1, Pallas kernels, local(): pl.pallas_call(lambda *refs: image_kernel(feature_count, plane_count, *re...  0.74 us
  transfers between devices with their start and end apart: 12, of which 7 were waited for; matrix products, arithmetic and copies ran while one was open for 0% of the time, Pallas kernels for 3%

profile of v22, /device:TPU:0, one launch (start us, length us, event | category | flops | bytes accessed | tf_op | source)
XLA Modules:
  0.0 27.6 jit_solution(14845842492178525393)
XLA Ops:
  0.6 0.0 copy-start
  0.6 0.9 %divide_convert_fusion.scaled_ref = bf16[128,256]{1,0:T(8,128)(2,1)S(1)} fusion(bf16[128,256]{1,0:T(8,128)(2,1)} %param.4, f32[128]{0:T(128)} %param.5), kind=kLoop, calls=%fused_computation | loop fusion | flops 98304 | bytes 131584 | tf_op jit(solution)/shard_map/convert_element_type | solution.py:230
  1.6 0.0 copy-done
  1.6 0.5 %collective-permute-start = (bf16[160,256]{1,0:T(8,128)(2,1)S(1)}, bf16[160,256]{1,0:T(8,128)(2,1)S(1)}, u32[]{:S(2)}, u32[]{:S(2)}) collective-permute-start(bf16[160,256]{1,0:T(8,128)(2,1)S(1)} %get-tuple-element.10.refs_0_), channel_id=1, source_target_pairs={{1,0},{0,1},{3,2},{2,3},{5,4},{4,5},{7,6},{6,7},{9,8},{8,9},{11,10... | collective-permute-start | bytes 245768 | tf_op jit(solution)/shard_map/ppermute | solution.py:196
  2.1 0.0 copy-start.1
  2.1 4.7 %collective-permute-start.3 = (bf16[144,256]{1,0:T(8,128)(2,1)S(1)}, bf16[144,256]{1,0:T(8,128)(2,1)S(1)}, u32[]{:S(2)}, u32[]{:S(2)}) collective-permute-start(bf16[144,256]{1,0:T(8,128)(2,1)S(1)} %get-tuple-element.11.refs_2_.refs_5_), channel_id=1, source_target_pairs={{13,0},{12,1},{9,4},{8,5},{5,8},{4,9},{1,12},{0,13},{15,2},{14,3},... | collective-permute-start | bytes 221192 | tf_op jit(solution)/shard_map/ppermute | solution.py:211
  6.9 0.0 collective-permute-start.4
  6.9 1.5 %collective-permute-start.1 = (bf16[160,256]{1,0:T(8,128)(2,1)S(1)}, bf16[160,256]{1,0:T(8,128)(2,1)S(1)}, u32[]{:S(2)}, u32[]{:S(2)}) collective-permute-start(bf16[160,256]{1,0:T(8,128)(2,1)S(1)} %get-tuple-element.10.refs_0_), channel_id=1, source_target_pairs={{2,0},{0,2},{3,1},{1,3},{6,4},{4,6},{7,5},{5,7},{10,8},{8,10},{11,... | collective-permute-start | bytes 245768 | tf_op jit(solution)/shard_map/ppermute | solution.py:196
  8.4 0.0 collective-permute-done.refs_1_
  8.4 0.5 %collective-permute-start.2 = (bf16[160,256]{1,0:T(8,128)(2,1)S(1)}, bf16[160,256]{1,0:T(8,128)(2,1)S(1)}, u32[]{:S(2)}, u32[]{:S(2)}) collective-permute-start(bf16[160,256]{1,0:T(8,128)(2,1)S(1)} %collective-permute-done.refs_1_), channel_id=1, source_target_pairs={{2,0},{0,2},{3,1},{1,3},{6,4},{4,6},{7,5},{5,7},{10,8},{8,10},{11,... | collective-permute-start | bytes 245768 | tf_op jit(solution)/shard_map/ppermute | solution.py:196
  8.9 0.0 collective-permute-start.5
  8.9 0.6 %collective-permute-done.3.refs_3_.refs_6_ = bf16[144,256]{1,0:T(8,128)(2,1)S(1)} collective-permute-done((bf16[144,256]{1,0:T(8,128)(2,1)S(1)}, bf16[144,256]{1,0:T(8,128)(2,1)S(1)}, u32[]{:S(2)}, u32[]{:S(2)}) %collective-permute-start.3) | collective-permute-done | bytes 73760 | tf_op jit(solution)/shard_map/ppermute | solution.py:211
  9.5 3.6 %collective-permute-done.4.refs_4_.refs_7_ = bf16[144,256]{1,0:T(8,128)(2,1)S(1)} collective-permute-done((bf16[144,256]{1,0:T(8,128)(2,1)S(1)}, bf16[144,256]{1,0:T(8,128)(2,1)S(1)}, u32[]{:S(2)}, u32[]{:S(2)}) %collective-permute-start.4) | collective-permute-done | bytes 73760 | tf_op jit(solution)/shard_map/ppermute | solution.py:211
  13.1 0.0 copy-done.1
  13.1 0.2 shard_map.68
  13.3 0.0 collective-permute-done.1.refs_2_
  13.3 0.0 collective-permute-done.2.refs_3_
  13.3 0.7 %shard_map.69.refs_1_ = f32[4,16,256]{2,1,0:T(8,128)S(1)} custom-call(bf16[2,144,256]{2,1,0:T(8,128)(2,1)S(1)} %get-tuple-element.12.refs_0_, f32[16,256]{1,0:T(8,128)S(1)} %get-tuple-element.13.refs_1_, bf16[160,256]{1,0:T(8,128)(2,1)S(1)} %collective-permute-done.1.refs_2_, bf16[160,256]{1,0:T(8,128)(2,1)S(1)} %collective-permute-done.2.refs_3_, ...), custom_call_target="tpu_custom_call" | custom-call | tf_op jit(solution)/shard_map/pallas_call | solution.py:260
  14.0 0.6 %collective-permute-done.5.refs_4_ = bf16[144,256]{1,0:T(8,128)(2,1)S(1)} collective-permute-done((bf16[144,256]{1,0:T(8,128)(2,1)S(1)}, bf16[144,256]{1,0:T(8,128)(2,1)S(1)}, u32[]{:S(2)}, u32[]{:S(2)}) %collective-permute-start.5) | collective-permute-done | bytes 73760 | tf_op jit(solution)/shard_map/ppermute | solution.py:211
  14.6 0.5 %shard_map.70.refs_5_ = f32[4,16,256]{2,1,0:T(8,128)S(1)} custom-call(bf16[2,144,256]{2,1,0:T(8,128)(2,1)S(1)} %get-tuple-element.12.refs_0_, f32[4,16,256]{2,1,0:T(8,128)S(1)} %shard_map.69.refs_1_, bf16[160,256]{1,0:T(8,128)(2,1)S(1)} %collective-permute-done.1.refs_2_, bf16[160,256]{1,0:T(8,128)(2,1)S(1)} %collective-permute-done.2.refs_3_, ...), custom_call_target="tpu_custom_call" | custom-call | tf_op jit(solution)/shard_map/pallas_call | solution.py:266
  15.1 1.5 %collective-permute-start.6 = (f32[4,16,256]{2,1,0:T(8,128)S(1)}, f32[4,16,256]{2,1,0:T(8,128)S(1)}, u32[]{:S(2)}, u32[]{:S(2)}) collective-permute-start(f32[4,16,256]{2,1,0:T(8,128)S(1)} %shard_map.70.refs_5_), channel_id=1, source_target_pairs={{2,0},{3,1},{0,2},{1,3},{6,4},{7,5},{4,6},{5,7},{10,8},{11,9},{8,1... | collective-permute-start | bytes 196616 | tf_op jit(solution)/shard_map/ppermute | solution.py:196
  16.6 0.0 collective-permute-start.7
  16.6 0.6 %collective-permute-start.8 = (f32[4,16,256]{2,1,0:T(8,128)S(1)}, f32[4,16,256]{2,1,0:T(8,128)S(1)}, u32[]{:S(2)}, u32[]{:S(2)}) collective-permute-start(f32[4,16,256]{2,1,0:T(8,128)S(1)} %shard_map.70.refs_5_), channel_id=1, source_target_pairs={{1,0},{0,1},{3,2},{2,3},{5,4},{4,5},{7,6},{6,7},{9,8},{8,9},{11,10... | collective-permute-start | bytes 196616 | tf_op jit(solution)/shard_map/ppermute | solution.py:196
  17.3 2.1 %collective-permute-done.6.refs_6_ = f32[4,16,256]{2,1,0:T(8,128)S(1)} collective-permute-done((f32[4,16,256]{2,1,0:T(8,128)S(1)}, f32[4,16,256]{2,1,0:T(8,128)S(1)}, u32[]{:S(2)}, u32[]{:S(2)}) %collective-permute-start.6) | collective-permute-done | bytes 65568 | tf_op jit(solution)/shard_map/ppermute | solution.py:196
  19.4 1.5 %collective-permute-done.7.refs_7_ = f32[4,16,256]{2,1,0:T(8,128)S(1)} collective-permute-done((f32[4,16,256]{2,1,0:T(8,128)S(1)}, f32[4,16,256]{2,1,0:T(8,128)S(1)}, u32[]{:S(2)}, u32[]{:S(2)}) %collective-permute-start.7) | collective-permute-done | bytes 65568 | tf_op jit(solution)/shard_map/ppermute | solution.py:196
  20.9 0.0 collective-permute-done.8.refs_8_
  20.9 0.1 shard_map.71
  21.0 1.9 %collective-permute-start.10 = (f32[16,128]{1,0:T(8,128)S(1)}, f32[16,128]{1,0:T(8,128)S(1)}, u32[]{:S(2)}, u32[]{:S(2)}) collective-permute-start(f32[16,128]{1,0:T(8,128)S(1)} %get-tuple-element.16.refs_0_), channel_id=1, source_target_pairs={{13,0},{12,1},{9,4},{8,5},{5,8},{4,9},{1,12},{0,13},{15,2},{14,3},... | collective-permute-start | bytes 24584 | tf_op jit(solution)/shard_map/ppermute | solution.py:211
  22.9 0.0 collective-permute-start.11
  22.9 1.8 %collective-permute-start.9 = (f32[16,128]{1,0:T(8,128)S(1)}, f32[16,128]{1,0:T(8,128)S(1)}, u32[]{:S(2)}, u32[]{:S(2)}) collective-permute-start(f32[16,128]{1,0:T(8,128)S(1)} %get-tuple-element.16.refs_0_), channel_id=1, source_target_pairs={{5,0},{4,1},{1,4},{0,5},{13,8},{12,9},{9,12},{8,13},{7,2},{6,3},{3... | collective-permute-start | bytes 24584 | tf_op jit(solution)/shard_map/ppermute | solution.py:211
  24.7 1.2 %collective-permute-done.10.refs_2_ = f32[16,128]{1,0:T(8,128)S(1)} collective-permute-done((f32[16,128]{1,0:T(8,128)S(1)}, f32[16,128]{1,0:T(8,128)S(1)}, u32[]{:S(2)}, u32[]{:S(2)}) %collective-permute-start.10) | collective-permute-done | bytes 8224 | tf_op jit(solution)/shard_map/ppermute | solution.py:211
  25.9 1.0 %collective-permute-done.11.refs_3_ = f32[16,128]{1,0:T(8,128)S(1)} collective-permute-done((f32[16,128]{1,0:T(8,128)S(1)}, f32[16,128]{1,0:T(8,128)S(1)}, u32[]{:S(2)}, u32[]{:S(2)}) %collective-permute-start.11) | collective-permute-done | bytes 8224 | tf_op jit(solution)/shard_map/ppermute | solution.py:211
  26.8 0.0 collective-permute-done.9.refs_1_
  26.8 0.8 %shard_map.72 = (f32[16,256]{1,0:T(8,128)}, f32[16,256]{1,0:T(8,128)}, f32[16,256]{1,0:T(8,128)}) custom-call(f32[16,256]{1,0:T(8,128)S(1)} %get-tuple-element.15.image_ref, f32[16,256]{1,0:T(8,128)S(1)} %copy-done, f32[16,128]{1,0:T(8,128)S(1)} %get-tuple-element.16.refs_0_, f32[16,128]{1,0:T(8,128)S(1)} %collective-permute-done.9.refs_1_, ...), custom_call_target="tpu_custom_call" | custom-call | tf_op jit(solution)/shard_map/pallas_call | solution.py:281
  (1 shorter events, 0.0 us)
Async XLA Ops:
  0.6 1.0 %copy-start = (f32[16,256]{1,0:T(8,128)S(1)}, f32[16,256]{1,0:T(8,128)}, u32[]{:S(2)}) copy-start(f32[16,256]{1,0:T(8,128)} %probes_ref.3) | copy-start | bytes 49156
  1.6 6.7 %collective-permute-start = (bf16[160,256]{1,0:T(8,128)(2,1)S(1)}, bf16[160,256]{1,0:T(8,128)(2,1)S(1)}, u32[]{:S(2)}, u32[]{:S(2)}) collective-permute-start(bf16[160,256]{1,0:T(8,128)(2,1)S(1)} %get-tuple-element.10.refs_0_), channel_id=1, source_target_pairs={{1,0},{0,1},{3,2},{2,3},{5,4},{4,5},{7,6},{6,7},{9,8},{8,9},{11,10... | collective-permute-start | bytes 245768 | tf_op jit(solution)/shard_map/ppermute | solution.py:196
  2.1 10.9 %copy-start.1 = (f32[256]{0:T(256)S(1)}, f32[256]{0:T(256)}, u32[]{:S(2)}) copy-start(f32[256]{0:T(256)} %param.6) | copy-start | bytes 3076
  2.1 7.4 %collective-permute-start.3 = (bf16[144,256]{1,0:T(8,128)(2,1)S(1)}, bf16[144,256]{1,0:T(8,128)(2,1)S(1)}, u32[]{:S(2)}, u32[]{:S(2)}) collective-permute-start(bf16[144,256]{1,0:T(8,128)(2,1)S(1)} %get-tuple-element.11.refs_2_.refs_5_), channel_id=1, source_target_pairs={{13,0},{12,1},{9,4},{8,5},{5,8},{4,9},{1,12},{0,13},{15,2},{14,3},... | collective-permute-start | bytes 221192 | tf_op jit(solution)/shard_map/ppermute | solution.py:211
  6.9 6.2 %collective-permute-start.4 = (bf16[144,256]{1,0:T(8,128)(2,1)S(1)}, bf16[144,256]{1,0:T(8,128)(2,1)S(1)}, u32[]{:S(2)}, u32[]{:S(2)}) collective-permute-start(bf16[144,256]{1,0:T(8,128)(2,1)S(1)} %get-tuple-element.11.refs_2_.refs_5_), channel_id=1, source_target_pairs={{9,0},{8,1},{13,4},{12,5},{1,8},{0,9},{5,12},{4,13},{11,2},{10,3},... | collective-permute-start | bytes 221192 | tf_op jit(solution)/shard_map/ppermute | solution.py:211
  6.9 6.4 %collective-permute-start.1 = (bf16[160,256]{1,0:T(8,128)(2,1)S(1)}, bf16[160,256]{1,0:T(8,128)(2,1)S(1)}, u32[]{:S(2)}, u32[]{:S(2)}) collective-permute-start(bf16[160,256]{1,0:T(8,128)(2,1)S(1)} %get-tuple-element.10.refs_0_), channel_id=1, source_target_pairs={{2,0},{0,2},{3,1},{1,3},{6,4},{4,6},{7,5},{5,7},{10,8},{8,10},{11,... | collective-permute-start | bytes 245768 | tf_op jit(solution)/shard_map/ppermute | solution.py:196
  8.4 4.9 %collective-permute-start.2 = (bf16[160,256]{1,0:T(8,128)(2,1)S(1)}, bf16[160,256]{1,0:T(8,128)(2,1)S(1)}, u32[]{:S(2)}, u32[]{:S(2)}) collective-permute-start(bf16[160,256]{1,0:T(8,128)(2,1)S(1)} %collective-permute-done.refs_1_), channel_id=1, source_target_pairs={{2,0},{0,2},{3,1},{1,3},{6,4},{4,6},{7,5},{5,7},{10,8},{8,10},{11,... | collective-permute-start | bytes 245768 | tf_op jit(solution)/shard_map/ppermute | solution.py:196
  8.9 5.8 %collective-permute-start.5 = (bf16[144,256]{1,0:T(8,128)(2,1)S(1)}, bf16[144,256]{1,0:T(8,128)(2,1)S(1)}, u32[]{:S(2)}, u32[]{:S(2)}) collective-permute-start(bf16[144,256]{1,0:T(8,128)(2,1)S(1)} %get-tuple-element.11.refs_2_.refs_5_), channel_id=1, source_target_pairs={{5,0},{4,1},{1,4},{0,5},{13,8},{12,9},{9,12},{8,13},{7,2},{6,3},{3... | collective-permute-start | bytes 221192 | tf_op jit(solution)/shard_map/ppermute | solution.py:211
  15.1 4.3 %collective-permute-start.6 = (f32[4,16,256]{2,1,0:T(8,128)S(1)}, f32[4,16,256]{2,1,0:T(8,128)S(1)}, u32[]{:S(2)}, u32[]{:S(2)}) collective-permute-start(f32[4,16,256]{2,1,0:T(8,128)S(1)} %shard_map.70.refs_5_), channel_id=1, source_target_pairs={{2,0},{3,1},{0,2},{1,3},{6,4},{7,5},{4,6},{5,7},{10,8},{11,9},{8,1... | collective-permute-start | bytes 196616 | tf_op jit(solution)/shard_map/ppermute | solution.py:196
  16.6 4.3 %collective-permute-start.7 = (f32[4,16,256]{2,1,0:T(8,128)S(1)}, f32[4,16,256]{2,1,0:T(8,128)S(1)}, u32[]{:S(2)}, u32[]{:S(2)}) collective-permute-start(f32[4,16,256]{2,1,0:T(8,128)S(1)} %shard_map.70.refs_5_), channel_id=1, source_target_pairs={{3,0},{2,1},{1,2},{0,3},{7,4},{6,5},{5,6},{4,7},{11,8},{10,9},{9,1... | collective-permute-start | bytes 196616 | tf_op jit(solution)/shard_map/ppermute | solution.py:196
  16.6 4.3 %collective-permute-start.8 = (f32[4,16,256]{2,1,0:T(8,128)S(1)}, f32[4,16,256]{2,1,0:T(8,128)S(1)}, u32[]{:S(2)}, u32[]{:S(2)}) collective-permute-start(f32[4,16,256]{2,1,0:T(8,128)S(1)} %shard_map.70.refs_5_), channel_id=1, source_target_pairs={{1,0},{0,1},{3,2},{2,3},{5,4},{4,5},{7,6},{6,7},{9,8},{8,9},{11,10... | collective-permute-start | bytes 196616 | tf_op jit(solution)/shard_map/ppermute | solution.py:196
  21.0 4.9 %collective-permute-start.10 = (f32[16,128]{1,0:T(8,128)S(1)}, f32[16,128]{1,0:T(8,128)S(1)}, u32[]{:S(2)}, u32[]{:S(2)}) collective-permute-start(f32[16,128]{1,0:T(8,128)S(1)} %get-tuple-element.16.refs_0_), channel_id=1, source_target_pairs={{13,0},{12,1},{9,4},{8,5},{5,8},{4,9},{1,12},{0,13},{15,2},{14,3},... | collective-permute-start | bytes 24584 | tf_op jit(solution)/shard_map/ppermute | solution.py:211
  22.9 4.0 %collective-permute-start.11 = (f32[16,128]{1,0:T(8,128)S(1)}, f32[16,128]{1,0:T(8,128)S(1)}, u32[]{:S(2)}, u32[]{:S(2)}) collective-permute-start(f32[16,128]{1,0:T(8,128)S(1)} %get-tuple-element.16.refs_0_), channel_id=1, source_target_pairs={{9,0},{8,1},{13,4},{12,5},{1,8},{0,9},{5,12},{4,13},{11,2},{10,3},... | collective-permute-start | bytes 24584 | tf_op jit(solution)/shard_map/ppermute | solution.py:211
  22.9 4.0 %collective-permute-start.9 = (f32[16,128]{1,0:T(8,128)S(1)}, f32[16,128]{1,0:T(8,128)S(1)}, u32[]{:S(2)}, u32[]{:S(2)}) collective-permute-start(f32[16,128]{1,0:T(8,128)S(1)} %get-tuple-element.16.refs_0_), channel_id=1, source_target_pairs={{5,0},{4,1},{1,4},{0,5},{13,8},{12,9},{9,12},{8,13},{7,2},{6,3},{3... | collective-permute-start | bytes 24584 | tf_op jit(solution)/shard_map/ppermute | solution.py:211

commit v23 on v20

--- a/solution.py
+++ b/solution.py
@@ -76,12 +76,17 @@
     totals = [jnp.zeros((start.shape[0], own.shape[1]), jnp.float32) for own in rows]
 
     def add_columns(columns, probes, totals):
-        exponent = [jnp.dot(columns, own, preferred_element_type=jnp.float32) for own in rows]
-        weights = [jnp.exp(value).astype(jnp.bfloat16) for value in exponent]
-        return [
-            total + jnp.dot(probes, value, preferred_element_type=jnp.float32)
-            for total, value in zip(totals, weights)
-        ]
+        height = min(512, columns.shape[0])
+        for place in range(0, columns.shape[0], height):
+            part = columns[place : place + height, :]
+            part_probes = probes[:, place : place + height]
+            exponents = [jnp.dot(part, own, preferred_element_type=jnp.float32) for own in rows]
+            weights = [jnp.exp(value).astype(jnp.bfloat16) for value in exponents]
+            totals = [
+                total + jnp.dot(part_probes, value, preferred_element_type=jnp.float32)
+                for total, value in zip(totals, weights)
+            ]
+        return totals
 
     if len(line_refs[0].shape) == 2:
         *early, late = [ref[...] for ref in line_refs]
@@ -132,7 +137,8 @@
 
 
 def finish_kernel(image_ref, probes_ref, *refs):
-    *sums_refs, solution_ref, residual_ref, direction_ref = refs
+    *sums_refs, solution_hbm, residual_hbm, direction_hbm = refs[:-4]
+    solution_ref, residual_ref, direction_ref, semaphores = refs[-4:]
     sums = jnp.zeros(sums_refs[0].shape[-2:], jnp.float32)
     for ref in sums_refs:
         value = ref[...]
@@ -141,10 +147,25 @@
     alpha = start_norms / curvature
     new_norms = start_norms - 2.0 * alpha * curvature + alpha * alpha * image_norms
     probes = probes_ref[...]
+    copies = [
+        pltpu.make_async_copy(source, target, semaphores.at[number])
+        for number, (source, target) in enumerate(
+            (
+                (solution_ref, solution_hbm),
+                (residual_ref, residual_hbm),
+                (direction_ref, direction_hbm),
+            )
+        )
+    ]
+    solution_ref[...] = alpha * probes
+    copies[0].start()
     residual = probes - alpha * image_ref[...]
-    solution_ref[...] = alpha * probes
     residual_ref[...] = residual
+    copies[1].start()
     direction_ref[...] = residual + (new_norms / start_norms) * probes
+    copies[2].start()
+    for copy in copies:
+        copy.wait()
 
 
 def paired(count):
@@ -245,7 +266,16 @@
             compiler_params=VMEM,
         )(*planes, probes, *in_order(partials, PARTIALS))
         outs = (jax.ShapeDtypeStruct(probes.shape, jnp.float32),) * 3
-        return pl.pallas_call(finish_kernel, out_shape=outs, compiler_params=VMEM)(
+        return pl.pallas_call(
+            finish_kernel,
+            out_shape=outs,
+            out_specs=(pl.BlockSpec(memory_space=pl.ANY),) * 3,
+            scratch_shapes=[
+                *[pltpu.VMEM(probes.shape, jnp.float32)] * 3,
+                pltpu.SemaphoreType.DMA((3,)),
+            ],
+            compiler_params=VMEM,
+        )(
             image, probes, *in_order(along_line(sums, line_count, plane_shape[1]), SUMS)
         )
 

time: 27.6 us -> 27.6 us (level)
  no operation moved by 1% of the time
where the time goes in v23:
time: 27.6 us; the launch traced here: 27.4 us
  starting transfers between devices  13.1 us (47%)
  waiting for transfers between devices  10.6 us (38%)
  Pallas kernels  2.08 us (8%)
  other arithmetic  0.93 us (3%)
  between operations  0.68 us (2%)
    ppermute x6, starting transfers between devices, along_line(): blocks.append(lax.ppermute(value, LINE + ('sub',), pairs))  8.42 us
    ppermute x6, waiting for transfers between devices, along_line(): blocks.append(lax.ppermute(value, LINE + ('sub',), pairs))  6.99 us
    ppermute x6, starting transfers between devices, everywhere(): lax.ppermute(value, axes, [(source_of(i, step, count), i) for i in range(...  4.69 us
    ppermute x6, waiting for transfers between devices, everywhere(): lax.ppermute(value, axes, [(source_of(i, step, count), i) for i in range(...  3.61 us
    pallas_call x1, Pallas kernels, local(): pl.pallas_call(lambda *refs: image_kernel(feature_count, plane_count, *re...  0.97 us
    convert_element_type x1, other arithmetic, local(): (features.astype(jnp.float32) / lengthscale[:, None]).astype(jnp.bfloat16)  0.93 us
    pallas_call x1, Pallas kernels, local(): pl.pallas_call(finish_kernel, out_shape=outs, out_specs=(pl.BlockSpec(mem...  0.79 us
  transfers between devices with their start and end apart: 12, of which 8 were waited for; matrix products, arithmetic and copies ran while one was open for 0% of the time, Pallas kernels for 1%

profile of v23, /device:TPU:0, one launch (start us, length us, event | category | flops | bytes accessed | tf_op | source)
XLA Modules:
  0.0 27.4 jit_solution(11086521817118775382)
XLA Ops:
  0.6 0.0 copy-start
  0.6 0.9 %divide_convert_fusion.scaled_ref = bf16[128,256]{1,0:T(8,128)(2,1)S(1)} fusion(bf16[128,256]{1,0:T(8,128)(2,1)} %param.4, f32[128]{0:T(128)} %param.5), kind=kLoop, calls=%fused_computation | loop fusion | flops 98304 | bytes 131584 | tf_op jit(solution)/shard_map/convert_element_type | solution.py:225
  1.6 0.0 copy-done
  1.6 0.5 %collective-permute-start = (bf16[160,256]{1,0:T(8,128)(2,1)S(1)}, bf16[160,256]{1,0:T(8,128)(2,1)S(1)}, u32[]{:S(2)}, u32[]{:S(2)}) collective-permute-start(bf16[160,256]{1,0:T(8,128)(2,1)S(1)} %get-tuple-element.10.refs_0_), channel_id=1, source_target_pairs={{1,0},{0,1},{3,2},{2,3},{5,4},{4,5},{7,6},{6,7},{9,8},{8,9},{11,10... | collective-permute-start | bytes 245768 | tf_op jit(solution)/shard_map/ppermute | solution.py:191
  2.1 0.0 copy-start.1
  2.1 4.7 %collective-permute-start.4 = (bf16[144,256]{1,0:T(8,128)(2,1)S(1)}, bf16[144,256]{1,0:T(8,128)(2,1)S(1)}, u32[]{:S(2)}, u32[]{:S(2)}) collective-permute-start(bf16[144,256]{1,0:T(8,128)(2,1)S(1)} %get-tuple-element.11.refs_2_.refs_5_), channel_id=1, source_target_pairs={{13,0},{12,1},{9,4},{8,5},{5,8},{4,9},{1,12},{0,13},{15,2},{14,3},... | collective-permute-start | bytes 221192 | tf_op jit(solution)/shard_map/ppermute | solution.py:206
  6.9 0.0 collective-permute-start.3
  6.9 1.5 %collective-permute-start.1 = (bf16[160,256]{1,0:T(8,128)(2,1)S(1)}, bf16[160,256]{1,0:T(8,128)(2,1)S(1)}, u32[]{:S(2)}, u32[]{:S(2)}) collective-permute-start(bf16[160,256]{1,0:T(8,128)(2,1)S(1)} %get-tuple-element.10.refs_0_), channel_id=1, source_target_pairs={{2,0},{0,2},{3,1},{1,3},{6,4},{4,6},{7,5},{5,7},{10,8},{8,10},{11,... | collective-permute-start | bytes 245768 | tf_op jit(solution)/shard_map/ppermute | solution.py:191
  8.4 0.0 collective-permute-done.refs_1_
  8.4 0.5 %collective-permute-start.2 = (bf16[160,256]{1,0:T(8,128)(2,1)S(1)}, bf16[160,256]{1,0:T(8,128)(2,1)S(1)}, u32[]{:S(2)}, u32[]{:S(2)}) collective-permute-start(bf16[160,256]{1,0:T(8,128)(2,1)S(1)} %collective-permute-done.refs_1_), channel_id=1, source_target_pairs={{2,0},{0,2},{3,1},{1,3},{6,4},{4,6},{7,5},{5,7},{10,8},{8,10},{11,... | collective-permute-start | bytes 245768 | tf_op jit(solution)/shard_map/ppermute | solution.py:191
  8.9 0.0 collective-permute-start.5
  8.9 0.6 %collective-permute-done.4.refs_4_.refs_7_ = bf16[144,256]{1,0:T(8,128)(2,1)S(1)} collective-permute-done((bf16[144,256]{1,0:T(8,128)(2,1)S(1)}, bf16[144,256]{1,0:T(8,128)(2,1)S(1)}, u32[]{:S(2)}, u32[]{:S(2)}) %collective-permute-start.4) | collective-permute-done | bytes 73760 | tf_op jit(solution)/shard_map/ppermute | solution.py:206
  9.5 3.6 %collective-permute-done.3.refs_3_.refs_6_ = bf16[144,256]{1,0:T(8,128)(2,1)S(1)} collective-permute-done((bf16[144,256]{1,0:T(8,128)(2,1)S(1)}, bf16[144,256]{1,0:T(8,128)(2,1)S(1)}, u32[]{:S(2)}, u32[]{:S(2)}) %collective-permute-start.3) | collective-permute-done | bytes 73760 | tf_op jit(solution)/shard_map/ppermute | solution.py:206
  13.1 0.0 copy-done.1
  13.1 0.2 shard_map.68
  13.3 1.4 %collective-permute-done.5.refs_8_ = bf16[144,256]{1,0:T(8,128)(2,1)S(1)} collective-permute-done((bf16[144,256]{1,0:T(8,128)(2,1)S(1)}, bf16[144,256]{1,0:T(8,128)(2,1)S(1)}, u32[]{:S(2)}, u32[]{:S(2)}) %collective-permute-start.5) | collective-permute-done | bytes 73760 | tf_op jit(solution)/shard_map/ppermute | solution.py:206
  14.6 0.0 collective-permute-done.1.refs_2_
  14.7 0.0 collective-permute-done.2.refs_3_
  14.7 1.0 %shard_map.69.refs_5_ = f32[4,16,256]{2,1,0:T(8,128)S(1)} custom-call(bf16[2,144,256]{2,1,0:T(8,128)(2,1)S(1)} %get-tuple-element.12.refs_0_, f32[16,256]{1,0:T(8,128)S(1)} %get-tuple-element.13.refs_1_, bf16[160,256]{1,0:T(8,128)(2,1)S(1)} %collective-permute-done.1.refs_2_, bf16[160,256]{1,0:T(8,128)(2,1)S(1)} %collective-permute-done.2.refs_3_, ...), custom_call_target="tpu_custom_call" | custom-call | tf_op jit(solution)/shard_map/pallas_call | solution.py:254
  15.6 1.5 %collective-permute-start.8 = (f32[4,16,256]{2,1,0:T(8,128)S(1)}, f32[4,16,256]{2,1,0:T(8,128)S(1)}, u32[]{:S(2)}, u32[]{:S(2)}) collective-permute-start(f32[4,16,256]{2,1,0:T(8,128)S(1)} %shard_map.69.refs_5_), channel_id=1, source_target_pairs={{2,0},{3,1},{0,2},{1,3},{6,4},{7,5},{4,6},{5,7},{10,8},{11,9},{8,1... | collective-permute-start | bytes 196616 | tf_op jit(solution)/shard_map/ppermute | solution.py:191
  17.1 0.0 collective-permute-start.7
  17.1 0.6 %collective-permute-start.6 = (f32[4,16,256]{2,1,0:T(8,128)S(1)}, f32[4,16,256]{2,1,0:T(8,128)S(1)}, u32[]{:S(2)}, u32[]{:S(2)}) collective-permute-start(f32[4,16,256]{2,1,0:T(8,128)S(1)} %shard_map.69.refs_5_), channel_id=1, source_target_pairs={{1,0},{0,1},{3,2},{2,3},{5,4},{4,5},{7,6},{6,7},{9,8},{8,9},{11,10... | collective-permute-start | bytes 196616 | tf_op jit(solution)/shard_map/ppermute | solution.py:191
  17.8 2.1 %collective-permute-done.8.refs_8_ = f32[4,16,256]{2,1,0:T(8,128)S(1)} collective-permute-done((f32[4,16,256]{2,1,0:T(8,128)S(1)}, f32[4,16,256]{2,1,0:T(8,128)S(1)}, u32[]{:S(2)}, u32[]{:S(2)}) %collective-permute-start.8) | collective-permute-done | bytes 65568 | tf_op jit(solution)/shard_map/ppermute | solution.py:191
  19.9 1.5 %collective-permute-done.7.refs_7_ = f32[4,16,256]{2,1,0:T(8,128)S(1)} collective-permute-done((f32[4,16,256]{2,1,0:T(8,128)S(1)}, f32[4,16,256]{2,1,0:T(8,128)S(1)}, u32[]{:S(2)}, u32[]{:S(2)}) %collective-permute-start.7) | collective-permute-done | bytes 65568 | tf_op jit(solution)/shard_map/ppermute | solution.py:191
  21.4 0.0 collective-permute-done.6.refs_6_
  21.4 0.1 shard_map.70
  21.5 1.0 %collective-permute-start.11 = (f32[16,128]{1,0:T(8,128)S(1)}, f32[16,128]{1,0:T(8,128)S(1)}, u32[]{:S(2)}, u32[]{:S(2)}) collective-permute-start(f32[16,128]{1,0:T(8,128)S(1)} %get-tuple-element.16.refs_0_), channel_id=1, source_target_pairs={{13,0},{12,1},{9,4},{8,5},{5,8},{4,9},{1,12},{0,13},{15,2},{14,3},... | collective-permute-start | bytes 24584 | tf_op jit(solution)/shard_map/ppermute | solution.py:206
  22.5 0.3 %collective-permute-start.10 = (f32[16,128]{1,0:T(8,128)S(1)}, f32[16,128]{1,0:T(8,128)S(1)}, u32[]{:S(2)}, u32[]{:S(2)}) collective-permute-start(f32[16,128]{1,0:T(8,128)S(1)} %get-tuple-element.16.refs_0_), channel_id=1, source_target_pairs={{9,0},{8,1},{13,4},{12,5},{1,8},{0,9},{5,12},{4,13},{11,2},{10,3},... | collective-permute-start | bytes 24584 | tf_op jit(solution)/shard_map/ppermute | solution.py:206
  22.8 2.4 %collective-permute-start.9 = (f32[16,128]{1,0:T(8,128)S(1)}, f32[16,128]{1,0:T(8,128)S(1)}, u32[]{:S(2)}, u32[]{:S(2)}) collective-permute-start(f32[16,128]{1,0:T(8,128)S(1)} %get-tuple-element.16.refs_0_), channel_id=1, source_target_pairs={{5,0},{4,1},{1,4},{0,5},{13,8},{12,9},{9,12},{8,13},{7,2},{6,3},{3... | collective-permute-start | bytes 24584 | tf_op jit(solution)/shard_map/ppermute | solution.py:206
  25.2 1.2 %collective-permute-done.11.refs_3_ = f32[16,128]{1,0:T(8,128)S(1)} collective-permute-done((f32[16,128]{1,0:T(8,128)S(1)}, f32[16,128]{1,0:T(8,128)S(1)}, u32[]{:S(2)}, u32[]{:S(2)}) %collective-permute-start.11) | collective-permute-done | bytes 8224 | tf_op jit(solution)/shard_map/ppermute | solution.py:206
  26.4 0.1 collective-permute-done.10.refs_2_
  26.5 0.2 collective-permute-done.9.refs_1_
  26.6 0.8 %shard_map.71 = (f32[16,256]{1,0:T(8,128)}, f32[16,256]{1,0:T(8,128)}, f32[16,256]{1,0:T(8,128)}) custom-call(f32[16,256]{1,0:T(8,128)S(1)} %get-tuple-element.15.image_ref, f32[16,256]{1,0:T(8,128)S(1)} %copy-done, f32[16,128]{1,0:T(8,128)S(1)} %get-tuple-element.16.refs_0_, f32[16,128]{1,0:T(8,128)S(1)} %collective-permute-done.9.refs_1_, ...), custom_call_target="tpu_custom_call" | custom-call | tf_op jit(solution)/shard_map/pallas_call | solution.py:269
  (1 shorter events, 0.0 us)
Async XLA Ops:
  0.6 1.0 %copy-start = (f32[16,256]{1,0:T(8,128)S(1)}, f32[16,256]{1,0:T(8,128)}, u32[]{:S(2)}) copy-start(f32[16,256]{1,0:T(8,128)} %probes_ref.3) | copy-start | bytes 49156
  1.6 6.7 %collective-permute-start = (bf16[160,256]{1,0:T(8,128)(2,1)S(1)}, bf16[160,256]{1,0:T(8,128)(2,1)S(1)}, u32[]{:S(2)}, u32[]{:S(2)}) collective-permute-start(bf16[160,256]{1,0:T(8,128)(2,1)S(1)} %get-tuple-element.10.refs_0_), channel_id=1, source_target_pairs={{1,0},{0,1},{3,2},{2,3},{5,4},{4,5},{7,6},{6,7},{9,8},{8,9},{11,10... | collective-permute-start | bytes 245768 | tf_op jit(solution)/shard_map/ppermute | solution.py:191
  2.1 10.9 %copy-start.1 = (f32[256]{0:T(256)S(1)}, f32[256]{0:T(256)}, u32[]{:S(2)}) copy-start(f32[256]{0:T(256)} %param.6) | copy-start | bytes 3076
  2.1 7.4 %collective-permute-start.4 = (bf16[144,256]{1,0:T(8,128)(2,1)S(1)}, bf16[144,256]{1,0:T(8,128)(2,1)S(1)}, u32[]{:S(2)}, u32[]{:S(2)}) collective-permute-start(bf16[144,256]{1,0:T(8,128)(2,1)S(1)} %get-tuple-element.11.refs_2_.refs_5_), channel_id=1, source_target_pairs={{13,0},{12,1},{9,4},{8,5},{5,8},{4,9},{1,12},{0,13},{15,2},{14,3},... | collective-permute-start | bytes 221192 | tf_op jit(solution)/shard_map/ppermute | solution.py:206
  6.9 6.2 %collective-permute-start.3 = (bf16[144,256]{1,0:T(8,128)(2,1)S(1)}, bf16[144,256]{1,0:T(8,128)(2,1)S(1)}, u32[]{:S(2)}, u32[]{:S(2)}) collective-permute-start(bf16[144,256]{1,0:T(8,128)(2,1)S(1)} %get-tuple-element.11.refs_2_.refs_5_), channel_id=1, source_target_pairs={{9,0},{8,1},{13,4},{12,5},{1,8},{0,9},{5,12},{4,13},{11,2},{10,3},... | collective-permute-start | bytes 221192 | tf_op jit(solution)/shard_map/ppermute | solution.py:206
  6.9 7.8 %collective-permute-start.1 = (bf16[160,256]{1,0:T(8,128)(2,1)S(1)}, bf16[160,256]{1,0:T(8,128)(2,1)S(1)}, u32[]{:S(2)}, u32[]{:S(2)}) collective-permute-start(bf16[160,256]{1,0:T(8,128)(2,1)S(1)} %get-tuple-element.10.refs_0_), channel_id=1, source_target_pairs={{2,0},{0,2},{3,1},{1,3},{6,4},{4,6},{7,5},{5,7},{10,8},{8,10},{11,... | collective-permute-start | bytes 245768 | tf_op jit(solution)/shard_map/ppermute | solution.py:191
  8.4 6.3 %collective-permute-start.2 = (bf16[160,256]{1,0:T(8,128)(2,1)S(1)}, bf16[160,256]{1,0:T(8,128)(2,1)S(1)}, u32[]{:S(2)}, u32[]{:S(2)}) collective-permute-start(bf16[160,256]{1,0:T(8,128)(2,1)S(1)} %collective-permute-done.refs_1_), channel_id=1, source_target_pairs={{2,0},{0,2},{3,1},{1,3},{6,4},{4,6},{7,5},{5,7},{10,8},{8,10},{11,... | collective-permute-start | bytes 245768 | tf_op jit(solution)/shard_map/ppermute | solution.py:191
  8.9 5.8 %collective-permute-start.5 = (bf16[144,256]{1,0:T(8,128)(2,1)S(1)}, bf16[144,256]{1,0:T(8,128)(2,1)S(1)}, u32[]{:S(2)}, u32[]{:S(2)}) collective-permute-start(bf16[144,256]{1,0:T(8,128)(2,1)S(1)} %get-tuple-element.11.refs_2_.refs_5_), channel_id=1, source_target_pairs={{5,0},{4,1},{1,4},{0,5},{13,8},{12,9},{9,12},{8,13},{7,2},{6,3},{3... | collective-permute-start | bytes 221192 | tf_op jit(solution)/shard_map/ppermute | solution.py:206
  15.6 4.3 %collective-permute-start.8 = (f32[4,16,256]{2,1,0:T(8,128)S(1)}, f32[4,16,256]{2,1,0:T(8,128)S(1)}, u32[]{:S(2)}, u32[]{:S(2)}) collective-permute-start(f32[4,16,256]{2,1,0:T(8,128)S(1)} %shard_map.69.refs_5_), channel_id=1, source_target_pairs={{2,0},{3,1},{0,2},{1,3},{6,4},{7,5},{4,6},{5,7},{10,8},{11,9},{8,1... | collective-permute-start | bytes 196616 | tf_op jit(solution)/shard_map/ppermute | solution.py:191
  17.1 4.3 %collective-permute-start.7 = (f32[4,16,256]{2,1,0:T(8,128)S(1)}, f32[4,16,256]{2,1,0:T(8,128)S(1)}, u32[]{:S(2)}, u32[]{:S(2)}) collective-permute-start(f32[4,16,256]{2,1,0:T(8,128)S(1)} %shard_map.69.refs_5_), channel_id=1, source_target_pairs={{3,0},{2,1},{1,2},{0,3},{7,4},{6,5},{5,6},{4,7},{11,8},{10,9},{9,1... | collective-permute-start | bytes 196616 | tf_op jit(solution)/shard_map/ppermute | solution.py:191
  17.1 4.3 %collective-permute-start.6 = (f32[4,16,256]{2,1,0:T(8,128)S(1)}, f32[4,16,256]{2,1,0:T(8,128)S(1)}, u32[]{:S(2)}, u32[]{:S(2)}) collective-permute-start(f32[4,16,256]{2,1,0:T(8,128)S(1)} %shard_map.69.refs_5_), channel_id=1, source_target_pairs={{1,0},{0,1},{3,2},{2,3},{5,4},{4,5},{7,6},{6,7},{9,8},{8,9},{11,10... | collective-permute-start | bytes 196616 | tf_op jit(solution)/shard_map/ppermute | solution.py:191
  21.5 4.9 %collective-permute-start.11 = (f32[16,128]{1,0:T(8,128)S(1)}, f32[16,128]{1,0:T(8,128)S(1)}, u32[]{:S(2)}, u32[]{:S(2)}) collective-permute-start(f32[16,128]{1,0:T(8,128)S(1)} %get-tuple-element.16.refs_0_), channel_id=1, source_target_pairs={{13,0},{12,1},{9,4},{8,5},{5,8},{4,9},{1,12},{0,13},{15,2},{14,3},... | collective-permute-start | bytes 24584 | tf_op jit(solution)/shard_map/ppermute | solution.py:206
  22.5 4.0 %collective-permute-start.10 = (f32[16,128]{1,0:T(8,128)S(1)}, f32[16,128]{1,0:T(8,128)S(1)}, u32[]{:S(2)}, u32[]{:S(2)}) collective-permute-start(f32[16,128]{1,0:T(8,128)S(1)} %get-tuple-element.16.refs_0_), channel_id=1, source_target_pairs={{9,0},{8,1},{13,4},{12,5},{1,8},{0,9},{5,12},{4,13},{11,2},{10,3},... | collective-permute-start | bytes 24584 | tf_op jit(solution)/shard_map/ppermute | solution.py:206
  22.8 3.8 %collective-permute-start.9 = (f32[16,128]{1,0:T(8,128)S(1)}, f32[16,128]{1,0:T(8,128)S(1)}, u32[]{:S(2)}, u32[]{:S(2)}) collective-permute-start(f32[16,128]{1,0:T(8,128)S(1)} %get-tuple-element.16.refs_0_), channel_id=1, source_target_pairs={{5,0},{4,1},{1,4},{0,5},{13,8},{12,9},{9,12},{8,13},{7,2},{6,3},{3... | collective-permute-start | bytes 24584 | tf_op jit(solution)/shard_map/ppermute | solution.py:206

commit v24 on v20

--- a/solution.py
+++ b/solution.py
@@ -33,11 +33,13 @@
     return rows.astype(jnp.bfloat16)
 
 
-def pack_kernel(scaled_ref, probes_ref, line_ref, plane_ref):
+def pack_kernel(scaled_ref, probes_ref, line_ref, plane_ref, across_ref):
     high, low, _ = pieces_of(probes_ref[...])
     high, low = high.astype(jnp.bfloat16), low.astype(jnp.bfloat16)
     line_ref[...] = jnp.concatenate([scaled_ref[...], high], axis=0)
     plane_ref[...] = jnp.concatenate([scaled_ref[...], high, low], axis=0)
+    norms = norm_rows(scaled_ref[...], 1)
+    across_ref[...] = jnp.concatenate([scaled_ref[...], high, low, norms], axis=0)
 
 
 def columns_of(block, feature_count):
@@ -67,7 +69,9 @@
     columns_ref, *line_refs = refs[plane_count:-1]
     partial_ref = refs[-1]
     rows = [rows_ref[number] for number in range(2)]
-    rows += [rows_of(ref, feature_count) for ref in plane_refs]
+    for number, ref in enumerate(plane_refs):
+        norms = ref[-2 * HALF :, :] if number % 2 == 0 else norm_rows(ref[:feature_count, :], 1)
+        rows.append(jnp.concatenate([ref[:feature_count, :], norms], axis=0))
     start = start_ref[...]
     width = start.shape[1]
     rows = [
@@ -121,7 +125,8 @@
         else:
             middle = feature_count + probe_count
             probes = plane_ref[feature_count:middle, :].astype(jnp.float32)
-            probes = probes + plane_ref[middle:, :].astype(jnp.float32)
+            low = plane_ref[middle : middle + probe_count, :]
+            probes = probes + low.astype(jnp.float32)
         products[0] += probes * probes
         products[1] += probes * image
         products[2] += image * image
@@ -186,13 +191,17 @@
     return blocks
 
 
-def plane_blocks(value, shape):
+def plane_blocks(value, across, shape):
     grp_count, sub_count = shape
     if sub_count != 2 or not paired(grp_count):
         return everywhere(value, PLANE, grp_count * sub_count)
-    blocks = everywhere(value, ("sub",), sub_count)
-    moved = [everywhere(block, ("grp",), grp_count) for block in blocks]
-    return [moved[sub][grp] for grp in range(grp_count) for sub in range(sub_count)]
+    own, other = everywhere(value, ("sub",), sub_count)
+    near = everywhere(across, ("grp",), grp_count)
+    far = everywhere(other, ("grp",), grp_count)
+    blocks = [own, other]
+    for grp in range(1, grp_count):
+        blocks += [near[grp], far[grp]]
+    return blocks
 
 
 def make_local(plane_shape, line_count):
@@ -202,16 +211,19 @@
         feature_count, width = features.shape
         probe_count = probes.shape[0]
         scaled = (features.astype(jnp.float32) / lengthscale[:, None]).astype(jnp.bfloat16)
-        line, plane = pl.pallas_call(
+        line, plane, across = pl.pallas_call(
             pack_kernel,
             out_shape=(
                 jax.ShapeDtypeStruct((feature_count + probe_count, width), jnp.bfloat16),
                 jax.ShapeDtypeStruct((feature_count + 2 * probe_count, width), jnp.bfloat16),
+                jax.ShapeDtypeStruct(
+                    (feature_count + 2 * probe_count + 2 * HALF, width), jnp.bfloat16
+                ),
             ),
             compiler_params=VMEM,
         )(scaled, probes)
         lines = along_line(line, line_count, plane_shape[1])
-        planes = plane_blocks(plane, plane_shape)
+        planes = plane_blocks(plane, across, plane_shape)
         if len(lines) > 1:
             early, late = lines[:1] + lines[2:], lines[1]
         else:
@@ -227,7 +239,7 @@
             ),
             compiler_params=VMEM,
             cost_estimate=pl.CostEstimate(
-                flops=6 * work * depth, bytes_accessed=4 * plane_count * width, transcendentals=3 * work
+                flops=24 * work * depth, bytes_accessed=4 * plane_count * width, transcendentals=12 * work
             ),
         )(*planes[:2], *early, noise_var[None, :], probes)
         partial = pl.pallas_call(

time: 27.6 us -> 27.9 us (1.011)
  starting transfers between devices: 13.1 us -> 13.7 us
    ppermute x6, waiting for transfers between devices: 3.61 us -> 2.64 us  [everywhere(): lax.ppermute(value, axes, [(source_of(i, step, count), i) for i in range(...]
    ppermute x6, waiting for transfers between devices: 6.98 us -> 7.76 us  [along_line(): blocks.append(lax.ppermute(value, LINE + ('sub',), pairs))]
    ppermute x6, starting transfers between devices: 8.43 us -> 9.18 us  [along_line(): blocks.append(lax.ppermute(value, LINE + ('sub',), pairs))]
  transfers between devices with their start and end apart: 12 -> 12, of which waited for: 8 -> 6; matrix products, arithmetic and copies ran while one was open for 0% -> 0% of each run, Pallas kernels for 1% -> 1%
where the time goes in v24:
time: 27.9 us; the launch traced here: 27.8 us
  starting transfers between devices  13.7 us (49%)
  waiting for transfers between devices  10.4 us (37%)
  Pallas kernels  2.07 us (7%)
  other arithmetic  0.93 us (3%)
  between operations  0.67 us (2%)
    ppermute x6, starting transfers between devices, along_line(): blocks.append(lax.ppermute(value, LINE + ('sub',), pairs))  9.18 us
    ppermute x6, waiting for transfers between devices, along_line(): blocks.append(lax.ppermute(value, LINE + ('sub',), pairs))  7.76 us
    ppermute x6, starting transfers between devices, everywhere(): lax.ppermute(value, axes, [(source_of(i, step, count), i) for i in range(...  4.5 us
    ppermute x6, waiting for transfers between devices, everywhere(): lax.ppermute(value, axes, [(source_of(i, step, count), i) for i in range(...  2.64 us
    pallas_call x1, Pallas kernels, local(): pl.pallas_call(lambda *refs: image_kernel(feature_count, plane_count, *re...  0.96 us
    convert_element_type x1, other arithmetic, local(): (features.astype(jnp.float32) / lengthscale[:, None]).astype(jnp.bfloat16)  0.93 us
    pallas_call x1, Pallas kernels, local(): pl.pallas_call(finish_kernel, out_shape=outs, compiler_params=VMEM)  0.77 us
  transfers between devices with their start and end apart: 12, of which 6 were waited for; matrix products, arithmetic and copies ran while one was open for 0% of the time, Pallas kernels for 1%

profile of v24, /device:TPU:0, one launch (start us, length us, event | category | flops | bytes accessed | tf_op | source)
XLA Modules:
  0.0 27.8 jit_solution(13534034019304865575)
XLA Ops:
  0.6 0.0 copy-start
  0.6 0.9 %divide_convert_fusion.scaled_ref = bf16[128,256]{1,0:T(8,128)(2,1)S(1)} fusion(bf16[128,256]{1,0:T(8,128)(2,1)} %param.4, f32[128]{0:T(128)} %param.5), kind=kLoop, calls=%fused_computation | loop fusion | flops 98304 | bytes 131584 | tf_op jit(solution)/shard_map/convert_element_type | solution.py:213
  1.6 0.0 copy-done
  1.6 0.5 %collective-permute-start = (bf16[160,256]{1,0:T(8,128)(2,1)S(1)}, bf16[160,256]{1,0:T(8,128)(2,1)S(1)}, u32[]{:S(2)}, u32[]{:S(2)}) collective-permute-start(bf16[160,256]{1,0:T(8,128)(2,1)S(1)} %get-tuple-element.11.refs_0_), channel_id=1, source_target_pairs={{1,0},{0,1},{3,2},{2,3},{5,4},{4,5},{7,6},{6,7},{9,8},{8,9},{11,10... | collective-permute-start | bytes 245768 | tf_op jit(solution)/shard_map/ppermute | solution.py:175
  2.1 4.7 %collective-permute-start.4 = (bf16[144,256]{1,0:T(8,128)(2,1)S(1)}, bf16[144,256]{1,0:T(8,128)(2,1)S(1)}, u32[]{:S(2)}, u32[]{:S(2)}) collective-permute-start(bf16[144,256]{1,0:T(8,128)(2,1)S(1)} %get-tuple-element.13.refs_2_.refs_5_), channel_id=1, source_target_pairs={{13,0},{12,1},{9,4},{8,5},{5,8},{4,9},{1,12},{0,13},{15,2},{14,3},... | collective-permute-start | bytes 221192 | tf_op jit(solution)/shard_map/ppermute | solution.py:190
  6.9 0.0 collective-permute-start.3
  6.9 0.0 copy-start.1
  6.9 1.5 %collective-permute-start.1 = (bf16[176,256]{1,0:T(8,128)(2,1)S(1)}, bf16[176,256]{1,0:T(8,128)(2,1)S(1)}, u32[]{:S(2)}, u32[]{:S(2)}) collective-permute-start(bf16[176,256]{1,0:T(8,128)(2,1)S(1)} %get-tuple-element.12), channel_id=1, source_target_pairs={{2,0},{0,2},{3,1},{1,3},{6,4},{4,6},{7,5},{5,7},{10,8},{8,10},{11,... | collective-permute-start | bytes 270344 | tf_op jit(solution)/shard_map/ppermute | solution.py:175
  8.4 0.2 collective-permute-start.5
  8.6 0.0 collective-permute-done.refs_1_
  8.6 0.3 %collective-permute-start.2 = (bf16[160,256]{1,0:T(8,128)(2,1)S(1)}, bf16[160,256]{1,0:T(8,128)(2,1)S(1)}, u32[]{:S(2)}, u32[]{:S(2)}) collective-permute-start(bf16[160,256]{1,0:T(8,128)(2,1)S(1)} %collective-permute-done.refs_1_), channel_id=1, source_target_pairs={{2,0},{0,2},{3,1},{1,3},{6,4},{4,6},{7,5},{5,7},{10,8},{8,10},{11,... | collective-permute-start | bytes 245768 | tf_op jit(solution)/shard_map/ppermute | solution.py:175
  8.9 0.6 %collective-permute-done.4.refs_4_.refs_7_ = bf16[144,256]{1,0:T(8,128)(2,1)S(1)} collective-permute-done((bf16[144,256]{1,0:T(8,128)(2,1)S(1)}, bf16[144,256]{1,0:T(8,128)(2,1)S(1)}, u32[]{:S(2)}, u32[]{:S(2)}) %collective-permute-start.4) | collective-permute-done | bytes 73760 | tf_op jit(solution)/shard_map/ppermute | solution.py:190
  9.5 3.6 %collective-permute-done.3.refs_3_.refs_6_ = bf16[144,256]{1,0:T(8,128)(2,1)S(1)} collective-permute-done((bf16[144,256]{1,0:T(8,128)(2,1)S(1)}, bf16[144,256]{1,0:T(8,128)(2,1)S(1)}, u32[]{:S(2)}, u32[]{:S(2)}) %collective-permute-start.3) | collective-permute-done | bytes 73760 | tf_op jit(solution)/shard_map/ppermute | solution.py:190
  13.1 0.0 copy-done.1
  13.1 0.2 shard_map.68
  13.3 1.2 %collective-permute-done.5.refs_8_ = bf16[144,256]{1,0:T(8,128)(2,1)S(1)} collective-permute-done((bf16[144,256]{1,0:T(8,128)(2,1)S(1)}, bf16[144,256]{1,0:T(8,128)(2,1)S(1)}, u32[]{:S(2)}, u32[]{:S(2)}) %collective-permute-start.5) | collective-permute-done | bytes 73760 | tf_op jit(solution)/shard_map/ppermute | solution.py:190
  14.5 0.0 collective-permute-done.1.refs_2_
  14.5 0.0 collective-permute-done.2.refs_3_
  14.5 1.0 %shard_map.69.refs_5_ = f32[4,16,256]{2,1,0:T(8,128)S(1)} custom-call(bf16[2,144,256]{2,1,0:T(8,128)(2,1)S(1)} %get-tuple-element.14.refs_0_, f32[16,256]{1,0:T(8,128)S(1)} %get-tuple-element.15.refs_1_, bf16[176,256]{1,0:T(8,128)(2,1)S(1)} %collective-permute-done.1.refs_2_, bf16[160,256]{1,0:T(8,128)(2,1)S(1)} %collective-permute-done.2.refs_3_, ...), custom_call_target="tpu_custom_call" | custom-call | tf_op jit(solution)/shard_map/pallas_call | solution.py:245
  15.4 0.2 collective-permute-start.8
  15.7 1.2 %collective-permute-start.7 = (f32[4,16,256]{2,1,0:T(8,128)S(1)}, f32[4,16,256]{2,1,0:T(8,128)S(1)}, u32[]{:S(2)}, u32[]{:S(2)}) collective-permute-start(f32[4,16,256]{2,1,0:T(8,128)S(1)} %shard_map.69.refs_5_), channel_id=1, source_target_pairs={{3,0},{2,1},{1,2},{0,3},{7,4},{6,5},{5,6},{4,7},{11,8},{10,9},{9,1... | collective-permute-start | bytes 196616 | tf_op jit(solution)/shard_map/ppermute | solution.py:175
  16.9 0.7 %collective-permute-start.6 = (f32[4,16,256]{2,1,0:T(8,128)S(1)}, f32[4,16,256]{2,1,0:T(8,128)S(1)}, u32[]{:S(2)}, u32[]{:S(2)}) collective-permute-start(f32[4,16,256]{2,1,0:T(8,128)S(1)} %shard_map.69.refs_5_), channel_id=1, source_target_pairs={{1,0},{0,1},{3,2},{2,3},{5,4},{4,5},{7,6},{6,7},{9,8},{8,9},{11,10... | collective-permute-start | bytes 196616 | tf_op jit(solution)/shard_map/ppermute | solution.py:175
  17.6 2.6 %collective-permute-done.8.refs_8_ = f32[4,16,256]{2,1,0:T(8,128)S(1)} collective-permute-done((f32[4,16,256]{2,1,0:T(8,128)S(1)}, f32[4,16,256]{2,1,0:T(8,128)S(1)}, u32[]{:S(2)}, u32[]{:S(2)}) %collective-permute-start.8) | collective-permute-done | bytes 65568 | tf_op jit(solution)/shard_map/ppermute | solution.py:175
  20.2 0.0 collective-permute-done.7.refs_7_
  20.2 0.0 collective-permute-done.6.refs_6_
  20.2 0.1 shard_map.70
  20.3 2.7 %collective-permute-start.11 = (f32[16,128]{1,0:T(8,128)S(1)}, f32[16,128]{1,0:T(8,128)S(1)}, u32[]{:S(2)}, u32[]{:S(2)}) collective-permute-start(f32[16,128]{1,0:T(8,128)S(1)} %get-tuple-element.18.refs_0_), channel_id=1, source_target_pairs={{13,0},{12,1},{9,4},{8,5},{5,8},{4,9},{1,12},{0,13},{15,2},{14,3},... | collective-permute-start | bytes 24584 | tf_op jit(solution)/shard_map/ppermute | solution.py:190
  23.0 0.0 collective-permute-start.10
  23.0 1.5 %collective-permute-start.9 = (f32[16,128]{1,0:T(8,128)S(1)}, f32[16,128]{1,0:T(8,128)S(1)}, u32[]{:S(2)}, u32[]{:S(2)}) collective-permute-start(f32[16,128]{1,0:T(8,128)S(1)} %get-tuple-element.18.refs_0_), channel_id=1, source_target_pairs={{5,0},{4,1},{1,4},{0,5},{13,8},{12,9},{9,12},{8,13},{7,2},{6,3},{3... | collective-permute-start | bytes 24584 | tf_op jit(solution)/shard_map/ppermute | solution.py:190
  24.6 0.6 %collective-permute-done.11.refs_3_ = f32[16,128]{1,0:T(8,128)S(1)} collective-permute-done((f32[16,128]{1,0:T(8,128)S(1)}, f32[16,128]{1,0:T(8,128)S(1)}, u32[]{:S(2)}, u32[]{:S(2)}) %collective-permute-start.11) | collective-permute-done | bytes 8224 | tf_op jit(solution)/shard_map/ppermute | solution.py:190
  25.2 1.8 %collective-permute-done.10.refs_2_ = f32[16,128]{1,0:T(8,128)S(1)} collective-permute-done((f32[16,128]{1,0:T(8,128)S(1)}, f32[16,128]{1,0:T(8,128)S(1)}, u32[]{:S(2)}, u32[]{:S(2)}) %collective-permute-start.10) | collective-permute-done | bytes 8224 | tf_op jit(solution)/shard_map/ppermute | solution.py:190
  27.0 0.0 collective-permute-done.9.refs_1_
  27.0 0.8 %shard_map.71 = (f32[16,256]{1,0:T(8,128)}, f32[16,256]{1,0:T(8,128)}, f32[16,256]{1,0:T(8,128)}) custom-call(f32[16,256]{1,0:T(8,128)S(1)} %get-tuple-element.17.image_ref, f32[16,256]{1,0:T(8,128)S(1)} %copy-done, f32[16,128]{1,0:T(8,128)S(1)} %get-tuple-element.18.refs_0_, f32[16,128]{1,0:T(8,128)S(1)} %collective-permute-done.9.refs_1_, ...), custom_call_target="tpu_custom_call" | custom-call | tf_op jit(solution)/shard_map/pallas_call | solution.py:260
  (1 shorter events, 0.0 us)
Async XLA Ops:
  0.6 1.0 %copy-start = (f32[16,256]{1,0:T(8,128)S(1)}, f32[16,256]{1,0:T(8,128)}, u32[]{:S(2)}) copy-start(f32[16,256]{1,0:T(8,128)} %probes_ref.3) | copy-start | bytes 49156
  1.6 7.0 %collective-permute-start = (bf16[160,256]{1,0:T(8,128)(2,1)S(1)}, bf16[160,256]{1,0:T(8,128)(2,1)S(1)}, u32[]{:S(2)}, u32[]{:S(2)}) collective-permute-start(bf16[160,256]{1,0:T(8,128)(2,1)S(1)} %get-tuple-element.11.refs_0_), channel_id=1, source_target_pairs={{1,0},{0,1},{3,2},{2,3},{5,4},{4,5},{7,6},{6,7},{9,8},{8,9},{11,10... | collective-permute-start | bytes 245768 | tf_op jit(solution)/shard_map/ppermute | solution.py:175
  2.1 7.4 %collective-permute-start.4 = (bf16[144,256]{1,0:T(8,128)(2,1)S(1)}, bf16[144,256]{1,0:T(8,128)(2,1)S(1)}, u32[]{:S(2)}, u32[]{:S(2)}) collective-permute-start(bf16[144,256]{1,0:T(8,128)(2,1)S(1)} %get-tuple-element.13.refs_2_.refs_5_), channel_id=1, source_target_pairs={{13,0},{12,1},{9,4},{8,5},{5,8},{4,9},{1,12},{0,13},{15,2},{14,3},... | collective-permute-start | bytes 221192 | tf_op jit(solution)/shard_map/ppermute | solution.py:190
  6.9 6.2 %collective-permute-start.3 = (bf16[144,256]{1,0:T(8,128)(2,1)S(1)}, bf16[144,256]{1,0:T(8,128)(2,1)S(1)}, u32[]{:S(2)}, u32[]{:S(2)}) collective-permute-start(bf16[144,256]{1,0:T(8,128)(2,1)S(1)} %get-tuple-element.13.refs_2_.refs_5_), channel_id=1, source_target_pairs={{9,0},{8,1},{13,4},{12,5},{1,8},{0,9},{5,12},{4,13},{11,2},{10,3},... | collective-permute-start | bytes 221192 | tf_op jit(solution)/shard_map/ppermute | solution.py:190
  6.9 6.2 %copy-start.1 = (f32[256]{0:T(256)S(1)}, f32[256]{0:T(256)}, u32[]{:S(2)}) copy-start(f32[256]{0:T(256)} %param.6) | copy-start | bytes 3076
  6.9 7.6 %collective-permute-start.1 = (bf16[176,256]{1,0:T(8,128)(2,1)S(1)}, bf16[176,256]{1,0:T(8,128)(2,1)S(1)}, u32[]{:S(2)}, u32[]{:S(2)}) collective-permute-start(bf16[176,256]{1,0:T(8,128)(2,1)S(1)} %get-tuple-element.12), channel_id=1, source_target_pairs={{2,0},{0,2},{3,1},{1,3},{6,4},{4,6},{7,5},{5,7},{10,8},{8,10},{11,... | collective-permute-start | bytes 270344 | tf_op jit(solution)/shard_map/ppermute | solution.py:175
  8.4 6.1 %collective-permute-start.5 = (bf16[144,256]{1,0:T(8,128)(2,1)S(1)}, bf16[144,256]{1,0:T(8,128)(2,1)S(1)}, u32[]{:S(2)}, u32[]{:S(2)}) collective-permute-start(bf16[144,256]{1,0:T(8,128)(2,1)S(1)} %get-tuple-element.13.refs_2_.refs_5_), channel_id=1, source_target_pairs={{5,0},{4,1},{1,4},{0,5},{13,8},{12,9},{9,12},{8,13},{7,2},{6,3},{3... | collective-permute-start | bytes 221192 | tf_op jit(solution)/shard_map/ppermute | solution.py:190
  8.6 5.9 %collective-permute-start.2 = (bf16[160,256]{1,0:T(8,128)(2,1)S(1)}, bf16[160,256]{1,0:T(8,128)(2,1)S(1)}, u32[]{:S(2)}, u32[]{:S(2)}) collective-permute-start(bf16[160,256]{1,0:T(8,128)(2,1)S(1)} %collective-permute-done.refs_1_), channel_id=1, source_target_pairs={{2,0},{0,2},{3,1},{1,3},{6,4},{4,6},{7,5},{5,7},{10,8},{8,10},{11,... | collective-permute-start | bytes 245768 | tf_op jit(solution)/shard_map/ppermute | solution.py:175
  15.4 4.8 %collective-permute-start.8 = (f32[4,16,256]{2,1,0:T(8,128)S(1)}, f32[4,16,256]{2,1,0:T(8,128)S(1)}, u32[]{:S(2)}, u32[]{:S(2)}) collective-permute-start(f32[4,16,256]{2,1,0:T(8,128)S(1)} %shard_map.69.refs_5_), channel_id=1, source_target_pairs={{2,0},{3,1},{0,2},{1,3},{6,4},{7,5},{4,6},{5,7},{10,8},{11,9},{8,1... | collective-permute-start | bytes 196616 | tf_op jit(solution)/shard_map/ppermute | solution.py:175
  15.7 4.5 %collective-permute-start.7 = (f32[4,16,256]{2,1,0:T(8,128)S(1)}, f32[4,16,256]{2,1,0:T(8,128)S(1)}, u32[]{:S(2)}, u32[]{:S(2)}) collective-permute-start(f32[4,16,256]{2,1,0:T(8,128)S(1)} %shard_map.69.refs_5_), channel_id=1, source_target_pairs={{3,0},{2,1},{1,2},{0,3},{7,4},{6,5},{5,6},{4,7},{11,8},{10,9},{9,1... | collective-permute-start | bytes 196616 | tf_op jit(solution)/shard_map/ppermute | solution.py:175
  16.9 3.4 %collective-permute-start.6 = (f32[4,16,256]{2,1,0:T(8,128)S(1)}, f32[4,16,256]{2,1,0:T(8,128)S(1)}, u32[]{:S(2)}, u32[]{:S(2)}) collective-permute-start(f32[4,16,256]{2,1,0:T(8,128)S(1)} %shard_map.69.refs_5_), channel_id=1, source_target_pairs={{1,0},{0,1},{3,2},{2,3},{5,4},{4,5},{7,6},{6,7},{9,8},{8,9},{11,10... | collective-permute-start | bytes 196616 | tf_op jit(solution)/shard_map/ppermute | solution.py:175
  20.3 4.9 %collective-permute-start.11 = (f32[16,128]{1,0:T(8,128)S(1)}, f32[16,128]{1,0:T(8,128)S(1)}, u32[]{:S(2)}, u32[]{:S(2)}) collective-permute-start(f32[16,128]{1,0:T(8,128)S(1)} %get-tuple-element.18.refs_0_), channel_id=1, source_target_pairs={{13,0},{12,1},{9,4},{8,5},{5,8},{4,9},{1,12},{0,13},{15,2},{14,3},... | collective-permute-start | bytes 24584 | tf_op jit(solution)/shard_map/ppermute | solution.py:190
  23.0 4.0 %collective-permute-start.10 = (f32[16,128]{1,0:T(8,128)S(1)}, f32[16,128]{1,0:T(8,128)S(1)}, u32[]{:S(2)}, u32[]{:S(2)}) collective-permute-start(f32[16,128]{1,0:T(8,128)S(1)} %get-tuple-element.18.refs_0_), channel_id=1, source_target_pairs={{9,0},{8,1},{13,4},{12,5},{1,8},{0,9},{5,12},{4,13},{11,2},{10,3},... | collective-permute-start | bytes 24584 | tf_op jit(solution)/shard_map/ppermute | solution.py:190
  23.0 4.0 %collective-permute-start.9 = (f32[16,128]{1,0:T(8,128)S(1)}, f32[16,128]{1,0:T(8,128)S(1)}, u32[]{:S(2)}, u32[]{:S(2)}) collective-permute-start(f32[16,128]{1,0:T(8,128)S(1)} %get-tuple-element.18.refs_0_), channel_id=1, source_target_pairs={{5,0},{4,1},{1,4},{0,5},{13,8},{12,9},{9,12},{8,13},{7,2},{6,3},{3... | collective-permute-start | bytes 24584 | tf_op jit(solution)/shard_map/ppermute | solution.py:190

commit v25 on v19

--- a/solution.py
+++ b/solution.py
@@ -51,51 +51,64 @@
     return jnp.concatenate([scaled, norm_rows(scaled, 1)], axis=0)
 
 
-def prepare_kernel(feature_count, plane_count, *refs):
-    plane_refs, line_refs = refs[:plane_count], refs[plane_count:-5]
-    noise_ref, probes_ref, rows_ref, columns_ref, start_ref = refs[-5:]
-    start_ref[...] = noise_ref[...] * probes_ref[...]
-    for number, ref in enumerate(plane_refs):
-        rows_ref[number] = rows_of(ref, feature_count)
-    for number, ref in enumerate(line_refs):
-        columns_ref[number] = columns_of(ref[...], feature_count)
+def product(columns, probes, rows):
+    exponent = jnp.dot(columns, rows, preferred_element_type=jnp.float32)
+    weights = jnp.exp(exponent).astype(jnp.bfloat16)
+    return jnp.dot(probes, weights, preferred_element_type=jnp.float32)
+
+
+def side_by_side(refs, feature_count):
+    return jnp.concatenate([rows_of(ref, feature_count) for ref in refs], axis=1)
+
+
+def near_kernel(feature_count, *refs):
+    plane_refs, line_refs = refs[:2], refs[2:-5]
+    noise_ref, probes_ref, rows_ref, columns_ref, total_ref = refs[-5:]
+    rows = side_by_side(plane_refs, feature_count)
+    rows_ref[...] = rows
+    start = noise_ref[...] * probes_ref[...]
+    total = jnp.concatenate([start, jnp.zeros_like(start)], axis=1)
+    if line_refs:
+        columns = [columns_of(ref[...], feature_count) for ref in line_refs]
+        for number, value in enumerate(columns):
+            columns_ref[number] = value
+        probes = jnp.concatenate([ref[feature_count:, :] for ref in line_refs], axis=1)
+        total += product(jnp.concatenate(columns, axis=0), probes, rows)
+    total_ref[...] = total
 
 
 def image_kernel(feature_count, plane_count, *refs):
-    rows_ref, start_ref = refs[:2]
+    rows_ref, total_ref = refs[:2]
     plane_refs = refs[2:plane_count]
     columns_ref, *line_refs = refs[plane_count:-1]
     partial_ref = refs[-1]
-    rows = [rows_ref[number] for number in range(2)]
-    rows += [rows_of(ref, feature_count) for ref in plane_refs]
-    totals = [start_ref[...]]
-    totals += [jnp.zeros(start_ref.shape, jnp.float32)] * (plane_count - 1)
-
-    def add_columns(columns, probes, totals):
-        result = []
-        for own, total in zip(rows, totals):
-            exponent = jnp.dot(columns, own, preferred_element_type=jnp.float32)
-            weights = jnp.exp(exponent).astype(jnp.bfloat16)
-            result.append(total + jnp.dot(probes, weights, preferred_element_type=jnp.float32))
-        return result
-
+    width = partial_ref.shape[2]
+    rows = [rows_ref[...]]
+    for place in range(0, len(plane_refs), 2):
+        rows.append(side_by_side(plane_refs[place : place + 2], feature_count))
+    totals = [total_ref[...]] + [jnp.zeros(total_ref.shape, jnp.float32)] * (len(rows) - 1)
     if len(line_refs[0].shape) == 2:
         *early, late = [ref[...] for ref in line_refs]
+        late_columns = columns_of(late, feature_count)
         columns = [columns_ref[number] for number in range(len(early))]
-        columns = jnp.concatenate(columns + [columns_of(late, feature_count)], axis=0)
-        probes = [block[feature_count:, :] for block in early + [late]]
-        totals = add_columns(columns, jnp.concatenate(probes, axis=1), totals)
+        columns = jnp.concatenate(columns + [late_columns], axis=0)
+        probes = jnp.concatenate([block[feature_count:, :] for block in early + [late]], axis=1)
+        near = totals[0] + product(late_columns, late[feature_count:, :], rows[0])
+        totals = [near] + [product(columns, probes, pair) for pair in rows[1:]]
     else:
 
         def add_block(number, totals):
             block = line_refs[0][number]
-            return add_columns(
-                columns_of(block, feature_count), block[feature_count:, :], totals
-            )
+            columns = columns_of(block, feature_count)
+            return [
+                total + product(columns, block[feature_count:, :], pair)
+                for pair, total in zip(rows, totals)
+            ]
 
         totals = lax.fori_loop(0, line_refs[0].shape[0], add_block, totals)
-    for number, total in enumerate(totals):
-        partial_ref[number] = total
+    for number in range(plane_count):
+        place = number % 2 * width
+        partial_ref[number] = totals[number // 2][:, place : place + width]
 
 
 def combine_kernel(feature_count, plane_count, *refs):
@@ -212,12 +225,12 @@
             early, late = [], lines[0]
         depth = feature_count + 2 * HALF
         work = plane_count * width * width
-        rows, columns, start = pl.pallas_call(
-            lambda *refs: prepare_kernel(feature_count, 2, *refs),
+        rows, columns, total = pl.pallas_call(
+            lambda *refs: near_kernel(feature_count, *refs),
             out_shape=(
-                jax.ShapeDtypeStruct((2, depth, width), jnp.bfloat16),
+                jax.ShapeDtypeStruct((depth, 2 * width), jnp.bfloat16),
                 jax.ShapeDtypeStruct((max(len(early), 1), width, depth), jnp.bfloat16),
-                jax.ShapeDtypeStruct(probes.shape, jnp.float32),
+                jax.ShapeDtypeStruct((probe_count, 2 * width), jnp.float32),
             ),
             compiler_params=VMEM,
             cost_estimate=pl.CostEstimate(
@@ -228,7 +241,7 @@
             lambda *refs: image_kernel(feature_count, plane_count, *refs),
             out_shape=jax.ShapeDtypeStruct((plane_count, probe_count, width), jnp.float32),
             compiler_params=VMEM,
-        )(rows, start, *planes[2:], columns, *early, late)
+        )(rows, total, *planes[2:], columns, *early, late)
         partials = everywhere(partial, PLANE, plane_count)
         image, sums = pl.pallas_call(
             lambda *refs: combine_kernel(feature_count, plane_count, *refs),

time: 28.4 us -> 27.8 us (0.979)
  Pallas kernels: 2.86 us -> 2.39 us
    pallas_call x1, Pallas kernels: 1.77 us -> 0.85 us  [local(): pl.pallas_call(lambda *refs: image_kernel(feature_count, plane_count, *re...]
    pallas_call x1, Pallas kernels: 0.2 us -> 0.65 us  [local(): pl.pallas_call(lambda *refs: near_kernel(feature_count, *refs), out_shape...]
  transfers between devices with their start and end apart: 12 -> 12, of which waited for: 8 -> 7; matrix products, arithmetic and copies ran while one was open for 0% -> 0% of each run, Pallas kernels for 1% -> 2%
where the time goes in v25:
time: 27.8 us; the launch traced here: 27.7 us
  starting transfers between devices  13.1 us (47%)
  waiting for transfers between devices  10.6 us (38%)
  Pallas kernels  2.39 us (9%)
  other arithmetic  0.93 us (3%)
  between operations  0.68 us (2%)
    ppermute x6, starting transfers between devices, along_line(): blocks.append(lax.ppermute(value, LINE + ('sub',), pairs))  8.42 us
    ppermute x6, waiting for transfers between devices, along_line(): blocks.append(lax.ppermute(value, LINE + ('sub',), pairs))  6.93 us
    ppermute x6, starting transfers between devices, everywhere(): lax.ppermute(value, axes, [(source_of(i, step, count), i) for i in range(...  4.69 us
    ppermute x6, waiting for transfers between devices, everywhere(): lax.ppermute(value, axes, [(source_of(i, step, count), i) for i in range(...  3.62 us
    convert_element_type x1, other arithmetic, local(): (features.astype(jnp.float32) / lengthscale[:, None]).astype(jnp.bfloat16)  0.93 us
    pallas_call x1, Pallas kernels, local(): pl.pallas_call(lambda *refs: image_kernel(feature_count, plane_count, *re...  0.85 us
    pallas_call x1, Pallas kernels, local(): pl.pallas_call(finish_kernel, out_shape=outs, compiler_params=VMEM)  0.77 us
    pallas_call x1, Pallas kernels, local(): pl.pallas_call(lambda *refs: near_kernel(feature_count, *refs), out_shape...  0.65 us
  transfers between devices with their start and end apart: 12, of which 7 were waited for; matrix products, arithmetic and copies ran while one was open for 0% of the time, Pallas kernels for 2%

profile of v25, /device:TPU:0, one launch (start us, length us, event | category | flops | bytes accessed | tf_op | source)
XLA Modules:
  0.0 27.7 jit_solution(2446822501746997303)
XLA Ops:
  0.6 0.0 copy-start
  0.6 0.9 %divide_convert_fusion.scaled_ref = bf16[128,256]{1,0:T(8,128)(2,1)S(1)} fusion(bf16[128,256]{1,0:T(8,128)(2,1)} %param.4, f32[128]{0:T(128)} %param.5), kind=kLoop, calls=%fused_computation | loop fusion | flops 98304 | bytes 131584 | tf_op jit(solution)/shard_map/convert_element_type | solution.py:211
  1.6 0.0 copy-done
  1.6 0.5 %collective-permute-start = (bf16[160,256]{1,0:T(8,128)(2,1)S(1)}, bf16[160,256]{1,0:T(8,128)(2,1)S(1)}, u32[]{:S(2)}, u32[]{:S(2)}) collective-permute-start(bf16[160,256]{1,0:T(8,128)(2,1)S(1)} %get-tuple-element.10.refs_0_), channel_id=1, source_target_pairs={{1,0},{0,1},{3,2},{2,3},{5,4},{4,5},{7,6},{6,7},{9,8},{8,9},{11,10... | collective-permute-start | bytes 245768 | tf_op jit(solution)/shard_map/ppermute | solution.py:177
  2.1 0.0 copy-start.1
  2.1 4.7 %collective-permute-start.4 = (bf16[144,256]{1,0:T(8,128)(2,1)S(1)}, bf16[144,256]{1,0:T(8,128)(2,1)S(1)}, u32[]{:S(2)}, u32[]{:S(2)}) collective-permute-start(bf16[144,256]{1,0:T(8,128)(2,1)S(1)} %get-tuple-element.11.refs_2_.refs_5_), channel_id=1, source_target_pairs={{13,0},{12,1},{9,4},{8,5},{5,8},{4,9},{1,12},{0,13},{15,2},{14,3},... | collective-permute-start | bytes 221192 | tf_op jit(solution)/shard_map/ppermute | solution.py:192
  6.9 0.0 collective-permute-start.3
  6.9 1.5 %collective-permute-start.1 = (bf16[160,256]{1,0:T(8,128)(2,1)S(1)}, bf16[160,256]{1,0:T(8,128)(2,1)S(1)}, u32[]{:S(2)}, u32[]{:S(2)}) collective-permute-start(bf16[160,256]{1,0:T(8,128)(2,1)S(1)} %get-tuple-element.10.refs_0_), channel_id=1, source_target_pairs={{2,0},{0,2},{3,1},{1,3},{6,4},{4,6},{7,5},{5,7},{10,8},{8,10},{11,... | collective-permute-start | bytes 245768 | tf_op jit(solution)/shard_map/ppermute | solution.py:177
  8.4 0.0 collective-permute-done.refs_1_
  8.4 0.5 %collective-permute-start.2 = (bf16[160,256]{1,0:T(8,128)(2,1)S(1)}, bf16[160,256]{1,0:T(8,128)(2,1)S(1)}, u32[]{:S(2)}, u32[]{:S(2)}) collective-permute-start(bf16[160,256]{1,0:T(8,128)(2,1)S(1)} %collective-permute-done.refs_1_), channel_id=1, source_target_pairs={{2,0},{0,2},{3,1},{1,3},{6,4},{4,6},{7,5},{5,7},{10,8},{8,10},{11,... | collective-permute-start | bytes 245768 | tf_op jit(solution)/shard_map/ppermute | solution.py:177
  8.9 0.0 collective-permute-start.5
  8.9 0.6 %collective-permute-done.4.refs_4_.refs_7_ = bf16[144,256]{1,0:T(8,128)(2,1)S(1)} collective-permute-done((bf16[144,256]{1,0:T(8,128)(2,1)S(1)}, bf16[144,256]{1,0:T(8,128)(2,1)S(1)}, u32[]{:S(2)}, u32[]{:S(2)}) %collective-permute-start.4) | collective-permute-done | bytes 73760 | tf_op jit(solution)/shard_map/ppermute | solution.py:192
  9.5 3.6 %collective-permute-done.3.refs_3_.refs_6_ = bf16[144,256]{1,0:T(8,128)(2,1)S(1)} collective-permute-done((bf16[144,256]{1,0:T(8,128)(2,1)S(1)}, bf16[144,256]{1,0:T(8,128)(2,1)S(1)}, u32[]{:S(2)}, u32[]{:S(2)}) %collective-permute-start.3) | collective-permute-done | bytes 73760 | tf_op jit(solution)/shard_map/ppermute | solution.py:192
  13.1 0.0 copy-done.1
  13.1 0.6 %shard_map.68 = (bf16[144,512]{1,0:T(8,128)(2,1)S(1)}, bf16[3,256,144]{2,1,0:T(8,128)(2,1)S(1)}, f32[16,512]{1,0:T(8,128)S(1)}) custom-call(bf16[160,256]{1,0:T(8,128)(2,1)S(1)} %get-tuple-element.10.refs_0_, bf16[160,256]{1,0:T(8,128)(2,1)S(1)} %collective-permute-done.refs_1_, bf16[144,256]{1,0:T(8,128)(2,1)S(1)} %get-tuple-element.11.refs_2_.refs_5_, ...), custom_call_target="tpu_custom_call" | custom-call | flops 226492416 | bytes 4096 | tf_op jit(solution)/shard_map/pallas_call | solution.py:228
  13.7 0.9 %collective-permute-done.5.refs_8_ = bf16[144,256]{1,0:T(8,128)(2,1)S(1)} collective-permute-done((bf16[144,256]{1,0:T(8,128)(2,1)S(1)}, bf16[144,256]{1,0:T(8,128)(2,1)S(1)}, u32[]{:S(2)}, u32[]{:S(2)}) %collective-permute-start.5) | collective-permute-done | bytes 73760 | tf_op jit(solution)/shard_map/ppermute | solution.py:192
  14.6 0.0 collective-permute-done.1.refs_2_
  14.7 0.0 collective-permute-done.2.refs_3_
  14.7 0.8 %shard_map.69.refs_5_ = f32[4,16,256]{2,1,0:T(8,128)S(1)} custom-call(bf16[144,512]{1,0:T(8,128)(2,1)S(1)} %get-tuple-element.12.refs_0_, f32[16,512]{1,0:T(8,128)S(1)} %get-tuple-element.13.refs_1_, bf16[160,256]{1,0:T(8,128)(2,1)S(1)} %collective-permute-done.1.refs_2_, bf16[160,256]{1,0:T(8,128)(2,1)S(1)} %collective-permute-done.2.refs_3_, ...), custom_call_target="tpu_custom_call" | custom-call | tf_op jit(solution)/shard_map/pallas_call | solution.py:240
  15.5 1.5 %collective-permute-start.8 = (f32[4,16,256]{2,1,0:T(8,128)S(1)}, f32[4,16,256]{2,1,0:T(8,128)S(1)}, u32[]{:S(2)}, u32[]{:S(2)}) collective-permute-start(f32[4,16,256]{2,1,0:T(8,128)S(1)} %shard_map.69.refs_5_), channel_id=1, source_target_pairs={{2,0},{3,1},{0,2},{1,3},{6,4},{7,5},{4,6},{5,7},{10,8},{11,9},{8,1... | collective-permute-start | bytes 196616 | tf_op jit(solution)/shard_map/ppermute | solution.py:177
  17.0 0.0 collective-permute-start.7
  17.0 0.6 %collective-permute-start.6 = (f32[4,16,256]{2,1,0:T(8,128)S(1)}, f32[4,16,256]{2,1,0:T(8,128)S(1)}, u32[]{:S(2)}, u32[]{:S(2)}) collective-permute-start(f32[4,16,256]{2,1,0:T(8,128)S(1)} %shard_map.69.refs_5_), channel_id=1, source_target_pairs={{1,0},{0,1},{3,2},{2,3},{5,4},{4,5},{7,6},{6,7},{9,8},{8,9},{11,10... | collective-permute-start | bytes 196616 | tf_op jit(solution)/shard_map/ppermute | solution.py:177
  17.7 2.1 %collective-permute-done.8.refs_8_ = f32[4,16,256]{2,1,0:T(8,128)S(1)} collective-permute-done((f32[4,16,256]{2,1,0:T(8,128)S(1)}, f32[4,16,256]{2,1,0:T(8,128)S(1)}, u32[]{:S(2)}, u32[]{:S(2)}) %collective-permute-start.8) | collective-permute-done | bytes 65568 | tf_op jit(solution)/shard_map/ppermute | solution.py:177
  19.8 1.5 %collective-permute-done.7.refs_7_ = f32[4,16,256]{2,1,0:T(8,128)S(1)} collective-permute-done((f32[4,16,256]{2,1,0:T(8,128)S(1)}, f32[4,16,256]{2,1,0:T(8,128)S(1)}, u32[]{:S(2)}, u32[]{:S(2)}) %collective-permute-start.7) | collective-permute-done | bytes 65568 | tf_op jit(solution)/shard_map/ppermute | solution.py:177
  21.3 0.0 collective-permute-done.6.refs_6_
  21.3 0.1 shard_map.70
  21.4 1.5 %collective-permute-start.11 = (f32[16,128]{1,0:T(8,128)S(1)}, f32[16,128]{1,0:T(8,128)S(1)}, u32[]{:S(2)}, u32[]{:S(2)}) collective-permute-start(f32[16,128]{1,0:T(8,128)S(1)} %get-tuple-element.16.refs_0_), channel_id=1, source_target_pairs={{13,0},{12,1},{9,4},{8,5},{5,8},{4,9},{1,12},{0,13},{15,2},{14,3},... | collective-permute-start | bytes 24584 | tf_op jit(solution)/shard_map/ppermute | solution.py:192
  22.9 0.0 collective-permute-start.10
  22.9 2.1 %collective-permute-start.9 = (f32[16,128]{1,0:T(8,128)S(1)}, f32[16,128]{1,0:T(8,128)S(1)}, u32[]{:S(2)}, u32[]{:S(2)}) collective-permute-start(f32[16,128]{1,0:T(8,128)S(1)} %get-tuple-element.16.refs_0_), channel_id=1, source_target_pairs={{5,0},{4,1},{1,4},{0,5},{13,8},{12,9},{9,12},{8,13},{7,2},{6,3},{3... | collective-permute-start | bytes 24584 | tf_op jit(solution)/shard_map/ppermute | solution.py:192
  25.1 1.2 %collective-permute-done.11.refs_3_ = f32[16,128]{1,0:T(8,128)S(1)} collective-permute-done((f32[16,128]{1,0:T(8,128)S(1)}, f32[16,128]{1,0:T(8,128)S(1)}, u32[]{:S(2)}, u32[]{:S(2)}) %collective-permute-start.11) | collective-permute-done | bytes 8224 | tf_op jit(solution)/shard_map/ppermute | solution.py:192
  26.2 0.6 %collective-permute-done.10.refs_2_ = f32[16,128]{1,0:T(8,128)S(1)} collective-permute-done((f32[16,128]{1,0:T(8,128)S(1)}, f32[16,128]{1,0:T(8,128)S(1)}, u32[]{:S(2)}, u32[]{:S(2)}) %collective-permute-start.10) | collective-permute-done | bytes 8224 | tf_op jit(solution)/shard_map/ppermute | solution.py:192
  26.9 0.0 collective-permute-done.9.refs_1_
  26.9 0.8 %shard_map.71 = (f32[16,256]{1,0:T(8,128)}, f32[16,256]{1,0:T(8,128)}, f32[16,256]{1,0:T(8,128)}) custom-call(f32[16,256]{1,0:T(8,128)S(1)} %get-tuple-element.15.image_ref, f32[16,256]{1,0:T(8,128)S(1)} %copy-done, f32[16,128]{1,0:T(8,128)S(1)} %get-tuple-element.16.refs_0_, f32[16,128]{1,0:T(8,128)S(1)} %collective-permute-done.9.refs_1_, ...), custom_call_target="tpu_custom_call" | custom-call | tf_op jit(solution)/shard_map/pallas_call | solution.py:255
  (1 shorter events, 0.0 us)
Async XLA Ops:
  0.6 1.0 %copy-start = (f32[16,256]{1,0:T(8,128)S(1)}, f32[16,256]{1,0:T(8,128)}, u32[]{:S(2)}) copy-start(f32[16,256]{1,0:T(8,128)} %probes_ref.3) | copy-start | bytes 49156
  1.6 6.7 %collective-permute-start = (bf16[160,256]{1,0:T(8,128)(2,1)S(1)}, bf16[160,256]{1,0:T(8,128)(2,1)S(1)}, u32[]{:S(2)}, u32[]{:S(2)}) collective-permute-start(bf16[160,256]{1,0:T(8,128)(2,1)S(1)} %get-tuple-element.10.refs_0_), channel_id=1, source_target_pairs={{1,0},{0,1},{3,2},{2,3},{5,4},{4,5},{7,6},{6,7},{9,8},{8,9},{11,10... | collective-permute-start | bytes 245768 | tf_op jit(solution)/shard_map/ppermute | solution.py:177
  2.1 10.9 %copy-start.1 = (f32[256]{0:T(256)S(1)}, f32[256]{0:T(256)}, u32[]{:S(2)}) copy-start(f32[256]{0:T(256)} %param.6) | copy-start | bytes 3076
  2.1 7.4 %collective-permute-start.4 = (bf16[144,256]{1,0:T(8,128)(2,1)S(1)}, bf16[144,256]{1,0:T(8,128)(2,1)S(1)}, u32[]{:S(2)}, u32[]{:S(2)}) collective-permute-start(bf16[144,256]{1,0:T(8,128)(2,1)S(1)} %get-tuple-element.11.refs_2_.refs_5_), channel_id=1, source_target_pairs={{13,0},{12,1},{9,4},{8,5},{5,8},{4,9},{1,12},{0,13},{15,2},{14,3},... | collective-permute-start | bytes 221192 | tf_op jit(solution)/shard_map/ppermute | solution.py:192
  6.9 6.2 %collective-permute-start.3 = (bf16[144,256]{1,0:T(8,128)(2,1)S(1)}, bf16[144,256]{1,0:T(8,128)(2,1)S(1)}, u32[]{:S(2)}, u32[]{:S(2)}) collective-permute-start(bf16[144,256]{1,0:T(8,128)(2,1)S(1)} %get-tuple-element.11.refs_2_.refs_5_), channel_id=1, source_target_pairs={{9,0},{8,1},{13,4},{12,5},{1,8},{0,9},{5,12},{4,13},{11,2},{10,3},... | collective-permute-start | bytes 221192 | tf_op jit(solution)/shard_map/ppermute | solution.py:192
  6.9 7.8 %collective-permute-start.1 = (bf16[160,256]{1,0:T(8,128)(2,1)S(1)}, bf16[160,256]{1,0:T(8,128)(2,1)S(1)}, u32[]{:S(2)}, u32[]{:S(2)}) collective-permute-start(bf16[160,256]{1,0:T(8,128)(2,1)S(1)} %get-tuple-element.10.refs_0_), channel_id=1, source_target_pairs={{2,0},{0,2},{3,1},{1,3},{6,4},{4,6},{7,5},{5,7},{10,8},{8,10},{11,... | collective-permute-start | bytes 245768 | tf_op jit(solution)/shard_map/ppermute | solution.py:177
  8.4 6.3 %collective-permute-start.2 = (bf16[160,256]{1,0:T(8,128)(2,1)S(1)}, bf16[160,256]{1,0:T(8,128)(2,1)S(1)}, u32[]{:S(2)}, u32[]{:S(2)}) collective-permute-start(bf16[160,256]{1,0:T(8,128)(2,1)S(1)} %collective-permute-done.refs_1_), channel_id=1, source_target_pairs={{2,0},{0,2},{3,1},{1,3},{6,4},{4,6},{7,5},{5,7},{10,8},{8,10},{11,... | collective-permute-start | bytes 245768 | tf_op jit(solution)/shard_map/ppermute | solution.py:177
  8.9 5.8 %collective-permute-start.5 = (bf16[144,256]{1,0:T(8,128)(2,1)S(1)}, bf16[144,256]{1,0:T(8,128)(2,1)S(1)}, u32[]{:S(2)}, u32[]{:S(2)}) collective-permute-start(bf16[144,256]{1,0:T(8,128)(2,1)S(1)} %get-tuple-element.11.refs_2_.refs_5_), channel_id=1, source_target_pairs={{5,0},{4,1},{1,4},{0,5},{13,8},{12,9},{9,12},{8,13},{7,2},{6,3},{3... | collective-permute-start | bytes 221192 | tf_op jit(solution)/shard_map/ppermute | solution.py:192
  15.5 4.3 %collective-permute-start.8 = (f32[4,16,256]{2,1,0:T(8,128)S(1)}, f32[4,16,256]{2,1,0:T(8,128)S(1)}, u32[]{:S(2)}, u32[]{:S(2)}) collective-permute-start(f32[4,16,256]{2,1,0:T(8,128)S(1)} %shard_map.69.refs_5_), channel_id=1, source_target_pairs={{2,0},{3,1},{0,2},{1,3},{6,4},{7,5},{4,6},{5,7},{10,8},{11,9},{8,1... | collective-permute-start | bytes 196616 | tf_op jit(solution)/shard_map/ppermute | solution.py:177
  17.0 4.3 %collective-permute-start.7 = (f32[4,16,256]{2,1,0:T(8,128)S(1)}, f32[4,16,256]{2,1,0:T(8,128)S(1)}, u32[]{:S(2)}, u32[]{:S(2)}) collective-permute-start(f32[4,16,256]{2,1,0:T(8,128)S(1)} %shard_map.69.refs_5_), channel_id=1, source_target_pairs={{3,0},{2,1},{1,2},{0,3},{7,4},{6,5},{5,6},{4,7},{11,8},{10,9},{9,1... | collective-permute-start | bytes 196616 | tf_op jit(solution)/shard_map/ppermute | solution.py:177
  17.0 4.3 %collective-permute-start.6 = (f32[4,16,256]{2,1,0:T(8,128)S(1)}, f32[4,16,256]{2,1,0:T(8,128)S(1)}, u32[]{:S(2)}, u32[]{:S(2)}) collective-permute-start(f32[4,16,256]{2,1,0:T(8,128)S(1)} %shard_map.69.refs_5_), channel_id=1, source_target_pairs={{1,0},{0,1},{3,2},{2,3},{5,4},{4,5},{7,6},{6,7},{9,8},{8,9},{11,10... | collective-permute-start | bytes 196616 | tf_op jit(solution)/shard_map/ppermute | solution.py:177
  21.4 4.9 %collective-permute-start.11 = (f32[16,128]{1,0:T(8,128)S(1)}, f32[16,128]{1,0:T(8,128)S(1)}, u32[]{:S(2)}, u32[]{:S(2)}) collective-permute-start(f32[16,128]{1,0:T(8,128)S(1)} %get-tuple-element.16.refs_0_), channel_id=1, source_target_pairs={{13,0},{12,1},{9,4},{8,5},{5,8},{4,9},{1,12},{0,13},{15,2},{14,3},... | collective-permute-start | bytes 24584 | tf_op jit(solution)/shard_map/ppermute | solution.py:192
  22.9 4.0 %collective-permute-start.10 = (f32[16,128]{1,0:T(8,128)S(1)}, f32[16,128]{1,0:T(8,128)S(1)}, u32[]{:S(2)}, u32[]{:S(2)}) collective-permute-start(f32[16,128]{1,0:T(8,128)S(1)} %get-tuple-element.16.refs_0_), channel_id=1, source_target_pairs={{9,0},{8,1},{13,4},{12,5},{1,8},{0,9},{5,12},{4,13},{11,2},{10,3},... | collective-permute-start | bytes 24584 | tf_op jit(solution)/shard_map/ppermute | solution.py:192
  22.9 4.0 %collective-permute-start.9 = (f32[16,128]{1,0:T(8,128)S(1)}, f32[16,128]{1,0:T(8,128)S(1)}, u32[]{:S(2)}, u32[]{:S(2)}) collective-permute-start(f32[16,128]{1,0:T(8,128)S(1)} %get-tuple-element.16.refs_0_), channel_id=1, source_target_pairs={{5,0},{4,1},{1,4},{0,5},{13,8},{12,9},{9,12},{8,13},{7,2},{6,3},{3... | collective-permute-start | bytes 24584 | tf_op jit(solution)/shard_map/ppermute | solution.py:192

commit v26 on v20

--- a/solution.py
+++ b/solution.py
@@ -9,7 +9,7 @@
 LINE = ("blk",)
 DIRECT = 8
 VMEM = pltpu.CompilerParams(vmem_limit_bytes=40 * 1024 * 1024)
-PARTIALS, PARTIALS_BACK = (0, 1, 3, 2), (0, 1, 3, 2)
+PARTIALS, PARTIALS_BACK = (0, 1, 2, 3), (0, 1, 2, 3)
 SUMS = (0, 1, 2, 3)
 HALF = 8
 

time: 27.6 us -> 27.6 us (level)
  starting transfers between devices: 13.1 us -> 12.7 us
  waiting for transfers between devices: 10.6 us -> 11 us
    ppermute x6, waiting for transfers between devices: 3.61 us -> 3.94 us  [everywhere(): lax.ppermute(value, axes, [(source_of(i, step, count), i) for i in range(...]
    ppermute x6, starting transfers between devices: 4.7 us -> 4.42 us  [everywhere(): lax.ppermute(value, axes, [(source_of(i, step, count), i) for i in range(...]
  transfers between devices with their start and end apart: 12 -> 12, of which waited for: 8 -> 6; matrix products, arithmetic and copies ran while one was open for 0% -> 0% of each run, Pallas kernels for 1% -> 1%
where the time goes in v26:
time: 27.6 us; the launch traced here: 27.4 us
  starting transfers between devices  12.7 us (46%)
  waiting for transfers between devices  11 us (40%)
  Pallas kernels  2.07 us (7%)
  other arithmetic  0.93 us (3%)
  between operations  0.69 us (2%)
    ppermute x6, starting transfers between devices, along_line(): blocks.append(lax.ppermute(value, LINE + ('sub',), pairs))  8.26 us
    ppermute x6, waiting for transfers between devices, along_line(): blocks.append(lax.ppermute(value, LINE + ('sub',), pairs))  7.05 us
    ppermute x6, starting transfers between devices, everywhere(): lax.ppermute(value, axes, [(source_of(i, step, count), i) for i in range(...  4.42 us
    ppermute x6, waiting for transfers between devices, everywhere(): lax.ppermute(value, axes, [(source_of(i, step, count), i) for i in range(...  3.94 us
    pallas_call x1, Pallas kernels, local(): pl.pallas_call(lambda *refs: image_kernel(feature_count, plane_count, *re...  0.98 us
    convert_element_type x1, other arithmetic, local(): (features.astype(jnp.float32) / lengthscale[:, None]).astype(jnp.bfloat16)  0.93 us
    pallas_call x1, Pallas kernels, local(): pl.pallas_call(finish_kernel, out_shape=outs, compiler_params=VMEM)  0.77 us
  transfers between devices with their start and end apart: 12, of which 6 were waited for; matrix products, arithmetic and copies ran while one was open for 0% of the time, Pallas kernels for 1%

profile of v26, /device:TPU:0, one launch (start us, length us, event | category | flops | bytes accessed | tf_op | source)
XLA Modules:
  0.0 27.4 jit_solution(6152940611470785049)
XLA Ops:
  0.6 0.0 copy-start
  0.6 0.9 %divide_convert_fusion.scaled_ref = bf16[128,256]{1,0:T(8,128)(2,1)S(1)} fusion(bf16[128,256]{1,0:T(8,128)(2,1)} %param.4, f32[128]{0:T(128)} %param.5), kind=kLoop, calls=%fused_computation | loop fusion | flops 98304 | bytes 131584 | tf_op jit(solution)/shard_map/convert_element_type | solution.py:204
  1.6 0.0 copy-done
  1.6 0.5 %collective-permute-start = (bf16[160,256]{1,0:T(8,128)(2,1)S(1)}, bf16[160,256]{1,0:T(8,128)(2,1)S(1)}, u32[]{:S(2)}, u32[]{:S(2)}) collective-permute-start(bf16[160,256]{1,0:T(8,128)(2,1)S(1)} %get-tuple-element.10.refs_0_), channel_id=1, source_target_pairs={{1,0},{0,1},{3,2},{2,3},{5,4},{4,5},{7,6},{6,7},{9,8},{8,9},{11,10... | collective-permute-start | bytes 245768 | tf_op jit(solution)/shard_map/ppermute | solution.py:170
  2.1 0.0 copy-start.1
  2.1 4.7 %collective-permute-start.4 = (bf16[144,256]{1,0:T(8,128)(2,1)S(1)}, bf16[144,256]{1,0:T(8,128)(2,1)S(1)}, u32[]{:S(2)}, u32[]{:S(2)}) collective-permute-start(bf16[144,256]{1,0:T(8,128)(2,1)S(1)} %get-tuple-element.11.refs_2_.refs_5_), channel_id=1, source_target_pairs={{13,0},{12,1},{9,4},{8,5},{5,8},{4,9},{1,12},{0,13},{15,2},{14,3},... | collective-permute-start | bytes 221192 | tf_op jit(solution)/shard_map/ppermute | solution.py:185
  6.9 0.0 collective-permute-start.3
  6.9 1.5 %collective-permute-start.1 = (bf16[160,256]{1,0:T(8,128)(2,1)S(1)}, bf16[160,256]{1,0:T(8,128)(2,1)S(1)}, u32[]{:S(2)}, u32[]{:S(2)}) collective-permute-start(bf16[160,256]{1,0:T(8,128)(2,1)S(1)} %get-tuple-element.10.refs_0_), channel_id=1, source_target_pairs={{2,0},{0,2},{3,1},{1,3},{6,4},{4,6},{7,5},{5,7},{10,8},{8,10},{11,... | collective-permute-start | bytes 245768 | tf_op jit(solution)/shard_map/ppermute | solution.py:170
  8.4 0.0 collective-permute-done.refs_1_
  8.4 0.5 %collective-permute-start.2 = (bf16[160,256]{1,0:T(8,128)(2,1)S(1)}, bf16[160,256]{1,0:T(8,128)(2,1)S(1)}, u32[]{:S(2)}, u32[]{:S(2)}) collective-permute-start(bf16[160,256]{1,0:T(8,128)(2,1)S(1)} %collective-permute-done.refs_1_), channel_id=1, source_target_pairs={{2,0},{0,2},{3,1},{1,3},{6,4},{4,6},{7,5},{5,7},{10,8},{8,10},{11,... | collective-permute-start | bytes 245768 | tf_op jit(solution)/shard_map/ppermute | solution.py:170
  8.9 0.0 collective-permute-start.5
  8.9 0.6 %collective-permute-done.4.refs_4_.refs_7_ = bf16[144,256]{1,0:T(8,128)(2,1)S(1)} collective-permute-done((bf16[144,256]{1,0:T(8,128)(2,1)S(1)}, bf16[144,256]{1,0:T(8,128)(2,1)S(1)}, u32[]{:S(2)}, u32[]{:S(2)}) %collective-permute-start.4) | collective-permute-done | bytes 73760 | tf_op jit(solution)/shard_map/ppermute | solution.py:185
  9.5 3.6 %collective-permute-done.3.refs_3_.refs_6_ = bf16[144,256]{1,0:T(8,128)(2,1)S(1)} collective-permute-done((bf16[144,256]{1,0:T(8,128)(2,1)S(1)}, bf16[144,256]{1,0:T(8,128)(2,1)S(1)}, u32[]{:S(2)}, u32[]{:S(2)}) %collective-permute-start.3) | collective-permute-done | bytes 73760 | tf_op jit(solution)/shard_map/ppermute | solution.py:185
  13.1 0.0 copy-done.1
  13.1 0.2 shard_map.68
  13.3 1.4 %collective-permute-done.5.refs_8_ = bf16[144,256]{1,0:T(8,128)(2,1)S(1)} collective-permute-done((bf16[144,256]{1,0:T(8,128)(2,1)S(1)}, bf16[144,256]{1,0:T(8,128)(2,1)S(1)}, u32[]{:S(2)}, u32[]{:S(2)}) %collective-permute-start.5) | collective-permute-done | bytes 73760 | tf_op jit(solution)/shard_map/ppermute | solution.py:185
  14.6 0.0 collective-permute-done.1.refs_2_
  14.7 0.0 collective-permute-done.2.refs_3_
  14.7 1.0 %shard_map.69.refs_5_ = f32[4,16,256]{2,1,0:T(8,128)S(1)} custom-call(bf16[2,144,256]{2,1,0:T(8,128)(2,1)S(1)} %get-tuple-element.12.refs_0_, f32[16,256]{1,0:T(8,128)S(1)} %get-tuple-element.13.refs_1_, bf16[160,256]{1,0:T(8,128)(2,1)S(1)} %collective-permute-done.1.refs_2_, bf16[160,256]{1,0:T(8,128)(2,1)S(1)} %collective-permute-done.2.refs_3_, ...), custom_call_target="tpu_custom_call" | custom-call | tf_op jit(solution)/shard_map/pallas_call | solution.py:233
  15.6 1.1 %collective-permute-start.8 = (f32[4,16,256]{2,1,0:T(8,128)S(1)}, f32[4,16,256]{2,1,0:T(8,128)S(1)}, u32[]{:S(2)}, u32[]{:S(2)}) collective-permute-start(f32[4,16,256]{2,1,0:T(8,128)S(1)} %shard_map.69.refs_5_), channel_id=1, source_target_pairs={{3,0},{2,1},{1,2},{0,3},{7,4},{6,5},{5,6},{4,7},{11,8},{10,9},{9,1... | collective-permute-start | bytes 196616 | tf_op jit(solution)/shard_map/ppermute | solution.py:170
  16.7 0.5 %collective-permute-start.7 = (f32[4,16,256]{2,1,0:T(8,128)S(1)}, f32[4,16,256]{2,1,0:T(8,128)S(1)}, u32[]{:S(2)}, u32[]{:S(2)}) collective-permute-start(f32[4,16,256]{2,1,0:T(8,128)S(1)} %shard_map.69.refs_5_), channel_id=1, source_target_pairs={{2,0},{3,1},{0,2},{1,3},{6,4},{7,5},{4,6},{5,7},{10,8},{11,9},{8,1... | collective-permute-start | bytes 196616 | tf_op jit(solution)/shard_map/ppermute | solution.py:170
  17.2 0.3 collective-permute-start.6
  17.5 2.4 %collective-permute-done.8.refs_8_ = f32[4,16,256]{2,1,0:T(8,128)S(1)} collective-permute-done((f32[4,16,256]{2,1,0:T(8,128)S(1)}, f32[4,16,256]{2,1,0:T(8,128)S(1)}, u32[]{:S(2)}, u32[]{:S(2)}) %collective-permute-start.8) | collective-permute-done | bytes 65568 | tf_op jit(solution)/shard_map/ppermute | solution.py:170
  19.9 1.5 %collective-permute-done.7.refs_7_ = f32[4,16,256]{2,1,0:T(8,128)S(1)} collective-permute-done((f32[4,16,256]{2,1,0:T(8,128)S(1)}, f32[4,16,256]{2,1,0:T(8,128)S(1)}, u32[]{:S(2)}, u32[]{:S(2)}) %collective-permute-start.7) | collective-permute-done | bytes 65568 | tf_op jit(solution)/shard_map/ppermute | solution.py:170
  21.4 0.0 collective-permute-done.6.refs_6_
  21.4 0.1 shard_map.70
  21.6 0.0 collective-permute-start.11
  21.6 0.8 %collective-permute-start.10 = (f32[16,128]{1,0:T(8,128)S(1)}, f32[16,128]{1,0:T(8,128)S(1)}, u32[]{:S(2)}, u32[]{:S(2)}) collective-permute-start(f32[16,128]{1,0:T(8,128)S(1)} %get-tuple-element.16.refs_0_), channel_id=1, source_target_pairs={{9,0},{8,1},{13,4},{12,5},{1,8},{0,9},{5,12},{4,13},{11,2},{10,3},... | collective-permute-start | bytes 24584 | tf_op jit(solution)/shard_map/ppermute | solution.py:185
  22.4 2.7 %collective-permute-start.9 = (f32[16,128]{1,0:T(8,128)S(1)}, f32[16,128]{1,0:T(8,128)S(1)}, u32[]{:S(2)}, u32[]{:S(2)}) collective-permute-start(f32[16,128]{1,0:T(8,128)S(1)} %get-tuple-element.16.refs_0_), channel_id=1, source_target_pairs={{5,0},{4,1},{1,4},{0,5},{13,8},{12,9},{9,12},{8,13},{7,2},{6,3},{3... | collective-permute-start | bytes 24584 | tf_op jit(solution)/shard_map/ppermute | solution.py:185
  25.1 1.5 %collective-permute-done.11.refs_3_ = f32[16,128]{1,0:T(8,128)S(1)} collective-permute-done((f32[16,128]{1,0:T(8,128)S(1)}, f32[16,128]{1,0:T(8,128)S(1)}, u32[]{:S(2)}, u32[]{:S(2)}) %collective-permute-start.11) | collective-permute-done | bytes 8224 | tf_op jit(solution)/shard_map/ppermute | solution.py:185
  26.6 0.0 collective-permute-done.10.refs_2_
  26.6 0.0 collective-permute-done.9.refs_1_
  26.6 0.8 %shard_map.71 = (f32[16,256]{1,0:T(8,128)}, f32[16,256]{1,0:T(8,128)}, f32[16,256]{1,0:T(8,128)}) custom-call(f32[16,256]{1,0:T(8,128)S(1)} %get-tuple-element.15.image_ref, f32[16,256]{1,0:T(8,128)S(1)} %copy-done, f32[16,128]{1,0:T(8,128)S(1)} %get-tuple-element.16.refs_0_, f32[16,128]{1,0:T(8,128)S(1)} %collective-permute-done.9.refs_1_, ...), custom_call_target="tpu_custom_call" | custom-call | tf_op jit(solution)/shard_map/pallas_call | solution.py:248
  (1 shorter events, 0.0 us)
Async XLA Ops:
  0.6 1.0 %copy-start = (f32[16,256]{1,0:T(8,128)S(1)}, f32[16,256]{1,0:T(8,128)}, u32[]{:S(2)}) copy-start(f32[16,256]{1,0:T(8,128)} %probes_ref.3) | copy-start | bytes 49156
  1.6 6.7 %collective-permute-start = (bf16[160,256]{1,0:T(8,128)(2,1)S(1)}, bf16[160,256]{1,0:T(8,128)(2,1)S(1)}, u32[]{:S(2)}, u32[]{:S(2)}) collective-permute-start(bf16[160,256]{1,0:T(8,128)(2,1)S(1)} %get-tuple-element.10.refs_0_), channel_id=1, source_target_pairs={{1,0},{0,1},{3,2},{2,3},{5,4},{4,5},{7,6},{6,7},{9,8},{8,9},{11,10... | collective-permute-start | bytes 245768 | tf_op jit(solution)/shard_map/ppermute | solution.py:170
  2.1 10.9 %copy-start.1 = (f32[256]{0:T(256)S(1)}, f32[256]{0:T(256)}, u32[]{:S(2)}) copy-start(f32[256]{0:T(256)} %param.6) | copy-start | bytes 3076
  2.1 7.4 %collective-permute-start.4 = (bf16[144,256]{1,0:T(8,128)(2,1)S(1)}, bf16[144,256]{1,0:T(8,128)(2,1)S(1)}, u32[]{:S(2)}, u32[]{:S(2)}) collective-permute-start(bf16[144,256]{1,0:T(8,128)(2,1)S(1)} %get-tuple-element.11.refs_2_.refs_5_), channel_id=1, source_target_pairs={{13,0},{12,1},{9,4},{8,5},{5,8},{4,9},{1,12},{0,13},{15,2},{14,3},... | collective-permute-start | bytes 221192 | tf_op jit(solution)/shard_map/ppermute | solution.py:185
  6.9 6.2 %collective-permute-start.3 = (bf16[144,256]{1,0:T(8,128)(2,1)S(1)}, bf16[144,256]{1,0:T(8,128)(2,1)S(1)}, u32[]{:S(2)}, u32[]{:S(2)}) collective-permute-start(bf16[144,256]{1,0:T(8,128)(2,1)S(1)} %get-tuple-element.11.refs_2_.refs_5_), channel_id=1, source_target_pairs={{9,0},{8,1},{13,4},{12,5},{1,8},{0,9},{5,12},{4,13},{11,2},{10,3},... | collective-permute-start | bytes 221192 | tf_op jit(solution)/shard_map/ppermute | solution.py:185
  6.9 7.8 %collective-permute-start.1 = (bf16[160,256]{1,0:T(8,128)(2,1)S(1)}, bf16[160,256]{1,0:T(8,128)(2,1)S(1)}, u32[]{:S(2)}, u32[]{:S(2)}) collective-permute-start(bf16[160,256]{1,0:T(8,128)(2,1)S(1)} %get-tuple-element.10.refs_0_), channel_id=1, source_target_pairs={{2,0},{0,2},{3,1},{1,3},{6,4},{4,6},{7,5},{5,7},{10,8},{8,10},{11,... | collective-permute-start | bytes 245768 | tf_op jit(solution)/shard_map/ppermute | solution.py:170
  8.4 6.3 %collective-permute-start.2 = (bf16[160,256]{1,0:T(8,128)(2,1)S(1)}, bf16[160,256]{1,0:T(8,128)(2,1)S(1)}, u32[]{:S(2)}, u32[]{:S(2)}) collective-permute-start(bf16[160,256]{1,0:T(8,128)(2,1)S(1)} %collective-permute-done.refs_1_), channel_id=1, source_target_pairs={{2,0},{0,2},{3,1},{1,3},{6,4},{4,6},{7,5},{5,7},{10,8},{8,10},{11,... | collective-permute-start | bytes 245768 | tf_op jit(solution)/shard_map/ppermute | solution.py:170
  8.9 5.8 %collective-permute-start.5 = (bf16[144,256]{1,0:T(8,128)(2,1)S(1)}, bf16[144,256]{1,0:T(8,128)(2,1)S(1)}, u32[]{:S(2)}, u32[]{:S(2)}) collective-permute-start(bf16[144,256]{1,0:T(8,128)(2,1)S(1)} %get-tuple-element.11.refs_2_.refs_5_), channel_id=1, source_target_pairs={{5,0},{4,1},{1,4},{0,5},{13,8},{12,9},{9,12},{8,13},{7,2},{6,3},{3... | collective-permute-start | bytes 221192 | tf_op jit(solution)/shard_map/ppermute | solution.py:185
  15.6 4.3 %collective-permute-start.8 = (f32[4,16,256]{2,1,0:T(8,128)S(1)}, f32[4,16,256]{2,1,0:T(8,128)S(1)}, u32[]{:S(2)}, u32[]{:S(2)}) collective-permute-start(f32[4,16,256]{2,1,0:T(8,128)S(1)} %shard_map.69.refs_5_), channel_id=1, source_target_pairs={{3,0},{2,1},{1,2},{0,3},{7,4},{6,5},{5,6},{4,7},{11,8},{10,9},{9,1... | collective-permute-start | bytes 196616 | tf_op jit(solution)/shard_map/ppermute | solution.py:170
  16.7 4.7 %collective-permute-start.7 = (f32[4,16,256]{2,1,0:T(8,128)S(1)}, f32[4,16,256]{2,1,0:T(8,128)S(1)}, u32[]{:S(2)}, u32[]{:S(2)}) collective-permute-start(f32[4,16,256]{2,1,0:T(8,128)S(1)} %shard_map.69.refs_5_), channel_id=1, source_target_pairs={{2,0},{3,1},{0,2},{1,3},{6,4},{7,5},{4,6},{5,7},{10,8},{11,9},{8,1... | collective-permute-start | bytes 196616 | tf_op jit(solution)/shard_map/ppermute | solution.py:170
  17.2 4.2 %collective-permute-start.6 = (f32[4,16,256]{2,1,0:T(8,128)S(1)}, f32[4,16,256]{2,1,0:T(8,128)S(1)}, u32[]{:S(2)}, u32[]{:S(2)}) collective-permute-start(f32[4,16,256]{2,1,0:T(8,128)S(1)} %shard_map.69.refs_5_), channel_id=1, source_target_pairs={{1,0},{0,1},{3,2},{2,3},{5,4},{4,5},{7,6},{6,7},{9,8},{8,9},{11,10... | collective-permute-start | bytes 196616 | tf_op jit(solution)/shard_map/ppermute | solution.py:170
  21.6 5.0 %collective-permute-start.11 = (f32[16,128]{1,0:T(8,128)S(1)}, f32[16,128]{1,0:T(8,128)S(1)}, u32[]{:S(2)}, u32[]{:S(2)}) collective-permute-start(f32[16,128]{1,0:T(8,128)S(1)} %get-tuple-element.16.refs_0_), channel_id=1, source_target_pairs={{13,0},{12,1},{9,4},{8,5},{5,8},{4,9},{1,12},{0,13},{15,2},{14,3},... | collective-permute-start | bytes 24584 | tf_op jit(solution)/shard_map/ppermute | solution.py:185
  21.6 5.0 %collective-permute-start.10 = (f32[16,128]{1,0:T(8,128)S(1)}, f32[16,128]{1,0:T(8,128)S(1)}, u32[]{:S(2)}, u32[]{:S(2)}) collective-permute-start(f32[16,128]{1,0:T(8,128)S(1)} %get-tuple-element.16.refs_0_), channel_id=1, source_target_pairs={{9,0},{8,1},{13,4},{12,5},{1,8},{0,9},{5,12},{4,13},{11,2},{10,3},... | collective-permute-start | bytes 24584 | tf_op jit(solution)/shard_map/ppermute | solution.py:185
  22.4 4.2 %collective-permute-start.9 = (f32[16,128]{1,0:T(8,128)S(1)}, f32[16,128]{1,0:T(8,128)S(1)}, u32[]{:S(2)}, u32[]{:S(2)}) collective-permute-start(f32[16,128]{1,0:T(8,128)S(1)} %get-tuple-element.16.refs_0_), channel_id=1, source_target_pairs={{5,0},{4,1},{1,4},{0,5},{13,8},{12,9},{9,12},{8,13},{7,2},{6,3},{3... | collective-permute-start | bytes 24584 | tf_op jit(solution)/shard_map/ppermute | solution.py:185

commit v27 on v25

--- a/solution.py
+++ b/solution.py
@@ -9,7 +9,7 @@
 LINE = ("blk",)
 DIRECT = 8
 VMEM = pltpu.CompilerParams(vmem_limit_bytes=40 * 1024 * 1024)
-PARTIALS, PARTIALS_BACK = (0, 1, 3, 2), (0, 1, 3, 2)
+PARTIALS, PARTIALS_BACK = (0, 1, 2, 3), (0, 1, 2, 3)
 SUMS = (0, 1, 2, 3)
 HALF = 8
 

time: 27.8 us -> 27.6 us (level)
  starting transfers between devices: 13.1 us -> 12.7 us
    ppermute x6, waiting for transfers between devices: 3.62 us -> 3.94 us  [everywhere(): lax.ppermute(value, axes, [(source_of(i, step, count), i) for i in range(...]
    ppermute x6, starting transfers between devices: 4.69 us -> 4.41 us  [everywhere(): lax.ppermute(value, axes, [(source_of(i, step, count), i) for i in range(...]
where the time goes in v27:
time: 27.6 us; the launch traced here: 27.3 us
  starting transfers between devices  12.7 us (46%)
  waiting for transfers between devices  10.6 us (38%)
  Pallas kernels  2.38 us (9%)
  other arithmetic  0.93 us (3%)
  between operations  0.68 us (2%)
    ppermute x6, starting transfers between devices, along_line(): blocks.append(lax.ppermute(value, LINE + ('sub',), pairs))  8.26 us
    ppermute x6, waiting for transfers between devices, along_line(): blocks.append(lax.ppermute(value, LINE + ('sub',), pairs))  6.66 us
    ppermute x6, starting transfers between devices, everywhere(): lax.ppermute(value, axes, [(source_of(i, step, count), i) for i in range(...  4.41 us
    ppermute x6, waiting for transfers between devices, everywhere(): lax.ppermute(value, axes, [(source_of(i, step, count), i) for i in range(...  3.94 us
    convert_element_type x1, other arithmetic, local(): (features.astype(jnp.float32) / lengthscale[:, None]).astype(jnp.bfloat16)  0.93 us
    pallas_call x1, Pallas kernels, local(): pl.pallas_call(lambda *refs: image_kernel(feature_count, plane_count, *re...  0.85 us
    pallas_call x1, Pallas kernels, local(): pl.pallas_call(finish_kernel, out_shape=outs, compiler_params=VMEM)  0.77 us
    pallas_call x1, Pallas kernels, local(): pl.pallas_call(lambda *refs: near_kernel(feature_count, *refs), out_shape...  0.65 us
  transfers between devices with their start and end apart: 12, of which 7 were waited for; matrix products, arithmetic and copies ran while one was open for 0% of the time, Pallas kernels for 2%

profile of v27, /device:TPU:0, one launch (start us, length us, event | category | flops | bytes accessed | tf_op | source)
XLA Modules:
  0.0 27.3 jit_solution(12610015216277515188)
XLA Ops:
  0.6 0.0 copy-start
  0.6 0.9 %divide_convert_fusion.scaled_ref = bf16[128,256]{1,0:T(8,128)(2,1)S(1)} fusion(bf16[128,256]{1,0:T(8,128)(2,1)} %param.4, f32[128]{0:T(128)} %param.5), kind=kLoop, calls=%fused_computation | loop fusion | flops 98304 | bytes 131584 | tf_op jit(solution)/shard_map/convert_element_type | solution.py:211
  1.6 0.0 copy-done
  1.6 0.5 %collective-permute-start = (bf16[160,256]{1,0:T(8,128)(2,1)S(1)}, bf16[160,256]{1,0:T(8,128)(2,1)S(1)}, u32[]{:S(2)}, u32[]{:S(2)}) collective-permute-start(bf16[160,256]{1,0:T(8,128)(2,1)S(1)} %get-tuple-element.10.refs_0_), channel_id=1, source_target_pairs={{1,0},{0,1},{3,2},{2,3},{5,4},{4,5},{7,6},{6,7},{9,8},{8,9},{11,10... | collective-permute-start | bytes 245768 | tf_op jit(solution)/shard_map/ppermute | solution.py:177
  2.1 0.0 copy-start.1
  2.1 4.7 %collective-permute-start.4 = (bf16[144,256]{1,0:T(8,128)(2,1)S(1)}, bf16[144,256]{1,0:T(8,128)(2,1)S(1)}, u32[]{:S(2)}, u32[]{:S(2)}) collective-permute-start(bf16[144,256]{1,0:T(8,128)(2,1)S(1)} %get-tuple-element.11.refs_2_.refs_5_), channel_id=1, source_target_pairs={{13,0},{12,1},{9,4},{8,5},{5,8},{4,9},{1,12},{0,13},{15,2},{14,3},... | collective-permute-start | bytes 221192 | tf_op jit(solution)/shard_map/ppermute | solution.py:192
  6.9 0.0 collective-permute-start.3
  6.9 1.5 %collective-permute-start.1 = (bf16[160,256]{1,0:T(8,128)(2,1)S(1)}, bf16[160,256]{1,0:T(8,128)(2,1)S(1)}, u32[]{:S(2)}, u32[]{:S(2)}) collective-permute-start(bf16[160,256]{1,0:T(8,128)(2,1)S(1)} %get-tuple-element.10.refs_0_), channel_id=1, source_target_pairs={{2,0},{0,2},{3,1},{1,3},{6,4},{4,6},{7,5},{5,7},{10,8},{8,10},{11,... | collective-permute-start | bytes 245768 | tf_op jit(solution)/shard_map/ppermute | solution.py:177
  8.4 0.0 collective-permute-done.refs_1_
  8.4 0.5 %collective-permute-start.2 = (bf16[160,256]{1,0:T(8,128)(2,1)S(1)}, bf16[160,256]{1,0:T(8,128)(2,1)S(1)}, u32[]{:S(2)}, u32[]{:S(2)}) collective-permute-start(bf16[160,256]{1,0:T(8,128)(2,1)S(1)} %collective-permute-done.refs_1_), channel_id=1, source_target_pairs={{2,0},{0,2},{3,1},{1,3},{6,4},{4,6},{7,5},{5,7},{10,8},{8,10},{11,... | collective-permute-start | bytes 245768 | tf_op jit(solution)/shard_map/ppermute | solution.py:177
  8.9 0.0 collective-permute-start.5
  8.9 0.6 %collective-permute-done.4.refs_4_.refs_7_ = bf16[144,256]{1,0:T(8,128)(2,1)S(1)} collective-permute-done((bf16[144,256]{1,0:T(8,128)(2,1)S(1)}, bf16[144,256]{1,0:T(8,128)(2,1)S(1)}, u32[]{:S(2)}, u32[]{:S(2)}) %collective-permute-start.4) | collective-permute-done | bytes 73760 | tf_op jit(solution)/shard_map/ppermute | solution.py:192
  9.5 3.6 %collective-permute-done.3.refs_3_.refs_6_ = bf16[144,256]{1,0:T(8,128)(2,1)S(1)} collective-permute-done((bf16[144,256]{1,0:T(8,128)(2,1)S(1)}, bf16[144,256]{1,0:T(8,128)(2,1)S(1)}, u32[]{:S(2)}, u32[]{:S(2)}) %collective-permute-start.3) | collective-permute-done | bytes 73760 | tf_op jit(solution)/shard_map/ppermute | solution.py:192
  13.1 0.0 copy-done.1
  13.1 0.6 %shard_map.68 = (bf16[144,512]{1,0:T(8,128)(2,1)S(1)}, bf16[3,256,144]{2,1,0:T(8,128)(2,1)S(1)}, f32[16,512]{1,0:T(8,128)S(1)}) custom-call(bf16[160,256]{1,0:T(8,128)(2,1)S(1)} %get-tuple-element.10.refs_0_, bf16[160,256]{1,0:T(8,128)(2,1)S(1)} %collective-permute-done.refs_1_, bf16[144,256]{1,0:T(8,128)(2,1)S(1)} %get-tuple-element.11.refs_2_.refs_5_, ...), custom_call_target="tpu_custom_call" | custom-call | flops 226492416 | bytes 4096 | tf_op jit(solution)/shard_map/pallas_call | solution.py:228
  13.7 0.9 %collective-permute-done.5.refs_8_ = bf16[144,256]{1,0:T(8,128)(2,1)S(1)} collective-permute-done((bf16[144,256]{1,0:T(8,128)(2,1)S(1)}, bf16[144,256]{1,0:T(8,128)(2,1)S(1)}, u32[]{:S(2)}, u32[]{:S(2)}) %collective-permute-start.5) | collective-permute-done | bytes 73760 | tf_op jit(solution)/shard_map/ppermute | solution.py:192
  14.6 0.0 collective-permute-done.1.refs_2_
  14.7 0.0 collective-permute-done.2.refs_3_
  14.7 0.8 %shard_map.69.refs_5_ = f32[4,16,256]{2,1,0:T(8,128)S(1)} custom-call(bf16[144,512]{1,0:T(8,128)(2,1)S(1)} %get-tuple-element.12.refs_0_, f32[16,512]{1,0:T(8,128)S(1)} %get-tuple-element.13.refs_1_, bf16[160,256]{1,0:T(8,128)(2,1)S(1)} %collective-permute-done.1.refs_2_, bf16[160,256]{1,0:T(8,128)(2,1)S(1)} %collective-permute-done.2.refs_3_, ...), custom_call_target="tpu_custom_call" | custom-call | tf_op jit(solution)/shard_map/pallas_call | solution.py:240
  15.5 1.1 %collective-permute-start.8 = (f32[4,16,256]{2,1,0:T(8,128)S(1)}, f32[4,16,256]{2,1,0:T(8,128)S(1)}, u32[]{:S(2)}, u32[]{:S(2)}) collective-permute-start(f32[4,16,256]{2,1,0:T(8,128)S(1)} %shard_map.69.refs_5_), channel_id=1, source_target_pairs={{3,0},{2,1},{1,2},{0,3},{7,4},{6,5},{5,6},{4,7},{11,8},{10,9},{9,1... | collective-permute-start | bytes 196616 | tf_op jit(solution)/shard_map/ppermute | solution.py:177
  16.6 0.5 %collective-permute-start.7 = (f32[4,16,256]{2,1,0:T(8,128)S(1)}, f32[4,16,256]{2,1,0:T(8,128)S(1)}, u32[]{:S(2)}, u32[]{:S(2)}) collective-permute-start(f32[4,16,256]{2,1,0:T(8,128)S(1)} %shard_map.69.refs_5_), channel_id=1, source_target_pairs={{2,0},{3,1},{0,2},{1,3},{6,4},{7,5},{4,6},{5,7},{10,8},{11,9},{8,1... | collective-permute-start | bytes 196616 | tf_op jit(solution)/shard_map/ppermute | solution.py:177
  17.1 0.3 collective-permute-start.6
  17.4 2.4 %collective-permute-done.8.refs_8_ = f32[4,16,256]{2,1,0:T(8,128)S(1)} collective-permute-done((f32[4,16,256]{2,1,0:T(8,128)S(1)}, f32[4,16,256]{2,1,0:T(8,128)S(1)}, u32[]{:S(2)}, u32[]{:S(2)}) %collective-permute-start.8) | collective-permute-done | bytes 65568 | tf_op jit(solution)/shard_map/ppermute | solution.py:177
  19.8 1.5 %collective-permute-done.7.refs_7_ = f32[4,16,256]{2,1,0:T(8,128)S(1)} collective-permute-done((f32[4,16,256]{2,1,0:T(8,128)S(1)}, f32[4,16,256]{2,1,0:T(8,128)S(1)}, u32[]{:S(2)}, u32[]{:S(2)}) %collective-permute-start.7) | collective-permute-done | bytes 65568 | tf_op jit(solution)/shard_map/ppermute | solution.py:177
  21.3 0.0 collective-permute-done.6.refs_6_
  21.3 0.1 shard_map.70
  21.4 0.8 %collective-permute-start.11 = (f32[16,128]{1,0:T(8,128)S(1)}, f32[16,128]{1,0:T(8,128)S(1)}, u32[]{:S(2)}, u32[]{:S(2)}) collective-permute-start(f32[16,128]{1,0:T(8,128)S(1)} %get-tuple-element.16.refs_0_), channel_id=1, source_target_pairs={{13,0},{12,1},{9,4},{8,5},{5,8},{4,9},{1,12},{0,13},{15,2},{14,3},... | collective-permute-start | bytes 24584 | tf_op jit(solution)/shard_map/ppermute | solution.py:192
  22.3 0.0 collective-permute-start.10
  22.3 2.7 %collective-permute-start.9 = (f32[16,128]{1,0:T(8,128)S(1)}, f32[16,128]{1,0:T(8,128)S(1)}, u32[]{:S(2)}, u32[]{:S(2)}) collective-permute-start(f32[16,128]{1,0:T(8,128)S(1)} %get-tuple-element.16.refs_0_), channel_id=1, source_target_pairs={{5,0},{4,1},{1,4},{0,5},{13,8},{12,9},{9,12},{8,13},{7,2},{6,3},{3... | collective-permute-start | bytes 24584 | tf_op jit(solution)/shard_map/ppermute | solution.py:192
  24.9 1.5 %collective-permute-done.11.refs_3_ = f32[16,128]{1,0:T(8,128)S(1)} collective-permute-done((f32[16,128]{1,0:T(8,128)S(1)}, f32[16,128]{1,0:T(8,128)S(1)}, u32[]{:S(2)}, u32[]{:S(2)}) %collective-permute-start.11) | collective-permute-done | bytes 8224 | tf_op jit(solution)/shard_map/ppermute | solution.py:192
  26.4 0.0 collective-permute-done.10.refs_2_
  26.4 0.1 collective-permute-done.9.refs_1_
  26.5 0.8 %shard_map.71 = (f32[16,256]{1,0:T(8,128)}, f32[16,256]{1,0:T(8,128)}, f32[16,256]{1,0:T(8,128)}) custom-call(f32[16,256]{1,0:T(8,128)S(1)} %get-tuple-element.15.image_ref, f32[16,256]{1,0:T(8,128)S(1)} %copy-done, f32[16,128]{1,0:T(8,128)S(1)} %get-tuple-element.16.refs_0_, f32[16,128]{1,0:T(8,128)S(1)} %collective-permute-done.9.refs_1_, ...), custom_call_target="tpu_custom_call" | custom-call | tf_op jit(solution)/shard_map/pallas_call | solution.py:255
  (1 shorter events, 0.0 us)
Async XLA Ops:
  0.6 1.0 %copy-start = (f32[16,256]{1,0:T(8,128)S(1)}, f32[16,256]{1,0:T(8,128)}, u32[]{:S(2)}) copy-start(f32[16,256]{1,0:T(8,128)} %probes_ref.3) | copy-start | bytes 49156
  1.6 6.7 %collective-permute-start = (bf16[160,256]{1,0:T(8,128)(2,1)S(1)}, bf16[160,256]{1,0:T(8,128)(2,1)S(1)}, u32[]{:S(2)}, u32[]{:S(2)}) collective-permute-start(bf16[160,256]{1,0:T(8,128)(2,1)S(1)} %get-tuple-element.10.refs_0_), channel_id=1, source_target_pairs={{1,0},{0,1},{3,2},{2,3},{5,4},{4,5},{7,6},{6,7},{9,8},{8,9},{11,10... | collective-permute-start | bytes 245768 | tf_op jit(solution)/shard_map/ppermute | solution.py:177
  2.1 10.9 %copy-start.1 = (f32[256]{0:T(256)S(1)}, f32[256]{0:T(256)}, u32[]{:S(2)}) copy-start(f32[256]{0:T(256)} %param.6) | copy-start | bytes 3076
  2.1 7.4 %collective-permute-start.4 = (bf16[144,256]{1,0:T(8,128)(2,1)S(1)}, bf16[144,256]{1,0:T(8,128)(2,1)S(1)}, u32[]{:S(2)}, u32[]{:S(2)}) collective-permute-start(bf16[144,256]{1,0:T(8,128)(2,1)S(1)} %get-tuple-element.11.refs_2_.refs_5_), channel_id=1, source_target_pairs={{13,0},{12,1},{9,4},{8,5},{5,8},{4,9},{1,12},{0,13},{15,2},{14,3},... | collective-permute-start | bytes 221192 | tf_op jit(solution)/shard_map/ppermute | solution.py:192
  6.9 6.2 %collective-permute-start.3 = (bf16[144,256]{1,0:T(8,128)(2,1)S(1)}, bf16[144,256]{1,0:T(8,128)(2,1)S(1)}, u32[]{:S(2)}, u32[]{:S(2)}) collective-permute-start(bf16[144,256]{1,0:T(8,128)(2,1)S(1)} %get-tuple-element.11.refs_2_.refs_5_), channel_id=1, source_target_pairs={{9,0},{8,1},{13,4},{12,5},{1,8},{0,9},{5,12},{4,13},{11,2},{10,3},... | collective-permute-start | bytes 221192 | tf_op jit(solution)/shard_map/ppermute | solution.py:192
  6.9 7.8 %collective-permute-start.1 = (bf16[160,256]{1,0:T(8,128)(2,1)S(1)}, bf16[160,256]{1,0:T(8,128)(2,1)S(1)}, u32[]{:S(2)}, u32[]{:S(2)}) collective-permute-start(bf16[160,256]{1,0:T(8,128)(2,1)S(1)} %get-tuple-element.10.refs_0_), channel_id=1, source_target_pairs={{2,0},{0,2},{3,1},{1,3},{6,4},{4,6},{7,5},{5,7},{10,8},{8,10},{11,... | collective-permute-start | bytes 245768 | tf_op jit(solution)/shard_map/ppermute | solution.py:177
  8.4 6.3 %collective-permute-start.2 = (bf16[160,256]{1,0:T(8,128)(2,1)S(1)}, bf16[160,256]{1,0:T(8,128)(2,1)S(1)}, u32[]{:S(2)}, u32[]{:S(2)}) collective-permute-start(bf16[160,256]{1,0:T(8,128)(2,1)S(1)} %collective-permute-done.refs_1_), channel_id=1, source_target_pairs={{2,0},{0,2},{3,1},{1,3},{6,4},{4,6},{7,5},{5,7},{10,8},{8,10},{11,... | collective-permute-start | bytes 245768 | tf_op jit(solution)/shard_map/ppermute | solution.py:177
  8.9 5.8 %collective-permute-start.5 = (bf16[144,256]{1,0:T(8,128)(2,1)S(1)}, bf16[144,256]{1,0:T(8,128)(2,1)S(1)}, u32[]{:S(2)}, u32[]{:S(2)}) collective-permute-start(bf16[144,256]{1,0:T(8,128)(2,1)S(1)} %get-tuple-element.11.refs_2_.refs_5_), channel_id=1, source_target_pairs={{5,0},{4,1},{1,4},{0,5},{13,8},{12,9},{9,12},{8,13},{7,2},{6,3},{3... | collective-permute-start | bytes 221192 | tf_op jit(solution)/shard_map/ppermute | solution.py:192
  15.5 4.3 %collective-permute-start.8 = (f32[4,16,256]{2,1,0:T(8,128)S(1)}, f32[4,16,256]{2,1,0:T(8,128)S(1)}, u32[]{:S(2)}, u32[]{:S(2)}) collective-permute-start(f32[4,16,256]{2,1,0:T(8,128)S(1)} %shard_map.69.refs_5_), channel_id=1, source_target_pairs={{3,0},{2,1},{1,2},{0,3},{7,4},{6,5},{5,6},{4,7},{11,8},{10,9},{9,1... | collective-permute-start | bytes 196616 | tf_op jit(solution)/shard_map/ppermute | solution.py:177
  16.6 4.7 %collective-permute-start.7 = (f32[4,16,256]{2,1,0:T(8,128)S(1)}, f32[4,16,256]{2,1,0:T(8,128)S(1)}, u32[]{:S(2)}, u32[]{:S(2)}) collective-permute-start(f32[4,16,256]{2,1,0:T(8,128)S(1)} %shard_map.69.refs_5_), channel_id=1, source_target_pairs={{2,0},{3,1},{0,2},{1,3},{6,4},{7,5},{4,6},{5,7},{10,8},{11,9},{8,1... | collective-permute-start | bytes 196616 | tf_op jit(solution)/shard_map/ppermute | solution.py:177
  17.1 4.2 %collective-permute-start.6 = (f32[4,16,256]{2,1,0:T(8,128)S(1)}, f32[4,16,256]{2,1,0:T(8,128)S(1)}, u32[]{:S(2)}, u32[]{:S(2)}) collective-permute-start(f32[4,16,256]{2,1,0:T(8,128)S(1)} %shard_map.69.refs_5_), channel_id=1, source_target_pairs={{1,0},{0,1},{3,2},{2,3},{5,4},{4,5},{7,6},{6,7},{9,8},{8,9},{11,10... | collective-permute-start | bytes 196616 | tf_op jit(solution)/shard_map/ppermute | solution.py:177
  21.4 5.0 %collective-permute-start.11 = (f32[16,128]{1,0:T(8,128)S(1)}, f32[16,128]{1,0:T(8,128)S(1)}, u32[]{:S(2)}, u32[]{:S(2)}) collective-permute-start(f32[16,128]{1,0:T(8,128)S(1)} %get-tuple-element.16.refs_0_), channel_id=1, source_target_pairs={{13,0},{12,1},{9,4},{8,5},{5,8},{4,9},{1,12},{0,13},{15,2},{14,3},... | collective-permute-start | bytes 24584 | tf_op jit(solution)/shard_map/ppermute | solution.py:192
  22.3 4.2 %collective-permute-start.10 = (f32[16,128]{1,0:T(8,128)S(1)}, f32[16,128]{1,0:T(8,128)S(1)}, u32[]{:S(2)}, u32[]{:S(2)}) collective-permute-start(f32[16,128]{1,0:T(8,128)S(1)} %get-tuple-element.16.refs_0_), channel_id=1, source_target_pairs={{9,0},{8,1},{13,4},{12,5},{1,8},{0,9},{5,12},{4,13},{11,2},{10,3},... | collective-permute-start | bytes 24584 | tf_op jit(solution)/shard_map/ppermute | solution.py:192
  22.3 4.2 %collective-permute-start.9 = (f32[16,128]{1,0:T(8,128)S(1)}, f32[16,128]{1,0:T(8,128)S(1)}, u32[]{:S(2)}, u32[]{:S(2)}) collective-permute-start(f32[16,128]{1,0:T(8,128)S(1)} %get-tuple-element.16.refs_0_), channel_id=1, source_target_pairs={{5,0},{4,1},{1,4},{0,5},{13,8},{12,9},{9,12},{8,13},{7,2},{6,3},{3... | collective-permute-start | bytes 24584 | tf_op jit(solution)/shard_map/ppermute | solution.py:192

commit v28 on v27

--- a/solution.py
+++ b/solution.py
@@ -179,13 +179,16 @@
     ]
 
 
-def along_line(value, line_count, sub_count):
+def along_line(value, line_count, sub_count, same_core=()):
     if line_count > DIRECT or sub_count != 2:
         return everywhere(value, LINE, line_count)
     blocks = [value]
     for step in range(1, line_count):
         pairs = [
-            (2 * source_of(place, step, line_count) + 1 - core, 2 * place + core)
+            (
+                2 * source_of(place, step, line_count) + (core if step in same_core else 1 - core),
+                2 * place + core,
+            )
             for place in range(line_count)
             for core in range(2)
         ]
@@ -253,7 +256,7 @@
         )(*planes, probes, *in_order(partials, PARTIALS))
         outs = (jax.ShapeDtypeStruct(probes.shape, jnp.float32),) * 3
         return pl.pallas_call(finish_kernel, out_shape=outs, compiler_params=VMEM)(
-            image, probes, *in_order(along_line(sums, line_count, plane_shape[1]), SUMS)
+            image, probes, *in_order(along_line(sums, line_count, plane_shape[1], (3,)), SUMS)
         )
 
     return local

time: 27.6 us -> 28 us (1.014)
  starting transfers between devices: 12.7 us -> 13.2 us
    ppermute x6, starting transfers between devices: 8.26 us -> 8.84 us  [along_line(): blocks.append(lax.ppermute(value, LINE + ('sub',), pairs))]
where the time goes in v28:
time: 28 us; the launch traced here: 27.8 us
  starting transfers between devices  13.2 us (47%)
  waiting for transfers between devices  10.6 us (38%)
  Pallas kernels  2.39 us (9%)
  other arithmetic  0.93 us (3%)
  between operations  0.68 us (2%)
    ppermute x6, starting transfers between devices, along_line(): blocks.append(lax.ppermute(value, LINE + ('sub',), pairs))  8.84 us
    ppermute x6, waiting for transfers between devices, along_line(): blocks.append(lax.ppermute(value, LINE + ('sub',), pairs))  6.63 us
    ppermute x6, starting transfers between devices, everywhere(): lax.ppermute(value, axes, [(source_of(i, step, count), i) for i in range(...  4.41 us
    ppermute x6, waiting for transfers between devices, everywhere(): lax.ppermute(value, axes, [(source_of(i, step, count), i) for i in range(...  3.94 us
    convert_element_type x1, other arithmetic, local(): (features.astype(jnp.float32) / lengthscale[:, None]).astype(jnp.bfloat16)  0.93 us
    pallas_call x1, Pallas kernels, local(): pl.pallas_call(lambda *refs: image_kernel(feature_count, plane_count, *re...  0.85 us
    pallas_call x1, Pallas kernels, local(): pl.pallas_call(finish_kernel, out_shape=outs, compiler_params=VMEM)  0.77 us
    pallas_call x1, Pallas kernels, local(): pl.pallas_call(lambda *refs: near_kernel(feature_count, *refs), out_shape...  0.65 us
  transfers between devices with their start and end apart: 12, of which 7 were waited for; matrix products, arithmetic and copies ran while one was open for 0% of the time, Pallas kernels for 2%

profile of v28, /device:TPU:0, one launch (start us, length us, event | category | flops | bytes accessed | tf_op | source)
XLA Modules:
  0.0 27.8 jit_solution(17728193794327704737)
XLA Ops:
  0.6 0.0 copy-start
  0.6 0.9 %divide_convert_fusion.scaled_ref = bf16[128,256]{1,0:T(8,128)(2,1)S(1)} fusion(bf16[128,256]{1,0:T(8,128)(2,1)} %param.4, f32[128]{0:T(128)} %param.5), kind=kLoop, calls=%fused_computation | loop fusion | flops 98304 | bytes 131584 | tf_op jit(solution)/shard_map/convert_element_type | solution.py:214
  1.6 0.0 copy-done
  1.6 0.5 %collective-permute-start = (bf16[160,256]{1,0:T(8,128)(2,1)S(1)}, bf16[160,256]{1,0:T(8,128)(2,1)S(1)}, u32[]{:S(2)}, u32[]{:S(2)}) collective-permute-start(bf16[160,256]{1,0:T(8,128)(2,1)S(1)} %get-tuple-element.10.refs_0_), channel_id=1, source_target_pairs={{1,0},{0,1},{3,2},{2,3},{5,4},{4,5},{7,6},{6,7},{9,8},{8,9},{11,10... | collective-permute-start | bytes 245768 | tf_op jit(solution)/shard_map/ppermute | solution.py:177
  2.1 0.0 copy-start.1
  2.1 4.7 %collective-permute-start.4 = (bf16[144,256]{1,0:T(8,128)(2,1)S(1)}, bf16[144,256]{1,0:T(8,128)(2,1)S(1)}, u32[]{:S(2)}, u32[]{:S(2)}) collective-permute-start(bf16[144,256]{1,0:T(8,128)(2,1)S(1)} %get-tuple-element.11.refs_2_.refs_5_), channel_id=1, source_target_pairs={{13,0},{12,1},{9,4},{8,5},{5,8},{4,9},{1,12},{0,13},{15,2},{14,3},... | collective-permute-start | bytes 221192 | tf_op jit(solution)/shard_map/ppermute | solution.py:195
  6.9 0.0 collective-permute-start.3
  6.9 1.5 %collective-permute-start.1 = (bf16[160,256]{1,0:T(8,128)(2,1)S(1)}, bf16[160,256]{1,0:T(8,128)(2,1)S(1)}, u32[]{:S(2)}, u32[]{:S(2)}) collective-permute-start(bf16[160,256]{1,0:T(8,128)(2,1)S(1)} %get-tuple-element.10.refs_0_), channel_id=1, source_target_pairs={{2,0},{0,2},{3,1},{1,3},{6,4},{4,6},{7,5},{5,7},{10,8},{8,10},{11,... | collective-permute-start | bytes 245768 | tf_op jit(solution)/shard_map/ppermute | solution.py:177
  8.4 0.0 collective-permute-done.refs_1_
  8.4 0.5 %collective-permute-start.2 = (bf16[160,256]{1,0:T(8,128)(2,1)S(1)}, bf16[160,256]{1,0:T(8,128)(2,1)S(1)}, u32[]{:S(2)}, u32[]{:S(2)}) collective-permute-start(bf16[160,256]{1,0:T(8,128)(2,1)S(1)} %collective-permute-done.refs_1_), channel_id=1, source_target_pairs={{2,0},{0,2},{3,1},{1,3},{6,4},{4,6},{7,5},{5,7},{10,8},{8,10},{11,... | collective-permute-start | bytes 245768 | tf_op jit(solution)/shard_map/ppermute | solution.py:177
  8.9 0.0 collective-permute-start.5
  8.9 0.6 %collective-permute-done.4.refs_4_.refs_7_ = bf16[144,256]{1,0:T(8,128)(2,1)S(1)} collective-permute-done((bf16[144,256]{1,0:T(8,128)(2,1)S(1)}, bf16[144,256]{1,0:T(8,128)(2,1)S(1)}, u32[]{:S(2)}, u32[]{:S(2)}) %collective-permute-start.4) | collective-permute-done | bytes 73760 | tf_op jit(solution)/shard_map/ppermute | solution.py:195
  9.5 3.6 %collective-permute-done.3.refs_3_.refs_6_ = bf16[144,256]{1,0:T(8,128)(2,1)S(1)} collective-permute-done((bf16[144,256]{1,0:T(8,128)(2,1)S(1)}, bf16[144,256]{1,0:T(8,128)(2,1)S(1)}, u32[]{:S(2)}, u32[]{:S(2)}) %collective-permute-start.3) | collective-permute-done | bytes 73760 | tf_op jit(solution)/shard_map/ppermute | solution.py:195
  13.1 0.0 copy-done.1
  13.1 0.6 %shard_map.68 = (bf16[144,512]{1,0:T(8,128)(2,1)S(1)}, bf16[3,256,144]{2,1,0:T(8,128)(2,1)S(1)}, f32[16,512]{1,0:T(8,128)S(1)}) custom-call(bf16[160,256]{1,0:T(8,128)(2,1)S(1)} %get-tuple-element.10.refs_0_, bf16[160,256]{1,0:T(8,128)(2,1)S(1)} %collective-permute-done.refs_1_, bf16[144,256]{1,0:T(8,128)(2,1)S(1)} %get-tuple-element.11.refs_2_.refs_5_, ...), custom_call_target="tpu_custom_call" | custom-call | flops 226492416 | bytes 4096 | tf_op jit(solution)/shard_map/pallas_call | solution.py:231
  13.7 0.9 %collective-permute-done.5.refs_8_ = bf16[144,256]{1,0:T(8,128)(2,1)S(1)} collective-permute-done((bf16[144,256]{1,0:T(8,128)(2,1)S(1)}, bf16[144,256]{1,0:T(8,128)(2,1)S(1)}, u32[]{:S(2)}, u32[]{:S(2)}) %collective-permute-start.5) | collective-permute-done | bytes 73760 | tf_op jit(solution)/shard_map/ppermute | solution.py:195
  14.6 0.0 collective-permute-done.1.refs_2_
  14.7 0.0 collective-permute-done.2.refs_3_
  14.7 0.8 %shard_map.69.refs_5_ = f32[4,16,256]{2,1,0:T(8,128)S(1)} custom-call(bf16[144,512]{1,0:T(8,128)(2,1)S(1)} %get-tuple-element.12.refs_0_, f32[16,512]{1,0:T(8,128)S(1)} %get-tuple-element.13.refs_1_, bf16[160,256]{1,0:T(8,128)(2,1)S(1)} %collective-permute-done.1.refs_2_, bf16[160,256]{1,0:T(8,128)(2,1)S(1)} %collective-permute-done.2.refs_3_, ...), custom_call_target="tpu_custom_call" | custom-call | tf_op jit(solution)/shard_map/pallas_call | solution.py:243
  15.5 1.1 %collective-permute-start.8 = (f32[4,16,256]{2,1,0:T(8,128)S(1)}, f32[4,16,256]{2,1,0:T(8,128)S(1)}, u32[]{:S(2)}, u32[]{:S(2)}) collective-permute-start(f32[4,16,256]{2,1,0:T(8,128)S(1)} %shard_map.69.refs_5_), channel_id=1, source_target_pairs={{3,0},{2,1},{1,2},{0,3},{7,4},{6,5},{5,6},{4,7},{11,8},{10,9},{9,1... | collective-permute-start | bytes 196616 | tf_op jit(solution)/shard_map/ppermute | solution.py:177
  16.6 0.5 %collective-permute-start.7 = (f32[4,16,256]{2,1,0:T(8,128)S(1)}, f32[4,16,256]{2,1,0:T(8,128)S(1)}, u32[]{:S(2)}, u32[]{:S(2)}) collective-permute-start(f32[4,16,256]{2,1,0:T(8,128)S(1)} %shard_map.69.refs_5_), channel_id=1, source_target_pairs={{2,0},{3,1},{0,2},{1,3},{6,4},{7,5},{4,6},{5,7},{10,8},{11,9},{8,1... | collective-permute-start | bytes 196616 | tf_op jit(solution)/shard_map/ppermute | solution.py:177
  17.1 0.3 collective-permute-start.6
  17.4 2.4 %collective-permute-done.8.refs_8_ = f32[4,16,256]{2,1,0:T(8,128)S(1)} collective-permute-done((f32[4,16,256]{2,1,0:T(8,128)S(1)}, f32[4,16,256]{2,1,0:T(8,128)S(1)}, u32[]{:S(2)}, u32[]{:S(2)}) %collective-permute-start.8) | collective-permute-done | bytes 65568 | tf_op jit(solution)/shard_map/ppermute | solution.py:177
  19.8 1.5 %collective-permute-done.7.refs_7_ = f32[4,16,256]{2,1,0:T(8,128)S(1)} collective-permute-done((f32[4,16,256]{2,1,0:T(8,128)S(1)}, f32[4,16,256]{2,1,0:T(8,128)S(1)}, u32[]{:S(2)}, u32[]{:S(2)}) %collective-permute-start.7) | collective-permute-done | bytes 65568 | tf_op jit(solution)/shard_map/ppermute | solution.py:177
  21.3 0.0 collective-permute-done.6.refs_6_
  21.3 0.1 shard_map.70
  21.4 1.7 %collective-permute-start.11 = (f32[16,128]{1,0:T(8,128)S(1)}, f32[16,128]{1,0:T(8,128)S(1)}, u32[]{:S(2)}, u32[]{:S(2)}) collective-permute-start(f32[16,128]{1,0:T(8,128)S(1)} %get-tuple-element.16.refs_0_), channel_id=1, source_target_pairs={{12,0},{13,1},{8,4},{9,5},{4,8},{5,9},{0,12},{1,13},{14,2},{15,3},... | collective-permute-start | bytes 24584 | tf_op jit(solution)/shard_map/ppermute | solution.py:195
  23.1 0.0 collective-permute-start.10
  23.1 2.4 %collective-permute-start.9 = (f32[16,128]{1,0:T(8,128)S(1)}, f32[16,128]{1,0:T(8,128)S(1)}, u32[]{:S(2)}, u32[]{:S(2)}) collective-permute-start(f32[16,128]{1,0:T(8,128)S(1)} %get-tuple-element.16.refs_0_), channel_id=1, source_target_pairs={{5,0},{4,1},{1,4},{0,5},{13,8},{12,9},{9,12},{8,13},{7,2},{6,3},{3... | collective-permute-start | bytes 24584 | tf_op jit(solution)/shard_map/ppermute | solution.py:195
  25.5 1.3 %collective-permute-done.11.refs_3_ = f32[16,128]{1,0:T(8,128)S(1)} collective-permute-done((f32[16,128]{1,0:T(8,128)S(1)}, f32[16,128]{1,0:T(8,128)S(1)}, u32[]{:S(2)}, u32[]{:S(2)}) %collective-permute-start.11) | collective-permute-done | bytes 8224 | tf_op jit(solution)/shard_map/ppermute | solution.py:195
  26.9 0.2 collective-permute-done.10.refs_2_
  27.1 0.0 collective-permute-done.9.refs_1_
  27.1 0.8 %shard_map.71 = (f32[16,256]{1,0:T(8,128)}, f32[16,256]{1,0:T(8,128)}, f32[16,256]{1,0:T(8,128)}) custom-call(f32[16,256]{1,0:T(8,128)S(1)} %get-tuple-element.15.image_ref, f32[16,256]{1,0:T(8,128)S(1)} %copy-done, f32[16,128]{1,0:T(8,128)S(1)} %get-tuple-element.16.refs_0_, f32[16,128]{1,0:T(8,128)S(1)} %collective-permute-done.9.refs_1_, ...), custom_call_target="tpu_custom_call" | custom-call | tf_op jit(solution)/shard_map/pallas_call | solution.py:258
  (1 shorter events, 0.0 us)
Async XLA Ops:
  0.6 1.0 %copy-start = (f32[16,256]{1,0:T(8,128)S(1)}, f32[16,256]{1,0:T(8,128)}, u32[]{:S(2)}) copy-start(f32[16,256]{1,0:T(8,128)} %probes_ref.3) | copy-start | bytes 49156
  1.6 6.7 %collective-permute-start = (bf16[160,256]{1,0:T(8,128)(2,1)S(1)}, bf16[160,256]{1,0:T(8,128)(2,1)S(1)}, u32[]{:S(2)}, u32[]{:S(2)}) collective-permute-start(bf16[160,256]{1,0:T(8,128)(2,1)S(1)} %get-tuple-element.10.refs_0_), channel_id=1, source_target_pairs={{1,0},{0,1},{3,2},{2,3},{5,4},{4,5},{7,6},{6,7},{9,8},{8,9},{11,10... | collective-permute-start | bytes 245768 | tf_op jit(solution)/shard_map/ppermute | solution.py:177
  2.1 10.9 %copy-start.1 = (f32[256]{0:T(256)S(1)}, f32[256]{0:T(256)}, u32[]{:S(2)}) copy-start(f32[256]{0:T(256)} %param.6) | copy-start | bytes 3076
  2.1 7.4 %collective-permute-start.4 = (bf16[144,256]{1,0:T(8,128)(2,1)S(1)}, bf16[144,256]{1,0:T(8,128)(2,1)S(1)}, u32[]{:S(2)}, u32[]{:S(2)}) collective-permute-start(bf16[144,256]{1,0:T(8,128)(2,1)S(1)} %get-tuple-element.11.refs_2_.refs_5_), channel_id=1, source_target_pairs={{13,0},{12,1},{9,4},{8,5},{5,8},{4,9},{1,12},{0,13},{15,2},{14,3},... | collective-permute-start | bytes 221192 | tf_op jit(solution)/shard_map/ppermute | solution.py:195
  6.9 6.2 %collective-permute-start.3 = (bf16[144,256]{1,0:T(8,128)(2,1)S(1)}, bf16[144,256]{1,0:T(8,128)(2,1)S(1)}, u32[]{:S(2)}, u32[]{:S(2)}) collective-permute-start(bf16[144,256]{1,0:T(8,128)(2,1)S(1)} %get-tuple-element.11.refs_2_.refs_5_), channel_id=1, source_target_pairs={{9,0},{8,1},{13,4},{12,5},{1,8},{0,9},{5,12},{4,13},{11,2},{10,3},... | collective-permute-start | bytes 221192 | tf_op jit(solution)/shard_map/ppermute | solution.py:195
  6.9 7.8 %collective-permute-start.1 = (bf16[160,256]{1,0:T(8,128)(2,1)S(1)}, bf16[160,256]{1,0:T(8,128)(2,1)S(1)}, u32[]{:S(2)}, u32[]{:S(2)}) collective-permute-start(bf16[160,256]{1,0:T(8,128)(2,1)S(1)} %get-tuple-element.10.refs_0_), channel_id=1, source_target_pairs={{2,0},{0,2},{3,1},{1,3},{6,4},{4,6},{7,5},{5,7},{10,8},{8,10},{11,... | collective-permute-start | bytes 245768 | tf_op jit(solution)/shard_map/ppermute | solution.py:177
  8.4 6.3 %collective-permute-start.2 = (bf16[160,256]{1,0:T(8,128)(2,1)S(1)}, bf16[160,256]{1,0:T(8,128)(2,1)S(1)}, u32[]{:S(2)}, u32[]{:S(2)}) collective-permute-start(bf16[160,256]{1,0:T(8,128)(2,1)S(1)} %collective-permute-done.refs_1_), channel_id=1, source_target_pairs={{2,0},{0,2},{3,1},{1,3},{6,4},{4,6},{7,5},{5,7},{10,8},{8,10},{11,... | collective-permute-start | bytes 245768 | tf_op jit(solution)/shard_map/ppermute | solution.py:177
  8.9 5.8 %collective-permute-start.5 = (bf16[144,256]{1,0:T(8,128)(2,1)S(1)}, bf16[144,256]{1,0:T(8,128)(2,1)S(1)}, u32[]{:S(2)}, u32[]{:S(2)}) collective-permute-start(bf16[144,256]{1,0:T(8,128)(2,1)S(1)} %get-tuple-element.11.refs_2_.refs_5_), channel_id=1, source_target_pairs={{5,0},{4,1},{1,4},{0,5},{13,8},{12,9},{9,12},{8,13},{7,2},{6,3},{3... | collective-permute-start | bytes 221192 | tf_op jit(solution)/shard_map/ppermute | solution.py:195
  15.5 4.3 %collective-permute-start.8 = (f32[4,16,256]{2,1,0:T(8,128)S(1)}, f32[4,16,256]{2,1,0:T(8,128)S(1)}, u32[]{:S(2)}, u32[]{:S(2)}) collective-permute-start(f32[4,16,256]{2,1,0:T(8,128)S(1)} %shard_map.69.refs_5_), channel_id=1, source_target_pairs={{3,0},{2,1},{1,2},{0,3},{7,4},{6,5},{5,6},{4,7},{11,8},{10,9},{9,1... | collective-permute-start | bytes 196616 | tf_op jit(solution)/shard_map/ppermute | solution.py:177
  16.6 4.7 %collective-permute-start.7 = (f32[4,16,256]{2,1,0:T(8,128)S(1)}, f32[4,16,256]{2,1,0:T(8,128)S(1)}, u32[]{:S(2)}, u32[]{:S(2)}) collective-permute-start(f32[4,16,256]{2,1,0:T(8,128)S(1)} %shard_map.69.refs_5_), channel_id=1, source_target_pairs={{2,0},{3,1},{0,2},{1,3},{6,4},{7,5},{4,6},{5,7},{10,8},{11,9},{8,1... | collective-permute-start | bytes 196616 | tf_op jit(solution)/shard_map/ppermute | solution.py:177
  17.1 4.2 %collective-permute-start.6 = (f32[4,16,256]{2,1,0:T(8,128)S(1)}, f32[4,16,256]{2,1,0:T(8,128)S(1)}, u32[]{:S(2)}, u32[]{:S(2)}) collective-permute-start(f32[4,16,256]{2,1,0:T(8,128)S(1)} %shard_map.69.refs_5_), channel_id=1, source_target_pairs={{1,0},{0,1},{3,2},{2,3},{5,4},{4,5},{7,6},{6,7},{9,8},{8,9},{11,10... | collective-permute-start | bytes 196616 | tf_op jit(solution)/shard_map/ppermute | solution.py:177
  21.4 5.5 %collective-permute-start.11 = (f32[16,128]{1,0:T(8,128)S(1)}, f32[16,128]{1,0:T(8,128)S(1)}, u32[]{:S(2)}, u32[]{:S(2)}) collective-permute-start(f32[16,128]{1,0:T(8,128)S(1)} %get-tuple-element.16.refs_0_), channel_id=1, source_target_pairs={{12,0},{13,1},{8,4},{9,5},{4,8},{5,9},{0,12},{1,13},{14,2},{15,3},... | collective-permute-start | bytes 24584 | tf_op jit(solution)/shard_map/ppermute | solution.py:195
  23.1 4.0 %collective-permute-start.10 = (f32[16,128]{1,0:T(8,128)S(1)}, f32[16,128]{1,0:T(8,128)S(1)}, u32[]{:S(2)}, u32[]{:S(2)}) collective-permute-start(f32[16,128]{1,0:T(8,128)S(1)} %get-tuple-element.16.refs_0_), channel_id=1, source_target_pairs={{9,0},{8,1},{13,4},{12,5},{1,8},{0,9},{5,12},{4,13},{11,2},{10,3},... | collective-permute-start | bytes 24584 | tf_op jit(solution)/shard_map/ppermute | solution.py:195
  23.1 4.0 %collective-permute-start.9 = (f32[16,128]{1,0:T(8,128)S(1)}, f32[16,128]{1,0:T(8,128)S(1)}, u32[]{:S(2)}, u32[]{:S(2)}) collective-permute-start(f32[16,128]{1,0:T(8,128)S(1)} %get-tuple-element.16.refs_0_), channel_id=1, source_target_pairs={{5,0},{4,1},{1,4},{0,5},{13,8},{12,9},{9,12},{8,13},{7,2},{6,3},{3... | collective-permute-start | bytes 24584 | tf_op jit(solution)/shard_map/ppermute | solution.py:195

commit v29 on v27

--- a/solution.py
+++ b/solution.py
@@ -77,15 +77,18 @@
     total_ref[...] = total
 
 
+def far_kernel(feature_count, *refs):
+    *plane_refs, far_ref = refs
+    for place in range(0, len(plane_refs), 2):
+        far_ref[place // 2] = side_by_side(plane_refs[place : place + 2], feature_count)
+
+
 def image_kernel(feature_count, plane_count, *refs):
     rows_ref, total_ref = refs[:2]
-    plane_refs = refs[2:plane_count]
-    columns_ref, *line_refs = refs[plane_count:-1]
+    far_ref, columns_ref, *line_refs = refs[2:-1]
     partial_ref = refs[-1]
     width = partial_ref.shape[2]
-    rows = [rows_ref[...]]
-    for place in range(0, len(plane_refs), 2):
-        rows.append(side_by_side(plane_refs[place : place + 2], feature_count))
+    rows = [rows_ref[...]] + [far_ref[number] for number in range(plane_count // 2 - 1)]
     totals = [total_ref[...]] + [jnp.zeros(total_ref.shape, jnp.float32)] * (len(rows) - 1)
     if len(line_refs[0].shape) == 2:
         *early, late = [ref[...] for ref in line_refs]
@@ -237,11 +240,18 @@
                 flops=6 * work * depth, bytes_accessed=4 * plane_count * width, transcendentals=3 * work
             ),
         )(*planes[:2], *early, noise_var[None, :], probes)
+        far = pl.pallas_call(
+            lambda *refs: far_kernel(feature_count, *refs),
+            out_shape=jax.ShapeDtypeStruct(
+                (plane_count // 2 - 1, depth, 2 * width), jnp.bfloat16
+            ),
+            compiler_params=VMEM,
+        )(*planes[2:])
         partial = pl.pallas_call(
             lambda *refs: image_kernel(feature_count, plane_count, *refs),
             out_shape=jax.ShapeDtypeStruct((plane_count, probe_count, width), jnp.float32),
             compiler_params=VMEM,
-        )(rows, total, *planes[2:], columns, *early, late)
+        )(rows, total, far, columns, *early, late)
         partials = everywhere(partial, PLANE, plane_count)
         image, sums = pl.pallas_call(
             lambda *refs: combine_kernel(feature_count, plane_count, *refs),

time: 27.6 us -> 27.7 us (level)
  no operation moved by 1% of the time
where the time goes in v29:
time: 27.7 us; the launch traced here: 27.3 us
  starting transfers between devices  12.7 us (46%)
  waiting for transfers between devices  10.6 us (38%)
  Pallas kernels  2.42 us (9%)
  other arithmetic  0.93 us (3%)
  between operations  0.69 us (2%)
    ppermute x6, starting transfers between devices, along_line(): blocks.append(lax.ppermute(value, LINE + ('sub',), pairs))  8.27 us
    ppermute x6, waiting for transfers between devices, along_line(): blocks.append(lax.ppermute(value, LINE + ('sub',), pairs))  6.63 us
    ppermute x6, starting transfers between devices, everywhere(): lax.ppermute(value, axes, [(source_of(i, step, count), i) for i in range(...  4.41 us
    ppermute x6, waiting for transfers between devices, everywhere(): lax.ppermute(value, axes, [(source_of(i, step, count), i) for i in range(...  3.94 us
    convert_element_type x1, other arithmetic, local(): (features.astype(jnp.float32) / lengthscale[:, None]).astype(jnp.bfloat16)  0.93 us
    pallas_call x1, Pallas kernels, local(): pl.pallas_call(lambda *refs: image_kernel(feature_count, plane_count, *re...  0.85 us
    pallas_call x1, Pallas kernels, local(): pl.pallas_call(finish_kernel, out_shape=outs, compiler_params=VMEM)  0.77 us
    pallas_call x1, Pallas kernels, local(): pl.pallas_call(lambda *refs: near_kernel(feature_count, *refs), out_shape...  0.65 us
  transfers between devices with their start and end apart: 12, of which 7 were waited for; matrix products, arithmetic and copies ran while one was open for 0% of the time, Pallas kernels for 2%

profile of v29, /device:TPU:0, one launch (start us, length us, event | category | flops | bytes accessed | tf_op | source)
XLA Modules:
  0.0 27.3 jit_solution(2801586905497195606)
XLA Ops:
  0.6 0.0 copy-start
  0.6 0.9 %divide_convert_fusion.scaled_ref = bf16[128,256]{1,0:T(8,128)(2,1)S(1)} fusion(bf16[128,256]{1,0:T(8,128)(2,1)} %param.4, f32[128]{0:T(128)} %param.5), kind=kLoop, calls=%fused_computation | loop fusion | flops 98304 | bytes 131584 | tf_op jit(solution)/shard_map/convert_element_type | solution.py:214
  1.6 0.0 copy-done
  1.6 0.5 %collective-permute-start = (bf16[160,256]{1,0:T(8,128)(2,1)S(1)}, bf16[160,256]{1,0:T(8,128)(2,1)S(1)}, u32[]{:S(2)}, u32[]{:S(2)}) collective-permute-start(bf16[160,256]{1,0:T(8,128)(2,1)S(1)} %get-tuple-element.10.refs_0_), channel_id=1, source_target_pairs={{1,0},{0,1},{3,2},{2,3},{5,4},{4,5},{7,6},{6,7},{9,8},{8,9},{11,10... | collective-permute-start | bytes 245768 | tf_op jit(solution)/shard_map/ppermute | solution.py:180
  2.1 0.0 copy-start.1
  2.1 4.7 %collective-permute-start.4 = (bf16[144,256]{1,0:T(8,128)(2,1)S(1)}, bf16[144,256]{1,0:T(8,128)(2,1)S(1)}, u32[]{:S(2)}, u32[]{:S(2)}) collective-permute-start(bf16[144,256]{1,0:T(8,128)(2,1)S(1)} %get-tuple-element.11.refs_2_.refs_4_), channel_id=1, source_target_pairs={{13,0},{12,1},{9,4},{8,5},{5,8},{4,9},{1,12},{0,13},{15,2},{14,3},... | collective-permute-start | bytes 221192 | tf_op jit(solution)/shard_map/ppermute | solution.py:195
  6.9 0.0 collective-permute-start.3
  6.9 1.5 %collective-permute-start.1 = (bf16[160,256]{1,0:T(8,128)(2,1)S(1)}, bf16[160,256]{1,0:T(8,128)(2,1)S(1)}, u32[]{:S(2)}, u32[]{:S(2)}) collective-permute-start(bf16[160,256]{1,0:T(8,128)(2,1)S(1)} %get-tuple-element.10.refs_0_), channel_id=1, source_target_pairs={{2,0},{0,2},{3,1},{1,3},{6,4},{4,6},{7,5},{5,7},{10,8},{8,10},{11,... | collective-permute-start | bytes 245768 | tf_op jit(solution)/shard_map/ppermute | solution.py:180
  8.4 0.0 collective-permute-done.refs_1_
  8.4 0.5 %collective-permute-start.2 = (bf16[160,256]{1,0:T(8,128)(2,1)S(1)}, bf16[160,256]{1,0:T(8,128)(2,1)S(1)}, u32[]{:S(2)}, u32[]{:S(2)}) collective-permute-start(bf16[160,256]{1,0:T(8,128)(2,1)S(1)} %collective-permute-done.refs_1_), channel_id=1, source_target_pairs={{2,0},{0,2},{3,1},{1,3},{6,4},{4,6},{7,5},{5,7},{10,8},{8,10},{11,... | collective-permute-start | bytes 245768 | tf_op jit(solution)/shard_map/ppermute | solution.py:180
  8.9 0.0 collective-permute-start.5
  8.9 0.6 %collective-permute-done.4.refs_4_.refs_6_ = bf16[144,256]{1,0:T(8,128)(2,1)S(1)} collective-permute-done((bf16[144,256]{1,0:T(8,128)(2,1)S(1)}, bf16[144,256]{1,0:T(8,128)(2,1)S(1)}, u32[]{:S(2)}, u32[]{:S(2)}) %collective-permute-start.4) | collective-permute-done | bytes 73760 | tf_op jit(solution)/shard_map/ppermute | solution.py:195
  9.5 3.6 %collective-permute-done.3.refs_3_.refs_5_ = bf16[144,256]{1,0:T(8,128)(2,1)S(1)} collective-permute-done((bf16[144,256]{1,0:T(8,128)(2,1)S(1)}, bf16[144,256]{1,0:T(8,128)(2,1)S(1)}, u32[]{:S(2)}, u32[]{:S(2)}) %collective-permute-start.3) | collective-permute-done | bytes 73760 | tf_op jit(solution)/shard_map/ppermute | solution.py:195
  13.1 0.0 copy-done.1
  13.1 0.6 %shard_map.68 = (bf16[144,512]{1,0:T(8,128)(2,1)S(1)}, bf16[3,256,144]{2,1,0:T(8,128)(2,1)S(1)}, f32[16,512]{1,0:T(8,128)S(1)}) custom-call(bf16[160,256]{1,0:T(8,128)(2,1)S(1)} %get-tuple-element.10.refs_0_, bf16[160,256]{1,0:T(8,128)(2,1)S(1)} %collective-permute-done.refs_1_, bf16[144,256]{1,0:T(8,128)(2,1)S(1)} %get-tuple-element.11.refs_2_.refs_4_, ...), custom_call_target="tpu_custom_call" | custom-call | flops 226492416 | bytes 4096 | tf_op jit(solution)/shard_map/pallas_call | solution.py:231
  13.7 0.0 collective-permute-done.1.refs_0_.refs_2_
  13.7 0.0 collective-permute-done.2.refs_1_.refs_3_
  13.8 0.9 %collective-permute-done.5.refs_7_ = bf16[144,256]{1,0:T(8,128)(2,1)S(1)} collective-permute-done((bf16[144,256]{1,0:T(8,128)(2,1)S(1)}, bf16[144,256]{1,0:T(8,128)(2,1)S(1)}, u32[]{:S(2)}, u32[]{:S(2)}) %collective-permute-start.5) | collective-permute-done | bytes 73760 | tf_op jit(solution)/shard_map/ppermute | solution.py:195
  14.6 0.8 %shard_map.70.refs_5_ = f32[4,16,256]{2,1,0:T(8,128)S(1)} custom-call(bf16[144,512]{1,0:T(8,128)(2,1)S(1)} %get-tuple-element.12.refs_0_, f32[16,512]{1,0:T(8,128)S(1)} %get-tuple-element.13.refs_1_, bf16[1,144,512]{2,1,0:T(8,128)(2,1)S(1)} %shard_map.69.refs_2_, bf16[3,256,144]{2,1,0:T(8,128)(2,1)S(1)} %get-tuple-element.14.refs_3_, ...), custom_call_target="tpu_custom_call" | custom-call | tf_op jit(solution)/shard_map/pallas_call | solution.py:250
  15.5 1.1 %collective-permute-start.8 = (f32[4,16,256]{2,1,0:T(8,128)S(1)}, f32[4,16,256]{2,1,0:T(8,128)S(1)}, u32[]{:S(2)}, u32[]{:S(2)}) collective-permute-start(f32[4,16,256]{2,1,0:T(8,128)S(1)} %shard_map.70.refs_5_), channel_id=1, source_target_pairs={{3,0},{2,1},{1,2},{0,3},{7,4},{6,5},{5,6},{4,7},{11,8},{10,9},{9,1... | collective-permute-start | bytes 196616 | tf_op jit(solution)/shard_map/ppermute | solution.py:180
  16.6 0.5 %collective-permute-start.7 = (f32[4,16,256]{2,1,0:T(8,128)S(1)}, f32[4,16,256]{2,1,0:T(8,128)S(1)}, u32[]{:S(2)}, u32[]{:S(2)}) collective-permute-start(f32[4,16,256]{2,1,0:T(8,128)S(1)} %shard_map.70.refs_5_), channel_id=1, source_target_pairs={{2,0},{3,1},{0,2},{1,3},{6,4},{7,5},{4,6},{5,7},{10,8},{11,9},{8,1... | collective-permute-start | bytes 196616 | tf_op jit(solution)/shard_map/ppermute | solution.py:180
  17.1 0.3 collective-permute-start.6
  17.4 2.4 %collective-permute-done.8.refs_8_ = f32[4,16,256]{2,1,0:T(8,128)S(1)} collective-permute-done((f32[4,16,256]{2,1,0:T(8,128)S(1)}, f32[4,16,256]{2,1,0:T(8,128)S(1)}, u32[]{:S(2)}, u32[]{:S(2)}) %collective-permute-start.8) | collective-permute-done | bytes 65568 | tf_op jit(solution)/shard_map/ppermute | solution.py:180
  19.8 1.5 %collective-permute-done.7.refs_7_ = f32[4,16,256]{2,1,0:T(8,128)S(1)} collective-permute-done((f32[4,16,256]{2,1,0:T(8,128)S(1)}, f32[4,16,256]{2,1,0:T(8,128)S(1)}, u32[]{:S(2)}, u32[]{:S(2)}) %collective-permute-start.7) | collective-permute-done | bytes 65568 | tf_op jit(solution)/shard_map/ppermute | solution.py:180
  21.3 0.0 collective-permute-done.6.refs_6_
  21.3 0.1 shard_map.71
  21.4 0.9 %collective-permute-start.11 = (f32[16,128]{1,0:T(8,128)S(1)}, f32[16,128]{1,0:T(8,128)S(1)}, u32[]{:S(2)}, u32[]{:S(2)}) collective-permute-start(f32[16,128]{1,0:T(8,128)S(1)} %get-tuple-element.16.refs_0_), channel_id=1, source_target_pairs={{13,0},{12,1},{9,4},{8,5},{5,8},{4,9},{1,12},{0,13},{15,2},{14,3},... | collective-permute-start | bytes 24584 | tf_op jit(solution)/shard_map/ppermute | solution.py:195
  22.3 0.0 collective-permute-start.10
  22.3 2.6 %collective-permute-start.9 = (f32[16,128]{1,0:T(8,128)S(1)}, f32[16,128]{1,0:T(8,128)S(1)}, u32[]{:S(2)}, u32[]{:S(2)}) collective-permute-start(f32[16,128]{1,0:T(8,128)S(1)} %get-tuple-element.16.refs_0_), channel_id=1, source_target_pairs={{5,0},{4,1},{1,4},{0,5},{13,8},{12,9},{9,12},{8,13},{7,2},{6,3},{3... | collective-permute-start | bytes 24584 | tf_op jit(solution)/shard_map/ppermute | solution.py:195
  24.9 1.5 %collective-permute-done.11.refs_3_ = f32[16,128]{1,0:T(8,128)S(1)} collective-permute-done((f32[16,128]{1,0:T(8,128)S(1)}, f32[16,128]{1,0:T(8,128)S(1)}, u32[]{:S(2)}, u32[]{:S(2)}) %collective-permute-start.11) | collective-permute-done | bytes 8224 | tf_op jit(solution)/shard_map/ppermute | solution.py:195
  26.5 0.0 collective-permute-done.10.refs_2_
  26.5 0.1 collective-permute-done.9.refs_1_
  26.5 0.8 %shard_map.72 = (f32[16,256]{1,0:T(8,128)}, f32[16,256]{1,0:T(8,128)}, f32[16,256]{1,0:T(8,128)}) custom-call(f32[16,256]{1,0:T(8,128)S(1)} %get-tuple-element.15.image_ref, f32[16,256]{1,0:T(8,128)S(1)} %copy-done, f32[16,128]{1,0:T(8,128)S(1)} %get-tuple-element.16.refs_0_, f32[16,128]{1,0:T(8,128)S(1)} %collective-permute-done.9.refs_1_, ...), custom_call_target="tpu_custom_call" | custom-call | tf_op jit(solution)/shard_map/pallas_call | solution.py:265
  (2 shorter events, 0.0 us)
Async XLA Ops:
  0.6 1.0 %copy-start = (f32[16,256]{1,0:T(8,128)S(1)}, f32[16,256]{1,0:T(8,128)}, u32[]{:S(2)}) copy-start(f32[16,256]{1,0:T(8,128)} %probes_ref.3) | copy-start | bytes 49156
  1.6 6.7 %collective-permute-start = (bf16[160,256]{1,0:T(8,128)(2,1)S(1)}, bf16[160,256]{1,0:T(8,128)(2,1)S(1)}, u32[]{:S(2)}, u32[]{:S(2)}) collective-permute-start(bf16[160,256]{1,0:T(8,128)(2,1)S(1)} %get-tuple-element.10.refs_0_), channel_id=1, source_target_pairs={{1,0},{0,1},{3,2},{2,3},{5,4},{4,5},{7,6},{6,7},{9,8},{8,9},{11,10... | collective-permute-start | bytes 245768 | tf_op jit(solution)/shard_map/ppermute | solution.py:180
  2.1 10.9 %copy-start.1 = (f32[256]{0:T(256)S(1)}, f32[256]{0:T(256)}, u32[]{:S(2)}) copy-start(f32[256]{0:T(256)} %param.6) | copy-start | bytes 3076
  2.1 7.4 %collective-permute-start.4 = (bf16[144,256]{1,0:T(8,128)(2,1)S(1)}, bf16[144,256]{1,0:T(8,128)(2,1)S(1)}, u32[]{:S(2)}, u32[]{:S(2)}) collective-permute-start(bf16[144,256]{1,0:T(8,128)(2,1)S(1)} %get-tuple-element.11.refs_2_.refs_4_), channel_id=1, source_target_pairs={{13,0},{12,1},{9,4},{8,5},{5,8},{4,9},{1,12},{0,13},{15,2},{14,3},... | collective-permute-start | bytes 221192 | tf_op jit(solution)/shard_map/ppermute | solution.py:195
  6.9 6.2 %collective-permute-start.3 = (bf16[144,256]{1,0:T(8,128)(2,1)S(1)}, bf16[144,256]{1,0:T(8,128)(2,1)S(1)}, u32[]{:S(2)}, u32[]{:S(2)}) collective-permute-start(bf16[144,256]{1,0:T(8,128)(2,1)S(1)} %get-tuple-element.11.refs_2_.refs_4_), channel_id=1, source_target_pairs={{9,0},{8,1},{13,4},{12,5},{1,8},{0,9},{5,12},{4,13},{11,2},{10,3},... | collective-permute-start | bytes 221192 | tf_op jit(solution)/shard_map/ppermute | solution.py:195
  6.9 6.9 %collective-permute-start.1 = (bf16[160,256]{1,0:T(8,128)(2,1)S(1)}, bf16[160,256]{1,0:T(8,128)(2,1)S(1)}, u32[]{:S(2)}, u32[]{:S(2)}) collective-permute-start(bf16[160,256]{1,0:T(8,128)(2,1)S(1)} %get-tuple-element.10.refs_0_), channel_id=1, source_target_pairs={{2,0},{0,2},{3,1},{1,3},{6,4},{4,6},{7,5},{5,7},{10,8},{8,10},{11,... | collective-permute-start | bytes 245768 | tf_op jit(solution)/shard_map/ppermute | solution.py:180
  8.4 5.4 %collective-permute-start.2 = (bf16[160,256]{1,0:T(8,128)(2,1)S(1)}, bf16[160,256]{1,0:T(8,128)(2,1)S(1)}, u32[]{:S(2)}, u32[]{:S(2)}) collective-permute-start(bf16[160,256]{1,0:T(8,128)(2,1)S(1)} %collective-permute-done.refs_1_), channel_id=1, source_target_pairs={{2,0},{0,2},{3,1},{1,3},{6,4},{4,6},{7,5},{5,7},{10,8},{8,10},{11,... | collective-permute-start | bytes 245768 | tf_op jit(solution)/shard_map/ppermute | solution.py:180
  8.9 5.8 %collective-permute-start.5 = (bf16[144,256]{1,0:T(8,128)(2,1)S(1)}, bf16[144,256]{1,0:T(8,128)(2,1)S(1)}, u32[]{:S(2)}, u32[]{:S(2)}) collective-permute-start(bf16[144,256]{1,0:T(8,128)(2,1)S(1)} %get-tuple-element.11.refs_2_.refs_4_), channel_id=1, source_target_pairs={{5,0},{4,1},{1,4},{0,5},{13,8},{12,9},{9,12},{8,13},{7,2},{6,3},{3... | collective-permute-start | bytes 221192 | tf_op jit(solution)/shard_map/ppermute | solution.py:195
  15.5 4.3 %collective-permute-start.8 = (f32[4,16,256]{2,1,0:T(8,128)S(1)}, f32[4,16,256]{2,1,0:T(8,128)S(1)}, u32[]{:S(2)}, u32[]{:S(2)}) collective-permute-start(f32[4,16,256]{2,1,0:T(8,128)S(1)} %shard_map.70.refs_5_), channel_id=1, source_target_pairs={{3,0},{2,1},{1,2},{0,3},{7,4},{6,5},{5,6},{4,7},{11,8},{10,9},{9,1... | collective-permute-start | bytes 196616 | tf_op jit(solution)/shard_map/ppermute | solution.py:180
  16.6 4.7 %collective-permute-start.7 = (f32[4,16,256]{2,1,0:T(8,128)S(1)}, f32[4,16,256]{2,1,0:T(8,128)S(1)}, u32[]{:S(2)}, u32[]{:S(2)}) collective-permute-start(f32[4,16,256]{2,1,0:T(8,128)S(1)} %shard_map.70.refs_5_), channel_id=1, source_target_pairs={{2,0},{3,1},{0,2},{1,3},{6,4},{7,5},{4,6},{5,7},{10,8},{11,9},{8,1... | collective-permute-start | bytes 196616 | tf_op jit(solution)/shard_map/ppermute | solution.py:180
  17.1 4.2 %collective-permute-start.6 = (f32[4,16,256]{2,1,0:T(8,128)S(1)}, f32[4,16,256]{2,1,0:T(8,128)S(1)}, u32[]{:S(2)}, u32[]{:S(2)}) collective-permute-start(f32[4,16,256]{2,1,0:T(8,128)S(1)} %shard_map.70.refs_5_), channel_id=1, source_target_pairs={{1,0},{0,1},{3,2},{2,3},{5,4},{4,5},{7,6},{6,7},{9,8},{8,9},{11,10... | collective-permute-start | bytes 196616 | tf_op jit(solution)/shard_map/ppermute | solution.py:180
  21.4 5.1 %collective-permute-start.11 = (f32[16,128]{1,0:T(8,128)S(1)}, f32[16,128]{1,0:T(8,128)S(1)}, u32[]{:S(2)}, u32[]{:S(2)}) collective-permute-start(f32[16,128]{1,0:T(8,128)S(1)} %get-tuple-element.16.refs_0_), channel_id=1, source_target_pairs={{13,0},{12,1},{9,4},{8,5},{5,8},{4,9},{1,12},{0,13},{15,2},{14,3},... | collective-permute-start | bytes 24584 | tf_op jit(solution)/shard_map/ppermute | solution.py:195
  22.3 4.2 %collective-permute-start.10 = (f32[16,128]{1,0:T(8,128)S(1)}, f32[16,128]{1,0:T(8,128)S(1)}, u32[]{:S(2)}, u32[]{:S(2)}) collective-permute-start(f32[16,128]{1,0:T(8,128)S(1)} %get-tuple-element.16.refs_0_), channel_id=1, source_target_pairs={{9,0},{8,1},{13,4},{12,5},{1,8},{0,9},{5,12},{4,13},{11,2},{10,3},... | collective-permute-start | bytes 24584 | tf_op jit(solution)/shard_map/ppermute | solution.py:195
  22.3 4.2 %collective-permute-start.9 = (f32[16,128]{1,0:T(8,128)S(1)}, f32[16,128]{1,0:T(8,128)S(1)}, u32[]{:S(2)}, u32[]{:S(2)}) collective-permute-start(f32[16,128]{1,0:T(8,128)S(1)} %get-tuple-element.16.refs_0_), channel_id=1, source_target_pairs={{5,0},{4,1},{1,4},{0,5},{13,8},{12,9},{9,12},{8,13},{7,2},{6,3},{3... | collective-permute-start | bytes 24584 | tf_op jit(solution)/shard_map/ppermute | solution.py:195

commit v30 on v27

--- a/solution.py
+++ b/solution.py
@@ -9,8 +9,8 @@
 LINE = ("blk",)
 DIRECT = 8
 VMEM = pltpu.CompilerParams(vmem_limit_bytes=40 * 1024 * 1024)
-PARTIALS, PARTIALS_BACK = (0, 1, 2, 3), (0, 1, 2, 3)
-SUMS = (0, 1, 2, 3)
+PARTIALS, PARTIALS_BACK = (0, 3, 2, 1), (0, 3, 2, 1)
+SUMS = (0, 3, 2, 1)
 HALF = 8
 
 
@@ -77,35 +77,39 @@
     total_ref[...] = total
 
 
+def far_kernel(feature_count, plane_count, *refs):
+    plane_refs, columns_ref = refs[: plane_count - 2], refs[plane_count - 2]
+    line_refs, (far_ref, totals_ref) = refs[plane_count - 1 : -2], refs[-2:]
+    totals_ref[...] = jnp.zeros(totals_ref.shape, jnp.float32)
+    for number in range(len(plane_refs) // 2):
+        rows = side_by_side(plane_refs[2 * number : 2 * number + 2], feature_count)
+        far_ref[number] = rows
+        if line_refs:
+            columns = [columns_ref[place] for place in range(len(line_refs))]
+            probes = jnp.concatenate([ref[feature_count:, :] for ref in line_refs], axis=1)
+            totals_ref[number] = product(jnp.concatenate(columns, axis=0), probes, rows)
+
+
 def image_kernel(feature_count, plane_count, *refs):
     rows_ref, total_ref = refs[:2]
-    plane_refs = refs[2:plane_count]
-    columns_ref, *line_refs = refs[plane_count:-1]
-    partial_ref = refs[-1]
+    far_ref, far_total_ref, line_ref, partial_ref = refs[2:]
     width = partial_ref.shape[2]
-    rows = [rows_ref[...]]
-    for place in range(0, len(plane_refs), 2):
-        rows.append(side_by_side(plane_refs[place : place + 2], feature_count))
-    totals = [total_ref[...]] + [jnp.zeros(total_ref.shape, jnp.float32)] * (len(rows) - 1)
-    if len(line_refs[0].shape) == 2:
-        *early, late = [ref[...] for ref in line_refs]
-        late_columns = columns_of(late, feature_count)
-        columns = [columns_ref[number] for number in range(len(early))]
-        columns = jnp.concatenate(columns + [late_columns], axis=0)
-        probes = jnp.concatenate([block[feature_count:, :] for block in early + [late]], axis=1)
-        near = totals[0] + product(late_columns, late[feature_count:, :], rows[0])
-        totals = [near] + [product(columns, probes, pair) for pair in rows[1:]]
+    rows = [rows_ref[...]] + [far_ref[number] for number in range(plane_count // 2 - 1)]
+    totals = [total_ref[...]] + [far_total_ref[number] for number in range(len(rows) - 1)]
+
+    def add_block(block, totals):
+        columns = columns_of(block, feature_count)
+        return [
+            total + product(columns, block[feature_count:, :], pair)
+            for pair, total in zip(rows, totals)
+        ]
+
+    if len(line_ref.shape) == 2:
+        totals = add_block(line_ref[...], totals)
     else:
-
-        def add_block(number, totals):
-            block = line_refs[0][number]
-            columns = columns_of(block, feature_count)
-            return [
-                total + product(columns, block[feature_count:, :], pair)
-                for pair, total in zip(rows, totals)
-            ]
-
-        totals = lax.fori_loop(0, line_refs[0].shape[0], add_block, totals)
+        totals = lax.fori_loop(
+            0, line_ref.shape[0], lambda number, value: add_block(line_ref[number], value), totals
+        )
     for number in range(plane_count):
         place = number % 2 * width
         partial_ref[number] = totals[number // 2][:, place : place + width]
@@ -220,7 +224,7 @@
         lines = along_line(line, line_count, plane_shape[1])
         planes = plane_blocks(plane, plane_shape)
         if len(lines) > 1:
-            early, late = lines[:1] + lines[2:], lines[1]
+            early, late = lines[:1] + lines[:1:-1], lines[1]
         else:
             early, late = [], lines[0]
         depth = feature_count + 2 * HALF
@@ -237,11 +241,20 @@
                 flops=6 * work * depth, bytes_accessed=4 * plane_count * width, transcendentals=3 * work
             ),
         )(*planes[:2], *early, noise_var[None, :], probes)
+        pairs = plane_count // 2 - 1
+        far, far_totals = pl.pallas_call(
+            lambda *refs: far_kernel(feature_count, plane_count, *refs),
+            out_shape=(
+                jax.ShapeDtypeStruct((pairs, depth, 2 * width), jnp.bfloat16),
+                jax.ShapeDtypeStruct((pairs, probe_count, 2 * width), jnp.float32),
+            ),
+            compiler_params=VMEM,
+        )(*planes[2:], columns, *early)
         partial = pl.pallas_call(
             lambda *refs: image_kernel(feature_count, plane_count, *refs),
             out_shape=jax.ShapeDtypeStruct((plane_count, probe_count, width), jnp.float32),
             compiler_params=VMEM,
-        )(rows, total, *planes[2:], columns, *early, late)
+        )(rows, total, far, far_totals, late)
         partials = everywhere(partial, PLANE, plane_count)
         image, sums = pl.pallas_call(
             lambda *refs: combine_kernel(feature_count, plane_count, *refs),

time: 27.6 us -> 27.9 us (1.011)
  the two profiles are of different devices: /device:TPU:0 before, /device:TPU:1 now
where the time goes in v30:
time: 27.9 us; the launch traced here: 27.8 us
  starting transfers between devices  14 us (50%)
  waiting for transfers between devices  9.4 us (34%)
  Pallas kernels  2.69 us (10%)
  other arithmetic  0.93 us (3%)
  between operations  0.68 us (2%)
    ppermute x6, starting transfers between devices, along_line(): blocks.append(lax.ppermute(value, LINE + ('sub',), pairs))  10.3 us
    ppermute x6, waiting for transfers between devices, along_line(): blocks.append(lax.ppermute(value, LINE + ('sub',), pairs))  5.91 us
    ppermute x6, starting transfers between devices, everywhere(): lax.ppermute(value, axes, [(source_of(i, step, count), i) for i in range(...  3.73 us
    ppermute x6, waiting for transfers between devices, everywhere(): lax.ppermute(value, axes, [(source_of(i, step, count), i) for i in range(...  3.49 us
    convert_element_type x1, other arithmetic, local(): (features.astype(jnp.float32) / lengthscale[:, None]).astype(jnp.bfloat16)  0.93 us
    pallas_call x1, Pallas kernels, local(): pl.pallas_call(finish_kernel, out_shape=outs, compiler_params=VMEM)  0.77 us
    pallas_call x1, Pallas kernels, local(): pl.pallas_call(lambda *refs: image_kernel(feature_count, plane_count, *re...  0.66 us
    pallas_call x1, Pallas kernels, local(): pl.pallas_call(lambda *refs: near_kernel(feature_count, *refs), out_shape...  0.66 us
  transfers between devices with their start and end apart: 12, of which 5 were waited for; matrix products, arithmetic and copies ran while one was open for 0% of the time, Pallas kernels for 4%

profile of v30, /device:TPU:1, one launch (start us, length us, event | category | flops | bytes accessed | tf_op | source)
XLA Modules:
  0.0 27.8 jit_solution(15682977723577215378)
XLA Ops:
  0.6 0.0 copy-start
  0.6 0.9 %divide_convert_fusion.scaled_ref = bf16[128,256]{1,0:T(8,128)(2,1)S(1)} fusion(bf16[128,256]{1,0:T(8,128)(2,1)} %param.4, f32[128]{0:T(128)} %param.5), kind=kLoop, calls=%fused_computation | loop fusion | flops 98304 | bytes 131584 | tf_op jit(solution)/shard_map/convert_element_type | solution.py:215
  1.6 0.0 copy-done
  1.6 0.1 collective-permute-start
  1.7 0.0 copy-start.1
  1.7 4.7 %collective-permute-start.3 = (bf16[144,256]{1,0:T(8,128)(2,1)S(1)}, bf16[144,256]{1,0:T(8,128)(2,1)S(1)}, u32[]{:S(2)}, u32[]{:S(2)}) collective-permute-start(bf16[144,256]{1,0:T(8,128)(2,1)S(1)} %get-tuple-element.13.refs_2_.refs_3_), channel_id=1, source_target_pairs={{13,0},{12,1},{9,4},{8,5},{5,8},{4,9},{1,12},{0,13},{15,2},{14,3},... | collective-permute-start | bytes 221192 | tf_op jit(solution)/shard_map/ppermute | solution.py:196
  6.5 0.0 collective-permute-start.4
  6.5 1.2 %collective-permute-start.1 = (bf16[160,256]{1,0:T(8,128)(2,1)S(1)}, bf16[160,256]{1,0:T(8,128)(2,1)S(1)}, u32[]{:S(2)}, u32[]{:S(2)}) collective-permute-start(bf16[160,256]{1,0:T(8,128)(2,1)S(1)} %get-tuple-element.12.refs_0_), channel_id=1, source_target_pairs={{2,0},{0,2},{3,1},{1,3},{6,4},{4,6},{7,5},{5,7},{10,8},{8,10},{11,... | collective-permute-start | bytes 245768 | tf_op jit(solution)/shard_map/ppermute | solution.py:181
  7.7 0.0 collective-permute-done.refs_1_
  7.7 0.3 collective-permute-start.2
  8.0 1.1 %collective-permute-start.5 = (bf16[144,256]{1,0:T(8,128)(2,1)S(1)}, bf16[144,256]{1,0:T(8,128)(2,1)S(1)}, u32[]{:S(2)}, u32[]{:S(2)}) collective-permute-start(bf16[144,256]{1,0:T(8,128)(2,1)S(1)} %get-tuple-element.13.refs_2_.refs_3_), channel_id=1, source_target_pairs={{5,0},{4,1},{1,4},{0,5},{13,8},{12,9},{9,12},{8,13},{7,2},{6,3},{3... | collective-permute-start | bytes 221192 | tf_op jit(solution)/shard_map/ppermute | solution.py:196
  9.1 0.0 collective-permute-done.3.refs_3_.refs_4_
  9.1 3.9 %collective-permute-done.4.refs_4_.refs_5_ = bf16[144,256]{1,0:T(8,128)(2,1)S(1)} collective-permute-done((bf16[144,256]{1,0:T(8,128)(2,1)S(1)}, bf16[144,256]{1,0:T(8,128)(2,1)S(1)}, u32[]{:S(2)}, u32[]{:S(2)}) %collective-permute-start.4) | collective-permute-done | bytes 73760 | tf_op jit(solution)/shard_map/ppermute | solution.py:196
  13.0 0.0 copy-done.1
  13.0 0.7 %shard_map.68 = (bf16[144,512]{1,0:T(8,128)(2,1)S(1)}, bf16[3,256,144]{2,1,0:T(8,128)(2,1)S(1)}, f32[16,512]{1,0:T(8,128)S(1)}) custom-call(bf16[160,256]{1,0:T(8,128)(2,1)S(1)} %get-tuple-element.12.refs_0_, bf16[160,256]{1,0:T(8,128)(2,1)S(1)} %collective-permute-done.refs_1_, bf16[144,256]{1,0:T(8,128)(2,1)S(1)} %get-tuple-element.13.refs_2_.refs_3_, ...), custom_call_target="tpu_custom_call" | custom-call | flops 226492416 | bytes 4096 | tf_op jit(solution)/shard_map/pallas_call | solution.py:232
  13.7 0.0 collective-permute-done.1.refs_0_.refs_2_
  13.7 0.0 collective-permute-done.2.refs_1_.refs_3_
  13.7 0.5 %shard_map.69 = (bf16[1,144,512]{2,1,0:T(8,128)(2,1)S(1)}, f32[1,16,512]{2,1,0:T(8,128)S(1)}) custom-call(bf16[160,256]{1,0:T(8,128)(2,1)S(1)} %collective-permute-done.1.refs_0_.refs_2_, bf16[160,256]{1,0:T(8,128)(2,1)S(1)} %collective-permute-done.2.refs_1_.refs_3_, bf16[3,256,144]{2,1,0:T(8,128)(2,1)S(1)} %get-tuple-element.16.refs_2_, ...), custom_call_target="tpu_custom_call" | custom-call | tf_op jit(solution)/shard_map/pallas_call | solution.py:245
  14.2 0.0 collective-permute-done.5.refs_4_
  14.2 0.7 %shard_map.70.refs_5_ = f32[4,16,256]{2,1,0:T(8,128)S(1)} custom-call(bf16[144,512]{1,0:T(8,128)(2,1)S(1)} %get-tuple-element.14.refs_0_, f32[16,512]{1,0:T(8,128)S(1)} %get-tuple-element.15.refs_1_, bf16[1,144,512]{2,1,0:T(8,128)(2,1)S(1)} %get-tuple-element.17.refs_2_, f32[1,16,512]{2,1,0:T(8,128)S(1)} %get-tuple-element.18.refs_3_, ...), custom_call_target="tpu_custom_call" | custom-call | tf_op jit(solution)/shard_map/pallas_call | solution.py:253
  14.8 1.6 %collective-permute-start.6 = (f32[4,16,256]{2,1,0:T(8,128)S(1)}, f32[4,16,256]{2,1,0:T(8,128)S(1)}, u32[]{:S(2)}, u32[]{:S(2)}) collective-permute-start(f32[4,16,256]{2,1,0:T(8,128)S(1)} %shard_map.70.refs_5_), channel_id=1, source_target_pairs={{3,0},{2,1},{1,2},{0,3},{7,4},{6,5},{5,6},{4,7},{11,8},{10,9},{9,1... | collective-permute-start | bytes 196616 | tf_op jit(solution)/shard_map/ppermute | solution.py:181
  16.5 0.3 collective-permute-start.7
  16.7 0.3 collective-permute-start.8
  17.0 2.2 %collective-permute-done.6.refs_6_ = f32[4,16,256]{2,1,0:T(8,128)S(1)} collective-permute-done((f32[4,16,256]{2,1,0:T(8,128)S(1)}, f32[4,16,256]{2,1,0:T(8,128)S(1)}, u32[]{:S(2)}, u32[]{:S(2)}) %collective-permute-start.6) | collective-permute-done | bytes 65568 | tf_op jit(solution)/shard_map/ppermute | solution.py:181
  19.2 1.2 %collective-permute-done.7.refs_7_ = f32[4,16,256]{2,1,0:T(8,128)S(1)} collective-permute-done((f32[4,16,256]{2,1,0:T(8,128)S(1)}, f32[4,16,256]{2,1,0:T(8,128)S(1)}, u32[]{:S(2)}, u32[]{:S(2)}) %collective-permute-start.7) | collective-permute-done | bytes 65568 | tf_op jit(solution)/shard_map/ppermute | solution.py:181
  20.5 0.0 collective-permute-done.8.refs_8_
  20.5 0.1 shard_map.71
  20.6 2.4 %collective-permute-start.9 = (f32[16,128]{1,0:T(8,128)S(1)}, f32[16,128]{1,0:T(8,128)S(1)}, u32[]{:S(2)}, u32[]{:S(2)}) collective-permute-start(f32[16,128]{1,0:T(8,128)S(1)} %get-tuple-element.20.refs_0_), channel_id=1, source_target_pairs={{13,0},{12,1},{9,4},{8,5},{5,8},{4,9},{1,12},{0,13},{15,2},{14,3},... | collective-permute-start | bytes 24584 | tf_op jit(solution)/shard_map/ppermute | solution.py:196
  23.0 0.0 collective-permute-start.10
  23.0 2.0 %collective-permute-start.11 = (f32[16,128]{1,0:T(8,128)S(1)}, f32[16,128]{1,0:T(8,128)S(1)}, u32[]{:S(2)}, u32[]{:S(2)}) collective-permute-start(f32[16,128]{1,0:T(8,128)S(1)} %get-tuple-element.20.refs_0_), channel_id=1, source_target_pairs={{5,0},{4,1},{1,4},{0,5},{13,8},{12,9},{9,12},{8,13},{7,2},{6,3},{3... | collective-permute-start | bytes 24584 | tf_op jit(solution)/shard_map/ppermute | solution.py:196
  25.0 0.8 %collective-permute-done.9.refs_1_ = f32[16,128]{1,0:T(8,128)S(1)} collective-permute-done((f32[16,128]{1,0:T(8,128)S(1)}, f32[16,128]{1,0:T(8,128)S(1)}, u32[]{:S(2)}, u32[]{:S(2)}) %collective-permute-start.9) | collective-permute-done | bytes 8224 | tf_op jit(solution)/shard_map/ppermute | solution.py:196
  25.8 1.2 %collective-permute-done.10.refs_2_ = f32[16,128]{1,0:T(8,128)S(1)} collective-permute-done((f32[16,128]{1,0:T(8,128)S(1)}, f32[16,128]{1,0:T(8,128)S(1)}, u32[]{:S(2)}, u32[]{:S(2)}) %collective-permute-start.10) | collective-permute-done | bytes 8224 | tf_op jit(solution)/shard_map/ppermute | solution.py:196
  27.0 0.0 collective-permute-done.11.refs_3_
  27.0 0.8 %shard_map.72 = (f32[16,256]{1,0:T(8,128)}, f32[16,256]{1,0:T(8,128)}, f32[16,256]{1,0:T(8,128)}) custom-call(f32[16,256]{1,0:T(8,128)S(1)} %get-tuple-element.19.image_ref, f32[16,256]{1,0:T(8,128)S(1)} %copy-done, f32[16,128]{1,0:T(8,128)S(1)} %get-tuple-element.20.refs_0_, f32[16,128]{1,0:T(8,128)S(1)} %collective-permute-done.9.refs_1_, ...), custom_call_target="tpu_custom_call" | custom-call | tf_op jit(solution)/shard_map/pallas_call | solution.py:268
  (1 shorter events, 0.0 us)
Async XLA Ops:
  0.6 1.0 %copy-start = (f32[16,256]{1,0:T(8,128)S(1)}, f32[16,256]{1,0:T(8,128)}, u32[]{:S(2)}) copy-start(f32[16,256]{1,0:T(8,128)} %probes_ref.3) | copy-start | bytes 49156
  1.6 6.1 %collective-permute-start = (bf16[160,256]{1,0:T(8,128)(2,1)S(1)}, bf16[160,256]{1,0:T(8,128)(2,1)S(1)}, u32[]{:S(2)}, u32[]{:S(2)}) collective-permute-start(bf16[160,256]{1,0:T(8,128)(2,1)S(1)} %get-tuple-element.12.refs_0_), channel_id=1, source_target_pairs={{1,0},{0,1},{3,2},{2,3},{5,4},{4,5},{7,6},{6,7},{9,8},{8,9},{11,10... | collective-permute-start | bytes 245768 | tf_op jit(solution)/shard_map/ppermute | solution.py:181
  1.7 11.3 %copy-start.1 = (f32[256]{0:T(256)S(1)}, f32[256]{0:T(256)}, u32[]{:S(2)}) copy-start(f32[256]{0:T(256)} %param.6) | copy-start | bytes 3076
  1.7 7.4 %collective-permute-start.3 = (bf16[144,256]{1,0:T(8,128)(2,1)S(1)}, bf16[144,256]{1,0:T(8,128)(2,1)S(1)}, u32[]{:S(2)}, u32[]{:S(2)}) collective-permute-start(bf16[144,256]{1,0:T(8,128)(2,1)S(1)} %get-tuple-element.13.refs_2_.refs_3_), channel_id=1, source_target_pairs={{13,0},{12,1},{9,4},{8,5},{5,8},{4,9},{1,12},{0,13},{15,2},{14,3},... | collective-permute-start | bytes 221192 | tf_op jit(solution)/shard_map/ppermute | solution.py:196
  6.5 6.5 %collective-permute-start.4 = (bf16[144,256]{1,0:T(8,128)(2,1)S(1)}, bf16[144,256]{1,0:T(8,128)(2,1)S(1)}, u32[]{:S(2)}, u32[]{:S(2)}) collective-permute-start(bf16[144,256]{1,0:T(8,128)(2,1)S(1)} %get-tuple-element.13.refs_2_.refs_3_), channel_id=1, source_target_pairs={{9,0},{8,1},{13,4},{12,5},{1,8},{0,9},{5,12},{4,13},{11,2},{10,3},... | collective-permute-start | bytes 221192 | tf_op jit(solution)/shard_map/ppermute | solution.py:196
  6.5 7.2 %collective-permute-start.1 = (bf16[160,256]{1,0:T(8,128)(2,1)S(1)}, bf16[160,256]{1,0:T(8,128)(2,1)S(1)}, u32[]{:S(2)}, u32[]{:S(2)}) collective-permute-start(bf16[160,256]{1,0:T(8,128)(2,1)S(1)} %get-tuple-element.12.refs_0_), channel_id=1, source_target_pairs={{2,0},{0,2},{3,1},{1,3},{6,4},{4,6},{7,5},{5,7},{10,8},{8,10},{11,... | collective-permute-start | bytes 245768 | tf_op jit(solution)/shard_map/ppermute | solution.py:181
  7.7 6.0 %collective-permute-start.2 = (bf16[160,256]{1,0:T(8,128)(2,1)S(1)}, bf16[160,256]{1,0:T(8,128)(2,1)S(1)}, u32[]{:S(2)}, u32[]{:S(2)}) collective-permute-start(bf16[160,256]{1,0:T(8,128)(2,1)S(1)} %collective-permute-done.refs_1_), channel_id=1, source_target_pairs={{2,0},{0,2},{3,1},{1,3},{6,4},{4,6},{7,5},{5,7},{10,8},{8,10},{11,... | collective-permute-start | bytes 245768 | tf_op jit(solution)/shard_map/ppermute | solution.py:181
  8.0 6.2 %collective-permute-start.5 = (bf16[144,256]{1,0:T(8,128)(2,1)S(1)}, bf16[144,256]{1,0:T(8,128)(2,1)S(1)}, u32[]{:S(2)}, u32[]{:S(2)}) collective-permute-start(bf16[144,256]{1,0:T(8,128)(2,1)S(1)} %get-tuple-element.13.refs_2_.refs_3_), channel_id=1, source_target_pairs={{5,0},{4,1},{1,4},{0,5},{13,8},{12,9},{9,12},{8,13},{7,2},{6,3},{3... | collective-permute-start | bytes 221192 | tf_op jit(solution)/shard_map/ppermute | solution.py:196
  14.8 4.4 %collective-permute-start.6 = (f32[4,16,256]{2,1,0:T(8,128)S(1)}, f32[4,16,256]{2,1,0:T(8,128)S(1)}, u32[]{:S(2)}, u32[]{:S(2)}) collective-permute-start(f32[4,16,256]{2,1,0:T(8,128)S(1)} %shard_map.70.refs_5_), channel_id=1, source_target_pairs={{3,0},{2,1},{1,2},{0,3},{7,4},{6,5},{5,6},{4,7},{11,8},{10,9},{9,1... | collective-permute-start | bytes 196616 | tf_op jit(solution)/shard_map/ppermute | solution.py:181
  16.5 4.0 %collective-permute-start.7 = (f32[4,16,256]{2,1,0:T(8,128)S(1)}, f32[4,16,256]{2,1,0:T(8,128)S(1)}, u32[]{:S(2)}, u32[]{:S(2)}) collective-permute-start(f32[4,16,256]{2,1,0:T(8,128)S(1)} %shard_map.70.refs_5_), channel_id=1, source_target_pairs={{2,0},{3,1},{0,2},{1,3},{6,4},{7,5},{4,6},{5,7},{10,8},{11,9},{8,1... | collective-permute-start | bytes 196616 | tf_op jit(solution)/shard_map/ppermute | solution.py:181
  16.7 3.7 %collective-permute-start.8 = (f32[4,16,256]{2,1,0:T(8,128)S(1)}, f32[4,16,256]{2,1,0:T(8,128)S(1)}, u32[]{:S(2)}, u32[]{:S(2)}) collective-permute-start(f32[4,16,256]{2,1,0:T(8,128)S(1)} %shard_map.70.refs_5_), channel_id=1, source_target_pairs={{1,0},{0,1},{3,2},{2,3},{5,4},{4,5},{7,6},{6,7},{9,8},{8,9},{11,10... | collective-permute-start | bytes 196616 | tf_op jit(solution)/shard_map/ppermute | solution.py:181
  20.6 5.2 %collective-permute-start.9 = (f32[16,128]{1,0:T(8,128)S(1)}, f32[16,128]{1,0:T(8,128)S(1)}, u32[]{:S(2)}, u32[]{:S(2)}) collective-permute-start(f32[16,128]{1,0:T(8,128)S(1)} %get-tuple-element.20.refs_0_), channel_id=1, source_target_pairs={{13,0},{12,1},{9,4},{8,5},{5,8},{4,9},{1,12},{0,13},{15,2},{14,3},... | collective-permute-start | bytes 24584 | tf_op jit(solution)/shard_map/ppermute | solution.py:196
  23.0 4.0 %collective-permute-start.10 = (f32[16,128]{1,0:T(8,128)S(1)}, f32[16,128]{1,0:T(8,128)S(1)}, u32[]{:S(2)}, u32[]{:S(2)}) collective-permute-start(f32[16,128]{1,0:T(8,128)S(1)} %get-tuple-element.20.refs_0_), channel_id=1, source_target_pairs={{9,0},{8,1},{13,4},{12,5},{1,8},{0,9},{5,12},{4,13},{11,2},{10,3},... | collective-permute-start | bytes 24584 | tf_op jit(solution)/shard_map/ppermute | solution.py:196
  23.0 4.0 %collective-permute-start.11 = (f32[16,128]{1,0:T(8,128)S(1)}, f32[16,128]{1,0:T(8,128)S(1)}, u32[]{:S(2)}, u32[]{:S(2)}) collective-permute-start(f32[16,128]{1,0:T(8,128)S(1)} %get-tuple-element.20.refs_0_), channel_id=1, source_target_pairs={{5,0},{4,1},{1,4},{0,5},{13,8},{12,9},{9,12},{8,13},{7,2},{6,3},{3... | collective-permute-start | bytes 24584 | tf_op jit(solution)/shard_map/ppermute | solution.py:196

commit v31 on v29

--- a/solution.py
+++ b/solution.py
@@ -9,7 +9,7 @@
 LINE = ("blk",)
 DIRECT = 8
 VMEM = pltpu.CompilerParams(vmem_limit_bytes=40 * 1024 * 1024)
-PARTIALS, PARTIALS_BACK = (0, 1, 2, 3), (0, 1, 2, 3)
+PARTIALS, PARTIALS_BACK = (0, 1, 3, 2), (0, 1, 3, 2)
 SUMS = (0, 1, 2, 3)
 HALF = 8
 

time: 27.7 us -> 27.9 us (level)
  starting transfers between devices: 12.7 us -> 13.1 us
    ppermute x6, waiting for transfers between devices: 3.94 us -> 3.61 us  [everywhere(): lax.ppermute(value, axes, [(source_of(i, step, count), i) for i in range(...]
    ppermute x6, waiting for transfers between devices: 6.63 us -> 6.93 us  [along_line(): blocks.append(lax.ppermute(value, LINE + ('sub',), pairs))]
    ppermute x6, starting transfers between devices: 4.41 us -> 4.69 us  [everywhere(): lax.ppermute(value, axes, [(source_of(i, step, count), i) for i in range(...]
where the time goes in v31:
time: 27.9 us; the launch traced here: 27.7 us
  starting transfers between devices  13.1 us (47%)
  waiting for transfers between devices  10.5 us (38%)
  Pallas kernels  2.42 us (9%)
  other arithmetic  0.93 us (3%)
  between operations  0.69 us (2%)
    ppermute x6, starting transfers between devices, along_line(): blocks.append(lax.ppermute(value, LINE + ('sub',), pairs))  8.42 us
    ppermute x6, waiting for transfers between devices, along_line(): blocks.append(lax.ppermute(value, LINE + ('sub',), pairs))  6.93 us
    ppermute x6, starting transfers between devices, everywhere(): lax.ppermute(value, axes, [(source_of(i, step, count), i) for i in range(...  4.69 us
    ppermute x6, waiting for transfers between devices, everywhere(): lax.ppermute(value, axes, [(source_of(i, step, count), i) for i in range(...  3.61 us
    convert_element_type x1, other arithmetic, local(): (features.astype(jnp.float32) / lengthscale[:, None]).astype(jnp.bfloat16)  0.93 us
    pallas_call x1, Pallas kernels, local(): pl.pallas_call(lambda *refs: image_kernel(feature_count, plane_count, *re...  0.85 us
    pallas_call x1, Pallas kernels, local(): pl.pallas_call(finish_kernel, out_shape=outs, compiler_params=VMEM)  0.77 us
    pallas_call x1, Pallas kernels, local(): pl.pallas_call(lambda *refs: near_kernel(feature_count, *refs), out_shape...  0.65 us
  transfers between devices with their start and end apart: 12, of which 7 were waited for; matrix products, arithmetic and copies ran while one was open for 0% of the time, Pallas kernels for 2%

profile of v31, /device:TPU:0, one launch (start us, length us, event | category | flops | bytes accessed | tf_op | source)
XLA Modules:
  0.0 27.7 jit_solution(10890640009018065731)
XLA Ops:
  0.6 0.0 copy-start
  0.6 0.9 %divide_convert_fusion.scaled_ref = bf16[128,256]{1,0:T(8,128)(2,1)S(1)} fusion(bf16[128,256]{1,0:T(8,128)(2,1)} %param.4, f32[128]{0:T(128)} %param.5), kind=kLoop, calls=%fused_computation | loop fusion | flops 98304 | bytes 131584 | tf_op jit(solution)/shard_map/convert_element_type | solution.py:214
  1.6 0.0 copy-done
  1.6 0.5 %collective-permute-start = (bf16[160,256]{1,0:T(8,128)(2,1)S(1)}, bf16[160,256]{1,0:T(8,128)(2,1)S(1)}, u32[]{:S(2)}, u32[]{:S(2)}) collective-permute-start(bf16[160,256]{1,0:T(8,128)(2,1)S(1)} %get-tuple-element.10.refs_0_), channel_id=1, source_target_pairs={{1,0},{0,1},{3,2},{2,3},{5,4},{4,5},{7,6},{6,7},{9,8},{8,9},{11,10... | collective-permute-start | bytes 245768 | tf_op jit(solution)/shard_map/ppermute | solution.py:180
  2.1 0.0 copy-start.1
  2.1 4.7 %collective-permute-start.4 = (bf16[144,256]{1,0:T(8,128)(2,1)S(1)}, bf16[144,256]{1,0:T(8,128)(2,1)S(1)}, u32[]{:S(2)}, u32[]{:S(2)}) collective-permute-start(bf16[144,256]{1,0:T(8,128)(2,1)S(1)} %get-tuple-element.11.refs_2_.refs_4_), channel_id=1, source_target_pairs={{13,0},{12,1},{9,4},{8,5},{5,8},{4,9},{1,12},{0,13},{15,2},{14,3},... | collective-permute-start | bytes 221192 | tf_op jit(solution)/shard_map/ppermute | solution.py:195
  6.9 0.0 collective-permute-start.3
  6.9 1.5 %collective-permute-start.1 = (bf16[160,256]{1,0:T(8,128)(2,1)S(1)}, bf16[160,256]{1,0:T(8,128)(2,1)S(1)}, u32[]{:S(2)}, u32[]{:S(2)}) collective-permute-start(bf16[160,256]{1,0:T(8,128)(2,1)S(1)} %get-tuple-element.10.refs_0_), channel_id=1, source_target_pairs={{2,0},{0,2},{3,1},{1,3},{6,4},{4,6},{7,5},{5,7},{10,8},{8,10},{11,... | collective-permute-start | bytes 245768 | tf_op jit(solution)/shard_map/ppermute | solution.py:180
  8.4 0.0 collective-permute-done.refs_1_
  8.4 0.5 %collective-permute-start.2 = (bf16[160,256]{1,0:T(8,128)(2,1)S(1)}, bf16[160,256]{1,0:T(8,128)(2,1)S(1)}, u32[]{:S(2)}, u32[]{:S(2)}) collective-permute-start(bf16[160,256]{1,0:T(8,128)(2,1)S(1)} %collective-permute-done.refs_1_), channel_id=1, source_target_pairs={{2,0},{0,2},{3,1},{1,3},{6,4},{4,6},{7,5},{5,7},{10,8},{8,10},{11,... | collective-permute-start | bytes 245768 | tf_op jit(solution)/shard_map/ppermute | solution.py:180
  8.9 0.0 collective-permute-start.5
  8.9 0.6 %collective-permute-done.4.refs_4_.refs_6_ = bf16[144,256]{1,0:T(8,128)(2,1)S(1)} collective-permute-done((bf16[144,256]{1,0:T(8,128)(2,1)S(1)}, bf16[144,256]{1,0:T(8,128)(2,1)S(1)}, u32[]{:S(2)}, u32[]{:S(2)}) %collective-permute-start.4) | collective-permute-done | bytes 73760 | tf_op jit(solution)/shard_map/ppermute | solution.py:195
  9.5 3.6 %collective-permute-done.3.refs_3_.refs_5_ = bf16[144,256]{1,0:T(8,128)(2,1)S(1)} collective-permute-done((bf16[144,256]{1,0:T(8,128)(2,1)S(1)}, bf16[144,256]{1,0:T(8,128)(2,1)S(1)}, u32[]{:S(2)}, u32[]{:S(2)}) %collective-permute-start.3) | collective-permute-done | bytes 73760 | tf_op jit(solution)/shard_map/ppermute | solution.py:195
  13.1 0.0 copy-done.1
  13.1 0.6 %shard_map.68 = (bf16[144,512]{1,0:T(8,128)(2,1)S(1)}, bf16[3,256,144]{2,1,0:T(8,128)(2,1)S(1)}, f32[16,512]{1,0:T(8,128)S(1)}) custom-call(bf16[160,256]{1,0:T(8,128)(2,1)S(1)} %get-tuple-element.10.refs_0_, bf16[160,256]{1,0:T(8,128)(2,1)S(1)} %collective-permute-done.refs_1_, bf16[144,256]{1,0:T(8,128)(2,1)S(1)} %get-tuple-element.11.refs_2_.refs_4_, ...), custom_call_target="tpu_custom_call" | custom-call | flops 226492416 | bytes 4096 | tf_op jit(solution)/shard_map/pallas_call | solution.py:231
  13.7 0.0 collective-permute-done.1.refs_0_.refs_2_
  13.7 0.0 collective-permute-done.2.refs_1_.refs_3_
  13.8 0.9 %collective-permute-done.5.refs_7_ = bf16[144,256]{1,0:T(8,128)(2,1)S(1)} collective-permute-done((bf16[144,256]{1,0:T(8,128)(2,1)S(1)}, bf16[144,256]{1,0:T(8,128)(2,1)S(1)}, u32[]{:S(2)}, u32[]{:S(2)}) %collective-permute-start.5) | collective-permute-done | bytes 73760 | tf_op jit(solution)/shard_map/ppermute | solution.py:195
  14.6 0.8 %shard_map.70.refs_5_ = f32[4,16,256]{2,1,0:T(8,128)S(1)} custom-call(bf16[144,512]{1,0:T(8,128)(2,1)S(1)} %get-tuple-element.12.refs_0_, f32[16,512]{1,0:T(8,128)S(1)} %get-tuple-element.13.refs_1_, bf16[1,144,512]{2,1,0:T(8,128)(2,1)S(1)} %shard_map.69.refs_2_, bf16[3,256,144]{2,1,0:T(8,128)(2,1)S(1)} %get-tuple-element.14.refs_3_, ...), custom_call_target="tpu_custom_call" | custom-call | tf_op jit(solution)/shard_map/pallas_call | solution.py:250
  15.5 1.5 %collective-permute-start.8 = (f32[4,16,256]{2,1,0:T(8,128)S(1)}, f32[4,16,256]{2,1,0:T(8,128)S(1)}, u32[]{:S(2)}, u32[]{:S(2)}) collective-permute-start(f32[4,16,256]{2,1,0:T(8,128)S(1)} %shard_map.70.refs_5_), channel_id=1, source_target_pairs={{2,0},{3,1},{0,2},{1,3},{6,4},{7,5},{4,6},{5,7},{10,8},{11,9},{8,1... | collective-permute-start | bytes 196616 | tf_op jit(solution)/shard_map/ppermute | solution.py:180
  17.0 0.0 collective-permute-start.7
  17.0 0.7 %collective-permute-start.6 = (f32[4,16,256]{2,1,0:T(8,128)S(1)}, f32[4,16,256]{2,1,0:T(8,128)S(1)}, u32[]{:S(2)}, u32[]{:S(2)}) collective-permute-start(f32[4,16,256]{2,1,0:T(8,128)S(1)} %shard_map.70.refs_5_), channel_id=1, source_target_pairs={{1,0},{0,1},{3,2},{2,3},{5,4},{4,5},{7,6},{6,7},{9,8},{8,9},{11,10... | collective-permute-start | bytes 196616 | tf_op jit(solution)/shard_map/ppermute | solution.py:180
  17.6 2.1 %collective-permute-done.8.refs_8_ = f32[4,16,256]{2,1,0:T(8,128)S(1)} collective-permute-done((f32[4,16,256]{2,1,0:T(8,128)S(1)}, f32[4,16,256]{2,1,0:T(8,128)S(1)}, u32[]{:S(2)}, u32[]{:S(2)}) %collective-permute-start.8) | collective-permute-done | bytes 65568 | tf_op jit(solution)/shard_map/ppermute | solution.py:180
  19.8 1.5 %collective-permute-done.7.refs_7_ = f32[4,16,256]{2,1,0:T(8,128)S(1)} collective-permute-done((f32[4,16,256]{2,1,0:T(8,128)S(1)}, f32[4,16,256]{2,1,0:T(8,128)S(1)}, u32[]{:S(2)}, u32[]{:S(2)}) %collective-permute-start.7) | collective-permute-done | bytes 65568 | tf_op jit(solution)/shard_map/ppermute | solution.py:180
  21.2 0.0 collective-permute-done.6.refs_6_
  21.2 0.1 shard_map.71
  21.4 1.6 %collective-permute-start.11 = (f32[16,128]{1,0:T(8,128)S(1)}, f32[16,128]{1,0:T(8,128)S(1)}, u32[]{:S(2)}, u32[]{:S(2)}) collective-permute-start(f32[16,128]{1,0:T(8,128)S(1)} %get-tuple-element.16.refs_0_), channel_id=1, source_target_pairs={{13,0},{12,1},{9,4},{8,5},{5,8},{4,9},{1,12},{0,13},{15,2},{14,3},... | collective-permute-start | bytes 24584 | tf_op jit(solution)/shard_map/ppermute | solution.py:195
  23.0 0.0 collective-permute-start.10
  23.0 2.1 %collective-permute-start.9 = (f32[16,128]{1,0:T(8,128)S(1)}, f32[16,128]{1,0:T(8,128)S(1)}, u32[]{:S(2)}, u32[]{:S(2)}) collective-permute-start(f32[16,128]{1,0:T(8,128)S(1)} %get-tuple-element.16.refs_0_), channel_id=1, source_target_pairs={{5,0},{4,1},{1,4},{0,5},{13,8},{12,9},{9,12},{8,13},{7,2},{6,3},{3... | collective-permute-start | bytes 24584 | tf_op jit(solution)/shard_map/ppermute | solution.py:195
  25.0 1.2 %collective-permute-done.11.refs_3_ = f32[16,128]{1,0:T(8,128)S(1)} collective-permute-done((f32[16,128]{1,0:T(8,128)S(1)}, f32[16,128]{1,0:T(8,128)S(1)}, u32[]{:S(2)}, u32[]{:S(2)}) %collective-permute-start.11) | collective-permute-done | bytes 8224 | tf_op jit(solution)/shard_map/ppermute | solution.py:195
  26.2 0.7 %collective-permute-done.10.refs_2_ = f32[16,128]{1,0:T(8,128)S(1)} collective-permute-done((f32[16,128]{1,0:T(8,128)S(1)}, f32[16,128]{1,0:T(8,128)S(1)}, u32[]{:S(2)}, u32[]{:S(2)}) %collective-permute-start.10) | collective-permute-done | bytes 8224 | tf_op jit(solution)/shard_map/ppermute | solution.py:195
  26.9 0.0 collective-permute-done.9.refs_1_
  26.9 0.8 %shard_map.72 = (f32[16,256]{1,0:T(8,128)}, f32[16,256]{1,0:T(8,128)}, f32[16,256]{1,0:T(8,128)}) custom-call(f32[16,256]{1,0:T(8,128)S(1)} %get-tuple-element.15.image_ref, f32[16,256]{1,0:T(8,128)S(1)} %copy-done, f32[16,128]{1,0:T(8,128)S(1)} %get-tuple-element.16.refs_0_, f32[16,128]{1,0:T(8,128)S(1)} %collective-permute-done.9.refs_1_, ...), custom_call_target="tpu_custom_call" | custom-call | tf_op jit(solution)/shard_map/pallas_call | solution.py:265
  (2 shorter events, 0.0 us)
Async XLA Ops:
  0.6 1.0 %copy-start = (f32[16,256]{1,0:T(8,128)S(1)}, f32[16,256]{1,0:T(8,128)}, u32[]{:S(2)}) copy-start(f32[16,256]{1,0:T(8,128)} %probes_ref.3) | copy-start | bytes 49156
  1.6 6.7 %collective-permute-start = (bf16[160,256]{1,0:T(8,128)(2,1)S(1)}, bf16[160,256]{1,0:T(8,128)(2,1)S(1)}, u32[]{:S(2)}, u32[]{:S(2)}) collective-permute-start(bf16[160,256]{1,0:T(8,128)(2,1)S(1)} %get-tuple-element.10.refs_0_), channel_id=1, source_target_pairs={{1,0},{0,1},{3,2},{2,3},{5,4},{4,5},{7,6},{6,7},{9,8},{8,9},{11,10... | collective-permute-start | bytes 245768 | tf_op jit(solution)/shard_map/ppermute | solution.py:180
  2.1 10.9 %copy-start.1 = (f32[256]{0:T(256)S(1)}, f32[256]{0:T(256)}, u32[]{:S(2)}) copy-start(f32[256]{0:T(256)} %param.6) | copy-start | bytes 3076
  2.1 7.4 %collective-permute-start.4 = (bf16[144,256]{1,0:T(8,128)(2,1)S(1)}, bf16[144,256]{1,0:T(8,128)(2,1)S(1)}, u32[]{:S(2)}, u32[]{:S(2)}) collective-permute-start(bf16[144,256]{1,0:T(8,128)(2,1)S(1)} %get-tuple-element.11.refs_2_.refs_4_), channel_id=1, source_target_pairs={{13,0},{12,1},{9,4},{8,5},{5,8},{4,9},{1,12},{0,13},{15,2},{14,3},... | collective-permute-start | bytes 221192 | tf_op jit(solution)/shard_map/ppermute | solution.py:195
  6.9 6.2 %collective-permute-start.3 = (bf16[144,256]{1,0:T(8,128)(2,1)S(1)}, bf16[144,256]{1,0:T(8,128)(2,1)S(1)}, u32[]{:S(2)}, u32[]{:S(2)}) collective-permute-start(bf16[144,256]{1,0:T(8,128)(2,1)S(1)} %get-tuple-element.11.refs_2_.refs_4_), channel_id=1, source_target_pairs={{9,0},{8,1},{13,4},{12,5},{1,8},{0,9},{5,12},{4,13},{11,2},{10,3},... | collective-permute-start | bytes 221192 | tf_op jit(solution)/shard_map/ppermute | solution.py:195
  6.9 6.9 %collective-permute-start.1 = (bf16[160,256]{1,0:T(8,128)(2,1)S(1)}, bf16[160,256]{1,0:T(8,128)(2,1)S(1)}, u32[]{:S(2)}, u32[]{:S(2)}) collective-permute-start(bf16[160,256]{1,0:T(8,128)(2,1)S(1)} %get-tuple-element.10.refs_0_), channel_id=1, source_target_pairs={{2,0},{0,2},{3,1},{1,3},{6,4},{4,6},{7,5},{5,7},{10,8},{8,10},{11,... | collective-permute-start | bytes 245768 | tf_op jit(solution)/shard_map/ppermute | solution.py:180
  8.4 5.4 %collective-permute-start.2 = (bf16[160,256]{1,0:T(8,128)(2,1)S(1)}, bf16[160,256]{1,0:T(8,128)(2,1)S(1)}, u32[]{:S(2)}, u32[]{:S(2)}) collective-permute-start(bf16[160,256]{1,0:T(8,128)(2,1)S(1)} %collective-permute-done.refs_1_), channel_id=1, source_target_pairs={{2,0},{0,2},{3,1},{1,3},{6,4},{4,6},{7,5},{5,7},{10,8},{8,10},{11,... | collective-permute-start | bytes 245768 | tf_op jit(solution)/shard_map/ppermute | solution.py:180
  8.9 5.8 %collective-permute-start.5 = (bf16[144,256]{1,0:T(8,128)(2,1)S(1)}, bf16[144,256]{1,0:T(8,128)(2,1)S(1)}, u32[]{:S(2)}, u32[]{:S(2)}) collective-permute-start(bf16[144,256]{1,0:T(8,128)(2,1)S(1)} %get-tuple-element.11.refs_2_.refs_4_), channel_id=1, source_target_pairs={{5,0},{4,1},{1,4},{0,5},{13,8},{12,9},{9,12},{8,13},{7,2},{6,3},{3... | collective-permute-start | bytes 221192 | tf_op jit(solution)/shard_map/ppermute | solution.py:195
  15.5 4.3 %collective-permute-start.8 = (f32[4,16,256]{2,1,0:T(8,128)S(1)}, f32[4,16,256]{2,1,0:T(8,128)S(1)}, u32[]{:S(2)}, u32[]{:S(2)}) collective-permute-start(f32[4,16,256]{2,1,0:T(8,128)S(1)} %shard_map.70.refs_5_), channel_id=1, source_target_pairs={{2,0},{3,1},{0,2},{1,3},{6,4},{7,5},{4,6},{5,7},{10,8},{11,9},{8,1... | collective-permute-start | bytes 196616 | tf_op jit(solution)/shard_map/ppermute | solution.py:180
  17.0 4.3 %collective-permute-start.7 = (f32[4,16,256]{2,1,0:T(8,128)S(1)}, f32[4,16,256]{2,1,0:T(8,128)S(1)}, u32[]{:S(2)}, u32[]{:S(2)}) collective-permute-start(f32[4,16,256]{2,1,0:T(8,128)S(1)} %shard_map.70.refs_5_), channel_id=1, source_target_pairs={{3,0},{2,1},{1,2},{0,3},{7,4},{6,5},{5,6},{4,7},{11,8},{10,9},{9,1... | collective-permute-start | bytes 196616 | tf_op jit(solution)/shard_map/ppermute | solution.py:180
  17.0 4.3 %collective-permute-start.6 = (f32[4,16,256]{2,1,0:T(8,128)S(1)}, f32[4,16,256]{2,1,0:T(8,128)S(1)}, u32[]{:S(2)}, u32[]{:S(2)}) collective-permute-start(f32[4,16,256]{2,1,0:T(8,128)S(1)} %shard_map.70.refs_5_), channel_id=1, source_target_pairs={{1,0},{0,1},{3,2},{2,3},{5,4},{4,5},{7,6},{6,7},{9,8},{8,9},{11,10... | collective-permute-start | bytes 196616 | tf_op jit(solution)/shard_map/ppermute | solution.py:180
  21.4 4.9 %collective-permute-start.11 = (f32[16,128]{1,0:T(8,128)S(1)}, f32[16,128]{1,0:T(8,128)S(1)}, u32[]{:S(2)}, u32[]{:S(2)}) collective-permute-start(f32[16,128]{1,0:T(8,128)S(1)} %get-tuple-element.16.refs_0_), channel_id=1, source_target_pairs={{13,0},{12,1},{9,4},{8,5},{5,8},{4,9},{1,12},{0,13},{15,2},{14,3},... | collective-permute-start | bytes 24584 | tf_op jit(solution)/shard_map/ppermute | solution.py:195
  23.0 4.0 %collective-permute-start.10 = (f32[16,128]{1,0:T(8,128)S(1)}, f32[16,128]{1,0:T(8,128)S(1)}, u32[]{:S(2)}, u32[]{:S(2)}) collective-permute-start(f32[16,128]{1,0:T(8,128)S(1)} %get-tuple-element.16.refs_0_), channel_id=1, source_target_pairs={{9,0},{8,1},{13,4},{12,5},{1,8},{0,9},{5,12},{4,13},{11,2},{10,3},... | collective-permute-start | bytes 24584 | tf_op jit(solution)/shard_map/ppermute | solution.py:195
  23.0 4.0 %collective-permute-start.9 = (f32[16,128]{1,0:T(8,128)S(1)}, f32[16,128]{1,0:T(8,128)S(1)}, u32[]{:S(2)}, u32[]{:S(2)}) collective-permute-start(f32[16,128]{1,0:T(8,128)S(1)} %get-tuple-element.16.refs_0_), channel_id=1, source_target_pairs={{5,0},{4,1},{1,4},{0,5},{13,8},{12,9},{9,12},{8,13},{7,2},{6,3},{3... | collective-permute-start | bytes 24584 | tf_op jit(solution)/shard_map/ppermute | solution.py:195

commit v32 on v29

--- a/solution.py
+++ b/solution.py
@@ -10,7 +10,7 @@
 DIRECT = 8
 VMEM = pltpu.CompilerParams(vmem_limit_bytes=40 * 1024 * 1024)
 PARTIALS, PARTIALS_BACK = (0, 1, 2, 3), (0, 1, 2, 3)
-SUMS = (0, 1, 2, 3)
+SUMS = (0, 2, 1, 3)
 HALF = 8
 
 

time: 27.7 us -> 28 us (1.011)
  waiting for transfers between devices: 10.6 us -> 11.1 us
    ppermute x6, waiting for transfers between devices: 6.63 us -> 7.17 us  [along_line(): blocks.append(lax.ppermute(value, LINE + ('sub',), pairs))]
where the time goes in v32:
time: 28 us; the launch traced here: 27.8 us
  starting transfers between devices  12.7 us (45%)
  waiting for transfers between devices  11.1 us (40%)
  Pallas kernels  2.42 us (9%)
  other arithmetic  0.93 us (3%)
  between operations  0.69 us (2%)
    ppermute x6, starting transfers between devices, along_line(): blocks.append(lax.ppermute(value, LINE + ('sub',), pairs))  8.27 us
    ppermute x6, waiting for transfers between devices, along_line(): blocks.append(lax.ppermute(value, LINE + ('sub',), pairs))  7.17 us
    ppermute x6, starting transfers between devices, everywhere(): lax.ppermute(value, axes, [(source_of(i, step, count), i) for i in range(...  4.41 us
    ppermute x6, waiting for transfers between devices, everywhere(): lax.ppermute(value, axes, [(source_of(i, step, count), i) for i in range(...  3.94 us
    convert_element_type x1, other arithmetic, local(): (features.astype(jnp.float32) / lengthscale[:, None]).astype(jnp.bfloat16)  0.93 us
    pallas_call x1, Pallas kernels, local(): pl.pallas_call(lambda *refs: image_kernel(feature_count, plane_count, *re...  0.85 us
    pallas_call x1, Pallas kernels, local(): pl.pallas_call(finish_kernel, out_shape=outs, compiler_params=VMEM)  0.77 us
    pallas_call x1, Pallas kernels, local(): pl.pallas_call(lambda *refs: near_kernel(feature_count, *refs), out_shape...  0.65 us
  transfers between devices with their start and end apart: 12, of which 7 were waited for; matrix products, arithmetic and copies ran while one was open for 0% of the time, Pallas kernels for 2%

profile of v32, /device:TPU:0, one launch (start us, length us, event | category | flops | bytes accessed | tf_op | source)
XLA Modules:
  0.0 27.8 jit_solution(10912166978034800088)
XLA Ops:
  0.6 0.0 copy-start
  0.6 0.9 %divide_convert_fusion.scaled_ref = bf16[128,256]{1,0:T(8,128)(2,1)S(1)} fusion(bf16[128,256]{1,0:T(8,128)(2,1)} %param.4, f32[128]{0:T(128)} %param.5), kind=kLoop, calls=%fused_computation | loop fusion | flops 98304 | bytes 131584 | tf_op jit(solution)/shard_map/convert_element_type | solution.py:214
  1.6 0.0 copy-done
  1.6 0.5 %collective-permute-start = (bf16[160,256]{1,0:T(8,128)(2,1)S(1)}, bf16[160,256]{1,0:T(8,128)(2,1)S(1)}, u32[]{:S(2)}, u32[]{:S(2)}) collective-permute-start(bf16[160,256]{1,0:T(8,128)(2,1)S(1)} %get-tuple-element.10.refs_0_), channel_id=1, source_target_pairs={{1,0},{0,1},{3,2},{2,3},{5,4},{4,5},{7,6},{6,7},{9,8},{8,9},{11,10... | collective-permute-start | bytes 245768 | tf_op jit(solution)/shard_map/ppermute | solution.py:180
  2.1 0.0 copy-start.1
  2.1 4.7 %collective-permute-start.4 = (bf16[144,256]{1,0:T(8,128)(2,1)S(1)}, bf16[144,256]{1,0:T(8,128)(2,1)S(1)}, u32[]{:S(2)}, u32[]{:S(2)}) collective-permute-start(bf16[144,256]{1,0:T(8,128)(2,1)S(1)} %get-tuple-element.11.refs_2_.refs_4_), channel_id=1, source_target_pairs={{13,0},{12,1},{9,4},{8,5},{5,8},{4,9},{1,12},{0,13},{15,2},{14,3},... | collective-permute-start | bytes 221192 | tf_op jit(solution)/shard_map/ppermute | solution.py:195
  6.9 0.0 collective-permute-start.3
  6.9 1.5 %collective-permute-start.1 = (bf16[160,256]{1,0:T(8,128)(2,1)S(1)}, bf16[160,256]{1,0:T(8,128)(2,1)S(1)}, u32[]{:S(2)}, u32[]{:S(2)}) collective-permute-start(bf16[160,256]{1,0:T(8,128)(2,1)S(1)} %get-tuple-element.10.refs_0_), channel_id=1, source_target_pairs={{2,0},{0,2},{3,1},{1,3},{6,4},{4,6},{7,5},{5,7},{10,8},{8,10},{11,... | collective-permute-start | bytes 245768 | tf_op jit(solution)/shard_map/ppermute | solution.py:180
  8.4 0.0 collective-permute-done.refs_1_
  8.4 0.5 %collective-permute-start.2 = (bf16[160,256]{1,0:T(8,128)(2,1)S(1)}, bf16[160,256]{1,0:T(8,128)(2,1)S(1)}, u32[]{:S(2)}, u32[]{:S(2)}) collective-permute-start(bf16[160,256]{1,0:T(8,128)(2,1)S(1)} %collective-permute-done.refs_1_), channel_id=1, source_target_pairs={{2,0},{0,2},{3,1},{1,3},{6,4},{4,6},{7,5},{5,7},{10,8},{8,10},{11,... | collective-permute-start | bytes 245768 | tf_op jit(solution)/shard_map/ppermute | solution.py:180
  8.9 0.0 collective-permute-start.5
  8.9 0.6 %collective-permute-done.4.refs_4_.refs_6_ = bf16[144,256]{1,0:T(8,128)(2,1)S(1)} collective-permute-done((bf16[144,256]{1,0:T(8,128)(2,1)S(1)}, bf16[144,256]{1,0:T(8,128)(2,1)S(1)}, u32[]{:S(2)}, u32[]{:S(2)}) %collective-permute-start.4) | collective-permute-done | bytes 73760 | tf_op jit(solution)/shard_map/ppermute | solution.py:195
  9.5 3.6 %collective-permute-done.3.refs_3_.refs_5_ = bf16[144,256]{1,0:T(8,128)(2,1)S(1)} collective-permute-done((bf16[144,256]{1,0:T(8,128)(2,1)S(1)}, bf16[144,256]{1,0:T(8,128)(2,1)S(1)}, u32[]{:S(2)}, u32[]{:S(2)}) %collective-permute-start.3) | collective-permute-done | bytes 73760 | tf_op jit(solution)/shard_map/ppermute | solution.py:195
  13.1 0.0 copy-done.1
  13.1 0.6 %shard_map.68 = (bf16[144,512]{1,0:T(8,128)(2,1)S(1)}, bf16[3,256,144]{2,1,0:T(8,128)(2,1)S(1)}, f32[16,512]{1,0:T(8,128)S(1)}) custom-call(bf16[160,256]{1,0:T(8,128)(2,1)S(1)} %get-tuple-element.10.refs_0_, bf16[160,256]{1,0:T(8,128)(2,1)S(1)} %collective-permute-done.refs_1_, bf16[144,256]{1,0:T(8,128)(2,1)S(1)} %get-tuple-element.11.refs_2_.refs_4_, ...), custom_call_target="tpu_custom_call" | custom-call | flops 226492416 | bytes 4096 | tf_op jit(solution)/shard_map/pallas_call | solution.py:231
  13.7 0.0 collective-permute-done.1.refs_0_.refs_2_
  13.7 0.0 collective-permute-done.2.refs_1_.refs_3_
  13.8 0.9 %collective-permute-done.5.refs_7_ = bf16[144,256]{1,0:T(8,128)(2,1)S(1)} collective-permute-done((bf16[144,256]{1,0:T(8,128)(2,1)S(1)}, bf16[144,256]{1,0:T(8,128)(2,1)S(1)}, u32[]{:S(2)}, u32[]{:S(2)}) %collective-permute-start.5) | collective-permute-done | bytes 73760 | tf_op jit(solution)/shard_map/ppermute | solution.py:195
  14.6 0.8 %shard_map.70.refs_5_ = f32[4,16,256]{2,1,0:T(8,128)S(1)} custom-call(bf16[144,512]{1,0:T(8,128)(2,1)S(1)} %get-tuple-element.12.refs_0_, f32[16,512]{1,0:T(8,128)S(1)} %get-tuple-element.13.refs_1_, bf16[1,144,512]{2,1,0:T(8,128)(2,1)S(1)} %shard_map.69.refs_2_, bf16[3,256,144]{2,1,0:T(8,128)(2,1)S(1)} %get-tuple-element.14.refs_3_, ...), custom_call_target="tpu_custom_call" | custom-call | tf_op jit(solution)/shard_map/pallas_call | solution.py:250
  15.5 1.1 %collective-permute-start.8 = (f32[4,16,256]{2,1,0:T(8,128)S(1)}, f32[4,16,256]{2,1,0:T(8,128)S(1)}, u32[]{:S(2)}, u32[]{:S(2)}) collective-permute-start(f32[4,16,256]{2,1,0:T(8,128)S(1)} %shard_map.70.refs_5_), channel_id=1, source_target_pairs={{3,0},{2,1},{1,2},{0,3},{7,4},{6,5},{5,6},{4,7},{11,8},{10,9},{9,1... | collective-permute-start | bytes 196616 | tf_op jit(solution)/shard_map/ppermute | solution.py:180
  16.6 0.5 %collective-permute-start.7 = (f32[4,16,256]{2,1,0:T(8,128)S(1)}, f32[4,16,256]{2,1,0:T(8,128)S(1)}, u32[]{:S(2)}, u32[]{:S(2)}) collective-permute-start(f32[4,16,256]{2,1,0:T(8,128)S(1)} %shard_map.70.refs_5_), channel_id=1, source_target_pairs={{2,0},{3,1},{0,2},{1,3},{6,4},{7,5},{4,6},{5,7},{10,8},{11,9},{8,1... | collective-permute-start | bytes 196616 | tf_op jit(solution)/shard_map/ppermute | solution.py:180
  17.1 0.3 collective-permute-start.6
  17.4 2.4 %collective-permute-done.8.refs_8_ = f32[4,16,256]{2,1,0:T(8,128)S(1)} collective-permute-done((f32[4,16,256]{2,1,0:T(8,128)S(1)}, f32[4,16,256]{2,1,0:T(8,128)S(1)}, u32[]{:S(2)}, u32[]{:S(2)}) %collective-permute-start.8) | collective-permute-done | bytes 65568 | tf_op jit(solution)/shard_map/ppermute | solution.py:180
  19.8 1.5 %collective-permute-done.7.refs_7_ = f32[4,16,256]{2,1,0:T(8,128)S(1)} collective-permute-done((f32[4,16,256]{2,1,0:T(8,128)S(1)}, f32[4,16,256]{2,1,0:T(8,128)S(1)}, u32[]{:S(2)}, u32[]{:S(2)}) %collective-permute-start.7) | collective-permute-done | bytes 65568 | tf_op jit(solution)/shard_map/ppermute | solution.py:180
  21.3 0.0 collective-permute-done.6.refs_6_
  21.3 0.1 shard_map.71
  21.4 0.9 %collective-permute-start.11 = (f32[16,128]{1,0:T(8,128)S(1)}, f32[16,128]{1,0:T(8,128)S(1)}, u32[]{:S(2)}, u32[]{:S(2)}) collective-permute-start(f32[16,128]{1,0:T(8,128)S(1)} %get-tuple-element.16.refs_0_), channel_id=1, source_target_pairs={{13,0},{12,1},{9,4},{8,5},{5,8},{4,9},{1,12},{0,13},{15,2},{14,3},... | collective-permute-start | bytes 24584 | tf_op jit(solution)/shard_map/ppermute | solution.py:195
  22.3 0.8 %collective-permute-start.10 = (f32[16,128]{1,0:T(8,128)S(1)}, f32[16,128]{1,0:T(8,128)S(1)}, u32[]{:S(2)}, u32[]{:S(2)}) collective-permute-start(f32[16,128]{1,0:T(8,128)S(1)} %get-tuple-element.16.refs_0_), channel_id=1, source_target_pairs={{5,0},{4,1},{1,4},{0,5},{13,8},{12,9},{9,12},{8,13},{7,2},{6,3},{3... | collective-permute-start | bytes 24584 | tf_op jit(solution)/shard_map/ppermute | solution.py:195
  23.1 1.9 %collective-permute-start.9 = (f32[16,128]{1,0:T(8,128)S(1)}, f32[16,128]{1,0:T(8,128)S(1)}, u32[]{:S(2)}, u32[]{:S(2)}) collective-permute-start(f32[16,128]{1,0:T(8,128)S(1)} %get-tuple-element.16.refs_0_), channel_id=1, source_target_pairs={{9,0},{8,1},{13,4},{12,5},{1,8},{0,9},{5,12},{4,13},{11,2},{10,3},... | collective-permute-start | bytes 24584 | tf_op jit(solution)/shard_map/ppermute | solution.py:195
  24.9 1.4 %collective-permute-done.11.refs_3_ = f32[16,128]{1,0:T(8,128)S(1)} collective-permute-done((f32[16,128]{1,0:T(8,128)S(1)}, f32[16,128]{1,0:T(8,128)S(1)}, u32[]{:S(2)}, u32[]{:S(2)}) %collective-permute-start.11) | collective-permute-done | bytes 8224 | tf_op jit(solution)/shard_map/ppermute | solution.py:195
  26.4 0.0 collective-permute-done.10.refs_2_
  26.4 0.7 %collective-permute-done.9.refs_1_ = f32[16,128]{1,0:T(8,128)S(1)} collective-permute-done((f32[16,128]{1,0:T(8,128)S(1)}, f32[16,128]{1,0:T(8,128)S(1)}, u32[]{:S(2)}, u32[]{:S(2)}) %collective-permute-start.9) | collective-permute-done | bytes 8224 | tf_op jit(solution)/shard_map/ppermute | solution.py:195
  27.1 0.8 %shard_map.72 = (f32[16,256]{1,0:T(8,128)}, f32[16,256]{1,0:T(8,128)}, f32[16,256]{1,0:T(8,128)}) custom-call(f32[16,256]{1,0:T(8,128)S(1)} %get-tuple-element.15.image_ref, f32[16,256]{1,0:T(8,128)S(1)} %copy-done, f32[16,128]{1,0:T(8,128)S(1)} %get-tuple-element.16.refs_0_, f32[16,128]{1,0:T(8,128)S(1)} %collective-permute-done.9.refs_1_, ...), custom_call_target="tpu_custom_call" | custom-call | tf_op jit(solution)/shard_map/pallas_call | solution.py:265
  (2 shorter events, 0.0 us)
Async XLA Ops:
  0.6 1.0 %copy-start = (f32[16,256]{1,0:T(8,128)S(1)}, f32[16,256]{1,0:T(8,128)}, u32[]{:S(2)}) copy-start(f32[16,256]{1,0:T(8,128)} %probes_ref.3) | copy-start | bytes 49156
  1.6 6.7 %collective-permute-start = (bf16[160,256]{1,0:T(8,128)(2,1)S(1)}, bf16[160,256]{1,0:T(8,128)(2,1)S(1)}, u32[]{:S(2)}, u32[]{:S(2)}) collective-permute-start(bf16[160,256]{1,0:T(8,128)(2,1)S(1)} %get-tuple-element.10.refs_0_), channel_id=1, source_target_pairs={{1,0},{0,1},{3,2},{2,3},{5,4},{4,5},{7,6},{6,7},{9,8},{8,9},{11,10... | collective-permute-start | bytes 245768 | tf_op jit(solution)/shard_map/ppermute | solution.py:180
  2.1 10.9 %copy-start.1 = (f32[256]{0:T(256)S(1)}, f32[256]{0:T(256)}, u32[]{:S(2)}) copy-start(f32[256]{0:T(256)} %param.6) | copy-start | bytes 3076
  2.1 7.4 %collective-permute-start.4 = (bf16[144,256]{1,0:T(8,128)(2,1)S(1)}, bf16[144,256]{1,0:T(8,128)(2,1)S(1)}, u32[]{:S(2)}, u32[]{:S(2)}) collective-permute-start(bf16[144,256]{1,0:T(8,128)(2,1)S(1)} %get-tuple-element.11.refs_2_.refs_4_), channel_id=1, source_target_pairs={{13,0},{12,1},{9,4},{8,5},{5,8},{4,9},{1,12},{0,13},{15,2},{14,3},... | collective-permute-start | bytes 221192 | tf_op jit(solution)/shard_map/ppermute | solution.py:195
  6.9 6.2 %collective-permute-start.3 = (bf16[144,256]{1,0:T(8,128)(2,1)S(1)}, bf16[144,256]{1,0:T(8,128)(2,1)S(1)}, u32[]{:S(2)}, u32[]{:S(2)}) collective-permute-start(bf16[144,256]{1,0:T(8,128)(2,1)S(1)} %get-tuple-element.11.refs_2_.refs_4_), channel_id=1, source_target_pairs={{9,0},{8,1},{13,4},{12,5},{1,8},{0,9},{5,12},{4,13},{11,2},{10,3},... | collective-permute-start | bytes 221192 | tf_op jit(solution)/shard_map/ppermute | solution.py:195
  6.9 6.9 %collective-permute-start.1 = (bf16[160,256]{1,0:T(8,128)(2,1)S(1)}, bf16[160,256]{1,0:T(8,128)(2,1)S(1)}, u32[]{:S(2)}, u32[]{:S(2)}) collective-permute-start(bf16[160,256]{1,0:T(8,128)(2,1)S(1)} %get-tuple-element.10.refs_0_), channel_id=1, source_target_pairs={{2,0},{0,2},{3,1},{1,3},{6,4},{4,6},{7,5},{5,7},{10,8},{8,10},{11,... | collective-permute-start | bytes 245768 | tf_op jit(solution)/shard_map/ppermute | solution.py:180
  8.4 5.4 %collective-permute-start.2 = (bf16[160,256]{1,0:T(8,128)(2,1)S(1)}, bf16[160,256]{1,0:T(8,128)(2,1)S(1)}, u32[]{:S(2)}, u32[]{:S(2)}) collective-permute-start(bf16[160,256]{1,0:T(8,128)(2,1)S(1)} %collective-permute-done.refs_1_), channel_id=1, source_target_pairs={{2,0},{0,2},{3,1},{1,3},{6,4},{4,6},{7,5},{5,7},{10,8},{8,10},{11,... | collective-permute-start | bytes 245768 | tf_op jit(solution)/shard_map/ppermute | solution.py:180
  8.9 5.8 %collective-permute-start.5 = (bf16[144,256]{1,0:T(8,128)(2,1)S(1)}, bf16[144,256]{1,0:T(8,128)(2,1)S(1)}, u32[]{:S(2)}, u32[]{:S(2)}) collective-permute-start(bf16[144,256]{1,0:T(8,128)(2,1)S(1)} %get-tuple-element.11.refs_2_.refs_4_), channel_id=1, source_target_pairs={{5,0},{4,1},{1,4},{0,5},{13,8},{12,9},{9,12},{8,13},{7,2},{6,3},{3... | collective-permute-start | bytes 221192 | tf_op jit(solution)/shard_map/ppermute | solution.py:195
  15.5 4.3 %collective-permute-start.8 = (f32[4,16,256]{2,1,0:T(8,128)S(1)}, f32[4,16,256]{2,1,0:T(8,128)S(1)}, u32[]{:S(2)}, u32[]{:S(2)}) collective-permute-start(f32[4,16,256]{2,1,0:T(8,128)S(1)} %shard_map.70.refs_5_), channel_id=1, source_target_pairs={{3,0},{2,1},{1,2},{0,3},{7,4},{6,5},{5,6},{4,7},{11,8},{10,9},{9,1... | collective-permute-start | bytes 196616 | tf_op jit(solution)/shard_map/ppermute | solution.py:180
  16.6 4.7 %collective-permute-start.7 = (f32[4,16,256]{2,1,0:T(8,128)S(1)}, f32[4,16,256]{2,1,0:T(8,128)S(1)}, u32[]{:S(2)}, u32[]{:S(2)}) collective-permute-start(f32[4,16,256]{2,1,0:T(8,128)S(1)} %shard_map.70.refs_5_), channel_id=1, source_target_pairs={{2,0},{3,1},{0,2},{1,3},{6,4},{7,5},{4,6},{5,7},{10,8},{11,9},{8,1... | collective-permute-start | bytes 196616 | tf_op jit(solution)/shard_map/ppermute | solution.py:180
  17.1 4.2 %collective-permute-start.6 = (f32[4,16,256]{2,1,0:T(8,128)S(1)}, f32[4,16,256]{2,1,0:T(8,128)S(1)}, u32[]{:S(2)}, u32[]{:S(2)}) collective-permute-start(f32[4,16,256]{2,1,0:T(8,128)S(1)} %shard_map.70.refs_5_), channel_id=1, source_target_pairs={{1,0},{0,1},{3,2},{2,3},{5,4},{4,5},{7,6},{6,7},{9,8},{8,9},{11,10... | collective-permute-start | bytes 196616 | tf_op jit(solution)/shard_map/ppermute | solution.py:180
  21.4 5.0 %collective-permute-start.11 = (f32[16,128]{1,0:T(8,128)S(1)}, f32[16,128]{1,0:T(8,128)S(1)}, u32[]{:S(2)}, u32[]{:S(2)}) collective-permute-start(f32[16,128]{1,0:T(8,128)S(1)} %get-tuple-element.16.refs_0_), channel_id=1, source_target_pairs={{13,0},{12,1},{9,4},{8,5},{5,8},{4,9},{1,12},{0,13},{15,2},{14,3},... | collective-permute-start | bytes 24584 | tf_op jit(solution)/shard_map/ppermute | solution.py:195
  22.3 4.1 %collective-permute-start.10 = (f32[16,128]{1,0:T(8,128)S(1)}, f32[16,128]{1,0:T(8,128)S(1)}, u32[]{:S(2)}, u32[]{:S(2)}) collective-permute-start(f32[16,128]{1,0:T(8,128)S(1)} %get-tuple-element.16.refs_0_), channel_id=1, source_target_pairs={{5,0},{4,1},{1,4},{0,5},{13,8},{12,9},{9,12},{8,13},{7,2},{6,3},{3... | collective-permute-start | bytes 24584 | tf_op jit(solution)/shard_map/ppermute | solution.py:195
  23.1 4.0 %collective-permute-start.9 = (f32[16,128]{1,0:T(8,128)S(1)}, f32[16,128]{1,0:T(8,128)S(1)}, u32[]{:S(2)}, u32[]{:S(2)}) collective-permute-start(f32[16,128]{1,0:T(8,128)S(1)} %get-tuple-element.16.refs_0_), channel_id=1, source_target_pairs={{9,0},{8,1},{13,4},{12,5},{1,8},{0,9},{5,12},{4,13},{11,2},{10,3},... | collective-permute-start | bytes 24584 | tf_op jit(solution)/shard_map/ppermute | solution.py:195
